TPU v7x, 128 devices: a whole 4x4x4 slice. The times are simulated.
128 devices in a mesh: row: 16 (over z, y_hi, core), col: 8 (over y_lo, x).
Axes of the slice: x: 4, y: 4 (y_hi: 2, y_lo: 2; y = y_hi * 2 + y_lo), z: 4, core: 2. Of those that a mesh axis runs over, the one named last changes fastest.
Arguments:
- query_rows: bfloat16 [8192, 8192], P('row', 'col'), may hold values from -100 to 100
- key_rows: bfloat16 [8192, 1024], P('row', 'col'), may hold values from -4 to 4
- value_rows: bfloat16 [8192, 1024], P('row', 'col'), may hold values from -6 to 6
- output_grad: bfloat16 [8192, 8192], P('row', 'col'), may hold values from -6 to 6
- out_proj: bfloat16 [8192, 8192], P('row', 'col'), may hold values from -0.0625 to 0.0625
- segment_ids: int32 [8192], replicated, may hold values from 0 to 3, as said below
Outputs:
- query_grad: bfloat16 [8192, 8192], P('row', 'col')
- key_grad: bfloat16 [8192, 1024], P('row', 'col')
- value_grad: bfloat16 [8192, 1024], P('row', 'col')
- proj_grad: bfloat16 [8192, 8192], P('row', 'col')
Inputs may be any that keep to these rules, and one draw needn't show every extreme that they name: `segment_ids`: ids never fall and start at 0 with token 0. Exactly three tokens have an id one more than their predecessor's; they lie in three different aligned blocks of 512 tokens and are never a block's first token.
All inputs are finite; a program needn't handle non-finite values.
Results may differ from a plain program's by a relative error of at most 0.017.
Values may be sent and summed in bfloat16 or wider, within the bound.
No kernel may reach another device: no remote copies, remote signals or barrier semaphores. Data moves between devices by JAX's collectives and lax.ppermute only.
A program may use at most 192 MiB of HBM per device.

v0:
```python
import math

import jax
import jax.numpy as jnp
from jax import lax
from jax.sharding import PartitionSpec as P

HD = 128


def passed_along(value, axis, steps):
    count = lax.axis_size(axis)
    first, last = (max(0, -steps), min(count, count - steps))
    return lax.ppermute(value, axis, [(source, source + steps) for source in range(first, last)])


def allowed_mask(segment_ids, block, count):
    query_pos = block * count + jnp.arange(count, dtype=jnp.int32)
    key_pos = (block - 1) * count + jnp.arange(2 * count, dtype=jnp.int32)
    seg_query = lax.dynamic_slice_in_dim(segment_ids, block * count, count, 0)
    seg_earlier = lax.dynamic_slice_in_dim(segment_ids, jnp.maximum(block - 1, 0) * count, count, 0)
    seg_keys = jnp.concatenate([seg_earlier, seg_query], 0)
    same_list = seg_keys[None, :] == seg_query[:, None]
    causal = key_pos[None, :] <= query_pos[:, None]
    present = key_pos[None, :] >= 0
    return same_list & causal & present


def block_pass(query_blk, key_pair, value_pair, grad_blk, allowed):
    head_count = query_blk.shape[1] // HD
    group_count = key_pair.shape[1] // HD
    per_group = head_count // group_count
    score_scale = 1.0 / math.sqrt(HD)

    def one_head(head_index):
        query_head = lax.dynamic_slice_in_dim(query_blk, head_index * HD, HD, 1)
        grad_head = lax.dynamic_slice_in_dim(grad_blk, head_index * HD, HD, 1)
        scores = (
            lax.dot_general(
                query_head, key_pair, (((1,), (1,)), ((), ())), preferred_element_type=jnp.float32
            )
            * score_scale
        )
        scores = jnp.where(allowed, scores, -jnp.inf)
        row_top = jnp.max(scores, axis=1, keepdims=True)
        expo = jnp.exp(scores - row_top)
        attn_probs = expo / jnp.sum(expo, axis=1, keepdims=True)
        probs_low = attn_probs.astype(jnp.bfloat16)
        out_head = jnp.dot(probs_low, value_pair, preferred_element_type=jnp.float32).astype(
            jnp.bfloat16
        )
        dprobs = lax.dot_general(
            grad_head, value_pair, (((1,), (1,)), ((), ())), preferred_element_type=jnp.float32
        )
        row_delta = jnp.sum(attn_probs * dprobs, axis=1, keepdims=True)
        dscore = (attn_probs * (dprobs - row_delta)).astype(jnp.bfloat16)
        dquery = jnp.dot(dscore, key_pair, preferred_element_type=jnp.float32) * score_scale
        dkey = (
            lax.dot_general(
                dscore, query_head, (((0,), (0,)), ((), ())), preferred_element_type=jnp.float32
            )
            * score_scale
        )
        dvalue = lax.dot_general(
            probs_low, grad_head, (((0,), (0,)), ((), ())), preferred_element_type=jnp.float32
        )
        return (out_head, dquery, dkey, dvalue)

    out_heads, dquery_heads, dkey_heads, dvalue_heads = lax.map(
        one_head, jnp.arange(head_count, dtype=jnp.int32)
    )
    count = query_blk.shape[0]
    attn_out = jnp.transpose(out_heads, (1, 0, 2)).reshape(count, head_count * HD)
    dquery_all = jnp.transpose(dquery_heads, (1, 0, 2)).reshape(count, head_count * HD)
    dkey_all = jnp.sum(dkey_heads.reshape(group_count, per_group, 2 * count, HD), axis=1)
    dvalue_all = jnp.sum(dvalue_heads.reshape(group_count, per_group, 2 * count, HD), axis=1)
    dkey_all = jnp.transpose(dkey_all, (1, 0, 2)).reshape(2 * count, group_count * HD)
    dvalue_all = jnp.transpose(dvalue_all, (1, 0, 2)).reshape(2 * count, group_count * HD)
    return (attn_out, dquery_all, dkey_all, dvalue_all)


def local(query_rows, key_rows, value_rows, output_grad, out_proj, segment_ids):
    tok_count = query_rows.shape[0]
    whole_grad = lax.all_gather(output_grad, "col", axis=1, tiled=True)
    columns = whole_grad
    attn_grad = jnp.dot(
        columns,
        lax.all_gather(out_proj, "row", axis=0, tiled=True),
        preferred_element_type=jnp.float32,
    ).astype(jnp.bfloat16)
    earlier_key, earlier_value = passed_along((key_rows, value_rows), "row", 1)
    block = lax.axis_index("row")
    allowed = allowed_mask(segment_ids, block, tok_count)
    key_pair = jnp.concatenate([earlier_key, key_rows], 0)
    value_pair = jnp.concatenate([earlier_value, value_rows], 0)
    attn_out, dquery_all, dkey_all, dvalue_all = block_pass(
        query_rows, key_pair, value_pair, attn_grad, allowed
    )
    back_key, back_value = (
        passed_along(dkey_all[:tok_count].astype(jnp.bfloat16), "row", -1).astype(jnp.float32),
        passed_along(dvalue_all[:tok_count].astype(jnp.bfloat16), "row", -1).astype(jnp.float32),
    )
    key_grad = (dkey_all[tok_count:] + back_key).astype(jnp.bfloat16)
    value_grad = (dvalue_all[tok_count:] + back_value).astype(jnp.bfloat16)
    query_grad = dquery_all.astype(jnp.bfloat16)
    columns = whole_grad
    proj_total = lax.psum_scatter(
        lax.dot_general(
            columns, attn_out, (((0,), (0,)), ((), ())), preferred_element_type=jnp.float32
        ).astype(jnp.bfloat16),
        "row",
        scatter_dimension=0,
        tiled=True,
    )
    return (query_grad, key_grad, value_grad, proj_total)


def solution(mesh):
    placed = (
        P("row", "col"),
        P("row", "col"),
        P("row", "col"),
        P("row", "col"),
        P("row", "col"),
        P(),
    )
    return jax.shard_map(
        local,
        mesh=mesh,
        in_specs=placed,
        out_specs=(P("row", "col"), P("row", "col"), P("row", "col"), P("row", "col")),
        check_vma=False,
    )
```

profile of v0, /device:TPU:1, one launch (start us, length us, event | category | flops | bytes accessed | tf_op | source)
XLA Modules:
  0.0 499.5 jit_solution(8904108957661906782)
XLA Ops:
  7.2 0.7 all-gather.3.cloned.1.call-update
  8.0 0.7 all-gather.5.cloned.1.call-update
  8.7 6.2 %collective-permute-start = (bf16[512,128]{1,0:T(8,128)(2,1)S(1)}, bf16[512,128]{1,0:T(8,128)(2,1)S(1)}, u32[]{:S(2)}, u32[]{:S(2)}) collective-permute-start(bf16[512,128]{1,0:T(8,128)(2,1)S(1)} %copy-done.1), channel_id=1, source_target_pairs={{0,8},{8,16},{16,24},{24,32},{32,40},{40,48},{48,56},{56,64},{64,7... | collective-permute-start | bytes 393224 | tf_op jit(solution)/shard_map/ppermute | solution.py:14
  15.0 1.9 collective-permute-start.1
  16.9 0.8 fusion.30
  17.8 1.0 collective-permute-done.1
  18.8 85.9 %all-gather.3.cloned.1.call-done = bf16[512,8192]{1,0:T(8,128)(2,1)} async-done(((bf16[512,1024]{1,0:T(8,128)(2,1)}), bf16[512,8192]{1,0:T(8,128)(2,1)}) %all-gather.3.cloned.1.call-update) | async-done | bytes 8388624 | tf_op jit(solution)/shard_map/all_gather | solution.py:84
  104.8 111.2 %all-gather.5.cloned.1.call-done = bf16[8192,1024]{1,0:T(8,128)(2,1)} async-done(((bf16[512,1024]{1,0:T(8,128)(2,1)}), bf16[8192,1024]{1,0:T(8,128)(2,1)}) %all-gather.5.cloned.1.call-update) | async-done | bytes 16777232 | tf_op jit(solution)/shard_map/all_gather | solution.py:88
  215.9 15.6 %convolution_convert_fusion.1 = bf16[512,1024]{1,0:T(8,128)(2,1)} fusion(bf16[512,8192]{1,0:T(8,128)(2,1)} %all-gather.3.cloned.1.call-done, bf16[8192,1024]{1,0:T(8,128)(2,1)} %all-gather.5.cloned.1.call-done), kind=kOutput, calls=%fused_computation.30 | convolution fusion | flops 8590458880 | bytes 26214400 | tf_op jit(solution)/shard_map/dot_general | solution.py:86
  231.5 101.0 %while.17 = (s32[]{:T(128)}, bf16[8,512,128]{1,2,0:T(8,128)(2,1)}, bf16[8,512,128]{2,1,0:T(8,128)(2,1)}, f32[8,1024,128]{2,1,0:T(8,128)}, f32[8,1024,128]{2,1,0:...) while((s32[]{:T(128)}, bf16[8,512,128]{1,2,0:T(8,128)(2,1)}, ...), condition=%wide.region_4.5_spmd.clone, body=%wide.region_0.4_spmd.clone.sunk | while | flops 818149888 | bytes 23502096 | solution.py:69
  232.8 1.7 fusion.68
  235.7 0.7 constant_dynamic-update-slice_fusion.2
  236.3 1.6 multiply_reduce_fusion.2
  238.5 1.1 fusion.71
  239.6 2.4 fusion.73
  242.0 2.2 fusion.72
  245.5 1.7 fusion.68
  248.3 0.7 constant_dynamic-update-slice_fusion.2
  249.0 1.5 multiply_reduce_fusion.2
  251.1 1.1 fusion.71
  252.3 2.4 fusion.73
  254.7 2.2 fusion.72
  258.1 1.7 fusion.68
  261.7 1.6 multiply_reduce_fusion.2
  263.9 1.1 fusion.71
  265.0 2.4 fusion.73
  267.3 2.2 fusion.72
  270.7 1.7 fusion.68
  274.3 1.6 multiply_reduce_fusion.2
  276.4 1.1 fusion.71
  277.5 2.4 fusion.73
  279.9 2.2 fusion.72
  283.3 1.7 fusion.68
  286.9 1.5 multiply_reduce_fusion.2
  289.0 1.1 fusion.71
  290.1 2.4 fusion.73
  292.5 2.2 fusion.72
  296.0 1.7 fusion.68
  299.5 1.6 multiply_reduce_fusion.2
  301.7 1.1 fusion.71
  302.8 2.4 fusion.73
  305.2 2.2 fusion.72
  308.6 1.7 fusion.68
  312.1 1.5 multiply_reduce_fusion.2
  314.3 1.1 fusion.71
  315.4 2.4 fusion.73
  317.8 2.2 fusion.72
  321.2 1.7 fusion.68
  324.7 1.6 multiply_reduce_fusion.2
  326.9 1.1 fusion.71
  328.0 2.4 fusion.73
  330.4 2.2 fusion.72
  332.5 14.7 %convert_bitcast_fusion = bf16[8192,1024]{0,1:T(8,128)(2,1)} fusion(bf16[512,1024]{0,1:T(8,128)(2,1)} %bitcast.82, bf16[512,8192]{1,0:T(8,128)(2,1)} %all-gather.3.cloned.1.call-done), kind=kOutput, calls=%fused_computation.29 | convolution fusion | flops 8598323200 | bytes 26214400 | tf_op jit(solution)/shard_map/dot_general | solution.py:108
  347.3 2.4 reduce_sum.42
  349.8 2.5 reduce_sum.40
  352.3 2.2 collective-permute-start.2
  354.5 1.9 collective-permute-start.3
  356.4 1.1 copy_bitcast_fusion
  357.6 2.5 collective-permute-done.2
  360.1 0.7 fusion.26
  360.8 1.5 collective-permute-done.3
  362.3 0.7 fusion.24
  363.0 127.7 %reduce-scatter.2.cloned.1.call-done = bf16[512,1024]{0,1:T(8,128)(2,1)} async-done(((bf16[8192,1024]{0,1:T(8,128)(2,1)}), bf16[512,1024]{0,1:T(8,128)(2,1)}) %reduce-scatter.2.cloned.1.call-update) | async-done | bytes 1048592 | tf_op jit(solution)/shard_map/reduce_scatter | solution.py:107
  490.7 2.3 copy.14
  (69 shorter events, 22.7 us)
Async XLA Ops:
  7.2 1.6 copy-start.1
  7.2 7.8 %copy-start.2 = (bf16[512,128]{1,0:T(8,128)(2,1)S(1)}, bf16[512,128]{1,0:T(8,128)(2,1)}, u32[]{:S(2)}) copy-start(bf16[512,128]{1,0:T(8,128)(2,1)} %param.10) | copy-start | bytes 393220
  7.2 97.6 %all-gather.3.cloned.1.call-start = ((), (), s32[]{:S(2)}) async-start(), calls=%async_computation.1 | async-start | bytes 9437184 | tf_op jit(solution)/shard_map/all_gather | solution.py:84
  7.9 208.0 %all-gather.5.cloned.1.call-start = ((), (), s32[]{:S(2)}) async-start(), calls=%async_computation.2 | async-start | bytes 17825792 | tf_op jit(solution)/shard_map/all_gather | solution.py:88
  8.7 482.0 %reduce-scatter.2.cloned.1.call-start = ((), (), s32[]{:S(2)}) async-start(), calls=%async_computation.3 | async-start | bytes 17825792 | tf_op jit(solution)/shard_map/reduce_scatter | solution.py:107
  8.7 9.1 %collective-permute-start = (bf16[512,128]{1,0:T(8,128)(2,1)S(1)}, bf16[512,128]{1,0:T(8,128)(2,1)S(1)}, u32[]{:S(2)}, u32[]{:S(2)}) collective-permute-start(bf16[512,128]{1,0:T(8,128)(2,1)S(1)} %copy-done.1), channel_id=1, source_target_pairs={{0,8},{8,16},{16,24},{24,32},{32,40},{40,48},{48,56},{56,64},{64,7... | collective-permute-start | bytes 393224 | tf_op jit(solution)/shard_map/ppermute | solution.py:14
  15.0 3.9 collective-permute-start.1
  349.8 6.7 %copy-start = (bf16[8,512,128]{2,1,0:T(8,128)(2,1)S(1)}, bf16[8,512,128]{2,1,0:T(8,128)(2,1)}, u32[]{:S(2)}) copy-start(bf16[8,512,128]{2,1,0:T(8,128)(2,1)} %get-tuple-element.64) | copy-start | bytes 3145732
  352.3 7.8 %collective-permute-start.2 = (bf16[512,128]{1,0:T(8,128)(2,1)S(1)}, bf16[512,128]{1,0:T(8,128)(2,1)S(1)}, u32[]{:S(2)}, u32[]{:S(2)}) collective-permute-start(bf16[512,128]{1,0:T(8,128)(2,1)S(1)} %fusion.27), channel_id=1, source_target_pairs={{8,0},{16,8},{24,16},{32,24},{40,32},{48,40},{56,48},{64,56},{72,6... | collective-permute-start | bytes 393224 | tf_op jit(solution)/shard_map/ppermute | solution.py:14
  354.5 7.8 %collective-permute-start.3 = (bf16[512,128]{1,0:T(8,128)(2,1)S(1)}, bf16[512,128]{1,0:T(8,128)(2,1)S(1)}, u32[]{:S(2)}, u32[]{:S(2)}) collective-permute-start(bf16[512,128]{1,0:T(8,128)(2,1)S(1)} %fusion.28), channel_id=1, source_target_pairs={{8,0},{16,8},{24,16},{32,24},{40,32},{48,40},{56,48},{64,56},{72,6... | collective-permute-start | bytes 393224 | tf_op jit(solution)/shard_map/ppermute | solution.py:14
Sparse Core Ops, SparseCore 0:
  9.7 95.0 all-gather.2
  107.2 108.6 all-gather.4
  347.4 143.2 reduce-scatter.1
where the time goes:
time: 500 us; the launch traced here: 499 us
  waiting for transfers between devices  331 us (66%)
  matrix products  106 us (21%)
  local copies, waits for them, and re-layouts  15.2 us (3%)
  other arithmetic  15 us (3%)
  between operations  13.9 us (3%)
  starting transfers between devices  12.3 us (2%)
  loops' own time  5.44 us (1%)
    reduce_scatter x1, waiting for transfers between devices, local(): lax.psum_scatter(lax.dot_general(columns, attn_out, (((0,), (0,)), ((), (...  128 us
    all_gather x1, waiting for transfers between devices, local(): lax.all_gather(out_proj, 'row', axis=0, tiled=True)  111 us
    all_gather x1, waiting for transfers between devices, local(): whole_grad = lax.all_gather(output_grad, 'col', axis=1, tiled=True)  85.9 us
    dot_general x8, matrix products, one_head(): lax.dot_general(probs_low, grad_head, (((0,), (0,)), ((), ())), preferred...  19.2 us
    dot_general x8, matrix products, one_head(): lax.dot_general(dscore, query_head, (((0,), (0,)), ((), ())), preferred_e...  17.4 us
    dot_general x1, matrix products, local(): jnp.dot(columns, lax.all_gather(out_proj, 'row', axis=0, tiled=True), pre...  15.6 us
    dot_general x1, matrix products, local(): lax.dot_general(columns, attn_out, (((0,), (0,)), ((), ())), preferred_el...  14.7 us
    dot_general x8, matrix products, one_head(): lax.dot_general(query_head, key_pair, (((1,), (1,)), ((), ())), preferred...  13.8 us
  transfers between devices with their start and end apart: 7, of which 6 were waited for; matrix products, arithmetic and copies ran while one was open for 2% of the time, Pallas kernels for 0%

commit v1 on v0

v1 whole, which is shorter than its diff:
```python
import functools
import math

import jax
import jax.numpy as jnp
from jax import lax
from jax.experimental import pallas as pl
from jax.experimental.pallas import tpu as pltpu
from jax.sharding import PartitionSpec as P

HD = 128
SCALE = 1.0 / math.sqrt(HD)
NEG = -1e30
BF = jnp.bfloat16
F32 = jnp.float32

ZN, YN, KN, LN, XN = 4, 2, 2, 2, 4


def move_row(value, dz=0, dyh=0, dk=0):
    pairs = []
    for z in range(ZN):
        for y in range(YN):
            for k in range(KN):
                source = (z * YN + y) * KN + k
                target = ((z + dz) % ZN * YN + (y + dyh) % YN) * KN + (k + dk) % KN
                pairs.append((source, target))
    return lax.ppermute(value, "row", pairs)


def move_col(value, dx=0, dyl=0):
    pairs = []
    for y in range(LN):
        for x in range(XN):
            pairs.append((y * XN + x, (y + dyl) % LN * XN + (x + dx) % XN))
    return lax.ppermute(value, "col", pairs)


def passed_along(value, axis, steps):
    count = lax.axis_size(axis)
    first, last = (max(0, -steps), min(count, count - steps))
    return lax.ppermute(value, axis, [(source, source + steps) for source in range(first, last)])


def tied(values, *others):
    held = lax.optimization_barrier((tuple(values), tuple(others)))
    return held[0]


def params(mib, **kw):
    return pltpu.CompilerParams(vmem_limit_bytes=mib * 1024 * 1024, **kw)


def fill_bias(bias_ref, segq, segk, first_block, count):
    key = lax.broadcasted_iota(jnp.int32, (2 * count, count), 0)
    query = lax.broadcasted_iota(jnp.int32, (2 * count, count), 1)
    ok = (key <= query + count) & (segk == segq) & (key >= first_block * count)
    bias_ref[...] = jnp.where(ok, 0.0, NEG).astype(F32)


def chunk_list(count, width):
    return [(i * width, count + (i + 1) * width) for i in range(count // width)]


def fwd_kernel(meta_ref, q_ref, k_ref, vt_ref, segq_ref, segk_ref, out_ref, top_ref, sum_ref, bias_ref):
    count = q_ref.shape[0]

    @pl.when(pl.program_id(0) == 0)
    def _():
        fill_bias(bias_ref, segq_ref[...], segk_ref[...], meta_ref[0], count)

    for start, keys in chunk_list(count, 256):
        cols = slice(start, start + 256)
        s = lax.dot_general(
            k_ref[:keys, :], q_ref[cols, :], (((1,), (1,)), ((), ())), preferred_element_type=F32
        )
        s = s * SCALE + bias_ref[:keys, cols]
        top = jnp.max(s, axis=0, keepdims=True)
        e = jnp.exp(s - top)
        total = jnp.sum(e, axis=0, keepdims=True)
        inv = 1.0 / total
        p = (e * inv).astype(BF)
        a = jnp.dot(vt_ref[:, :keys], p, preferred_element_type=F32)
        out_ref[cols, :] = a.T.astype(BF)
        top_ref[0, :, cols] = top
        sum_ref[0, :, cols] = inv


def attend(query, key_pair, vt, segq, segk, first):
    count, width = query.shape
    heads = width // HD
    whole = lambda shape: pl.BlockSpec(shape, lambda h, m: (0,) * len(shape))
    head = pl.BlockSpec((count, HD), lambda h, m: (0, h))
    stat = pl.BlockSpec((1, 1, count), lambda h, m: (h, 0, 0))
    return pl.pallas_call(
        fwd_kernel,
        grid_spec=pltpu.PrefetchScalarGridSpec(
            num_scalar_prefetch=1,
            grid=(heads,),
            in_specs=[
                head,
                whole((2 * count, HD)),
                whole((HD, 2 * count)),
                whole((1, count)),
                whole((2 * count, 1)),
            ],
            out_specs=[head, stat, stat],
            scratch_shapes=[pltpu.VMEM((2 * count, count), F32)],
        ),
        out_shape=[
            jax.ShapeDtypeStruct((count, width), BF),
            jax.ShapeDtypeStruct((heads, 1, count), F32),
            jax.ShapeDtypeStruct((heads, 1, count), F32),
        ],
        compiler_params=params(40),
        cost_estimate=pl.CostEstimate(
            flops=heads * 4 * 2 * 2 * count * count * HD,
            bytes_accessed=8 * 2**20,
            transcendentals=heads * 2 * count * count,
        ),
        name="attend",
    )(first, query, key_pair, vt, segq, segk)


def bwd_kernel(
    meta_ref, q_ref, g_ref, k_ref, kt_ref, v_ref, segq_ref, segk_ref, top_ref, sum_ref,
    dq_ref, dk_ref, dv_ref, bias_ref,
):
    count = q_ref.shape[0]

    @pl.when(pl.program_id(0) == 0)
    def _():
        fill_bias(bias_ref, segq_ref[...], segk_ref[...], meta_ref[0], count)
        dk_ref[...] = jnp.zeros_like(dk_ref)
        dv_ref[...] = jnp.zeros_like(dv_ref)

    for start, keys in chunk_list(count, 256):
        cols = slice(start, start + 256)
        q = q_ref[cols, :]
        g = g_ref[cols, :]
        s = lax.dot_general(
            k_ref[:keys, :], q, (((1,), (1,)), ((), ())), preferred_element_type=F32
        )
        s = s * SCALE + bias_ref[:keys, cols]
        p = jnp.exp(s - top_ref[0, :, cols]) * sum_ref[0, :, cols]
        dp = lax.dot_general(
            v_ref[:keys, :], g, (((1,), (1,)), ((), ())), preferred_element_type=F32
        )
        delta = jnp.sum(p * dp, axis=0, keepdims=True)
        ds = (p * (dp - delta)).astype(BF)
        dq = jnp.dot(kt_ref[:, :keys], ds, preferred_element_type=F32) * SCALE
        dq_ref[cols, :] = dq.T.astype(BF)
        dk_ref[:keys, :] += jnp.dot(ds, q, preferred_element_type=F32)
        dv_ref[:keys, :] += jnp.dot(p.astype(BF), g, preferred_element_type=F32)

    @pl.when(pl.program_id(0) == pl.num_programs(0) - 1)
    def _():
        dk_ref[...] = dk_ref[...] * SCALE


def attend_back(query, grad, key_pair, kt, value_pair, segq, segk, first, top, total):
    count, width = query.shape
    heads = width // HD
    whole = lambda shape: pl.BlockSpec(shape, lambda h, m: (0,) * len(shape))
    head = pl.BlockSpec((count, HD), lambda h, m: (0, h))
    stat = pl.BlockSpec((1, 1, count), lambda h, m: (h, 0, 0))
    pair = whole((2 * count, HD))
    return pl.pallas_call(
        bwd_kernel,
        grid_spec=pltpu.PrefetchScalarGridSpec(
            num_scalar_prefetch=1,
            grid=(heads,),
            in_specs=[
                head,
                head,
                pair,
                whole((HD, 2 * count)),
                pair,
                whole((1, count)),
                whole((2 * count, 1)),
                stat,
                stat,
            ],
            out_specs=[head, pair, pair],
            scratch_shapes=[pltpu.VMEM((2 * count, count), F32)],
        ),
        out_shape=[
            jax.ShapeDtypeStruct((count, width), BF),
            jax.ShapeDtypeStruct((2 * count, HD), F32),
            jax.ShapeDtypeStruct((2 * count, HD), F32),
        ],
        compiler_params=params(40),
        cost_estimate=pl.CostEstimate(
            flops=heads * 10 * 2 * 2 * count * count * HD,
            bytes_accessed=12 * 2**20,
            transcendentals=heads * 2 * count * count,
        ),
        name="attend_back",
    )(first, query, grad, key_pair, kt, value_pair, segq, segk, top, total)


def load_pieces(meta_ref, refs, plan, buffer, sems):
    copies = []
    for n, (ref_at, source, block, start, rows) in enumerate(plan):
        copies.append(
            pltpu.make_async_copy(
                refs[ref_at].at[pl.ds(source, rows)],
                buffer.at[meta_ref[block], pl.ds(start, rows)],
                sems.at[n],
            )
        )
    for copy in copies:
        copy.start()
    return copies


def proj_kernel(plan, n_in, meta_ref, *refs):
    pieces, a_ref = refs[:n_in], refs[n_in]
    out_ref = refs[n_in + 1]
    buffer, sems = refs[n_in + 2:]
    step = pl.program_id(0)

    @pl.when(step == 0)
    def _():
        for copy in load_pieces(meta_ref, pieces, plan, buffer, sems):
            copy.wait()

    block = buffer[meta_ref[8 + step]]
    out_ref[0] = lax.dot_general(
        block, a_ref[...], (((0,), (0,)), ((), ())), preferred_element_type=F32
    ).astype(BF)


def project(pieces, plan, meta, a_pair, first, count):
    tokens, width = a_pair.shape
    depth = pieces[0].shape[1]
    kernel = functools.partial(proj_kernel, plan, len(pieces))
    return pl.pallas_call(
        kernel,
        grid_spec=pltpu.PrefetchScalarGridSpec(
            num_scalar_prefetch=1,
            grid=(count,),
            in_specs=[pl.BlockSpec(memory_space=pl.ANY)] * len(pieces)
            + [pl.BlockSpec((tokens, width), lambda j, m: (0, 0))],
            out_specs=pl.BlockSpec((1, depth, width), lambda j, m: (j, 0, 0)),
            scratch_shapes=[
                pltpu.VMEM((8, tokens, depth), BF),
                pltpu.SemaphoreType.DMA((len(plan),)),
            ],
        ),
        out_shape=jax.ShapeDtypeStruct((count, depth, width), BF),
        compiler_params=params(44),
        cost_estimate=pl.CostEstimate(
            flops=2 * count * tokens * depth * width,
            bytes_accessed=(8 + 2 + count) * 2**20,
            transcendentals=0,
        ),
        name="project",
    )(jnp.concatenate([meta[:8], meta[8 + first:]]), *pieces, a_pair)


def grad_kernel(gplan, wplan, n_g, n_w, meta_ref, *refs):
    g_in, w_in = refs[:n_g], refs[n_g:n_g + n_w]
    own_ref, other_ref = refs[n_g + n_w:n_g + n_w + 2]
    gbuf, wbuf, total, gsems, wsems = refs[n_g + n_w + 2:]
    step = pl.program_id(0)
    half = own_ref.shape[0]

    @pl.when(step == 0)
    def _():
        copies = load_pieces(meta_ref, g_in, gplan, gbuf, gsems)
        copies += load_pieces(meta_ref, w_in, wplan, wbuf, wsems)
        for copy in copies:
            copy.wait()
        total[...] = jnp.dot(gbuf[0], wbuf[0], preferred_element_type=F32)

    @pl.when(step > 0)
    def _():
        total[...] += jnp.dot(gbuf[step], wbuf[step], preferred_element_type=F32)

    @pl.when(step == 7)
    def _():
        own_ref[...] = total[:half, :]
        other_ref[...] = total[half:, :].astype(BF)


def attn_grad_part(g_pieces, gplan, w_pieces, wplan, meta):
    tokens, depth = g_pieces[0].shape
    width = w_pieces[0].shape[1]
    half = tokens // 2
    kernel = functools.partial(grad_kernel, gplan, wplan, len(g_pieces), len(w_pieces))
    whole = pl.BlockSpec((half, width), lambda j, m: (0, 0))
    return pl.pallas_call(
        kernel,
        grid_spec=pltpu.PrefetchScalarGridSpec(
            num_scalar_prefetch=1,
            grid=(8,),
            in_specs=[pl.BlockSpec(memory_space=pl.ANY)] * (len(g_pieces) + len(w_pieces)),
            out_specs=[whole, whole],
            scratch_shapes=[
                pltpu.VMEM((8, tokens, depth), BF),
                pltpu.VMEM((8, depth, width), BF),
                pltpu.VMEM((tokens, width), F32),
                pltpu.SemaphoreType.DMA((len(gplan),)),
                pltpu.SemaphoreType.DMA((len(wplan),)),
            ],
        ),
        out_shape=[
            jax.ShapeDtypeStruct((half, width), F32),
            jax.ShapeDtypeStruct((half, width), BF),
        ],
        compiler_params=params(48),
        cost_estimate=pl.CostEstimate(
            flops=16 * tokens * depth * width,
            bytes_accessed=20 * 2**20,
            transcendentals=0,
        ),
        name="attn_grad",
    )(meta, *g_pieces, *w_pieces)


def add_up(*terms):
    total = terms[0].astype(F32)
    for term in terms[1:]:
        total = total + term.astype(F32)
    return total.astype(BF)


def local(query_rows, key_rows, value_rows, output_grad, out_proj, segment_ids):
    count = query_rows.shape[0]
    half_d = output_grad.shape[1] // 2
    row, col = lax.axis_index("row"), lax.axis_index("col")
    z, yh, k = row // 4, row // 2 % 2, row % 2
    yl, x = col // 4, col % 4

    def gblock(dyl, dx):
        return (yl + dyl) % 2 * 4 + (x + dx) % 4

    def wblock(dz, dy):
        return (z + dz) % 4 * 2 + (yh + dy) % 2

    def ints(*values):
        return jnp.stack([jnp.asarray(v, jnp.int32) for v in values])

    g_keep = lax.dynamic_slice_in_dim(output_grad, k * half_d, half_d, 1)
    g_give = lax.dynamic_slice_in_dim(output_grad, (1 - k) * half_d, half_d, 1)
    g0 = jnp.concatenate([g_keep, move_row(g_give, dk=1)], 0)
    kv = jnp.concatenate([key_rows, value_rows], 1)
    kv_earlier = passed_along(kv, "row", 1)

    gxm = move_col(g0, dx=1)
    gxp = move_col(g0, dx=-1)
    gy = move_col(g0, dyl=1)
    wzm = move_row(out_proj, dz=1)
    wzp = move_row(out_proj, dz=-1)

    kv_pair = jnp.concatenate([kv_earlier, kv], 0)
    key_pair, value_pair = kv_pair[:, :HD], kv_pair[:, HD:]
    key_t, value_t = key_pair.T, value_pair.T
    seg_query = lax.dynamic_slice_in_dim(segment_ids, row * count, count, 0)
    seg_earlier = lax.dynamic_slice_in_dim(
        segment_ids, jnp.maximum(row - 1, 0) * count, count, 0
    )
    segk = jnp.concatenate([seg_earlier, seg_query], 0)[:, None]
    segq = seg_query[None, :]
    first = ints(row == 0)
    (query_held,) = tied((query_rows,), g0)
    attn_out, top, total = attend(query_held, key_pair, value_t, segq, segk, first)
    a_other = move_row(attn_out, dk=1)
    a_pair = jnp.concatenate([attn_out, a_other], 0)

    gxm, gxp, gy, wzm, wzp, a_pair = tied((gxm, gxp, gy, wzm, wzp, a_pair))

    h = g0.shape[0] // 2
    hw = out_proj.shape[0] // 2
    gyxm = move_col(gy, dx=1)
    gyxp = move_col(gy, dx=-1)
    wom = move_row(wzm[:hw], dz=1)
    wop = move_row(wzp[hw:], dz=-1)
    wy = move_row(out_proj, dyh=1)

    gyxm, gyxp, wom, wop, wy = tied((gyxm, gyxp, wom, wop, wy))

    gom = move_col(jnp.concatenate([gxm[:h], gyxm[:h]], 0), dx=1)
    gop = move_col(jnp.concatenate([gxp[h:], gyxp[h:]], 0), dx=-1)
    wyzm = move_row(wy, dz=1)
    wyzp = move_row(wy, dz=-1)

    gom, gop, wyzm, wyzp = tied((gom, gop, wyzm, wyzp))

    wyom = move_row(wyzm[:hw], dz=1)
    wyop = move_row(wyzp[hw:], dz=-1)

    g_pieces = [g0, gxm, gxp, gy, gyxm, gyxp, gom, gop]
    gplan = [(i, 0, i, 0, 2 * h) for i in range(6)] + [
        (6, 0, 6, 0, h),
        (6, h, 7, 0, h),
        (7, 0, 6, h, h),
        (7, h, 7, h, h),
    ]
    g_order = ints(
        gblock(0, 0), gblock(0, -1), gblock(0, 1), gblock(1, 0),
        gblock(1, -1), gblock(1, 1), gblock(0, 2), gblock(1, 2),
        wblock(2, 1), wblock(2, 0), wblock(1, 1), wblock(-1, 1),
        wblock(1, 0), wblock(-1, 0), wblock(0, 1), wblock(0, 0),
    )
    far = project(g_pieces, gplan, g_order, a_pair, 0, 2)
    fm = move_row(jnp.concatenate([far[0, :hw], far[1, :hw]], 0), dz=1)
    fp = move_row(jnp.concatenate([far[0, hw:], far[1, hw:]], 0), dz=-1)
    near = project(g_pieces, gplan, g_order, a_pair, 2, 6)

    w_pieces = [out_proj, wzm, wzp, wy, wyzm, wyzp, wom, wop, wyom, wyop]
    wplan = [(i, 0, i, 0, 2 * hw) for i in range(6)] + [
        (6, 0, 6, 0, hw),
        (7, 0, 6, hw, hw),
        (8, 0, 7, 0, hw),
        (9, 0, 7, hw, hw),
    ]
    w_order = ints(
        wblock(0, 0), wblock(-1, 0), wblock(1, 0), wblock(0, 1),
        wblock(-1, 1), wblock(1, 1), wblock(2, 0), wblock(2, 1),
    )
    meta = jnp.concatenate([g_order[:8], w_order])
    wplan = [(i, s, b + 8, t, n) for i, s, b, t, n in wplan]
    grad_own, grad_give = attn_grad_part(g_pieces, gplan, w_pieces, wplan, meta)
    grad_got = move_row(grad_give, dk=1)
    attn_grad = (grad_own + grad_got.astype(F32)).astype(BF)

    fm, fp, near = tied((fm, fp, near))

    up = lambda block, extra: jnp.concatenate([add_up(block[:hw], extra), block[hw:]], 0)
    down = lambda block, extra: jnp.concatenate([block[:hw], add_up(block[hw:], extra)], 0)
    sup1 = move_row(up(near[0], fm[:hw]), dz=1)
    sdn1 = move_row(down(near[1], fp[:hw]), dz=-1)

    query_grad, dkey, dvalue = attend_back(
        query_rows, attn_grad, key_pair, key_t, value_pair, segq, segk, first, top, total
    )
    back = passed_along(
        jnp.concatenate([dkey[:count], dvalue[:count]], 1).astype(BF), "row", -1
    ).astype(F32)

    sup1, sdn1, = tied((sup1, sdn1))

    other = move_row(add_up(near[4], sup1, sdn1), dyh=1)
    sup0 = move_row(up(near[2], fm[hw:]), dz=1)
    sdn0 = move_row(down(near[3], fp[hw:]), dz=-1)
    proj_grad = add_up(near[5], sup0, sdn0, other)

    key_grad = (dkey[count:] + back[:, :HD]).astype(BF)
    value_grad = (dvalue[count:] + back[:, HD:]).astype(BF)
    return (query_grad, key_grad, value_grad, proj_grad)


def solution(mesh):
    placed = (
        P("row", "col"),
        P("row", "col"),
        P("row", "col"),
        P("row", "col"),
        P("row", "col"),
        P(),
    )
    return jax.shard_map(
        local,
        mesh=mesh,
        in_specs=placed,
        out_specs=(P("row", "col"), P("row", "col"), P("row", "col"), P("row", "col")),
        check_vma=False,
    )
```

time: 500 us -> 239 us (0.48)
  waiting for transfers between devices: 331 us -> 84.3 us
  matrix products: 106 us -> 0 us
  Pallas kernels: 0 us -> 69.7 us
  starting transfers between devices: 12.3 us -> 49.7 us
  between operations: 13.9 us -> 1.21 us
  loops' own time: 5.44 us -> 0 us
    all_gather x2 -> x0, waiting for transfers between devices: 197 us -> none  [the longest x1 111 us: local(): lax.all_gather(out_proj, 'row', axis=0, tiled=True)]
    reduce_scatter x1 -> x0, waiting for transfers between devices: 128 us -> none  [local(): lax.psum_scatter(lax.dot_general(columns, attn_out, (((0,), (0,)), ((), (...]
    dot_general x50 -> x0, matrix products: 106 us -> none  [the longest x8 19.2 us: one_head(): lax.dot_general(probs_low, grad_head, (((0,), (0,)), ((), ())), preferred...]
    ppermute x0 -> x26, waiting for transfers between devices: none -> 75.8 us  [the longest x19 55.9 us: move_row(): return lax.ppermute(value, 'row', pairs)]
    pallas_call x0 -> x5, Pallas kernels: none -> 69.7 us  [the longest x2 20.8 us: project(): pl.pallas_call(kernel, grid_spec=pltpu.PrefetchScalarGridSpec(num_scalar_...]
    ppermute x0 -> x26, starting transfers between devices: none -> 40.8 us  [the longest x19 31.5 us: move_row(): return lax.ppermute(value, 'row', pairs)]
    concatenate x3 -> x13, other arithmetic: 0.05 us -> 9.58 us  [the longest x2 2.3 us: local(): jnp.concatenate([block[:hw], add_up(block[hw:], extra)], 0)]
    reduce_sum x10 -> x0, other arithmetic: 8.82 us -> none  [the longest x8 3.84 us: one_head(): attn_probs = expo / jnp.sum(expo, axis=1, keepdims=True)]
  transfers between devices with their start and end apart: 7 -> 28, of which waited for: 6 -> 9; matrix products, arithmetic and copies ran while one was open for 2% -> 8% of each run, Pallas kernels for 0% -> 23%
where the time goes in v1:
time: 239 us
  waiting for transfers between devices  84.3 us (35%)
  Pallas kernels  69.7 us (29%)
  starting transfers between devices  49.7 us (21%)
  other arithmetic  18.6 us (8%)
  local copies, waits for them, and re-layouts  15.1 us (6%)
    ppermute x19, waiting for transfers between devices, move_row(): return lax.ppermute(value, 'row', pairs)  55.9 us
    ppermute x19, starting transfers between devices, move_row(): return lax.ppermute(value, 'row', pairs)  31.5 us
    pallas_call x2, Pallas kernels, project(): pl.pallas_call(kernel, grid_spec=pltpu.PrefetchScalarGridSpec(num_scalar_...  20.8 us
    ppermute x7, waiting for transfers between devices, move_col(): return lax.ppermute(value, 'col', pairs)  19.8 us
    pallas_call x1, Pallas kernels, attn_grad_part(): pl.pallas_call(kernel, grid_spec=pltpu.PrefetchScalarGridSpec(num_scalar_...  17.7 us
    pallas_call x1, Pallas kernels, attend_back(): pl.pallas_call(bwd_kernel, grid_spec=pltpu.PrefetchScalarGridSpec(num_sca...  16.9 us
    pallas_call x1, Pallas kernels, attend(): pl.pallas_call(fwd_kernel, grid_spec=pltpu.PrefetchScalarGridSpec(num_sca...  14.3 us
    ppermute x7, starting transfers between devices, move_col(): return lax.ppermute(value, 'col', pairs)  9.32 us
  transfers between devices with their start and end apart: 28, of which 9 were waited for; matrix products, arithmetic and copies ran while one was open for 8% of the time, Pallas kernels for 23%

profile of v1, /device:TPU:1, one launch (start us, length us, event | category | flops | bytes accessed | tf_op | source)
XLA Modules:
  0.0 238.5 jit_solution(5485595406486025894)
XLA Ops:
  0.7 2.1 constant_dynamic-slice_fusion.1
  2.8 1.4 collective-permute-start
  4.3 4.8 %collective-permute-start.6 = (bf16[512,256]{1,0:T(8,128)(2,1)S(1)}, bf16[512,256]{1,0:T(8,128)(2,1)}, u32[]{:S(2)}, u32[]{:S(2)}) collective-permute-start(bf16[512,256]{1,0:T(8,128)(2,1)S(1)} %constant_dynamic-update-slice_fusion), channel_id=1, source_target_pairs={{0,8},{8,16},{16,24},{24,32},{32,40},{40,48},{48,56},{56,64},{64,7... | collective-permute-start | bytes 786440 | tf_op jit(solution)/shard_map/ppermute | solution.py:42
  9.1 0.8 fusion.12
  10.0 0.2 copy.13.segk_ref
  10.2 2.2 collective-permute-done.6
  12.4 1.0 pad_maximum_fusion.10
  13.4 0.1 copy.12.vt_ref
  13.6 0.8 copy-done.21
  14.4 1.3 pad_maximum_fusion.1.refs_0_
  15.7 14.3 %attend.1 = (bf16[512,1024]{1,0:T(8,128)(2,1)S(1)}, f32[8,1,512]{2,1,0:T(1,128)S(1)}, f32[8,1,512]{2,1,0:T(1,128)S(1)}) custom-call(s32[1]{0:T(128)} %bitcast.meta_ref, bf16[512,1024]{1,0:T(8,128)(2,1)S(1)} %copy-done.12, bf16[1024,128]{1,0:T(8,128)(2,1)S(1)} %get-tuple-element.81.k_ref, bf16[128,1024]{1,0:T(8,128)(2,1)S(1)} %copy.12.vt_ref, ...), custom_call_target="tpu_custom_call" | custom-call | flops 4294967296 | bytes 8388608 | tf_op jit(solution)/shard_map/attend/pallas_call | solution.py:95
  30.1 3.8 %collective-permute-start.4 = (bf16[512,1024]{1,0:T(8,128)(2,1)S(1)}, bf16[512,1024]{1,0:T(8,128)(2,1)S(1)}, u32[]{:S(2)}, u32[]{:S(2)}) collective-permute-start(bf16[512,1024]{1,0:T(8,128)(2,1)S(1)} %copy-done.26), channel_id=1, source_target_pairs={{0,32},{8,40},{16,48},{24,56},{32,64},{40,72},{48,80},{56,88},{64,... | collective-permute-start | bytes 3145736 | tf_op jit(solution)/shard_map/ppermute | solution.py:28
  33.9 2.1 collective-permute-start.5
  36.0 1.2 collective-permute-start.1
  37.2 1.5 collective-permute-start.2
  38.7 1.3 collective-permute-start.3
  40.0 1.6 pad_maximum_fusion.refs_8_
  41.6 17.9 %collective-permute-done.4.refs_9_ = bf16[512,1024]{1,0:T(8,128)(2,1)S(1)} collective-permute-done((bf16[512,1024]{1,0:T(8,128)(2,1)S(1)}, bf16[512,1024]{1,0:T(8,128)(2,1)S(1)}, u32[]{:S(2)}, u32[]{:S(2)}) %collective-permute-start.4) | collective-permute-done | bytes 1048608 | tf_op jit(solution)/shard_map/ppermute | solution.py:28
  59.5 2.0 collective-permute-start.12
  61.5 0.8 collective-permute-done.3.refs_3_
  62.3 0.5 collective-permute-start.8
  62.8 2.2 collective-permute-start.9
  65.2 2.7 %collective-permute-start.11 = (bf16[256,1024]{1,0:T(8,128)(2,1)S(1)}, bf16[256,1024]{1,0:T(8,128)(2,1)S(1)}, u32[]{:S(2)}, u32[]{:S(2)}) collective-permute-start(bf16[256,1024]{1,0:T(8,128)(2,1)S(1)} %slice.143), channel_id=1, source_target_pairs={{0,96},{8,104},{16,112},{24,120},{32,0},{40,8},{48,16},{56,24},{64... | collective-permute-start | bytes 1572872 | tf_op jit(solution)/shard_map/ppermute | solution.py:28
  68.0 18.5 %collective-permute-done.12.refs_11_ = bf16[512,1024]{1,0:T(8,128)(2,1)} collective-permute-done((bf16[512,1024]{1,0:T(8,128)(2,1)S(1)}, bf16[512,1024]{1,0:T(8,128)(2,1)}, u32[]{:S(2)}, u32[]{:S(2)}) %collective-permute-start.12) | collective-permute-done | bytes 1048608 | tf_op jit(solution)/shard_map/ppermute | solution.py:28
  86.5 0.8 copy-done.14
  87.3 0.8 copy-done.16
  88.1 1.1 copy-done.2
  89.2 1.1 pad_maximum_fusion.2
  90.3 0.9 collective-permute-start.13
  91.3 1.1 pad_maximum_fusion.3
  92.4 1.7 collective-permute-start.14
  94.1 2.7 %collective-permute-start.16 = (bf16[512,1024]{1,0:T(8,128)(2,1)}, bf16[512,1024]{1,0:T(8,128)(2,1)}, u32[]{:S(2)}, u32[]{:S(2)}) collective-permute-start(bf16[512,1024]{1,0:T(8,128)(2,1)} %collective-permute-done.12.refs_11_), channel_id=1, source_target_pairs={{0,96},{8,104},{16,112},{24,120},{32,0},{40,8},{48,16},{56,24},{64... | collective-permute-start | bytes 3145736 | tf_op jit(solution)/shard_map/ppermute | solution.py:28
  96.9 0.1 concatenate.69.meta_ref
  97.1 17.5 %collective-permute-done.13.refs_6_ = bf16[1024,512]{1,0:T(8,128)(2,1)} collective-permute-done((bf16[1024,512]{1,0:T(8,128)(2,1)}, bf16[1024,512]{1,0:T(8,128)(2,1)}, u32[]{:S(2)}, u32[]{:S(2)}) %collective-permute-start.13) | collective-permute-done | bytes 1048608 | tf_op jit(solution)/shard_map/ppermute | solution.py:36
  114.6 1.5 collective-permute-done.14.refs_7_
  116.1 1.7 collective-permute-done.15.refs_12_
  117.8 1.1 slice.148
  119.0 1.1 slice.149
  120.1 2.7 %collective-permute-start.18 = (bf16[256,1024]{1,0:T(8,128)(2,1)S(1)}, bf16[256,1024]{1,0:T(8,128)(2,1)S(1)}, u32[]{:S(2)}, u32[]{:S(2)}) collective-permute-start(bf16[256,1024]{1,0:T(8,128)(2,1)S(1)} %slice.149), channel_id=1, source_target_pairs={{0,96},{8,104},{16,112},{24,120},{32,0},{40,8},{48,16},{56,24},{64... | collective-permute-start | bytes 1572872 | tf_op jit(solution)/shard_map/ppermute | solution.py:28
  122.8 1.2 copy-done.5
  124.0 1.2 copy-done.7
  125.2 7.8 %project.2 = bf16[2,512,1024]{2,1,0:T(8,128)(2,1)} custom-call(s32[16]{0:T(128)S(1)} %concatenate.69.meta_ref, bf16[1024,512]{1,0:T(8,128)(2,1)S(1)} %pad_maximum_fusion.1.refs_0_, bf16[1024,512]{1,0:T(8,128)(2,1)S(1)} %collective-permute-done.1.refs_1_, bf16[1024,512]{1,0:T(8,128)(2,1)S(1)} %copy-done.1, bf16[1024,512]{1,0:T(8,128)(2,1)S(1)} %copy-done.7, ...), custom_call_target="tpu_custom_call" | custom-call | flops 2147483648 | bytes 12582912 | tf_op jit(solution)/shard_map/project/pallas_call | solution.py:238
  133.0 1.7 slice_bitcast_fusion.1
  135.0 2.9 %collective-permute-start.22 = (bf16[512,1024]{1,0:T(8,128)(2,1)S(1)}, bf16[512,1024]{1,0:T(8,128)(2,1)S(1)}, u32[]{:S(2)}, u32[]{:S(2)}) collective-permute-start(bf16[512,1024]{1,0:T(8,128)(2,1)S(1)} %pad_maximum_fusion.5), channel_id=1, source_target_pairs={{0,96},{8,104},{16,112},{24,120},{32,0},{40,8},{48,16},{56,24},{64... | collective-permute-start | bytes 3145736 | tf_op jit(solution)/shard_map/ppermute | solution.py:28
  137.9 13.0 %project.3 = bf16[6,512,1024]{2,1,0:T(8,128)(2,1)} custom-call(s32[14]{0:T(128)S(1)} %concatenate.72.meta_ref, bf16[1024,512]{1,0:T(8,128)(2,1)S(1)} %pad_maximum_fusion.1.refs_0_, bf16[1024,512]{1,0:T(8,128)(2,1)S(1)} %collective-permute-done.1.refs_1_, bf16[1024,512]{1,0:T(8,128)(2,1)S(1)} %copy-done.1, bf16[1024,512]{1,0:T(8,128)(2,1)S(1)} %copy-done.7, ...), custom_call_target="tpu_custom_call" | custom-call | flops 6442450944 | bytes 16777216 | tf_op jit(solution)/shard_map/project/pallas_call | solution.py:238
  150.9 17.7 %attn_grad.1 = (f32[512,1024]{1,0:T(8,128)}, bf16[512,1024]{1,0:T(8,128)(2,1)S(1)}) custom-call(s32[16]{0:T(128)S(1)} %concatenate.60.meta_ref, bf16[1024,512]{1,0:T(8,128)(2,1)S(1)} %pad_maximum_fusion.1.refs_0_, bf16[1024,512]{1,0:T(8,128)(2,1)S(1)} %collective-permute-done.1.refs_1_, bf16[1024,512]{1,0:T(8,128)(2,1)} %copy-done, ...), custom_call_target="tpu_custom_call" | custom-call | flops 8589934592 | bytes 20971520 | tf_op jit(solution)/shard_map/attn_grad/pallas_call | solution.py:293
  168.7 4.6 %collective-permute-start.19 = (bf16[512,1024]{1,0:T(8,128)(2,1)S(1)}, bf16[512,1024]{1,0:T(8,128)(2,1)}, u32[]{:S(2)}, u32[]{:S(2)}) collective-permute-start(bf16[512,1024]{1,0:T(8,128)(2,1)S(1)} %get-tuple-element.50), channel_id=1, source_target_pairs={{0,8},{8,0},{16,24},{24,16},{32,40},{40,32},{48,56},{56,48},{64,72... | collective-permute-start | bytes 3145736 | tf_op jit(solution)/shard_map/ppermute | solution.py:28
  173.3 1.0 fusion.8
  174.3 1.2 slice_bitcast_fusion.7
  175.5 1.0 pad_maximum_fusion.8
  176.6 1.0 pad_maximum_fusion.9
  177.6 2.7 %collective-permute-start.26 = (bf16[512,1024]{1,0:T(8,128)(2,1)}, bf16[512,1024]{1,0:T(8,128)(2,1)}, u32[]{:S(2)}, u32[]{:S(2)}) collective-permute-start(bf16[512,1024]{1,0:T(8,128)(2,1)} %pad_maximum_fusion.9), channel_id=1, source_target_pairs={{0,96},{8,104},{16,112},{24,120},{32,0},{40,8},{48,16},{56,24},{64... | collective-permute-start | bytes 3145736 | tf_op jit(solution)/shard_map/ppermute | solution.py:28
  180.3 0.1 copy.14.kt_ref
  180.4 1.3 pad_maximum_fusion.7
  181.9 1.5 collective-permute-start.23
  183.4 1.6 add_convert_fusion.g_ref
  185.0 17.8 %collective-permute-done.25 = bf16[512,1024]{1,0:T(8,128)(2,1)} collective-permute-done((bf16[512,1024]{1,0:T(8,128)(2,1)}, bf16[512,1024]{1,0:T(8,128)(2,1)}, u32[]{:S(2)}, u32[]{:S(2)}) %collective-permute-start.25) | collective-permute-done | bytes 1048608 | tf_op jit(solution)/shard_map/ppermute | solution.py:28
  202.8 2.5 %fusion.1 = bf16[512,1024]{1,0:T(8,128)(2,1)S(1)} fusion(bf16[512,1024]{1,0:T(8,128)(2,1)} %collective-permute-done.26, bf16[512,1024]{1,0:T(8,128)(2,1)} %collective-permute-done.25, bf16[6,512,1024]{2,1,0:T(8,128)(2,1)} %project.3), kind=kLoop, calls=%fused_computation.3 | loop fusion | flops 3145728 | bytes 4194304 | tf_op jit(solution)/shard_map/convert_element_type | solution.py:326
  205.3 1.9 collective-permute-start.27
  207.3 16.9 %attend_back.1 = (bf16[512,1024]{1,0:T(8,128)(2,1)}, f32[1024,128]{1,0:T(8,128)S(1)}, f32[1024,128]{1,0:T(8,128)S(1)}) custom-call(s32[1]{0:T(128)} %bitcast.meta_ref, bf16[512,1024]{1,0:T(8,128)(2,1)S(1)} %copy-done.13, bf16[512,1024]{1,0:T(8,128)(2,1)S(1)} %add_convert_fusion.g_ref, bf16[1024,128]{1,0:T(8,128)(2,1)S(1)} %copy-done.9, ...), custom_call_target="tpu_custom_call" | custom-call | flops 10737418240 | bytes 12582912 | tf_op jit(solution)/shard_map/attend_back/pallas_call | solution.py:168
  224.2 4.1 %collective-permute-start.20 = (bf16[512,256]{1,0:T(8,128)(2,1)S(1)}, bf16[512,256]{1,0:T(8,128)(2,1)S(1)}, u32[]{:S(2)}, u32[]{:S(2)}) collective-permute-start(bf16[512,256]{1,0:T(8,128)(2,1)S(1)} %pad_maximum_fusion.11), channel_id=1, source_target_pairs={{8,0},{16,8},{24,16},{32,24},{40,32},{48,40},{56,48},{64,56},{72,6... | collective-permute-start | bytes 786440 | tf_op jit(solution)/shard_map/ppermute | solution.py:42
  228.3 6.3 %collective-permute-done.20 = bf16[512,256]{1,0:T(8,128)(2,1)S(1)} collective-permute-done((bf16[512,256]{1,0:T(8,128)(2,1)S(1)}, bf16[512,256]{1,0:T(8,128)(2,1)S(1)}, u32[]{:S(2)}, u32[]{:S(2)}) %collective-permute-start.20) | collective-permute-done | bytes 262176 | tf_op jit(solution)/shard_map/ppermute | solution.py:42
  234.6 0.8 fusion.10
  235.4 3.1 %fusion.4 = bf16[512,1024]{1,0:T(8,128)(2,1)} fusion(bf16[512,1024]{1,0:T(8,128)(2,1)S(1)} %collective-permute-done.27, bf16[512,1024]{1,0:T(8,128)(2,1)S(1)} %collective-permute-done.24, bf16[512,1024]{1,0:T(8,128)(2,1)S(1)} %collective-permute-done.23, bf16[6,512,1024]{2,1,0:T(8,128)(2,1)} %project.3), kind=kLoop, calls=%fused_computation.7 | loop fusion | flops 4194304 | bytes 5242880 | tf_op jit(solution)/shard_map/convert_element_type | solution.py:326
  (93 shorter events, 1.3 us)
Async XLA Ops:
  0.6 3.6 %copy-start.24 = (bf16[512,128]{1,0:T(8,128)(2,1)S(1)}, bf16[512,128]{1,0:T(8,128)(2,1)}, u32[]{:S(2)}) copy-start(bf16[512,128]{1,0:T(8,128)(2,1)} %param.7) | copy-start | bytes 393220
  0.6 3.6 %copy-start.25 = (bf16[512,128]{1,0:T(8,128)(2,1)S(1)}, bf16[512,128]{1,0:T(8,128)(2,1)}, u32[]{:S(2)}) copy-start(bf16[512,128]{1,0:T(8,128)(2,1)} %param.8) | copy-start | bytes 393220
  2.8 10.8 %collective-permute-start = (bf16[512,512]{1,0:T(8,128)(2,1)S(1)}, bf16[512,512]{1,0:T(8,128)(2,1)S(1)}, u32[]{:S(2)}, u32[]{:S(2)}) collective-permute-start(bf16[512,512]{1,0:T(8,128)(2,1)S(1)} %get-tuple-element.77), channel_id=1, source_target_pairs={{0,8},{8,0},{16,24},{24,16},{32,40},{40,32},{48,56},{56,48},{64,72... | collective-permute-start | bytes 1572872 | tf_op jit(solution)/shard_map/ppermute | solution.py:28
  4.3 8.1 %collective-permute-start.6 = (bf16[512,256]{1,0:T(8,128)(2,1)S(1)}, bf16[512,256]{1,0:T(8,128)(2,1)}, u32[]{:S(2)}, u32[]{:S(2)}) collective-permute-start(bf16[512,256]{1,0:T(8,128)(2,1)S(1)} %constant_dynamic-update-slice_fusion), channel_id=1, source_target_pairs={{0,8},{8,16},{16,24},{24,32},{32,40},{40,48},{48,56},{56,64},{64,7... | collective-permute-start | bytes 786440 | tf_op jit(solution)/shard_map/ppermute | solution.py:42
  10.0 5.7 %copy-start.12 = (bf16[512,1024]{1,0:T(8,128)(2,1)S(1)}, bf16[512,1024]{1,0:T(8,128)(2,1)}, u32[]{:S(2)}) copy-start(bf16[512,1024]{1,0:T(8,128)(2,1)} %q_ref.2) | copy-start | bytes 3145732
  10.2 19.8 %copy-start.10 = (s32[1024,1]{1,0:T(8,128)}, s32[1024,1]{1,0:T(8,128)S(1)}, u32[]{:S(2)}) copy-start(s32[1024,1]{1,0:T(8,128)S(1)} %copy.13.segk_ref) | copy-start | bytes 12292
  13.4 16.6 %copy-start.8 = (bf16[1024,128]{1,0:T(8,128)(2,1)}, bf16[1024,128]{1,0:T(8,128)(2,1)S(1)}, u32[]{:S(2)}) copy-start(bf16[1024,128]{1,0:T(8,128)(2,1)S(1)} %get-tuple-element.81.k_ref) | copy-start | bytes 786436
  13.6 0.8 copy-start.21
  15.7 14.4 %copy-start.26 = (bf16[512,1024]{1,0:T(8,128)(2,1)S(1)}, bf16[512,1024]{1,0:T(8,128)(2,1)}, u32[]{:S(2)}) copy-start(bf16[512,1024]{1,0:T(8,128)(2,1)} %refs_8_.1) | copy-start | bytes 3145732
  30.0 8.7 %collective-permute-start.7 = (bf16[512,1024]{1,0:T(8,128)(2,1)S(1)}, bf16[512,1024]{1,0:T(8,128)(2,1)S(1)}, u32[]{:S(2)}, u32[]{:S(2)}) collective-permute-start(bf16[512,1024]{1,0:T(8,128)(2,1)S(1)} %get-tuple-element.34), channel_id=1, source_target_pairs={{0,8},{8,0},{16,24},{24,16},{32,40},{40,32},{48,56},{56,48},{64,72... | collective-permute-start | bytes 3145736 | tf_op jit(solution)/shard_map/ppermute | solution.py:28
  30.1 29.4 %collective-permute-start.4 = (bf16[512,1024]{1,0:T(8,128)(2,1)S(1)}, bf16[512,1024]{1,0:T(8,128)(2,1)S(1)}, u32[]{:S(2)}, u32[]{:S(2)}) collective-permute-start(bf16[512,1024]{1,0:T(8,128)(2,1)S(1)} %copy-done.26), channel_id=1, source_target_pairs={{0,32},{8,40},{16,48},{24,56},{32,64},{40,72},{48,80},{56,88},{64,... | collective-permute-start | bytes 3145736 | tf_op jit(solution)/shard_map/ppermute | solution.py:28
  33.9 27.6 %collective-permute-start.5 = (bf16[512,1024]{1,0:T(8,128)(2,1)S(1)}, bf16[512,1024]{1,0:T(8,128)(2,1)S(1)}, u32[]{:S(2)}, u32[]{:S(2)}) collective-permute-start(bf16[512,1024]{1,0:T(8,128)(2,1)S(1)} %copy-done.26), channel_id=1, source_target_pairs={{0,96},{8,104},{16,112},{24,120},{32,0},{40,8},{48,16},{56,24},{64... | collective-permute-start | bytes 3145736 | tf_op jit(solution)/shard_map/ppermute | solution.py:28
  36.0 25.5 %collective-permute-start.1 = (bf16[1024,512]{1,0:T(8,128)(2,1)S(1)}, bf16[1024,512]{1,0:T(8,128)(2,1)S(1)}, u32[]{:S(2)}, u32[]{:S(2)}) collective-permute-start(bf16[1024,512]{1,0:T(8,128)(2,1)S(1)} %pad_maximum_fusion.1.refs_0_), channel_id=1, source_target_pairs={{0,1},{1,2},{2,3},{3,0},{4,5},{5,6},{6,7},{7,4},{8,9},{9,10},{10,1... | collective-permute-start | bytes 3145736 | tf_op jit(solution)/shard_map/ppermute | solution.py:36
  37.2 24.3 %collective-permute-start.2 = (bf16[1024,512]{1,0:T(8,128)(2,1)S(1)}, bf16[1024,512]{1,0:T(8,128)(2,1)S(1)}, u32[]{:S(2)}, u32[]{:S(2)}) collective-permute-start(bf16[1024,512]{1,0:T(8,128)(2,1)S(1)} %pad_maximum_fusion.1.refs_0_), channel_id=1, source_target_pairs={{0,3},{1,0},{2,1},{3,2},{4,7},{5,4},{6,5},{7,6},{8,11},{9,8},{10,9... | collective-permute-start | bytes 3145736 | tf_op jit(solution)/shard_map/ppermute | solution.py:36
  38.7 23.6 %collective-permute-start.3 = (bf16[1024,512]{1,0:T(8,128)(2,1)S(1)}, bf16[1024,512]{1,0:T(8,128)(2,1)S(1)}, u32[]{:S(2)}, u32[]{:S(2)}) collective-permute-start(bf16[1024,512]{1,0:T(8,128)(2,1)S(1)} %pad_maximum_fusion.1.refs_0_), channel_id=1, source_target_pairs={{0,4},{1,5},{2,6},{3,7},{4,0},{5,1},{6,2},{7,3},{8,12},{9,13},{10,... | collective-permute-start | bytes 3145736 | tf_op jit(solution)/shard_map/ppermute | solution.py:36
  59.5 8.5 %copy-start.22 = (bf16[512,1024]{1,0:T(8,128)(2,1)}, bf16[512,1024]{1,0:T(8,128)(2,1)S(1)}, u32[]{:S(2)}) copy-start(bf16[512,1024]{1,0:T(8,128)(2,1)S(1)} %collective-permute-done.4.refs_9_) | copy-start | bytes 3145732
  59.5 27.0 %collective-permute-start.12 = (bf16[512,1024]{1,0:T(8,128)(2,1)S(1)}, bf16[512,1024]{1,0:T(8,128)(2,1)}, u32[]{:S(2)}, u32[]{:S(2)}) collective-permute-start(bf16[512,1024]{1,0:T(8,128)(2,1)S(1)} %copy-done.26), channel_id=1, source_target_pairs={{0,16},{8,24},{16,0},{24,8},{32,48},{40,56},{48,32},{56,40},{64,80... | collective-permute-start | bytes 3145736 | tf_op jit(solution)/shard_map/ppermute | solution.py:28
  61.5 6.5 %copy-start.23 = (bf16[512,1024]{1,0:T(8,128)(2,1)}, bf16[512,1024]{1,0:T(8,128)(2,1)S(1)}, u32[]{:S(2)}) copy-start(bf16[512,1024]{1,0:T(8,128)(2,1)S(1)} %collective-permute-done.5.refs_10_) | copy-start | bytes 3145732
  61.5 6.5 %copy-start = (bf16[1024,512]{1,0:T(8,128)(2,1)}, bf16[1024,512]{1,0:T(8,128)(2,1)S(1)}, u32[]{:S(2)}) copy-start(bf16[1024,512]{1,0:T(8,128)(2,1)S(1)} %collective-permute-done.2.refs_2_) | copy-start | bytes 3145732
  62.3 5.6 %copy-start.6 = (bf16[1024,512]{1,0:T(8,128)(2,1)}, bf16[1024,512]{1,0:T(8,128)(2,1)S(1)}, u32[]{:S(2)}) copy-start(bf16[1024,512]{1,0:T(8,128)(2,1)S(1)} %collective-permute-done.3.refs_3_) | copy-start | bytes 3145732
  62.3 25.7 %collective-permute-start.8 = (bf16[1024,512]{1,0:T(8,128)(2,1)S(1)}, bf16[1024,512]{1,0:T(8,128)(2,1)S(1)}, u32[]{:S(2)}, u32[]{:S(2)}) collective-permute-start(bf16[1024,512]{1,0:T(8,128)(2,1)S(1)} %collective-permute-done.3.refs_3_), channel_id=1, source_target_pairs={{0,1},{1,2},{2,3},{3,0},{4,5},{5,6},{6,7},{7,4},{8,9},{9,10},{10,1... | collective-permute-start | bytes 3145736 | tf_op jit(solution)/shard_map/ppermute | solution.py:36
  62.8 25.3 %collective-permute-start.9 = (bf16[1024,512]{1,0:T(8,128)(2,1)S(1)}, bf16[1024,512]{1,0:T(8,128)(2,1)S(1)}, u32[]{:S(2)}, u32[]{:S(2)}) collective-permute-start(bf16[1024,512]{1,0:T(8,128)(2,1)S(1)} %collective-permute-done.3.refs_3_), channel_id=1, source_target_pairs={{0,3},{1,0},{2,1},{3,2},{4,7},{5,4},{6,5},{7,6},{8,11},{9,8},{10,9... | collective-permute-start | bytes 3145736 | tf_op jit(solution)/shard_map/ppermute | solution.py:36
  65.1 21.4 %collective-permute-start.10 = (bf16[256,1024]{1,0:T(8,128)(2,1)S(1)}, bf16[256,1024]{1,0:T(8,128)(2,1)S(1)}, u32[]{:S(2)}, u32[]{:S(2)}) collective-permute-start(bf16[256,1024]{1,0:T(8,128)(2,1)S(1)} %slice.142), channel_id=1, source_target_pairs={{0,32},{8,40},{16,48},{24,56},{32,64},{40,72},{48,80},{56,88},{64,... | collective-permute-start | bytes 1572872 | tf_op jit(solution)/shard_map/ppermute | solution.py:28
  65.2 22.1 %collective-permute-start.11 = (bf16[256,1024]{1,0:T(8,128)(2,1)S(1)}, bf16[256,1024]{1,0:T(8,128)(2,1)S(1)}, u32[]{:S(2)}, u32[]{:S(2)}) collective-permute-start(bf16[256,1024]{1,0:T(8,128)(2,1)S(1)} %slice.143), channel_id=1, source_target_pairs={{0,96},{8,104},{16,112},{24,120},{32,0},{40,8},{48,16},{56,24},{64... | collective-permute-start | bytes 1572872 | tf_op jit(solution)/shard_map/ppermute | solution.py:28
  86.5 4.8 %slice-start = ((bf16[1024,512]{1,0:T(8,128)(2,1)}), bf16[512,512]{1,0:T(8,128)(2,1)S(1)}, s32[]{:S(2)}) async-start(bf16[1024,512]{1,0:T(8,128)(2,1)} %copy-done), calls=%async_computation | async-start | bytes 1048576 | tf_op jit(solution)/shard_map/slice | solution.py:385
  86.5 0.8 copy-start.14
  87.3 0.8 copy-start.16
  88.1 3.2 %copy-start.4 = (bf16[1024,512]{1,0:T(8,128)(2,1)}, bf16[1024,512]{1,0:T(8,128)(2,1)S(1)}, u32[]{:S(2)}) copy-start(bf16[1024,512]{1,0:T(8,128)(2,1)S(1)} %collective-permute-done.9.refs_5_) | copy-start | bytes 3145732
  88.1 1.1 copy-start.2
  90.3 24.2 %collective-permute-start.13 = (bf16[1024,512]{1,0:T(8,128)(2,1)}, bf16[1024,512]{1,0:T(8,128)(2,1)}, u32[]{:S(2)}, u32[]{:S(2)}) collective-permute-start(bf16[1024,512]{1,0:T(8,128)(2,1)} %pad_maximum_fusion.2), channel_id=1, source_target_pairs={{0,1},{1,2},{2,3},{3,0},{4,5},{5,6},{6,7},{7,4},{8,9},{9,10},{10,1... | collective-permute-start | bytes 3145736 | tf_op jit(solution)/shard_map/ppermute | solution.py:36
  92.4 30.4 %copy-start.1 = (bf16[1024,512]{1,0:T(8,128)(2,1)S(1)}, bf16[1024,512]{1,0:T(8,128)(2,1)}, u32[]{:S(2)}) copy-start(bf16[1024,512]{1,0:T(8,128)(2,1)} %copy-done) | copy-start | bytes 3145732
  92.4 23.7 %collective-permute-start.14 = (bf16[1024,512]{1,0:T(8,128)(2,1)}, bf16[1024,512]{1,0:T(8,128)(2,1)}, u32[]{:S(2)}, u32[]{:S(2)}) collective-permute-start(bf16[1024,512]{1,0:T(8,128)(2,1)} %pad_maximum_fusion.3), channel_id=1, source_target_pairs={{0,3},{1,0},{2,1},{3,2},{4,7},{5,4},{6,5},{7,6},{8,11},{9,8},{10,9... | collective-permute-start | bytes 3145736 | tf_op jit(solution)/shard_map/ppermute | solution.py:36
  94.1 23.7 %collective-permute-start.15 = (bf16[512,1024]{1,0:T(8,128)(2,1)}, bf16[512,1024]{1,0:T(8,128)(2,1)}, u32[]{:S(2)}, u32[]{:S(2)}) collective-permute-start(bf16[512,1024]{1,0:T(8,128)(2,1)} %collective-permute-done.12.refs_11_), channel_id=1, source_target_pairs={{0,32},{8,40},{16,48},{24,56},{32,64},{40,72},{48,80},{56,88},{64,... | collective-permute-start | bytes 3145736 | tf_op jit(solution)/shard_map/ppermute | solution.py:28
  94.1 23.7 %collective-permute-start.16 = (bf16[512,1024]{1,0:T(8,128)(2,1)}, bf16[512,1024]{1,0:T(8,128)(2,1)}, u32[]{:S(2)}, u32[]{:S(2)}) collective-permute-start(bf16[512,1024]{1,0:T(8,128)(2,1)} %collective-permute-done.12.refs_11_), channel_id=1, source_target_pairs={{0,96},{8,104},{16,112},{24,120},{32,0},{40,8},{48,16},{56,24},{64... | collective-permute-start | bytes 3145736 | tf_op jit(solution)/shard_map/ppermute | solution.py:28
  97.1 25.7 %copy-start.3 = (bf16[1024,512]{1,0:T(8,128)(2,1)S(1)}, bf16[1024,512]{1,0:T(8,128)(2,1)}, u32[]{:S(2)}) copy-start(bf16[1024,512]{1,0:T(8,128)(2,1)} %copy-done.2) | copy-start | bytes 3145732
  118.9 32.0 %collective-permute-start.17 = (bf16[256,1024]{1,0:T(8,128)(2,1)S(1)}, bf16[256,1024]{1,0:T(8,128)(2,1)S(1)}, u32[]{:S(2)}, u32[]{:S(2)}) collective-permute-start(bf16[256,1024]{1,0:T(8,128)(2,1)S(1)} %slice.148), channel_id=1, source_target_pairs={{0,32},{8,40},{16,48},{24,56},{32,64},{40,72},{48,80},{56,88},{64,... | collective-permute-start | bytes 1572872 | tf_op jit(solution)/shard_map/ppermute | solution.py:28
  120.1 30.9 %collective-permute-start.18 = (bf16[256,1024]{1,0:T(8,128)(2,1)S(1)}, bf16[256,1024]{1,0:T(8,128)(2,1)S(1)}, u32[]{:S(2)}, u32[]{:S(2)}) collective-permute-start(bf16[256,1024]{1,0:T(8,128)(2,1)S(1)} %slice.149), channel_id=1, source_target_pairs={{0,96},{8,104},{16,112},{24,120},{32,0},{40,8},{48,16},{56,24},{64... | collective-permute-start | bytes 1572872 | tf_op jit(solution)/shard_map/ppermute | solution.py:28
  122.8 1.2 copy-start.5
  124.0 1.2 copy-start.7
  134.8 38.5 %collective-permute-start.21 = (bf16[512,1024]{1,0:T(8,128)(2,1)S(1)}, bf16[512,1024]{1,0:T(8,128)(2,1)S(1)}, u32[]{:S(2)}, u32[]{:S(2)}) collective-permute-start(bf16[512,1024]{1,0:T(8,128)(2,1)S(1)} %pad_maximum_fusion.4), channel_id=1, source_target_pairs={{0,32},{8,40},{16,48},{24,56},{32,64},{40,72},{48,80},{56,88},{64,... | collective-permute-start | bytes 3145736 | tf_op jit(solution)/shard_map/ppermute | solution.py:28
  135.0 16.0 %copy-start.15 = (bf16[256,1024]{1,0:T(8,128)(2,1)S(1)}, bf16[256,1024]{1,0:T(8,128)(2,1)}, u32[]{:S(2)}) copy-start(bf16[256,1024]{1,0:T(8,128)(2,1)} %copy-done.14) | copy-start | bytes 1572868
  135.0 16.0 %copy-start.17 = (bf16[256,1024]{1,0:T(8,128)(2,1)S(1)}, bf16[256,1024]{1,0:T(8,128)(2,1)}, u32[]{:S(2)}) copy-start(bf16[256,1024]{1,0:T(8,128)(2,1)} %copy-done.16) | copy-start | bytes 1572868
  135.0 38.3 %collective-permute-start.22 = (bf16[512,1024]{1,0:T(8,128)(2,1)S(1)}, bf16[512,1024]{1,0:T(8,128)(2,1)S(1)}, u32[]{:S(2)}, u32[]{:S(2)}) collective-permute-start(bf16[512,1024]{1,0:T(8,128)(2,1)S(1)} %pad_maximum_fusion.5), channel_id=1, source_target_pairs={{0,96},{8,104},{16,112},{24,120},{32,0},{40,8},{48,16},{56,24},{64... | collective-permute-start | bytes 3145736 | tf_op jit(solution)/shard_map/ppermute | solution.py:28
  150.9 22.4 %copy-start.18 = (bf16[6,512,1024]{2,1,0:T(8,128)(2,1)S(1)}, bf16[6,512,1024]{2,1,0:T(8,128)(2,1)}, u32[]{:S(2)}) copy-start(bf16[6,512,1024]{2,1,0:T(8,128)(2,1)} %project.3) | copy-start | bytes 18874372
  168.7 14.7 %collective-permute-start.19 = (bf16[512,1024]{1,0:T(8,128)(2,1)S(1)}, bf16[512,1024]{1,0:T(8,128)(2,1)}, u32[]{:S(2)}, u32[]{:S(2)}) collective-permute-start(bf16[512,1024]{1,0:T(8,128)(2,1)S(1)} %get-tuple-element.50), channel_id=1, source_target_pairs={{0,8},{8,0},{16,24},{24,16},{32,40},{40,32},{48,56},{56,48},{64,72... | collective-permute-start | bytes 3145736 | tf_op jit(solution)/shard_map/ppermute | solution.py:28
  175.5 4.8 %copy-start.9 = (bf16[1024,128]{1,0:T(8,128)(2,1)S(1)}, bf16[1024,128]{1,0:T(8,128)(2,1)}, u32[]{:S(2)}) copy-start(bf16[1024,128]{1,0:T(8,128)(2,1)} %copy-done.8) | copy-start | bytes 786436
  176.6 26.3 %collective-permute-start.25 = (bf16[512,1024]{1,0:T(8,128)(2,1)}, bf16[512,1024]{1,0:T(8,128)(2,1)}, u32[]{:S(2)}, u32[]{:S(2)}) collective-permute-start(bf16[512,1024]{1,0:T(8,128)(2,1)} %pad_maximum_fusion.8), channel_id=1, source_target_pairs={{0,32},{8,40},{16,48},{24,56},{32,64},{40,72},{48,80},{56,88},{64,... | collective-permute-start | bytes 3145736 | tf_op jit(solution)/shard_map/ppermute | solution.py:28
  177.6 4.2 %copy-start.20 = (bf16[256,1024]{1,0:T(8,128)(2,1)S(1)}, bf16[256,1024]{1,0:T(8,128)(2,1)}, u32[]{:S(2)}) copy-start(bf16[256,1024]{1,0:T(8,128)(2,1)} %get-tuple-element.68) | copy-start | bytes 1572868
  177.6 25.2 %collective-permute-start.26 = (bf16[512,1024]{1,0:T(8,128)(2,1)}, bf16[512,1024]{1,0:T(8,128)(2,1)}, u32[]{:S(2)}, u32[]{:S(2)}) collective-permute-start(bf16[512,1024]{1,0:T(8,128)(2,1)} %pad_maximum_fusion.9), channel_id=1, source_target_pairs={{0,96},{8,104},{16,112},{24,120},{32,0},{40,8},{48,16},{56,24},{64... | collective-permute-start | bytes 3145736 | tf_op jit(solution)/shard_map/ppermute | solution.py:28
  180.4 3.0 %copy-start.19 = (f32[512,1024]{1,0:T(8,128)S(1)}, f32[512,1024]{1,0:T(8,128)}, u32[]{:S(2)}) copy-start(f32[512,1024]{1,0:T(8,128)} %get-tuple-element.49) | copy-start | bytes 6291460
  181.7 53.7 %collective-permute-start.24 = (bf16[512,1024]{1,0:T(8,128)(2,1)S(1)}, bf16[512,1024]{1,0:T(8,128)(2,1)S(1)}, u32[]{:S(2)}, u32[]{:S(2)}) collective-permute-start(bf16[512,1024]{1,0:T(8,128)(2,1)S(1)} %pad_maximum_fusion.7), channel_id=1, source_target_pairs={{0,96},{8,104},{16,112},{24,120},{32,0},{40,8},{48,16},{56,24},{64... | collective-permute-start | bytes 3145736 | tf_op jit(solution)/shard_map/ppermute | solution.py:28
  181.9 53.5 %collective-permute-start.23 = (bf16[512,1024]{1,0:T(8,128)(2,1)S(1)}, bf16[512,1024]{1,0:T(8,128)(2,1)S(1)}, u32[]{:S(2)}, u32[]{:S(2)}) collective-permute-start(bf16[512,1024]{1,0:T(8,128)(2,1)S(1)} %pad_maximum_fusion.6), channel_id=1, source_target_pairs={{0,32},{8,40},{16,48},{24,56},{32,64},{40,72},{48,80},{56,88},{64,... | collective-permute-start | bytes 3145736 | tf_op jit(solution)/shard_map/ppermute | solution.py:28
  185.0 22.2 %copy-start.11 = (s32[1024,1]{1,0:T(8,128)S(1)}, s32[1024,1]{1,0:T(8,128)}, u32[]{:S(2)}) copy-start(s32[1024,1]{1,0:T(8,128)} %copy-done.10) | copy-start | bytes 12292
  185.0 22.2 %copy-start.13 = (bf16[512,1024]{1,0:T(8,128)(2,1)S(1)}, bf16[512,1024]{1,0:T(8,128)(2,1)}, u32[]{:S(2)}) copy-start(bf16[512,1024]{1,0:T(8,128)(2,1)} %q_ref.2) | copy-start | bytes 3145732
  205.3 30.1 %collective-permute-start.27 = (bf16[512,1024]{1,0:T(8,128)(2,1)S(1)}, bf16[512,1024]{1,0:T(8,128)(2,1)S(1)}, u32[]{:S(2)}, u32[]{:S(2)}) collective-permute-start(bf16[512,1024]{1,0:T(8,128)(2,1)S(1)} %fusion.1), channel_id=1, source_target_pairs={{0,16},{8,24},{16,0},{24,8},{32,48},{40,56},{48,32},{56,40},{64,80... | collective-permute-start | bytes 3145736 | tf_op jit(solution)/shard_map/ppermute | solution.py:28
  224.2 10.4 %collective-permute-start.20 = (bf16[512,256]{1,0:T(8,128)(2,1)S(1)}, bf16[512,256]{1,0:T(8,128)(2,1)S(1)}, u32[]{:S(2)}, u32[]{:S(2)}) collective-permute-start(bf16[512,256]{1,0:T(8,128)(2,1)S(1)} %pad_maximum_fusion.11), channel_id=1, source_target_pairs={{8,0},{16,8},{24,16},{32,24},{40,32},{48,40},{56,48},{64,56},{72,6... | collective-permute-start | bytes 786440 | tf_op jit(solution)/shard_map/ppermute | solution.py:42

commit v2 on v1

--- a/solution.py
+++ b/solution.py
@@ -199,64 +199,68 @@
     )(first, query, grad, key_pair, kt, value_pair, segq, segk, top, total)
 
 
-def load_pieces(meta_ref, refs, plan, buffer, sems):
-    copies = []
-    for n, (ref_at, source, block, start, rows) in enumerate(plan):
-        copies.append(
-            pltpu.make_async_copy(
-                refs[ref_at].at[pl.ds(source, rows)],
-                buffer.at[meta_ref[block], pl.ds(start, rows)],
-                sems.at[n],
-            )
-        )
-    for copy in copies:
-        copy.start()
-    return copies
-
-
-def proj_kernel(plan, n_in, meta_ref, *refs):
+def proj_kernel(split, n_blocks, n_in, held, meta_ref, *refs):
     pieces, a_ref = refs[:n_in], refs[n_in]
-    out_ref = refs[n_in + 1]
-    buffer, sems = refs[n_in + 2:]
+    out_ref = refs[n_in + 1 + held]
     step = pl.program_id(0)
-
-    @pl.when(step == 0)
-    def _():
-        for copy in load_pieces(meta_ref, pieces, plan, buffer, sems):
-            copy.wait()
-
-    block = buffer[meta_ref[8 + step]]
-    out_ref[0] = lax.dot_general(
-        block, a_ref[...], (((0,), (0,)), ((), ())), preferred_element_type=F32
-    ).astype(BF)
-
-
-def project(pieces, plan, meta, a_pair, first, count):
+    h = a_ref.shape[0] // 2
+    over_tokens = (((0,), (0,)), ((), ()))
+
+    def store(value):
+        value = value.astype(BF)
+        rows = value.shape[0] // 2
+        out_ref[0, 0] = value[:rows]
+        out_ref[1, 0] = value[rows:]
+
+    for j in range(n_blocks):
+
+        @pl.when(step == j)
+        def _():
+            if split:
+                part = slice(j * h, (j + 1) * h)
+                store(
+                    lax.dot_general(
+                        pieces[0][part, :], a_ref[:h, :], over_tokens, preferred_element_type=F32
+                    )
+                    + lax.dot_general(
+                        pieces[1][part, :], a_ref[h:, :], over_tokens, preferred_element_type=F32
+                    )
+                )
+            else:
+                store(
+                    lax.dot_general(
+                        pieces[j][...], a_ref[...], over_tokens, preferred_element_type=F32
+                    )
+                )
+
+
+def project(pieces, split, a_pair, blocks, buffer):
     tokens, width = a_pair.shape
     depth = pieces[0].shape[1]
-    kernel = functools.partial(proj_kernel, plan, len(pieces))
+    n_blocks = 2 if split else len(pieces)
+    held = int(buffer is not None)
+    whole = lambda shape: pl.BlockSpec(shape, lambda j, m: (0,) * len(shape))
+    operands = (*pieces, a_pair) + ((buffer,) if held else ())
     return pl.pallas_call(
-        kernel,
+        functools.partial(proj_kernel, split, n_blocks, len(pieces), held),
         grid_spec=pltpu.PrefetchScalarGridSpec(
             num_scalar_prefetch=1,
-            grid=(count,),
-            in_specs=[pl.BlockSpec(memory_space=pl.ANY)] * len(pieces)
-            + [pl.BlockSpec((tokens, width), lambda j, m: (0, 0))],
-            out_specs=pl.BlockSpec((1, depth, width), lambda j, m: (j, 0, 0)),
-            scratch_shapes=[
-                pltpu.VMEM((8, tokens, depth), BF),
-                pltpu.SemaphoreType.DMA((len(plan),)),
-            ],
-        ),
-        out_shape=jax.ShapeDtypeStruct((count, depth, width), BF),
-        compiler_params=params(44),
+            grid=(n_blocks,),
+            in_specs=[whole((tokens, depth))] * len(pieces)
+            + [whole((tokens, width))]
+            + [pl.BlockSpec(memory_space=pl.ANY)] * held,
+            out_specs=pl.BlockSpec((2, 1, depth // 2, width), lambda j, m: (0, m[j], 0, 0)),
+        ),
+        out_shape=jax.ShapeDtypeStruct((2, 8, depth // 2, width), BF),
+        input_output_aliases={len(pieces) + 2: 0} if held else {},
+        compiler_params=params(40),
         cost_estimate=pl.CostEstimate(
-            flops=2 * count * tokens * depth * width,
-            bytes_accessed=(8 + 2 + count) * 2**20,
+            flops=2 * n_blocks * tokens * depth * width,
+            bytes_accessed=(2 * n_blocks + 2) * 2**20,
             transcendentals=0,
         ),
         name="project",
-    )(jnp.concatenate([meta[:8], meta[8 + first:]]), *pieces, a_pair)
+    )(blocks, *operands)
 
 
 def grad_kernel(gplan, wplan, n_g, n_w, meta_ref, *refs):
@@ -265,18 +269,50 @@
     gbuf, wbuf, total, gsems, wsems = refs[n_g + n_w + 2:]
     step = pl.program_id(0)
     half = own_ref.shape[0]
+    gh, wh = gbuf.shape[1] // 2, wbuf.shape[1] // 2
+
+    def g_copy(n):
+        ref, source, block, part = gplan[n]
+        return pltpu.make_async_copy(
+            g_in[ref].at[pl.ds(source, gh)], gbuf.at[block, pl.ds(part * gh, gh)], gsems.at[n]
+        )
+
+    def w_copy(n):
+        ref, source, block, part = wplan[n]
+        place = meta_ref[8 + block]
+        return pltpu.make_async_copy(
+            w_in[ref].at[pl.ds(source, wh)],
+            wbuf.at[place, pl.ds(part * wh, wh)],
+            wsems.at[part, place],
+        )
 
     @pl.when(step == 0)
     def _():
-        copies = load_pieces(meta_ref, g_in, gplan, gbuf, gsems)
-        copies += load_pieces(meta_ref, w_in, wplan, wbuf, wsems)
-        for copy in copies:
-            copy.wait()
-        total[...] = jnp.dot(gbuf[0], wbuf[0], preferred_element_type=F32)
+        for n in range(16):
+            w_copy(n).start()
+            g_copy(n).start()
+
+    for j in range(8):
+
+        @pl.when(step == j)
+        def _():
+            for n in range(16):
+                if gplan[n][2] == j:
+                    g_copy(n).wait()
+
+    place = meta_ref[step]
+    for part in range(2):
+        pltpu.make_async_copy(
+            w_in[0].at[pl.ds(0, wh)], wbuf.at[place, pl.ds(part * wh, wh)], wsems.at[part, place]
+        ).wait()
+
+    @pl.when(step == 0)
+    def _():
+        total[...] = jnp.dot(gbuf[step], wbuf[place], preferred_element_type=F32)
 
     @pl.when(step > 0)
     def _():
-        total[...] += jnp.dot(gbuf[step], wbuf[step], preferred_element_type=F32)
+        total[...] += jnp.dot(gbuf[step], wbuf[place], preferred_element_type=F32)
 
     @pl.when(step == 7)
     def _():
@@ -301,8 +337,8 @@
                 pltpu.VMEM((8, tokens, depth), BF),
                 pltpu.VMEM((8, depth, width), BF),
                 pltpu.VMEM((tokens, width), F32),
-                pltpu.SemaphoreType.DMA((len(gplan),)),
-                pltpu.SemaphoreType.DMA((len(wplan),)),
+                pltpu.SemaphoreType.DMA((16,)),
+                pltpu.SemaphoreType.DMA((2, 8)),
             ],
         ),
         out_shape=[
@@ -319,11 +355,49 @@
     )(meta, *g_pieces, *w_pieces)
 
 
-def add_up(*terms):
-    total = terms[0].astype(F32)
-    for term in terms[1:]:
-        total = total + term.astype(F32)
-    return total.astype(BF)
+def add_kernel(n_blocks, plan, meta_ref, *refs):
+    blocks = refs[:n_blocks]
+    n_out = len(plan)
+    terms = refs[n_blocks:len(refs) - n_out]
+    for out_ref, (block, part, extra) in zip(refs[len(refs) - n_out:], plan):
+        if part is None:
+            for p in range(2):
+                value = blocks[block][p, 0]
+                added = [e if isinstance(e, int) else e[0] for e in extra if isinstance(e, int) or e[1] == p]
+                if added:
+                    value = value.astype(F32)
+                    for e in added:
+                        term = terms[e]
+                        value = value + (term[p] if term.shape[0] == 2 else term[0]).astype(F32)
+                out_ref[p] = value.astype(BF)
+        else:
+            value = blocks[block][part, 0].astype(F32)
+            for e in extra:
+                value = value + terms[e][part].astype(F32)
+            out_ref[0] = value.astype(BF)
+
+
+def add_blocks(buffer, blocks, terms, plan):
+    _, _, rows, width = buffer.shape
+    n_blocks = blocks.shape[0]
+    place = lambda n: pl.BlockSpec((2, 1, rows, width), lambda i, m: (0, m[n], 0, 0))
+    whole = lambda shape: pl.BlockSpec(shape, lambda i, m: (0,) * len(shape))
+    shapes = [(2 if part is None else 1, rows, width) for _, part, _ in plan]
+    return pl.pallas_call(
+        functools.partial(add_kernel, n_blocks, plan),
+        grid_spec=pltpu.PrefetchScalarGridSpec(
+            num_scalar_prefetch=1,
+            grid=(1,),
+            in_specs=[place(n) for n in range(n_blocks)] + [whole(t.shape) for t in terms],
+            out_specs=[whole(shape) for shape in shapes],
+        ),
+        out_shape=[jax.ShapeDtypeStruct(shape, BF) for shape in shapes],
+        compiler_params=params(32),
+        cost_estimate=pl.CostEstimate(
+            flops=2**21, bytes_accessed=5 * 2**20, transcendentals=0
+        ),
+        name="add_blocks",
+    )(blocks, *([buffer] * n_blocks), *terms)
 
 
 def local(query_rows, key_rows, value_rows, output_grad, out_proj, segment_ids):
@@ -366,90 +440,105 @@
     first = ints(row == 0)
     (query_held,) = tied((query_rows,), g0)
     attn_out, top, total = attend(query_held, key_pair, value_t, segq, segk, first)
-    a_other = move_row(attn_out, dk=1)
-    a_pair = jnp.concatenate([attn_out, a_other], 0)
-
-    gxm, gxp, gy, wzm, wzp, a_pair = tied((gxm, gxp, gy, wzm, wzp, a_pair))
+
+    gxm, gxp, gy, wzm, wzp, attn_out = tied((gxm, gxp, gy, wzm, wzp, attn_out))
 
     h = g0.shape[0] // 2
     hw = out_proj.shape[0] // 2
+    a_other = move_row(attn_out, dk=1)
     gyxm = move_col(gy, dx=1)
     gyxp = move_col(gy, dx=-1)
     wom = move_row(wzm[:hw], dz=1)
     wop = move_row(wzp[hw:], dz=-1)
     wy = move_row(out_proj, dyh=1)
 
-    gyxm, gyxp, wom, wop, wy = tied((gyxm, gyxp, wom, wop, wy))
+    a_pair = jnp.concatenate([attn_out, a_other], 0)
+    proj = project(
+        [g0, gxm, gxp, gy],
+        False,
+        a_pair,
+        ints(gblock(0, 0), gblock(0, -1), gblock(0, 1), gblock(1, 0)),
+        None,
+    )
+
+    gyxm, gyxp, wom, wop, wy, proj = tied((gyxm, gyxp, wom, wop, wy, proj))
 
     gom = move_col(jnp.concatenate([gxm[:h], gyxm[:h]], 0), dx=1)
     gop = move_col(jnp.concatenate([gxp[h:], gyxp[h:]], 0), dx=-1)
     wyzm = move_row(wy, dz=1)
     wyzp = move_row(wy, dz=-1)
-
-    gom, gop, wyzm, wyzp = tied((gom, gop, wyzm, wyzp))
-
-    wyom = move_row(wyzm[:hw], dz=1)
-    wyop = move_row(wyzp[hw:], dz=-1)
+    wyo = move_row(jnp.concatenate([wom, wop], 0), dyh=1)
+
+    proj = project([gyxm, gyxp], False, a_pair, ints(gblock(1, -1), gblock(1, 1)), proj)
+
+    gom, gop, wyzm, wyzp, wyo, proj = tied((gom, gop, wyzm, wyzp, wyo, proj))
+
+    proj = project([gom, gop], True, a_pair, ints(gblock(0, 2), gblock(1, 2)), proj)
+
+    def block_at(dz, dy):
+        return lax.dynamic_slice_in_dim(proj, wblock(dz, dy), 1, 1)[:, 0]
+
+    rup = move_row(block_at(1, 1), dz=1)
+    rdn = move_row(block_at(-1, 1), dz=-1)
+    ry = move_row(block_at(2, 1), dyh=1)
 
     g_pieces = [g0, gxm, gxp, gy, gyxm, gyxp, gom, gop]
-    gplan = [(i, 0, i, 0, 2 * h) for i in range(6)] + [
-        (6, 0, 6, 0, h),
-        (6, h, 7, 0, h),
-        (7, 0, 6, h, h),
-        (7, h, 7, h, h),
+    gplan = [(i, p * h, i, p) for i in range(6) for p in range(2)] + [
+        (6, 0, 6, 0),
+        (6, h, 7, 0),
+        (7, 0, 6, 1),
+        (7, h, 7, 1),
     ]
-    g_order = ints(
+    w_pieces = [out_proj, wzm, wzp, wy, wyzm, wyzp, wyo, wom, wop]
+    wplan = [(i, p * hw, i, p) for i in range(7) for p in range(2)] + [(7, 0, 7, 0), (8, 0, 7, 1)]
+    meta = ints(
         gblock(0, 0), gblock(0, -1), gblock(0, 1), gblock(1, 0),
         gblock(1, -1), gblock(1, 1), gblock(0, 2), gblock(1, 2),
-        wblock(2, 1), wblock(2, 0), wblock(1, 1), wblock(-1, 1),
-        wblock(1, 0), wblock(-1, 0), wblock(0, 1), wblock(0, 0),
-    )
-    far = project(g_pieces, gplan, g_order, a_pair, 0, 2)
-    fm = move_row(jnp.concatenate([far[0, :hw], far[1, :hw]], 0), dz=1)
-    fp = move_row(jnp.concatenate([far[0, hw:], far[1, hw:]], 0), dz=-1)
-    near = project(g_pieces, gplan, g_order, a_pair, 2, 6)
-
-    w_pieces = [out_proj, wzm, wzp, wy, wyzm, wyzp, wom, wop, wyom, wyop]
-    wplan = [(i, 0, i, 0, 2 * hw) for i in range(6)] + [
-        (6, 0, 6, 0, hw),
-        (7, 0, 6, hw, hw),
-        (8, 0, 7, 0, hw),
-        (9, 0, 7, hw, hw),
-    ]
-    w_order = ints(
         wblock(0, 0), wblock(-1, 0), wblock(1, 0), wblock(0, 1),
-        wblock(-1, 1), wblock(1, 1), wblock(2, 0), wblock(2, 1),
-    )
-    meta = jnp.concatenate([g_order[:8], w_order])
-    wplan = [(i, s, b + 8, t, n) for i, s, b, t, n in wplan]
+        wblock(-1, 1), wblock(1, 1), wblock(2, 1), wblock(2, 0),
+    )
+    (meta,) = tied((meta,), proj)
     grad_own, grad_give = attn_grad_part(g_pieces, gplan, w_pieces, wplan, meta)
+
+    rup, rdn, ry, grad_own, grad_give = tied((rup, rdn, ry, grad_own, grad_give))
+
+    across, far_up, far_dn = add_blocks(
+        proj,
+        ints(wblock(0, 1), wblock(2, 0)),
+        [rup, rdn, ry],
+        [(0, None, (0, 1)), (1, 0, (2,)), (1, 1, (2,))],
+    )
+    fup = move_row(far_up, dz=1)
+    fdn = move_row(far_dn, dz=-1)
+    across = move_row(across, dyh=1)
     grad_got = move_row(grad_give, dk=1)
     attn_grad = (grad_own + grad_got.astype(F32)).astype(BF)
 
-    fm, fp, near = tied((fm, fp, near))
-
-    up = lambda block, extra: jnp.concatenate([add_up(block[:hw], extra), block[hw:]], 0)
-    down = lambda block, extra: jnp.concatenate([block[:hw], add_up(block[hw:], extra)], 0)
-    sup1 = move_row(up(near[0], fm[:hw]), dz=1)
-    sdn1 = move_row(down(near[1], fp[:hw]), dz=-1)
-
+    fup, fdn, attn_grad = tied((fup, fdn, attn_grad))
+
+    near_up, near_dn = add_blocks(
+        proj,
+        ints(wblock(1, 0), wblock(-1, 0)),
+        [fup, fdn],
+        [(0, None, ((0, 0),)), (1, None, ((1, 1),))],
+    )
+    nup = move_row(near_up, dz=1)
+    ndn = move_row(near_dn, dz=-1)
+
+    (attn_grad,) = tied((attn_grad,), near_up)
     query_grad, dkey, dvalue = attend_back(
         query_rows, attn_grad, key_pair, key_t, value_pair, segq, segk, first, top, total
     )
     back = passed_along(
         jnp.concatenate([dkey[:count], dvalue[:count]], 1).astype(BF), "row", -1
     ).astype(F32)
-
-    sup1, sdn1, = tied((sup1, sdn1))
-
-    other = move_row(add_up(near[4], sup1, sdn1), dyh=1)
-    sup0 = move_row(up(near[2], fm[hw:]), dz=1)
-    sdn0 = move_row(down(near[3], fp[hw:]), dz=-1)
-    proj_grad = add_up(near[5], sup0, sdn0, other)
-
     key_grad = (dkey[count:] + back[:, :HD]).astype(BF)
     value_grad = (dvalue[count:] + back[:, HD:]).astype(BF)
-    return (query_grad, key_grad, value_grad, proj_grad)
+
+    (proj_grad,) = add_blocks(
+        proj, ints(wblock(0, 0)), [nup, ndn, across], [(0, None, (0, 1, 2))]
+    )
+    return (query_grad, key_grad, value_grad, proj_grad.reshape(2 * hw, out_proj.shape[1]))
 
 
 def solution(mesh):

time: 239 us -> 198 us (0.83)
  waiting for transfers between devices: 84.3 us -> 40 us
  local copies, waits for them, and re-layouts: 15.1 us -> 33.5 us
  other arithmetic: 18.6 us -> 8.01 us
  starting transfers between devices: 49.7 us -> 45 us
    ppermute x19, waiting for transfers between devices: 55.9 us -> 22.7 us  [move_row(): return lax.ppermute(value, 'row', pairs)]
    unnamed x55 -> x56, local copies, waits for them, and re-layouts: 6.03 us -> 22.4 us
    ppermute x7, waiting for transfers between devices: 19.8 us -> 11.4 us  [move_col(): return lax.ppermute(value, 'col', pairs)]
    convert_element_type x3 -> x0, other arithmetic: 6.59 us -> none  [add_up(): return total.astype(BF)]
    concatenate x7 -> x1, other arithmetic: 5.11 us -> 1.14 us  [local(): wyo = move_row(jnp.concatenate([wom, wop], 0), dyh=1)]
    slice x3 -> x0, local copies, waits for them, and re-layouts: 3.37 us -> none  [the longest x1 1.21 us: local(): block[hw:]]
    ppermute x2, waiting for transfers between devices: 8.49 us -> 5.93 us  [passed_along(): lax.ppermute(value, axis, [(source, source + steps) for source in range(f...]
    pallas_call x2 -> x6, Pallas kernels: 20.8 us -> 21.7 us  [the longest x3 17.7 us: project(): pl.pallas_call(functools.partial(proj_kernel, split, n_blocks, len(pieces...]
  transfers between devices with their start and end apart: 28 -> 28, of which waited for: 9 -> 12; matrix products, arithmetic and copies ran while one was open for 8% -> 8% of each run, Pallas kernels for 23% -> 32%
where the time goes in v2:
time: 198 us; the launch traced here: 197 us
  Pallas kernels  69.2 us (35%)
  starting transfers between devices  45 us (23%)
  waiting for transfers between devices  40 us (20%)
  local copies, waits for them, and re-layouts  33.5 us (17%)
  other arithmetic  8.01 us (4%)
    ppermute x19, starting transfers between devices, move_row(): return lax.ppermute(value, 'row', pairs)  29.4 us
    ppermute x19, waiting for transfers between devices, move_row(): return lax.ppermute(value, 'row', pairs)  22.7 us
    unnamed x56, local copies, waits for them, and re-layouts  22.4 us
    pallas_call x3, Pallas kernels, project(): pl.pallas_call(functools.partial(proj_kernel, split, n_blocks, len(pieces...  17.7 us
    pallas_call x1, Pallas kernels, attend_back(): pl.pallas_call(bwd_kernel, grid_spec=pltpu.PrefetchScalarGridSpec(num_sca...  16.9 us
    pallas_call x1, Pallas kernels, attn_grad_part(): pl.pallas_call(kernel, grid_spec=pltpu.PrefetchScalarGridSpec(num_scalar_...  15.7 us
    pallas_call x1, Pallas kernels, attend(): pl.pallas_call(fwd_kernel, grid_spec=pltpu.PrefetchScalarGridSpec(num_sca...  14.9 us
    ppermute x7, waiting for transfers between devices, move_col(): return lax.ppermute(value, 'col', pairs)  11.4 us
  transfers between devices with their start and end apart: 28, of which 12 were waited for; matrix products, arithmetic and copies ran while one was open for 8% of the time, Pallas kernels for 32%

profile of v2, /device:TPU:1, one launch (start us, length us, event | category | flops | bytes accessed | tf_op | source)
XLA Modules:
  0.0 196.8 jit_solution(10989130379712207937)
XLA Ops:
  0.7 1.3 constant_dynamic-slice_fusion.1
  2.0 1.5 collective-permute-start
  3.6 4.8 %collective-permute-start.6 = (bf16[512,256]{1,0:T(8,128)(2,1)S(1)}, bf16[512,256]{1,0:T(8,128)(2,1)S(1)}, u32[]{:S(2)}, u32[]{:S(2)}) collective-permute-start(bf16[512,256]{1,0:T(8,128)(2,1)S(1)} %constant_dynamic-update-slice_fusion), channel_id=1, source_target_pairs={{0,8},{8,16},{16,24},{24,32},{32,40},{40,48},{48,56},{56,64},{64,7... | collective-permute-start | bytes 786440 | tf_op jit(solution)/shard_map/ppermute | solution.py:42
  8.4 1.7 collective-permute-start.4
  10.1 2.2 %collective-permute-start.5 = (bf16[512,1024]{1,0:T(8,128)(2,1)}, bf16[512,1024]{1,0:T(8,128)(2,1)}, u32[]{:S(2)}, u32[]{:S(2)}) collective-permute-start(bf16[512,1024]{1,0:T(8,128)(2,1)} %refs_8_.1), channel_id=1, source_target_pairs={{0,96},{8,104},{16,112},{24,120},{32,0},{40,8},{48,16},{56,24},{64... | collective-permute-start | bytes 3145736 | tf_op jit(solution)/shard_map/ppermute | solution.py:28
  12.4 1.3 collective-permute-start.1
  13.7 1.5 collective-permute-start.2
  16.3 0.8 fusion.3
  17.4 1.2 pad_maximum_fusion.4
  18.7 1.2 copy-done.19
  20.0 14.9 %attend.1 = (bf16[512,1024]{1,0:T(8,128)(2,1)}, f32[8,1,512]{2,1,0:T(1,128)S(1)}, f32[8,1,512]{2,1,0:T(1,128)S(1)}) custom-call(s32[1]{0:T(128)} %bitcast.meta_ref, bf16[512,1024]{1,0:T(8,128)(2,1)S(1)} %copy-done.19, bf16[1024,128]{1,0:T(8,128)(2,1)S(1)} %get-tuple-element.96.k_ref, bf16[128,1024]{1,0:T(8,128)(2,1)S(1)} %copy.14.vt_ref, ...), custom_call_target="tpu_custom_call" | custom-call | flops 4294967296 | bytes 8388608 | tf_op jit(solution)/shard_map/attend/pallas_call | solution.py:95
  34.8 2.2 %collective-permute-done.1.refs_1_ = bf16[1024,512]{1,0:T(8,128)(2,1)S(1)} collective-permute-done((bf16[1024,512]{1,0:T(8,128)(2,1)S(1)}, bf16[1024,512]{1,0:T(8,128)(2,1)S(1)}, u32[]{:S(2)}, u32[]{:S(2)}) %collective-permute-start.1) | collective-permute-done | bytes 1048608 | tf_op jit(solution)/shard_map/ppermute | solution.py:36
  37.7 2.2 %collective-permute-done.3.refs_3_ = bf16[1024,512]{1,0:T(8,128)(2,1)} collective-permute-done((bf16[1024,512]{1,0:T(8,128)(2,1)S(1)}, bf16[1024,512]{1,0:T(8,128)(2,1)}, u32[]{:S(2)}, u32[]{:S(2)}) %collective-permute-start.3) | collective-permute-done | bytes 1048608 | tf_op jit(solution)/shard_map/ppermute | solution.py:36
  39.9 2.4 %collective-permute-start.11 = (bf16[512,1024]{1,0:T(8,128)(2,1)}, bf16[512,1024]{1,0:T(8,128)(2,1)}, u32[]{:S(2)}, u32[]{:S(2)}) collective-permute-start(bf16[512,1024]{1,0:T(8,128)(2,1)} %refs_8_.1), channel_id=1, source_target_pairs={{0,16},{8,24},{16,0},{24,8},{32,48},{40,56},{48,32},{56,40},{64,80... | collective-permute-start | bytes 3145736 | tf_op jit(solution)/shard_map/ppermute | solution.py:28
  42.2 2.7 %collective-permute-start.8 = (bf16[1024,512]{1,0:T(8,128)(2,1)}, bf16[1024,512]{1,0:T(8,128)(2,1)}, u32[]{:S(2)}, u32[]{:S(2)}) collective-permute-start(bf16[1024,512]{1,0:T(8,128)(2,1)} %collective-permute-done.3.refs_3_), channel_id=1, source_target_pairs={{0,3},{1,0},{2,1},{3,2},{4,7},{5,4},{6,5},{7,6},{8,11},{9,8},{10,9... | collective-permute-start | bytes 3145736 | tf_op jit(solution)/shard_map/ppermute | solution.py:36
  45.0 1.1 slice.48
  46.1 1.1 collective-permute-start.10
  47.1 1.1 slice.47
  48.2 1.1 slice.50
  49.3 1.4 constant_dynamic-update-slice_fusion.3
  51.3 1.3 constant_dynamic-update-slice_fusion.2.refs_4_.refs_2_
  52.6 8.3 %project.3.refs_3_ = bf16[2,8,256,1024]{3,2,1,0:T(8,128)(2,1)} custom-call(s32[4]{0:T(128)S(1)} %pad_add_fusion.3.meta_ref, bf16[1024,512]{1,0:T(8,128)(2,1)S(1)} %copy-done.6, bf16[1024,512]{1,0:T(8,128)(2,1)S(1)} %copy-done.17, bf16[1024,512]{1,0:T(8,128)(2,1)} %collective-permute-done.2.refs_2_, bf16[1024,512]{1,0:T(8,128)(2,1)} %collective-permute-done.3.refs_3_, ...), custom_call_target="tpu_custom_call" | custom-call | flops 4294967296 | bytes 10485760 | tf_op jit(solution)/shard_map/project/pallas_call | solution.py:244
  61.0 4.9 %collective-permute-done.11.refs_11_ = bf16[512,1024]{1,0:T(8,128)(2,1)} collective-permute-done((bf16[512,1024]{1,0:T(8,128)(2,1)}, bf16[512,1024]{1,0:T(8,128)(2,1)}, u32[]{:S(2)}, u32[]{:S(2)}) %collective-permute-start.11) | collective-permute-done | bytes 1048608 | tf_op jit(solution)/shard_map/ppermute | solution.py:28
  65.9 2.2 %collective-permute-done.7.refs_0_.refs_4_ = bf16[1024,512]{1,0:T(8,128)(2,1)S(1)} collective-permute-done((bf16[1024,512]{1,0:T(8,128)(2,1)}, bf16[1024,512]{1,0:T(8,128)(2,1)S(1)}, u32[]{:S(2)}, u32[]{:S(2)}) %collective-permute-start.7) | collective-permute-done | bytes 1048608 | tf_op jit(solution)/shard_map/ppermute | solution.py:36
  68.1 1.1 pad_maximum_fusion.3
  70.0 1.1 slice.51
  71.1 1.1 pad_maximum_fusion.2
  72.3 1.8 collective-permute-start.14
  74.1 1.0 pad_maximum_fusion.1
  75.1 1.6 collective-permute-start.15
  76.7 1.9 collective-permute-start.16
  78.8 3.4 %copy-done = bf16[2,8,256,1024]{3,2,1,0:T(8,128)(2,1)S(1)} copy-done((bf16[2,8,256,1024]{3,2,1,0:T(8,128)(2,1)S(1)}, bf16[2,8,256,1024]{3,2,1,0:T(8,128)(2,1)}, u32[]{:S(2)}) %copy-start) | copy-done | bytes 8388632
  82.1 4.5 %project.4.refs_3_ = bf16[2,8,256,1024]{3,2,1,0:T(8,128)(2,1)S(1)} custom-call(s32[2]{0:T(128)S(1)} %pad_add_fusion.4.meta_ref, bf16[1024,512]{1,0:T(8,128)(2,1)S(1)} %collective-permute-done.7.refs_0_.refs_4_, bf16[1024,512]{1,0:T(8,128)(2,1)} %collective-permute-done.8.refs_1_.refs_5_, ...), custom_call_target="tpu_custom_call", output_to_operand_aliasing={{}: (4, {})} | custom-call | flops 2147483648 | bytes 6291456 | tf_op jit(solution)/shard_map/project/pallas_call | solution.py:244
  86.7 8.0 %collective-permute-done.17.refs_14_ = bf16[512,1024]{1,0:T(8,128)(2,1)} collective-permute-done((bf16[512,1024]{1,0:T(8,128)(2,1)}, bf16[512,1024]{1,0:T(8,128)(2,1)}, u32[]{:S(2)}, u32[]{:S(2)}) %collective-permute-start.17) | collective-permute-done | bytes 1048608 | tf_op jit(solution)/shard_map/ppermute | solution.py:28
  94.7 1.3 collective-permute-done.14.refs_1_.refs_7_
  95.9 2.9 %collective-permute-done.13.refs_0_.refs_6_ = bf16[1024,512]{1,0:T(8,128)(2,1)} collective-permute-done((bf16[1024,512]{1,0:T(8,128)(2,1)}, bf16[1024,512]{1,0:T(8,128)(2,1)}, u32[]{:S(2)}, u32[]{:S(2)}) %collective-permute-start.13) | collective-permute-done | bytes 1048608 | tf_op jit(solution)/shard_map/ppermute | solution.py:36
  98.8 1.6 collective-permute-done.15.refs_12_
  100.4 4.8 %project.5.refs_0_.refs_1_ = bf16[2,8,256,1024]{3,2,1,0:T(8,128)(2,1)S(1)} custom-call(s32[2]{0:T(128)S(1)} %get-tuple-element.100.meta_ref, bf16[1024,512]{1,0:T(8,128)(2,1)} %collective-permute-done.13.refs_0_.refs_6_, bf16[1024,512]{1,0:T(8,128)(2,1)} %collective-permute-done.14.refs_1_.refs_7_, ...), custom_call_target="tpu_custom_call", output_to_operand_aliasing={{}: (4, {})} | custom-call | flops 2147483648 | bytes 6291456 | tf_op jit(solution)/shard_map/project/pallas_call | solution.py:244
  105.2 1.7 dynamic-slice_bitcast_fusion
  107.0 3.3 %copy-done.1 = bf16[2,8,256,1024]{3,2,1,0:T(8,128)(2,1)} copy-done((bf16[2,8,256,1024]{3,2,1,0:T(8,128)(2,1)}, bf16[2,8,256,1024]{3,2,1,0:T(8,128)(2,1)S(1)}, u32[]{:S(2)}) %copy-start.1) | copy-done | bytes 8388632
  110.7 2.2 %collective-permute-start.19 = (bf16[2,256,1024]{2,1,0:T(8,128)(2,1)}, bf16[2,256,1024]{2,1,0:T(8,128)(2,1)S(1)}, u32[]{:S(2)}, u32[]{:S(2)}) collective-permute-start(bf16[2,256,1024]{2,1,0:T(8,128)(2,1)} %get-tuple-element.89), channel_id=1, source_target_pairs={{0,96},{8,104},{16,112},{24,120},{32,0},{40,8},{48,16},{56,24},{64... | collective-permute-start | bytes 3145736 | tf_op jit(solution)/shard_map/ppermute | solution.py:28
  112.9 1.7 collective-permute-start.20
  114.7 1.2 copy-done.7
  115.9 1.0 copy-done.13
  117.0 1.0 copy-done.15
  118.0 1.2 copy-done.18
  119.2 15.7 %attn_grad.1 = (f32[512,1024]{1,0:T(8,128)}, bf16[512,1024]{1,0:T(8,128)(2,1)}) custom-call(s32[16]{0:T(128)S(1)} %stack.106.meta_ref, bf16[1024,512]{1,0:T(8,128)(2,1)S(1)} %copy-done.7, bf16[1024,512]{1,0:T(8,128)(2,1)S(1)} %copy-done.18, bf16[1024,512]{1,0:T(8,128)(2,1)} %collective-permute-done.2.refs_2_, ...), custom_call_target="tpu_custom_call" | custom-call | flops 8589934592 | bytes 20971520 | tf_op jit(solution)/shard_map/attn_grad/pallas_call | solution.py:329
  134.9 1.1 collective-permute-done.20.refs_4_
  136.1 4.1 %collective-permute-start.23 = (bf16[512,1024]{1,0:T(8,128)(2,1)}, bf16[512,1024]{1,0:T(8,128)(2,1)}, u32[]{:S(2)}, u32[]{:S(2)}) collective-permute-start(bf16[512,1024]{1,0:T(8,128)(2,1)} %get-tuple-element.75), channel_id=1, source_target_pairs={{0,8},{8,0},{16,24},{24,16},{32,40},{40,32},{48,56},{56,48},{64,72... | collective-permute-start | bytes 3145736 | tf_op jit(solution)/shard_map/ppermute | solution.py:28
  140.2 3.4 %copy-done.2 = bf16[2,8,256,1024]{3,2,1,0:T(8,128)(2,1)S(1)} copy-done((bf16[2,8,256,1024]{3,2,1,0:T(8,128)(2,1)S(1)}, bf16[2,8,256,1024]{3,2,1,0:T(8,128)(2,1)}, u32[]{:S(2)}) %copy-start.2) | copy-done | bytes 8388632
  143.6 1.8 add_blocks.3
  145.4 1.0 copy-done.21
  146.4 2.7 %collective-permute-start.22 = (bf16[1,256,1024]{2,1,0:T(8,128)(2,1)}, bf16[1,256,1024]{2,1,0:T(8,128)(2,1)S(1)}, u32[]{:S(2)}, u32[]{:S(2)}) collective-permute-start(bf16[1,256,1024]{2,1,0:T(8,128)(2,1)} %get-tuple-element.73), channel_id=1, source_target_pairs={{0,96},{8,104},{16,112},{24,120},{32,0},{40,8},{48,16},{56,24},{64... | collective-permute-start | bytes 1572872 | tf_op jit(solution)/shard_map/ppermute | solution.py:28
  149.1 1.1 copy.16.kt_ref
  150.2 1.8 collective-permute-start.27
  152.0 2.3 %add_convert_fusion.g_ref = bf16[512,1024]{1,0:T(8,128)(2,1)S(1)} fusion(f32[512,1024]{1,0:T(8,128)} %get-tuple-element.74, bf16[512,1024]{1,0:T(8,128)(2,1)} %collective-permute-done.23), kind=kLoop, calls=%fused_computation | loop fusion | flops 1572864 | bytes 4194304 | tf_op jit(solution)/shard_map/convert_element_type | solution.py:515
  154.3 7.0 %collective-permute-done.21.refs_2_ = bf16[1,256,1024]{2,1,0:T(8,128)(2,1)S(1)} collective-permute-done((bf16[1,256,1024]{2,1,0:T(8,128)(2,1)}, bf16[1,256,1024]{2,1,0:T(8,128)(2,1)S(1)}, u32[]{:S(2)}, u32[]{:S(2)}) %collective-permute-start.21) | collective-permute-done | bytes 524320 | tf_op jit(solution)/shard_map/ppermute | solution.py:28
  161.3 3.4 %copy-done.3 = bf16[2,8,256,1024]{3,2,1,0:T(8,128)(2,1)S(1)} copy-done((bf16[2,8,256,1024]{3,2,1,0:T(8,128)(2,1)S(1)}, bf16[2,8,256,1024]{3,2,1,0:T(8,128)(2,1)}, u32[]{:S(2)}) %copy-start.3) | copy-done | bytes 8388632
  164.7 0.8 add_blocks.4
  165.6 2.7 %collective-permute-start.26 = (bf16[2,256,1024]{2,1,0:T(8,128)(2,1)S(1)}, bf16[2,256,1024]{2,1,0:T(8,128)(2,1)S(1)}, u32[]{:S(2)}, u32[]{:S(2)}) collective-permute-start(bf16[2,256,1024]{2,1,0:T(8,128)(2,1)S(1)} %get-tuple-element.86), channel_id=1, source_target_pairs={{0,96},{8,104},{16,112},{24,120},{32,0},{40,8},{48,16},{56,24},{64... | collective-permute-start | bytes 3145736 | tf_op jit(solution)/shard_map/ppermute | solution.py:28
  168.3 16.9 %attend_back.1 = (bf16[512,1024]{1,0:T(8,128)(2,1)}, f32[1024,128]{1,0:T(8,128)S(1)}, f32[1024,128]{1,0:T(8,128)S(1)}) custom-call(s32[1]{0:T(128)} %bitcast.meta_ref, bf16[512,1024]{1,0:T(8,128)(2,1)S(1)} %copy-done.20, bf16[512,1024]{1,0:T(8,128)(2,1)S(1)} %add_convert_fusion.g_ref, bf16[1024,128]{1,0:T(8,128)(2,1)S(1)} %copy-done.9, ...), custom_call_target="tpu_custom_call" | custom-call | flops 10737418240 | bytes 12582912 | tf_op jit(solution)/shard_map/attend_back/pallas_call | solution.py:168
  185.3 3.3 %collective-permute-start.24 = (bf16[512,256]{1,0:T(8,128)(2,1)S(1)}, bf16[512,256]{1,0:T(8,128)(2,1)S(1)}, u32[]{:S(2)}, u32[]{:S(2)}) collective-permute-start(bf16[512,256]{1,0:T(8,128)(2,1)S(1)} %pad_maximum_fusion.5), channel_id=1, source_target_pairs={{8,0},{16,8},{24,16},{32,24},{40,32},{48,40},{56,48},{64,56},{72,6... | collective-permute-start | bytes 786440 | tf_op jit(solution)/shard_map/ppermute | solution.py:42
  188.6 5.9 %collective-permute-done.24 = bf16[512,256]{1,0:T(8,128)(2,1)S(1)} collective-permute-done((bf16[512,256]{1,0:T(8,128)(2,1)S(1)}, bf16[512,256]{1,0:T(8,128)(2,1)S(1)}, u32[]{:S(2)}, u32[]{:S(2)}) %collective-permute-start.24) | collective-permute-done | bytes 262176 | tf_op jit(solution)/shard_map/ppermute | solution.py:42
  195.3 1.5 add_blocks.5
  (90 shorter events, 5.5 us)
Async XLA Ops:
  0.6 2.9 %copy-start.23 = (bf16[512,128]{1,0:T(8,128)(2,1)S(1)}, bf16[512,128]{1,0:T(8,128)(2,1)}, u32[]{:S(2)}) copy-start(bf16[512,128]{1,0:T(8,128)(2,1)} %param.7) | copy-start | bytes 393220
  0.6 2.9 %copy-start.24 = (bf16[512,128]{1,0:T(8,128)(2,1)S(1)}, bf16[512,128]{1,0:T(8,128)(2,1)}, u32[]{:S(2)}) copy-start(bf16[512,128]{1,0:T(8,128)(2,1)} %param.8) | copy-start | bytes 393220
  2.0 10.3 %collective-permute-start = (bf16[512,512]{1,0:T(8,128)(2,1)S(1)}, bf16[512,512]{1,0:T(8,128)(2,1)S(1)}, u32[]{:S(2)}, u32[]{:S(2)}) collective-permute-start(bf16[512,512]{1,0:T(8,128)(2,1)S(1)} %get-tuple-element.92), channel_id=1, source_target_pairs={{0,8},{8,0},{16,24},{24,16},{32,40},{40,32},{48,56},{56,48},{64,72... | collective-permute-start | bytes 1572872 | tf_op jit(solution)/shard_map/ppermute | solution.py:28
  3.6 11.6 %collective-permute-start.6 = (bf16[512,256]{1,0:T(8,128)(2,1)S(1)}, bf16[512,256]{1,0:T(8,128)(2,1)S(1)}, u32[]{:S(2)}, u32[]{:S(2)}) collective-permute-start(bf16[512,256]{1,0:T(8,128)(2,1)S(1)} %constant_dynamic-update-slice_fusion), channel_id=1, source_target_pairs={{0,8},{8,16},{16,24},{24,32},{32,40},{40,48},{48,56},{56,64},{64,7... | collective-permute-start | bytes 786440 | tf_op jit(solution)/shard_map/ppermute | solution.py:42
  8.4 26.4 %collective-permute-start.4 = (bf16[512,1024]{1,0:T(8,128)(2,1)}, bf16[512,1024]{1,0:T(8,128)(2,1)}, u32[]{:S(2)}, u32[]{:S(2)}) collective-permute-start(bf16[512,1024]{1,0:T(8,128)(2,1)} %refs_8_.1), channel_id=1, source_target_pairs={{0,32},{8,40},{16,48},{24,56},{32,64},{40,72},{48,80},{56,88},{64,... | collective-permute-start | bytes 3145736 | tf_op jit(solution)/shard_map/ppermute | solution.py:28
  10.1 24.7 %collective-permute-start.5 = (bf16[512,1024]{1,0:T(8,128)(2,1)}, bf16[512,1024]{1,0:T(8,128)(2,1)}, u32[]{:S(2)}, u32[]{:S(2)}) collective-permute-start(bf16[512,1024]{1,0:T(8,128)(2,1)} %refs_8_.1), channel_id=1, source_target_pairs={{0,96},{8,104},{16,112},{24,120},{32,0},{40,8},{48,16},{56,24},{64... | collective-permute-start | bytes 3145736 | tf_op jit(solution)/shard_map/ppermute | solution.py:28
  12.4 22.4 %copy-start.5 = (bf16[1024,512]{1,0:T(8,128)(2,1)}, bf16[1024,512]{1,0:T(8,128)(2,1)S(1)}, u32[]{:S(2)}) copy-start(bf16[1024,512]{1,0:T(8,128)(2,1)S(1)} %pad_maximum_fusion.refs_0_) | copy-start | bytes 3145732
  12.4 24.6 %collective-permute-start.1 = (bf16[1024,512]{1,0:T(8,128)(2,1)S(1)}, bf16[1024,512]{1,0:T(8,128)(2,1)S(1)}, u32[]{:S(2)}, u32[]{:S(2)}) collective-permute-start(bf16[1024,512]{1,0:T(8,128)(2,1)S(1)} %pad_maximum_fusion.refs_0_), channel_id=1, source_target_pairs={{0,1},{1,2},{2,3},{3,0},{4,5},{5,6},{6,7},{7,4},{8,9},{9,10},{10,1... | collective-permute-start | bytes 3145736 | tf_op jit(solution)/shard_map/ppermute | solution.py:36
  13.7 24.0 %collective-permute-start.2 = (bf16[1024,512]{1,0:T(8,128)(2,1)S(1)}, bf16[1024,512]{1,0:T(8,128)(2,1)}, u32[]{:S(2)}, u32[]{:S(2)}) collective-permute-start(bf16[1024,512]{1,0:T(8,128)(2,1)S(1)} %pad_maximum_fusion.refs_0_), channel_id=1, source_target_pairs={{0,3},{1,0},{2,1},{3,2},{4,7},{5,4},{6,5},{7,6},{8,11},{9,8},{10,9... | collective-permute-start | bytes 3145736 | tf_op jit(solution)/shard_map/ppermute | solution.py:36
  15.2 0.7 copy-start.22
  15.9 24.0 %collective-permute-start.3 = (bf16[1024,512]{1,0:T(8,128)(2,1)S(1)}, bf16[1024,512]{1,0:T(8,128)(2,1)}, u32[]{:S(2)}, u32[]{:S(2)}) collective-permute-start(bf16[1024,512]{1,0:T(8,128)(2,1)S(1)} %pad_maximum_fusion.refs_0_), channel_id=1, source_target_pairs={{0,4},{1,5},{2,6},{3,7},{4,0},{5,1},{6,2},{7,3},{8,12},{9,13},{10,... | collective-permute-start | bytes 3145736 | tf_op jit(solution)/shard_map/ppermute | solution.py:36
  17.4 17.5 %copy-start.10 = (s32[1024,1]{1,0:T(8,128)}, s32[1024,1]{1,0:T(8,128)S(1)}, u32[]{:S(2)}) copy-start(s32[1024,1]{1,0:T(8,128)S(1)} %copy.15.segk_ref) | copy-start | bytes 12292
  18.6 16.2 %copy-start.8 = (bf16[1024,128]{1,0:T(8,128)(2,1)}, bf16[1024,128]{1,0:T(8,128)(2,1)S(1)}, u32[]{:S(2)}) copy-start(bf16[1024,128]{1,0:T(8,128)(2,1)S(1)} %get-tuple-element.96.k_ref) | copy-start | bytes 786436
  18.7 1.2 copy-start.19
  37.0 12.3 %copy-start.16 = (bf16[1024,512]{1,0:T(8,128)(2,1)}, bf16[1024,512]{1,0:T(8,128)(2,1)S(1)}, u32[]{:S(2)}) copy-start(bf16[1024,512]{1,0:T(8,128)(2,1)S(1)} %collective-permute-done.1.refs_1_) | copy-start | bytes 3145732
  39.9 10.9 %collective-permute-start.12 = (bf16[512,1024]{1,0:T(8,128)(2,1)}, bf16[512,1024]{1,0:T(8,128)(2,1)}, u32[]{:S(2)}, u32[]{:S(2)}) collective-permute-start(bf16[512,1024]{1,0:T(8,128)(2,1)} %get-tuple-element.53), channel_id=1, source_target_pairs={{0,8},{8,0},{16,24},{24,16},{32,40},{40,32},{48,56},{56,48},{64,72... | collective-permute-start | bytes 3145736 | tf_op jit(solution)/shard_map/ppermute | solution.py:28
  39.9 26.0 %collective-permute-start.11 = (bf16[512,1024]{1,0:T(8,128)(2,1)}, bf16[512,1024]{1,0:T(8,128)(2,1)}, u32[]{:S(2)}, u32[]{:S(2)}) collective-permute-start(bf16[512,1024]{1,0:T(8,128)(2,1)} %refs_8_.1), channel_id=1, source_target_pairs={{0,16},{8,24},{16,0},{24,8},{32,48},{40,56},{48,32},{56,40},{64,80... | collective-permute-start | bytes 3145736 | tf_op jit(solution)/shard_map/ppermute | solution.py:28
  42.2 25.9 %collective-permute-start.7 = (bf16[1024,512]{1,0:T(8,128)(2,1)}, bf16[1024,512]{1,0:T(8,128)(2,1)S(1)}, u32[]{:S(2)}, u32[]{:S(2)}) collective-permute-start(bf16[1024,512]{1,0:T(8,128)(2,1)} %collective-permute-done.3.refs_3_), channel_id=1, source_target_pairs={{0,1},{1,2},{2,3},{3,0},{4,5},{5,6},{6,7},{7,4},{8,9},{9,10},{10,1... | collective-permute-start | bytes 3145736 | tf_op jit(solution)/shard_map/ppermute | solution.py:36
  42.2 25.9 %collective-permute-start.8 = (bf16[1024,512]{1,0:T(8,128)(2,1)}, bf16[1024,512]{1,0:T(8,128)(2,1)}, u32[]{:S(2)}, u32[]{:S(2)}) collective-permute-start(bf16[1024,512]{1,0:T(8,128)(2,1)} %collective-permute-done.3.refs_3_), channel_id=1, source_target_pairs={{0,3},{1,0},{2,1},{3,2},{4,7},{5,4},{6,5},{7,6},{8,11},{9,8},{10,9... | collective-permute-start | bytes 3145736 | tf_op jit(solution)/shard_map/ppermute | solution.py:36
  46.1 19.8 %collective-permute-start.10 = (bf16[256,1024]{1,0:T(8,128)(2,1)S(1)}, bf16[256,1024]{1,0:T(8,128)(2,1)S(1)}, u32[]{:S(2)}, u32[]{:S(2)}) collective-permute-start(bf16[256,1024]{1,0:T(8,128)(2,1)S(1)} %slice.48), channel_id=1, source_target_pairs={{0,96},{8,104},{16,112},{24,120},{32,0},{40,8},{48,16},{56,24},{64... | collective-permute-start | bytes 1572872 | tf_op jit(solution)/shard_map/ppermute | solution.py:28
  49.3 3.3 %copy-start.6 = (bf16[1024,512]{1,0:T(8,128)(2,1)S(1)}, bf16[1024,512]{1,0:T(8,128)(2,1)}, u32[]{:S(2)}) copy-start(bf16[1024,512]{1,0:T(8,128)(2,1)} %copy-done.5) | copy-start | bytes 3145732
  49.3 3.3 %copy-start.17 = (bf16[1024,512]{1,0:T(8,128)(2,1)S(1)}, bf16[1024,512]{1,0:T(8,128)(2,1)}, u32[]{:S(2)}) copy-start(bf16[1024,512]{1,0:T(8,128)(2,1)} %copy-done.16) | copy-start | bytes 3145732
  50.8 15.1 %collective-permute-start.9 = (bf16[256,1024]{1,0:T(8,128)(2,1)S(1)}, bf16[256,1024]{1,0:T(8,128)(2,1)S(1)}, u32[]{:S(2)}, u32[]{:S(2)}) collective-permute-start(bf16[256,1024]{1,0:T(8,128)(2,1)S(1)} %slice.47), channel_id=1, source_target_pairs={{0,32},{8,40},{16,48},{24,56},{32,64},{40,72},{48,80},{56,88},{64,... | collective-permute-start | bytes 1572872 | tf_op jit(solution)/shard_map/ppermute | solution.py:28
  65.9 6.4 %copy-start.12 = (bf16[256,1024]{1,0:T(8,128)(2,1)}, bf16[256,1024]{1,0:T(8,128)(2,1)S(1)}, u32[]{:S(2)}) copy-start(bf16[256,1024]{1,0:T(8,128)(2,1)S(1)} %collective-permute-done.10.refs_16_) | copy-start | bytes 1572868
  65.9 6.3 %copy-start.14 = (bf16[256,1024]{1,0:T(8,128)(2,1)}, bf16[256,1024]{1,0:T(8,128)(2,1)S(1)}, u32[]{:S(2)}) copy-start(bf16[256,1024]{1,0:T(8,128)(2,1)S(1)} %collective-permute-done.9.refs_15_) | copy-start | bytes 1572868
  68.1 10.6 %copy-start.4 = (bf16[1024,512]{1,0:T(8,128)(2,1)}, bf16[1024,512]{1,0:T(8,128)(2,1)S(1)}, u32[]{:S(2)}) copy-start(bf16[1024,512]{1,0:T(8,128)(2,1)S(1)} %collective-permute-done.7.refs_0_.refs_4_) | copy-start | bytes 3145732
  69.3 4.8 %slice-start.2 = ((bf16[1024,512]{1,0:T(8,128)(2,1)}), bf16[512,512]{1,0:T(8,128)(2,1)S(1)}, s32[]{:S(2)}) async-start(bf16[1024,512]{1,0:T(8,128)(2,1)} %copy-done.16), calls=%async_computation.2 | async-start | bytes 1048576 | tf_op jit(solution)/shard_map/slice | solution.py:466
  69.3 25.4 %collective-permute-start.17 = (bf16[512,1024]{1,0:T(8,128)(2,1)}, bf16[512,1024]{1,0:T(8,128)(2,1)}, u32[]{:S(2)}, u32[]{:S(2)}) collective-permute-start(bf16[512,1024]{1,0:T(8,128)(2,1)} %pad_maximum_fusion.3), channel_id=1, source_target_pairs={{0,16},{8,24},{16,0},{24,8},{32,48},{40,56},{48,32},{56,40},{64,80... | collective-permute-start | bytes 3145736 | tf_op jit(solution)/shard_map/ppermute | solution.py:28
  72.3 23.7 %collective-permute-start.14 = (bf16[1024,512]{1,0:T(8,128)(2,1)}, bf16[1024,512]{1,0:T(8,128)(2,1)}, u32[]{:S(2)}, u32[]{:S(2)}) collective-permute-start(bf16[1024,512]{1,0:T(8,128)(2,1)} %pad_maximum_fusion.2), channel_id=1, source_target_pairs={{0,3},{1,0},{2,1},{3,2},{4,7},{5,4},{6,5},{7,6},{8,11},{9,8},{10,9... | collective-permute-start | bytes 3145736 | tf_op jit(solution)/shard_map/ppermute | solution.py:36
  75.1 23.8 %collective-permute-start.13 = (bf16[1024,512]{1,0:T(8,128)(2,1)}, bf16[1024,512]{1,0:T(8,128)(2,1)}, u32[]{:S(2)}, u32[]{:S(2)}) collective-permute-start(bf16[1024,512]{1,0:T(8,128)(2,1)} %pad_maximum_fusion.1), channel_id=1, source_target_pairs={{0,1},{1,2},{2,3},{3,0},{4,5},{5,6},{6,7},{7,4},{8,9},{9,10},{10,1... | collective-permute-start | bytes 3145736 | tf_op jit(solution)/shard_map/ppermute | solution.py:36
  75.1 25.3 %collective-permute-start.15 = (bf16[512,1024]{1,0:T(8,128)(2,1)}, bf16[512,1024]{1,0:T(8,128)(2,1)}, u32[]{:S(2)}, u32[]{:S(2)}) collective-permute-start(bf16[512,1024]{1,0:T(8,128)(2,1)} %collective-permute-done.11.refs_11_), channel_id=1, source_target_pairs={{0,32},{8,40},{16,48},{24,56},{32,64},{40,72},{48,80},{56,88},{64,... | collective-permute-start | bytes 3145736 | tf_op jit(solution)/shard_map/ppermute | solution.py:28
  76.7 23.8 %collective-permute-start.16 = (bf16[512,1024]{1,0:T(8,128)(2,1)}, bf16[512,1024]{1,0:T(8,128)(2,1)}, u32[]{:S(2)}, u32[]{:S(2)}) collective-permute-start(bf16[512,1024]{1,0:T(8,128)(2,1)} %collective-permute-done.11.refs_11_), channel_id=1, source_target_pairs={{0,96},{8,104},{16,112},{24,120},{32,0},{40,8},{48,16},{56,24},{64... | collective-permute-start | bytes 3145736 | tf_op jit(solution)/shard_map/ppermute | solution.py:28
  78.8 3.4 %copy-start = (bf16[2,8,256,1024]{3,2,1,0:T(8,128)(2,1)S(1)}, bf16[2,8,256,1024]{3,2,1,0:T(8,128)(2,1)}, u32[]{:S(2)}) copy-start(bf16[2,8,256,1024]{3,2,1,0:T(8,128)(2,1)} %project.3.refs_3_) | copy-start | bytes 25165828
  107.0 3.3 %copy-start.1 = (bf16[2,8,256,1024]{3,2,1,0:T(8,128)(2,1)}, bf16[2,8,256,1024]{3,2,1,0:T(8,128)(2,1)S(1)}, u32[]{:S(2)}) copy-start(bf16[2,8,256,1024]{3,2,1,0:T(8,128)(2,1)S(1)} %project.5.refs_0_.refs_1_) | copy-start | bytes 25165828
  110.2 24.7 %collective-permute-start.18 = (bf16[2,256,1024]{2,1,0:T(8,128)(2,1)}, bf16[2,256,1024]{2,1,0:T(8,128)(2,1)S(1)}, u32[]{:S(2)}, u32[]{:S(2)}) collective-permute-start(bf16[2,256,1024]{2,1,0:T(8,128)(2,1)} %get-tuple-element.90), channel_id=1, source_target_pairs={{0,32},{8,40},{16,48},{24,56},{32,64},{40,72},{48,80},{56,88},{64,... | collective-permute-start | bytes 3145736 | tf_op jit(solution)/shard_map/ppermute | solution.py:28
  110.7 24.3 %collective-permute-start.19 = (bf16[2,256,1024]{2,1,0:T(8,128)(2,1)}, bf16[2,256,1024]{2,1,0:T(8,128)(2,1)S(1)}, u32[]{:S(2)}, u32[]{:S(2)}) collective-permute-start(bf16[2,256,1024]{2,1,0:T(8,128)(2,1)} %get-tuple-element.89), channel_id=1, source_target_pairs={{0,96},{8,104},{16,112},{24,120},{32,0},{40,8},{48,16},{56,24},{64... | collective-permute-start | bytes 3145736 | tf_op jit(solution)/shard_map/ppermute | solution.py:28
  112.9 23.2 %collective-permute-start.20 = (bf16[2,256,1024]{2,1,0:T(8,128)(2,1)}, bf16[2,256,1024]{2,1,0:T(8,128)(2,1)S(1)}, u32[]{:S(2)}, u32[]{:S(2)}) collective-permute-start(bf16[2,256,1024]{2,1,0:T(8,128)(2,1)} %get-tuple-element.88), channel_id=1, source_target_pairs={{0,16},{8,24},{16,0},{24,8},{32,48},{40,56},{48,32},{56,40},{64,80... | collective-permute-start | bytes 3145736 | tf_op jit(solution)/shard_map/ppermute | solution.py:28
  114.7 1.2 copy-start.7
  115.9 1.0 copy-start.13
  117.0 1.0 copy-start.15
  118.0 1.2 copy-start.18
  136.1 15.9 %collective-permute-start.23 = (bf16[512,1024]{1,0:T(8,128)(2,1)}, bf16[512,1024]{1,0:T(8,128)(2,1)}, u32[]{:S(2)}, u32[]{:S(2)}) collective-permute-start(bf16[512,1024]{1,0:T(8,128)(2,1)} %get-tuple-element.75), channel_id=1, source_target_pairs={{0,8},{8,0},{16,24},{24,16},{32,40},{40,32},{48,56},{56,48},{64,72... | collective-permute-start | bytes 3145736 | tf_op jit(solution)/shard_map/ppermute | solution.py:28
  140.2 3.4 %copy-start.2 = (bf16[2,8,256,1024]{3,2,1,0:T(8,128)(2,1)S(1)}, bf16[2,8,256,1024]{3,2,1,0:T(8,128)(2,1)}, u32[]{:S(2)}) copy-start(bf16[2,8,256,1024]{3,2,1,0:T(8,128)(2,1)} %copy-done.1) | copy-start | bytes 25165828
  145.4 1.0 copy-start.21
  146.4 15.0 %collective-permute-start.21 = (bf16[1,256,1024]{2,1,0:T(8,128)(2,1)}, bf16[1,256,1024]{2,1,0:T(8,128)(2,1)S(1)}, u32[]{:S(2)}, u32[]{:S(2)}) collective-permute-start(bf16[1,256,1024]{2,1,0:T(8,128)(2,1)} %get-tuple-element.72), channel_id=1, source_target_pairs={{0,32},{8,40},{16,48},{24,56},{32,64},{40,72},{48,80},{56,88},{64,... | collective-permute-start | bytes 1572872 | tf_op jit(solution)/shard_map/ppermute | solution.py:28
  146.4 15.0 %collective-permute-start.22 = (bf16[1,256,1024]{2,1,0:T(8,128)(2,1)}, bf16[1,256,1024]{2,1,0:T(8,128)(2,1)S(1)}, u32[]{:S(2)}, u32[]{:S(2)}) collective-permute-start(bf16[1,256,1024]{2,1,0:T(8,128)(2,1)} %get-tuple-element.73), channel_id=1, source_target_pairs={{0,96},{8,104},{16,112},{24,120},{32,0},{40,8},{48,16},{56,24},{64... | collective-permute-start | bytes 1572872 | tf_op jit(solution)/shard_map/ppermute | solution.py:28
  150.2 45.1 %collective-permute-start.27 = (bf16[2,256,1024]{2,1,0:T(8,128)(2,1)}, bf16[2,256,1024]{2,1,0:T(8,128)(2,1)S(1)}, u32[]{:S(2)}, u32[]{:S(2)}) collective-permute-start(bf16[2,256,1024]{2,1,0:T(8,128)(2,1)} %copy-done.21), channel_id=1, source_target_pairs={{0,16},{8,24},{16,0},{24,8},{32,48},{40,56},{48,32},{56,40},{64,80... | collective-permute-start | bytes 3145736 | tf_op jit(solution)/shard_map/ppermute | solution.py:28
  152.0 16.3 %copy-start.9 = (bf16[1024,128]{1,0:T(8,128)(2,1)S(1)}, bf16[1024,128]{1,0:T(8,128)(2,1)}, u32[]{:S(2)}) copy-start(bf16[1024,128]{1,0:T(8,128)(2,1)} %copy-done.8) | copy-start | bytes 786436
  152.0 16.3 %copy-start.11 = (s32[1024,1]{1,0:T(8,128)S(1)}, s32[1024,1]{1,0:T(8,128)}, u32[]{:S(2)}) copy-start(s32[1024,1]{1,0:T(8,128)} %copy-done.10) | copy-start | bytes 12292
  152.0 16.3 %copy-start.20 = (bf16[512,1024]{1,0:T(8,128)(2,1)S(1)}, bf16[512,1024]{1,0:T(8,128)(2,1)}, u32[]{:S(2)}) copy-start(bf16[512,1024]{1,0:T(8,128)(2,1)} %q_ref.2) | copy-start | bytes 3145732
  161.3 3.4 %copy-start.3 = (bf16[2,8,256,1024]{3,2,1,0:T(8,128)(2,1)S(1)}, bf16[2,8,256,1024]{3,2,1,0:T(8,128)(2,1)}, u32[]{:S(2)}) copy-start(bf16[2,8,256,1024]{3,2,1,0:T(8,128)(2,1)} %copy-done.1) | copy-start | bytes 25165828
  165.6 29.8 %collective-permute-start.25 = (bf16[2,256,1024]{2,1,0:T(8,128)(2,1)S(1)}, bf16[2,256,1024]{2,1,0:T(8,128)(2,1)S(1)}, u32[]{:S(2)}, u32[]{:S(2)}) collective-permute-start(bf16[2,256,1024]{2,1,0:T(8,128)(2,1)S(1)} %get-tuple-element.79), channel_id=1, source_target_pairs={{0,32},{8,40},{16,48},{24,56},{32,64},{40,72},{48,80},{56,88},{64,... | collective-permute-start | bytes 3145736 | tf_op jit(solution)/shard_map/ppermute | solution.py:28
  165.6 29.7 %collective-permute-start.26 = (bf16[2,256,1024]{2,1,0:T(8,128)(2,1)S(1)}, bf16[2,256,1024]{2,1,0:T(8,128)(2,1)S(1)}, u32[]{:S(2)}, u32[]{:S(2)}) collective-permute-start(bf16[2,256,1024]{2,1,0:T(8,128)(2,1)S(1)} %get-tuple-element.86), channel_id=1, source_target_pairs={{0,96},{8,104},{16,112},{24,120},{32,0},{40,8},{48,16},{56,24},{64... | collective-permute-start | bytes 3145736 | tf_op jit(solution)/shard_map/ppermute | solution.py:28
  168.3 27.0 %slice-start = ((s8[8388608]{0:T(1024)(128)(4,1)}), s8[4194304]{0:T(1024)(128)(4,1)S(1)}, s32[]{:S(2)}) async-start(s8[8388608]{0:T(1024)(128)(4,1)} %bitcast.28), calls=%async_computation | async-start | bytes 8388608
  168.3 27.0 %slice-start.1 = ((s8[8388608]{0:T(1024)(128)(4,1)}), s8[4194304]{0:T(1024)(128)(4,1)S(1)}, s32[]{:S(2)}) async-start(s8[8388608]{0:T(1024)(128)(4,1)} %bitcast.28), calls=%async_computation.1 | async-start | bytes 8388608
  185.3 9.2 %collective-permute-start.24 = (bf16[512,256]{1,0:T(8,128)(2,1)S(1)}, bf16[512,256]{1,0:T(8,128)(2,1)S(1)}, u32[]{:S(2)}, u32[]{:S(2)}) collective-permute-start(bf16[512,256]{1,0:T(8,128)(2,1)S(1)} %pad_maximum_fusion.5), channel_id=1, source_target_pairs={{8,0},{16,8},{24,16},{32,24},{40,32},{48,40},{56,48},{64,56},{72,6... | collective-permute-start | bytes 786440 | tf_op jit(solution)/shard_map/ppermute | solution.py:42

commit v3 on v2

--- a/solution.py
+++ b/solution.py
@@ -112,7 +112,7 @@
             jax.ShapeDtypeStruct((heads, 1, count), F32),
             jax.ShapeDtypeStruct((heads, 1, count), F32),
         ],
-        compiler_params=params(40),
+        compiler_params=params(53),
         cost_estimate=pl.CostEstimate(
             flops=heads * 4 * 2 * 2 * count * count * HD,
             bytes_accessed=8 * 2**20,
@@ -189,7 +189,7 @@
             jax.ShapeDtypeStruct((2 * count, HD), F32),
             jax.ShapeDtypeStruct((2 * count, HD), F32),
         ],
-        compiler_params=params(40),
+        compiler_params=params(53),
         cost_estimate=pl.CostEstimate(
             flops=heads * 10 * 2 * 2 * count * count * HD,
             bytes_accessed=12 * 2**20,
@@ -199,50 +199,32 @@
     )(first, query, grad, key_pair, kt, value_pair, segq, segk, top, total)
 
 
-def proj_kernel(split, n_blocks, n_in, held, meta_ref, *refs):
+def proj_kernel(n_in, held, meta_ref, *refs):
     pieces, a_ref = refs[:n_in], refs[n_in]
     out_ref = refs[n_in + 1 + held]
     step = pl.program_id(0)
-    h = a_ref.shape[0] // 2
-    over_tokens = (((0,), (0,)), ((), ()))
-
-    def store(value):
-        value = value.astype(BF)
-        rows = value.shape[0] // 2
-        out_ref[0, 0] = value[:rows]
-        out_ref[1, 0] = value[rows:]
-
-    for j in range(n_blocks):
+    rows = out_ref.shape[2]
+
+    for j in range(n_in):
 
         @pl.when(step == j)
         def _():
-            if split:
-                part = slice(j * h, (j + 1) * h)
-                store(
-                    lax.dot_general(
-                        pieces[0][part, :], a_ref[:h, :], over_tokens, preferred_element_type=F32
-                    )
-                    + lax.dot_general(
-                        pieces[1][part, :], a_ref[h:, :], over_tokens, preferred_element_type=F32
-                    )
-                )
-            else:
-                store(
-                    lax.dot_general(
-                        pieces[j][...], a_ref[...], over_tokens, preferred_element_type=F32
-                    )
-                )
-
-
-def project(pieces, split, a_pair, blocks, buffer):
+            value = lax.dot_general(
+                pieces[j][...], a_ref[...], (((0,), (0,)), ((), ())), preferred_element_type=F32
+            ).astype(BF)
+            out_ref[0, 0] = value[:rows]
+            out_ref[1, 0] = value[rows:]
+
+
+def project(pieces, a_pair, blocks, buffer):
     tokens, width = a_pair.shape
     depth = pieces[0].shape[1]
-    n_blocks = 2 if split else len(pieces)
+    n_blocks = len(pieces)
     held = int(buffer is not None)
     whole = lambda shape: pl.BlockSpec(shape, lambda j, m: (0,) * len(shape))
     operands = (*pieces, a_pair) + ((buffer,) if held else ())
     return pl.pallas_call(
-        functools.partial(proj_kernel, split, n_blocks, len(pieces), held),
+        functools.partial(proj_kernel, n_blocks, held),
         grid_spec=pltpu.PrefetchScalarGridSpec(
             num_scalar_prefetch=1,
             grid=(n_blocks,),
@@ -253,7 +235,7 @@
         ),
         out_shape=jax.ShapeDtypeStruct((2, 8, depth // 2, width), BF),
         input_output_aliases={len(pieces) + 2: 0} if held else {},
-        compiler_params=params(40),
+        compiler_params=params(53),
         cost_estimate=pl.CostEstimate(
             flops=2 * n_blocks * tokens * depth * width,
             bytes_accessed=(2 * n_blocks + 2) * 2**20,
@@ -345,7 +327,7 @@
             jax.ShapeDtypeStruct((half, width), F32),
             jax.ShapeDtypeStruct((half, width), BF),
         ],
-        compiler_params=params(48),
+        compiler_params=params(53),
         cost_estimate=pl.CostEstimate(
             flops=16 * tokens * depth * width,
             bytes_accessed=20 * 2**20,
@@ -355,49 +337,51 @@
     )(meta, *g_pieces, *w_pieces)
 
 
-def add_kernel(n_blocks, plan, meta_ref, *refs):
-    blocks = refs[:n_blocks]
-    n_out = len(plan)
-    terms = refs[n_blocks:len(refs) - n_out]
-    for out_ref, (block, part, extra) in zip(refs[len(refs) - n_out:], plan):
-        if part is None:
-            for p in range(2):
-                value = blocks[block][p, 0]
-                added = [e if isinstance(e, int) else e[0] for e in extra if isinstance(e, int) or e[1] == p]
-                if added:
-                    value = value.astype(F32)
-                    for e in added:
-                        term = terms[e]
-                        value = value + (term[p] if term.shape[0] == 2 else term[0]).astype(F32)
-                out_ref[p] = value.astype(BF)
-        else:
-            value = blocks[block][part, 0].astype(F32)
-            for e in extra:
-                value = value + terms[e][part].astype(F32)
-            out_ref[0] = value.astype(BF)
+def add_kernel(n_terms, plan, meta_ref, buffer_ref, *refs):
+    terms, outs = refs[:n_terms], refs[n_terms:n_terms + len(plan)]
+    blocks, sems = refs[n_terms + len(plan):]
+    copies = [
+        pltpu.make_async_copy(buffer_ref.at[:, meta_ref[n]], blocks.at[n], sems.at[n])
+        for n in range(blocks.shape[0])
+    ]
+    for copy in copies:
+        copy.start()
+    for copy in copies:
+        copy.wait()
+    for out_ref, (block, half, extra) in zip(outs, plan):
+        for place, part in enumerate((0, 1) if half is None else (half,)):
+            value = blocks[block, part].astype(F32)
+            for term, at in extra:
+                if at is None:
+                    value = value + terms[term][part].astype(F32)
+                elif at == part:
+                    value = value + terms[term][0].astype(F32)
+            out_ref[place] = value.astype(BF)
 
 
 def add_blocks(buffer, blocks, terms, plan):
     _, _, rows, width = buffer.shape
-    n_blocks = blocks.shape[0]
-    place = lambda n: pl.BlockSpec((2, 1, rows, width), lambda i, m: (0, m[n], 0, 0))
     whole = lambda shape: pl.BlockSpec(shape, lambda i, m: (0,) * len(shape))
-    shapes = [(2 if part is None else 1, rows, width) for _, part, _ in plan]
+    shapes = [(2 if half is None else 1, rows, width) for _, half, _ in plan]
     return pl.pallas_call(
-        functools.partial(add_kernel, n_blocks, plan),
+        functools.partial(add_kernel, len(terms), plan),
         grid_spec=pltpu.PrefetchScalarGridSpec(
             num_scalar_prefetch=1,
             grid=(1,),
-            in_specs=[place(n) for n in range(n_blocks)] + [whole(t.shape) for t in terms],
+            in_specs=[pl.BlockSpec(memory_space=pl.ANY)] + [whole(t.shape) for t in terms],
             out_specs=[whole(shape) for shape in shapes],
+            scratch_shapes=[
+                pltpu.VMEM((blocks.shape[0], 2, rows, width), BF),
+                pltpu.SemaphoreType.DMA((blocks.shape[0],)),
+            ],
         ),
         out_shape=[jax.ShapeDtypeStruct(shape, BF) for shape in shapes],
-        compiler_params=params(32),
+        compiler_params=params(53),
         cost_estimate=pl.CostEstimate(
             flops=2**21, bytes_accessed=5 * 2**20, transcendentals=0
         ),
         name="add_blocks",
-    )(blocks, *([buffer] * n_blocks), *terms)
+    )(blocks, buffer, *terms)
 
 
 def local(query_rows, key_rows, value_rows, output_grad, out_proj, segment_ids):
@@ -445,59 +429,55 @@
 
     h = g0.shape[0] // 2
     hw = out_proj.shape[0] // 2
-    a_other = move_row(attn_out, dk=1)
     gyxm = move_col(gy, dx=1)
     gyxp = move_col(gy, dx=-1)
-    wom = move_row(wzm[:hw], dz=1)
-    wop = move_row(wzp[hw:], dz=-1)
+    a_other = move_row(attn_out, dk=1)
+    wo = move_row(wzm, dz=1)
     wy = move_row(out_proj, dyh=1)
 
     a_pair = jnp.concatenate([attn_out, a_other], 0)
     proj = project(
         [g0, gxm, gxp, gy],
-        False,
         a_pair,
         ints(gblock(0, 0), gblock(0, -1), gblock(0, 1), gblock(1, 0)),
         None,
     )
 
-    gyxm, gyxp, wom, wop, wy, proj = tied((gyxm, gyxp, wom, wop, wy, proj))
-
-    gom = move_col(jnp.concatenate([gxm[:h], gyxm[:h]], 0), dx=1)
-    gop = move_col(jnp.concatenate([gxp[h:], gyxp[h:]], 0), dx=-1)
+    gyxm, gyxp, wo, wy, proj = tied((gyxm, gyxp, wo, wy, proj))
+
+    go = move_col(gxm, dx=1)
+    gyo = move_col(gyxp, dx=-1)
     wyzm = move_row(wy, dz=1)
     wyzp = move_row(wy, dz=-1)
-    wyo = move_row(jnp.concatenate([wom, wop], 0), dyh=1)
-
-    proj = project([gyxm, gyxp], False, a_pair, ints(gblock(1, -1), gblock(1, 1)), proj)
-
-    gom, gop, wyzm, wyzp, wyo, proj = tied((gom, gop, wyzm, wyzp, wyo, proj))
-
-    proj = project([gom, gop], True, a_pair, ints(gblock(0, 2), gblock(1, 2)), proj)
-
-    def block_at(dz, dy):
-        return lax.dynamic_slice_in_dim(proj, wblock(dz, dy), 1, 1)[:, 0]
-
-    rup = move_row(block_at(1, 1), dz=1)
-    rdn = move_row(block_at(-1, 1), dz=-1)
-    ry = move_row(block_at(2, 1), dyh=1)
-
-    g_pieces = [g0, gxm, gxp, gy, gyxm, gyxp, gom, gop]
-    gplan = [(i, p * h, i, p) for i in range(6) for p in range(2)] + [
-        (6, 0, 6, 0),
-        (6, h, 7, 0),
-        (7, 0, 6, 1),
-        (7, h, 7, 1),
-    ]
-    w_pieces = [out_proj, wzm, wzp, wy, wyzm, wyzp, wyo, wom, wop]
-    wplan = [(i, p * hw, i, p) for i in range(7) for p in range(2)] + [(7, 0, 7, 0), (8, 0, 7, 1)]
+    wyo = move_row(wo, dyh=1)
+
+    proj = project([gyxm, gyxp], a_pair, ints(gblock(1, -1), gblock(1, 1)), proj)
+
+    go, gyo, wyzm, wyzp, wyo, proj = tied((go, gyo, wyzm, wyzp, wyo, proj))
+
+    proj = project([go, gyo], a_pair, ints(gblock(0, 2), gblock(1, 2)), proj)
+
+    give_up, give_dn, give_far = add_blocks(
+        proj,
+        ints(wblock(1, 1), wblock(-1, 1), wblock(2, 1)),
+        [],
+        [(0, None, ()), (1, None, ()), (2, None, ())],
+    )
+    rup = move_row(give_up, dz=1)
+    rdn = move_row(give_dn, dz=-1)
+    ry = move_row(give_far, dyh=1)
+
+    g_pieces = [g0, gxm, gxp, gy, gyxm, gyxp, go, gyo]
+    gplan = [(i, p * h, i, p) for i in range(8) for p in range(2)]
+    w_pieces = [out_proj, wzm, wzp, wy, wyzm, wyzp, wyo, wo]
+    wplan = [(i, p * hw, i, p) for i in range(8) for p in range(2)]
     meta = ints(
         gblock(0, 0), gblock(0, -1), gblock(0, 1), gblock(1, 0),
         gblock(1, -1), gblock(1, 1), gblock(0, 2), gblock(1, 2),
         wblock(0, 0), wblock(-1, 0), wblock(1, 0), wblock(0, 1),
         wblock(-1, 1), wblock(1, 1), wblock(2, 1), wblock(2, 0),
     )
-    (meta,) = tied((meta,), proj)
+    (meta,) = tied((meta,), give_up)
     grad_own, grad_give = attn_grad_part(g_pieces, gplan, w_pieces, wplan, meta)
 
     rup, rdn, ry, grad_own, grad_give = tied((rup, rdn, ry, grad_own, grad_give))
@@ -506,7 +486,7 @@
         proj,
         ints(wblock(0, 1), wblock(2, 0)),
         [rup, rdn, ry],
-        [(0, None, (0, 1)), (1, 0, (2,)), (1, 1, (2,))],
+        [(0, None, ((0, None), (1, None))), (1, 0, ((2, None),)), (1, 1, ((2, None),))],
     )
     fup = move_row(far_up, dz=1)
     fdn = move_row(far_dn, dz=-1)
@@ -536,7 +516,7 @@
     value_grad = (dvalue[count:] + back[:, HD:]).astype(BF)
 
     (proj_grad,) = add_blocks(
-        proj, ints(wblock(0, 0)), [nup, ndn, across], [(0, None, (0, 1, 2))]
+        proj, ints(wblock(0, 0)), [nup, ndn, across], [(0, None, ((0, None), (1, None), (2, None)))]
     )
     return (query_grad, key_grad, value_grad, proj_grad.reshape(2 * hw, out_proj.shape[1]))
 

time: 198 us -> 205 us (1.035)
  Pallas kernels: 69.2 us -> 91.8 us
  local copies, waits for them, and re-layouts: 33.5 us -> 12.5 us
  waiting for transfers between devices: 40 us -> 48.6 us
  other arithmetic: 8.01 us -> 5.61 us
    pallas_call x6 -> x7, Pallas kernels: 21.7 us -> 41.3 us  [the longest x3 22.4 us: project(): pl.pallas_call(functools.partial(proj_kernel, n_blocks, held), grid_spec=...]
    unnamed x56 -> x26, local copies, waits for them, and re-layouts: 22.4 us -> 5.69 us
    ppermute x19 -> x18, waiting for transfers between devices: 22.7 us -> 27.7 us  [move_row(): return lax.ppermute(value, 'row', pairs)]
    slice x7 -> x0, local copies, waits for them, and re-layouts: 4.34 us -> none  [the longest x2 2.15 us: local(): gop = move_col(jnp.concatenate([gxp[h:], gyxp[h:]], 0), dx=-1)]
    ppermute x7, waiting for transfers between devices: 11.4 us -> 15 us  [move_col(): return lax.ppermute(value, 'col', pairs)]
    concatenate x3 -> x0, other arithmetic: 3.28 us -> none  [the longest x1 1.14 us: local(): wyo = move_row(jnp.concatenate([wom, wop], 0), dyh=1)]
    ppermute x19 -> x18, starting transfers between devices: 29.4 us -> 28.2 us  [move_row(): return lax.ppermute(value, 'row', pairs)]
  transfers between devices with their start and end apart: 28 -> 27, of which waited for: 12 -> 15; matrix products, arithmetic and copies ran while one was open for 8% -> 6% of each run, Pallas kernels for 32% -> 38%
where the time goes in v3:
time: 205 us; the launch traced here: 204 us
  Pallas kernels  91.8 us (45%)
  waiting for transfers between devices  48.6 us (24%)
  starting transfers between devices  44.5 us (22%)
  local copies, waits for them, and re-layouts  12.5 us (6%)
  other arithmetic  5.61 us (3%)
    ppermute x18, starting transfers between devices, move_row(): return lax.ppermute(value, 'row', pairs)  28.2 us
    ppermute x18, waiting for transfers between devices, move_row(): return lax.ppermute(value, 'row', pairs)  27.7 us
    pallas_call x3, Pallas kernels, project(): pl.pallas_call(functools.partial(proj_kernel, n_blocks, held), grid_spec=...  22.4 us
    pallas_call x4, Pallas kernels, add_blocks(): pl.pallas_call(functools.partial(add_kernel, len(terms), plan), grid_spec...  18.9 us
    pallas_call x1, Pallas kernels, attend_back(): pl.pallas_call(bwd_kernel, grid_spec=pltpu.PrefetchScalarGridSpec(num_sca...  18.1 us
    pallas_call x1, Pallas kernels, attn_grad_part(): pl.pallas_call(kernel, grid_spec=pltpu.PrefetchScalarGridSpec(num_scalar_...  16.6 us
    pallas_call x1, Pallas kernels, attend(): pl.pallas_call(fwd_kernel, grid_spec=pltpu.PrefetchScalarGridSpec(num_sca...  15.8 us
    ppermute x7, waiting for transfers between devices, move_col(): return lax.ppermute(value, 'col', pairs)  15 us
  transfers between devices with their start and end apart: 27, of which 15 were waited for; matrix products, arithmetic and copies ran while one was open for 6% of the time, Pallas kernels for 38%

profile of v3, /device:TPU:1, one launch (start us, length us, event | category | flops | bytes accessed | tf_op | source)
XLA Modules:
  0.0 204.1 jit_solution(6075123623242145378)
XLA Ops:
  0.7 1.3 constant_dynamic-slice_fusion.1
  2.0 1.5 collective-permute-start
  3.6 4.8 %collective-permute-start.6 = (bf16[512,256]{1,0:T(8,128)(2,1)S(1)}, bf16[512,256]{1,0:T(8,128)(2,1)S(1)}, u32[]{:S(2)}, u32[]{:S(2)}) collective-permute-start(bf16[512,256]{1,0:T(8,128)(2,1)S(1)} %constant_dynamic-update-slice_fusion), channel_id=1, source_target_pairs={{0,8},{8,16},{16,24},{24,32},{32,40},{40,48},{48,56},{56,64},{64,7... | collective-permute-start | bytes 786440 | tf_op jit(solution)/shard_map/ppermute | solution.py:42
  8.4 1.7 collective-permute-start.4
  10.1 2.2 %collective-permute-start.5 = (bf16[512,1024]{1,0:T(8,128)(2,1)}, bf16[512,1024]{1,0:T(8,128)(2,1)}, u32[]{:S(2)}, u32[]{:S(2)}) collective-permute-start(bf16[512,1024]{1,0:T(8,128)(2,1)} %refs_8_.1), channel_id=1, source_target_pairs={{0,96},{8,104},{16,112},{24,120},{32,0},{40,8},{48,16},{56,24},{64... | collective-permute-start | bytes 3145736 | tf_op jit(solution)/shard_map/ppermute | solution.py:28
  12.4 1.3 collective-permute-start.1
  13.7 1.5 collective-permute-start.2
  15.2 0.4 collective-permute-start.3
  15.6 0.8 fusion.3
  16.4 1.0 copy.15.segk_ref
  17.5 0.1 copy.14.vt_ref
  17.7 15.8 %attend.1 = (bf16[512,1024]{1,0:T(8,128)(2,1)}, f32[8,1,512]{2,1,0:T(1,128)S(1)}, f32[8,1,512]{2,1,0:T(1,128)S(1)}) custom-call(s32[1]{0:T(128)} %bitcast.meta_ref, bf16[512,1024]{1,0:T(8,128)(2,1)} %q_ref.2, bf16[1024,128]{1,0:T(8,128)(2,1)S(1)} %get-tuple-element.97.k_ref, bf16[128,1024]{1,0:T(8,128)(2,1)S(1)} %copy.14.vt_ref, s32[1,512]{1,0:T(1,128)S(1)} %bitcast.24, ...), custom_call_target="tpu_custom_call" | custom-call | flops 4294967296 | bytes 8388608 | tf_op jit(solution)/shard_map/attend/pallas_call | solution.py:95
  33.5 0.9 collective-permute-done.4.refs_9_
  34.4 2.7 %collective-permute-done.1.refs_1_ = bf16[1024,512]{1,0:T(8,128)(2,1)} collective-permute-done((bf16[1024,512]{1,0:T(8,128)(2,1)S(1)}, bf16[1024,512]{1,0:T(8,128)(2,1)}, u32[]{:S(2)}, u32[]{:S(2)}) %collective-permute-start.1) | collective-permute-done | bytes 1048608 | tf_op jit(solution)/shard_map/ppermute | solution.py:36
  37.1 0.6 collective-permute-done.2.refs_2_
  37.7 1.5 collective-permute-done.3.refs_3_
  39.2 2.4 %collective-permute-start.11 = (bf16[512,1024]{1,0:T(8,128)(2,1)}, bf16[512,1024]{1,0:T(8,128)(2,1)}, u32[]{:S(2)}, u32[]{:S(2)}) collective-permute-start(bf16[512,1024]{1,0:T(8,128)(2,1)} %refs_8_.1), channel_id=1, source_target_pairs={{0,16},{8,24},{16,0},{24,8},{32,48},{40,56},{48,32},{56,40},{64,80... | collective-permute-start | bytes 3145736 | tf_op jit(solution)/shard_map/ppermute | solution.py:28
  41.5 0.4 collective-permute-start.10
  42.0 0.1 collective-permute-start.8
  42.1 2.5 %collective-permute-start.9 = (bf16[1024,512]{1,0:T(8,128)(2,1)}, bf16[1024,512]{1,0:T(8,128)(2,1)S(1)}, u32[]{:S(2)}, u32[]{:S(2)}) collective-permute-start(bf16[1024,512]{1,0:T(8,128)(2,1)} %collective-permute-done.3.refs_3_), channel_id=1, source_target_pairs={{0,3},{1,0},{2,1},{3,2},{4,7},{5,4},{6,5},{7,6},{8,11},{9,8},{10,9... | collective-permute-start | bytes 3145736 | tf_op jit(solution)/shard_map/ppermute | solution.py:36
  44.7 1.3 constant_dynamic-update-slice_fusion.3
  46.1 1.3 constant_dynamic-update-slice_fusion.2.refs_4_.refs_2_
  47.4 1.3 copy-done
  48.7 9.7 %project.3.refs_3_ = bf16[2,8,256,1024]{3,2,1,0:T(8,128)(2,1)} custom-call(s32[4]{0:T(128)S(1)} %pad_add_fusion.3.meta_ref, bf16[1024,512]{1,0:T(8,128)(2,1)} %copy-done.8, bf16[1024,512]{1,0:T(8,128)(2,1)} %collective-permute-done.1.refs_1_, bf16[1024,512]{1,0:T(8,128)(2,1)} %collective-permute-done.2.refs_2_, ...), custom_call_target="tpu_custom_call" | custom-call | flops 4294967296 | bytes 10485760 | tf_op jit(solution)/shard_map/project/pallas_call | solution.py:226
  58.4 6.8 %collective-permute-done.11.refs_11_ = bf16[512,1024]{1,0:T(8,128)(2,1)} collective-permute-done((bf16[512,1024]{1,0:T(8,128)(2,1)}, bf16[512,1024]{1,0:T(8,128)(2,1)}, u32[]{:S(2)}, u32[]{:S(2)}) %collective-permute-start.11) | collective-permute-done | bytes 1048608 | tf_op jit(solution)/shard_map/ppermute | solution.py:28
  65.2 2.3 %collective-permute-done.10.refs_15_ = bf16[512,1024]{1,0:T(8,128)(2,1)} collective-permute-done((bf16[512,1024]{1,0:T(8,128)(2,1)}, bf16[512,1024]{1,0:T(8,128)(2,1)}, u32[]{:S(2)}, u32[]{:S(2)}) %collective-permute-start.10) | collective-permute-done | bytes 1048608 | tf_op jit(solution)/shard_map/ppermute | solution.py:28
  67.5 0.1 collective-permute-done.8.refs_0_.refs_4_
  67.7 2.2 %collective-permute-start.13 = (bf16[1024,512]{1,0:T(8,128)(2,1)S(1)}, bf16[1024,512]{1,0:T(8,128)(2,1)}, u32[]{:S(2)}, u32[]{:S(2)}) collective-permute-start(bf16[1024,512]{1,0:T(8,128)(2,1)S(1)} %collective-permute-done.9.refs_1_.refs_5_), channel_id=1, source_target_pairs={{0,3},{1,0},{2,1},{3,2},{4,7},{5,4},{6,5},{7,6},{8,11},{9,8},{10,9... | collective-permute-start | bytes 3145736 | tf_op jit(solution)/shard_map/ppermute | solution.py:36
  69.9 1.3 collective-permute-start.14
  71.2 1.3 collective-permute-start.15
  72.6 1.3 collective-permute-start.16
  74.1 6.4 %project.4.refs_3_ = bf16[2,8,256,1024]{3,2,1,0:T(8,128)(2,1)} custom-call(s32[2]{0:T(128)S(1)} %pad_add_fusion.4.meta_ref, bf16[1024,512]{1,0:T(8,128)(2,1)} %copy-done.1, bf16[1024,512]{1,0:T(8,128)(2,1)} %copy-done.2, bf16[1024,1024]{1,0:T(8,128)(2,1)} %copy-done, bf16[2,8,256,1024]{3,2,1,0:T(8,128)(2,1)} %project.3.refs_3_), custom_call_target="tpu_custom_call", output_to_operand_aliasing={{}: (4, {})} | custom-call | flops 2147483648 | bytes 6291456 | tf_op jit(solution)/shard_map/project/pallas_call | solution.py:226
  80.5 9.7 %collective-permute-done.7.refs_0_.refs_6_ = bf16[1024,512]{1,0:T(8,128)(2,1)} collective-permute-done((bf16[1024,512]{1,0:T(8,128)(2,1)}, bf16[1024,512]{1,0:T(8,128)(2,1)}, u32[]{:S(2)}, u32[]{:S(2)}) %collective-permute-start.7) | collective-permute-done | bytes 1048608 | tf_op jit(solution)/shard_map/ppermute | solution.py:36
  90.1 0.5 collective-permute-done.13.refs_1_.refs_7_
  90.6 3.4 %collective-permute-done.14.refs_12_ = bf16[512,1024]{1,0:T(8,128)(2,1)} collective-permute-done((bf16[512,1024]{1,0:T(8,128)(2,1)}, bf16[512,1024]{1,0:T(8,128)(2,1)}, u32[]{:S(2)}, u32[]{:S(2)}) %collective-permute-start.14) | collective-permute-done | bytes 1048608 | tf_op jit(solution)/shard_map/ppermute | solution.py:28
  94.1 2.4 %collective-permute-done.16.refs_14_ = bf16[512,1024]{1,0:T(8,128)(2,1)} collective-permute-done((bf16[512,1024]{1,0:T(8,128)(2,1)}, bf16[512,1024]{1,0:T(8,128)(2,1)}, u32[]{:S(2)}, u32[]{:S(2)}) %collective-permute-start.16) | collective-permute-done | bytes 1048608 | tf_op jit(solution)/shard_map/ppermute | solution.py:28
  96.5 6.4 %project.5.buffer_ref = bf16[2,8,256,1024]{3,2,1,0:T(8,128)(2,1)} custom-call(s32[2]{0:T(128)S(1)} %pad_add_fusion.2.meta_ref, bf16[1024,512]{1,0:T(8,128)(2,1)} %collective-permute-done.7.refs_0_.refs_6_, bf16[1024,512]{1,0:T(8,128)(2,1)} %collective-permute-done.13.refs_1_.refs_7_, bf16[1024,1024]{1,0:T(8,128)(2,1)} %copy-done, ...), custom_call_target="tpu_custom_call", output_to_operand_aliasing={{}: (4, {})} | custom-call | flops 2147483648 | bytes 6291456 | tf_op jit(solution)/shard_map/project/pallas_call | solution.py:226
  102.9 4.2 %add_blocks.4 = (bf16[2,256,1024]{2,1,0:T(8,128)(2,1)}, bf16[2,256,1024]{2,1,0:T(8,128)(2,1)}, bf16[2,256,1024]{2,1,0:T(8,128)(2,1)}) custom-call(s32[3]{0:T(128)S(1)} %pad_add_fusion.5.meta_ref, bf16[2,8,256,1024]{3,2,1,0:T(8,128)(2,1)} %project.5.buffer_ref), custom_call_target="tpu_custom_call" | custom-call | flops 2097152 | bytes 5242880 | tf_op jit(solution)/shard_map/add_blocks/pallas_call | solution.py:366
  107.0 0.2 collective-permute-start.17
  107.2 2.6 %collective-permute-start.18 = (bf16[2,256,1024]{2,1,0:T(8,128)(2,1)}, bf16[2,256,1024]{2,1,0:T(8,128)(2,1)S(1)}, u32[]{:S(2)}, u32[]{:S(2)}) collective-permute-start(bf16[2,256,1024]{2,1,0:T(8,128)(2,1)} %get-tuple-element.64), channel_id=1, source_target_pairs={{0,96},{8,104},{16,112},{24,120},{32,0},{40,8},{48,16},{56,24},{64... | collective-permute-start | bytes 3145736 | tf_op jit(solution)/shard_map/ppermute | solution.py:28
  109.8 1.3 collective-permute-start.19
  111.2 16.6 %attn_grad.1 = (f32[512,1024]{1,0:T(8,128)}, bf16[512,1024]{1,0:T(8,128)(2,1)}) custom-call(s32[16]{0:T(128)S(1)} %stack.113.meta_ref, bf16[1024,512]{1,0:T(8,128)(2,1)} %copy-done.8, bf16[1024,512]{1,0:T(8,128)(2,1)} %collective-permute-done.1.refs_1_, bf16[1024,512]{1,0:T(8,128)(2,1)} %collective-permute-done.2.refs_2_, ...), custom_call_target="tpu_custom_call" | custom-call | flops 8589934592 | bytes 20971520 | tf_op jit(solution)/shard_map/attn_grad/pallas_call | solution.py:311
  127.7 2.1 %collective-permute-done.17.refs_0_ = bf16[2,256,1024]{2,1,0:T(8,128)(2,1)S(1)} collective-permute-done((bf16[2,256,1024]{2,1,0:T(8,128)(2,1)}, bf16[2,256,1024]{2,1,0:T(8,128)(2,1)S(1)}, u32[]{:S(2)}, u32[]{:S(2)}) %collective-permute-start.17) | collective-permute-done | bytes 1048608 | tf_op jit(solution)/shard_map/ppermute | solution.py:28
  129.8 2.4 %collective-permute-done.19.refs_2_ = bf16[2,256,1024]{2,1,0:T(8,128)(2,1)} collective-permute-done((bf16[2,256,1024]{2,1,0:T(8,128)(2,1)}, bf16[2,256,1024]{2,1,0:T(8,128)(2,1)}, u32[]{:S(2)}, u32[]{:S(2)}) %collective-permute-start.19) | collective-permute-done | bytes 1048608 | tf_op jit(solution)/shard_map/ppermute | solution.py:28
  132.2 5.0 %collective-permute-start.22 = (bf16[512,1024]{1,0:T(8,128)(2,1)}, bf16[512,1024]{1,0:T(8,128)(2,1)}, u32[]{:S(2)}, u32[]{:S(2)}) collective-permute-start(bf16[512,1024]{1,0:T(8,128)(2,1)} %get-tuple-element.79), channel_id=1, source_target_pairs={{0,8},{8,0},{16,24},{24,16},{32,40},{40,32},{48,56},{56,48},{64,72... | collective-permute-start | bytes 3145736 | tf_op jit(solution)/shard_map/ppermute | solution.py:28
  137.3 5.5 %add_blocks.5 = (bf16[2,256,1024]{2,1,0:T(8,128)(2,1)}, bf16[1,256,1024]{2,1,0:T(8,128)(2,1)S(1)}, bf16[1,256,1024]{2,1,0:T(8,128)(2,1)}) custom-call(s32[2]{0:T(128)S(1)} %pad_add_fusion.1.meta_ref, bf16[2,8,256,1024]{3,2,1,0:T(8,128)(2,1)} %project.5.buffer_ref, bf16[2,256,1024]{2,1,0:T(8,128)(2,1)} %copy-done.3, bf16[2,256,1024]{2,1,0:T(8,128)(2,1)} %copy-done.4, ...), custom_call_target="tpu_custom_call" | custom-call | flops 2097152 | bytes 5242880 | tf_op jit(solution)/shard_map/add_blocks/pallas_call | solution.py:366
  142.9 2.7 %collective-permute-start.21 = (bf16[1,256,1024]{2,1,0:T(8,128)(2,1)}, bf16[1,256,1024]{2,1,0:T(8,128)(2,1)S(1)}, u32[]{:S(2)}, u32[]{:S(2)}) collective-permute-start(bf16[1,256,1024]{2,1,0:T(8,128)(2,1)} %get-tuple-element.77), channel_id=1, source_target_pairs={{0,96},{8,104},{16,112},{24,120},{32,0},{40,8},{48,16},{56,24},{64... | collective-permute-start | bytes 1572872 | tf_op jit(solution)/shard_map/ppermute | solution.py:28
  145.6 0.1 copy.16.kt_ref
  145.8 1.4 collective-permute-start.26
  147.1 3.2 %add_convert_fusion.g_ref = bf16[512,1024]{1,0:T(8,128)(2,1)} fusion(f32[512,1024]{1,0:T(8,128)} %get-tuple-element.78, bf16[512,1024]{1,0:T(8,128)(2,1)} %collective-permute-done.22), kind=kLoop, calls=%fused_computation | loop fusion | flops 1572864 | bytes 4194304 | tf_op jit(solution)/shard_map/convert_element_type | solution.py:495
  150.3 7.3 %collective-permute-done.20.refs_0_ = bf16[1,256,1024]{2,1,0:T(8,128)(2,1)S(1)} collective-permute-done((bf16[1,256,1024]{2,1,0:T(8,128)(2,1)S(1)}, bf16[1,256,1024]{2,1,0:T(8,128)(2,1)S(1)}, u32[]{:S(2)}, u32[]{:S(2)}) %collective-permute-start.20) | collective-permute-done | bytes 524320 | tf_op jit(solution)/shard_map/ppermute | solution.py:28
  157.6 0.8 copy-done.9
  158.4 4.7 %add_blocks.6 = (bf16[2,256,1024]{2,1,0:T(8,128)(2,1)}, bf16[2,256,1024]{2,1,0:T(8,128)(2,1)}) custom-call(s32[2]{0:T(128)S(1)} %pad_add_fusion.6.meta_ref, bf16[2,8,256,1024]{3,2,1,0:T(8,128)(2,1)} %project.5.buffer_ref, bf16[1,256,1024]{2,1,0:T(8,128)(2,1)S(1)} %collective-permute-done.20.refs_0_, bf16[1,256,1024]{2,1,0:T(8,128)(2,1)} %copy-done.9), custom_call_target="tpu_custom_call" | custom-call | flops 2097152 | bytes 5242880 | tf_op jit(solution)/shard_map/add_blocks/pallas_call | solution.py:366
  163.2 2.9 %collective-permute-start.25 = (bf16[2,256,1024]{2,1,0:T(8,128)(2,1)}, bf16[2,256,1024]{2,1,0:T(8,128)(2,1)S(1)}, u32[]{:S(2)}, u32[]{:S(2)}) collective-permute-start(bf16[2,256,1024]{2,1,0:T(8,128)(2,1)} %get-tuple-element.90), channel_id=1, source_target_pairs={{0,96},{8,104},{16,112},{24,120},{32,0},{40,8},{48,16},{56,24},{64... | collective-permute-start | bytes 3145736 | tf_op jit(solution)/shard_map/ppermute | solution.py:28
  166.0 18.1 %attend_back.1 = (bf16[512,1024]{1,0:T(8,128)(2,1)}, f32[1024,128]{1,0:T(8,128)}, f32[1024,128]{1,0:T(8,128)}) custom-call(s32[1]{0:T(128)} %bitcast.meta_ref, bf16[512,1024]{1,0:T(8,128)(2,1)} %q_ref.2, bf16[512,1024]{1,0:T(8,128)(2,1)} %add_convert_fusion.g_ref, bf16[1024,128]{1,0:T(8,128)(2,1)S(1)} %get-tuple-element.97.k_ref, ...), custom_call_target="tpu_custom_call" | custom-call | flops 10737418240 | bytes 12582912 | tf_op jit(solution)/shard_map/attend_back/pallas_call | solution.py:168
  184.1 1.0 slice.56
  185.1 1.0 slice.57
  186.1 3.3 %collective-permute-start.23 = (bf16[512,256]{1,0:T(8,128)(2,1)S(1)}, bf16[512,256]{1,0:T(8,128)(2,1)S(1)}, u32[]{:S(2)}, u32[]{:S(2)}) collective-permute-start(bf16[512,256]{1,0:T(8,128)(2,1)S(1)} %pad_maximum_fusion.2), channel_id=1, source_target_pairs={{8,0},{16,8},{24,16},{32,24},{40,32},{48,40},{56,48},{64,56},{72,6... | collective-permute-start | bytes 786440 | tf_op jit(solution)/shard_map/ppermute | solution.py:42
  189.4 5.9 %collective-permute-done.23 = bf16[512,256]{1,0:T(8,128)(2,1)S(1)} collective-permute-done((bf16[512,256]{1,0:T(8,128)(2,1)S(1)}, bf16[512,256]{1,0:T(8,128)(2,1)S(1)}, u32[]{:S(2)}, u32[]{:S(2)}) %collective-permute-start.23) | collective-permute-done | bytes 262176 | tf_op jit(solution)/shard_map/ppermute | solution.py:42
  195.3 1.8 fusion.1
  197.1 1.0 copy-done.5
  198.1 0.3 copy-done.6
  198.4 1.0 copy-done.7
  199.4 4.6 %add_blocks.7 = bf16[2,256,1024]{2,1,0:T(8,128)(2,1)} custom-call(s32[1]{0:T(128)} %bitcast.17.meta_ref, bf16[2,8,256,1024]{3,2,1,0:T(8,128)(2,1)} %project.5.buffer_ref, bf16[2,256,1024]{2,1,0:T(8,128)(2,1)} %copy-done.6, bf16[2,256,1024]{2,1,0:T(8,128)(2,1)} %copy-done.7, bf16[2,256,1024]{2,1,0:T(8,128)(2,1)} %copy-done.5), custom_call_target="tpu_custom_call" | custom-call | flops 2097152 | bytes 5242880 | tf_op jit(solution)/shard_map/add_blocks/pallas_call | solution.py:366
  (49 shorter events, 1.1 us)
Async XLA Ops:
  0.6 2.9 %copy-start.10 = (bf16[512,128]{1,0:T(8,128)(2,1)S(1)}, bf16[512,128]{1,0:T(8,128)(2,1)}, u32[]{:S(2)}) copy-start(bf16[512,128]{1,0:T(8,128)(2,1)} %param.7) | copy-start | bytes 393220
  0.6 2.9 %copy-start.11 = (bf16[512,128]{1,0:T(8,128)(2,1)S(1)}, bf16[512,128]{1,0:T(8,128)(2,1)}, u32[]{:S(2)}) copy-start(bf16[512,128]{1,0:T(8,128)(2,1)} %param.8) | copy-start | bytes 393220
  2.0 10.3 %collective-permute-start = (bf16[512,512]{1,0:T(8,128)(2,1)S(1)}, bf16[512,512]{1,0:T(8,128)(2,1)S(1)}, u32[]{:S(2)}, u32[]{:S(2)}) collective-permute-start(bf16[512,512]{1,0:T(8,128)(2,1)S(1)} %get-tuple-element.93), channel_id=1, source_target_pairs={{0,8},{8,0},{16,24},{24,16},{32,40},{40,32},{48,56},{56,48},{64,72... | collective-permute-start | bytes 1572872 | tf_op jit(solution)/shard_map/ppermute | solution.py:28
  3.6 11.6 %collective-permute-start.6 = (bf16[512,256]{1,0:T(8,128)(2,1)S(1)}, bf16[512,256]{1,0:T(8,128)(2,1)S(1)}, u32[]{:S(2)}, u32[]{:S(2)}) collective-permute-start(bf16[512,256]{1,0:T(8,128)(2,1)S(1)} %constant_dynamic-update-slice_fusion), channel_id=1, source_target_pairs={{0,8},{8,16},{16,24},{24,32},{32,40},{40,48},{48,56},{56,64},{64,7... | collective-permute-start | bytes 786440 | tf_op jit(solution)/shard_map/ppermute | solution.py:42
  8.4 26.0 %collective-permute-start.4 = (bf16[512,1024]{1,0:T(8,128)(2,1)}, bf16[512,1024]{1,0:T(8,128)(2,1)}, u32[]{:S(2)}, u32[]{:S(2)}) collective-permute-start(bf16[512,1024]{1,0:T(8,128)(2,1)} %refs_8_.1), channel_id=1, source_target_pairs={{0,32},{8,40},{16,48},{24,56},{32,64},{40,72},{48,80},{56,88},{64,... | collective-permute-start | bytes 3145736 | tf_op jit(solution)/shard_map/ppermute | solution.py:28
  10.1 24.3 %collective-permute-start.5 = (bf16[512,1024]{1,0:T(8,128)(2,1)}, bf16[512,1024]{1,0:T(8,128)(2,1)}, u32[]{:S(2)}, u32[]{:S(2)}) collective-permute-start(bf16[512,1024]{1,0:T(8,128)(2,1)} %refs_8_.1), channel_id=1, source_target_pairs={{0,96},{8,104},{16,112},{24,120},{32,0},{40,8},{48,16},{56,24},{64... | collective-permute-start | bytes 3145736 | tf_op jit(solution)/shard_map/ppermute | solution.py:28
  12.4 21.1 %copy-start.8 = (bf16[1024,512]{1,0:T(8,128)(2,1)}, bf16[1024,512]{1,0:T(8,128)(2,1)S(1)}, u32[]{:S(2)}) copy-start(bf16[1024,512]{1,0:T(8,128)(2,1)S(1)} %pad_maximum_fusion.refs_0_) | copy-start | bytes 3145732
  12.4 24.7 %collective-permute-start.1 = (bf16[1024,512]{1,0:T(8,128)(2,1)S(1)}, bf16[1024,512]{1,0:T(8,128)(2,1)}, u32[]{:S(2)}, u32[]{:S(2)}) collective-permute-start(bf16[1024,512]{1,0:T(8,128)(2,1)S(1)} %pad_maximum_fusion.refs_0_), channel_id=1, source_target_pairs={{0,1},{1,2},{2,3},{3,0},{4,5},{5,6},{6,7},{7,4},{8,9},{9,10},{10,1... | collective-permute-start | bytes 3145736 | tf_op jit(solution)/shard_map/ppermute | solution.py:36
  13.7 24.0 %collective-permute-start.2 = (bf16[1024,512]{1,0:T(8,128)(2,1)S(1)}, bf16[1024,512]{1,0:T(8,128)(2,1)}, u32[]{:S(2)}, u32[]{:S(2)}) collective-permute-start(bf16[1024,512]{1,0:T(8,128)(2,1)S(1)} %pad_maximum_fusion.refs_0_), channel_id=1, source_target_pairs={{0,3},{1,0},{2,1},{3,2},{4,7},{5,4},{6,5},{7,6},{8,11},{9,8},{10,9... | collective-permute-start | bytes 3145736 | tf_op jit(solution)/shard_map/ppermute | solution.py:36
  15.2 24.0 %collective-permute-start.3 = (bf16[1024,512]{1,0:T(8,128)(2,1)S(1)}, bf16[1024,512]{1,0:T(8,128)(2,1)}, u32[]{:S(2)}, u32[]{:S(2)}) collective-permute-start(bf16[1024,512]{1,0:T(8,128)(2,1)S(1)} %pad_maximum_fusion.refs_0_), channel_id=1, source_target_pairs={{0,4},{1,5},{2,6},{3,7},{4,0},{5,1},{6,2},{7,3},{8,12},{9,13},{10,... | collective-permute-start | bytes 3145736 | tf_op jit(solution)/shard_map/ppermute | solution.py:36
  39.2 6.9 %collective-permute-start.12 = (bf16[512,1024]{1,0:T(8,128)(2,1)}, bf16[512,1024]{1,0:T(8,128)(2,1)}, u32[]{:S(2)}, u32[]{:S(2)}) collective-permute-start(bf16[512,1024]{1,0:T(8,128)(2,1)} %get-tuple-element.54), channel_id=1, source_target_pairs={{0,8},{8,0},{16,24},{24,16},{32,40},{40,32},{48,56},{56,48},{64,72... | collective-permute-start | bytes 3145736 | tf_op jit(solution)/shard_map/ppermute | solution.py:28
  39.2 26.0 %collective-permute-start.11 = (bf16[512,1024]{1,0:T(8,128)(2,1)}, bf16[512,1024]{1,0:T(8,128)(2,1)}, u32[]{:S(2)}, u32[]{:S(2)}) collective-permute-start(bf16[512,1024]{1,0:T(8,128)(2,1)} %refs_8_.1), channel_id=1, source_target_pairs={{0,16},{8,24},{16,0},{24,8},{32,48},{40,56},{48,32},{56,40},{64,80... | collective-permute-start | bytes 3145736 | tf_op jit(solution)/shard_map/ppermute | solution.py:28
  41.5 26.0 %collective-permute-start.10 = (bf16[512,1024]{1,0:T(8,128)(2,1)}, bf16[512,1024]{1,0:T(8,128)(2,1)}, u32[]{:S(2)}, u32[]{:S(2)}) collective-permute-start(bf16[512,1024]{1,0:T(8,128)(2,1)} %collective-permute-done.4.refs_9_), channel_id=1, source_target_pairs={{0,32},{8,40},{16,48},{24,56},{32,64},{40,72},{48,80},{56,88},{64,... | collective-permute-start | bytes 3145736 | tf_op jit(solution)/shard_map/ppermute | solution.py:28
  42.0 25.7 %collective-permute-start.8 = (bf16[1024,512]{1,0:T(8,128)(2,1)}, bf16[1024,512]{1,0:T(8,128)(2,1)S(1)}, u32[]{:S(2)}, u32[]{:S(2)}) collective-permute-start(bf16[1024,512]{1,0:T(8,128)(2,1)} %collective-permute-done.3.refs_3_), channel_id=1, source_target_pairs={{0,1},{1,2},{2,3},{3,0},{4,5},{5,6},{6,7},{7,4},{8,9},{9,10},{10,1... | collective-permute-start | bytes 3145736 | tf_op jit(solution)/shard_map/ppermute | solution.py:36
  42.1 25.6 %collective-permute-start.9 = (bf16[1024,512]{1,0:T(8,128)(2,1)}, bf16[1024,512]{1,0:T(8,128)(2,1)S(1)}, u32[]{:S(2)}, u32[]{:S(2)}) collective-permute-start(bf16[1024,512]{1,0:T(8,128)(2,1)} %collective-permute-done.3.refs_3_), channel_id=1, source_target_pairs={{0,3},{1,0},{2,1},{3,2},{4,7},{5,4},{6,5},{7,6},{8,11},{9,8},{10,9... | collective-permute-start | bytes 3145736 | tf_op jit(solution)/shard_map/ppermute | solution.py:36
  46.0 44.1 %collective-permute-start.7 = (bf16[1024,512]{1,0:T(8,128)(2,1)}, bf16[1024,512]{1,0:T(8,128)(2,1)}, u32[]{:S(2)}, u32[]{:S(2)}) collective-permute-start(bf16[1024,512]{1,0:T(8,128)(2,1)} %collective-permute-done.1.refs_1_), channel_id=1, source_target_pairs={{0,1},{1,2},{2,3},{3,0},{4,5},{5,6},{6,7},{7,4},{8,9},{9,10},{10,1... | collective-permute-start | bytes 3145736 | tf_op jit(solution)/shard_map/ppermute | solution.py:36
  47.4 1.3 copy-start
  67.6 6.5 %copy-start.1 = (bf16[1024,512]{1,0:T(8,128)(2,1)}, bf16[1024,512]{1,0:T(8,128)(2,1)S(1)}, u32[]{:S(2)}) copy-start(bf16[1024,512]{1,0:T(8,128)(2,1)S(1)} %collective-permute-done.8.refs_0_.refs_4_) | copy-start | bytes 3145732
  67.7 6.5 %copy-start.2 = (bf16[1024,512]{1,0:T(8,128)(2,1)}, bf16[1024,512]{1,0:T(8,128)(2,1)S(1)}, u32[]{:S(2)}) copy-start(bf16[1024,512]{1,0:T(8,128)(2,1)S(1)} %collective-permute-done.9.refs_1_.refs_5_) | copy-start | bytes 3145732
  67.7 23.0 %collective-permute-start.13 = (bf16[1024,512]{1,0:T(8,128)(2,1)S(1)}, bf16[1024,512]{1,0:T(8,128)(2,1)}, u32[]{:S(2)}, u32[]{:S(2)}) collective-permute-start(bf16[1024,512]{1,0:T(8,128)(2,1)S(1)} %collective-permute-done.9.refs_1_.refs_5_), channel_id=1, source_target_pairs={{0,3},{1,0},{2,1},{3,2},{4,7},{5,4},{6,5},{7,6},{8,11},{9,8},{10,9... | collective-permute-start | bytes 3145736 | tf_op jit(solution)/shard_map/ppermute | solution.py:36
  69.9 24.2 %collective-permute-start.14 = (bf16[512,1024]{1,0:T(8,128)(2,1)}, bf16[512,1024]{1,0:T(8,128)(2,1)}, u32[]{:S(2)}, u32[]{:S(2)}) collective-permute-start(bf16[512,1024]{1,0:T(8,128)(2,1)} %collective-permute-done.11.refs_11_), channel_id=1, source_target_pairs={{0,32},{8,40},{16,48},{24,56},{32,64},{40,72},{48,80},{56,88},{64,... | collective-permute-start | bytes 3145736 | tf_op jit(solution)/shard_map/ppermute | solution.py:28
  71.2 22.8 %collective-permute-start.15 = (bf16[512,1024]{1,0:T(8,128)(2,1)}, bf16[512,1024]{1,0:T(8,128)(2,1)}, u32[]{:S(2)}, u32[]{:S(2)}) collective-permute-start(bf16[512,1024]{1,0:T(8,128)(2,1)} %collective-permute-done.11.refs_11_), channel_id=1, source_target_pairs={{0,96},{8,104},{16,112},{24,120},{32,0},{40,8},{48,16},{56,24},{64... | collective-permute-start | bytes 3145736 | tf_op jit(solution)/shard_map/ppermute | solution.py:28
  72.6 23.9 %collective-permute-start.16 = (bf16[512,1024]{1,0:T(8,128)(2,1)}, bf16[512,1024]{1,0:T(8,128)(2,1)}, u32[]{:S(2)}, u32[]{:S(2)}) collective-permute-start(bf16[512,1024]{1,0:T(8,128)(2,1)} %collective-permute-done.10.refs_15_), channel_id=1, source_target_pairs={{0,16},{8,24},{16,0},{24,8},{32,48},{40,56},{48,32},{56,40},{64,80... | collective-permute-start | bytes 3145736 | tf_op jit(solution)/shard_map/ppermute | solution.py:28
  107.0 22.8 %collective-permute-start.17 = (bf16[2,256,1024]{2,1,0:T(8,128)(2,1)}, bf16[2,256,1024]{2,1,0:T(8,128)(2,1)S(1)}, u32[]{:S(2)}, u32[]{:S(2)}) collective-permute-start(bf16[2,256,1024]{2,1,0:T(8,128)(2,1)} %get-tuple-element.63), channel_id=1, source_target_pairs={{0,32},{8,40},{16,48},{24,56},{32,64},{40,72},{48,80},{56,88},{64,... | collective-permute-start | bytes 3145736 | tf_op jit(solution)/shard_map/ppermute | solution.py:28
  107.2 22.6 %collective-permute-start.18 = (bf16[2,256,1024]{2,1,0:T(8,128)(2,1)}, bf16[2,256,1024]{2,1,0:T(8,128)(2,1)S(1)}, u32[]{:S(2)}, u32[]{:S(2)}) collective-permute-start(bf16[2,256,1024]{2,1,0:T(8,128)(2,1)} %get-tuple-element.64), channel_id=1, source_target_pairs={{0,96},{8,104},{16,112},{24,120},{32,0},{40,8},{48,16},{56,24},{64... | collective-permute-start | bytes 3145736 | tf_op jit(solution)/shard_map/ppermute | solution.py:28
  109.8 22.4 %collective-permute-start.19 = (bf16[2,256,1024]{2,1,0:T(8,128)(2,1)}, bf16[2,256,1024]{2,1,0:T(8,128)(2,1)}, u32[]{:S(2)}, u32[]{:S(2)}) collective-permute-start(bf16[2,256,1024]{2,1,0:T(8,128)(2,1)} %get-tuple-element.65), channel_id=1, source_target_pairs={{0,16},{8,24},{16,0},{24,8},{32,48},{40,56},{48,32},{56,40},{64,80... | collective-permute-start | bytes 3145736 | tf_op jit(solution)/shard_map/ppermute | solution.py:28
  129.8 7.5 %copy-start.3 = (bf16[2,256,1024]{2,1,0:T(8,128)(2,1)}, bf16[2,256,1024]{2,1,0:T(8,128)(2,1)S(1)}, u32[]{:S(2)}) copy-start(bf16[2,256,1024]{2,1,0:T(8,128)(2,1)S(1)} %collective-permute-done.17.refs_0_) | copy-start | bytes 3145732
  129.8 7.4 %copy-start.4 = (bf16[2,256,1024]{2,1,0:T(8,128)(2,1)}, bf16[2,256,1024]{2,1,0:T(8,128)(2,1)S(1)}, u32[]{:S(2)}) copy-start(bf16[2,256,1024]{2,1,0:T(8,128)(2,1)S(1)} %collective-permute-done.18.refs_1_) | copy-start | bytes 3145732
  132.2 14.9 %collective-permute-start.22 = (bf16[512,1024]{1,0:T(8,128)(2,1)}, bf16[512,1024]{1,0:T(8,128)(2,1)}, u32[]{:S(2)}, u32[]{:S(2)}) collective-permute-start(bf16[512,1024]{1,0:T(8,128)(2,1)} %get-tuple-element.79), channel_id=1, source_target_pairs={{0,8},{8,0},{16,24},{24,16},{32,40},{40,32},{48,56},{56,48},{64,72... | collective-permute-start | bytes 3145736 | tf_op jit(solution)/shard_map/ppermute | solution.py:28
  142.8 14.8 %collective-permute-start.20 = (bf16[1,256,1024]{2,1,0:T(8,128)(2,1)S(1)}, bf16[1,256,1024]{2,1,0:T(8,128)(2,1)S(1)}, u32[]{:S(2)}, u32[]{:S(2)}) collective-permute-start(bf16[1,256,1024]{2,1,0:T(8,128)(2,1)S(1)} %get-tuple-element.76), channel_id=1, source_target_pairs={{0,32},{8,40},{16,48},{24,56},{32,64},{40,72},{48,80},{56,88},{64,... | collective-permute-start | bytes 1572872 | tf_op jit(solution)/shard_map/ppermute | solution.py:28
  142.9 14.8 %collective-permute-start.21 = (bf16[1,256,1024]{2,1,0:T(8,128)(2,1)}, bf16[1,256,1024]{2,1,0:T(8,128)(2,1)S(1)}, u32[]{:S(2)}, u32[]{:S(2)}) collective-permute-start(bf16[1,256,1024]{2,1,0:T(8,128)(2,1)} %get-tuple-element.77), channel_id=1, source_target_pairs={{0,96},{8,104},{16,112},{24,120},{32,0},{40,8},{48,16},{56,24},{64... | collective-permute-start | bytes 1572872 | tf_op jit(solution)/shard_map/ppermute | solution.py:28
  145.8 51.4 %collective-permute-start.26 = (bf16[2,256,1024]{2,1,0:T(8,128)(2,1)}, bf16[2,256,1024]{2,1,0:T(8,128)(2,1)S(1)}, u32[]{:S(2)}, u32[]{:S(2)}) collective-permute-start(bf16[2,256,1024]{2,1,0:T(8,128)(2,1)} %get-tuple-element.91), channel_id=1, source_target_pairs={{0,16},{8,24},{16,0},{24,8},{32,48},{40,56},{48,32},{56,40},{64,80... | collective-permute-start | bytes 3145736 | tf_op jit(solution)/shard_map/ppermute | solution.py:28
  157.6 0.8 copy-start.9
  163.1 34.0 %collective-permute-start.24 = (bf16[2,256,1024]{2,1,0:T(8,128)(2,1)}, bf16[2,256,1024]{2,1,0:T(8,128)(2,1)S(1)}, u32[]{:S(2)}, u32[]{:S(2)}) collective-permute-start(bf16[2,256,1024]{2,1,0:T(8,128)(2,1)} %get-tuple-element.83), channel_id=1, source_target_pairs={{0,32},{8,40},{16,48},{24,56},{32,64},{40,72},{48,80},{56,88},{64,... | collective-permute-start | bytes 3145736 | tf_op jit(solution)/shard_map/ppermute | solution.py:28
  163.2 34.0 %collective-permute-start.25 = (bf16[2,256,1024]{2,1,0:T(8,128)(2,1)}, bf16[2,256,1024]{2,1,0:T(8,128)(2,1)S(1)}, u32[]{:S(2)}, u32[]{:S(2)}) collective-permute-start(bf16[2,256,1024]{2,1,0:T(8,128)(2,1)} %get-tuple-element.90), channel_id=1, source_target_pairs={{0,96},{8,104},{16,112},{24,120},{32,0},{40,8},{48,16},{56,24},{64... | collective-permute-start | bytes 3145736 | tf_op jit(solution)/shard_map/ppermute | solution.py:28
  186.1 9.2 %collective-permute-start.23 = (bf16[512,256]{1,0:T(8,128)(2,1)S(1)}, bf16[512,256]{1,0:T(8,128)(2,1)S(1)}, u32[]{:S(2)}, u32[]{:S(2)}) collective-permute-start(bf16[512,256]{1,0:T(8,128)(2,1)S(1)} %pad_maximum_fusion.2), channel_id=1, source_target_pairs={{8,0},{16,8},{24,16},{32,24},{40,32},{48,40},{56,48},{64,56},{72,6... | collective-permute-start | bytes 786440 | tf_op jit(solution)/shard_map/ppermute | solution.py:42
  197.1 1.0 copy-start.5
  197.1 1.3 copy-start.6
  198.4 1.0 copy-start.7

commit v4 on v3

--- a/solution.py
+++ b/solution.py
@@ -112,7 +112,7 @@
             jax.ShapeDtypeStruct((heads, 1, count), F32),
             jax.ShapeDtypeStruct((heads, 1, count), F32),
         ],
-        compiler_params=params(53),
+        compiler_params=params(16),
         cost_estimate=pl.CostEstimate(
             flops=heads * 4 * 2 * 2 * count * count * HD,
             bytes_accessed=8 * 2**20,
@@ -189,7 +189,7 @@
             jax.ShapeDtypeStruct((2 * count, HD), F32),
             jax.ShapeDtypeStruct((2 * count, HD), F32),
         ],
-        compiler_params=params(53),
+        compiler_params=params(22),
         cost_estimate=pl.CostEstimate(
             flops=heads * 10 * 2 * 2 * count * count * HD,
             bytes_accessed=12 * 2**20,
@@ -201,9 +201,14 @@
 
 def proj_kernel(n_in, held, meta_ref, *refs):
     pieces, a_ref = refs[:n_in], refs[n_in]
-    out_ref = refs[n_in + 1 + held]
+    refs = refs[n_in + 1 + held:]
+    buffer_ref, taken = refs[0], refs[1:-3]
+    done, sems, take_sems = refs[-3:]
     step = pl.program_id(0)
-    rows = out_ref.shape[2]
+    rows = done.shape[2]
+
+    def put(j):
+        return pltpu.make_async_copy(done.at[j], buffer_ref.at[:, meta_ref[j]], sems.at[j])
 
     for j in range(n_in):
 
@@ -212,30 +217,50 @@
             value = lax.dot_general(
                 pieces[j][...], a_ref[...], (((0,), (0,)), ((), ())), preferred_element_type=F32
             ).astype(BF)
-            out_ref[0, 0] = value[:rows]
-            out_ref[1, 0] = value[rows:]
-
-
-def project(pieces, a_pair, blocks, buffer):
+            done[j, 0] = value[:rows]
+            done[j, 1] = value[rows:]
+            put(j).start()
+
+    @pl.when(step == n_in - 1)
+    def _():
+        for j in range(n_in):
+            put(j).wait()
+        takes = [
+            pltpu.make_async_copy(buffer_ref.at[:, meta_ref[n_in + i]], ref, take_sems.at[i])
+            for i, ref in enumerate(taken)
+        ]
+        for take in takes:
+            take.start()
+        for take in takes:
+            take.wait()
+
+
+def project(pieces, a_pair, blocks, buffer, n_taken=0):
     tokens, width = a_pair.shape
     depth = pieces[0].shape[1]
     n_blocks = len(pieces)
     held = int(buffer is not None)
-    whole = lambda shape: pl.BlockSpec(shape, lambda j, m: (0,) * len(shape))
+    here = pl.BlockSpec(memory_space=pltpu.VMEM)
+    there = pl.BlockSpec(memory_space=pltpu.HBM)
     operands = (*pieces, a_pair) + ((buffer,) if held else ())
-    return pl.pallas_call(
+    shape = (2, depth // 2, width)
+    out = pl.pallas_call(
         functools.partial(proj_kernel, n_blocks, held),
         grid_spec=pltpu.PrefetchScalarGridSpec(
             num_scalar_prefetch=1,
             grid=(n_blocks,),
-            in_specs=[whole((tokens, depth))] * len(pieces)
-            + [whole((tokens, width))]
-            + [pl.BlockSpec(memory_space=pl.ANY)] * held,
-            out_specs=pl.BlockSpec((2, 1, depth // 2, width), lambda j, m: (0, m[j], 0, 0)),
-        ),
-        out_shape=jax.ShapeDtypeStruct((2, 8, depth // 2, width), BF),
-        input_output_aliases={len(pieces) + 2: 0} if held else {},
-        compiler_params=params(53),
+            in_specs=[here] * (n_blocks + 1) + [there] * held,
+            out_specs=[there] + [here] * n_taken,
+            scratch_shapes=[
+                pltpu.VMEM((n_blocks, *shape), BF),
+                pltpu.SemaphoreType.DMA((n_blocks,)),
+                pltpu.SemaphoreType.DMA((max(n_taken, 1),)),
+            ],
+        ),
+        out_shape=[jax.ShapeDtypeStruct((2, 8, depth // 2, width), BF)]
+        + [jax.ShapeDtypeStruct(shape, BF)] * n_taken,
+        input_output_aliases={n_blocks + 2: 0} if held else {},
+        compiler_params=params(16),
         cost_estimate=pl.CostEstimate(
             flops=2 * n_blocks * tokens * depth * width,
             bytes_accessed=(2 * n_blocks + 2) * 2**20,
@@ -243,6 +268,7 @@
         ),
         name="project",
     )(blocks, *operands)
+    return out if n_taken else out[0]
 
 
 def grad_kernel(gplan, wplan, n_g, n_w, meta_ref, *refs):
@@ -313,7 +339,7 @@
         grid_spec=pltpu.PrefetchScalarGridSpec(
             num_scalar_prefetch=1,
             grid=(8,),
-            in_specs=[pl.BlockSpec(memory_space=pl.ANY)] * (len(g_pieces) + len(w_pieces)),
+            in_specs=[pl.BlockSpec(memory_space=pltpu.HBM)] * (len(g_pieces) + len(w_pieces)),
             out_specs=[whole, whole],
             scratch_shapes=[
                 pltpu.VMEM((8, tokens, depth), BF),
@@ -327,7 +353,7 @@
             jax.ShapeDtypeStruct((half, width), F32),
             jax.ShapeDtypeStruct((half, width), BF),
         ],
-        compiler_params=params(53),
+        compiler_params=params(34),
         cost_estimate=pl.CostEstimate(
             flops=16 * tokens * depth * width,
             bytes_accessed=20 * 2**20,
@@ -361,22 +387,22 @@
 
 def add_blocks(buffer, blocks, terms, plan):
     _, _, rows, width = buffer.shape
-    whole = lambda shape: pl.BlockSpec(shape, lambda i, m: (0,) * len(shape))
+    here = pl.BlockSpec(memory_space=pltpu.VMEM)
     shapes = [(2 if half is None else 1, rows, width) for _, half, _ in plan]
     return pl.pallas_call(
         functools.partial(add_kernel, len(terms), plan),
         grid_spec=pltpu.PrefetchScalarGridSpec(
             num_scalar_prefetch=1,
             grid=(1,),
-            in_specs=[pl.BlockSpec(memory_space=pl.ANY)] + [whole(t.shape) for t in terms],
-            out_specs=[whole(shape) for shape in shapes],
+            in_specs=[pl.BlockSpec(memory_space=pltpu.HBM)] + [here] * len(terms),
+            out_specs=[here] * len(plan),
             scratch_shapes=[
                 pltpu.VMEM((blocks.shape[0], 2, rows, width), BF),
                 pltpu.SemaphoreType.DMA((blocks.shape[0],)),
             ],
         ),
         out_shape=[jax.ShapeDtypeStruct(shape, BF) for shape in shapes],
-        compiler_params=params(53),
+        compiler_params=params(12),
         cost_estimate=pl.CostEstimate(
             flops=2**21, bytes_accessed=5 * 2**20, transcendentals=0
         ),
@@ -404,6 +430,7 @@
     g_give = lax.dynamic_slice_in_dim(output_grad, (1 - k) * half_d, half_d, 1)
     g0 = jnp.concatenate([g_keep, move_row(g_give, dk=1)], 0)
     kv = jnp.concatenate([key_rows, value_rows], 1)
+    (kv,) = tied((kv,), g0)
     kv_earlier = passed_along(kv, "row", 1)
 
     gxm = move_col(g0, dx=1)
@@ -455,13 +482,12 @@
 
     go, gyo, wyzm, wyzp, wyo, proj = tied((go, gyo, wyzm, wyzp, wyo, proj))
 
-    proj = project([go, gyo], a_pair, ints(gblock(0, 2), gblock(1, 2)), proj)
-
-    give_up, give_dn, give_far = add_blocks(
+    proj, give_up, give_dn, give_far = project(
+        [go, gyo],
+        a_pair,
+        ints(gblock(0, 2), gblock(1, 2), wblock(1, 1), wblock(-1, 1), wblock(2, 1)),
         proj,
-        ints(wblock(1, 1), wblock(-1, 1), wblock(2, 1)),
-        [],
-        [(0, None, ()), (1, None, ()), (2, None, ())],
+        3,
     )
     rup = move_row(give_up, dz=1)
     rdn = move_row(give_dn, dz=-1)

time: 205 us -> 197 us (0.961)
  Pallas kernels: 91.8 us -> 72.6 us
  local copies, waits for them, and re-layouts: 12.5 us -> 25.5 us
  waiting for transfers between devices: 48.6 us -> 55.1 us
  starting transfers between devices: 44.5 us -> 39.3 us
  other arithmetic: 5.61 us -> 2.95 us
    unnamed x26 -> x42, local copies, waits for them, and re-layouts: 5.69 us -> 19.4 us
    pallas_call x4 -> x3, Pallas kernels: 18.9 us -> 6.19 us  [add_blocks(): pl.pallas_call(functools.partial(add_kernel, len(terms), plan), grid_spec...]
    ppermute x18, waiting for transfers between devices: 27.7 us -> 33.2 us  [move_row(): return lax.ppermute(value, 'row', pairs)]
    ppermute x7, starting transfers between devices: 8.14 us -> 4.64 us  [move_col(): return lax.ppermute(value, 'col', pairs)]
    pallas_call x3, Pallas kernels: 22.4 us -> 19.3 us  [project(): pl.pallas_call(functools.partial(proj_kernel, n_blocks, held), grid_spec=...]
    ppermute x18, starting transfers between devices: 28.2 us -> 26.2 us  [move_row(): return lax.ppermute(value, 'row', pairs)]
  transfers between devices with their start and end apart: 27 -> 27, of which waited for: 15 -> 16; matrix products, arithmetic and copies ran while one was open for 6% -> 5% of each run, Pallas kernels for 38% -> 33%
where the time goes in v4:
time: 197 us
  Pallas kernels  72.6 us (37%)
  waiting for transfers between devices  55.1 us (28%)
  starting transfers between devices  39.3 us (20%)
  local copies, waits for them, and re-layouts  25.5 us (13%)
  other arithmetic  2.95 us (1%)
    ppermute x18, waiting for transfers between devices, move_row(): return lax.ppermute(value, 'row', pairs)  33.2 us
    ppermute x18, starting transfers between devices, move_row(): return lax.ppermute(value, 'row', pairs)  26.2 us
    unnamed x42, local copies, waits for them, and re-layouts  19.4 us
    pallas_call x3, Pallas kernels, project(): pl.pallas_call(functools.partial(proj_kernel, n_blocks, held), grid_spec=...  19.3 us
    pallas_call x1, Pallas kernels, attend_back(): pl.pallas_call(bwd_kernel, grid_spec=pltpu.PrefetchScalarGridSpec(num_sca...  17.2 us
    ppermute x7, waiting for transfers between devices, move_col(): return lax.ppermute(value, 'col', pairs)  15.4 us
    pallas_call x1, Pallas kernels, attn_grad_part(): pl.pallas_call(kernel, grid_spec=pltpu.PrefetchScalarGridSpec(num_scalar_...  15.1 us
    pallas_call x1, Pallas kernels, attend(): pl.pallas_call(fwd_kernel, grid_spec=pltpu.PrefetchScalarGridSpec(num_sca...  14.8 us
  transfers between devices with their start and end apart: 27, of which 16 were waited for; matrix products, arithmetic and copies ran while one was open for 5% of the time, Pallas kernels for 33%

profile of v4, /device:TPU:1, one launch (start us, length us, event | category | flops | bytes accessed | tf_op | source)
XLA Modules:
  0.0 196.8 jit_solution(11961561171767329402)
XLA Ops:
  0.7 1.3 constant_dynamic-slice_fusion.1
  2.0 1.5 collective-permute-start
  3.6 1.5 collective-permute-done
  5.2 5.3 %collective-permute-start.6 = (bf16[512,256]{1,0:T(8,128)(2,1)S(1)}, bf16[512,256]{1,0:T(8,128)(2,1)S(1)}, u32[]{:S(2)}, u32[]{:S(2)}) collective-permute-start(bf16[512,256]{1,0:T(8,128)(2,1)S(1)} %pad_maximum_fusion.1), channel_id=1, source_target_pairs={{0,8},{8,16},{16,24},{24,32},{32,40},{40,48},{48,56},{56,64},{64,7... | collective-permute-start | bytes 786440 | tf_op jit(solution)/shard_map/ppermute | solution.py:42
  10.5 3.8 %collective-permute-start.5 = (bf16[512,1024]{1,0:T(8,128)(2,1)}, bf16[512,1024]{1,0:T(8,128)(2,1)}, u32[]{:S(2)}, u32[]{:S(2)}) collective-permute-start(bf16[512,1024]{1,0:T(8,128)(2,1)} %refs_8_.1), channel_id=1, source_target_pairs={{0,96},{8,104},{16,112},{24,120},{32,0},{40,8},{48,16},{56,24},{64... | collective-permute-start | bytes 3145736 | tf_op jit(solution)/shard_map/ppermute | solution.py:28
  14.3 0.4 collective-permute-start.3
  14.7 2.5 %collective-permute-start.2 = (bf16[1024,512]{1,0:T(8,128)(2,1)S(1)}, bf16[1024,512]{1,0:T(8,128)(2,1)}, u32[]{:S(2)}, u32[]{:S(2)}) collective-permute-start(bf16[1024,512]{1,0:T(8,128)(2,1)S(1)} %pad_maximum_fusion.refs_0_), channel_id=1, source_target_pairs={{0,3},{1,0},{2,1},{3,2},{4,7},{5,4},{6,5},{7,6},{8,11},{9,8},{10,9... | collective-permute-start | bytes 3145736 | tf_op jit(solution)/shard_map/ppermute | solution.py:36
  17.2 0.8 fusion.3
  18.0 0.2 copy.15.segk_ref
  18.3 0.9 fusion.2
  19.3 0.1 copy.14.vt_ref
  19.4 14.8 %attend.1 = (bf16[512,1024]{1,0:T(8,128)(2,1)}, f32[8,1,512]{2,1,0:T(1,128)S(1)}, f32[8,1,512]{2,1,0:T(1,128)S(1)}) custom-call(s32[1]{0:T(128)} %bitcast.meta_ref, bf16[512,1024]{1,0:T(8,128)(2,1)S(1)} %copy-done.13, bf16[1024,128]{1,0:T(8,128)(2,1)S(1)} %get-tuple-element.103.k_ref, bf16[128,1024]{1,0:T(8,128)(2,1)S(1)} %copy.14.vt_ref, ...), custom_call_target="tpu_custom_call" | custom-call | flops 4294967296 | bytes 8388608 | tf_op jit(solution)/shard_map/attend/pallas_call | solution.py:95
  34.3 1.1 collective-permute-done.5.refs_10_
  35.4 3.7 %collective-permute-done.4.refs_9_ = bf16[512,1024]{1,0:T(8,128)(2,1)} collective-permute-done((bf16[512,1024]{1,0:T(8,128)(2,1)}, bf16[512,1024]{1,0:T(8,128)(2,1)}, u32[]{:S(2)}, u32[]{:S(2)}) %collective-permute-start.4) | collective-permute-done | bytes 1048608 | tf_op jit(solution)/shard_map/ppermute | solution.py:28
  39.1 0.3 collective-permute-done.2.refs_2_
  39.4 3.5 %collective-permute-done.1.refs_1_ = bf16[1024,512]{1,0:T(8,128)(2,1)} collective-permute-done((bf16[1024,512]{1,0:T(8,128)(2,1)S(1)}, bf16[1024,512]{1,0:T(8,128)(2,1)}, u32[]{:S(2)}, u32[]{:S(2)}) %collective-permute-start.1) | collective-permute-done | bytes 1048608 | tf_op jit(solution)/shard_map/ppermute | solution.py:36
  42.9 0.3 collective-permute-start.12
  43.2 1.7 collective-permute-start.11
  44.9 1.4 collective-permute-start.10
  46.3 1.5 collective-permute-start.8
  47.9 1.4 constant_dynamic-update-slice_fusion.3
  49.3 1.3 constant_dynamic-update-slice_fusion.2.refs_4_.refs_2_
  50.7 8.0 %project.3.refs_3_ = bf16[2,8,256,1024]{3,2,1,0:T(8,128)(2,1)S(1)} custom-call(s32[4]{0:T(128)S(1)} %pad_add_fusion.2.meta_ref, bf16[1024,512]{1,0:T(8,128)(2,1)S(1)} %copy-done.6, bf16[1024,512]{1,0:T(8,128)(2,1)} %collective-permute-done.1.refs_1_, bf16[1024,512]{1,0:T(8,128)(2,1)} %collective-permute-done.2.refs_2_, ...), custom_call_target="tpu_custom_call" | custom-call | flops 4294967296 | bytes 10485760 | tf_op jit(solution)/shard_map/project/pallas_call | solution.py:247
  58.7 3.3 %copy-done = bf16[2,8,256,1024]{3,2,1,0:T(8,128)(2,1)} copy-done((bf16[2,8,256,1024]{3,2,1,0:T(8,128)(2,1)}, bf16[2,8,256,1024]{3,2,1,0:T(8,128)(2,1)S(1)}, u32[]{:S(2)}) %copy-start) | copy-done | bytes 8388632
  62.0 7.6 %collective-permute-done.11.refs_11_ = bf16[512,1024]{1,0:T(8,128)(2,1)} collective-permute-done((bf16[512,1024]{1,0:T(8,128)(2,1)}, bf16[512,1024]{1,0:T(8,128)(2,1)}, u32[]{:S(2)}, u32[]{:S(2)}) %collective-permute-start.11) | collective-permute-done | bytes 1048608 | tf_op jit(solution)/shard_map/ppermute | solution.py:28
  69.6 1.4 collective-permute-done.10.refs_15_
  70.9 1.1 collective-permute-done.8.refs_0_.refs_4_
  72.0 1.5 collective-permute-start.16
  73.5 0.2 collective-permute-start.13
  73.7 2.3 %collective-permute-start.15 = (bf16[512,1024]{1,0:T(8,128)(2,1)}, bf16[512,1024]{1,0:T(8,128)(2,1)}, u32[]{:S(2)}, u32[]{:S(2)}) collective-permute-start(bf16[512,1024]{1,0:T(8,128)(2,1)} %collective-permute-done.11.refs_11_), channel_id=1, source_target_pairs={{0,96},{8,104},{16,112},{24,120},{32,0},{40,8},{48,16},{56,24},{64... | collective-permute-start | bytes 3145736 | tf_op jit(solution)/shard_map/ppermute | solution.py:28
  76.1 3.4 %copy-done.1 = bf16[2,8,256,1024]{3,2,1,0:T(8,128)(2,1)S(1)} copy-done((bf16[2,8,256,1024]{3,2,1,0:T(8,128)(2,1)S(1)}, bf16[2,8,256,1024]{3,2,1,0:T(8,128)(2,1)}, u32[]{:S(2)}) %copy-start.1) | copy-done | bytes 8388632
  79.5 4.5 %project.4.refs_3_ = bf16[2,8,256,1024]{3,2,1,0:T(8,128)(2,1)S(1)} custom-call(s32[2]{0:T(128)S(1)} %pad_add_fusion.3.meta_ref, bf16[1024,512]{1,0:T(8,128)(2,1)} %collective-permute-done.8.refs_0_.refs_4_, bf16[1024,512]{1,0:T(8,128)(2,1)S(1)} %collective-permute-done.9.refs_1_.refs_5_, ...), custom_call_target="tpu_custom_call", output_to_operand_aliasing={{}: (4, {})} | custom-call | flops 2147483648 | bytes 6291456 | tf_op jit(solution)/shard_map/project/pallas_call | solution.py:247
  84.0 10.5 %collective-permute-done.7.refs_0_.refs_6_ = bf16[1024,512]{1,0:T(8,128)(2,1)} collective-permute-done((bf16[1024,512]{1,0:T(8,128)(2,1)}, bf16[1024,512]{1,0:T(8,128)(2,1)}, u32[]{:S(2)}, u32[]{:S(2)}) %collective-permute-start.7) | collective-permute-done | bytes 1048608 | tf_op jit(solution)/shard_map/ppermute | solution.py:36
  94.5 1.6 collective-permute-done.16.refs_14_
  96.0 0.8 collective-permute-done.15.refs_13_
  96.8 3.1 %collective-permute-done.14.refs_12_ = bf16[512,1024]{1,0:T(8,128)(2,1)} collective-permute-done((bf16[512,1024]{1,0:T(8,128)(2,1)}, bf16[512,1024]{1,0:T(8,128)(2,1)}, u32[]{:S(2)}, u32[]{:S(2)}) %collective-permute-start.14) | collective-permute-done | bytes 1048608 | tf_op jit(solution)/shard_map/ppermute | solution.py:28
  100.0 6.8 %project.5 = (bf16[2,8,256,1024]{3,2,1,0:T(8,128)(2,1)S(1)}, bf16[2,256,1024]{2,1,0:T(8,128)(2,1)}, bf16[2,256,1024]{2,1,0:T(8,128)(2,1)}, bf16[2,256,1024]{2,1,0:T(8,128)(2,1)}) custom-call(s32[5]{0:T(128)S(1)} %stack.97.meta_ref, bf16[1024,512]{1,0:T(8,128)(2,1)} %collective-permute-done.7.refs_0_.refs_6_, ...), custom_call_target="tpu_custom_call", output_to_operand_aliasing={{0}: (4, {})} | custom-call | flops 2147483648 | bytes 6291456 | tf_op jit(solution)/shard_map/project/pallas_call | solution.py:247
  106.7 3.3 %copy-done.2 = bf16[2,8,256,1024]{3,2,1,0:T(8,128)(2,1)} copy-done((bf16[2,8,256,1024]{3,2,1,0:T(8,128)(2,1)}, bf16[2,8,256,1024]{3,2,1,0:T(8,128)(2,1)S(1)}, u32[]{:S(2)}) %copy-start.2) | copy-done | bytes 8388632
  110.0 0.3 collective-permute-start.18
  110.3 0.1 collective-permute-start.19
  110.5 1.0 collective-permute-start.17
  111.5 0.1 stack.109.meta_ref
  111.6 1.2 copy-done.7
  112.8 15.1 %attn_grad.1 = (f32[512,1024]{1,0:T(8,128)S(1)}, bf16[512,1024]{1,0:T(8,128)(2,1)}) custom-call(s32[16]{0:T(128)S(1)} %stack.109.meta_ref, bf16[1024,512]{1,0:T(8,128)(2,1)S(1)} %copy-done.7, bf16[1024,512]{1,0:T(8,128)(2,1)} %collective-permute-done.1.refs_1_, bf16[1024,512]{1,0:T(8,128)(2,1)} %collective-permute-done.2.refs_2_, ...), custom_call_target="tpu_custom_call" | custom-call | flops 8589934592 | bytes 20971520 | tf_op jit(solution)/shard_map/attn_grad/pallas_call | solution.py:337
  128.0 4.0 %collective-permute-done.18.refs_1_ = bf16[2,256,1024]{2,1,0:T(8,128)(2,1)} collective-permute-done((bf16[2,256,1024]{2,1,0:T(8,128)(2,1)}, bf16[2,256,1024]{2,1,0:T(8,128)(2,1)}, u32[]{:S(2)}, u32[]{:S(2)}) %collective-permute-start.18) | collective-permute-done | bytes 1048608 | tf_op jit(solution)/shard_map/ppermute | solution.py:28
  131.9 1.8 collective-permute-done.19.refs_2_
  133.7 4.0 %collective-permute-start.22 = (bf16[512,1024]{1,0:T(8,128)(2,1)}, bf16[512,1024]{1,0:T(8,128)(2,1)}, u32[]{:S(2)}, u32[]{:S(2)}) collective-permute-start(bf16[512,1024]{1,0:T(8,128)(2,1)} %get-tuple-element.83), channel_id=1, source_target_pairs={{0,8},{8,0},{16,24},{24,16},{32,40},{40,32},{48,56},{56,48},{64,72... | collective-permute-start | bytes 3145736 | tf_op jit(solution)/shard_map/ppermute | solution.py:28
  137.8 3.4 %copy-done.3 = bf16[2,8,256,1024]{3,2,1,0:T(8,128)(2,1)S(1)} copy-done((bf16[2,8,256,1024]{3,2,1,0:T(8,128)(2,1)S(1)}, bf16[2,8,256,1024]{3,2,1,0:T(8,128)(2,1)}, u32[]{:S(2)}) %copy-start.3) | copy-done | bytes 8388632
  141.2 3.6 %add_blocks.3 = (bf16[2,256,1024]{2,1,0:T(8,128)(2,1)S(1)}, bf16[1,256,1024]{2,1,0:T(8,128)(2,1)}, bf16[1,256,1024]{2,1,0:T(8,128)(2,1)}) custom-call(s32[2]{0:T(128)S(1)} %pad_add_fusion.1.meta_ref, bf16[2,8,256,1024]{3,2,1,0:T(8,128)(2,1)S(1)} %copy-done.3, bf16[2,256,1024]{2,1,0:T(8,128)(2,1)} %collective-permute-done.17.refs_0_, ...), custom_call_target="tpu_custom_call" | custom-call | flops 2097152 | bytes 5242880 | tf_op jit(solution)/shard_map/add_blocks/pallas_call | solution.py:392
  144.8 1.2 collective-permute-start.20
  146.1 1.5 collective-permute-start.21
  147.7 1.1 copy.16.kt_ref
  148.8 2.8 %collective-permute-start.26 = (bf16[2,256,1024]{2,1,0:T(8,128)(2,1)}, bf16[2,256,1024]{2,1,0:T(8,128)(2,1)S(1)}, u32[]{:S(2)}, u32[]{:S(2)}) collective-permute-start(bf16[2,256,1024]{2,1,0:T(8,128)(2,1)} %copy-done.15), channel_id=1, source_target_pairs={{0,16},{8,24},{16,0},{24,8},{32,48},{40,56},{48,32},{56,40},{64,80... | collective-permute-start | bytes 3145736 | tf_op jit(solution)/shard_map/ppermute | solution.py:28
  151.5 1.7 add_convert_fusion.g_ref
  153.3 6.6 %collective-permute-done.20.refs_0_ = bf16[1,256,1024]{2,1,0:T(8,128)(2,1)S(1)} collective-permute-done((bf16[1,256,1024]{2,1,0:T(8,128)(2,1)}, bf16[1,256,1024]{2,1,0:T(8,128)(2,1)S(1)}, u32[]{:S(2)}, u32[]{:S(2)}) %collective-permute-start.20) | collective-permute-done | bytes 524320 | tf_op jit(solution)/shard_map/ppermute | solution.py:28
  159.9 3.4 %copy-done.4 = bf16[2,8,256,1024]{3,2,1,0:T(8,128)(2,1)S(1)} copy-done((bf16[2,8,256,1024]{3,2,1,0:T(8,128)(2,1)S(1)}, bf16[2,8,256,1024]{3,2,1,0:T(8,128)(2,1)}, u32[]{:S(2)}) %copy-start.4) | copy-done | bytes 8388632
  163.3 1.0 add_blocks.4
  164.3 0.1 collective-permute-start.24
  164.4 2.6 %collective-permute-start.25 = (bf16[2,256,1024]{2,1,0:T(8,128)(2,1)S(1)}, bf16[2,256,1024]{2,1,0:T(8,128)(2,1)S(1)}, u32[]{:S(2)}, u32[]{:S(2)}) collective-permute-start(bf16[2,256,1024]{2,1,0:T(8,128)(2,1)S(1)} %get-tuple-element.94), channel_id=1, source_target_pairs={{0,96},{8,104},{16,112},{24,120},{32,0},{40,8},{48,16},{56,24},{64... | collective-permute-start | bytes 3145736 | tf_op jit(solution)/shard_map/ppermute | solution.py:28
  167.0 17.2 %attend_back.1 = (bf16[512,1024]{1,0:T(8,128)(2,1)}, f32[1024,128]{1,0:T(8,128)S(1)}, f32[1024,128]{1,0:T(8,128)S(1)}) custom-call(s32[1]{0:T(128)} %bitcast.meta_ref, bf16[512,1024]{1,0:T(8,128)(2,1)S(1)} %copy-done.14, bf16[512,1024]{1,0:T(8,128)(2,1)S(1)} %add_convert_fusion.g_ref, bf16[1024,128]{1,0:T(8,128)(2,1)S(1)} %copy-done.12, ...), custom_call_target="tpu_custom_call" | custom-call | flops 10737418240 | bytes 12582912 | tf_op jit(solution)/shard_map/attend_back/pallas_call | solution.py:168
  184.3 3.3 %collective-permute-start.23 = (bf16[512,256]{1,0:T(8,128)(2,1)S(1)}, bf16[512,256]{1,0:T(8,128)(2,1)S(1)}, u32[]{:S(2)}, u32[]{:S(2)}) collective-permute-start(bf16[512,256]{1,0:T(8,128)(2,1)S(1)} %pad_maximum_fusion.2), channel_id=1, source_target_pairs={{8,0},{16,8},{24,16},{32,24},{40,32},{48,40},{56,48},{64,56},{72,6... | collective-permute-start | bytes 786440 | tf_op jit(solution)/shard_map/ppermute | solution.py:42
  187.6 6.6 %collective-permute-done.23 = bf16[512,256]{1,0:T(8,128)(2,1)S(1)} collective-permute-done((bf16[512,256]{1,0:T(8,128)(2,1)S(1)}, bf16[512,256]{1,0:T(8,128)(2,1)S(1)}, u32[]{:S(2)}, u32[]{:S(2)}) %collective-permute-start.23) | collective-permute-done | bytes 262176 | tf_op jit(solution)/shard_map/ppermute | solution.py:42
  194.2 0.8 fusion
  195.0 1.6 add_blocks.5
  (65 shorter events, 0.8 us)
Async XLA Ops:
  0.6 2.9 %copy-start.16 = (bf16[512,128]{1,0:T(8,128)(2,1)S(1)}, bf16[512,128]{1,0:T(8,128)(2,1)}, u32[]{:S(2)}) copy-start(bf16[512,128]{1,0:T(8,128)(2,1)} %param.8) | copy-start | bytes 393220
  0.6 2.9 %copy-start.17 = (bf16[512,128]{1,0:T(8,128)(2,1)S(1)}, bf16[512,128]{1,0:T(8,128)(2,1)}, u32[]{:S(2)}) copy-start(bf16[512,128]{1,0:T(8,128)(2,1)} %param.7) | copy-start | bytes 393220
  2.0 3.0 %collective-permute-start = (bf16[512,512]{1,0:T(8,128)(2,1)S(1)}, bf16[512,512]{1,0:T(8,128)(2,1)S(1)}, u32[]{:S(2)}, u32[]{:S(2)}) collective-permute-start(bf16[512,512]{1,0:T(8,128)(2,1)S(1)} %get-tuple-element.97), channel_id=1, source_target_pairs={{0,8},{8,0},{16,24},{24,16},{32,40},{40,32},{48,56},{56,48},{64,72... | collective-permute-start | bytes 1572872 | tf_op jit(solution)/shard_map/ppermute | solution.py:28
  5.1 29.1 %copy-start.5 = (bf16[1024,512]{1,0:T(8,128)(2,1)}, bf16[1024,512]{1,0:T(8,128)(2,1)S(1)}, u32[]{:S(2)}) copy-start(bf16[1024,512]{1,0:T(8,128)(2,1)S(1)} %pad_maximum_fusion.refs_0_) | copy-start | bytes 3145732
  5.1 14.3 %copy-start.13 = (bf16[512,1024]{1,0:T(8,128)(2,1)S(1)}, bf16[512,1024]{1,0:T(8,128)(2,1)}, u32[]{:S(2)}) copy-start(bf16[512,1024]{1,0:T(8,128)(2,1)} %q_ref.2) | copy-start | bytes 3145732
  5.2 12.0 %collective-permute-start.6 = (bf16[512,256]{1,0:T(8,128)(2,1)S(1)}, bf16[512,256]{1,0:T(8,128)(2,1)S(1)}, u32[]{:S(2)}, u32[]{:S(2)}) collective-permute-start(bf16[512,256]{1,0:T(8,128)(2,1)S(1)} %pad_maximum_fusion.1), channel_id=1, source_target_pairs={{0,8},{8,16},{16,24},{24,32},{32,40},{40,48},{48,56},{56,64},{64,7... | collective-permute-start | bytes 786440 | tf_op jit(solution)/shard_map/ppermute | solution.py:42
  10.5 24.9 %collective-permute-start.5 = (bf16[512,1024]{1,0:T(8,128)(2,1)}, bf16[512,1024]{1,0:T(8,128)(2,1)}, u32[]{:S(2)}, u32[]{:S(2)}) collective-permute-start(bf16[512,1024]{1,0:T(8,128)(2,1)} %refs_8_.1), channel_id=1, source_target_pairs={{0,96},{8,104},{16,112},{24,120},{32,0},{40,8},{48,16},{56,24},{64... | collective-permute-start | bytes 3145736 | tf_op jit(solution)/shard_map/ppermute | solution.py:28
  14.3 24.8 %collective-permute-start.4 = (bf16[512,1024]{1,0:T(8,128)(2,1)}, bf16[512,1024]{1,0:T(8,128)(2,1)}, u32[]{:S(2)}, u32[]{:S(2)}) collective-permute-start(bf16[512,1024]{1,0:T(8,128)(2,1)} %refs_8_.1), channel_id=1, source_target_pairs={{0,32},{8,40},{16,48},{24,56},{32,64},{40,72},{48,80},{56,88},{64,... | collective-permute-start | bytes 3145736 | tf_op jit(solution)/shard_map/ppermute | solution.py:28
  14.3 24.8 %collective-permute-start.3 = (bf16[1024,512]{1,0:T(8,128)(2,1)S(1)}, bf16[1024,512]{1,0:T(8,128)(2,1)}, u32[]{:S(2)}, u32[]{:S(2)}) collective-permute-start(bf16[1024,512]{1,0:T(8,128)(2,1)S(1)} %pad_maximum_fusion.refs_0_), channel_id=1, source_target_pairs={{0,4},{1,5},{2,6},{3,7},{4,0},{5,1},{6,2},{7,3},{8,12},{9,13},{10,... | collective-permute-start | bytes 3145736 | tf_op jit(solution)/shard_map/ppermute | solution.py:36
  14.7 24.7 %collective-permute-start.2 = (bf16[1024,512]{1,0:T(8,128)(2,1)S(1)}, bf16[1024,512]{1,0:T(8,128)(2,1)}, u32[]{:S(2)}, u32[]{:S(2)}) collective-permute-start(bf16[1024,512]{1,0:T(8,128)(2,1)S(1)} %pad_maximum_fusion.refs_0_), channel_id=1, source_target_pairs={{0,3},{1,0},{2,1},{3,2},{4,7},{5,4},{6,5},{7,6},{8,11},{9,8},{10,9... | collective-permute-start | bytes 3145736 | tf_op jit(solution)/shard_map/ppermute | solution.py:36
  17.2 25.7 %collective-permute-start.1 = (bf16[1024,512]{1,0:T(8,128)(2,1)S(1)}, bf16[1024,512]{1,0:T(8,128)(2,1)}, u32[]{:S(2)}, u32[]{:S(2)}) collective-permute-start(bf16[1024,512]{1,0:T(8,128)(2,1)S(1)} %pad_maximum_fusion.refs_0_), channel_id=1, source_target_pairs={{0,1},{1,2},{2,3},{3,0},{4,5},{5,6},{6,7},{7,4},{8,9},{9,10},{10,1... | collective-permute-start | bytes 3145736 | tf_op jit(solution)/shard_map/ppermute | solution.py:36
  18.2 16.0 %copy-start.8 = (s32[1024,1]{1,0:T(8,128)}, s32[1024,1]{1,0:T(8,128)S(1)}, u32[]{:S(2)}) copy-start(s32[1024,1]{1,0:T(8,128)S(1)} %copy.15.segk_ref) | copy-start | bytes 12292
  19.3 15.0 %copy-start.11 = (bf16[1024,128]{1,0:T(8,128)(2,1)}, bf16[1024,128]{1,0:T(8,128)(2,1)S(1)}, u32[]{:S(2)}) copy-start(bf16[1024,128]{1,0:T(8,128)(2,1)S(1)} %get-tuple-element.103.k_ref) | copy-start | bytes 786436
  42.9 6.3 %collective-permute-start.12 = (bf16[512,1024]{1,0:T(8,128)(2,1)}, bf16[512,1024]{1,0:T(8,128)(2,1)}, u32[]{:S(2)}, u32[]{:S(2)}) collective-permute-start(bf16[512,1024]{1,0:T(8,128)(2,1)} %get-tuple-element.57), channel_id=1, source_target_pairs={{0,8},{8,0},{16,24},{24,16},{32,40},{40,32},{48,56},{56,48},{64,72... | collective-permute-start | bytes 3145736 | tf_op jit(solution)/shard_map/ppermute | solution.py:28
  43.2 26.4 %collective-permute-start.11 = (bf16[512,1024]{1,0:T(8,128)(2,1)}, bf16[512,1024]{1,0:T(8,128)(2,1)}, u32[]{:S(2)}, u32[]{:S(2)}) collective-permute-start(bf16[512,1024]{1,0:T(8,128)(2,1)} %refs_8_.1), channel_id=1, source_target_pairs={{0,16},{8,24},{16,0},{24,8},{32,48},{40,56},{48,32},{56,40},{64,80... | collective-permute-start | bytes 3145736 | tf_op jit(solution)/shard_map/ppermute | solution.py:28
  44.9 26.0 %collective-permute-start.10 = (bf16[512,1024]{1,0:T(8,128)(2,1)}, bf16[512,1024]{1,0:T(8,128)(2,1)}, u32[]{:S(2)}, u32[]{:S(2)}) collective-permute-start(bf16[512,1024]{1,0:T(8,128)(2,1)} %collective-permute-done.4.refs_9_), channel_id=1, source_target_pairs={{0,32},{8,40},{16,48},{24,56},{32,64},{40,72},{48,80},{56,88},{64,... | collective-permute-start | bytes 3145736 | tf_op jit(solution)/shard_map/ppermute | solution.py:28
  46.3 24.6 %collective-permute-start.9 = (bf16[1024,512]{1,0:T(8,128)(2,1)}, bf16[1024,512]{1,0:T(8,128)(2,1)S(1)}, u32[]{:S(2)}, u32[]{:S(2)}) collective-permute-start(bf16[1024,512]{1,0:T(8,128)(2,1)} %collective-permute-done.3.refs_3_), channel_id=1, source_target_pairs={{0,3},{1,0},{2,1},{3,2},{4,7},{5,4},{6,5},{7,6},{8,11},{9,8},{10,9... | collective-permute-start | bytes 3145736 | tf_op jit(solution)/shard_map/ppermute | solution.py:36
  46.3 25.7 %collective-permute-start.8 = (bf16[1024,512]{1,0:T(8,128)(2,1)}, bf16[1024,512]{1,0:T(8,128)(2,1)}, u32[]{:S(2)}, u32[]{:S(2)}) collective-permute-start(bf16[1024,512]{1,0:T(8,128)(2,1)} %collective-permute-done.3.refs_3_), channel_id=1, source_target_pairs={{0,1},{1,2},{2,3},{3,0},{4,5},{5,6},{6,7},{7,4},{8,9},{9,10},{10,1... | collective-permute-start | bytes 3145736 | tf_op jit(solution)/shard_map/ppermute | solution.py:36
  47.9 2.8 %copy-start.6 = (bf16[1024,512]{1,0:T(8,128)(2,1)S(1)}, bf16[1024,512]{1,0:T(8,128)(2,1)}, u32[]{:S(2)}) copy-start(bf16[1024,512]{1,0:T(8,128)(2,1)} %copy-done.5) | copy-start | bytes 3145732
  49.3 45.2 %collective-permute-start.7 = (bf16[1024,512]{1,0:T(8,128)(2,1)}, bf16[1024,512]{1,0:T(8,128)(2,1)}, u32[]{:S(2)}, u32[]{:S(2)}) collective-permute-start(bf16[1024,512]{1,0:T(8,128)(2,1)} %collective-permute-done.1.refs_1_), channel_id=1, source_target_pairs={{0,1},{1,2},{2,3},{3,0},{4,5},{5,6},{6,7},{7,4},{8,9},{9,10},{10,1... | collective-permute-start | bytes 3145736 | tf_op jit(solution)/shard_map/ppermute | solution.py:36
  58.6 3.3 %copy-start = (bf16[2,8,256,1024]{3,2,1,0:T(8,128)(2,1)}, bf16[2,8,256,1024]{3,2,1,0:T(8,128)(2,1)S(1)}, u32[]{:S(2)}) copy-start(bf16[2,8,256,1024]{3,2,1,0:T(8,128)(2,1)S(1)} %project.3.refs_3_) | copy-start | bytes 25165828
  72.0 24.0 %collective-permute-start.16 = (bf16[512,1024]{1,0:T(8,128)(2,1)}, bf16[512,1024]{1,0:T(8,128)(2,1)}, u32[]{:S(2)}, u32[]{:S(2)}) collective-permute-start(bf16[512,1024]{1,0:T(8,128)(2,1)} %collective-permute-done.10.refs_15_), channel_id=1, source_target_pairs={{0,16},{8,24},{16,0},{24,8},{32,48},{40,56},{48,32},{56,40},{64,80... | collective-permute-start | bytes 3145736 | tf_op jit(solution)/shard_map/ppermute | solution.py:28
  73.5 22.6 %collective-permute-start.13 = (bf16[1024,512]{1,0:T(8,128)(2,1)S(1)}, bf16[1024,512]{1,0:T(8,128)(2,1)}, u32[]{:S(2)}, u32[]{:S(2)}) collective-permute-start(bf16[1024,512]{1,0:T(8,128)(2,1)S(1)} %collective-permute-done.9.refs_1_.refs_5_), channel_id=1, source_target_pairs={{0,3},{1,0},{2,1},{3,2},{4,7},{5,4},{6,5},{7,6},{8,11},{9,8},{10,9... | collective-permute-start | bytes 3145736 | tf_op jit(solution)/shard_map/ppermute | solution.py:36
  73.7 23.2 %collective-permute-start.15 = (bf16[512,1024]{1,0:T(8,128)(2,1)}, bf16[512,1024]{1,0:T(8,128)(2,1)}, u32[]{:S(2)}, u32[]{:S(2)}) collective-permute-start(bf16[512,1024]{1,0:T(8,128)(2,1)} %collective-permute-done.11.refs_11_), channel_id=1, source_target_pairs={{0,96},{8,104},{16,112},{24,120},{32,0},{40,8},{48,16},{56,24},{64... | collective-permute-start | bytes 3145736 | tf_op jit(solution)/shard_map/ppermute | solution.py:28
  75.9 24.0 %collective-permute-start.14 = (bf16[512,1024]{1,0:T(8,128)(2,1)}, bf16[512,1024]{1,0:T(8,128)(2,1)}, u32[]{:S(2)}, u32[]{:S(2)}) collective-permute-start(bf16[512,1024]{1,0:T(8,128)(2,1)} %collective-permute-done.11.refs_11_), channel_id=1, source_target_pairs={{0,32},{8,40},{16,48},{24,56},{32,64},{40,72},{48,80},{56,88},{64,... | collective-permute-start | bytes 3145736 | tf_op jit(solution)/shard_map/ppermute | solution.py:28
  76.1 3.4 %copy-start.1 = (bf16[2,8,256,1024]{3,2,1,0:T(8,128)(2,1)S(1)}, bf16[2,8,256,1024]{3,2,1,0:T(8,128)(2,1)}, u32[]{:S(2)}) copy-start(bf16[2,8,256,1024]{3,2,1,0:T(8,128)(2,1)} %copy-done) | copy-start | bytes 25165828
  106.7 3.3 %copy-start.2 = (bf16[2,8,256,1024]{3,2,1,0:T(8,128)(2,1)}, bf16[2,8,256,1024]{3,2,1,0:T(8,128)(2,1)S(1)}, u32[]{:S(2)}) copy-start(bf16[2,8,256,1024]{3,2,1,0:T(8,128)(2,1)S(1)} %get-tuple-element.66.buffer_ref) | copy-start | bytes 25165828
  110.0 21.9 %collective-permute-start.18 = (bf16[2,256,1024]{2,1,0:T(8,128)(2,1)}, bf16[2,256,1024]{2,1,0:T(8,128)(2,1)}, u32[]{:S(2)}, u32[]{:S(2)}) collective-permute-start(bf16[2,256,1024]{2,1,0:T(8,128)(2,1)} %get-tuple-element.68), channel_id=1, source_target_pairs={{0,96},{8,104},{16,112},{24,120},{32,0},{40,8},{48,16},{56,24},{64... | collective-permute-start | bytes 3145736 | tf_op jit(solution)/shard_map/ppermute | solution.py:28
  110.3 23.4 %collective-permute-start.19 = (bf16[2,256,1024]{2,1,0:T(8,128)(2,1)}, bf16[2,256,1024]{2,1,0:T(8,128)(2,1)}, u32[]{:S(2)}, u32[]{:S(2)}) collective-permute-start(bf16[2,256,1024]{2,1,0:T(8,128)(2,1)} %get-tuple-element.69), channel_id=1, source_target_pairs={{0,16},{8,24},{16,0},{24,8},{32,48},{40,56},{48,32},{56,40},{64,80... | collective-permute-start | bytes 3145736 | tf_op jit(solution)/shard_map/ppermute | solution.py:28
  110.5 23.3 %collective-permute-start.17 = (bf16[2,256,1024]{2,1,0:T(8,128)(2,1)}, bf16[2,256,1024]{2,1,0:T(8,128)(2,1)}, u32[]{:S(2)}, u32[]{:S(2)}) collective-permute-start(bf16[2,256,1024]{2,1,0:T(8,128)(2,1)} %get-tuple-element.67), channel_id=1, source_target_pairs={{0,32},{8,40},{16,48},{24,56},{32,64},{40,72},{48,80},{56,88},{64,... | collective-permute-start | bytes 3145736 | tf_op jit(solution)/shard_map/ppermute | solution.py:28
  111.6 1.2 copy-start.7
  133.7 17.8 %collective-permute-start.22 = (bf16[512,1024]{1,0:T(8,128)(2,1)}, bf16[512,1024]{1,0:T(8,128)(2,1)}, u32[]{:S(2)}, u32[]{:S(2)}) collective-permute-start(bf16[512,1024]{1,0:T(8,128)(2,1)} %get-tuple-element.83), channel_id=1, source_target_pairs={{0,8},{8,0},{16,24},{24,16},{32,40},{40,32},{48,56},{56,48},{64,72... | collective-permute-start | bytes 3145736 | tf_op jit(solution)/shard_map/ppermute | solution.py:28
  137.8 3.4 %copy-start.3 = (bf16[2,8,256,1024]{3,2,1,0:T(8,128)(2,1)S(1)}, bf16[2,8,256,1024]{3,2,1,0:T(8,128)(2,1)}, u32[]{:S(2)}) copy-start(bf16[2,8,256,1024]{3,2,1,0:T(8,128)(2,1)} %copy-done.2) | copy-start | bytes 25165828
  144.8 2.8 %copy-start.15 = (bf16[2,256,1024]{2,1,0:T(8,128)(2,1)}, bf16[2,256,1024]{2,1,0:T(8,128)(2,1)S(1)}, u32[]{:S(2)}) copy-start(bf16[2,256,1024]{2,1,0:T(8,128)(2,1)S(1)} %get-tuple-element.95) | copy-start | bytes 3145732
  144.8 15.0 %collective-permute-start.20 = (bf16[1,256,1024]{2,1,0:T(8,128)(2,1)}, bf16[1,256,1024]{2,1,0:T(8,128)(2,1)S(1)}, u32[]{:S(2)}, u32[]{:S(2)}) collective-permute-start(bf16[1,256,1024]{2,1,0:T(8,128)(2,1)} %get-tuple-element.80), channel_id=1, source_target_pairs={{0,32},{8,40},{16,48},{24,56},{32,64},{40,72},{48,80},{56,88},{64,... | collective-permute-start | bytes 1572872 | tf_op jit(solution)/shard_map/ppermute | solution.py:28
  146.1 13.8 %collective-permute-start.21 = (bf16[1,256,1024]{2,1,0:T(8,128)(2,1)}, bf16[1,256,1024]{2,1,0:T(8,128)(2,1)S(1)}, u32[]{:S(2)}, u32[]{:S(2)}) collective-permute-start(bf16[1,256,1024]{2,1,0:T(8,128)(2,1)} %get-tuple-element.81), channel_id=1, source_target_pairs={{0,96},{8,104},{16,112},{24,120},{32,0},{40,8},{48,16},{56,24},{64... | collective-permute-start | bytes 1572872 | tf_op jit(solution)/shard_map/ppermute | solution.py:28
  148.8 46.2 %collective-permute-start.26 = (bf16[2,256,1024]{2,1,0:T(8,128)(2,1)}, bf16[2,256,1024]{2,1,0:T(8,128)(2,1)S(1)}, u32[]{:S(2)}, u32[]{:S(2)}) collective-permute-start(bf16[2,256,1024]{2,1,0:T(8,128)(2,1)} %copy-done.15), channel_id=1, source_target_pairs={{0,16},{8,24},{16,0},{24,8},{32,48},{40,56},{48,32},{56,40},{64,80... | collective-permute-start | bytes 3145736 | tf_op jit(solution)/shard_map/ppermute | solution.py:28
  151.5 15.5 %copy-start.9 = (s32[1024,1]{1,0:T(8,128)S(1)}, s32[1024,1]{1,0:T(8,128)}, u32[]{:S(2)}) copy-start(s32[1024,1]{1,0:T(8,128)} %copy-done.8) | copy-start | bytes 12292
  151.5 15.5 %copy-start.10 = (bf16[1024,128]{1,0:T(8,128)(2,1)S(1)}, bf16[1024,128]{1,0:T(8,128)(2,1)}, u32[]{:S(2)}) copy-start(bf16[1024,128]{1,0:T(8,128)(2,1)} %get-tuple-element.100.v_ref) | copy-start | bytes 786436
  151.5 15.5 %copy-start.12 = (bf16[1024,128]{1,0:T(8,128)(2,1)S(1)}, bf16[1024,128]{1,0:T(8,128)(2,1)}, u32[]{:S(2)}) copy-start(bf16[1024,128]{1,0:T(8,128)(2,1)} %copy-done.11) | copy-start | bytes 786436
  151.5 15.5 %copy-start.14 = (bf16[512,1024]{1,0:T(8,128)(2,1)S(1)}, bf16[512,1024]{1,0:T(8,128)(2,1)}, u32[]{:S(2)}) copy-start(bf16[512,1024]{1,0:T(8,128)(2,1)} %q_ref.2) | copy-start | bytes 3145732
  159.9 3.4 %copy-start.4 = (bf16[2,8,256,1024]{3,2,1,0:T(8,128)(2,1)S(1)}, bf16[2,8,256,1024]{3,2,1,0:T(8,128)(2,1)}, u32[]{:S(2)}) copy-start(bf16[2,8,256,1024]{3,2,1,0:T(8,128)(2,1)} %copy-done.2) | copy-start | bytes 25165828
  164.3 30.8 %collective-permute-start.24 = (bf16[2,256,1024]{2,1,0:T(8,128)(2,1)S(1)}, bf16[2,256,1024]{2,1,0:T(8,128)(2,1)S(1)}, u32[]{:S(2)}, u32[]{:S(2)}) collective-permute-start(bf16[2,256,1024]{2,1,0:T(8,128)(2,1)S(1)} %get-tuple-element.87), channel_id=1, source_target_pairs={{0,32},{8,40},{16,48},{24,56},{32,64},{40,72},{48,80},{56,88},{64,... | collective-permute-start | bytes 3145736 | tf_op jit(solution)/shard_map/ppermute | solution.py:28
  164.4 30.6 %collective-permute-start.25 = (bf16[2,256,1024]{2,1,0:T(8,128)(2,1)S(1)}, bf16[2,256,1024]{2,1,0:T(8,128)(2,1)S(1)}, u32[]{:S(2)}, u32[]{:S(2)}) collective-permute-start(bf16[2,256,1024]{2,1,0:T(8,128)(2,1)S(1)} %get-tuple-element.94), channel_id=1, source_target_pairs={{0,96},{8,104},{16,112},{24,120},{32,0},{40,8},{48,16},{56,24},{64... | collective-permute-start | bytes 3145736 | tf_op jit(solution)/shard_map/ppermute | solution.py:28
  167.0 28.0 %slice-start = ((s8[8388608]{0:T(1024)(128)(4,1)}), s8[4194304]{0:T(1024)(128)(4,1)S(1)}, s32[]{:S(2)}) async-start(s8[8388608]{0:T(1024)(128)(4,1)} %bitcast.24), calls=%async_computation | async-start | bytes 8388608
  167.0 28.0 %slice-start.1 = ((s8[8388608]{0:T(1024)(128)(4,1)}), s8[4194304]{0:T(1024)(128)(4,1)S(1)}, s32[]{:S(2)}) async-start(s8[8388608]{0:T(1024)(128)(4,1)} %bitcast.24), calls=%async_computation.1 | async-start | bytes 8388608
  184.3 9.9 %collective-permute-start.23 = (bf16[512,256]{1,0:T(8,128)(2,1)S(1)}, bf16[512,256]{1,0:T(8,128)(2,1)S(1)}, u32[]{:S(2)}, u32[]{:S(2)}) collective-permute-start(bf16[512,256]{1,0:T(8,128)(2,1)S(1)} %pad_maximum_fusion.2), channel_id=1, source_target_pairs={{8,0},{16,8},{24,16},{32,24},{40,32},{48,40},{56,48},{64,56},{72,6... | collective-permute-start | bytes 786440 | tf_op jit(solution)/shard_map/ppermute | solution.py:42

commit v5 on v4

--- a/solution.py
+++ b/solution.py
@@ -13,6 +13,8 @@
 NEG = -1e30
 BF = jnp.bfloat16
 F32 = jnp.float32
+
+PLACES = 64
 
 ZN, YN, KN, LN, XN = 4, 2, 2, 2, 4
 
@@ -123,16 +125,22 @@
 
 
 def bwd_kernel(
-    meta_ref, q_ref, g_ref, k_ref, kt_ref, v_ref, segq_ref, segk_ref, top_ref, sum_ref,
-    dq_ref, dk_ref, dv_ref, bias_ref,
+    n_held, last, meta_ref, q_ref, g_ref, k_ref, kt_ref, v_ref, segq_ref, segk_ref, top_ref, sum_ref,
+    *refs,
 ):
+    dk_in, dv_in = refs[:2] if n_held else (None, None)
+    dq_ref, dk_ref, dv_ref, bias_ref = refs[n_held:]
     count = q_ref.shape[0]
 
     @pl.when(pl.program_id(0) == 0)
     def _():
         fill_bias(bias_ref, segq_ref[...], segk_ref[...], meta_ref[0], count)
-        dk_ref[...] = jnp.zeros_like(dk_ref)
-        dv_ref[...] = jnp.zeros_like(dv_ref)
+        if n_held:
+            dk_ref[...] = dk_in[...]
+            dv_ref[...] = dv_in[...]
+        else:
+            dk_ref[...] = jnp.zeros_like(dk_ref)
+            dv_ref[...] = jnp.zeros_like(dv_ref)
 
     for start, keys in chunk_list(count, 256):
         cols = slice(start, start + 256)
@@ -153,23 +161,27 @@
         dk_ref[:keys, :] += jnp.dot(ds, q, preferred_element_type=F32)
         dv_ref[:keys, :] += jnp.dot(p.astype(BF), g, preferred_element_type=F32)
 
-    @pl.when(pl.program_id(0) == pl.num_programs(0) - 1)
-    def _():
-        dk_ref[...] = dk_ref[...] * SCALE
-
-
-def attend_back(query, grad, key_pair, kt, value_pair, segq, segk, first, top, total):
+    if last:
+
+        @pl.when(pl.program_id(0) == pl.num_programs(0) - 1)
+        def _():
+            dk_ref[...] = dk_ref[...] * SCALE
+
+
+def attend_back(query, grad, key_pair, kt, value_pair, segq, segk, first, top, total, heads, held):
     count, width = query.shape
-    heads = width // HD
+    begin, end = heads
+    last = end == width // HD
     whole = lambda shape: pl.BlockSpec(shape, lambda h, m: (0,) * len(shape))
-    head = pl.BlockSpec((count, HD), lambda h, m: (0, h))
-    stat = pl.BlockSpec((1, 1, count), lambda h, m: (h, 0, 0))
+    head = pl.BlockSpec((count, HD), lambda h, m: (0, h + begin))
+    stat = pl.BlockSpec((1, 1, count), lambda h, m: (h + begin, 0, 0))
     pair = whole((2 * count, HD))
+    earlier = () if held is None else (held[1], held[2], held[0])
     return pl.pallas_call(
-        bwd_kernel,
+        functools.partial(bwd_kernel, len(earlier), last),
         grid_spec=pltpu.PrefetchScalarGridSpec(
             num_scalar_prefetch=1,
-            grid=(heads,),
+            grid=(end - begin,),
             in_specs=[
                 head,
                 head,
@@ -180,7 +192,8 @@
                 whole((2 * count, 1)),
                 stat,
                 stat,
-            ],
+            ]
+            + ([pair, pair, pl.BlockSpec(memory_space=pl.ANY)] if earlier else []),
             out_specs=[head, pair, pair],
             scratch_shapes=[pltpu.VMEM((2 * count, count), F32)],
         ),
@@ -189,17 +202,18 @@
             jax.ShapeDtypeStruct((2 * count, HD), F32),
             jax.ShapeDtypeStruct((2 * count, HD), F32),
         ],
+        input_output_aliases={12: 0} if earlier else {},
         compiler_params=params(22),
         cost_estimate=pl.CostEstimate(
-            flops=heads * 10 * 2 * 2 * count * count * HD,
-            bytes_accessed=12 * 2**20,
-            transcendentals=heads * 2 * count * count,
+            flops=(end - begin) * 10 * 2 * 2 * count * count * HD,
+            bytes_accessed=6 * 2**20,
+            transcendentals=(end - begin) * 2 * count * count,
         ),
         name="attend_back",
-    )(first, query, grad, key_pair, kt, value_pair, segq, segk, top, total)
-
-
-def proj_kernel(n_in, held, meta_ref, *refs):
+    )(first, query, grad, key_pair, kt, value_pair, segq, segk, top, total, *earlier)
+
+
+def proj_kernel(n_in, held, plan, meta_ref, *refs):
     pieces, a_ref = refs[:n_in], refs[n_in]
     refs = refs[n_in + 1 + held:]
     buffer_ref, taken = refs[0], refs[1:-3]
@@ -225,17 +239,18 @@
     def _():
         for j in range(n_in):
             put(j).wait()
-        takes = [
-            pltpu.make_async_copy(buffer_ref.at[:, meta_ref[n_in + i]], ref, take_sems.at[i])
-            for i, ref in enumerate(taken)
-        ]
+        takes = []
+        for i, (out, start, at, half, first, count) in enumerate(plan):
+            source = buffer_ref.at[half, meta_ref[n_in + at], pl.ds(first, count)]
+            target = taken[out].at[pl.ds(start, count)]
+            takes.append(pltpu.make_async_copy(source, target, take_sems.at[i]))
         for take in takes:
             take.start()
         for take in takes:
             take.wait()
 
 
-def project(pieces, a_pair, blocks, buffer, n_taken=0):
+def project(pieces, a_pair, blocks, buffer, plan=()):
     tokens, width = a_pair.shape
     depth = pieces[0].shape[1]
     n_blocks = len(pieces)
@@ -244,8 +259,10 @@
     there = pl.BlockSpec(memory_space=pltpu.HBM)
     operands = (*pieces, a_pair) + ((buffer,) if held else ())
     shape = (2, depth // 2, width)
+    n_taken = 1 + max((entry[0] for entry in plan), default=-1)
+    taken = [(sum(e[5] for e in plan if e[0] == i), width) for i in range(n_taken)]
     out = pl.pallas_call(
-        functools.partial(proj_kernel, n_blocks, held),
+        functools.partial(proj_kernel, n_blocks, held, plan),
         grid_spec=pltpu.PrefetchScalarGridSpec(
             num_scalar_prefetch=1,
             grid=(n_blocks,),
@@ -254,11 +271,11 @@
             scratch_shapes=[
                 pltpu.VMEM((n_blocks, *shape), BF),
                 pltpu.SemaphoreType.DMA((n_blocks,)),
-                pltpu.SemaphoreType.DMA((max(n_taken, 1),)),
+                pltpu.SemaphoreType.DMA((max(len(plan), 1),)),
             ],
         ),
-        out_shape=[jax.ShapeDtypeStruct((2, 8, depth // 2, width), BF)]
-        + [jax.ShapeDtypeStruct(shape, BF)] * n_taken,
+        out_shape=[jax.ShapeDtypeStruct((2, PLACES, depth // 2, width), BF)]
+        + [jax.ShapeDtypeStruct(t, BF) for t in taken],
         input_output_aliases={n_blocks + 2: 0} if held else {},
         compiler_params=params(16),
         cost_estimate=pl.CostEstimate(
@@ -363,9 +380,10 @@
     )(meta, *g_pieces, *w_pieces)
 
 
-def add_kernel(n_terms, plan, meta_ref, buffer_ref, *refs):
-    terms, outs = refs[:n_terms], refs[n_terms:n_terms + len(plan)]
-    blocks, sems = refs[n_terms + len(plan):]
+def add_kernel(n_terms, plan, joined, meta_ref, buffer_ref, *refs):
+    terms, outs = refs[:n_terms], refs[n_terms:-2]
+    blocks, sems = refs[-2:]
+    rows = blocks.shape[2]
     copies = [
         pltpu.make_async_copy(buffer_ref.at[:, meta_ref[n]], blocks.at[n], sems.at[n])
         for n in range(blocks.shape[0])
@@ -374,28 +392,27 @@
         copy.start()
     for copy in copies:
         copy.wait()
-    for out_ref, (block, half, extra) in zip(outs, plan):
-        for place, part in enumerate((0, 1) if half is None else (half,)):
-            value = blocks[block, part].astype(F32)
-            for term, at in extra:
-                if at is None:
-                    value = value + terms[term][part].astype(F32)
-                elif at == part:
-                    value = value + terms[term][0].astype(F32)
-            out_ref[place] = value.astype(BF)
-
-
-def add_blocks(buffer, blocks, terms, plan):
+    for n, (block, half, extra) in enumerate(plan):
+        value = blocks[block, half].astype(F32)
+        for term, first in extra:
+            value = value + terms[term][first:first + rows, :].astype(F32)
+        if joined:
+            outs[0][n * rows:(n + 1) * rows, :] = value.astype(BF)
+        else:
+            outs[n][...] = value.astype(BF)
+
+
+def add_blocks(buffer, blocks, terms, plan, joined=False):
     _, _, rows, width = buffer.shape
     here = pl.BlockSpec(memory_space=pltpu.VMEM)
-    shapes = [(2 if half is None else 1, rows, width) for _, half, _ in plan]
+    shapes = [(len(plan) * rows, width)] if joined else [(rows, width)] * len(plan)
     return pl.pallas_call(
-        functools.partial(add_kernel, len(terms), plan),
+        functools.partial(add_kernel, len(terms), plan, joined),
         grid_spec=pltpu.PrefetchScalarGridSpec(
             num_scalar_prefetch=1,
             grid=(1,),
             in_specs=[pl.BlockSpec(memory_space=pltpu.HBM)] + [here] * len(terms),
-            out_specs=[here] * len(plan),
+            out_specs=[here] * len(shapes),
             scratch_shapes=[
                 pltpu.VMEM((blocks.shape[0], 2, rows, width), BF),
                 pltpu.SemaphoreType.DMA((blocks.shape[0],)),
@@ -408,6 +425,49 @@
         ),
         name="add_blocks",
     )(blocks, buffer, *terms)
+
+
+def last_kernel(meta_ref, buffer_ref, across, nup, ndn, rup, up2, rdn, dn2, out_ref, block, sem):
+    copy = pltpu.make_async_copy(buffer_ref.at[:, meta_ref[0]], block, sem)
+    copy.start()
+    copy.wait()
+    half, quarter = nup.shape[0], up2.shape[0]
+    for part in range(2):
+        for n in range(2):
+            rows = slice(n * quarter, (n + 1) * quarter)
+            place = slice(part * half + n * quarter, part * half + (n + 1) * quarter)
+            up, dn = nup[rows, :], ndn[rows, :]
+            if part == 1:
+                up = up2[...] if n else rup[2 * half:, :]
+            else:
+                dn = dn2[...] if n else rdn[2 * half:, :]
+            out_ref[place, :] = (
+                block[part, rows].astype(F32)
+                + across[place, :].astype(F32)
+                + up.astype(F32)
+                + dn.astype(F32)
+            ).astype(BF)
+
+
+def last_sum(buffer, place, *terms):
+    _, _, rows, width = buffer.shape
+    here = pl.BlockSpec(memory_space=pltpu.VMEM)
+    return pl.pallas_call(
+        last_kernel,
+        grid_spec=pltpu.PrefetchScalarGridSpec(
+            num_scalar_prefetch=1,
+            grid=(1,),
+            in_specs=[pl.BlockSpec(memory_space=pltpu.HBM)] + [here] * len(terms),
+            out_specs=pl.BlockSpec((2 * rows, width), lambda i, m: (0, 0)),
+            scratch_shapes=[pltpu.VMEM((2, rows, width), BF), pltpu.SemaphoreType.DMA],
+        ),
+        out_shape=jax.ShapeDtypeStruct((2 * rows, width), BF),
+        compiler_params=params(12),
+        cost_estimate=pl.CostEstimate(
+            flops=2**21, bytes_accessed=5 * 2**20, transcendentals=0
+        ),
+        name="last_sum",
+    )(place, buffer, *terms)
 
 
 def local(query_rows, key_rows, value_rows, output_grad, out_proj, segment_ids):
@@ -430,7 +490,6 @@
     g_give = lax.dynamic_slice_in_dim(output_grad, (1 - k) * half_d, half_d, 1)
     g0 = jnp.concatenate([g_keep, move_row(g_give, dk=1)], 0)
     kv = jnp.concatenate([key_rows, value_rows], 1)
-    (kv,) = tied((kv,), g0)
     kv_earlier = passed_along(kv, "row", 1)
 
     gxm = move_col(g0, dx=1)
@@ -470,9 +529,8 @@
         None,
     )
 
+    go = move_col(gxm, dx=1)
     gyxm, gyxp, wo, wy, proj = tied((gyxm, gyxp, wo, wy, proj))
-
-    go = move_col(gxm, dx=1)
     gyo = move_col(gyxp, dx=-1)
     wyzm = move_row(wy, dz=1)
     wyzp = move_row(wy, dz=-1)
@@ -480,18 +538,31 @@
 
     proj = project([gyxm, gyxp], a_pair, ints(gblock(1, -1), gblock(1, 1)), proj)
 
-    go, gyo, wyzm, wyzp, wyo, proj = tied((go, gyo, wyzm, wyzp, wyo, proj))
-
-    proj, give_up, give_dn, give_far = project(
+    go, gyo, proj = tied((go, gyo, proj))
+
+    q = hw // 2
+    proj, give_far, give_up, give_dn, up2, dn2 = project(
         [go, gyo],
         a_pair,
-        ints(gblock(0, 2), gblock(1, 2), wblock(1, 1), wblock(-1, 1), wblock(2, 1)),
+        ints(
+            gblock(0, 2), gblock(1, 2),
+            wblock(2, 1), wblock(1, 1), wblock(-1, 1), wblock(1, 0), wblock(-1, 0),
+        ),
         proj,
-        3,
-    )
+        (
+            (0, 0, 0, 0, 0, hw), (0, hw, 0, 1, 0, hw),
+            (1, 0, 1, 0, 0, hw), (1, hw, 1, 1, 0, hw), (1, 2 * hw, 3, 1, 0, q),
+            (2, 0, 2, 0, 0, hw), (2, hw, 2, 1, 0, hw), (2, 2 * hw, 4, 0, 0, q),
+            (3, 0, 3, 1, q, q),
+            (4, 0, 4, 0, q, q),
+        ),
+    )
+    give_far, give_up, give_dn, wyzm, wyzp, wyo = tied(
+        (give_far, give_up, give_dn, wyzm, wyzp, wyo)
+    )
+    ry = move_row(give_far, dyh=1)
     rup = move_row(give_up, dz=1)
     rdn = move_row(give_dn, dz=-1)
-    ry = move_row(give_far, dyh=1)
 
     g_pieces = [g0, gxm, gxp, gy, gyxm, gyxp, go, gyo]
     gplan = [(i, p * h, i, p) for i in range(8) for p in range(2)]
@@ -506,45 +577,56 @@
     (meta,) = tied((meta,), give_up)
     grad_own, grad_give = attn_grad_part(g_pieces, gplan, w_pieces, wplan, meta)
 
-    rup, rdn, ry, grad_own, grad_give = tied((rup, rdn, ry, grad_own, grad_give))
-
-    across, far_up, far_dn = add_blocks(
-        proj,
-        ints(wblock(0, 1), wblock(2, 0)),
-        [rup, rdn, ry],
-        [(0, None, ((0, None), (1, None))), (1, 0, ((2, None),)), (1, 1, ((2, None),))],
-    )
+    ry, grad_own, grad_give = tied((ry, grad_own, grad_give))
+
+    far_up, far_dn = add_blocks(proj, ints(wblock(2, 0)), [ry], ((0, 0, ((0, 0),)), (0, 1, ((0, hw),))))
     fup = move_row(far_up, dz=1)
     fdn = move_row(far_dn, dz=-1)
+    grad_got = move_row(grad_give, dk=1)
+    rup, rdn = tied((rup, rdn), far_up)
+    (across,) = add_blocks(
+        proj,
+        ints(wblock(0, 1)),
+        [rup, rdn],
+        ((0, 0, ((0, 0), (1, 0))), (0, 1, ((0, hw), (1, hw)))),
+        joined=True,
+    )
     across = move_row(across, dyh=1)
-    grad_got = move_row(grad_give, dk=1)
+    up2, dn2 = tied((up2, dn2), far_up)
+    up2 = move_row(up2, dz=1)
+    dn2 = move_row(dn2, dz=-1)
+
     attn_grad = (grad_own + grad_got.astype(F32)).astype(BF)
-
-    fup, fdn, attn_grad = tied((fup, fdn, attn_grad))
+    (attn_grad,) = tied((attn_grad,), rup)
+    part = functools.partial(
+        attend_back, query_rows, attn_grad, key_pair, key_t, value_pair, segq, segk, first, top, total
+    )
+    heads = query_rows.shape[1] // HD
+    cut = 3 * heads // 8
+    held = part((0, cut), None)
+
+    fup, fdn, *held = tied((fup, fdn, *held))
 
     near_up, near_dn = add_blocks(
         proj,
         ints(wblock(1, 0), wblock(-1, 0)),
         [fup, fdn],
-        [(0, None, ((0, 0),)), (1, None, ((1, 1),))],
+        ((0, 0, ((0, 0),)), (1, 1, ((1, 0),))),
     )
     nup = move_row(near_up, dz=1)
     ndn = move_row(near_dn, dz=-1)
 
-    (attn_grad,) = tied((attn_grad,), near_up)
-    query_grad, dkey, dvalue = attend_back(
-        query_rows, attn_grad, key_pair, key_t, value_pair, segq, segk, first, top, total
-    )
+    *held, up2, dn2 = tied((*held, up2, dn2), near_up)
+    query_grad, dkey, dvalue = part((cut, heads), held)
+    dkey, dvalue, nup, ndn = tied((dkey, dvalue, nup, ndn))
     back = passed_along(
         jnp.concatenate([dkey[:count], dvalue[:count]], 1).astype(BF), "row", -1
     ).astype(F32)
     key_grad = (dkey[count:] + back[:, :HD]).astype(BF)
     value_grad = (dvalue[count:] + back[:, HD:]).astype(BF)
 
-    (proj_grad,) = add_blocks(
-        proj, ints(wblock(0, 0)), [nup, ndn, across], [(0, None, ((0, None), (1, None), (2, None)))]
-    )
-    return (query_grad, key_grad, value_grad, proj_grad.reshape(2 * hw, out_proj.shape[1]))
+    proj_grad = last_sum(proj, ints(wblock(0, 0)), across, nup, ndn, rup, up2, rdn, dn2)
+    return (query_grad, key_grad, value_grad, proj_grad)
 
 
 def solution(mesh):

time: 197 us -> 180 us (0.914)
  waiting for transfers between devices: 55.1 us -> 31.3 us
  local copies, waits for them, and re-layouts: 25.5 us -> 16.4 us
  Pallas kernels: 72.6 us -> 80.6 us
  starting transfers between devices: 39.3 us -> 45.5 us
    ppermute x18 -> x20, waiting for transfers between devices: 33.2 us -> 13.4 us  [move_row(): return lax.ppermute(value, 'row', pairs)]
    pallas_call x7 -> x9, Pallas kernels: 42.7 us -> 50.4 us  [the longest x3 22.8 us: project(): pl.pallas_call(functools.partial(proj_kernel, n_blocks, held, plan), grid...]
    unnamed x42 -> x50, local copies, waits for them, and re-layouts: 19.4 us -> 12.2 us
    ppermute x2, waiting for transfers between devices: 6.6 us -> 2.81 us  [passed_along(): lax.ppermute(value, axis, [(source, source + steps) for source in range(f...]
    ppermute x7, starting transfers between devices: 4.64 us -> 8.25 us  [move_col(): return lax.ppermute(value, 'col', pairs)]
    ppermute x18 -> x20, starting transfers between devices: 26.2 us -> 28.8 us  [move_row(): return lax.ppermute(value, 'row', pairs)]
  transfers between devices with their start and end apart: 27 -> 29, of which waited for: 16 -> 13; matrix products, arithmetic and copies ran while one was open for 5% -> 4% of each run, Pallas kernels for 33% -> 45%
where the time goes in v5:
time: 180 us; the launch traced here: 179 us
  Pallas kernels  80.6 us (45%)
  starting transfers between devices  45.5 us (25%)
  waiting for transfers between devices  31.3 us (17%)
  local copies, waits for them, and re-layouts  16.4 us (9%)
  other arithmetic  3.95 us (2%)
    ppermute x20, starting transfers between devices, move_row(): return lax.ppermute(value, 'row', pairs)  28.8 us
    pallas_call x3, Pallas kernels, project(): pl.pallas_call(functools.partial(proj_kernel, n_blocks, held, plan), grid...  22.8 us
    pallas_call x2, Pallas kernels, attend_back(): pl.pallas_call(functools.partial(bwd_kernel, len(earlier), last), grid_sp...  18 us
    pallas_call x1, Pallas kernels, attn_grad_part(): pl.pallas_call(kernel, grid_spec=pltpu.PrefetchScalarGridSpec(num_scalar_...  15.3 us
    ppermute x7, waiting for transfers between devices, move_col(): return lax.ppermute(value, 'col', pairs)  15 us
    pallas_call x1, Pallas kernels, attend(): pl.pallas_call(fwd_kernel, grid_spec=pltpu.PrefetchScalarGridSpec(num_sca...  14.9 us
    ppermute x20, waiting for transfers between devices, move_row(): return lax.ppermute(value, 'row', pairs)  13.4 us
    unnamed x50, local copies, waits for them, and re-layouts  12.2 us
  transfers between devices with their start and end apart: 29, of which 13 were waited for; matrix products, arithmetic and copies ran while one was open for 4% of the time, Pallas kernels for 45%

profile of v5, /device:TPU:1, one launch (start us, length us, event | category | flops | bytes accessed | tf_op | source)
XLA Modules:
  0.0 178.8 jit_solution(11727639812508601019)
XLA Ops:
  0.7 1.3 constant_dynamic-slice_fusion.1
  2.0 1.5 collective-permute-start
  3.6 4.8 %collective-permute-start.6 = (bf16[512,256]{1,0:T(8,128)(2,1)S(1)}, bf16[512,256]{1,0:T(8,128)(2,1)S(1)}, u32[]{:S(2)}, u32[]{:S(2)}) collective-permute-start(bf16[512,256]{1,0:T(8,128)(2,1)S(1)} %constant_dynamic-update-slice_fusion), channel_id=1, source_target_pairs={{0,8},{8,16},{16,24},{24,32},{32,40},{40,48},{48,56},{56,64},{64,7... | collective-permute-start | bytes 786440 | tf_op jit(solution)/shard_map/ppermute | solution.py:44
  8.4 1.7 collective-permute-start.4
  10.1 2.2 %collective-permute-start.5 = (bf16[512,1024]{1,0:T(8,128)(2,1)}, bf16[512,1024]{1,0:T(8,128)(2,1)}, u32[]{:S(2)}, u32[]{:S(2)}) collective-permute-start(bf16[512,1024]{1,0:T(8,128)(2,1)} %refs_8_.1), channel_id=1, source_target_pairs={{0,96},{8,104},{16,112},{24,120},{32,0},{40,8},{48,16},{56,24},{64... | collective-permute-start | bytes 3145736 | tf_op jit(solution)/shard_map/ppermute | solution.py:30
  12.4 1.3 collective-permute-start.1
  13.7 1.5 collective-permute-start.2
  15.2 0.4 collective-permute-start.3
  15.6 0.8 fusion.3
  16.4 0.2 copy.17.segk_ref
  16.7 1.2 pad_maximum_fusion.1
  18.1 1.2 copy-done.15
  19.3 14.9 %attend.1 = (bf16[512,1024]{1,0:T(8,128)(2,1)}, f32[8,1,512]{2,1,0:T(1,128)S(1)}, f32[8,1,512]{2,1,0:T(1,128)S(1)}) custom-call(s32[1]{0:T(128)} %bitcast.meta_ref, bf16[512,1024]{1,0:T(8,128)(2,1)S(1)} %copy-done.15, bf16[1024,128]{1,0:T(8,128)(2,1)S(1)} %get-tuple-element.139.k_ref, bf16[128,1024]{1,0:T(8,128)(2,1)S(1)} %copy.16.vt_ref, ...), custom_call_target="tpu_custom_call" | custom-call | flops 4294967296 | bytes 8388608 | tf_op jit(solution)/shard_map/attend/pallas_call | solution.py:97
  34.4 2.7 %collective-permute-done.1.refs_1_ = bf16[1024,512]{1,0:T(8,128)(2,1)} collective-permute-done((bf16[1024,512]{1,0:T(8,128)(2,1)S(1)}, bf16[1024,512]{1,0:T(8,128)(2,1)}, u32[]{:S(2)}, u32[]{:S(2)}) %collective-permute-start.1) | collective-permute-done | bytes 1048608 | tf_op jit(solution)/shard_map/ppermute | solution.py:38
  37.1 0.6 collective-permute-done.2.refs_2_
  37.7 1.0 copy-done.4
  38.7 0.5 collective-permute-done.3.refs_3_
  39.2 2.4 %collective-permute-start.11 = (bf16[512,1024]{1,0:T(8,128)(2,1)}, bf16[512,1024]{1,0:T(8,128)(2,1)}, u32[]{:S(2)}, u32[]{:S(2)}) collective-permute-start(bf16[512,1024]{1,0:T(8,128)(2,1)} %refs_8_.1), channel_id=1, source_target_pairs={{0,16},{8,24},{16,0},{24,8},{32,48},{40,56},{48,32},{56,40},{64,80... | collective-permute-start | bytes 3145736 | tf_op jit(solution)/shard_map/ppermute | solution.py:30
  41.5 0.4 collective-permute-start.10
  42.1 2.5 %collective-permute-start.9 = (bf16[1024,512]{1,0:T(8,128)(2,1)}, bf16[1024,512]{1,0:T(8,128)(2,1)}, u32[]{:S(2)}, u32[]{:S(2)}) collective-permute-start(bf16[1024,512]{1,0:T(8,128)(2,1)} %collective-permute-done.3.refs_3_), channel_id=1, source_target_pairs={{0,3},{1,0},{2,1},{3,2},{4,7},{5,4},{6,5},{7,6},{8,11},{9,8},{10,9... | collective-permute-start | bytes 3145736 | tf_op jit(solution)/shard_map/ppermute | solution.py:38
  44.7 1.4 constant_dynamic-update-slice_fusion.3
  46.2 1.3 constant_dynamic-update-slice_fusion.2.refs_4_.refs_2_
  47.5 8.4 %project.3.refs_3_ = bf16[2,64,256,1024]{3,2,1,0:T(8,128)(2,1)} custom-call(s32[4]{0:T(128)S(1)} %pad_add_fusion.1.meta_ref, bf16[1024,512]{1,0:T(8,128)(2,1)S(1)} %pad_maximum_fusion.refs_0_, bf16[1024,512]{1,0:T(8,128)(2,1)} %collective-permute-done.1.refs_1_, bf16[1024,512]{1,0:T(8,128)(2,1)S(1)} %copy-done.5, ...), custom_call_target="tpu_custom_call" | custom-call | flops 4294967296 | bytes 10485760 | tf_op jit(solution)/shard_map/project/pallas_call | solution.py:264
  55.9 9.3 %collective-permute-done.11.refs_11_ = bf16[512,1024]{1,0:T(8,128)(2,1)} collective-permute-done((bf16[512,1024]{1,0:T(8,128)(2,1)}, bf16[512,1024]{1,0:T(8,128)(2,1)}, u32[]{:S(2)}, u32[]{:S(2)}) %collective-permute-start.11) | collective-permute-done | bytes 1048608 | tf_op jit(solution)/shard_map/ppermute | solution.py:30
  65.2 2.3 %collective-permute-done.10.refs_15_ = bf16[512,1024]{1,0:T(8,128)(2,1)} collective-permute-done((bf16[512,1024]{1,0:T(8,128)(2,1)}, bf16[512,1024]{1,0:T(8,128)(2,1)}, u32[]{:S(2)}, u32[]{:S(2)}) %collective-permute-start.10) | collective-permute-done | bytes 1048608 | tf_op jit(solution)/shard_map/ppermute | solution.py:30
  67.7 2.4 %collective-permute-start.13 = (bf16[1024,512]{1,0:T(8,128)(2,1)}, bf16[1024,512]{1,0:T(8,128)(2,1)S(1)}, u32[]{:S(2)}, u32[]{:S(2)}) collective-permute-start(bf16[1024,512]{1,0:T(8,128)(2,1)} %collective-permute-done.9.refs_1_.refs_5_), channel_id=1, source_target_pairs={{0,3},{1,0},{2,1},{3,2},{4,7},{5,4},{6,5},{7,6},{8,11},{9,8},{10,9... | collective-permute-start | bytes 3145736 | tf_op jit(solution)/shard_map/ppermute | solution.py:38
  70.0 1.3 collective-permute-start.14
  71.4 1.3 collective-permute-start.15
  72.7 1.3 collective-permute-start.16
  74.1 5.8 %project.4.refs_3_ = bf16[2,64,256,1024]{3,2,1,0:T(8,128)(2,1)} custom-call(s32[2]{0:T(128)S(1)} %pad_add_fusion.2.meta_ref, bf16[1024,512]{1,0:T(8,128)(2,1)} %collective-permute-done.8.refs_0_.refs_4_, bf16[1024,512]{1,0:T(8,128)(2,1)} %collective-permute-done.9.refs_1_.refs_5_, ...), custom_call_target="tpu_custom_call", output_to_operand_aliasing={{}: (4, {})} | custom-call | flops 2147483648 | bytes 6291456 | tf_op jit(solution)/shard_map/project/pallas_call | solution.py:264
  79.9 10.2 %collective-permute-done.7.refs_0_.refs_6_ = bf16[1024,512]{1,0:T(8,128)(2,1)} collective-permute-done((bf16[1024,512]{1,0:T(8,128)(2,1)}, bf16[1024,512]{1,0:T(8,128)(2,1)}, u32[]{:S(2)}, u32[]{:S(2)}) %collective-permute-start.7) | collective-permute-done | bytes 1048608 | tf_op jit(solution)/shard_map/ppermute | solution.py:38
  90.1 0.9 collective-permute-done.13.refs_1_.refs_7_
  91.0 8.6 %project.5 = (bf16[2,64,256,1024]{3,2,1,0:T(8,128)(2,1)}, bf16[512,1024]{1,0:T(8,128)(2,1)}, bf16[640,1024]{1,0:T(8,128)(2,1)S(1)}, bf16[640,1024]{1,0:T(8,128)(...) custom-call(s32[7]{0:T(128)S(1)} %stack.95.meta_ref, ...), custom_call_target="tpu_custom_call", output_to_operand_aliasing={{0}: (4, {})} | custom-call | flops 2147483648 | bytes 6291456 | tf_op jit(solution)/shard_map/project/pallas_call | solution.py:264
  99.7 1.1 copy-done.13
  100.8 1.1 copy-done.14
  101.8 0.7 copy-done.17
  102.5 0.7 copy-done.19
  103.2 1.4 collective-permute-start.17
  104.7 1.5 collective-permute-start.19
  106.2 1.2 collective-permute-start.20
  107.4 1.2 copy-done.1
  108.7 1.2 copy-done.6
  109.9 1.2 copy-done.8
  111.1 15.3 %attn_grad.1 = (f32[512,1024]{1,0:T(8,128)S(1)}, bf16[512,1024]{1,0:T(8,128)(2,1)}) custom-call(s32[16]{0:T(128)S(1)} %stack.107.meta_ref, bf16[1024,512]{1,0:T(8,128)(2,1)S(1)} %copy-done.1, bf16[1024,512]{1,0:T(8,128)(2,1)} %collective-permute-done.1.refs_1_, bf16[1024,512]{1,0:T(8,128)(2,1)S(1)} %copy-done.6, ...), custom_call_target="tpu_custom_call" | custom-call | flops 8589934592 | bytes 20971520 | tf_op jit(solution)/shard_map/attn_grad/pallas_call | solution.py:354
  126.4 1.4 copy-done.2
  127.8 3.5 %collective-permute-start.18 = (bf16[512,1024]{1,0:T(8,128)(2,1)}, bf16[512,1024]{1,0:T(8,128)(2,1)}, u32[]{:S(2)}, u32[]{:S(2)}) collective-permute-start(bf16[512,1024]{1,0:T(8,128)(2,1)} %get-tuple-element.97), channel_id=1, source_target_pairs={{0,8},{8,0},{16,24},{24,16},{32,40},{40,32},{48,56},{56,48},{64,72... | collective-permute-start | bytes 3145736 | tf_op jit(solution)/shard_map/ppermute | solution.py:30
  131.5 2.8 %add_blocks.3 = (bf16[256,1024]{1,0:T(8,128)(2,1)S(1)}, bf16[256,1024]{1,0:T(8,128)(2,1)S(1)}) custom-call(s32[1]{0:T(128)} %bitcast.19.meta_ref, bf16[2,64,256,1024]{3,2,1,0:T(8,128)(2,1)} %get-tuple-element.99.buffer_ref, bf16[512,1024]{1,0:T(8,128)(2,1)} %collective-permute-done.17.refs_0_), custom_call_target="tpu_custom_call" | custom-call | flops 2097152 | bytes 5242880 | tf_op jit(solution)/shard_map/add_blocks/pallas_call | solution.py:409
  134.3 0.9 collective-permute-start.21
  135.1 1.9 %collective-permute-start.22 = (bf16[256,1024]{1,0:T(8,128)(2,1)S(1)}, bf16[256,1024]{1,0:T(8,128)(2,1)S(1)}, u32[]{:S(2)}, u32[]{:S(2)}) collective-permute-start(bf16[256,1024]{1,0:T(8,128)(2,1)S(1)} %get-tuple-element.106), channel_id=1, source_target_pairs={{0,96},{8,104},{16,112},{24,120},{32,0},{40,8},{48,16},{56,24},{64... | collective-permute-start | bytes 1572872 | tf_op jit(solution)/shard_map/ppermute | solution.py:30
  137.0 1.4 collective-permute-start.23
  138.4 1.4 collective-permute-start.24
  139.8 1.6 add_blocks.5
  141.4 2.1 %collective-permute-start.28 = (bf16[512,1024]{1,0:T(8,128)(2,1)S(1)}, bf16[512,1024]{1,0:T(8,128)(2,1)S(1)}, u32[]{:S(2)}, u32[]{:S(2)}) collective-permute-start(bf16[512,1024]{1,0:T(8,128)(2,1)S(1)} %add_blocks.5), channel_id=1, source_target_pairs={{0,16},{8,24},{16,0},{24,8},{32,48},{40,56},{48,32},{56,40},{64,80... | collective-permute-start | bytes 3145736 | tf_op jit(solution)/shard_map/ppermute | solution.py:30
  143.5 1.6 add_convert_fusion.g_ref
  145.1 7.0 %attend_back.2 = (bf16[512,1024]{1,0:T(8,128)(2,1)}, f32[1024,128]{1,0:T(8,128)S(1)}, f32[1024,128]{1,0:T(8,128)S(1)}) custom-call(s32[1]{0:T(128)} %bitcast.meta_ref, bf16[512,1024]{1,0:T(8,128)(2,1)S(1)} %copy-done.16, bf16[512,1024]{1,0:T(8,128)(2,1)S(1)} %add_convert_fusion.g_ref, bf16[1024,128]{1,0:T(8,128)(2,1)S(1)} %copy-done.10, ...), custom_call_target="tpu_custom_call" | custom-call | flops 4026531840 | bytes 6291456 | tf_op jit(solution)/shard_map/attend_back/pallas_call | solution.py:180
  152.1 2.4 %add_blocks.4 = (bf16[256,1024]{1,0:T(8,128)(2,1)S(1)}, bf16[256,1024]{1,0:T(8,128)(2,1)S(1)}) custom-call(s32[2]{0:T(128)S(1)} %pad_add_fusion.3.meta_ref, bf16[2,64,256,1024]{3,2,1,0:T(8,128)(2,1)} %get-tuple-element.99.buffer_ref, bf16[256,1024]{1,0:T(8,128)(2,1)S(1)} %collective-permute-done.21.refs_0_, bf16[256,1024]{1,0:T(8,128)(2,1)S(1)} %collective-permute-done.22.refs_1_), custom_call_target="tpu_custom_call" | custom-call | flops 2097152 | bytes 5242880 | tf_op jit(solution)/shard_map/add_blocks/pallas_call | solution.py:409
  154.7 1.3 collective-permute-done.24.dn2
  156.0 1.3 collective-permute-start.26
  157.3 11.0 %attend_back.3 = (bf16[512,1024]{1,0:T(8,128)(2,1)}, f32[1024,128]{1,0:T(8,128)S(1)}, f32[1024,128]{1,0:T(8,128)S(1)}) custom-call(s32[1]{0:T(128)} %bitcast.meta_ref, bf16[512,1024]{1,0:T(8,128)(2,1)S(1)} %copy-done.16, bf16[512,1024]{1,0:T(8,128)(2,1)S(1)} %add_convert_fusion.g_ref, ...), custom_call_target="tpu_custom_call", output_to_operand_aliasing={{0}: (12, {})} | custom-call | flops 6710886400 | bytes 6291456 | tf_op jit(solution)/shard_map/attend_back/pallas_call | solution.py:180
  168.4 0.3 collective-permute-done.26.ndn
  168.8 3.6 %collective-permute-start.27 = (bf16[512,256]{1,0:T(8,128)(2,1)S(1)}, bf16[512,256]{1,0:T(8,128)(2,1)S(1)}, u32[]{:S(2)}, u32[]{:S(2)}) collective-permute-start(bf16[512,256]{1,0:T(8,128)(2,1)S(1)} %pad_maximum_fusion.2), channel_id=1, source_target_pairs={{8,0},{16,8},{24,16},{32,24},{40,32},{48,40},{56,48},{64,56},{72,6... | collective-permute-start | bytes 786440 | tf_op jit(solution)/shard_map/ppermute | solution.py:44
  172.4 2.8 %last_sum.1 = bf16[512,1024]{1,0:T(8,128)(2,1)} custom-call(s32[1]{0:T(128)} %bitcast.17.meta_ref, bf16[2,64,256,1024]{3,2,1,0:T(8,128)(2,1)} %get-tuple-element.99.buffer_ref, bf16[512,1024]{1,0:T(8,128)(2,1)S(1)} %collective-permute-done.28.across, bf16[256,1024]{1,0:T(8,128)(2,1)S(1)} %collective-permute-done.25.nup, ...), custom_call_target="tpu_custom_call" | custom-call | flops 2097152 | bytes 5242880 | tf_op jit(solution)/shard_map/last_sum/pallas_call | solution.py:455
  175.1 2.8 %collective-permute-done.27 = bf16[512,256]{1,0:T(8,128)(2,1)S(1)} collective-permute-done((bf16[512,256]{1,0:T(8,128)(2,1)S(1)}, bf16[512,256]{1,0:T(8,128)(2,1)S(1)}, u32[]{:S(2)}, u32[]{:S(2)}) %collective-permute-start.27) | collective-permute-done | bytes 262176 | tf_op jit(solution)/shard_map/ppermute | solution.py:44
  178.0 0.8 fusion.1
  (76 shorter events, 1.7 us)
Async XLA Ops:
  0.6 2.9 %copy-start.22 = (bf16[512,128]{1,0:T(8,128)(2,1)S(1)}, bf16[512,128]{1,0:T(8,128)(2,1)}, u32[]{:S(2)}) copy-start(bf16[512,128]{1,0:T(8,128)(2,1)} %param.7) | copy-start | bytes 393220
  0.6 2.9 %copy-start.23 = (bf16[512,128]{1,0:T(8,128)(2,1)S(1)}, bf16[512,128]{1,0:T(8,128)(2,1)}, u32[]{:S(2)}) copy-start(bf16[512,128]{1,0:T(8,128)(2,1)} %param.8) | copy-start | bytes 393220
  2.0 10.3 %collective-permute-start = (bf16[512,512]{1,0:T(8,128)(2,1)S(1)}, bf16[512,512]{1,0:T(8,128)(2,1)S(1)}, u32[]{:S(2)}, u32[]{:S(2)}) collective-permute-start(bf16[512,512]{1,0:T(8,128)(2,1)S(1)} %get-tuple-element.135), channel_id=1, source_target_pairs={{0,8},{8,0},{16,24},{24,16},{32,40},{40,32},{48,56},{56,48},{64,72... | collective-permute-start | bytes 1572872 | tf_op jit(solution)/shard_map/ppermute | solution.py:30
  3.6 11.6 %collective-permute-start.6 = (bf16[512,256]{1,0:T(8,128)(2,1)S(1)}, bf16[512,256]{1,0:T(8,128)(2,1)S(1)}, u32[]{:S(2)}, u32[]{:S(2)}) collective-permute-start(bf16[512,256]{1,0:T(8,128)(2,1)S(1)} %constant_dynamic-update-slice_fusion), channel_id=1, source_target_pairs={{0,8},{8,16},{16,24},{24,32},{32,40},{40,48},{48,56},{56,64},{64,7... | collective-permute-start | bytes 786440 | tf_op jit(solution)/shard_map/ppermute | solution.py:44
  8.4 26.0 %collective-permute-start.4 = (bf16[512,1024]{1,0:T(8,128)(2,1)}, bf16[512,1024]{1,0:T(8,128)(2,1)}, u32[]{:S(2)}, u32[]{:S(2)}) collective-permute-start(bf16[512,1024]{1,0:T(8,128)(2,1)} %refs_8_.1), channel_id=1, source_target_pairs={{0,32},{8,40},{16,48},{24,56},{32,64},{40,72},{48,80},{56,88},{64,... | collective-permute-start | bytes 3145736 | tf_op jit(solution)/shard_map/ppermute | solution.py:30
  10.1 24.3 %collective-permute-start.5 = (bf16[512,1024]{1,0:T(8,128)(2,1)}, bf16[512,1024]{1,0:T(8,128)(2,1)}, u32[]{:S(2)}, u32[]{:S(2)}) collective-permute-start(bf16[512,1024]{1,0:T(8,128)(2,1)} %refs_8_.1), channel_id=1, source_target_pairs={{0,96},{8,104},{16,112},{24,120},{32,0},{40,8},{48,16},{56,24},{64... | collective-permute-start | bytes 3145736 | tf_op jit(solution)/shard_map/ppermute | solution.py:30
  12.4 35.1 %copy-start = (bf16[1024,512]{1,0:T(8,128)(2,1)}, bf16[1024,512]{1,0:T(8,128)(2,1)S(1)}, u32[]{:S(2)}) copy-start(bf16[1024,512]{1,0:T(8,128)(2,1)S(1)} %pad_maximum_fusion.refs_0_) | copy-start | bytes 3145732
  12.4 24.7 %collective-permute-start.1 = (bf16[1024,512]{1,0:T(8,128)(2,1)S(1)}, bf16[1024,512]{1,0:T(8,128)(2,1)}, u32[]{:S(2)}, u32[]{:S(2)}) collective-permute-start(bf16[1024,512]{1,0:T(8,128)(2,1)S(1)} %pad_maximum_fusion.refs_0_), channel_id=1, source_target_pairs={{0,1},{1,2},{2,3},{3,0},{4,5},{5,6},{6,7},{7,4},{8,9},{9,10},{10,1... | collective-permute-start | bytes 3145736 | tf_op jit(solution)/shard_map/ppermute | solution.py:38
  13.7 24.0 %collective-permute-start.2 = (bf16[1024,512]{1,0:T(8,128)(2,1)S(1)}, bf16[1024,512]{1,0:T(8,128)(2,1)S(1)}, u32[]{:S(2)}, u32[]{:S(2)}) collective-permute-start(bf16[1024,512]{1,0:T(8,128)(2,1)S(1)} %pad_maximum_fusion.refs_0_), channel_id=1, source_target_pairs={{0,3},{1,0},{2,1},{3,2},{4,7},{5,4},{6,5},{7,6},{8,11},{9,8},{10,9... | collective-permute-start | bytes 3145736 | tf_op jit(solution)/shard_map/ppermute | solution.py:38
  15.2 1.5 copy-start.21
  15.2 24.0 %collective-permute-start.3 = (bf16[1024,512]{1,0:T(8,128)(2,1)S(1)}, bf16[1024,512]{1,0:T(8,128)(2,1)}, u32[]{:S(2)}, u32[]{:S(2)}) collective-permute-start(bf16[1024,512]{1,0:T(8,128)(2,1)S(1)} %pad_maximum_fusion.refs_0_), channel_id=1, source_target_pairs={{0,4},{1,5},{2,6},{3,7},{4,0},{5,1},{6,2},{7,3},{8,12},{9,13},{10,... | collective-permute-start | bytes 3145736 | tf_op jit(solution)/shard_map/ppermute | solution.py:38
  16.7 17.5 %copy-start.11 = (s32[1024,1]{1,0:T(8,128)}, s32[1024,1]{1,0:T(8,128)S(1)}, u32[]{:S(2)}) copy-start(s32[1024,1]{1,0:T(8,128)S(1)} %copy.17.segk_ref) | copy-start | bytes 12292
  17.9 16.3 %copy-start.9 = (bf16[1024,128]{1,0:T(8,128)(2,1)}, bf16[1024,128]{1,0:T(8,128)(2,1)S(1)}, u32[]{:S(2)}) copy-start(bf16[1024,128]{1,0:T(8,128)(2,1)S(1)} %get-tuple-element.139.k_ref) | copy-start | bytes 786436
  18.0 1.2 copy-start.15
  37.7 1.0 copy-start.4
  39.2 7.0 %collective-permute-start.12 = (bf16[512,1024]{1,0:T(8,128)(2,1)}, bf16[512,1024]{1,0:T(8,128)(2,1)}, u32[]{:S(2)}, u32[]{:S(2)}) collective-permute-start(bf16[512,1024]{1,0:T(8,128)(2,1)} %get-tuple-element.75), channel_id=1, source_target_pairs={{0,8},{8,0},{16,24},{24,16},{32,40},{40,32},{48,56},{56,48},{64,72... | collective-permute-start | bytes 3145736 | tf_op jit(solution)/shard_map/ppermute | solution.py:30
  39.2 26.0 %collective-permute-start.11 = (bf16[512,1024]{1,0:T(8,128)(2,1)}, bf16[512,1024]{1,0:T(8,128)(2,1)}, u32[]{:S(2)}, u32[]{:S(2)}) collective-permute-start(bf16[512,1024]{1,0:T(8,128)(2,1)} %refs_8_.1), channel_id=1, source_target_pairs={{0,16},{8,24},{16,0},{24,8},{32,48},{40,56},{48,32},{56,40},{64,80... | collective-permute-start | bytes 3145736 | tf_op jit(solution)/shard_map/ppermute | solution.py:30
  41.5 26.0 %collective-permute-start.10 = (bf16[512,1024]{1,0:T(8,128)(2,1)}, bf16[512,1024]{1,0:T(8,128)(2,1)}, u32[]{:S(2)}, u32[]{:S(2)}) collective-permute-start(bf16[512,1024]{1,0:T(8,128)(2,1)} %collective-permute-done.4.refs_9_), channel_id=1, source_target_pairs={{0,32},{8,40},{16,48},{24,56},{32,64},{40,72},{48,80},{56,88},{64,... | collective-permute-start | bytes 3145736 | tf_op jit(solution)/shard_map/ppermute | solution.py:30
  42.0 25.7 %collective-permute-start.8 = (bf16[1024,512]{1,0:T(8,128)(2,1)}, bf16[1024,512]{1,0:T(8,128)(2,1)}, u32[]{:S(2)}, u32[]{:S(2)}) collective-permute-start(bf16[1024,512]{1,0:T(8,128)(2,1)} %collective-permute-done.3.refs_3_), channel_id=1, source_target_pairs={{0,1},{1,2},{2,3},{3,0},{4,5},{5,6},{6,7},{7,4},{8,9},{9,10},{10,1... | collective-permute-start | bytes 3145736 | tf_op jit(solution)/shard_map/ppermute | solution.py:38
  42.1 25.5 %collective-permute-start.9 = (bf16[1024,512]{1,0:T(8,128)(2,1)}, bf16[1024,512]{1,0:T(8,128)(2,1)}, u32[]{:S(2)}, u32[]{:S(2)}) collective-permute-start(bf16[1024,512]{1,0:T(8,128)(2,1)} %collective-permute-done.3.refs_3_), channel_id=1, source_target_pairs={{0,3},{1,0},{2,1},{3,2},{4,7},{5,4},{6,5},{7,6},{8,11},{9,8},{10,9... | collective-permute-start | bytes 3145736 | tf_op jit(solution)/shard_map/ppermute | solution.py:38
  44.7 2.8 %copy-start.5 = (bf16[1024,512]{1,0:T(8,128)(2,1)S(1)}, bf16[1024,512]{1,0:T(8,128)(2,1)}, u32[]{:S(2)}) copy-start(bf16[1024,512]{1,0:T(8,128)(2,1)} %copy-done.4) | copy-start | bytes 3145732
  46.1 44.0 %collective-permute-start.7 = (bf16[1024,512]{1,0:T(8,128)(2,1)}, bf16[1024,512]{1,0:T(8,128)(2,1)}, u32[]{:S(2)}, u32[]{:S(2)}) collective-permute-start(bf16[1024,512]{1,0:T(8,128)(2,1)} %collective-permute-done.1.refs_1_), channel_id=1, source_target_pairs={{0,1},{1,2},{2,3},{3,0},{4,5},{5,6},{6,7},{7,4},{8,9},{9,10},{10,1... | collective-permute-start | bytes 3145736 | tf_op jit(solution)/shard_map/ppermute | solution.py:38
  67.7 23.4 %collective-permute-start.13 = (bf16[1024,512]{1,0:T(8,128)(2,1)}, bf16[1024,512]{1,0:T(8,128)(2,1)S(1)}, u32[]{:S(2)}, u32[]{:S(2)}) collective-permute-start(bf16[1024,512]{1,0:T(8,128)(2,1)} %collective-permute-done.9.refs_1_.refs_5_), channel_id=1, source_target_pairs={{0,3},{1,0},{2,1},{3,2},{4,7},{5,4},{6,5},{7,6},{8,11},{9,8},{10,9... | collective-permute-start | bytes 3145736 | tf_op jit(solution)/shard_map/ppermute | solution.py:38
  70.0 33.2 %collective-permute-start.14 = (bf16[512,1024]{1,0:T(8,128)(2,1)}, bf16[512,1024]{1,0:T(8,128)(2,1)}, u32[]{:S(2)}, u32[]{:S(2)}) collective-permute-start(bf16[512,1024]{1,0:T(8,128)(2,1)} %collective-permute-done.11.refs_11_), channel_id=1, source_target_pairs={{0,32},{8,40},{16,48},{24,56},{32,64},{40,72},{48,80},{56,88},{64,... | collective-permute-start | bytes 3145736 | tf_op jit(solution)/shard_map/ppermute | solution.py:30
  71.4 31.9 %collective-permute-start.15 = (bf16[512,1024]{1,0:T(8,128)(2,1)}, bf16[512,1024]{1,0:T(8,128)(2,1)}, u32[]{:S(2)}, u32[]{:S(2)}) collective-permute-start(bf16[512,1024]{1,0:T(8,128)(2,1)} %collective-permute-done.11.refs_11_), channel_id=1, source_target_pairs={{0,96},{8,104},{16,112},{24,120},{32,0},{40,8},{48,16},{56,24},{64... | collective-permute-start | bytes 3145736 | tf_op jit(solution)/shard_map/ppermute | solution.py:30
  72.7 30.5 %collective-permute-start.16 = (bf16[512,1024]{1,0:T(8,128)(2,1)}, bf16[512,1024]{1,0:T(8,128)(2,1)}, u32[]{:S(2)}, u32[]{:S(2)}) collective-permute-start(bf16[512,1024]{1,0:T(8,128)(2,1)} %collective-permute-done.10.refs_15_), channel_id=1, source_target_pairs={{0,16},{8,24},{16,0},{24,8},{32,48},{40,56},{48,32},{56,40},{64,80... | collective-permute-start | bytes 3145736 | tf_op jit(solution)/shard_map/ppermute | solution.py:30
  91.0 8.6 %copy-start.7 = (bf16[1024,512]{1,0:T(8,128)(2,1)}, bf16[1024,512]{1,0:T(8,128)(2,1)S(1)}, u32[]{:S(2)}) copy-start(bf16[1024,512]{1,0:T(8,128)(2,1)S(1)} %collective-permute-done.13.refs_1_.refs_7_) | copy-start | bytes 3145732
  99.7 1.1 copy-start.13
  100.8 1.1 copy-start.14
  101.8 0.7 copy-start.17
  102.5 0.7 copy-start.19
  103.2 24.5 %collective-permute-start.17 = (bf16[512,1024]{1,0:T(8,128)(2,1)}, bf16[512,1024]{1,0:T(8,128)(2,1)}, u32[]{:S(2)}, u32[]{:S(2)}) collective-permute-start(bf16[512,1024]{1,0:T(8,128)(2,1)} %get-tuple-element.87), channel_id=1, source_target_pairs={{0,16},{8,24},{16,0},{24,8},{32,48},{40,56},{48,32},{56,40},{64,80... | collective-permute-start | bytes 3145736 | tf_op jit(solution)/shard_map/ppermute | solution.py:30
  104.7 32.3 %collective-permute-start.19 = (bf16[640,1024]{1,0:T(8,128)(2,1)}, bf16[640,1024]{1,0:T(8,128)(2,1)S(1)}, u32[]{:S(2)}, u32[]{:S(2)}) collective-permute-start(bf16[640,1024]{1,0:T(8,128)(2,1)} %copy-done.14), channel_id=1, source_target_pairs={{0,32},{8,40},{16,48},{24,56},{32,64},{40,72},{48,80},{56,88},{64,... | collective-permute-start | bytes 3932168 | tf_op jit(solution)/shard_map/ppermute | solution.py:30
  106.2 32.2 %collective-permute-start.20 = (bf16[640,1024]{1,0:T(8,128)(2,1)}, bf16[640,1024]{1,0:T(8,128)(2,1)S(1)}, u32[]{:S(2)}, u32[]{:S(2)}) collective-permute-start(bf16[640,1024]{1,0:T(8,128)(2,1)} %copy-done.13), channel_id=1, source_target_pairs={{0,96},{8,104},{16,112},{24,120},{32,0},{40,8},{48,16},{56,24},{64... | collective-permute-start | bytes 3932168 | tf_op jit(solution)/shard_map/ppermute | solution.py:30
  107.4 1.2 copy-start.1
  108.7 1.2 copy-start.6
  109.9 1.2 copy-start.8
  111.1 20.2 %copy-start.10 = (bf16[1024,128]{1,0:T(8,128)(2,1)S(1)}, bf16[1024,128]{1,0:T(8,128)(2,1)}, u32[]{:S(2)}) copy-start(bf16[1024,128]{1,0:T(8,128)(2,1)} %copy-done.9) | copy-start | bytes 786436
  126.4 1.4 copy-start.2
  127.8 13.7 %collective-permute-start.18 = (bf16[512,1024]{1,0:T(8,128)(2,1)}, bf16[512,1024]{1,0:T(8,128)(2,1)}, u32[]{:S(2)}, u32[]{:S(2)}) collective-permute-start(bf16[512,1024]{1,0:T(8,128)(2,1)} %get-tuple-element.97), channel_id=1, source_target_pairs={{0,8},{8,0},{16,24},{24,16},{32,40},{40,32},{48,56},{56,48},{64,72... | collective-permute-start | bytes 3145736 | tf_op jit(solution)/shard_map/ppermute | solution.py:30
  131.5 5.5 %copy-start.20 = (bf16[128,1024]{1,0:T(8,128)(2,1)S(1)}, bf16[128,1024]{1,0:T(8,128)(2,1)}, u32[]{:S(2)}) copy-start(bf16[128,1024]{1,0:T(8,128)(2,1)} %copy-done.19) | copy-start | bytes 786436
  131.5 6.9 %copy-start.18 = (bf16[128,1024]{1,0:T(8,128)(2,1)S(1)}, bf16[128,1024]{1,0:T(8,128)(2,1)}, u32[]{:S(2)}) copy-start(bf16[128,1024]{1,0:T(8,128)(2,1)} %copy-done.17) | copy-start | bytes 786436
  134.3 17.9 %collective-permute-start.21 = (bf16[256,1024]{1,0:T(8,128)(2,1)S(1)}, bf16[256,1024]{1,0:T(8,128)(2,1)S(1)}, u32[]{:S(2)}, u32[]{:S(2)}) collective-permute-start(bf16[256,1024]{1,0:T(8,128)(2,1)S(1)} %get-tuple-element.101), channel_id=1, source_target_pairs={{0,32},{8,40},{16,48},{24,56},{32,64},{40,72},{48,80},{56,88},{64,... | collective-permute-start | bytes 1572872 | tf_op jit(solution)/shard_map/ppermute | solution.py:30
  135.1 17.0 %collective-permute-start.22 = (bf16[256,1024]{1,0:T(8,128)(2,1)S(1)}, bf16[256,1024]{1,0:T(8,128)(2,1)S(1)}, u32[]{:S(2)}, u32[]{:S(2)}) collective-permute-start(bf16[256,1024]{1,0:T(8,128)(2,1)S(1)} %get-tuple-element.106), channel_id=1, source_target_pairs={{0,96},{8,104},{16,112},{24,120},{32,0},{40,8},{48,16},{56,24},{64... | collective-permute-start | bytes 1572872 | tf_op jit(solution)/shard_map/ppermute | solution.py:30
  137.0 6.5 %copy-start.3 = (f32[512,1024]{1,0:T(8,128)S(1)}, f32[512,1024]{1,0:T(8,128)}, u32[]{:S(2)}) copy-start(f32[512,1024]{1,0:T(8,128)} %copy-done.2) | copy-start | bytes 6291460
  137.0 17.7 %collective-permute-start.23 = (bf16[128,1024]{1,0:T(8,128)(2,1)S(1)}, bf16[128,1024]{1,0:T(8,128)(2,1)S(1)}, u32[]{:S(2)}, u32[]{:S(2)}) collective-permute-start(bf16[128,1024]{1,0:T(8,128)(2,1)S(1)} %copy-done.20), channel_id=1, source_target_pairs={{0,32},{8,40},{16,48},{24,56},{32,64},{40,72},{48,80},{56,88},{64,... | collective-permute-start | bytes 786440 | tf_op jit(solution)/shard_map/ppermute | solution.py:30
  138.4 17.6 %collective-permute-start.24 = (bf16[128,1024]{1,0:T(8,128)(2,1)S(1)}, bf16[128,1024]{1,0:T(8,128)(2,1)S(1)}, u32[]{:S(2)}, u32[]{:S(2)}) collective-permute-start(bf16[128,1024]{1,0:T(8,128)(2,1)S(1)} %copy-done.18), channel_id=1, source_target_pairs={{0,96},{8,104},{16,112},{24,120},{32,0},{40,8},{48,16},{56,24},{64... | collective-permute-start | bytes 786440 | tf_op jit(solution)/shard_map/ppermute | solution.py:30
  141.4 3.7 %copy-start.12 = (s32[1024,1]{1,0:T(8,128)S(1)}, s32[1024,1]{1,0:T(8,128)}, u32[]{:S(2)}) copy-start(s32[1024,1]{1,0:T(8,128)} %copy-done.11) | copy-start | bytes 12292
  141.4 3.7 %copy-start.16 = (bf16[512,1024]{1,0:T(8,128)(2,1)S(1)}, bf16[512,1024]{1,0:T(8,128)(2,1)}, u32[]{:S(2)}) copy-start(bf16[512,1024]{1,0:T(8,128)(2,1)} %q_ref.4) | copy-start | bytes 3145732
  141.4 31.0 %collective-permute-start.28 = (bf16[512,1024]{1,0:T(8,128)(2,1)S(1)}, bf16[512,1024]{1,0:T(8,128)(2,1)S(1)}, u32[]{:S(2)}, u32[]{:S(2)}) collective-permute-start(bf16[512,1024]{1,0:T(8,128)(2,1)S(1)} %add_blocks.5), channel_id=1, source_target_pairs={{0,16},{8,24},{16,0},{24,8},{32,48},{40,56},{48,32},{56,40},{64,80... | collective-permute-start | bytes 3145736 | tf_op jit(solution)/shard_map/ppermute | solution.py:30
  154.6 13.8 %collective-permute-start.25 = (bf16[256,1024]{1,0:T(8,128)(2,1)S(1)}, bf16[256,1024]{1,0:T(8,128)(2,1)S(1)}, u32[]{:S(2)}, u32[]{:S(2)}) collective-permute-start(bf16[256,1024]{1,0:T(8,128)(2,1)S(1)} %get-tuple-element.119), channel_id=1, source_target_pairs={{0,32},{8,40},{16,48},{24,56},{32,64},{40,72},{48,80},{56,88},{64,... | collective-permute-start | bytes 1572872 | tf_op jit(solution)/shard_map/ppermute | solution.py:30
  156.0 12.7 %collective-permute-start.26 = (bf16[256,1024]{1,0:T(8,128)(2,1)S(1)}, bf16[256,1024]{1,0:T(8,128)(2,1)S(1)}, u32[]{:S(2)}, u32[]{:S(2)}) collective-permute-start(bf16[256,1024]{1,0:T(8,128)(2,1)S(1)} %get-tuple-element.126), channel_id=1, source_target_pairs={{0,96},{8,104},{16,112},{24,120},{32,0},{40,8},{48,16},{56,24},{64... | collective-permute-start | bytes 1572872 | tf_op jit(solution)/shard_map/ppermute | solution.py:30
  168.8 9.2 %collective-permute-start.27 = (bf16[512,256]{1,0:T(8,128)(2,1)S(1)}, bf16[512,256]{1,0:T(8,128)(2,1)S(1)}, u32[]{:S(2)}, u32[]{:S(2)}) collective-permute-start(bf16[512,256]{1,0:T(8,128)(2,1)S(1)} %pad_maximum_fusion.2), channel_id=1, source_target_pairs={{8,0},{16,8},{24,16},{32,24},{40,32},{48,40},{56,48},{64,56},{72,6... | collective-permute-start | bytes 786440 | tf_op jit(solution)/shard_map/ppermute | solution.py:44

commit v6 on v5

--- a/solution.py
+++ b/solution.py
@@ -224,6 +224,29 @@
     def put(j):
         return pltpu.make_async_copy(done.at[j], buffer_ref.at[:, meta_ref[j]], sems.at[j])
 
+    def take(i, made):
+        out, start, at, half, first, count = plan[i]
+        if made is None:
+            source = buffer_ref.at[half, meta_ref[n_in + at], pl.ds(first, count)]
+        else:
+            source = done.at[made, half, pl.ds(first, count)]
+        target = taken[out].at[pl.ds(start, count)]
+        return pltpu.make_async_copy(source, target, take_sems.at[i])
+
+    def made_here(i, j):
+        return meta_ref[n_in + plan[i][2]] == meta_ref[j]
+
+    @pl.when(step == 0)
+    def _():
+        for i in range(len(plan)):
+            here = made_here(i, 0)
+            for j in range(1, n_in):
+                here = here | made_here(i, j)
+
+            @pl.when(jnp.logical_not(here))
+            def _():
+                take(i, None).start()
+
     for j in range(n_in):
 
         @pl.when(step == j)
@@ -234,20 +257,18 @@
             done[j, 0] = value[:rows]
             done[j, 1] = value[rows:]
             put(j).start()
+            for i in range(len(plan)):
+
+                @pl.when(made_here(i, j))
+                def _():
+                    take(i, j).start()
 
     @pl.when(step == n_in - 1)
     def _():
         for j in range(n_in):
             put(j).wait()
-        takes = []
-        for i, (out, start, at, half, first, count) in enumerate(plan):
-            source = buffer_ref.at[half, meta_ref[n_in + at], pl.ds(first, count)]
-            target = taken[out].at[pl.ds(start, count)]
-            takes.append(pltpu.make_async_copy(source, target, take_sems.at[i]))
-        for take in takes:
-            take.start()
-        for take in takes:
-            take.wait()
+        for i in range(len(plan)):
+            take(i, None).wait()
 
 
 def project(pieces, a_pair, blocks, buffer, plan=()):
@@ -288,19 +309,18 @@
     return out if n_taken else out[0]
 
 
-def grad_kernel(gplan, wplan, n_g, n_w, meta_ref, *refs):
+def grad_kernel(wplan, n_g, n_w, meta_ref, *refs):
     g_in, w_in = refs[:n_g], refs[n_g:n_g + n_w]
     own_ref, other_ref = refs[n_g + n_w:n_g + n_w + 2]
     gbuf, wbuf, total, gsems, wsems = refs[n_g + n_w + 2:]
     step = pl.program_id(0)
     half = own_ref.shape[0]
-    gh, wh = gbuf.shape[1] // 2, wbuf.shape[1] // 2
-
-    def g_copy(n):
-        ref, source, block, part = gplan[n]
-        return pltpu.make_async_copy(
-            g_in[ref].at[pl.ds(source, gh)], gbuf.at[block, pl.ds(part * gh, gh)], gsems.at[n]
-        )
+    wh = wbuf.shape[1] // 2
+
+    slots = gbuf.shape[0]
+
+    def g_copy(j):
+        return pltpu.make_async_copy(g_in[j], gbuf.at[j % slots], gsems.at[j])
 
     def w_copy(n):
         ref, source, block, part = wplan[n]
@@ -313,17 +333,16 @@
 
     @pl.when(step == 0)
     def _():
+        for j in range(slots):
+            g_copy(j).start()
         for n in range(16):
             w_copy(n).start()
-            g_copy(n).start()
 
     for j in range(8):
 
         @pl.when(step == j)
         def _():
-            for n in range(16):
-                if gplan[n][2] == j:
-                    g_copy(n).wait()
+            g_copy(j).wait()
 
     place = meta_ref[step]
     for part in range(2):
@@ -333,11 +352,17 @@
 
     @pl.when(step == 0)
     def _():
-        total[...] = jnp.dot(gbuf[step], wbuf[place], preferred_element_type=F32)
+        total[...] = jnp.dot(gbuf[0], wbuf[place], preferred_element_type=F32)
 
     @pl.when(step > 0)
     def _():
-        total[...] += jnp.dot(gbuf[step], wbuf[place], preferred_element_type=F32)
+        total[...] += jnp.dot(gbuf[step % slots], wbuf[place], preferred_element_type=F32)
+
+    for j in range(8 - slots):
+
+        @pl.when(step == j)
+        def _():
+            g_copy(j + slots).start()
 
     @pl.when(step == 7)
     def _():
@@ -345,12 +370,12 @@
         other_ref[...] = total[half:, :].astype(BF)
 
 
-def attn_grad_part(g_pieces, gplan, w_pieces, wplan, meta):
+def attn_grad_part(g_pieces, w_pieces, wplan, meta):
     tokens, depth = g_pieces[0].shape
     width = w_pieces[0].shape[1]
     half = tokens // 2
-    kernel = functools.partial(grad_kernel, gplan, wplan, len(g_pieces), len(w_pieces))
-    whole = pl.BlockSpec((half, width), lambda j, m: (0, 0))
+    kernel = functools.partial(grad_kernel, wplan, len(g_pieces), len(w_pieces))
+    whole = pl.BlockSpec(memory_space=pltpu.VMEM)
     return pl.pallas_call(
         kernel,
         grid_spec=pltpu.PrefetchScalarGridSpec(
@@ -359,10 +384,10 @@
             in_specs=[pl.BlockSpec(memory_space=pltpu.HBM)] * (len(g_pieces) + len(w_pieces)),
             out_specs=[whole, whole],
             scratch_shapes=[
-                pltpu.VMEM((8, tokens, depth), BF),
+                pltpu.VMEM((3, tokens, depth), BF),
                 pltpu.VMEM((8, depth, width), BF),
                 pltpu.VMEM((tokens, width), F32),
-                pltpu.SemaphoreType.DMA((16,)),
+                pltpu.SemaphoreType.DMA((8,)),
                 pltpu.SemaphoreType.DMA((2, 8)),
             ],
         ),
@@ -370,7 +395,7 @@
             jax.ShapeDtypeStruct((half, width), F32),
             jax.ShapeDtypeStruct((half, width), BF),
         ],
-        compiler_params=params(34),
+        compiler_params=params(26),
         cost_estimate=pl.CostEstimate(
             flops=16 * tokens * depth * width,
             bytes_accessed=20 * 2**20,
@@ -511,9 +536,8 @@
     (query_held,) = tied((query_rows,), g0)
     attn_out, top, total = attend(query_held, key_pair, value_t, segq, segk, first)
 
-    gxm, gxp, gy, wzm, wzp, attn_out = tied((gxm, gxp, gy, wzm, wzp, attn_out))
-
-    h = g0.shape[0] // 2
+    wzm, wzp, gxm, gxp, gy, attn_out = tied((wzm, wzp, gxm, gxp, gy, attn_out))
+
     hw = out_proj.shape[0] // 2
     gyxm = move_col(gy, dx=1)
     gyxp = move_col(gy, dx=-1)
@@ -530,7 +554,7 @@
     )
 
     go = move_col(gxm, dx=1)
-    gyxm, gyxp, wo, wy, proj = tied((gyxm, gyxp, wo, wy, proj))
+    wo, wy, gyxm, gyxp, proj = tied((wo, wy, gyxm, gyxp, proj))
     gyo = move_col(gyxp, dx=-1)
     wyzm = move_row(wy, dz=1)
     wyzp = move_row(wy, dz=-1)
@@ -565,7 +589,6 @@
     rdn = move_row(give_dn, dz=-1)
 
     g_pieces = [g0, gxm, gxp, gy, gyxm, gyxp, go, gyo]
-    gplan = [(i, p * h, i, p) for i in range(8) for p in range(2)]
     w_pieces = [out_proj, wzm, wzp, wy, wyzm, wyzp, wyo, wo]
     wplan = [(i, p * hw, i, p) for i in range(8) for p in range(2)]
     meta = ints(
@@ -575,7 +598,7 @@
         wblock(-1, 1), wblock(1, 1), wblock(2, 1), wblock(2, 0),
     )
     (meta,) = tied((meta,), give_up)
-    grad_own, grad_give = attn_grad_part(g_pieces, gplan, w_pieces, wplan, meta)
+    grad_own, grad_give = attn_grad_part(g_pieces, w_pieces, wplan, meta)
 
     ry, grad_own, grad_give = tied((ry, grad_own, grad_give))
 

time: 180 us -> 179 us (level)
  waiting for transfers between devices: 31.3 us -> 34.2 us
  Pallas kernels: 80.6 us -> 77.8 us
    ppermute x7, waiting for transfers between devices: 15 us -> 19.4 us  [move_col(): return lax.ppermute(value, 'col', pairs)]
    pallas_call x3, Pallas kernels: 22.8 us -> 20.8 us  [project(): pl.pallas_call(functools.partial(proj_kernel, n_blocks, held, plan), grid...]
    ppermute x7, starting transfers between devices: 8.25 us -> 6.32 us  [move_col(): return lax.ppermute(value, 'col', pairs)]
  transfers between devices with their start and end apart: 29 -> 29, of which waited for: 13 -> 11; matrix products, arithmetic and copies ran while one was open for 4% -> 4% of each run, Pallas kernels for 45% -> 44%
where the time goes in v6:
time: 179 us; the launch traced here: 178 us
  Pallas kernels  77.8 us (43%)
  starting transfers between devices  44.4 us (25%)
  waiting for transfers between devices  34.2 us (19%)
  local copies, waits for them, and re-layouts  16.4 us (9%)
  other arithmetic  3.95 us (2%)
    ppermute x20, starting transfers between devices, move_row(): return lax.ppermute(value, 'row', pairs)  29.4 us
    pallas_call x3, Pallas kernels, project(): pl.pallas_call(functools.partial(proj_kernel, n_blocks, held, plan), grid...  20.8 us
    ppermute x7, waiting for transfers between devices, move_col(): return lax.ppermute(value, 'col', pairs)  19.4 us
    pallas_call x2, Pallas kernels, attend_back(): pl.pallas_call(functools.partial(bwd_kernel, len(earlier), last), grid_sp...  18 us
    pallas_call x1, Pallas kernels, attend(): pl.pallas_call(fwd_kernel, grid_spec=pltpu.PrefetchScalarGridSpec(num_sca...  14.9 us
    pallas_call x1, Pallas kernels, attn_grad_part(): pl.pallas_call(kernel, grid_spec=pltpu.PrefetchScalarGridSpec(num_scalar_...  14.5 us
    ppermute x20, waiting for transfers between devices, move_row(): return lax.ppermute(value, 'row', pairs)  12.3 us
    unnamed x50, local copies, waits for them, and re-layouts  12.2 us
  transfers between devices with their start and end apart: 29, of which 11 were waited for; matrix products, arithmetic and copies ran while one was open for 4% of the time, Pallas kernels for 44%

profile of v6, /device:TPU:1, one launch (start us, length us, event | category | flops | bytes accessed | tf_op | source)
XLA Modules:
  0.0 177.9 jit_solution(9145805560170330990)
XLA Ops:
  0.7 1.3 constant_dynamic-slice_fusion.1
  2.0 1.5 collective-permute-start.2
  3.6 4.8 %collective-permute-start.6 = (bf16[512,256]{1,0:T(8,128)(2,1)S(1)}, bf16[512,256]{1,0:T(8,128)(2,1)S(1)}, u32[]{:S(2)}, u32[]{:S(2)}) collective-permute-start(bf16[512,256]{1,0:T(8,128)(2,1)S(1)} %constant_dynamic-update-slice_fusion), channel_id=1, source_target_pairs={{0,8},{8,16},{16,24},{24,32},{32,40},{40,48},{48,56},{56,64},{64,7... | collective-permute-start | bytes 786440 | tf_op jit(solution)/shard_map/ppermute | solution.py:44
  8.4 1.7 collective-permute-start
  10.1 2.2 %collective-permute-start.1 = (bf16[512,1024]{1,0:T(8,128)(2,1)}, bf16[512,1024]{1,0:T(8,128)(2,1)}, u32[]{:S(2)}, u32[]{:S(2)}) collective-permute-start(bf16[512,1024]{1,0:T(8,128)(2,1)} %refs_8_.1), channel_id=1, source_target_pairs={{0,96},{8,104},{16,112},{24,120},{32,0},{40,8},{48,16},{56,24},{64... | collective-permute-start | bytes 3145736 | tf_op jit(solution)/shard_map/ppermute | solution.py:30
  12.4 1.3 collective-permute-start.3
  13.7 1.5 collective-permute-start.4
  15.2 0.4 collective-permute-start.5
  15.6 0.8 fusion.3
  16.4 0.2 copy.17.segk_ref
  16.7 1.2 pad_maximum_fusion.1
  17.9 0.1 copy.16.vt_ref
  18.1 1.2 copy-done.15
  19.3 14.9 %attend.1 = (bf16[512,1024]{1,0:T(8,128)(2,1)}, f32[8,1,512]{2,1,0:T(1,128)S(1)}, f32[8,1,512]{2,1,0:T(1,128)S(1)}) custom-call(s32[1]{0:T(128)} %bitcast.meta_ref, bf16[512,1024]{1,0:T(8,128)(2,1)S(1)} %copy-done.15, bf16[1024,128]{1,0:T(8,128)(2,1)S(1)} %get-tuple-element.139.k_ref, bf16[128,1024]{1,0:T(8,128)(2,1)S(1)} %copy.16.vt_ref, ...), custom_call_target="tpu_custom_call" | custom-call | flops 4294967296 | bytes 8388608 | tf_op jit(solution)/shard_map/attend/pallas_call | solution.py:97
  34.2 0.2 collective-permute-done.refs_9_
  34.4 2.7 %collective-permute-done.3.refs_1_ = bf16[1024,512]{1,0:T(8,128)(2,1)} collective-permute-done((bf16[1024,512]{1,0:T(8,128)(2,1)S(1)}, bf16[1024,512]{1,0:T(8,128)(2,1)}, u32[]{:S(2)}, u32[]{:S(2)}) %collective-permute-start.3) | collective-permute-done | bytes 1048608 | tf_op jit(solution)/shard_map/ppermute | solution.py:38
  37.1 0.6 collective-permute-done.4.refs_2_
  37.7 1.0 copy-done.4
  38.7 0.5 collective-permute-done.5.refs_3_
  39.2 2.4 %collective-permute-start.9 = (bf16[512,1024]{1,0:T(8,128)(2,1)}, bf16[512,1024]{1,0:T(8,128)(2,1)}, u32[]{:S(2)}, u32[]{:S(2)}) collective-permute-start(bf16[512,1024]{1,0:T(8,128)(2,1)} %refs_8_.1), channel_id=1, source_target_pairs={{0,16},{8,24},{16,0},{24,8},{32,48},{40,56},{48,32},{56,40},{64,80... | collective-permute-start | bytes 3145736 | tf_op jit(solution)/shard_map/ppermute | solution.py:30
  41.5 0.2 collective-permute-start.10
  41.7 2.5 %collective-permute-start.11 = (bf16[1024,512]{1,0:T(8,128)(2,1)}, bf16[1024,512]{1,0:T(8,128)(2,1)}, u32[]{:S(2)}, u32[]{:S(2)}) collective-permute-start(bf16[1024,512]{1,0:T(8,128)(2,1)} %collective-permute-done.5.refs_3_), channel_id=1, source_target_pairs={{0,3},{1,0},{2,1},{3,2},{4,7},{5,4},{6,5},{7,6},{8,11},{9,8},{10,9... | collective-permute-start | bytes 3145736 | tf_op jit(solution)/shard_map/ppermute | solution.py:38
  44.2 0.4 collective-permute-start.8
  44.7 1.4 constant_dynamic-update-slice_fusion.3
  46.2 1.3 constant_dynamic-update-slice_fusion.2.refs_4_.refs_2_
  47.5 8.4 %project.3.refs_3_ = bf16[2,64,256,1024]{3,2,1,0:T(8,128)(2,1)} custom-call(s32[4]{0:T(128)S(1)} %pad_add_fusion.1.meta_ref, bf16[1024,512]{1,0:T(8,128)(2,1)S(1)} %pad_maximum_fusion.refs_0_, bf16[1024,512]{1,0:T(8,128)(2,1)} %collective-permute-done.3.refs_1_, bf16[1024,512]{1,0:T(8,128)(2,1)S(1)} %copy-done.5, ...), custom_call_target="tpu_custom_call" | custom-call | flops 4294967296 | bytes 10485760 | tf_op jit(solution)/shard_map/project/pallas_call | solution.py:285
  55.9 9.3 %collective-permute-done.9.refs_11_ = bf16[512,1024]{1,0:T(8,128)(2,1)} collective-permute-done((bf16[512,1024]{1,0:T(8,128)(2,1)}, bf16[512,1024]{1,0:T(8,128)(2,1)}, u32[]{:S(2)}, u32[]{:S(2)}) %collective-permute-start.9) | collective-permute-done | bytes 1048608 | tf_op jit(solution)/shard_map/ppermute | solution.py:30
  65.2 2.3 %collective-permute-done.10.refs_0_.refs_4_ = bf16[1024,512]{1,0:T(8,128)(2,1)} collective-permute-done((bf16[1024,512]{1,0:T(8,128)(2,1)}, bf16[1024,512]{1,0:T(8,128)(2,1)}, u32[]{:S(2)}, u32[]{:S(2)}) %collective-permute-start.10) | collective-permute-done | bytes 1048608 | tf_op jit(solution)/shard_map/ppermute | solution.py:38
  67.5 2.0 %collective-permute-done.8.refs_15_ = bf16[512,1024]{1,0:T(8,128)(2,1)} collective-permute-done((bf16[512,1024]{1,0:T(8,128)(2,1)}, bf16[512,1024]{1,0:T(8,128)(2,1)}, u32[]{:S(2)}, u32[]{:S(2)}) %collective-permute-start.8) | collective-permute-done | bytes 1048608 | tf_op jit(solution)/shard_map/ppermute | solution.py:30
  69.6 0.4 collective-permute-start.13
  70.0 0.3 collective-permute-start.14
  70.3 2.4 %collective-permute-start.15 = (bf16[512,1024]{1,0:T(8,128)(2,1)}, bf16[512,1024]{1,0:T(8,128)(2,1)}, u32[]{:S(2)}, u32[]{:S(2)}) collective-permute-start(bf16[512,1024]{1,0:T(8,128)(2,1)} %collective-permute-done.9.refs_11_), channel_id=1, source_target_pairs={{0,96},{8,104},{16,112},{24,120},{32,0},{40,8},{48,16},{56,24},{64... | collective-permute-start | bytes 3145736 | tf_op jit(solution)/shard_map/ppermute | solution.py:30
  72.7 0.9 collective-permute-start.16
  73.7 5.8 %project.4.refs_3_ = bf16[2,64,256,1024]{3,2,1,0:T(8,128)(2,1)} custom-call(s32[2]{0:T(128)S(1)} %pad_add_fusion.2.meta_ref, bf16[1024,512]{1,0:T(8,128)(2,1)} %collective-permute-done.10.refs_0_.refs_4_, bf16[1024,512]{1,0:T(8,128)(2,1)} %collective-permute-done.11.refs_1_.refs_5_, ...), custom_call_target="tpu_custom_call", output_to_operand_aliasing={{}: (4, {})} | custom-call | flops 2147483648 | bytes 6291456 | tf_op jit(solution)/shard_map/project/pallas_call | solution.py:285
  79.5 10.5 %collective-permute-done.7.refs_0_.refs_6_ = bf16[1024,512]{1,0:T(8,128)(2,1)} collective-permute-done((bf16[1024,512]{1,0:T(8,128)(2,1)}, bf16[1024,512]{1,0:T(8,128)(2,1)}, u32[]{:S(2)}, u32[]{:S(2)}) %collective-permute-start.7) | collective-permute-done | bytes 1048608 | tf_op jit(solution)/shard_map/ppermute | solution.py:38
  90.0 2.8 %collective-permute-done.13.refs_1_.refs_7_ = bf16[1024,512]{1,0:T(8,128)(2,1)S(1)} collective-permute-done((bf16[1024,512]{1,0:T(8,128)(2,1)}, bf16[1024,512]{1,0:T(8,128)(2,1)S(1)}, u32[]{:S(2)}, u32[]{:S(2)}) %collective-permute-start.13) | collective-permute-done | bytes 1048608 | tf_op jit(solution)/shard_map/ppermute | solution.py:38
  92.8 6.6 %project.5 = (bf16[2,64,256,1024]{3,2,1,0:T(8,128)(2,1)}, bf16[512,1024]{1,0:T(8,128)(2,1)}, bf16[640,1024]{1,0:T(8,128)(2,1)S(1)}, bf16[640,1024]{1,0:T(8,128)(...) custom-call(s32[7]{0:T(128)S(1)} %stack.95.meta_ref, ...), custom_call_target="tpu_custom_call", output_to_operand_aliasing={{0}: (4, {})} | custom-call | flops 2147483648 | bytes 6291456 | tf_op jit(solution)/shard_map/project/pallas_call | solution.py:285
  99.5 1.1 copy-done.13
  100.5 1.1 copy-done.14
  101.6 0.7 copy-done.17
  102.3 0.7 copy-done.19
  103.0 0.9 collective-permute-start.17
  104.1 2.7 %collective-permute-start.20 = (bf16[640,1024]{1,0:T(8,128)(2,1)}, bf16[640,1024]{1,0:T(8,128)(2,1)S(1)}, u32[]{:S(2)}, u32[]{:S(2)}) collective-permute-start(bf16[640,1024]{1,0:T(8,128)(2,1)} %copy-done.13), channel_id=1, source_target_pairs={{0,96},{8,104},{16,112},{24,120},{32,0},{40,8},{48,16},{56,24},{64... | collective-permute-start | bytes 3932168 | tf_op jit(solution)/shard_map/ppermute | solution.py:30
  106.7 1.2 copy-done.1
  107.9 1.2 copy-done.6
  109.2 1.2 copy-done.8
  110.4 14.5 %attn_grad.1 = (f32[512,1024]{1,0:T(8,128)S(1)}, bf16[512,1024]{1,0:T(8,128)(2,1)}) custom-call(s32[16]{0:T(128)S(1)} %stack.107.meta_ref, bf16[1024,512]{1,0:T(8,128)(2,1)S(1)} %copy-done.1, bf16[1024,512]{1,0:T(8,128)(2,1)} %collective-permute-done.3.refs_1_, bf16[1024,512]{1,0:T(8,128)(2,1)S(1)} %copy-done.6, ...), custom_call_target="tpu_custom_call" | custom-call | flops 8589934592 | bytes 20971520 | tf_op jit(solution)/shard_map/attn_grad/pallas_call | solution.py:379
  124.9 1.4 copy-done.2
  126.2 0.7 collective-permute-done.17.refs_0_
  127.0 3.5 %collective-permute-start.18 = (bf16[512,1024]{1,0:T(8,128)(2,1)}, bf16[512,1024]{1,0:T(8,128)(2,1)}, u32[]{:S(2)}, u32[]{:S(2)}) collective-permute-start(bf16[512,1024]{1,0:T(8,128)(2,1)} %get-tuple-element.97), channel_id=1, source_target_pairs={{0,8},{8,0},{16,24},{24,16},{32,40},{40,32},{48,56},{56,48},{64,72... | collective-permute-start | bytes 3145736 | tf_op jit(solution)/shard_map/ppermute | solution.py:30
  130.7 2.8 %add_blocks.3 = (bf16[256,1024]{1,0:T(8,128)(2,1)S(1)}, bf16[256,1024]{1,0:T(8,128)(2,1)S(1)}) custom-call(s32[1]{0:T(128)} %bitcast.19.meta_ref, bf16[2,64,256,1024]{3,2,1,0:T(8,128)(2,1)} %get-tuple-element.99.buffer_ref, bf16[512,1024]{1,0:T(8,128)(2,1)} %collective-permute-done.17.refs_0_), custom_call_target="tpu_custom_call" | custom-call | flops 2097152 | bytes 5242880 | tf_op jit(solution)/shard_map/add_blocks/pallas_call | solution.py:434
  133.6 2.7 %collective-permute-start.22 = (bf16[256,1024]{1,0:T(8,128)(2,1)S(1)}, bf16[256,1024]{1,0:T(8,128)(2,1)S(1)}, u32[]{:S(2)}, u32[]{:S(2)}) collective-permute-start(bf16[256,1024]{1,0:T(8,128)(2,1)S(1)} %get-tuple-element.106), channel_id=1, source_target_pairs={{0,96},{8,104},{16,112},{24,120},{32,0},{40,8},{48,16},{56,24},{64... | collective-permute-start | bytes 1572872 | tf_op jit(solution)/shard_map/ppermute | solution.py:30
  136.3 2.6 %collective-permute-start.24 = (bf16[128,1024]{1,0:T(8,128)(2,1)S(1)}, bf16[128,1024]{1,0:T(8,128)(2,1)S(1)}, u32[]{:S(2)}, u32[]{:S(2)}) collective-permute-start(bf16[128,1024]{1,0:T(8,128)(2,1)S(1)} %copy-done.18), channel_id=1, source_target_pairs={{0,96},{8,104},{16,112},{24,120},{32,0},{40,8},{48,16},{56,24},{64... | collective-permute-start | bytes 786440 | tf_op jit(solution)/shard_map/ppermute | solution.py:30
  139.0 1.6 add_blocks.5
  140.6 2.3 %collective-permute-start.28 = (bf16[512,1024]{1,0:T(8,128)(2,1)S(1)}, bf16[512,1024]{1,0:T(8,128)(2,1)S(1)}, u32[]{:S(2)}, u32[]{:S(2)}) collective-permute-start(bf16[512,1024]{1,0:T(8,128)(2,1)S(1)} %add_blocks.5), channel_id=1, source_target_pairs={{0,16},{8,24},{16,0},{24,8},{32,48},{40,56},{48,32},{56,40},{64,80... | collective-permute-start | bytes 3145736 | tf_op jit(solution)/shard_map/ppermute | solution.py:30
  143.0 1.6 add_convert_fusion.g_ref
  144.6 7.0 %attend_back.2 = (bf16[512,1024]{1,0:T(8,128)(2,1)}, f32[1024,128]{1,0:T(8,128)S(1)}, f32[1024,128]{1,0:T(8,128)S(1)}) custom-call(s32[1]{0:T(128)} %bitcast.meta_ref, bf16[512,1024]{1,0:T(8,128)(2,1)S(1)} %copy-done.16, bf16[512,1024]{1,0:T(8,128)(2,1)S(1)} %add_convert_fusion.g_ref, bf16[1024,128]{1,0:T(8,128)(2,1)S(1)} %copy-done.10, ...), custom_call_target="tpu_custom_call" | custom-call | flops 4026531840 | bytes 6291456 | tf_op jit(solution)/shard_map/attend_back/pallas_call | solution.py:180
  151.6 2.4 %add_blocks.4 = (bf16[256,1024]{1,0:T(8,128)(2,1)S(1)}, bf16[256,1024]{1,0:T(8,128)(2,1)S(1)}) custom-call(s32[2]{0:T(128)S(1)} %pad_add_fusion.3.meta_ref, bf16[2,64,256,1024]{3,2,1,0:T(8,128)(2,1)} %get-tuple-element.99.buffer_ref, bf16[256,1024]{1,0:T(8,128)(2,1)S(1)} %collective-permute-done.21.refs_0_, bf16[256,1024]{1,0:T(8,128)(2,1)S(1)} %collective-permute-done.22.refs_1_), custom_call_target="tpu_custom_call" | custom-call | flops 2097152 | bytes 5242880 | tf_op jit(solution)/shard_map/add_blocks/pallas_call | solution.py:434
  154.1 2.6 %collective-permute-start.26 = (bf16[256,1024]{1,0:T(8,128)(2,1)S(1)}, bf16[256,1024]{1,0:T(8,128)(2,1)S(1)}, u32[]{:S(2)}, u32[]{:S(2)}) collective-permute-start(bf16[256,1024]{1,0:T(8,128)(2,1)S(1)} %get-tuple-element.126), channel_id=1, source_target_pairs={{0,96},{8,104},{16,112},{24,120},{32,0},{40,8},{48,16},{56,24},{64... | collective-permute-start | bytes 1572872 | tf_op jit(solution)/shard_map/ppermute | solution.py:30
  156.8 11.0 %attend_back.3 = (bf16[512,1024]{1,0:T(8,128)(2,1)}, f32[1024,128]{1,0:T(8,128)S(1)}, f32[1024,128]{1,0:T(8,128)S(1)}) custom-call(s32[1]{0:T(128)} %bitcast.meta_ref, bf16[512,1024]{1,0:T(8,128)(2,1)S(1)} %copy-done.16, bf16[512,1024]{1,0:T(8,128)(2,1)S(1)} %add_convert_fusion.g_ref, ...), custom_call_target="tpu_custom_call", output_to_operand_aliasing={{0}: (12, {})} | custom-call | flops 6710886400 | bytes 6291456 | tf_op jit(solution)/shard_map/attend_back/pallas_call | solution.py:180
  167.9 3.9 %collective-permute-start.27 = (bf16[512,256]{1,0:T(8,128)(2,1)S(1)}, bf16[512,256]{1,0:T(8,128)(2,1)S(1)}, u32[]{:S(2)}, u32[]{:S(2)}) collective-permute-start(bf16[512,256]{1,0:T(8,128)(2,1)S(1)} %pad_maximum_fusion.2), channel_id=1, source_target_pairs={{8,0},{16,8},{24,16},{32,24},{40,32},{48,40},{56,48},{64,56},{72,6... | collective-permute-start | bytes 786440 | tf_op jit(solution)/shard_map/ppermute | solution.py:44
  171.8 2.8 %last_sum.1 = bf16[512,1024]{1,0:T(8,128)(2,1)} custom-call(s32[1]{0:T(128)} %bitcast.17.meta_ref, bf16[2,64,256,1024]{3,2,1,0:T(8,128)(2,1)} %get-tuple-element.99.buffer_ref, bf16[512,1024]{1,0:T(8,128)(2,1)S(1)} %collective-permute-done.28.across, bf16[256,1024]{1,0:T(8,128)(2,1)S(1)} %collective-permute-done.25.nup, ...), custom_call_target="tpu_custom_call" | custom-call | flops 2097152 | bytes 5242880 | tf_op jit(solution)/shard_map/last_sum/pallas_call | solution.py:480
  174.6 2.5 %collective-permute-done.27 = bf16[512,256]{1,0:T(8,128)(2,1)S(1)} collective-permute-done((bf16[512,256]{1,0:T(8,128)(2,1)S(1)}, bf16[512,256]{1,0:T(8,128)(2,1)S(1)}, u32[]{:S(2)}, u32[]{:S(2)}) %collective-permute-start.27) | collective-permute-done | bytes 262176 | tf_op jit(solution)/shard_map/ppermute | solution.py:44
  177.2 0.8 fusion.1
  (76 shorter events, 1.3 us)
Async XLA Ops:
  0.6 2.9 %copy-start.22 = (bf16[512,128]{1,0:T(8,128)(2,1)S(1)}, bf16[512,128]{1,0:T(8,128)(2,1)}, u32[]{:S(2)}) copy-start(bf16[512,128]{1,0:T(8,128)(2,1)} %param.7) | copy-start | bytes 393220
  0.6 2.9 %copy-start.23 = (bf16[512,128]{1,0:T(8,128)(2,1)S(1)}, bf16[512,128]{1,0:T(8,128)(2,1)}, u32[]{:S(2)}) copy-start(bf16[512,128]{1,0:T(8,128)(2,1)} %param.8) | copy-start | bytes 393220
  2.0 10.3 %collective-permute-start.2 = (bf16[512,512]{1,0:T(8,128)(2,1)S(1)}, bf16[512,512]{1,0:T(8,128)(2,1)S(1)}, u32[]{:S(2)}, u32[]{:S(2)}) collective-permute-start(bf16[512,512]{1,0:T(8,128)(2,1)S(1)} %get-tuple-element.135), channel_id=1, source_target_pairs={{0,8},{8,0},{16,24},{24,16},{32,40},{40,32},{48,56},{56,48},{64,72... | collective-permute-start | bytes 1572872 | tf_op jit(solution)/shard_map/ppermute | solution.py:30
  3.6 11.6 %collective-permute-start.6 = (bf16[512,256]{1,0:T(8,128)(2,1)S(1)}, bf16[512,256]{1,0:T(8,128)(2,1)S(1)}, u32[]{:S(2)}, u32[]{:S(2)}) collective-permute-start(bf16[512,256]{1,0:T(8,128)(2,1)S(1)} %constant_dynamic-update-slice_fusion), channel_id=1, source_target_pairs={{0,8},{8,16},{16,24},{24,32},{32,40},{40,48},{48,56},{56,64},{64,7... | collective-permute-start | bytes 786440 | tf_op jit(solution)/shard_map/ppermute | solution.py:44
  8.4 26.0 %collective-permute-start = (bf16[512,1024]{1,0:T(8,128)(2,1)}, bf16[512,1024]{1,0:T(8,128)(2,1)}, u32[]{:S(2)}, u32[]{:S(2)}) collective-permute-start(bf16[512,1024]{1,0:T(8,128)(2,1)} %refs_8_.1), channel_id=1, source_target_pairs={{0,32},{8,40},{16,48},{24,56},{32,64},{40,72},{48,80},{56,88},{64,... | collective-permute-start | bytes 3145736 | tf_op jit(solution)/shard_map/ppermute | solution.py:30
  10.1 24.3 %collective-permute-start.1 = (bf16[512,1024]{1,0:T(8,128)(2,1)}, bf16[512,1024]{1,0:T(8,128)(2,1)}, u32[]{:S(2)}, u32[]{:S(2)}) collective-permute-start(bf16[512,1024]{1,0:T(8,128)(2,1)} %refs_8_.1), channel_id=1, source_target_pairs={{0,96},{8,104},{16,112},{24,120},{32,0},{40,8},{48,16},{56,24},{64... | collective-permute-start | bytes 3145736 | tf_op jit(solution)/shard_map/ppermute | solution.py:30
  12.4 35.1 %copy-start = (bf16[1024,512]{1,0:T(8,128)(2,1)}, bf16[1024,512]{1,0:T(8,128)(2,1)S(1)}, u32[]{:S(2)}) copy-start(bf16[1024,512]{1,0:T(8,128)(2,1)S(1)} %pad_maximum_fusion.refs_0_) | copy-start | bytes 3145732
  12.4 24.7 %collective-permute-start.3 = (bf16[1024,512]{1,0:T(8,128)(2,1)S(1)}, bf16[1024,512]{1,0:T(8,128)(2,1)}, u32[]{:S(2)}, u32[]{:S(2)}) collective-permute-start(bf16[1024,512]{1,0:T(8,128)(2,1)S(1)} %pad_maximum_fusion.refs_0_), channel_id=1, source_target_pairs={{0,1},{1,2},{2,3},{3,0},{4,5},{5,6},{6,7},{7,4},{8,9},{9,10},{10,1... | collective-permute-start | bytes 3145736 | tf_op jit(solution)/shard_map/ppermute | solution.py:38
  13.7 24.0 %collective-permute-start.4 = (bf16[1024,512]{1,0:T(8,128)(2,1)S(1)}, bf16[1024,512]{1,0:T(8,128)(2,1)S(1)}, u32[]{:S(2)}, u32[]{:S(2)}) collective-permute-start(bf16[1024,512]{1,0:T(8,128)(2,1)S(1)} %pad_maximum_fusion.refs_0_), channel_id=1, source_target_pairs={{0,3},{1,0},{2,1},{3,2},{4,7},{5,4},{6,5},{7,6},{8,11},{9,8},{10,9... | collective-permute-start | bytes 3145736 | tf_op jit(solution)/shard_map/ppermute | solution.py:38
  15.2 1.5 copy-start.21
  15.2 24.0 %collective-permute-start.5 = (bf16[1024,512]{1,0:T(8,128)(2,1)S(1)}, bf16[1024,512]{1,0:T(8,128)(2,1)}, u32[]{:S(2)}, u32[]{:S(2)}) collective-permute-start(bf16[1024,512]{1,0:T(8,128)(2,1)S(1)} %pad_maximum_fusion.refs_0_), channel_id=1, source_target_pairs={{0,4},{1,5},{2,6},{3,7},{4,0},{5,1},{6,2},{7,3},{8,12},{9,13},{10,... | collective-permute-start | bytes 3145736 | tf_op jit(solution)/shard_map/ppermute | solution.py:38
  16.7 17.5 %copy-start.11 = (s32[1024,1]{1,0:T(8,128)}, s32[1024,1]{1,0:T(8,128)S(1)}, u32[]{:S(2)}) copy-start(s32[1024,1]{1,0:T(8,128)S(1)} %copy.17.segk_ref) | copy-start | bytes 12292
  17.9 16.3 %copy-start.9 = (bf16[1024,128]{1,0:T(8,128)(2,1)}, bf16[1024,128]{1,0:T(8,128)(2,1)S(1)}, u32[]{:S(2)}) copy-start(bf16[1024,128]{1,0:T(8,128)(2,1)S(1)} %get-tuple-element.139.k_ref) | copy-start | bytes 786436
  18.0 1.2 copy-start.15
  37.7 1.0 copy-start.4
  39.2 7.0 %collective-permute-start.12 = (bf16[512,1024]{1,0:T(8,128)(2,1)}, bf16[512,1024]{1,0:T(8,128)(2,1)}, u32[]{:S(2)}, u32[]{:S(2)}) collective-permute-start(bf16[512,1024]{1,0:T(8,128)(2,1)} %get-tuple-element.75), channel_id=1, source_target_pairs={{0,8},{8,0},{16,24},{24,16},{32,40},{40,32},{48,56},{56,48},{64,72... | collective-permute-start | bytes 3145736 | tf_op jit(solution)/shard_map/ppermute | solution.py:30
  39.2 26.0 %collective-permute-start.9 = (bf16[512,1024]{1,0:T(8,128)(2,1)}, bf16[512,1024]{1,0:T(8,128)(2,1)}, u32[]{:S(2)}, u32[]{:S(2)}) collective-permute-start(bf16[512,1024]{1,0:T(8,128)(2,1)} %refs_8_.1), channel_id=1, source_target_pairs={{0,16},{8,24},{16,0},{24,8},{32,48},{40,56},{48,32},{56,40},{64,80... | collective-permute-start | bytes 3145736 | tf_op jit(solution)/shard_map/ppermute | solution.py:30
  41.5 26.0 %collective-permute-start.10 = (bf16[1024,512]{1,0:T(8,128)(2,1)}, bf16[1024,512]{1,0:T(8,128)(2,1)}, u32[]{:S(2)}, u32[]{:S(2)}) collective-permute-start(bf16[1024,512]{1,0:T(8,128)(2,1)} %collective-permute-done.5.refs_3_), channel_id=1, source_target_pairs={{0,1},{1,2},{2,3},{3,0},{4,5},{5,6},{6,7},{7,4},{8,9},{9,10},{10,1... | collective-permute-start | bytes 3145736 | tf_op jit(solution)/shard_map/ppermute | solution.py:38
  41.7 25.8 %collective-permute-start.11 = (bf16[1024,512]{1,0:T(8,128)(2,1)}, bf16[1024,512]{1,0:T(8,128)(2,1)}, u32[]{:S(2)}, u32[]{:S(2)}) collective-permute-start(bf16[1024,512]{1,0:T(8,128)(2,1)} %collective-permute-done.5.refs_3_), channel_id=1, source_target_pairs={{0,3},{1,0},{2,1},{3,2},{4,7},{5,4},{6,5},{7,6},{8,11},{9,8},{10,9... | collective-permute-start | bytes 3145736 | tf_op jit(solution)/shard_map/ppermute | solution.py:38
  44.2 25.4 %collective-permute-start.8 = (bf16[512,1024]{1,0:T(8,128)(2,1)}, bf16[512,1024]{1,0:T(8,128)(2,1)}, u32[]{:S(2)}, u32[]{:S(2)}) collective-permute-start(bf16[512,1024]{1,0:T(8,128)(2,1)} %collective-permute-done.refs_9_), channel_id=1, source_target_pairs={{0,32},{8,40},{16,48},{24,56},{32,64},{40,72},{48,80},{56,88},{64,... | collective-permute-start | bytes 3145736 | tf_op jit(solution)/shard_map/ppermute | solution.py:30
  44.7 2.8 %copy-start.5 = (bf16[1024,512]{1,0:T(8,128)(2,1)S(1)}, bf16[1024,512]{1,0:T(8,128)(2,1)}, u32[]{:S(2)}) copy-start(bf16[1024,512]{1,0:T(8,128)(2,1)} %copy-done.4) | copy-start | bytes 3145732
  46.1 43.9 %collective-permute-start.7 = (bf16[1024,512]{1,0:T(8,128)(2,1)}, bf16[1024,512]{1,0:T(8,128)(2,1)}, u32[]{:S(2)}, u32[]{:S(2)}) collective-permute-start(bf16[1024,512]{1,0:T(8,128)(2,1)} %collective-permute-done.3.refs_1_), channel_id=1, source_target_pairs={{0,1},{1,2},{2,3},{3,0},{4,5},{5,6},{6,7},{7,4},{8,9},{9,10},{10,1... | collective-permute-start | bytes 3145736 | tf_op jit(solution)/shard_map/ppermute | solution.py:38
  69.6 23.2 %collective-permute-start.13 = (bf16[1024,512]{1,0:T(8,128)(2,1)}, bf16[1024,512]{1,0:T(8,128)(2,1)S(1)}, u32[]{:S(2)}, u32[]{:S(2)}) collective-permute-start(bf16[1024,512]{1,0:T(8,128)(2,1)} %collective-permute-done.11.refs_1_.refs_5_), channel_id=1, source_target_pairs={{0,3},{1,0},{2,1},{3,2},{4,7},{5,4},{6,5},{7,6},{8,11},{9,8},{10,9... | collective-permute-start | bytes 3145736 | tf_op jit(solution)/shard_map/ppermute | solution.py:38
  70.0 33.0 %collective-permute-start.14 = (bf16[512,1024]{1,0:T(8,128)(2,1)}, bf16[512,1024]{1,0:T(8,128)(2,1)}, u32[]{:S(2)}, u32[]{:S(2)}) collective-permute-start(bf16[512,1024]{1,0:T(8,128)(2,1)} %collective-permute-done.9.refs_11_), channel_id=1, source_target_pairs={{0,32},{8,40},{16,48},{24,56},{32,64},{40,72},{48,80},{56,88},{64,... | collective-permute-start | bytes 3145736 | tf_op jit(solution)/shard_map/ppermute | solution.py:30
  70.3 32.7 %collective-permute-start.15 = (bf16[512,1024]{1,0:T(8,128)(2,1)}, bf16[512,1024]{1,0:T(8,128)(2,1)}, u32[]{:S(2)}, u32[]{:S(2)}) collective-permute-start(bf16[512,1024]{1,0:T(8,128)(2,1)} %collective-permute-done.9.refs_11_), channel_id=1, source_target_pairs={{0,96},{8,104},{16,112},{24,120},{32,0},{40,8},{48,16},{56,24},{64... | collective-permute-start | bytes 3145736 | tf_op jit(solution)/shard_map/ppermute | solution.py:30
  72.7 30.3 %collective-permute-start.16 = (bf16[512,1024]{1,0:T(8,128)(2,1)}, bf16[512,1024]{1,0:T(8,128)(2,1)}, u32[]{:S(2)}, u32[]{:S(2)}) collective-permute-start(bf16[512,1024]{1,0:T(8,128)(2,1)} %collective-permute-done.8.refs_15_), channel_id=1, source_target_pairs={{0,16},{8,24},{16,0},{24,8},{32,48},{40,56},{48,32},{56,40},{64,80... | collective-permute-start | bytes 3145736 | tf_op jit(solution)/shard_map/ppermute | solution.py:30
  92.8 6.6 %copy-start.7 = (bf16[1024,512]{1,0:T(8,128)(2,1)}, bf16[1024,512]{1,0:T(8,128)(2,1)S(1)}, u32[]{:S(2)}) copy-start(bf16[1024,512]{1,0:T(8,128)(2,1)S(1)} %collective-permute-done.13.refs_1_.refs_7_) | copy-start | bytes 3145732
  99.5 1.1 copy-start.13
  100.5 1.1 copy-start.14
  101.6 0.7 copy-start.17
  102.3 0.7 copy-start.19
  103.0 24.0 %collective-permute-start.17 = (bf16[512,1024]{1,0:T(8,128)(2,1)}, bf16[512,1024]{1,0:T(8,128)(2,1)}, u32[]{:S(2)}, u32[]{:S(2)}) collective-permute-start(bf16[512,1024]{1,0:T(8,128)(2,1)} %get-tuple-element.87), channel_id=1, source_target_pairs={{0,16},{8,24},{16,0},{24,8},{32,48},{40,56},{48,32},{56,40},{64,80... | collective-permute-start | bytes 3145736 | tf_op jit(solution)/shard_map/ppermute | solution.py:30
  104.0 32.3 %collective-permute-start.19 = (bf16[640,1024]{1,0:T(8,128)(2,1)}, bf16[640,1024]{1,0:T(8,128)(2,1)S(1)}, u32[]{:S(2)}, u32[]{:S(2)}) collective-permute-start(bf16[640,1024]{1,0:T(8,128)(2,1)} %copy-done.14), channel_id=1, source_target_pairs={{0,32},{8,40},{16,48},{24,56},{32,64},{40,72},{48,80},{56,88},{64,... | collective-permute-start | bytes 3932168 | tf_op jit(solution)/shard_map/ppermute | solution.py:30
  104.1 32.3 %collective-permute-start.20 = (bf16[640,1024]{1,0:T(8,128)(2,1)}, bf16[640,1024]{1,0:T(8,128)(2,1)S(1)}, u32[]{:S(2)}, u32[]{:S(2)}) collective-permute-start(bf16[640,1024]{1,0:T(8,128)(2,1)} %copy-done.13), channel_id=1, source_target_pairs={{0,96},{8,104},{16,112},{24,120},{32,0},{40,8},{48,16},{56,24},{64... | collective-permute-start | bytes 3932168 | tf_op jit(solution)/shard_map/ppermute | solution.py:30
  106.7 1.2 copy-start.1
  107.9 1.2 copy-start.6
  109.2 1.2 copy-start.8
  110.4 20.2 %copy-start.10 = (bf16[1024,128]{1,0:T(8,128)(2,1)S(1)}, bf16[1024,128]{1,0:T(8,128)(2,1)}, u32[]{:S(2)}) copy-start(bf16[1024,128]{1,0:T(8,128)(2,1)} %copy-done.9) | copy-start | bytes 786436
  124.9 1.4 copy-start.2
  127.0 13.6 %collective-permute-start.18 = (bf16[512,1024]{1,0:T(8,128)(2,1)}, bf16[512,1024]{1,0:T(8,128)(2,1)}, u32[]{:S(2)}, u32[]{:S(2)}) collective-permute-start(bf16[512,1024]{1,0:T(8,128)(2,1)} %get-tuple-element.97), channel_id=1, source_target_pairs={{0,8},{8,0},{16,24},{24,16},{32,40},{40,32},{48,56},{56,48},{64,72... | collective-permute-start | bytes 3145736 | tf_op jit(solution)/shard_map/ppermute | solution.py:30
  130.7 5.5 %copy-start.20 = (bf16[128,1024]{1,0:T(8,128)(2,1)S(1)}, bf16[128,1024]{1,0:T(8,128)(2,1)}, u32[]{:S(2)}) copy-start(bf16[128,1024]{1,0:T(8,128)(2,1)} %copy-done.19) | copy-start | bytes 786436
  130.7 5.6 %copy-start.18 = (bf16[128,1024]{1,0:T(8,128)(2,1)S(1)}, bf16[128,1024]{1,0:T(8,128)(2,1)}, u32[]{:S(2)}) copy-start(bf16[128,1024]{1,0:T(8,128)(2,1)} %copy-done.17) | copy-start | bytes 786436
  133.5 18.1 %collective-permute-start.21 = (bf16[256,1024]{1,0:T(8,128)(2,1)S(1)}, bf16[256,1024]{1,0:T(8,128)(2,1)S(1)}, u32[]{:S(2)}, u32[]{:S(2)}) collective-permute-start(bf16[256,1024]{1,0:T(8,128)(2,1)S(1)} %get-tuple-element.101), channel_id=1, source_target_pairs={{0,32},{8,40},{16,48},{24,56},{32,64},{40,72},{48,80},{56,88},{64,... | collective-permute-start | bytes 1572872 | tf_op jit(solution)/shard_map/ppermute | solution.py:30
  133.6 18.0 %collective-permute-start.22 = (bf16[256,1024]{1,0:T(8,128)(2,1)S(1)}, bf16[256,1024]{1,0:T(8,128)(2,1)S(1)}, u32[]{:S(2)}, u32[]{:S(2)}) collective-permute-start(bf16[256,1024]{1,0:T(8,128)(2,1)S(1)} %get-tuple-element.106), channel_id=1, source_target_pairs={{0,96},{8,104},{16,112},{24,120},{32,0},{40,8},{48,16},{56,24},{64... | collective-permute-start | bytes 1572872 | tf_op jit(solution)/shard_map/ppermute | solution.py:30
  136.2 6.7 %copy-start.3 = (f32[512,1024]{1,0:T(8,128)S(1)}, f32[512,1024]{1,0:T(8,128)}, u32[]{:S(2)}) copy-start(f32[512,1024]{1,0:T(8,128)} %copy-done.2) | copy-start | bytes 6291460
  136.2 17.9 %collective-permute-start.23 = (bf16[128,1024]{1,0:T(8,128)(2,1)S(1)}, bf16[128,1024]{1,0:T(8,128)(2,1)S(1)}, u32[]{:S(2)}, u32[]{:S(2)}) collective-permute-start(bf16[128,1024]{1,0:T(8,128)(2,1)S(1)} %copy-done.20), channel_id=1, source_target_pairs={{0,32},{8,40},{16,48},{24,56},{32,64},{40,72},{48,80},{56,88},{64,... | collective-permute-start | bytes 786440 | tf_op jit(solution)/shard_map/ppermute | solution.py:30
  136.3 17.8 %collective-permute-start.24 = (bf16[128,1024]{1,0:T(8,128)(2,1)S(1)}, bf16[128,1024]{1,0:T(8,128)(2,1)S(1)}, u32[]{:S(2)}, u32[]{:S(2)}) collective-permute-start(bf16[128,1024]{1,0:T(8,128)(2,1)S(1)} %copy-done.18), channel_id=1, source_target_pairs={{0,96},{8,104},{16,112},{24,120},{32,0},{40,8},{48,16},{56,24},{64... | collective-permute-start | bytes 786440 | tf_op jit(solution)/shard_map/ppermute | solution.py:30
  140.6 4.0 %copy-start.12 = (s32[1024,1]{1,0:T(8,128)S(1)}, s32[1024,1]{1,0:T(8,128)}, u32[]{:S(2)}) copy-start(s32[1024,1]{1,0:T(8,128)} %copy-done.11) | copy-start | bytes 12292
  140.6 4.0 %copy-start.16 = (bf16[512,1024]{1,0:T(8,128)(2,1)S(1)}, bf16[512,1024]{1,0:T(8,128)(2,1)}, u32[]{:S(2)}) copy-start(bf16[512,1024]{1,0:T(8,128)(2,1)} %q_ref.4) | copy-start | bytes 3145732
  140.6 31.2 %collective-permute-start.28 = (bf16[512,1024]{1,0:T(8,128)(2,1)S(1)}, bf16[512,1024]{1,0:T(8,128)(2,1)S(1)}, u32[]{:S(2)}, u32[]{:S(2)}) collective-permute-start(bf16[512,1024]{1,0:T(8,128)(2,1)S(1)} %add_blocks.5), channel_id=1, source_target_pairs={{0,16},{8,24},{16,0},{24,8},{32,48},{40,56},{48,32},{56,40},{64,80... | collective-permute-start | bytes 3145736 | tf_op jit(solution)/shard_map/ppermute | solution.py:30
  154.0 13.8 %collective-permute-start.25 = (bf16[256,1024]{1,0:T(8,128)(2,1)S(1)}, bf16[256,1024]{1,0:T(8,128)(2,1)S(1)}, u32[]{:S(2)}, u32[]{:S(2)}) collective-permute-start(bf16[256,1024]{1,0:T(8,128)(2,1)S(1)} %get-tuple-element.119), channel_id=1, source_target_pairs={{0,32},{8,40},{16,48},{24,56},{32,64},{40,72},{48,80},{56,88},{64,... | collective-permute-start | bytes 1572872 | tf_op jit(solution)/shard_map/ppermute | solution.py:30
  154.1 13.7 %collective-permute-start.26 = (bf16[256,1024]{1,0:T(8,128)(2,1)S(1)}, bf16[256,1024]{1,0:T(8,128)(2,1)S(1)}, u32[]{:S(2)}, u32[]{:S(2)}) collective-permute-start(bf16[256,1024]{1,0:T(8,128)(2,1)S(1)} %get-tuple-element.126), channel_id=1, source_target_pairs={{0,96},{8,104},{16,112},{24,120},{32,0},{40,8},{48,16},{56,24},{64... | collective-permute-start | bytes 1572872 | tf_op jit(solution)/shard_map/ppermute | solution.py:30
  167.9 9.2 %collective-permute-start.27 = (bf16[512,256]{1,0:T(8,128)(2,1)S(1)}, bf16[512,256]{1,0:T(8,128)(2,1)S(1)}, u32[]{:S(2)}, u32[]{:S(2)}) collective-permute-start(bf16[512,256]{1,0:T(8,128)(2,1)S(1)} %pad_maximum_fusion.2), channel_id=1, source_target_pairs={{8,0},{16,8},{24,16},{32,24},{40,32},{48,40},{56,48},{64,56},{72,6... | collective-permute-start | bytes 786440 | tf_op jit(solution)/shard_map/ppermute | solution.py:44

commit v7 on v6

--- a/solution.py
+++ b/solution.py
@@ -17,6 +17,26 @@
 PLACES = 64
 
 ZN, YN, KN, LN, XN = 4, 2, 2, 2, 4
+
+
+AT_FIRST, AT_ROW, AT_EARLIER, AT_G, AT_W = 0, 1, 2, 8, 16
+G_STEPS = [(0, 0), (0, -1), (0, 1), (1, 0), (1, -1), (1, 1), (0, 2), (1, 2)]
+W_STEPS = [(0, 0), (-1, 0), (1, 0), (0, 1), (-1, 1), (1, 1), (2, 1), (2, 0)]
+LANES = 128
+
+
+def positions(row, col):
+    z, yh, yl, x = row // 4, row // 2 % 2, col // 4, col % 4
+    head = jnp.stack([(row == 0).astype(jnp.int32), row, jnp.maximum(row - 1, 0)] + [row] * 5)
+    steps = [jnp.asarray([step[i] for step in order], jnp.int32) for order in (G_STEPS, W_STEPS) for i in (0, 1)]
+    dyl, dx, dz, dyh = steps
+    g = ((yl + dyl) & 1) * 4 + ((x + dx) & 3)
+    w = ((z + dz) & 3) * 2 + ((yh + dyh) & 1)
+    return jnp.concatenate([head, g, w])
+
+
+def at_w(dz, dyh):
+    return AT_W + W_STEPS.index((dz, dyh))
 
 
 def move_row(value, dz=0, dyh=0, dk=0):
@@ -53,28 +73,59 @@
     return pltpu.CompilerParams(vmem_limit_bytes=mib * 1024 * 1024, **kw)
 
 
-def fill_bias(bias_ref, segq, segk, first_block, count):
-    key = lax.broadcasted_iota(jnp.int32, (2 * count, count), 0)
-    query = lax.broadcasted_iota(jnp.int32, (2 * count, count), 1)
-    ok = (key <= query + count) & (segk == segq) & (key >= first_block * count)
-    bias_ref[...] = jnp.where(ok, 0.0, NEG).astype(F32)
+def prepare(meta_ref, seg_ref, kv_ref, k_ref, v_ref, bias_ref, k_pair, v_pair, turned, of_keys):
+    count = k_ref.shape[0]
+    parts = count // LANES
+    first, row, earlier = meta_ref[AT_FIRST], meta_ref[AT_ROW], meta_ref[AT_EARLIER]
+    own = [seg_ref[pl.ds(row * parts + i, 1), :] for i in range(parts)]
+    before = [seg_ref[pl.ds(earlier * parts + i, 1), :] for i in range(parts)]
+    key_at = lax.broadcasted_iota(jnp.int32, (LANES, LANES), 0)
+    query_at = lax.broadcasted_iota(jnp.int32, (LANES, LANES), 1)
+    for i, keys in enumerate(before + own):
+        column = jnp.broadcast_to(keys.astype(F32), (LANES, LANES)).T
+        for j in range(parts):
+            ok = column == own[j].astype(F32)
+            if i < parts:
+                ok = ok & (first == 0)
+            else:
+                ok = ok & (key_at + (i - parts) * LANES <= query_at + j * LANES)
+            bias_ref[i * LANES:(i + 1) * LANES, j * LANES:(j + 1) * LANES] = jnp.where(
+                ok, 0.0, NEG
+            ).astype(F32)
+    k_pair[:count, :] = kv_ref[:, :HD]
+    k_pair[count:, :] = k_ref[...]
+    v_pair[:count, :] = kv_ref[:, HD:]
+    v_pair[count:, :] = v_ref[...]
+    turned[...] = (k_pair if of_keys else v_pair)[...].astype(F32).T.astype(BF)
+
+
+def pair_scratch(count):
+    return [
+        pltpu.VMEM((2 * count, count), F32),
+        pltpu.VMEM((2 * count, HD), BF),
+        pltpu.VMEM((2 * count, HD), BF),
+        pltpu.VMEM((HD, 2 * count), BF),
+    ]
 
 
 def chunk_list(count, width):
     return [(i * width, count + (i + 1) * width) for i in range(count // width)]
 
 
-def fwd_kernel(meta_ref, q_ref, k_ref, vt_ref, segq_ref, segk_ref, out_ref, top_ref, sum_ref, bias_ref):
+def fwd_kernel(
+    meta_ref, q_ref, kv_ref, k_ref, v_ref, seg_ref, out_ref, top_ref, sum_ref,
+    bias_ref, k_pair, v_pair, vt_ref,
+):
     count = q_ref.shape[0]
 
     @pl.when(pl.program_id(0) == 0)
     def _():
-        fill_bias(bias_ref, segq_ref[...], segk_ref[...], meta_ref[0], count)
+        prepare(meta_ref, seg_ref, kv_ref, k_ref, v_ref, bias_ref, k_pair, v_pair, vt_ref, False)
 
     for start, keys in chunk_list(count, 256):
         cols = slice(start, start + 256)
         s = lax.dot_general(
-            k_ref[:keys, :], q_ref[cols, :], (((1,), (1,)), ((), ())), preferred_element_type=F32
+            k_pair[:keys, :], q_ref[cols, :], (((1,), (1,)), ((), ())), preferred_element_type=F32
         )
         s = s * SCALE + bias_ref[:keys, cols]
         top = jnp.max(s, axis=0, keepdims=True)
@@ -88,10 +139,10 @@
         sum_ref[0, :, cols] = inv
 
 
-def attend(query, key_pair, vt, segq, segk, first):
+def attend(meta, query, kv_earlier, key_rows, value_rows, segments):
     count, width = query.shape
     heads = width // HD
-    whole = lambda shape: pl.BlockSpec(shape, lambda h, m: (0,) * len(shape))
+    whole = lambda value: pl.BlockSpec(value.shape, lambda h, m: (0, 0))
     head = pl.BlockSpec((count, HD), lambda h, m: (0, h))
     stat = pl.BlockSpec((1, 1, count), lambda h, m: (h, 0, 0))
     return pl.pallas_call(
@@ -99,15 +150,9 @@
         grid_spec=pltpu.PrefetchScalarGridSpec(
             num_scalar_prefetch=1,
             grid=(heads,),
-            in_specs=[
-                head,
-                whole((2 * count, HD)),
-                whole((HD, 2 * count)),
-                whole((1, count)),
-                whole((2 * count, 1)),
-            ],
+            in_specs=[head] + [whole(v) for v in (kv_earlier, key_rows, value_rows, segments)],
             out_specs=[head, stat, stat],
-            scratch_shapes=[pltpu.VMEM((2 * count, count), F32)],
+            scratch_shapes=pair_scratch(count),
         ),
         out_shape=[
             jax.ShapeDtypeStruct((count, width), BF),
@@ -121,20 +166,19 @@
             transcendentals=heads * 2 * count * count,
         ),
         name="attend",
-    )(first, query, key_pair, vt, segq, segk)
+    )(meta, query, kv_earlier, key_rows, value_rows, segments)
 
 
 def bwd_kernel(
-    n_held, last, meta_ref, q_ref, g_ref, k_ref, kt_ref, v_ref, segq_ref, segk_ref, top_ref, sum_ref,
-    *refs,
+    n_held, last, meta_ref, q_ref, g_ref, kv_ref, k_ref, v_ref, seg_ref, top_ref, sum_ref, *refs
 ):
     dk_in, dv_in = refs[:2] if n_held else (None, None)
-    dq_ref, dk_ref, dv_ref, bias_ref = refs[n_held:]
+    dq_ref, dk_ref, dv_ref, bias_ref, k_pair, v_pair, kt_ref = refs[n_held:]
     count = q_ref.shape[0]
 
     @pl.when(pl.program_id(0) == 0)
     def _():
-        fill_bias(bias_ref, segq_ref[...], segk_ref[...], meta_ref[0], count)
+        prepare(meta_ref, seg_ref, kv_ref, k_ref, v_ref, bias_ref, k_pair, v_pair, kt_ref, True)
         if n_held:
             dk_ref[...] = dk_in[...]
             dv_ref[...] = dv_in[...]
@@ -147,12 +191,12 @@
         q = q_ref[cols, :]
         g = g_ref[cols, :]
         s = lax.dot_general(
-            k_ref[:keys, :], q, (((1,), (1,)), ((), ())), preferred_element_type=F32
+            k_pair[:keys, :], q, (((1,), (1,)), ((), ())), preferred_element_type=F32
         )
         s = s * SCALE + bias_ref[:keys, cols]
         p = jnp.exp(s - top_ref[0, :, cols]) * sum_ref[0, :, cols]
         dp = lax.dot_general(
-            v_ref[:keys, :], g, (((1,), (1,)), ((), ())), preferred_element_type=F32
+            v_pair[:keys, :], g, (((1,), (1,)), ((), ())), preferred_element_type=F32
         )
         delta = jnp.sum(p * dp, axis=0, keepdims=True)
         ds = (p * (dp - delta)).astype(BF)
@@ -168,41 +212,35 @@
             dk_ref[...] = dk_ref[...] * SCALE
 
 
-def attend_back(query, grad, key_pair, kt, value_pair, segq, segk, first, top, total, heads, held):
+def attend_back(
+    meta, query, grad, kv_earlier, key_rows, value_rows, segments, top, total, heads, held
+):
     count, width = query.shape
     begin, end = heads
     last = end == width // HD
-    whole = lambda shape: pl.BlockSpec(shape, lambda h, m: (0,) * len(shape))
+    whole = lambda value: pl.BlockSpec(value.shape, lambda h, m: (0, 0))
     head = pl.BlockSpec((count, HD), lambda h, m: (0, h + begin))
     stat = pl.BlockSpec((1, 1, count), lambda h, m: (h + begin, 0, 0))
-    pair = whole((2 * count, HD))
+    pair = pl.BlockSpec((2 * count, HD), lambda h, m: (0, 0))
     earlier = () if held is None else (held[1], held[2], held[0])
     return pl.pallas_call(
         functools.partial(bwd_kernel, len(earlier), last),
         grid_spec=pltpu.PrefetchScalarGridSpec(
             num_scalar_prefetch=1,
             grid=(end - begin,),
-            in_specs=[
-                head,
-                head,
-                pair,
-                whole((HD, 2 * count)),
-                pair,
-                whole((1, count)),
-                whole((2 * count, 1)),
-                stat,
-                stat,
-            ]
+            in_specs=[head, head]
+            + [whole(v) for v in (kv_earlier, key_rows, value_rows, segments)]
+            + [stat, stat]
             + ([pair, pair, pl.BlockSpec(memory_space=pl.ANY)] if earlier else []),
             out_specs=[head, pair, pair],
-            scratch_shapes=[pltpu.VMEM((2 * count, count), F32)],
+            scratch_shapes=pair_scratch(count),
         ),
         out_shape=[
             jax.ShapeDtypeStruct((count, width), BF),
             jax.ShapeDtypeStruct((2 * count, HD), F32),
             jax.ShapeDtypeStruct((2 * count, HD), F32),
         ],
-        input_output_aliases={12: 0} if earlier else {},
+        input_output_aliases={11: 0} if earlier else {},
         compiler_params=params(22),
         cost_estimate=pl.CostEstimate(
             flops=(end - begin) * 10 * 2 * 2 * count * count * HD,
@@ -210,10 +248,11 @@
             transcendentals=(end - begin) * 2 * count * count,
         ),
         name="attend_back",
-    )(first, query, grad, key_pair, kt, value_pair, segq, segk, top, total, *earlier)
-
-
-def proj_kernel(n_in, held, plan, meta_ref, *refs):
+    )(meta, query, grad, kv_earlier, key_rows, value_rows, segments, top, total, *earlier)
+
+
+def proj_kernel(slots, held, plan, meta_ref, *refs):
+    n_in = len(slots)
     pieces, a_ref = refs[:n_in], refs[n_in]
     refs = refs[n_in + 1 + held:]
     buffer_ref, taken = refs[0], refs[1:-3]
@@ -222,19 +261,19 @@
     rows = done.shape[2]
 
     def put(j):
-        return pltpu.make_async_copy(done.at[j], buffer_ref.at[:, meta_ref[j]], sems.at[j])
+        return pltpu.make_async_copy(done.at[j], buffer_ref.at[:, meta_ref[AT_G + slots[j]]], sems.at[j])
 
     def take(i, made):
         out, start, at, half, first, count = plan[i]
         if made is None:
-            source = buffer_ref.at[half, meta_ref[n_in + at], pl.ds(first, count)]
+            source = buffer_ref.at[half, meta_ref[at], pl.ds(first, count)]
         else:
             source = done.at[made, half, pl.ds(first, count)]
         target = taken[out].at[pl.ds(start, count)]
         return pltpu.make_async_copy(source, target, take_sems.at[i])
 
     def made_here(i, j):
-        return meta_ref[n_in + plan[i][2]] == meta_ref[j]
+        return meta_ref[plan[i][2]] == meta_ref[AT_G + slots[j]]
 
     @pl.when(step == 0)
     def _():
@@ -271,7 +310,7 @@
             take(i, None).wait()
 
 
-def project(pieces, a_pair, blocks, buffer, plan=()):
+def project(pieces, a_pair, meta, slots, buffer, plan=()):
     tokens, width = a_pair.shape
     depth = pieces[0].shape[1]
     n_blocks = len(pieces)
@@ -283,7 +322,7 @@
     n_taken = 1 + max((entry[0] for entry in plan), default=-1)
     taken = [(sum(e[5] for e in plan if e[0] == i), width) for i in range(n_taken)]
     out = pl.pallas_call(
-        functools.partial(proj_kernel, n_blocks, held, plan),
+        functools.partial(proj_kernel, tuple(slots), held, plan),
         grid_spec=pltpu.PrefetchScalarGridSpec(
             num_scalar_prefetch=1,
             grid=(n_blocks,),
@@ -305,7 +344,7 @@
             transcendentals=0,
         ),
         name="project",
-    )(blocks, *operands)
+    )(meta, *operands)
     return out if n_taken else out[0]
 
 
@@ -324,7 +363,7 @@
 
     def w_copy(n):
         ref, source, block, part = wplan[n]
-        place = meta_ref[8 + block]
+        place = meta_ref[AT_W + block]
         return pltpu.make_async_copy(
             w_in[ref].at[pl.ds(source, wh)],
             wbuf.at[place, pl.ds(part * wh, wh)],
@@ -344,7 +383,7 @@
         def _():
             g_copy(j).wait()
 
-    place = meta_ref[step]
+    place = meta_ref[AT_G + step]
     for part in range(2):
         pltpu.make_async_copy(
             w_in[0].at[pl.ds(0, wh)], wbuf.at[place, pl.ds(part * wh, wh)], wsems.at[part, place]
@@ -405,12 +444,12 @@
     )(meta, *g_pieces, *w_pieces)
 
 
-def add_kernel(n_terms, plan, joined, meta_ref, buffer_ref, *refs):
+def add_kernel(places, n_terms, plan, joined, meta_ref, buffer_ref, *refs):
     terms, outs = refs[:n_terms], refs[n_terms:-2]
     blocks, sems = refs[-2:]
     rows = blocks.shape[2]
     copies = [
-        pltpu.make_async_copy(buffer_ref.at[:, meta_ref[n]], blocks.at[n], sems.at[n])
+        pltpu.make_async_copy(buffer_ref.at[:, meta_ref[places[n]]], blocks.at[n], sems.at[n])
         for n in range(blocks.shape[0])
     ]
     for copy in copies:
@@ -427,20 +466,20 @@
             outs[n][...] = value.astype(BF)
 
 
-def add_blocks(buffer, blocks, terms, plan, joined=False):
+def add_blocks(buffer, meta, places, terms, plan, joined=False):
     _, _, rows, width = buffer.shape
     here = pl.BlockSpec(memory_space=pltpu.VMEM)
     shapes = [(len(plan) * rows, width)] if joined else [(rows, width)] * len(plan)
     return pl.pallas_call(
-        functools.partial(add_kernel, len(terms), plan, joined),
+        functools.partial(add_kernel, tuple(places), len(terms), plan, joined),
         grid_spec=pltpu.PrefetchScalarGridSpec(
             num_scalar_prefetch=1,
             grid=(1,),
             in_specs=[pl.BlockSpec(memory_space=pltpu.HBM)] + [here] * len(terms),
             out_specs=[here] * len(shapes),
             scratch_shapes=[
-                pltpu.VMEM((blocks.shape[0], 2, rows, width), BF),
-                pltpu.SemaphoreType.DMA((blocks.shape[0],)),
+                pltpu.VMEM((len(places), 2, rows, width), BF),
+                pltpu.SemaphoreType.DMA((len(places),)),
             ],
         ),
         out_shape=[jax.ShapeDtypeStruct(shape, BF) for shape in shapes],
@@ -449,11 +488,11 @@
             flops=2**21, bytes_accessed=5 * 2**20, transcendentals=0
         ),
         name="add_blocks",
-    )(blocks, buffer, *terms)
+    )(meta, buffer, *terms)
 
 
 def last_kernel(meta_ref, buffer_ref, across, nup, ndn, rup, up2, rdn, dn2, out_ref, block, sem):
-    copy = pltpu.make_async_copy(buffer_ref.at[:, meta_ref[0]], block, sem)
+    copy = pltpu.make_async_copy(buffer_ref.at[:, meta_ref[at_w(0, 0)]], block, sem)
     copy.start()
     copy.wait()
     half, quarter = nup.shape[0], up2.shape[0]
@@ -474,7 +513,7 @@
             ).astype(BF)
 
 
-def last_sum(buffer, place, *terms):
+def last_sum(buffer, meta, *terms):
     _, _, rows, width = buffer.shape
     here = pl.BlockSpec(memory_space=pltpu.VMEM)
     return pl.pallas_call(
@@ -492,49 +531,32 @@
             flops=2**21, bytes_accessed=5 * 2**20, transcendentals=0
         ),
         name="last_sum",
-    )(place, buffer, *terms)
+    )(meta, buffer, *terms)
 
 
 def local(query_rows, key_rows, value_rows, output_grad, out_proj, segment_ids):
     count = query_rows.shape[0]
     half_d = output_grad.shape[1] // 2
     row, col = lax.axis_index("row"), lax.axis_index("col")
-    z, yh, k = row // 4, row // 2 % 2, row % 2
-    yl, x = col // 4, col % 4
-
-    def gblock(dyl, dx):
-        return (yl + dyl) % 2 * 4 + (x + dx) % 4
-
-    def wblock(dz, dy):
-        return (z + dz) % 4 * 2 + (yh + dy) % 2
-
-    def ints(*values):
-        return jnp.stack([jnp.asarray(v, jnp.int32) for v in values])
+    meta = positions(row, col)
+    k = row % 2
 
     g_keep = lax.dynamic_slice_in_dim(output_grad, k * half_d, half_d, 1)
     g_give = lax.dynamic_slice_in_dim(output_grad, (1 - k) * half_d, half_d, 1)
-    g0 = jnp.concatenate([g_keep, move_row(g_give, dk=1)], 0)
-    kv = jnp.concatenate([key_rows, value_rows], 1)
-    kv_earlier = passed_along(kv, "row", 1)
-
+    g_got, meta = tied((move_row(g_give, dk=1), meta))
+    g0 = jnp.concatenate([g_keep, g_got], 0)
+    kv_earlier = passed_along(jnp.concatenate([key_rows, value_rows], 1), "row", 1)
+    segments = segment_ids.reshape(-1, LANES)
+
+    (out_proj,) = tied((out_proj,), g0)
     gxm = move_col(g0, dx=1)
     gxp = move_col(g0, dx=-1)
     gy = move_col(g0, dyl=1)
     wzm = move_row(out_proj, dz=1)
     wzp = move_row(out_proj, dz=-1)
 
-    kv_pair = jnp.concatenate([kv_earlier, kv], 0)
-    key_pair, value_pair = kv_pair[:, :HD], kv_pair[:, HD:]
-    key_t, value_t = key_pair.T, value_pair.T
-    seg_query = lax.dynamic_slice_in_dim(segment_ids, row * count, count, 0)
-    seg_earlier = lax.dynamic_slice_in_dim(
-        segment_ids, jnp.maximum(row - 1, 0) * count, count, 0
-    )
-    segk = jnp.concatenate([seg_earlier, seg_query], 0)[:, None]
-    segq = seg_query[None, :]
-    first = ints(row == 0)
     (query_held,) = tied((query_rows,), g0)
-    attn_out, top, total = attend(query_held, key_pair, value_t, segq, segk, first)
+    attn_out, top, total = attend(meta, query_held, kv_earlier, key_rows, value_rows, segments)
 
     wzm, wzp, gxm, gxp, gy, attn_out = tied((wzm, wzp, gxm, gxp, gy, attn_out))
 
@@ -546,12 +568,7 @@
     wy = move_row(out_proj, dyh=1)
 
     a_pair = jnp.concatenate([attn_out, a_other], 0)
-    proj = project(
-        [g0, gxm, gxp, gy],
-        a_pair,
-        ints(gblock(0, 0), gblock(0, -1), gblock(0, 1), gblock(1, 0)),
-        None,
-    )
+    proj = project([g0, gxm, gxp, gy], a_pair, meta, range(4), None)
 
     go = move_col(gxm, dx=1)
     wo, wy, gyxm, gyxp, proj = tied((wo, wy, gyxm, gyxp, proj))
@@ -560,25 +577,24 @@
     wyzp = move_row(wy, dz=-1)
     wyo = move_row(wo, dyh=1)
 
-    proj = project([gyxm, gyxp], a_pair, ints(gblock(1, -1), gblock(1, 1)), proj)
-
-    go, gyo, proj = tied((go, gyo, proj))
+    proj = project([gyxm, gyxp], a_pair, meta, (4, 5), proj)
+    proj = project([go], a_pair, meta, (6,), proj)
 
     q = hw // 2
+    far, up, dn = at_w(2, 1), at_w(1, 1), at_w(-1, 1)
+    own_up, own_dn = at_w(1, 0), at_w(-1, 0)
     proj, give_far, give_up, give_dn, up2, dn2 = project(
-        [go, gyo],
+        [gyo],
         a_pair,
-        ints(
-            gblock(0, 2), gblock(1, 2),
-            wblock(2, 1), wblock(1, 1), wblock(-1, 1), wblock(1, 0), wblock(-1, 0),
-        ),
+        meta,
+        (7,),
         proj,
         (
-            (0, 0, 0, 0, 0, hw), (0, hw, 0, 1, 0, hw),
-            (1, 0, 1, 0, 0, hw), (1, hw, 1, 1, 0, hw), (1, 2 * hw, 3, 1, 0, q),
-            (2, 0, 2, 0, 0, hw), (2, hw, 2, 1, 0, hw), (2, 2 * hw, 4, 0, 0, q),
-            (3, 0, 3, 1, q, q),
-            (4, 0, 4, 0, q, q),
+            (0, 0, far, 0, 0, hw), (0, hw, far, 1, 0, hw),
+            (1, 0, up, 0, 0, hw), (1, hw, up, 1, 0, hw), (1, 2 * hw, own_up, 1, 0, q),
+            (2, 0, dn, 0, 0, hw), (2, hw, dn, 1, 0, hw), (2, 2 * hw, own_dn, 0, 0, q),
+            (3, 0, own_up, 1, q, q),
+            (4, 0, own_dn, 0, q, q),
         ),
     )
     give_far, give_up, give_dn, wyzm, wyzp, wyo = tied(
@@ -591,25 +607,22 @@
     g_pieces = [g0, gxm, gxp, gy, gyxm, gyxp, go, gyo]
     w_pieces = [out_proj, wzm, wzp, wy, wyzm, wyzp, wyo, wo]
     wplan = [(i, p * hw, i, p) for i in range(8) for p in range(2)]
-    meta = ints(
-        gblock(0, 0), gblock(0, -1), gblock(0, 1), gblock(1, 0),
-        gblock(1, -1), gblock(1, 1), gblock(0, 2), gblock(1, 2),
-        wblock(0, 0), wblock(-1, 0), wblock(1, 0), wblock(0, 1),
-        wblock(-1, 1), wblock(1, 1), wblock(2, 1), wblock(2, 0),
-    )
     (meta,) = tied((meta,), give_up)
     grad_own, grad_give = attn_grad_part(g_pieces, w_pieces, wplan, meta)
 
     ry, grad_own, grad_give = tied((ry, grad_own, grad_give))
 
-    far_up, far_dn = add_blocks(proj, ints(wblock(2, 0)), [ry], ((0, 0, ((0, 0),)), (0, 1, ((0, hw),))))
+    far_up, far_dn = add_blocks(
+        proj, meta, [at_w(2, 0)], [ry], ((0, 0, ((0, 0),)), (0, 1, ((0, hw),)))
+    )
     fup = move_row(far_up, dz=1)
     fdn = move_row(far_dn, dz=-1)
     grad_got = move_row(grad_give, dk=1)
     rup, rdn = tied((rup, rdn), far_up)
     (across,) = add_blocks(
         proj,
-        ints(wblock(0, 1)),
+        meta,
+        [at_w(0, 1)],
         [rup, rdn],
         ((0, 0, ((0, 0), (1, 0))), (0, 1, ((0, hw), (1, hw)))),
         joined=True,
@@ -622,7 +635,7 @@
     attn_grad = (grad_own + grad_got.astype(F32)).astype(BF)
     (attn_grad,) = tied((attn_grad,), rup)
     part = functools.partial(
-        attend_back, query_rows, attn_grad, key_pair, key_t, value_pair, segq, segk, first, top, total
+        attend_back, meta, query_rows, attn_grad, kv_earlier, key_rows, value_rows, segments, top, total
     )
     heads = query_rows.shape[1] // HD
     cut = 3 * heads // 8
@@ -632,7 +645,8 @@
 
     near_up, near_dn = add_blocks(
         proj,
-        ints(wblock(1, 0), wblock(-1, 0)),
+        meta,
+        [own_up, own_dn],
         [fup, fdn],
         ((0, 0, ((0, 0),)), (1, 1, ((1, 0),))),
     )
@@ -648,7 +662,7 @@
     key_grad = (dkey[count:] + back[:, :HD]).astype(BF)
     value_grad = (dvalue[count:] + back[:, HD:]).astype(BF)
 
-    proj_grad = last_sum(proj, ints(wblock(0, 0)), across, nup, ndn, rup, up2, rdn, dn2)
+    proj_grad = last_sum(proj, meta, across, nup, ndn, rup, up2, rdn, dn2)
     return (query_grad, key_grad, value_grad, proj_grad)
 
 

time: 179 us -> 174 us (0.972)
  waiting for transfers between devices: 34.2 us -> 51.1 us
  local copies, waits for them, and re-layouts: 16.4 us -> 2.52 us
  Pallas kernels: 77.8 us -> 74 us
    ppermute x20, waiting for transfers between devices: 12.3 us -> 29.6 us  [move_row(): return lax.ppermute(value, 'row', pairs)]
    unnamed x50 -> x17, local copies, waits for them, and re-layouts: 12.2 us -> 0.11 us
    pallas_call x6 -> x7, Pallas kernels: 27.6 us -> 24.1 us  [the longest x4 17.6 us: project(): pl.pallas_call(functools.partial(proj_kernel, tuple(slots), held, plan),...]
    ppermute x20, starting transfers between devices: 29.4 us -> 27.5 us  [move_row(): return lax.ppermute(value, 'row', pairs)]
    pallas_call x1, Pallas kernels: 14.5 us -> 12.6 us  [attn_grad_part(): pl.pallas_call(kernel, grid_spec=pltpu.PrefetchScalarGridSpec(num_scalar_...]
  transfers between devices with their start and end apart: 29 -> 29, of which waited for: 11 -> 12; matrix products, arithmetic and copies ran while one was open for 4% -> 1% of each run, Pallas kernels for 44% -> 43%
where the time goes in v7:
time: 174 us
  Pallas kernels  74 us (43%)
  waiting for transfers between devices  51.1 us (29%)
  starting transfers between devices  42.9 us (25%)
  local copies, waits for them, and re-layouts  2.52 us (1%)
  other arithmetic  2.35 us (1%)
    ppermute x20, waiting for transfers between devices, move_row(): return lax.ppermute(value, 'row', pairs)  29.6 us
    ppermute x20, starting transfers between devices, move_row(): return lax.ppermute(value, 'row', pairs)  27.5 us
    ppermute x7, waiting for transfers between devices, move_col(): return lax.ppermute(value, 'col', pairs)  20.3 us
    pallas_call x2, Pallas kernels, attend_back(): pl.pallas_call(functools.partial(bwd_kernel, len(earlier), last), grid_sp...  19.1 us
    pallas_call x4, Pallas kernels, project(): pl.pallas_call(functools.partial(proj_kernel, tuple(slots), held, plan),...  17.6 us
    pallas_call x1, Pallas kernels, attend(): pl.pallas_call(fwd_kernel, grid_spec=pltpu.PrefetchScalarGridSpec(num_sca...  14.9 us
    pallas_call x1, Pallas kernels, attn_grad_part(): pl.pallas_call(kernel, grid_spec=pltpu.PrefetchScalarGridSpec(num_scalar_...  12.6 us
    ppermute x2, starting transfers between devices, passed_along(): lax.ppermute(value, axis, [(source, source + steps) for source in range(f...  10.3 us
  transfers between devices with their start and end apart: 29, of which 12 were waited for; matrix products, arithmetic and copies ran while one was open for 1% of the time, Pallas kernels for 43%

profile of v7, /device:TPU:1, one launch (start us, length us, event | category | flops | bytes accessed | tf_op | source)
XLA Modules:
  0.0 173.8 jit_solution(9487044679525939140)
XLA Ops:
  0.6 0.0 copy-start.5
  0.6 0.0 copy-start.6
  0.7 0.0 copy-start.7
  0.7 2.2 %constant_dynamic-slice_fusion = (bf16[512,512]{1,0:T(8,128)(2,1)S(1)}, bf16[512,512]{1,0:T(8,128)(2,1)}) fusion(bf16[512,1024]{1,0:T(8,128)(2,1)} %param.13, s32[]{:T(128)S(6)} %select_n.38, s32[]{:T(128)S(6)} %select_n.32), kind=kLoop, calls=%fused_computation.14 | loop fusion | bytes 2097160 | tf_op jit(solution)/shard_map/dynamic_slice | solution.py:544
  3.0 1.4 collective-permute-start
  4.4 4.8 %collective-permute-start.6 = (bf16[512,256]{1,0:T(8,128)(2,1)S(1)}, bf16[512,256]{1,0:T(8,128)(2,1)S(1)}, u32[]{:S(2)}, u32[]{:S(2)}) collective-permute-start(bf16[512,256]{1,0:T(8,128)(2,1)S(1)} %pad_maximum_fusion.1), channel_id=1, source_target_pairs={{0,8},{8,16},{16,24},{24,32},{32,40},{40,48},{48,56},{56,64},{64,7... | collective-permute-start | bytes 786440 | tf_op jit(solution)/shard_map/ppermute | solution.py:64
  9.3 0.1 concatenate.16.meta_ref
  9.4 0.0 collective-permute-done
  9.4 1.1 pad_maximum_fusion.refs_0_
  10.6 1.7 collective-permute-start.1
  12.3 2.2 %collective-permute-start.2 = (bf16[512,1024]{1,0:T(8,128)(2,1)S(1)}, bf16[512,1024]{1,0:T(8,128)(2,1)S(1)}, u32[]{:S(2)}, u32[]{:S(2)}) collective-permute-start(bf16[512,1024]{1,0:T(8,128)(2,1)S(1)} %copy-done.2), channel_id=1, source_target_pairs={{0,96},{8,104},{16,112},{24,120},{32,0},{40,8},{48,16},{56,24},{64... | collective-permute-start | bytes 3145736 | tf_op jit(solution)/shard_map/ppermute | solution.py:50
  14.5 1.2 collective-permute-start.3
  15.7 1.5 collective-permute-start.4
  17.2 0.4 collective-permute-start.5
  17.6 14.9 %attend.1 = (bf16[512,1024]{1,0:T(8,128)(2,1)S(1)}, f32[8,1,512]{2,1,0:T(1,128)S(1)}, f32[8,1,512]{2,1,0:T(1,128)S(1)}) custom-call(s32[24]{0:T(128)S(1)} %concatenate.16.meta_ref, bf16[512,1024]{1,0:T(8,128)(2,1)S(1)} %copy-done.3, bf16[512,256]{1,0:T(8,128)(2,1)S(1)} %collective-permute-done.6.kv_ref, bf16[512,128]{1,0:T(8,128)(2,1)S(1)} %copy-done.1, ...), custom_call_target="tpu_custom_call" | custom-call | flops 4294967296 | bytes 8388608 | tf_op jit(solution)/shard_map/attend/pallas_call | solution.py:148
  32.5 3.8 %collective-permute-done.1.refs_9_ = bf16[512,1024]{1,0:T(8,128)(2,1)S(1)} collective-permute-done((bf16[512,1024]{1,0:T(8,128)(2,1)S(1)}, bf16[512,1024]{1,0:T(8,128)(2,1)S(1)}, u32[]{:S(2)}, u32[]{:S(2)}) %collective-permute-start.1) | collective-permute-done | bytes 1048608 | tf_op jit(solution)/shard_map/ppermute | solution.py:50
  36.2 0.0 collective-permute-done.2.refs_10_
  36.2 2.8 %collective-permute-done.3.refs_1_ = bf16[1024,512]{1,0:T(8,128)(2,1)S(1)} collective-permute-done((bf16[1024,512]{1,0:T(8,128)(2,1)S(1)}, bf16[1024,512]{1,0:T(8,128)(2,1)S(1)}, u32[]{:S(2)}, u32[]{:S(2)}) %collective-permute-start.3) | collective-permute-done | bytes 1048608 | tf_op jit(solution)/shard_map/ppermute | solution.py:58
  39.0 0.6 collective-permute-done.4.refs_2_
  39.6 1.5 collective-permute-done.5.refs_3_
  41.0 2.4 %collective-permute-start.8 = (bf16[512,1024]{1,0:T(8,128)(2,1)S(1)}, bf16[512,1024]{1,0:T(8,128)(2,1)S(1)}, u32[]{:S(2)}, u32[]{:S(2)}) collective-permute-start(bf16[512,1024]{1,0:T(8,128)(2,1)S(1)} %copy-done.2), channel_id=1, source_target_pairs={{0,16},{8,24},{16,0},{24,8},{32,48},{40,56},{48,32},{56,40},{64,80... | collective-permute-start | bytes 3145736 | tf_op jit(solution)/shard_map/ppermute | solution.py:50
  43.4 1.3 collective-permute-start.10
  44.7 0.4 collective-permute-start.7
  45.1 0.2 collective-permute-start.9
  45.3 0.1 constant_dynamic-update-slice_fusion.1
  45.4 0.1 collective-permute-start.13
  45.5 0.1 constant_dynamic-update-slice_fusion.refs_4_.refs_2_.refs_1_
  45.6 6.7 %project.4.refs_3_ = bf16[2,64,256,1024]{3,2,1,0:T(8,128)(2,1)} custom-call(s32[24]{0:T(128)S(1)} %concatenate.16.meta_ref, bf16[1024,512]{1,0:T(8,128)(2,1)S(1)} %pad_maximum_fusion.refs_0_, bf16[1024,512]{1,0:T(8,128)(2,1)S(1)} %collective-permute-done.3.refs_1_, bf16[1024,512]{1,0:T(8,128)(2,1)S(1)} %collective-permute-done.4.refs_2_, ...), custom_call_target="tpu_custom_call" | custom-call | flops 4294967296 | bytes 10485760 | tf_op jit(solution)/shard_map/project/pallas_call | solution.py:324
  52.3 14.5 %collective-permute-done.8.refs_11_ = bf16[512,1024]{1,0:T(8,128)(2,1)S(1)} collective-permute-done((bf16[512,1024]{1,0:T(8,128)(2,1)S(1)}, bf16[512,1024]{1,0:T(8,128)(2,1)S(1)}, u32[]{:S(2)}, u32[]{:S(2)}) %collective-permute-start.8) | collective-permute-done | bytes 1048608 | tf_op jit(solution)/shard_map/ppermute | solution.py:50
  66.8 1.1 collective-permute-done.10.refs_1_.refs_5_
  67.9 2.2 %collective-permute-done.7.refs_15_ = bf16[512,1024]{1,0:T(8,128)(2,1)S(1)} collective-permute-done((bf16[512,1024]{1,0:T(8,128)(2,1)S(1)}, bf16[512,1024]{1,0:T(8,128)(2,1)S(1)}, u32[]{:S(2)}, u32[]{:S(2)}) %collective-permute-start.7) | collective-permute-done | bytes 1048608 | tf_op jit(solution)/shard_map/ppermute | solution.py:50
  70.1 0.1 collective-permute-done.9.refs_0_.refs_4_
  70.2 0.4 collective-permute-start.12
  70.6 0.9 collective-permute-start.14
  71.5 1.8 %collective-permute-start.15 = (bf16[512,1024]{1,0:T(8,128)(2,1)S(1)}, bf16[512,1024]{1,0:T(8,128)(2,1)S(1)}, u32[]{:S(2)}, u32[]{:S(2)}) collective-permute-start(bf16[512,1024]{1,0:T(8,128)(2,1)S(1)} %collective-permute-done.8.refs_11_), channel_id=1, source_target_pairs={{0,96},{8,104},{16,112},{24,120},{32,0},{40,8},{48,16},{56,24},{64... | collective-permute-start | bytes 3145736 | tf_op jit(solution)/shard_map/ppermute | solution.py:50
  73.3 0.9 collective-permute-start.16
  74.2 4.2 %project.5.refs_2_ = bf16[2,64,256,1024]{3,2,1,0:T(8,128)(2,1)} custom-call(s32[24]{0:T(128)S(1)} %concatenate.16.meta_ref, bf16[1024,512]{1,0:T(8,128)(2,1)S(1)} %collective-permute-done.9.refs_0_.refs_4_, bf16[1024,512]{1,0:T(8,128)(2,1)S(1)} %collective-permute-done.10.refs_1_.refs_5_, ...), custom_call_target="tpu_custom_call", output_to_operand_aliasing={{}: (4, {})} | custom-call | flops 2147483648 | bytes 6291456 | tf_op jit(solution)/shard_map/project/pallas_call | solution.py:324
  78.4 14.3 %collective-permute-done.13.refs_0_.refs_6_ = bf16[1024,512]{1,0:T(8,128)(2,1)S(1)} collective-permute-done((bf16[1024,512]{1,0:T(8,128)(2,1)S(1)}, bf16[1024,512]{1,0:T(8,128)(2,1)S(1)}, u32[]{:S(2)}, u32[]{:S(2)}) %collective-permute-start.13) | collective-permute-done | bytes 1048608 | tf_op jit(solution)/shard_map/ppermute | solution.py:58
  92.6 2.8 %project.6.refs_2_ = bf16[2,64,256,1024]{3,2,1,0:T(8,128)(2,1)} custom-call(s32[24]{0:T(128)S(1)} %concatenate.16.meta_ref, bf16[1024,512]{1,0:T(8,128)(2,1)S(1)} %collective-permute-done.13.refs_0_.refs_6_, bf16[1024,1024]{1,0:T(8,128)(2,1)S(1)} %constant_dynamic-update-slice_fusion.refs_4_.refs_2_.refs_1_, ...), custom_call_target="tpu_custom_call", output_to_operand_aliasing={{}: (3, {})} | custom-call | flops 1073741824 | bytes 4194304 | tf_op jit(solution)/shard_map/project/pallas_call | solution.py:324
  95.4 3.9 %project.7 = (bf16[2,64,256,1024]{3,2,1,0:T(8,128)(2,1)}, bf16[512,1024]{1,0:T(8,128)(2,1)S(1)}, bf16[640,1024]{1,0:T(8,128)(2,1)S(1)}, bf16[640,1024]{1,0:T(8,1...) custom-call(s32[24]{0:T(128)S(1)} %concatenate.16.meta_ref, ...), custom_call_target="tpu_custom_call", output_to_operand_aliasing={{0}: (3, {})} | custom-call | flops 1073741824 | bytes 4194304 | tf_op jit(solution)/shard_map/project/pallas_call | solution.py:324
  99.4 1.2 collective-permute-start.17
  100.6 1.5 collective-permute-start.19
  102.1 1.2 collective-permute-start.20
  103.3 12.6 %attn_grad.1 = (f32[512,1024]{1,0:T(8,128)S(1)}, bf16[512,1024]{1,0:T(8,128)(2,1)S(1)}) custom-call(s32[24]{0:T(128)S(1)} %concatenate.16.meta_ref, bf16[1024,512]{1,0:T(8,128)(2,1)S(1)} %pad_maximum_fusion.refs_0_, bf16[1024,512]{1,0:T(8,128)(2,1)S(1)} %collective-permute-done.3.refs_1_, bf16[1024,512]{1,0:T(8,128)(2,1)S(1)} %collective-permute-done.4.refs_2_, ...), custom_call_target="tpu_custom_call" | custom-call | flops 8589934592 | bytes 20971520 | tf_op jit(solution)/shard_map/attn_grad/pallas_call | solution.py:418
  115.9 8.0 %collective-permute-done.17.refs_0_ = bf16[512,1024]{1,0:T(8,128)(2,1)S(1)} collective-permute-done((bf16[512,1024]{1,0:T(8,128)(2,1)S(1)}, bf16[512,1024]{1,0:T(8,128)(2,1)S(1)}, u32[]{:S(2)}, u32[]{:S(2)}) %collective-permute-start.17) | collective-permute-done | bytes 1048608 | tf_op jit(solution)/shard_map/ppermute | solution.py:50
  123.9 2.7 %collective-permute-start.18 = (bf16[512,1024]{1,0:T(8,128)(2,1)S(1)}, bf16[512,1024]{1,0:T(8,128)(2,1)S(1)}, u32[]{:S(2)}, u32[]{:S(2)}) collective-permute-start(bf16[512,1024]{1,0:T(8,128)(2,1)S(1)} %get-tuple-element.97), channel_id=1, source_target_pairs={{0,8},{8,0},{16,24},{24,16},{32,40},{40,32},{48,56},{56,48},{64,72... | collective-permute-start | bytes 3145736 | tf_op jit(solution)/shard_map/ppermute | solution.py:50
  126.6 2.0 %add_blocks.3 = (bf16[256,1024]{1,0:T(8,128)(2,1)S(1)}, bf16[256,1024]{1,0:T(8,128)(2,1)S(1)}) custom-call(s32[24]{0:T(128)S(1)} %concatenate.16.meta_ref, bf16[2,64,256,1024]{3,2,1,0:T(8,128)(2,1)} %get-tuple-element.99.buffer_ref, bf16[512,1024]{1,0:T(8,128)(2,1)S(1)} %collective-permute-done.17.refs_0_), custom_call_target="tpu_custom_call" | custom-call | flops 2097152 | bytes 5242880 | tf_op jit(solution)/shard_map/add_blocks/pallas_call | solution.py:473
  128.6 1.6 collective-permute-start.21
  130.1 1.2 collective-permute-start.22
  131.3 0.3 collective-permute-start.23
  131.6 2.4 %collective-permute-start.24 = (bf16[128,1024]{1,0:T(8,128)(2,1)S(1)}, bf16[128,1024]{1,0:T(8,128)(2,1)S(1)}, u32[]{:S(2)}, u32[]{:S(2)}) collective-permute-start(bf16[128,1024]{1,0:T(8,128)(2,1)S(1)} %get-tuple-element.116), channel_id=1, source_target_pairs={{0,96},{8,104},{16,112},{24,120},{32,0},{40,8},{48,16},{56,24},{64... | collective-permute-start | bytes 786440 | tf_op jit(solution)/shard_map/ppermute | solution.py:50
  134.0 2.1 %add_blocks.5 = bf16[512,1024]{1,0:T(8,128)(2,1)S(1)} custom-call(s32[24]{0:T(128)S(1)} %concatenate.16.meta_ref, bf16[2,64,256,1024]{3,2,1,0:T(8,128)(2,1)} %get-tuple-element.99.buffer_ref, bf16[640,1024]{1,0:T(8,128)(2,1)S(1)} %collective-permute-done.19.refs_0_.rup, bf16[640,1024]{1,0:T(8,128)(2,1)S(1)} %collective-permute-done.20.refs_1_.rdn), custom_call_target="tpu_custom_call" | custom-call | flops 2097152 | bytes 5242880 | tf_op jit(solution)/shard_map/add_blocks/pallas_call | solution.py:473
  136.2 1.4 collective-permute-start.28
  137.6 0.3 add_convert_fusion.g_ref
  138.0 7.5 %attend_back.2 = (bf16[512,1024]{1,0:T(8,128)(2,1)}, f32[1024,128]{1,0:T(8,128)S(1)}, f32[1024,128]{1,0:T(8,128)S(1)}) custom-call(s32[24]{0:T(128)S(1)} %concatenate.16.meta_ref, bf16[512,1024]{1,0:T(8,128)(2,1)S(1)} %copy-done.3, bf16[512,1024]{1,0:T(8,128)(2,1)S(1)} %add_convert_fusion.g_ref, bf16[512,256]{1,0:T(8,128)(2,1)S(1)} %collective-permute-done.6.kv_ref, ...), custom_call_target="tpu_custom_call" | custom-call | flops 4026531840 | bytes 6291456 | tf_op jit(solution)/shard_map/attend_back/pallas_call | solution.py:226
  145.5 2.3 %add_blocks.4 = (bf16[256,1024]{1,0:T(8,128)(2,1)S(1)}, bf16[256,1024]{1,0:T(8,128)(2,1)S(1)}) custom-call(s32[24]{0:T(128)S(1)} %concatenate.16.meta_ref, bf16[2,64,256,1024]{3,2,1,0:T(8,128)(2,1)} %get-tuple-element.99.buffer_ref, bf16[256,1024]{1,0:T(8,128)(2,1)S(1)} %collective-permute-done.21.refs_0_, bf16[256,1024]{1,0:T(8,128)(2,1)S(1)} %collective-permute-done.22.refs_1_), custom_call_target="tpu_custom_call" | custom-call | flops 2097152 | bytes 5242880 | tf_op jit(solution)/shard_map/add_blocks/pallas_call | solution.py:473
  147.8 0.1 collective-permute-start.25
  147.9 1.2 collective-permute-done.23.up2
  149.2 2.4 %collective-permute-start.26 = (bf16[256,1024]{1,0:T(8,128)(2,1)S(1)}, bf16[256,1024]{1,0:T(8,128)(2,1)S(1)}, u32[]{:S(2)}, u32[]{:S(2)}) collective-permute-start(bf16[256,1024]{1,0:T(8,128)(2,1)S(1)} %get-tuple-element.126), channel_id=1, source_target_pairs={{0,96},{8,104},{16,112},{24,120},{32,0},{40,8},{48,16},{56,24},{64... | collective-permute-start | bytes 1572872 | tf_op jit(solution)/shard_map/ppermute | solution.py:50
  151.5 11.6 %attend_back.3 = (bf16[512,1024]{1,0:T(8,128)(2,1)}, f32[1024,128]{1,0:T(8,128)S(1)}, f32[1024,128]{1,0:T(8,128)S(1)}) custom-call(s32[24]{0:T(128)S(1)} %concatenate.16.meta_ref, bf16[512,1024]{1,0:T(8,128)(2,1)S(1)} %copy-done.3, bf16[512,1024]{1,0:T(8,128)(2,1)S(1)} %add_convert_fusion.g_ref, ...), custom_call_target="tpu_custom_call", output_to_operand_aliasing={{0}: (11, {})} | custom-call | flops 6710886400 | bytes 6291456 | tf_op jit(solution)/shard_map/attend_back/pallas_call | solution.py:226
  163.2 5.5 %collective-permute-start.27 = (bf16[512,256]{1,0:T(8,128)(2,1)S(1)}, bf16[512,256]{1,0:T(8,128)(2,1)S(1)}, u32[]{:S(2)}, u32[]{:S(2)}) collective-permute-start(bf16[512,256]{1,0:T(8,128)(2,1)S(1)} %pad_maximum_fusion.2), channel_id=1, source_target_pairs={{8,0},{16,8},{24,16},{32,24},{40,32},{48,40},{56,48},{64,56},{72,6... | collective-permute-start | bytes 786440 | tf_op jit(solution)/shard_map/ppermute | solution.py:64
  168.6 3.3 %last_sum.1 = bf16[512,1024]{1,0:T(8,128)(2,1)} custom-call(s32[24]{0:T(128)S(1)} %concatenate.16.meta_ref, bf16[2,64,256,1024]{3,2,1,0:T(8,128)(2,1)} %get-tuple-element.99.buffer_ref, bf16[512,1024]{1,0:T(8,128)(2,1)S(1)} %collective-permute-done.28.across, bf16[256,1024]{1,0:T(8,128)(2,1)S(1)} %collective-permute-done.25.nup, ...), custom_call_target="tpu_custom_call" | custom-call | flops 2097152 | bytes 5242880 | tf_op jit(solution)/shard_map/last_sum/pallas_call | solution.py:519
  171.9 1.1 collective-permute-done.27
  173.0 0.8 fusion
  (35 shorter events, 0.2 us)
Async XLA Ops:
  0.6 8.7 %copy-start.5 = (s32[8]{0:T(128)S(1)}, s32[8]{0:T(128)}, u32[]{:S(2)}) copy-start(s32[8]{0:T(128)} %constant.79.clone) | copy-start | bytes 100
  0.6 8.7 %copy-start.6 = (s32[8]{0:T(128)S(1)}, s32[8]{0:T(128)}, u32[]{:S(2)}) copy-start(s32[8]{0:T(128)} %constant.80.clone) | copy-start | bytes 100
  0.7 8.7 %copy-start.7 = (s32[8]{0:T(128)S(1)}, s32[8]{0:T(128)}, u32[]{:S(2)}) copy-start(s32[8]{0:T(128)} %constant.81.clone) | copy-start | bytes 100
  0.7 3.7 %copy-start.1 = (bf16[512,128]{1,0:T(8,128)(2,1)S(1)}, bf16[512,128]{1,0:T(8,128)(2,1)}, u32[]{:S(2)}) copy-start(bf16[512,128]{1,0:T(8,128)(2,1)} %k_ref.5) | copy-start | bytes 393220
  0.7 3.7 %copy-start = (bf16[512,128]{1,0:T(8,128)(2,1)S(1)}, bf16[512,128]{1,0:T(8,128)(2,1)}, u32[]{:S(2)}) copy-start(bf16[512,128]{1,0:T(8,128)(2,1)} %v_ref.5) | copy-start | bytes 393220
  0.7 9.8 %copy-start.2 = (bf16[512,1024]{1,0:T(8,128)(2,1)S(1)}, bf16[512,1024]{1,0:T(8,128)(2,1)}, u32[]{:S(2)}) copy-start(bf16[512,1024]{1,0:T(8,128)(2,1)} %refs_8_) | copy-start | bytes 3145732
  0.7 16.8 %copy-start.3 = (bf16[512,1024]{1,0:T(8,128)(2,1)S(1)}, bf16[512,1024]{1,0:T(8,128)(2,1)}, u32[]{:S(2)}) copy-start(bf16[512,1024]{1,0:T(8,128)(2,1)} %q_ref.4) | copy-start | bytes 3145732
  0.7 16.8 %copy-start.4 = (s32[8192]{0:T(1024)S(1)}, s32[8192]{0:T(1024)}, u32[]{:S(2)}) copy-start(s32[8192]{0:T(1024)} %param.15) | copy-start | bytes 98308
  3.0 6.5 %collective-permute-start = (bf16[512,512]{1,0:T(8,128)(2,1)}, bf16[512,512]{1,0:T(8,128)(2,1)}, u32[]{:S(2)}, u32[]{:S(2)}) collective-permute-start(bf16[512,512]{1,0:T(8,128)(2,1)} %get-tuple-element.135), channel_id=1, source_target_pairs={{0,8},{8,0},{16,24},{24,16},{32,40},{40,32},{48,56},{56,48},{64,72... | collective-permute-start | bytes 1572872 | tf_op jit(solution)/shard_map/ppermute | solution.py:50
  4.4 12.7 %collective-permute-start.6 = (bf16[512,256]{1,0:T(8,128)(2,1)S(1)}, bf16[512,256]{1,0:T(8,128)(2,1)S(1)}, u32[]{:S(2)}, u32[]{:S(2)}) collective-permute-start(bf16[512,256]{1,0:T(8,128)(2,1)S(1)} %pad_maximum_fusion.1), channel_id=1, source_target_pairs={{0,8},{8,16},{16,24},{24,32},{32,40},{40,48},{48,56},{56,64},{64,7... | collective-permute-start | bytes 786440 | tf_op jit(solution)/shard_map/ppermute | solution.py:64
  10.6 25.6 %collective-permute-start.1 = (bf16[512,1024]{1,0:T(8,128)(2,1)S(1)}, bf16[512,1024]{1,0:T(8,128)(2,1)S(1)}, u32[]{:S(2)}, u32[]{:S(2)}) collective-permute-start(bf16[512,1024]{1,0:T(8,128)(2,1)S(1)} %copy-done.2), channel_id=1, source_target_pairs={{0,32},{8,40},{16,48},{24,56},{32,64},{40,72},{48,80},{56,88},{64,... | collective-permute-start | bytes 3145736 | tf_op jit(solution)/shard_map/ppermute | solution.py:50
  12.3 23.9 %collective-permute-start.2 = (bf16[512,1024]{1,0:T(8,128)(2,1)S(1)}, bf16[512,1024]{1,0:T(8,128)(2,1)S(1)}, u32[]{:S(2)}, u32[]{:S(2)}) collective-permute-start(bf16[512,1024]{1,0:T(8,128)(2,1)S(1)} %copy-done.2), channel_id=1, source_target_pairs={{0,96},{8,104},{16,112},{24,120},{32,0},{40,8},{48,16},{56,24},{64... | collective-permute-start | bytes 3145736 | tf_op jit(solution)/shard_map/ppermute | solution.py:50
  14.5 24.5 %collective-permute-start.3 = (bf16[1024,512]{1,0:T(8,128)(2,1)S(1)}, bf16[1024,512]{1,0:T(8,128)(2,1)S(1)}, u32[]{:S(2)}, u32[]{:S(2)}) collective-permute-start(bf16[1024,512]{1,0:T(8,128)(2,1)S(1)} %pad_maximum_fusion.refs_0_), channel_id=1, source_target_pairs={{0,1},{1,2},{2,3},{3,0},{4,5},{5,6},{6,7},{7,4},{8,9},{9,10},{10,1... | collective-permute-start | bytes 3145736 | tf_op jit(solution)/shard_map/ppermute | solution.py:58
  15.7 23.9 %collective-permute-start.4 = (bf16[1024,512]{1,0:T(8,128)(2,1)S(1)}, bf16[1024,512]{1,0:T(8,128)(2,1)S(1)}, u32[]{:S(2)}, u32[]{:S(2)}) collective-permute-start(bf16[1024,512]{1,0:T(8,128)(2,1)S(1)} %pad_maximum_fusion.refs_0_), channel_id=1, source_target_pairs={{0,3},{1,0},{2,1},{3,2},{4,7},{5,4},{6,5},{7,6},{8,11},{9,8},{10,9... | collective-permute-start | bytes 3145736 | tf_op jit(solution)/shard_map/ppermute | solution.py:58
  17.2 23.9 %collective-permute-start.5 = (bf16[1024,512]{1,0:T(8,128)(2,1)S(1)}, bf16[1024,512]{1,0:T(8,128)(2,1)S(1)}, u32[]{:S(2)}, u32[]{:S(2)}) collective-permute-start(bf16[1024,512]{1,0:T(8,128)(2,1)S(1)} %pad_maximum_fusion.refs_0_), channel_id=1, source_target_pairs={{0,4},{1,5},{2,6},{3,7},{4,0},{5,1},{6,2},{7,3},{8,12},{9,13},{10,... | collective-permute-start | bytes 3145736 | tf_op jit(solution)/shard_map/ppermute | solution.py:58
  41.0 4.3 %collective-permute-start.11 = (bf16[512,1024]{1,0:T(8,128)(2,1)S(1)}, bf16[512,1024]{1,0:T(8,128)(2,1)S(1)}, u32[]{:S(2)}, u32[]{:S(2)}) collective-permute-start(bf16[512,1024]{1,0:T(8,128)(2,1)S(1)} %get-tuple-element.78), channel_id=1, source_target_pairs={{0,8},{8,0},{16,24},{24,16},{32,40},{40,32},{48,56},{56,48},{64,72... | collective-permute-start | bytes 3145736 | tf_op jit(solution)/shard_map/ppermute | solution.py:50
  41.0 25.7 %collective-permute-start.8 = (bf16[512,1024]{1,0:T(8,128)(2,1)S(1)}, bf16[512,1024]{1,0:T(8,128)(2,1)S(1)}, u32[]{:S(2)}, u32[]{:S(2)}) collective-permute-start(bf16[512,1024]{1,0:T(8,128)(2,1)S(1)} %copy-done.2), channel_id=1, source_target_pairs={{0,16},{8,24},{16,0},{24,8},{32,48},{40,56},{48,32},{56,40},{64,80... | collective-permute-start | bytes 3145736 | tf_op jit(solution)/shard_map/ppermute | solution.py:50
  43.4 24.5 %collective-permute-start.10 = (bf16[1024,512]{1,0:T(8,128)(2,1)S(1)}, bf16[1024,512]{1,0:T(8,128)(2,1)S(1)}, u32[]{:S(2)}, u32[]{:S(2)}) collective-permute-start(bf16[1024,512]{1,0:T(8,128)(2,1)S(1)} %collective-permute-done.5.refs_3_), channel_id=1, source_target_pairs={{0,3},{1,0},{2,1},{3,2},{4,7},{5,4},{6,5},{7,6},{8,11},{9,8},{10,9... | collective-permute-start | bytes 3145736 | tf_op jit(solution)/shard_map/ppermute | solution.py:58
  44.7 25.4 %collective-permute-start.7 = (bf16[512,1024]{1,0:T(8,128)(2,1)S(1)}, bf16[512,1024]{1,0:T(8,128)(2,1)S(1)}, u32[]{:S(2)}, u32[]{:S(2)}) collective-permute-start(bf16[512,1024]{1,0:T(8,128)(2,1)S(1)} %collective-permute-done.1.refs_9_), channel_id=1, source_target_pairs={{0,32},{8,40},{16,48},{24,56},{32,64},{40,72},{48,80},{56,88},{64,... | collective-permute-start | bytes 3145736 | tf_op jit(solution)/shard_map/ppermute | solution.py:50
  45.1 25.0 %collective-permute-start.9 = (bf16[1024,512]{1,0:T(8,128)(2,1)S(1)}, bf16[1024,512]{1,0:T(8,128)(2,1)S(1)}, u32[]{:S(2)}, u32[]{:S(2)}) collective-permute-start(bf16[1024,512]{1,0:T(8,128)(2,1)S(1)} %collective-permute-done.5.refs_3_), channel_id=1, source_target_pairs={{0,1},{1,2},{2,3},{3,0},{4,5},{5,6},{6,7},{7,4},{8,9},{9,10},{10,1... | collective-permute-start | bytes 3145736 | tf_op jit(solution)/shard_map/ppermute | solution.py:58
  45.4 47.2 %collective-permute-start.13 = (bf16[1024,512]{1,0:T(8,128)(2,1)S(1)}, bf16[1024,512]{1,0:T(8,128)(2,1)S(1)}, u32[]{:S(2)}, u32[]{:S(2)}) collective-permute-start(bf16[1024,512]{1,0:T(8,128)(2,1)S(1)} %collective-permute-done.3.refs_1_), channel_id=1, source_target_pairs={{0,1},{1,2},{2,3},{3,0},{4,5},{5,6},{6,7},{7,4},{8,9},{9,10},{10,1... | collective-permute-start | bytes 3145736 | tf_op jit(solution)/shard_map/ppermute | solution.py:58
  70.2 25.3 %collective-permute-start.12 = (bf16[1024,512]{1,0:T(8,128)(2,1)S(1)}, bf16[1024,512]{1,0:T(8,128)(2,1)S(1)}, u32[]{:S(2)}, u32[]{:S(2)}) collective-permute-start(bf16[1024,512]{1,0:T(8,128)(2,1)S(1)} %collective-permute-done.10.refs_1_.refs_5_), channel_id=1, source_target_pairs={{0,3},{1,0},{2,1},{3,2},{4,7},{5,4},{6,5},{7,6},{8,11},{9,8},{10,9... | collective-permute-start | bytes 3145736 | tf_op jit(solution)/shard_map/ppermute | solution.py:58
  70.6 28.8 %collective-permute-start.14 = (bf16[512,1024]{1,0:T(8,128)(2,1)S(1)}, bf16[512,1024]{1,0:T(8,128)(2,1)S(1)}, u32[]{:S(2)}, u32[]{:S(2)}) collective-permute-start(bf16[512,1024]{1,0:T(8,128)(2,1)S(1)} %collective-permute-done.8.refs_11_), channel_id=1, source_target_pairs={{0,32},{8,40},{16,48},{24,56},{32,64},{40,72},{48,80},{56,88},{64,... | collective-permute-start | bytes 3145736 | tf_op jit(solution)/shard_map/ppermute | solution.py:50
  71.5 27.9 %collective-permute-start.15 = (bf16[512,1024]{1,0:T(8,128)(2,1)S(1)}, bf16[512,1024]{1,0:T(8,128)(2,1)S(1)}, u32[]{:S(2)}, u32[]{:S(2)}) collective-permute-start(bf16[512,1024]{1,0:T(8,128)(2,1)S(1)} %collective-permute-done.8.refs_11_), channel_id=1, source_target_pairs={{0,96},{8,104},{16,112},{24,120},{32,0},{40,8},{48,16},{56,24},{64... | collective-permute-start | bytes 3145736 | tf_op jit(solution)/shard_map/ppermute | solution.py:50
  73.3 26.1 %collective-permute-start.16 = (bf16[512,1024]{1,0:T(8,128)(2,1)S(1)}, bf16[512,1024]{1,0:T(8,128)(2,1)S(1)}, u32[]{:S(2)}, u32[]{:S(2)}) collective-permute-start(bf16[512,1024]{1,0:T(8,128)(2,1)S(1)} %collective-permute-done.7.refs_15_), channel_id=1, source_target_pairs={{0,16},{8,24},{16,0},{24,8},{32,48},{40,56},{48,32},{56,40},{64,80... | collective-permute-start | bytes 3145736 | tf_op jit(solution)/shard_map/ppermute | solution.py:50
  99.4 24.5 %collective-permute-start.17 = (bf16[512,1024]{1,0:T(8,128)(2,1)S(1)}, bf16[512,1024]{1,0:T(8,128)(2,1)S(1)}, u32[]{:S(2)}, u32[]{:S(2)}) collective-permute-start(bf16[512,1024]{1,0:T(8,128)(2,1)S(1)} %get-tuple-element.89), channel_id=1, source_target_pairs={{0,16},{8,24},{16,0},{24,8},{32,48},{40,56},{48,32},{56,40},{64,80... | collective-permute-start | bytes 3145736 | tf_op jit(solution)/shard_map/ppermute | solution.py:50
  100.6 30.7 %collective-permute-start.19 = (bf16[640,1024]{1,0:T(8,128)(2,1)S(1)}, bf16[640,1024]{1,0:T(8,128)(2,1)S(1)}, u32[]{:S(2)}, u32[]{:S(2)}) collective-permute-start(bf16[640,1024]{1,0:T(8,128)(2,1)S(1)} %get-tuple-element.87), channel_id=1, source_target_pairs={{0,32},{8,40},{16,48},{24,56},{32,64},{40,72},{48,80},{56,88},{64,... | collective-permute-start | bytes 3932168 | tf_op jit(solution)/shard_map/ppermute | solution.py:50
  102.1 29.5 %collective-permute-start.20 = (bf16[640,1024]{1,0:T(8,128)(2,1)S(1)}, bf16[640,1024]{1,0:T(8,128)(2,1)S(1)}, u32[]{:S(2)}, u32[]{:S(2)}) collective-permute-start(bf16[640,1024]{1,0:T(8,128)(2,1)S(1)} %get-tuple-element.98), channel_id=1, source_target_pairs={{0,96},{8,104},{16,112},{24,120},{32,0},{40,8},{48,16},{56,24},{64... | collective-permute-start | bytes 3932168 | tf_op jit(solution)/shard_map/ppermute | solution.py:50
  123.9 12.3 %collective-permute-start.18 = (bf16[512,1024]{1,0:T(8,128)(2,1)S(1)}, bf16[512,1024]{1,0:T(8,128)(2,1)S(1)}, u32[]{:S(2)}, u32[]{:S(2)}) collective-permute-start(bf16[512,1024]{1,0:T(8,128)(2,1)S(1)} %get-tuple-element.97), channel_id=1, source_target_pairs={{0,8},{8,0},{16,24},{24,16},{32,40},{40,32},{48,56},{56,48},{64,72... | collective-permute-start | bytes 3145736 | tf_op jit(solution)/shard_map/ppermute | solution.py:50
  128.6 16.9 %collective-permute-start.21 = (bf16[256,1024]{1,0:T(8,128)(2,1)S(1)}, bf16[256,1024]{1,0:T(8,128)(2,1)S(1)}, u32[]{:S(2)}, u32[]{:S(2)}) collective-permute-start(bf16[256,1024]{1,0:T(8,128)(2,1)S(1)} %get-tuple-element.101), channel_id=1, source_target_pairs={{0,32},{8,40},{16,48},{24,56},{32,64},{40,72},{48,80},{56,88},{64,... | collective-permute-start | bytes 1572872 | tf_op jit(solution)/shard_map/ppermute | solution.py:50
  130.1 15.3 %collective-permute-start.22 = (bf16[256,1024]{1,0:T(8,128)(2,1)S(1)}, bf16[256,1024]{1,0:T(8,128)(2,1)S(1)}, u32[]{:S(2)}, u32[]{:S(2)}) collective-permute-start(bf16[256,1024]{1,0:T(8,128)(2,1)S(1)} %get-tuple-element.106), channel_id=1, source_target_pairs={{0,96},{8,104},{16,112},{24,120},{32,0},{40,8},{48,16},{56,24},{64... | collective-permute-start | bytes 1572872 | tf_op jit(solution)/shard_map/ppermute | solution.py:50
  131.3 17.8 %collective-permute-start.23 = (bf16[128,1024]{1,0:T(8,128)(2,1)S(1)}, bf16[128,1024]{1,0:T(8,128)(2,1)S(1)}, u32[]{:S(2)}, u32[]{:S(2)}) collective-permute-start(bf16[128,1024]{1,0:T(8,128)(2,1)S(1)} %get-tuple-element.115), channel_id=1, source_target_pairs={{0,32},{8,40},{16,48},{24,56},{32,64},{40,72},{48,80},{56,88},{64,... | collective-permute-start | bytes 786440 | tf_op jit(solution)/shard_map/ppermute | solution.py:50
  131.6 17.5 %collective-permute-start.24 = (bf16[128,1024]{1,0:T(8,128)(2,1)S(1)}, bf16[128,1024]{1,0:T(8,128)(2,1)S(1)}, u32[]{:S(2)}, u32[]{:S(2)}) collective-permute-start(bf16[128,1024]{1,0:T(8,128)(2,1)S(1)} %get-tuple-element.116), channel_id=1, source_target_pairs={{0,96},{8,104},{16,112},{24,120},{32,0},{40,8},{48,16},{56,24},{64... | collective-permute-start | bytes 786440 | tf_op jit(solution)/shard_map/ppermute | solution.py:50
  136.2 32.5 %collective-permute-start.28 = (bf16[512,1024]{1,0:T(8,128)(2,1)S(1)}, bf16[512,1024]{1,0:T(8,128)(2,1)S(1)}, u32[]{:S(2)}, u32[]{:S(2)}) collective-permute-start(bf16[512,1024]{1,0:T(8,128)(2,1)S(1)} %add_blocks.5), channel_id=1, source_target_pairs={{0,16},{8,24},{16,0},{24,8},{32,48},{40,56},{48,32},{56,40},{64,80... | collective-permute-start | bytes 3145736 | tf_op jit(solution)/shard_map/ppermute | solution.py:50
  147.8 15.2 %collective-permute-start.25 = (bf16[256,1024]{1,0:T(8,128)(2,1)S(1)}, bf16[256,1024]{1,0:T(8,128)(2,1)S(1)}, u32[]{:S(2)}, u32[]{:S(2)}) collective-permute-start(bf16[256,1024]{1,0:T(8,128)(2,1)S(1)} %get-tuple-element.119), channel_id=1, source_target_pairs={{0,32},{8,40},{16,48},{24,56},{32,64},{40,72},{48,80},{56,88},{64,... | collective-permute-start | bytes 1572872 | tf_op jit(solution)/shard_map/ppermute | solution.py:50
  149.2 13.9 %collective-permute-start.26 = (bf16[256,1024]{1,0:T(8,128)(2,1)S(1)}, bf16[256,1024]{1,0:T(8,128)(2,1)S(1)}, u32[]{:S(2)}, u32[]{:S(2)}) collective-permute-start(bf16[256,1024]{1,0:T(8,128)(2,1)S(1)} %get-tuple-element.126), channel_id=1, source_target_pairs={{0,96},{8,104},{16,112},{24,120},{32,0},{40,8},{48,16},{56,24},{64... | collective-permute-start | bytes 1572872 | tf_op jit(solution)/shard_map/ppermute | solution.py:50
  163.2 9.9 %collective-permute-start.27 = (bf16[512,256]{1,0:T(8,128)(2,1)S(1)}, bf16[512,256]{1,0:T(8,128)(2,1)S(1)}, u32[]{:S(2)}, u32[]{:S(2)}) collective-permute-start(bf16[512,256]{1,0:T(8,128)(2,1)S(1)} %pad_maximum_fusion.2), channel_id=1, source_target_pairs={{8,0},{16,8},{24,16},{32,24},{40,32},{48,40},{56,48},{64,56},{72,6... | collective-permute-start | bytes 786440 | tf_op jit(solution)/shard_map/ppermute | solution.py:64

commit v8 on v7

--- a/solution.py
+++ b/solution.py
@@ -243,9 +243,9 @@
         input_output_aliases={11: 0} if earlier else {},
         compiler_params=params(22),
         cost_estimate=pl.CostEstimate(
-            flops=(end - begin) * 10 * 2 * 2 * count * count * HD,
-            bytes_accessed=6 * 2**20,
-            transcendentals=(end - begin) * 2 * count * count,
+            flops=(end - begin) * 10 * 2 * 2 * count * count * HD if begin else 2**20,
+            bytes_accessed=6 * 2**20 if begin else 2**16,
+            transcendentals=(end - begin) * 2 * count * count if begin else 0,
         ),
         name="attend_back",
     )(meta, query, grad, kv_earlier, key_rows, value_rows, segments, top, total, *earlier)
@@ -350,8 +350,8 @@
 
 def grad_kernel(wplan, n_g, n_w, meta_ref, *refs):
     g_in, w_in = refs[:n_g], refs[n_g:n_g + n_w]
-    own_ref, other_ref = refs[n_g + n_w:n_g + n_w + 2]
-    gbuf, wbuf, total, gsems, wsems = refs[n_g + n_w + 2:]
+    own_ref, lo_ref, hi_ref = refs[n_g + n_w:n_g + n_w + 3]
+    gbuf, wbuf, total, gsems, wsems = refs[n_g + n_w + 3:]
     step = pl.program_id(0)
     half = own_ref.shape[0]
     wh = wbuf.shape[1] // 2
@@ -406,7 +406,8 @@
     @pl.when(step == 7)
     def _():
         own_ref[...] = total[:half, :]
-        other_ref[...] = total[half:, :].astype(BF)
+        lo_ref[...] = total[half:half + half // 2, :].astype(BF)
+        hi_ref[...] = total[half + half // 2:, :].astype(BF)
 
 
 def attn_grad_part(g_pieces, w_pieces, wplan, meta):
@@ -421,7 +422,7 @@
             num_scalar_prefetch=1,
             grid=(8,),
             in_specs=[pl.BlockSpec(memory_space=pltpu.HBM)] * (len(g_pieces) + len(w_pieces)),
-            out_specs=[whole, whole],
+            out_specs=[whole] * 3,
             scratch_shapes=[
                 pltpu.VMEM((3, tokens, depth), BF),
                 pltpu.VMEM((8, depth, width), BF),
@@ -432,7 +433,8 @@
         ),
         out_shape=[
             jax.ShapeDtypeStruct((half, width), F32),
-            jax.ShapeDtypeStruct((half, width), BF),
+            jax.ShapeDtypeStruct((half // 2, width), BF),
+            jax.ShapeDtypeStruct((half // 2, width), BF),
         ],
         compiler_params=params(26),
         cost_estimate=pl.CostEstimate(
@@ -444,94 +446,69 @@
     )(meta, *g_pieces, *w_pieces)
 
 
-def add_kernel(places, n_terms, plan, joined, meta_ref, buffer_ref, *refs):
-    terms, outs = refs[:n_terms], refs[n_terms:-2]
-    blocks, sems = refs[-2:]
-    rows = blocks.shape[2]
-    copies = [
-        pltpu.make_async_copy(buffer_ref.at[:, meta_ref[places[n]]], blocks.at[n], sems.at[n])
-        for n in range(blocks.shape[0])
-    ]
+def fetch_kernel(plan, meta_ref, buffer_ref, *refs):
+    outs, sems = refs[:-1], refs[-1]
+    copies = []
+    for n, (out, start, at, half) in enumerate(plan):
+        source = buffer_ref.at[half, meta_ref[at]]
+        target = outs[out].at[pl.ds(start, source.shape[0])]
+        copies.append(pltpu.make_async_copy(source, target, sems.at[n]))
     for copy in copies:
         copy.start()
     for copy in copies:
         copy.wait()
-    for n, (block, half, extra) in enumerate(plan):
-        value = blocks[block, half].astype(F32)
-        for term, first in extra:
-            value = value + terms[term][first:first + rows, :].astype(F32)
-        if joined:
-            outs[0][n * rows:(n + 1) * rows, :] = value.astype(BF)
-        else:
-            outs[n][...] = value.astype(BF)
-
-
-def add_blocks(buffer, meta, places, terms, plan, joined=False):
+
+
+def fetch(buffer, meta, plan):
     _, _, rows, width = buffer.shape
+    n_out = 1 + plan[-1][0]
     here = pl.BlockSpec(memory_space=pltpu.VMEM)
-    shapes = [(len(plan) * rows, width)] if joined else [(rows, width)] * len(plan)
     return pl.pallas_call(
-        functools.partial(add_kernel, tuple(places), len(terms), plan, joined),
+        functools.partial(fetch_kernel, plan),
         grid_spec=pltpu.PrefetchScalarGridSpec(
             num_scalar_prefetch=1,
             grid=(1,),
-            in_specs=[pl.BlockSpec(memory_space=pltpu.HBM)] + [here] * len(terms),
-            out_specs=[here] * len(shapes),
-            scratch_shapes=[
-                pltpu.VMEM((len(places), 2, rows, width), BF),
-                pltpu.SemaphoreType.DMA((len(places),)),
-            ],
-        ),
+            in_specs=[pl.BlockSpec(memory_space=pltpu.HBM)],
+            out_specs=[here] * n_out,
+            scratch_shapes=[pltpu.SemaphoreType.DMA((len(plan),))],
+        ),
+        out_shape=[jax.ShapeDtypeStruct((2 * rows, width), BF)] * n_out,
+        compiler_params=params(8),
+        cost_estimate=pl.CostEstimate(
+            flops=0, bytes_accessed=2**16, transcendentals=0
+        ),
+        name="fetch",
+    )(meta, buffer)
+
+
+def add_kernel(n_terms, plan, *refs):
+    terms, outs = refs[:n_terms], refs[n_terms:]
+    for out, start, rows, parts in plan:
+        value = None
+        for term, first in parts:
+            part = terms[term][first:first + rows, :].astype(F32)
+            value = part if value is None else value + part
+        outs[out][start:start + rows, :] = value.astype(BF)
+
+
+def add_rows(terms, plan, result=False):
+    width = terms[0].shape[1]
+    n_out = 1 + plan[-1][0]
+    shapes = [(sum(p[2] for p in plan if p[0] == n), width) for n in range(n_out)]
+    here = pl.BlockSpec(memory_space=pltpu.VMEM)
+    outs = [pl.BlockSpec(shape, lambda i: (0, 0)) if result else here for shape in shapes]
+    return pl.pallas_call(
+        functools.partial(add_kernel, len(terms), plan),
+        grid=(1,),
+        in_specs=[here] * len(terms),
+        out_specs=outs,
         out_shape=[jax.ShapeDtypeStruct(shape, BF) for shape in shapes],
         compiler_params=params(12),
         cost_estimate=pl.CostEstimate(
             flops=2**21, bytes_accessed=5 * 2**20, transcendentals=0
         ),
-        name="add_blocks",
-    )(meta, buffer, *terms)
-
-
-def last_kernel(meta_ref, buffer_ref, across, nup, ndn, rup, up2, rdn, dn2, out_ref, block, sem):
-    copy = pltpu.make_async_copy(buffer_ref.at[:, meta_ref[at_w(0, 0)]], block, sem)
-    copy.start()
-    copy.wait()
-    half, quarter = nup.shape[0], up2.shape[0]
-    for part in range(2):
-        for n in range(2):
-            rows = slice(n * quarter, (n + 1) * quarter)
-            place = slice(part * half + n * quarter, part * half + (n + 1) * quarter)
-            up, dn = nup[rows, :], ndn[rows, :]
-            if part == 1:
-                up = up2[...] if n else rup[2 * half:, :]
-            else:
-                dn = dn2[...] if n else rdn[2 * half:, :]
-            out_ref[place, :] = (
-                block[part, rows].astype(F32)
-                + across[place, :].astype(F32)
-                + up.astype(F32)
-                + dn.astype(F32)
-            ).astype(BF)
-
-
-def last_sum(buffer, meta, *terms):
-    _, _, rows, width = buffer.shape
-    here = pl.BlockSpec(memory_space=pltpu.VMEM)
-    return pl.pallas_call(
-        last_kernel,
-        grid_spec=pltpu.PrefetchScalarGridSpec(
-            num_scalar_prefetch=1,
-            grid=(1,),
-            in_specs=[pl.BlockSpec(memory_space=pltpu.HBM)] + [here] * len(terms),
-            out_specs=pl.BlockSpec((2 * rows, width), lambda i, m: (0, 0)),
-            scratch_shapes=[pltpu.VMEM((2, rows, width), BF), pltpu.SemaphoreType.DMA],
-        ),
-        out_shape=jax.ShapeDtypeStruct((2 * rows, width), BF),
-        compiler_params=params(12),
-        cost_estimate=pl.CostEstimate(
-            flops=2**21, bytes_accessed=5 * 2**20, transcendentals=0
-        ),
-        name="last_sum",
-    )(meta, buffer, *terms)
+        name="add_rows",
+    )(*terms)
 
 
 def local(query_rows, key_rows, value_rows, output_grad, out_proj, segment_ids):
@@ -558,7 +535,8 @@
     (query_held,) = tied((query_rows,), g0)
     attn_out, top, total = attend(meta, query_held, kv_earlier, key_rows, value_rows, segments)
 
-    wzm, wzp, gxm, gxp, gy, attn_out = tied((wzm, wzp, gxm, gxp, gy, attn_out))
+    gxm, gxp, gy, attn_out = tied((gxm, gxp, gy, attn_out))
+    wzm, wzp, out_proj = tied((wzm, wzp, out_proj), gxm)
 
     hw = out_proj.shape[0] // 2
     gyxm = move_col(gy, dx=1)
@@ -571,8 +549,9 @@
     proj = project([g0, gxm, gxp, gy], a_pair, meta, range(4), None)
 
     go = move_col(gxm, dx=1)
-    wo, wy, gyxm, gyxp, proj = tied((wo, wy, gyxm, gyxp, proj))
+    gyxm, gyxp, proj = tied((gyxm, gyxp, proj))
     gyo = move_col(gyxp, dx=-1)
+    wo, wy = tied((wo, wy), gyxp)
     wyzm = move_row(wy, dz=1)
     wyzp = move_row(wy, dz=-1)
     wyo = move_row(wo, dyh=1)
@@ -608,61 +587,70 @@
     w_pieces = [out_proj, wzm, wzp, wy, wyzm, wyzp, wyo, wo]
     wplan = [(i, p * hw, i, p) for i in range(8) for p in range(2)]
     (meta,) = tied((meta,), give_up)
-    grad_own, grad_give = attn_grad_part(g_pieces, w_pieces, wplan, meta)
-
-    ry, grad_own, grad_give = tied((ry, grad_own, grad_give))
-
-    far_up, far_dn = add_blocks(
-        proj, meta, [at_w(2, 0)], [ry], ((0, 0, ((0, 0),)), (0, 1, ((0, hw),)))
+    grad_own, give_lo, give_hi = attn_grad_part(g_pieces, w_pieces, wplan, meta)
+    got_lo, got_hi = move_row(give_lo, dk=1), move_row(give_hi, dk=1)
+    far, middle, near, own = fetch(
+        proj,
+        meta,
+        (
+            (0, 0, at_w(2, 0), 0), (0, hw, at_w(2, 0), 1),
+            (1, 0, at_w(0, 1), 0), (1, hw, at_w(0, 1), 1),
+            (2, 0, own_up, 0), (2, hw, own_dn, 1),
+            (3, 0, at_w(0, 0), 0), (3, hw, at_w(0, 0), 1),
+        ),
+    )
+    (attn_grad,) = add_rows(
+        [grad_own, got_lo, got_hi],
+        ((0, 0, hw, ((0, 0), (1, 0))), (0, hw, hw, ((0, hw), (2, 0)))),
+    )
+    part = functools.partial(
+        attend_back, meta, query_rows, attn_grad, kv_earlier, key_rows, value_rows, segments, top, total
+    )
+    heads = query_rows.shape[1] // HD
+    cuts = heads // 4, 5 * heads // 8
+    held = part((0, cuts[0]), None)
+
+    ry, *held = tied((ry, *held))
+
+    far_up, far_dn = add_rows(
+        [far, ry], ((0, 0, hw, ((0, 0), (1, 0))), (1, 0, hw, ((0, hw), (1, hw))))
     )
     fup = move_row(far_up, dz=1)
     fdn = move_row(far_dn, dz=-1)
-    grad_got = move_row(grad_give, dk=1)
-    rup, rdn = tied((rup, rdn), far_up)
-    (across,) = add_blocks(
-        proj,
-        meta,
-        [at_w(0, 1)],
-        [rup, rdn],
-        ((0, 0, ((0, 0), (1, 0))), (0, 1, ((0, hw), (1, hw)))),
-        joined=True,
-    )
+    rup, rdn, up2, dn2 = tied((rup, rdn, up2, dn2), far_up)
+    (across,) = add_rows([middle, rup, rdn], ((0, 0, 2 * hw, ((0, 0), (1, 0), (2, 0))),))
+    held = tied(held, across)
     across = move_row(across, dyh=1)
-    up2, dn2 = tied((up2, dn2), far_up)
     up2 = move_row(up2, dz=1)
     dn2 = move_row(dn2, dz=-1)
-
-    attn_grad = (grad_own + grad_got.astype(F32)).astype(BF)
-    (attn_grad,) = tied((attn_grad,), rup)
-    part = functools.partial(
-        attend_back, meta, query_rows, attn_grad, kv_earlier, key_rows, value_rows, segments, top, total
-    )
-    heads = query_rows.shape[1] // HD
-    cut = 3 * heads // 8
-    held = part((0, cut), None)
+    held = part(cuts, held)
 
     fup, fdn, *held = tied((fup, fdn, *held))
 
-    near_up, near_dn = add_blocks(
-        proj,
-        meta,
-        [own_up, own_dn],
-        [fup, fdn],
-        ((0, 0, ((0, 0),)), (1, 1, ((1, 0),))),
+    near_up, near_dn = add_rows(
+        [near, fup, fdn], ((0, 0, hw, ((0, 0), (1, 0))), (1, 0, hw, ((0, hw), (2, 0))))
     )
     nup = move_row(near_up, dz=1)
     ndn = move_row(near_dn, dz=-1)
 
     *held, up2, dn2 = tied((*held, up2, dn2), near_up)
-    query_grad, dkey, dvalue = part((cut, heads), held)
-    dkey, dvalue, nup, ndn = tied((dkey, dvalue, nup, ndn))
+    query_grad, dkey, dvalue = part((cuts[1], heads), held)
     back = passed_along(
         jnp.concatenate([dkey[:count], dvalue[:count]], 1).astype(BF), "row", -1
     ).astype(F32)
     key_grad = (dkey[count:] + back[:, :HD]).astype(BF)
     value_grad = (dvalue[count:] + back[:, HD:]).astype(BF)
 
-    proj_grad = last_sum(proj, meta, across, nup, ndn, rup, up2, rdn, dn2)
+    (proj_grad,) = add_rows(
+        [own, across, nup, ndn, rup, up2, rdn, dn2],
+        (
+            (0, 0, q, ((0, 0), (1, 0), (2, 0), (6, 2 * hw))),
+            (0, q, q, ((0, q), (1, q), (2, q), (7, 0))),
+            (0, 2 * q, q, ((0, 2 * q), (1, 2 * q), (4, 2 * hw), (3, 0))),
+            (0, 3 * q, q, ((0, 3 * q), (1, 3 * q), (5, 0), (3, q))),
+        ),
+        result=True,
+    )
     return (query_grad, key_grad, value_grad, proj_grad)
 
 

time: 174 us -> 183 us (1.052)
  starting transfers between devices: 42.9 us -> 53 us
  waiting for transfers between devices: 51.1 us -> 54.3 us
  Pallas kernels: 74 us -> 71 us
    ppermute x20 -> x21, waiting for transfers between devices: 29.6 us -> 2.61 us  [move_row(): return lax.ppermute(value, 'row', pairs)]
    ppermute x2, waiting for transfers between devices: 1.1 us -> 25 us  [passed_along(): lax.ppermute(value, axis, [(source, source + steps) for source in range(f...]
    ppermute x20 -> x21, starting transfers between devices: 27.5 us -> 34.2 us  [move_row(): return lax.ppermute(value, 'row', pairs)]
    ppermute x7, waiting for transfers between devices: 20.3 us -> 26.8 us  [move_col(): return lax.ppermute(value, 'col', pairs)]
    pallas_call x4 -> x6, Pallas kernels: 9.76 us -> 5.27 us  [the longest x1 2.76 us: fetch(): pl.pallas_call(functools.partial(fetch_kernel, plan), grid_spec=pltpu.Pre...]
    ppermute x7, starting transfers between devices: 5.06 us -> 9.25 us  [move_col(): return lax.ppermute(value, 'col', pairs)]
    pallas_call x2 -> x3, Pallas kernels: 19.1 us -> 20.6 us  [attend_back(): pl.pallas_call(functools.partial(bwd_kernel, len(earlier), last), grid_sp...]
  transfers between devices with their start and end apart: 29 -> 30, of which waited for: 12 -> 6; matrix products, arithmetic and copies ran while one was open for 1% -> 1% of each run, Pallas kernels for 43% -> 38%
where the time goes in v8:
time: 183 us
  Pallas kernels  71 us (39%)
  waiting for transfers between devices  54.3 us (30%)
  starting transfers between devices  53 us (29%)
  other arithmetic  1.97 us (1%)
    ppermute x21, starting transfers between devices, move_row(): return lax.ppermute(value, 'row', pairs)  34.2 us
    ppermute x7, waiting for transfers between devices, move_col(): return lax.ppermute(value, 'col', pairs)  26.8 us
    ppermute x2, waiting for transfers between devices, passed_along(): lax.ppermute(value, axis, [(source, source + steps) for source in range(f...  25 us
    pallas_call x3, Pallas kernels, attend_back(): pl.pallas_call(functools.partial(bwd_kernel, len(earlier), last), grid_sp...  20.6 us
    pallas_call x4, Pallas kernels, project(): pl.pallas_call(functools.partial(proj_kernel, tuple(slots), held, plan),...  17.7 us
    pallas_call x1, Pallas kernels, attend(): pl.pallas_call(fwd_kernel, grid_spec=pltpu.PrefetchScalarGridSpec(num_sca...  14.9 us
    pallas_call x1, Pallas kernels, attn_grad_part(): pl.pallas_call(kernel, grid_spec=pltpu.PrefetchScalarGridSpec(num_scalar_...  12.6 us
    ppermute x2, starting transfers between devices, passed_along(): lax.ppermute(value, axis, [(source, source + steps) for source in range(f...  9.59 us
  transfers between devices with their start and end apart: 30, of which 6 were waited for; matrix products, arithmetic and copies ran while one was open for 1% of the time, Pallas kernels for 38%

profile of v8, /device:TPU:1, one launch (start us, length us, event | category | flops | bytes accessed | tf_op | source)
XLA Modules:
  0.0 183.1 jit_solution(13965375252640812517)
XLA Ops:
  0.6 0.0 copy-start.5
  0.6 0.0 copy-start.6
  0.7 0.0 copy-start.7
  0.7 1.4 constant_dynamic-slice_fusion
  2.2 1.5 collective-permute-start
  3.7 0.1 concatenate.16.meta_ref
  3.8 1.6 collective-permute-done
  5.3 1.1 pad_maximum_fusion.refs_0_
  6.5 1.4 collective-permute-start.1
  7.8 1.4 collective-permute-start.2
  9.2 1.4 collective-permute-start.3
  10.6 5.6 %collective-permute-start.4 = (bf16[512,256]{1,0:T(8,128)(2,1)S(1)}, bf16[512,256]{1,0:T(8,128)(2,1)S(1)}, u32[]{:S(2)}, u32[]{:S(2)}) collective-permute-start(bf16[512,256]{1,0:T(8,128)(2,1)S(1)} %pad_maximum_fusion.1), channel_id=1, source_target_pairs={{0,8},{8,16},{16,24},{24,32},{32,40},{40,48},{48,56},{56,64},{64,7... | collective-permute-start | bytes 786440 | tf_op jit(solution)/shard_map/ppermute | solution.py:64
  16.3 1.7 collective-permute-start.10
  18.0 18.4 %collective-permute-done.4.kv_ref = bf16[512,256]{1,0:T(8,128)(2,1)S(1)} collective-permute-done((bf16[512,256]{1,0:T(8,128)(2,1)S(1)}, bf16[512,256]{1,0:T(8,128)(2,1)S(1)}, u32[]{:S(2)}, u32[]{:S(2)}) %collective-permute-start.4) | collective-permute-done | bytes 262176 | tf_op jit(solution)/shard_map/ppermute | solution.py:64
  36.4 3.8 %collective-permute-start.11 = (bf16[512,1024]{1,0:T(8,128)(2,1)S(1)}, bf16[512,1024]{1,0:T(8,128)(2,1)S(1)}, u32[]{:S(2)}, u32[]{:S(2)}) collective-permute-start(bf16[512,1024]{1,0:T(8,128)(2,1)S(1)} %copy-done.4), channel_id=1, source_target_pairs={{0,96},{8,104},{16,112},{24,120},{32,0},{40,8},{48,16},{56,24},{64... | collective-permute-start | bytes 3145736 | tf_op jit(solution)/shard_map/ppermute | solution.py:50
  40.1 14.9 %attend.1 = (bf16[512,1024]{1,0:T(8,128)(2,1)S(1)}, f32[8,1,512]{2,1,0:T(1,128)S(1)}, f32[8,1,512]{2,1,0:T(1,128)S(1)}) custom-call(s32[24]{0:T(128)S(1)} %concatenate.16.meta_ref, bf16[512,1024]{1,0:T(8,128)(2,1)S(1)} %copy-done, bf16[512,256]{1,0:T(8,128)(2,1)S(1)} %collective-permute-done.4.kv_ref, bf16[512,128]{1,0:T(8,128)(2,1)S(1)} %copy-done.2, ...), custom_call_target="tpu_custom_call" | custom-call | flops 4294967296 | bytes 8388608 | tf_op jit(solution)/shard_map/attend/pallas_call | solution.py:148
  55.0 0.0 collective-permute-done.1.refs_1_
  55.1 4.1 %collective-permute-start.7 = (bf16[512,1024]{1,0:T(8,128)(2,1)S(1)}, bf16[512,1024]{1,0:T(8,128)(2,1)S(1)}, u32[]{:S(2)}, u32[]{:S(2)}) collective-permute-start(bf16[512,1024]{1,0:T(8,128)(2,1)S(1)} %get-tuple-element.84), channel_id=1, source_target_pairs={{0,8},{8,0},{16,24},{24,16},{32,40},{40,32},{48,56},{56,48},{64,72... | collective-permute-start | bytes 3145736 | tf_op jit(solution)/shard_map/ppermute | solution.py:50
  59.1 0.0 collective-permute-start.5
  59.1 2.7 %collective-permute-start.6 = (bf16[1024,512]{1,0:T(8,128)(2,1)S(1)}, bf16[1024,512]{1,0:T(8,128)(2,1)S(1)}, u32[]{:S(2)}, u32[]{:S(2)}) collective-permute-start(bf16[1024,512]{1,0:T(8,128)(2,1)S(1)} %collective-permute-done.3.refs_3_), channel_id=1, source_target_pairs={{0,3},{1,0},{2,1},{3,2},{4,7},{5,4},{6,5},{7,6},{8,11},{9,8},{10,9... | collective-permute-start | bytes 3145736 | tf_op jit(solution)/shard_map/ppermute | solution.py:58
  61.8 0.0 collective-permute-done.10.refs_9_
  61.8 2.3 %collective-permute-start.13 = (bf16[512,1024]{1,0:T(8,128)(2,1)S(1)}, bf16[512,1024]{1,0:T(8,128)(2,1)S(1)}, u32[]{:S(2)}, u32[]{:S(2)}) collective-permute-start(bf16[512,1024]{1,0:T(8,128)(2,1)S(1)} %copy-done.4), channel_id=1, source_target_pairs={{0,16},{8,24},{16,0},{24,8},{32,48},{40,56},{48,32},{56,40},{64,80... | collective-permute-start | bytes 3145736 | tf_op jit(solution)/shard_map/ppermute | solution.py:50
  64.2 0.1 constant_dynamic-update-slice_fusion.1
  64.2 0.0 collective-permute-done.7
  64.2 0.1 collective-permute-start.9
  64.3 0.1 constant_dynamic-update-slice_fusion.refs_4_.refs_2_.refs_1_
  64.4 6.7 %project.4.refs_3_ = bf16[2,64,256,1024]{3,2,1,0:T(8,128)(2,1)} custom-call(s32[24]{0:T(128)S(1)} %concatenate.16.meta_ref, bf16[1024,512]{1,0:T(8,128)(2,1)S(1)} %pad_maximum_fusion.refs_0_, bf16[1024,512]{1,0:T(8,128)(2,1)S(1)} %collective-permute-done.1.refs_1_, bf16[1024,512]{1,0:T(8,128)(2,1)S(1)} %collective-permute-done.2.refs_2_, ...), custom_call_target="tpu_custom_call" | custom-call | flops 4294967296 | bytes 10485760 | tf_op jit(solution)/shard_map/project/pallas_call | solution.py:324
  71.1 13.9 %collective-permute-done.5.refs_0_.refs_4_ = bf16[1024,512]{1,0:T(8,128)(2,1)S(1)} collective-permute-done((bf16[1024,512]{1,0:T(8,128)(2,1)S(1)}, bf16[1024,512]{1,0:T(8,128)(2,1)S(1)}, u32[]{:S(2)}, u32[]{:S(2)}) %collective-permute-start.5) | collective-permute-done | bytes 1048608 | tf_op jit(solution)/shard_map/ppermute | solution.py:58
  85.1 0.0 collective-permute-done.6.refs_1_.refs_5_
  85.1 2.4 %collective-permute-start.8 = (bf16[1024,512]{1,0:T(8,128)(2,1)S(1)}, bf16[1024,512]{1,0:T(8,128)(2,1)S(1)}, u32[]{:S(2)}, u32[]{:S(2)}) collective-permute-start(bf16[1024,512]{1,0:T(8,128)(2,1)S(1)} %collective-permute-done.6.refs_1_.refs_5_), channel_id=1, source_target_pairs={{0,3},{1,0},{2,1},{3,2},{4,7},{5,4},{6,5},{7,6},{8,11},{9,8},{10,9... | collective-permute-start | bytes 3145736 | tf_op jit(solution)/shard_map/ppermute | solution.py:58
  87.4 0.0 collective-permute-done.12.refs_15_
  87.4 0.0 collective-permute-done.13.refs_11_
  87.4 0.0 collective-permute-start.14
  87.4 2.7 %collective-permute-start.15 = (bf16[512,1024]{1,0:T(8,128)(2,1)S(1)}, bf16[512,1024]{1,0:T(8,128)(2,1)S(1)}, u32[]{:S(2)}, u32[]{:S(2)}) collective-permute-start(bf16[512,1024]{1,0:T(8,128)(2,1)S(1)} %collective-permute-done.13.refs_11_), channel_id=1, source_target_pairs={{0,96},{8,104},{16,112},{24,120},{32,0},{40,8},{48,16},{56,24},{64... | collective-permute-start | bytes 3145736 | tf_op jit(solution)/shard_map/ppermute | solution.py:50
  90.1 0.4 collective-permute-start.16
  90.5 4.2 %project.5.refs_2_ = bf16[2,64,256,1024]{3,2,1,0:T(8,128)(2,1)} custom-call(s32[24]{0:T(128)S(1)} %concatenate.16.meta_ref, bf16[1024,512]{1,0:T(8,128)(2,1)S(1)} %collective-permute-done.5.refs_0_.refs_4_, bf16[1024,512]{1,0:T(8,128)(2,1)S(1)} %collective-permute-done.6.refs_1_.refs_5_, ...), custom_call_target="tpu_custom_call", output_to_operand_aliasing={{}: (4, {})} | custom-call | flops 2147483648 | bytes 6291456 | tf_op jit(solution)/shard_map/project/pallas_call | solution.py:324
  94.7 12.8 %collective-permute-done.9.refs_0_.refs_6_ = bf16[1024,512]{1,0:T(8,128)(2,1)S(1)} collective-permute-done((bf16[1024,512]{1,0:T(8,128)(2,1)S(1)}, bf16[1024,512]{1,0:T(8,128)(2,1)S(1)}, u32[]{:S(2)}, u32[]{:S(2)}) %collective-permute-start.9) | collective-permute-done | bytes 1048608 | tf_op jit(solution)/shard_map/ppermute | solution.py:58
  107.5 2.8 %project.6.refs_2_ = bf16[2,64,256,1024]{3,2,1,0:T(8,128)(2,1)} custom-call(s32[24]{0:T(128)S(1)} %concatenate.16.meta_ref, bf16[1024,512]{1,0:T(8,128)(2,1)S(1)} %collective-permute-done.9.refs_0_.refs_6_, bf16[1024,1024]{1,0:T(8,128)(2,1)S(1)} %constant_dynamic-update-slice_fusion.refs_4_.refs_2_.refs_1_, ...), custom_call_target="tpu_custom_call", output_to_operand_aliasing={{}: (3, {})} | custom-call | flops 1073741824 | bytes 4194304 | tf_op jit(solution)/shard_map/project/pallas_call | solution.py:324
  110.4 3.9 %project.7 = (bf16[2,64,256,1024]{3,2,1,0:T(8,128)(2,1)}, bf16[512,1024]{1,0:T(8,128)(2,1)S(1)}, bf16[640,1024]{1,0:T(8,128)(2,1)S(1)}, bf16[640,1024]{1,0:T(8,1...) custom-call(s32[24]{0:T(128)S(1)} %concatenate.16.meta_ref, ...), custom_call_target="tpu_custom_call", output_to_operand_aliasing={{0}: (3, {})} | custom-call | flops 1073741824 | bytes 4194304 | tf_op jit(solution)/shard_map/project/pallas_call | solution.py:324
  114.3 0.1 collective-permute-start.22
  114.4 0.3 collective-permute-start.19
  114.7 2.6 %collective-permute-start.23 = (bf16[640,1024]{1,0:T(8,128)(2,1)S(1)}, bf16[640,1024]{1,0:T(8,128)(2,1)S(1)}, u32[]{:S(2)}, u32[]{:S(2)}) collective-permute-start(bf16[640,1024]{1,0:T(8,128)(2,1)S(1)} %get-tuple-element.120), channel_id=1, source_target_pairs={{0,96},{8,104},{16,112},{24,120},{32,0},{40,8},{48,16},{56,24},{64... | collective-permute-start | bytes 3932168 | tf_op jit(solution)/shard_map/ppermute | solution.py:50
  117.3 12.6 %attn_grad.1 = (f32[512,1024]{1,0:T(8,128)S(1)}, bf16[256,1024]{1,0:T(8,128)(2,1)S(1)}, bf16[256,1024]{1,0:T(8,128)(2,1)S(1)}) custom-call(s32[24]{0:T(128)S(1)} %concatenate.16.meta_ref, bf16[1024,512]{1,0:T(8,128)(2,1)S(1)} %pad_maximum_fusion.refs_0_, bf16[1024,512]{1,0:T(8,128)(2,1)S(1)} %collective-permute-done.1.refs_1_, ...), custom_call_target="tpu_custom_call" | custom-call | flops 8589934592 | bytes 20971520 | tf_op jit(solution)/shard_map/attn_grad/pallas_call | solution.py:419
  129.9 3.9 %collective-permute-start.17 = (bf16[256,1024]{1,0:T(8,128)(2,1)S(1)}, bf16[256,1024]{1,0:T(8,128)(2,1)S(1)}, u32[]{:S(2)}, u32[]{:S(2)}) collective-permute-start(bf16[256,1024]{1,0:T(8,128)(2,1)S(1)} %get-tuple-element.103), channel_id=1, source_target_pairs={{0,8},{8,0},{16,24},{24,16},{32,40},{40,32},{48,56},{56,48},{64,72... | collective-permute-start | bytes 1572872 | tf_op jit(solution)/shard_map/ppermute | solution.py:50
  133.8 0.1 collective-permute-start.18
  133.9 2.8 %fetch.1 = (bf16[512,1024]{1,0:T(8,128)(2,1)S(1)}, bf16[512,1024]{1,0:T(8,128)(2,1)S(1)}, bf16[512,1024]{1,0:T(8,128)(2,1)S(1)}, bf16[512,1024]{1,0:T(8,128)(2,1)S(1)}) custom-call(s32[24]{0:T(128)S(1)} %concatenate.16.meta_ref, bf16[2,64,256,1024]{3,2,1,0:T(8,128)(2,1)} %get-tuple-element.107.buffer_ref), custom_call_target="tpu_custom_call" | custom-call | bytes 65536 | tf_op jit(solution)/shard_map/fetch/pallas_call | solution.py:466
  136.7 0.2 add_rows.5.g_ref
  136.8 5.5 %attend_back.3 = (bf16[512,1024]{1,0:T(8,128)(2,1)}, f32[1024,128]{1,0:T(8,128)S(1)}, f32[1024,128]{1,0:T(8,128)S(1)}) custom-call(s32[24]{0:T(128)S(1)} %concatenate.16.meta_ref, bf16[512,1024]{1,0:T(8,128)(2,1)S(1)} %copy-done, bf16[512,1024]{1,0:T(8,128)(2,1)S(1)} %add_rows.5.g_ref, bf16[512,256]{1,0:T(8,128)(2,1)S(1)} %collective-permute-done.4.kv_ref, ...), custom_call_target="tpu_custom_call" | custom-call | flops 1048576 | bytes 65536 | tf_op jit(solution)/shard_map/attend_back/pallas_call | solution.py:226
  142.4 0.2 add_rows.6
  142.6 0.1 collective-permute-start.20
  142.7 2.7 %collective-permute-start.21 = (bf16[256,1024]{1,0:T(8,128)(2,1)S(1)}, bf16[256,1024]{1,0:T(8,128)(2,1)S(1)}, u32[]{:S(2)}, u32[]{:S(2)}) collective-permute-start(bf16[256,1024]{1,0:T(8,128)(2,1)S(1)} %get-tuple-element.115), channel_id=1, source_target_pairs={{0,96},{8,104},{16,112},{24,120},{32,0},{40,8},{48,16},{56,24},{64... | collective-permute-start | bytes 1572872 | tf_op jit(solution)/shard_map/ppermute | solution.py:50
  145.4 0.4 add_rows.7
  145.8 2.6 %collective-permute-start.27 = (bf16[512,1024]{1,0:T(8,128)(2,1)S(1)}, bf16[512,1024]{1,0:T(8,128)(2,1)S(1)}, u32[]{:S(2)}, u32[]{:S(2)}) collective-permute-start(bf16[512,1024]{1,0:T(8,128)(2,1)S(1)} %add_rows.7), channel_id=1, source_target_pairs={{0,16},{8,24},{16,0},{24,8},{32,48},{40,56},{48,32},{56,40},{64,80... | collective-permute-start | bytes 3145736 | tf_op jit(solution)/shard_map/ppermute | solution.py:50
  148.4 2.7 %collective-permute-start.25 = (bf16[128,1024]{1,0:T(8,128)(2,1)S(1)}, bf16[128,1024]{1,0:T(8,128)(2,1)S(1)}, u32[]{:S(2)}, u32[]{:S(2)}) collective-permute-start(bf16[128,1024]{1,0:T(8,128)(2,1)S(1)} %get-tuple-element.135), channel_id=1, source_target_pairs={{0,96},{8,104},{16,112},{24,120},{32,0},{40,8},{48,16},{56,24},{64... | collective-permute-start | bytes 786440 | tf_op jit(solution)/shard_map/ppermute | solution.py:50
  151.1 7.5 %attend_back.4 = (bf16[512,1024]{1,0:T(8,128)(2,1)}, f32[1024,128]{1,0:T(8,128)S(1)}, f32[1024,128]{1,0:T(8,128)S(1)}) custom-call(s32[24]{0:T(128)S(1)} %concatenate.16.meta_ref, bf16[512,1024]{1,0:T(8,128)(2,1)S(1)} %copy-done, bf16[512,1024]{1,0:T(8,128)(2,1)S(1)} %add_rows.5.g_ref, ...), custom_call_target="tpu_custom_call", output_to_operand_aliasing={{0}: (11, {})} | custom-call | flops 4026531840 | bytes 6291456 | tf_op jit(solution)/shard_map/attend_back/pallas_call | solution.py:226
  158.6 0.2 add_rows.8
  158.8 0.1 collective-permute-start.28
  158.9 2.7 %collective-permute-start.29 = (bf16[256,1024]{1,0:T(8,128)(2,1)S(1)}, bf16[256,1024]{1,0:T(8,128)(2,1)S(1)}, u32[]{:S(2)}, u32[]{:S(2)}) collective-permute-start(bf16[256,1024]{1,0:T(8,128)(2,1)S(1)} %get-tuple-element.147), channel_id=1, source_target_pairs={{0,96},{8,104},{16,112},{24,120},{32,0},{40,8},{48,16},{56,24},{64... | collective-permute-start | bytes 1572872 | tf_op jit(solution)/shard_map/ppermute | solution.py:50
  161.6 1.0 collective-permute-done.24.refs_5_
  162.6 7.6 %attend_back.5 = (bf16[512,1024]{1,0:T(8,128)(2,1)}, f32[1024,128]{1,0:T(8,128)S(1)}, f32[1024,128]{1,0:T(8,128)S(1)}) custom-call(s32[24]{0:T(128)S(1)} %concatenate.16.meta_ref, bf16[512,1024]{1,0:T(8,128)(2,1)S(1)} %copy-done, bf16[512,1024]{1,0:T(8,128)(2,1)S(1)} %add_rows.5.g_ref, ...), custom_call_target="tpu_custom_call", output_to_operand_aliasing={{0}: (11, {})} | custom-call | flops 4026531840 | bytes 6291456 | tf_op jit(solution)/shard_map/attend_back/pallas_call | solution.py:226
  170.3 4.0 %collective-permute-start.26 = (bf16[512,256]{1,0:T(8,128)(2,1)S(1)}, bf16[512,256]{1,0:T(8,128)(2,1)S(1)}, u32[]{:S(2)}, u32[]{:S(2)}) collective-permute-start(bf16[512,256]{1,0:T(8,128)(2,1)S(1)} %pad_maximum_fusion.2), channel_id=1, source_target_pairs={{8,0},{16,8},{24,16},{32,24},{40,32},{48,40},{56,48},{64,56},{72,6... | collective-permute-start | bytes 786440 | tf_op jit(solution)/shard_map/ppermute | solution.py:64
  174.2 6.6 %collective-permute-done.26 = bf16[512,256]{1,0:T(8,128)(2,1)S(1)} collective-permute-done((bf16[512,256]{1,0:T(8,128)(2,1)S(1)}, bf16[512,256]{1,0:T(8,128)(2,1)S(1)}, u32[]{:S(2)}, u32[]{:S(2)}) %collective-permute-start.26) | collective-permute-done | bytes 262176 | tf_op jit(solution)/shard_map/ppermute | solution.py:64
  180.8 0.8 fusion
  181.6 1.5 add_rows.9
  (39 shorter events, 0.2 us)
Async XLA Ops:
  0.6 3.0 %copy-start.5 = (s32[8]{0:T(128)S(1)}, s32[8]{0:T(128)}, u32[]{:S(2)}) copy-start(s32[8]{0:T(128)} %constant.79.clone) | copy-start | bytes 100
  0.6 3.0 %copy-start.6 = (s32[8]{0:T(128)S(1)}, s32[8]{0:T(128)}, u32[]{:S(2)}) copy-start(s32[8]{0:T(128)} %constant.80.clone) | copy-start | bytes 100
  0.7 3.0 %copy-start.7 = (s32[8]{0:T(128)S(1)}, s32[8]{0:T(128)}, u32[]{:S(2)}) copy-start(s32[8]{0:T(128)} %constant.81.clone) | copy-start | bytes 100
  0.7 9.9 %copy-start.1 = (bf16[512,128]{1,0:T(8,128)(2,1)S(1)}, bf16[512,128]{1,0:T(8,128)(2,1)}, u32[]{:S(2)}) copy-start(bf16[512,128]{1,0:T(8,128)(2,1)} %v_ref.7) | copy-start | bytes 393220
  0.7 9.9 %copy-start.2 = (bf16[512,128]{1,0:T(8,128)(2,1)S(1)}, bf16[512,128]{1,0:T(8,128)(2,1)}, u32[]{:S(2)}) copy-start(bf16[512,128]{1,0:T(8,128)(2,1)} %k_ref.7) | copy-start | bytes 393220
  0.7 15.5 %copy-start.4 = (bf16[512,1024]{1,0:T(8,128)(2,1)S(1)}, bf16[512,1024]{1,0:T(8,128)(2,1)}, u32[]{:S(2)}) copy-start(bf16[512,1024]{1,0:T(8,128)(2,1)} %refs_8_) | copy-start | bytes 3145732
  0.7 39.4 %copy-start = (bf16[512,1024]{1,0:T(8,128)(2,1)S(1)}, bf16[512,1024]{1,0:T(8,128)(2,1)}, u32[]{:S(2)}) copy-start(bf16[512,1024]{1,0:T(8,128)(2,1)} %q_ref.6) | copy-start | bytes 3145732
  0.7 39.4 %copy-start.3 = (s32[8192]{0:T(1024)S(1)}, s32[8192]{0:T(1024)}, u32[]{:S(2)}) copy-start(s32[8192]{0:T(1024)} %param.15) | copy-start | bytes 98308
  2.2 3.2 %collective-permute-start = (bf16[512,512]{1,0:T(8,128)(2,1)S(1)}, bf16[512,512]{1,0:T(8,128)(2,1)}, u32[]{:S(2)}, u32[]{:S(2)}) collective-permute-start(bf16[512,512]{1,0:T(8,128)(2,1)S(1)} %get-tuple-element.151), channel_id=1, source_target_pairs={{0,8},{8,0},{16,24},{24,16},{32,40},{40,32},{48,56},{56,48},{64,72... | collective-permute-start | bytes 1572872 | tf_op jit(solution)/shard_map/ppermute | solution.py:50
  6.5 48.6 %collective-permute-start.1 = (bf16[1024,512]{1,0:T(8,128)(2,1)S(1)}, bf16[1024,512]{1,0:T(8,128)(2,1)S(1)}, u32[]{:S(2)}, u32[]{:S(2)}) collective-permute-start(bf16[1024,512]{1,0:T(8,128)(2,1)S(1)} %pad_maximum_fusion.refs_0_), channel_id=1, source_target_pairs={{0,1},{1,2},{2,3},{3,0},{4,5},{5,6},{6,7},{7,4},{8,9},{9,10},{10,1... | collective-permute-start | bytes 3145736 | tf_op jit(solution)/shard_map/ppermute | solution.py:58
  7.8 47.2 %collective-permute-start.2 = (bf16[1024,512]{1,0:T(8,128)(2,1)S(1)}, bf16[1024,512]{1,0:T(8,128)(2,1)S(1)}, u32[]{:S(2)}, u32[]{:S(2)}) collective-permute-start(bf16[1024,512]{1,0:T(8,128)(2,1)S(1)} %pad_maximum_fusion.refs_0_), channel_id=1, source_target_pairs={{0,3},{1,0},{2,1},{3,2},{4,7},{5,4},{6,5},{7,6},{8,11},{9,8},{10,9... | collective-permute-start | bytes 3145736 | tf_op jit(solution)/shard_map/ppermute | solution.py:58
  9.2 45.9 %collective-permute-start.3 = (bf16[1024,512]{1,0:T(8,128)(2,1)S(1)}, bf16[1024,512]{1,0:T(8,128)(2,1)S(1)}, u32[]{:S(2)}, u32[]{:S(2)}) collective-permute-start(bf16[1024,512]{1,0:T(8,128)(2,1)S(1)} %pad_maximum_fusion.refs_0_), channel_id=1, source_target_pairs={{0,4},{1,5},{2,6},{3,7},{4,0},{5,1},{6,2},{7,3},{8,12},{9,13},{10,... | collective-permute-start | bytes 3145736 | tf_op jit(solution)/shard_map/ppermute | solution.py:58
  10.6 25.7 %collective-permute-start.4 = (bf16[512,256]{1,0:T(8,128)(2,1)S(1)}, bf16[512,256]{1,0:T(8,128)(2,1)S(1)}, u32[]{:S(2)}, u32[]{:S(2)}) collective-permute-start(bf16[512,256]{1,0:T(8,128)(2,1)S(1)} %pad_maximum_fusion.1), channel_id=1, source_target_pairs={{0,8},{8,16},{16,24},{24,32},{32,40},{40,48},{48,56},{56,64},{64,7... | collective-permute-start | bytes 786440 | tf_op jit(solution)/shard_map/ppermute | solution.py:64
  16.3 45.5 %collective-permute-start.10 = (bf16[512,1024]{1,0:T(8,128)(2,1)S(1)}, bf16[512,1024]{1,0:T(8,128)(2,1)S(1)}, u32[]{:S(2)}, u32[]{:S(2)}) collective-permute-start(bf16[512,1024]{1,0:T(8,128)(2,1)S(1)} %copy-done.4), channel_id=1, source_target_pairs={{0,32},{8,40},{16,48},{24,56},{32,64},{40,72},{48,80},{56,88},{64,... | collective-permute-start | bytes 3145736 | tf_op jit(solution)/shard_map/ppermute | solution.py:50
  36.4 25.4 %collective-permute-start.11 = (bf16[512,1024]{1,0:T(8,128)(2,1)S(1)}, bf16[512,1024]{1,0:T(8,128)(2,1)S(1)}, u32[]{:S(2)}, u32[]{:S(2)}) collective-permute-start(bf16[512,1024]{1,0:T(8,128)(2,1)S(1)} %copy-done.4), channel_id=1, source_target_pairs={{0,96},{8,104},{16,112},{24,120},{32,0},{40,8},{48,16},{56,24},{64... | collective-permute-start | bytes 3145736 | tf_op jit(solution)/shard_map/ppermute | solution.py:50
  55.1 9.2 %collective-permute-start.7 = (bf16[512,1024]{1,0:T(8,128)(2,1)S(1)}, bf16[512,1024]{1,0:T(8,128)(2,1)S(1)}, u32[]{:S(2)}, u32[]{:S(2)}) collective-permute-start(bf16[512,1024]{1,0:T(8,128)(2,1)S(1)} %get-tuple-element.84), channel_id=1, source_target_pairs={{0,8},{8,0},{16,24},{24,16},{32,40},{40,32},{48,56},{56,48},{64,72... | collective-permute-start | bytes 3145736 | tf_op jit(solution)/shard_map/ppermute | solution.py:50
  59.1 25.9 %collective-permute-start.5 = (bf16[1024,512]{1,0:T(8,128)(2,1)S(1)}, bf16[1024,512]{1,0:T(8,128)(2,1)S(1)}, u32[]{:S(2)}, u32[]{:S(2)}) collective-permute-start(bf16[1024,512]{1,0:T(8,128)(2,1)S(1)} %collective-permute-done.3.refs_3_), channel_id=1, source_target_pairs={{0,1},{1,2},{2,3},{3,0},{4,5},{5,6},{6,7},{7,4},{8,9},{9,10},{10,1... | collective-permute-start | bytes 3145736 | tf_op jit(solution)/shard_map/ppermute | solution.py:58
  59.1 25.9 %collective-permute-start.6 = (bf16[1024,512]{1,0:T(8,128)(2,1)S(1)}, bf16[1024,512]{1,0:T(8,128)(2,1)S(1)}, u32[]{:S(2)}, u32[]{:S(2)}) collective-permute-start(bf16[1024,512]{1,0:T(8,128)(2,1)S(1)} %collective-permute-done.3.refs_3_), channel_id=1, source_target_pairs={{0,3},{1,0},{2,1},{3,2},{4,7},{5,4},{6,5},{7,6},{8,11},{9,8},{10,9... | collective-permute-start | bytes 3145736 | tf_op jit(solution)/shard_map/ppermute | solution.py:58
  61.8 25.6 %collective-permute-start.12 = (bf16[512,1024]{1,0:T(8,128)(2,1)S(1)}, bf16[512,1024]{1,0:T(8,128)(2,1)S(1)}, u32[]{:S(2)}, u32[]{:S(2)}) collective-permute-start(bf16[512,1024]{1,0:T(8,128)(2,1)S(1)} %collective-permute-done.10.refs_9_), channel_id=1, source_target_pairs={{0,32},{8,40},{16,48},{24,56},{32,64},{40,72},{48,80},{56,88},{64,... | collective-permute-start | bytes 3145736 | tf_op jit(solution)/shard_map/ppermute | solution.py:50
  61.8 25.6 %collective-permute-start.13 = (bf16[512,1024]{1,0:T(8,128)(2,1)S(1)}, bf16[512,1024]{1,0:T(8,128)(2,1)S(1)}, u32[]{:S(2)}, u32[]{:S(2)}) collective-permute-start(bf16[512,1024]{1,0:T(8,128)(2,1)S(1)} %copy-done.4), channel_id=1, source_target_pairs={{0,16},{8,24},{16,0},{24,8},{32,48},{40,56},{48,32},{56,40},{64,80... | collective-permute-start | bytes 3145736 | tf_op jit(solution)/shard_map/ppermute | solution.py:50
  64.2 43.3 %collective-permute-start.9 = (bf16[1024,512]{1,0:T(8,128)(2,1)S(1)}, bf16[1024,512]{1,0:T(8,128)(2,1)S(1)}, u32[]{:S(2)}, u32[]{:S(2)}) collective-permute-start(bf16[1024,512]{1,0:T(8,128)(2,1)S(1)} %collective-permute-done.1.refs_1_), channel_id=1, source_target_pairs={{0,1},{1,2},{2,3},{3,0},{4,5},{5,6},{6,7},{7,4},{8,9},{9,10},{10,1... | collective-permute-start | bytes 3145736 | tf_op jit(solution)/shard_map/ppermute | solution.py:58
  85.1 25.3 %collective-permute-start.8 = (bf16[1024,512]{1,0:T(8,128)(2,1)S(1)}, bf16[1024,512]{1,0:T(8,128)(2,1)S(1)}, u32[]{:S(2)}, u32[]{:S(2)}) collective-permute-start(bf16[1024,512]{1,0:T(8,128)(2,1)S(1)} %collective-permute-done.6.refs_1_.refs_5_), channel_id=1, source_target_pairs={{0,3},{1,0},{2,1},{3,2},{4,7},{5,4},{6,5},{7,6},{8,11},{9,8},{10,9... | collective-permute-start | bytes 3145736 | tf_op jit(solution)/shard_map/ppermute | solution.py:58
  87.4 26.9 %collective-permute-start.14 = (bf16[512,1024]{1,0:T(8,128)(2,1)S(1)}, bf16[512,1024]{1,0:T(8,128)(2,1)S(1)}, u32[]{:S(2)}, u32[]{:S(2)}) collective-permute-start(bf16[512,1024]{1,0:T(8,128)(2,1)S(1)} %collective-permute-done.13.refs_11_), channel_id=1, source_target_pairs={{0,32},{8,40},{16,48},{24,56},{32,64},{40,72},{48,80},{56,88},{64,... | collective-permute-start | bytes 3145736 | tf_op jit(solution)/shard_map/ppermute | solution.py:50
  87.4 26.9 %collective-permute-start.15 = (bf16[512,1024]{1,0:T(8,128)(2,1)S(1)}, bf16[512,1024]{1,0:T(8,128)(2,1)S(1)}, u32[]{:S(2)}, u32[]{:S(2)}) collective-permute-start(bf16[512,1024]{1,0:T(8,128)(2,1)S(1)} %collective-permute-done.13.refs_11_), channel_id=1, source_target_pairs={{0,96},{8,104},{16,112},{24,120},{32,0},{40,8},{48,16},{56,24},{64... | collective-permute-start | bytes 3145736 | tf_op jit(solution)/shard_map/ppermute | solution.py:50
  90.1 24.2 %collective-permute-start.16 = (bf16[512,1024]{1,0:T(8,128)(2,1)S(1)}, bf16[512,1024]{1,0:T(8,128)(2,1)S(1)}, u32[]{:S(2)}, u32[]{:S(2)}) collective-permute-start(bf16[512,1024]{1,0:T(8,128)(2,1)S(1)} %collective-permute-done.12.refs_15_), channel_id=1, source_target_pairs={{0,16},{8,24},{16,0},{24,8},{32,48},{40,56},{48,32},{56,40},{64,80... | collective-permute-start | bytes 3145736 | tf_op jit(solution)/shard_map/ppermute | solution.py:50
  114.3 31.1 %collective-permute-start.22 = (bf16[640,1024]{1,0:T(8,128)(2,1)S(1)}, bf16[640,1024]{1,0:T(8,128)(2,1)S(1)}, u32[]{:S(2)}, u32[]{:S(2)}) collective-permute-start(bf16[640,1024]{1,0:T(8,128)(2,1)S(1)} %get-tuple-element.96), channel_id=1, source_target_pairs={{0,32},{8,40},{16,48},{24,56},{32,64},{40,72},{48,80},{56,88},{64,... | collective-permute-start | bytes 3932168 | tf_op jit(solution)/shard_map/ppermute | solution.py:50
  114.4 28.0 %collective-permute-start.19 = (bf16[512,1024]{1,0:T(8,128)(2,1)S(1)}, bf16[512,1024]{1,0:T(8,128)(2,1)S(1)}, u32[]{:S(2)}, u32[]{:S(2)}) collective-permute-start(bf16[512,1024]{1,0:T(8,128)(2,1)S(1)} %get-tuple-element.109), channel_id=1, source_target_pairs={{0,16},{8,24},{16,0},{24,8},{32,48},{40,56},{48,32},{56,40},{64,80... | collective-permute-start | bytes 3145736 | tf_op jit(solution)/shard_map/ppermute | solution.py:50
  114.7 30.7 %collective-permute-start.23 = (bf16[640,1024]{1,0:T(8,128)(2,1)S(1)}, bf16[640,1024]{1,0:T(8,128)(2,1)S(1)}, u32[]{:S(2)}, u32[]{:S(2)}) collective-permute-start(bf16[640,1024]{1,0:T(8,128)(2,1)S(1)} %get-tuple-element.120), channel_id=1, source_target_pairs={{0,96},{8,104},{16,112},{24,120},{32,0},{40,8},{48,16},{56,24},{64... | collective-permute-start | bytes 3932168 | tf_op jit(solution)/shard_map/ppermute | solution.py:50
  129.9 6.7 %collective-permute-start.17 = (bf16[256,1024]{1,0:T(8,128)(2,1)S(1)}, bf16[256,1024]{1,0:T(8,128)(2,1)S(1)}, u32[]{:S(2)}, u32[]{:S(2)}) collective-permute-start(bf16[256,1024]{1,0:T(8,128)(2,1)S(1)} %get-tuple-element.103), channel_id=1, source_target_pairs={{0,8},{8,0},{16,24},{24,16},{32,40},{40,32},{48,56},{56,48},{64,72... | collective-permute-start | bytes 1572872 | tf_op jit(solution)/shard_map/ppermute | solution.py:50
  133.8 2.9 %collective-permute-start.18 = (bf16[256,1024]{1,0:T(8,128)(2,1)S(1)}, bf16[256,1024]{1,0:T(8,128)(2,1)S(1)}, u32[]{:S(2)}, u32[]{:S(2)}) collective-permute-start(bf16[256,1024]{1,0:T(8,128)(2,1)S(1)} %get-tuple-element.104), channel_id=1, source_target_pairs={{0,8},{8,0},{16,24},{24,16},{32,40},{40,32},{48,56},{56,48},{64,72... | collective-permute-start | bytes 1572872 | tf_op jit(solution)/shard_map/ppermute | solution.py:50
  142.6 16.0 %collective-permute-start.20 = (bf16[256,1024]{1,0:T(8,128)(2,1)S(1)}, bf16[256,1024]{1,0:T(8,128)(2,1)S(1)}, u32[]{:S(2)}, u32[]{:S(2)}) collective-permute-start(bf16[256,1024]{1,0:T(8,128)(2,1)S(1)} %get-tuple-element.114), channel_id=1, source_target_pairs={{0,32},{8,40},{16,48},{24,56},{32,64},{40,72},{48,80},{56,88},{64,... | collective-permute-start | bytes 1572872 | tf_op jit(solution)/shard_map/ppermute | solution.py:50
  142.7 15.9 %collective-permute-start.21 = (bf16[256,1024]{1,0:T(8,128)(2,1)S(1)}, bf16[256,1024]{1,0:T(8,128)(2,1)S(1)}, u32[]{:S(2)}, u32[]{:S(2)}) collective-permute-start(bf16[256,1024]{1,0:T(8,128)(2,1)S(1)} %get-tuple-element.115), channel_id=1, source_target_pairs={{0,96},{8,104},{16,112},{24,120},{32,0},{40,8},{48,16},{56,24},{64... | collective-permute-start | bytes 1572872 | tf_op jit(solution)/shard_map/ppermute | solution.py:50
  145.8 35.9 %collective-permute-start.27 = (bf16[512,1024]{1,0:T(8,128)(2,1)S(1)}, bf16[512,1024]{1,0:T(8,128)(2,1)S(1)}, u32[]{:S(2)}, u32[]{:S(2)}) collective-permute-start(bf16[512,1024]{1,0:T(8,128)(2,1)S(1)} %add_rows.7), channel_id=1, source_target_pairs={{0,16},{8,24},{16,0},{24,8},{32,48},{40,56},{48,32},{56,40},{64,80... | collective-permute-start | bytes 3145736 | tf_op jit(solution)/shard_map/ppermute | solution.py:50
  148.4 14.2 %collective-permute-start.24 = (bf16[128,1024]{1,0:T(8,128)(2,1)S(1)}, bf16[128,1024]{1,0:T(8,128)(2,1)S(1)}, u32[]{:S(2)}, u32[]{:S(2)}) collective-permute-start(bf16[128,1024]{1,0:T(8,128)(2,1)S(1)} %get-tuple-element.134), channel_id=1, source_target_pairs={{0,32},{8,40},{16,48},{24,56},{32,64},{40,72},{48,80},{56,88},{64,... | collective-permute-start | bytes 786440 | tf_op jit(solution)/shard_map/ppermute | solution.py:50
  148.4 14.2 %collective-permute-start.25 = (bf16[128,1024]{1,0:T(8,128)(2,1)S(1)}, bf16[128,1024]{1,0:T(8,128)(2,1)S(1)}, u32[]{:S(2)}, u32[]{:S(2)}) collective-permute-start(bf16[128,1024]{1,0:T(8,128)(2,1)S(1)} %get-tuple-element.135), channel_id=1, source_target_pairs={{0,96},{8,104},{16,112},{24,120},{32,0},{40,8},{48,16},{56,24},{64... | collective-permute-start | bytes 786440 | tf_op jit(solution)/shard_map/ppermute | solution.py:50
  158.8 22.8 %collective-permute-start.28 = (bf16[256,1024]{1,0:T(8,128)(2,1)S(1)}, bf16[256,1024]{1,0:T(8,128)(2,1)S(1)}, u32[]{:S(2)}, u32[]{:S(2)}) collective-permute-start(bf16[256,1024]{1,0:T(8,128)(2,1)S(1)} %get-tuple-element.139), channel_id=1, source_target_pairs={{0,32},{8,40},{16,48},{24,56},{32,64},{40,72},{48,80},{56,88},{64,... | collective-permute-start | bytes 1572872 | tf_op jit(solution)/shard_map/ppermute | solution.py:50
  158.9 22.7 %collective-permute-start.29 = (bf16[256,1024]{1,0:T(8,128)(2,1)S(1)}, bf16[256,1024]{1,0:T(8,128)(2,1)S(1)}, u32[]{:S(2)}, u32[]{:S(2)}) collective-permute-start(bf16[256,1024]{1,0:T(8,128)(2,1)S(1)} %get-tuple-element.147), channel_id=1, source_target_pairs={{0,96},{8,104},{16,112},{24,120},{32,0},{40,8},{48,16},{56,24},{64... | collective-permute-start | bytes 1572872 | tf_op jit(solution)/shard_map/ppermute | solution.py:50
  170.3 10.5 %collective-permute-start.26 = (bf16[512,256]{1,0:T(8,128)(2,1)S(1)}, bf16[512,256]{1,0:T(8,128)(2,1)S(1)}, u32[]{:S(2)}, u32[]{:S(2)}) collective-permute-start(bf16[512,256]{1,0:T(8,128)(2,1)S(1)} %pad_maximum_fusion.2), channel_id=1, source_target_pairs={{8,0},{16,8},{24,16},{32,24},{40,32},{48,40},{56,48},{64,56},{72,6... | collective-permute-start | bytes 786440 | tf_op jit(solution)/shard_map/ppermute | solution.py:64

commit v9 on v8

--- a/solution.py
+++ b/solution.py
@@ -520,9 +520,9 @@
 
     g_keep = lax.dynamic_slice_in_dim(output_grad, k * half_d, half_d, 1)
     g_give = lax.dynamic_slice_in_dim(output_grad, (1 - k) * half_d, half_d, 1)
-    g_got, meta = tied((move_row(g_give, dk=1), meta))
+    kv_earlier = passed_along(jnp.concatenate([key_rows, value_rows], 1), "row", 1)
+    g_got, kv_earlier, meta = tied((move_row(g_give, dk=1), kv_earlier, meta))
     g0 = jnp.concatenate([g_keep, g_got], 0)
-    kv_earlier = passed_along(jnp.concatenate([key_rows, value_rows], 1), "row", 1)
     segments = segment_ids.reshape(-1, LANES)
 
     (out_proj,) = tied((out_proj,), g0)

time: 183 us -> 168 us (0.918)
  waiting for transfers between devices: 54.3 us -> 38.5 us
    ppermute x2, waiting for transfers between devices: 25 us -> 8.24 us  [passed_along(): lax.ppermute(value, axis, [(source, source + steps) for source in range(f...]
    ppermute x21, waiting for transfers between devices: 2.61 us -> 9.47 us  [move_row(): return lax.ppermute(value, 'row', pairs)]
    ppermute x7, waiting for transfers between devices: 26.8 us -> 20.8 us  [move_col(): return lax.ppermute(value, 'col', pairs)]
  transfers between devices with their start and end apart: 30 -> 30, of which waited for: 6 -> 13; matrix products, arithmetic and copies ran while one was open for 1% -> 1% of each run, Pallas kernels for 38% -> 42%
where the time goes in v9:
time: 168 us; the launch traced here: 167 us
  Pallas kernels  71 us (42%)
  starting transfers between devices  52.3 us (31%)
  waiting for transfers between devices  38.5 us (23%)
  local copies, waits for them, and re-layouts  2.52 us (2%)
  other arithmetic  1.97 us (1%)
    ppermute x21, starting transfers between devices, move_row(): return lax.ppermute(value, 'row', pairs)  35.2 us
    ppermute x7, waiting for transfers between devices, move_col(): return lax.ppermute(value, 'col', pairs)  20.8 us
    pallas_call x3, Pallas kernels, attend_back(): pl.pallas_call(functools.partial(bwd_kernel, len(earlier), last), grid_sp...  20.6 us
    pallas_call x4, Pallas kernels, project(): pl.pallas_call(functools.partial(proj_kernel, tuple(slots), held, plan),...  17.7 us
    pallas_call x1, Pallas kernels, attend(): pl.pallas_call(fwd_kernel, grid_spec=pltpu.PrefetchScalarGridSpec(num_sca...  14.9 us
    pallas_call x1, Pallas kernels, attn_grad_part(): pl.pallas_call(kernel, grid_spec=pltpu.PrefetchScalarGridSpec(num_scalar_...  12.6 us
    ppermute x21, waiting for transfers between devices, move_row(): return lax.ppermute(value, 'row', pairs)  9.47 us
    ppermute x2, starting transfers between devices, passed_along(): lax.ppermute(value, axis, [(source, source + steps) for source in range(f...  8.84 us
  transfers between devices with their start and end apart: 30, of which 13 were waited for; matrix products, arithmetic and copies ran while one was open for 1% of the time, Pallas kernels for 42%

profile of v9, /device:TPU:1, one launch (start us, length us, event | category | flops | bytes accessed | tf_op | source)
XLA Modules:
  0.0 167.4 jit_solution(2383032706295716107)
XLA Ops:
  0.6 0.0 copy-start.6
  0.7 2.2 %constant_dynamic-slice_fusion = (bf16[512,512]{1,0:T(8,128)(2,1)S(1)}, bf16[512,512]{1,0:T(8,128)(2,1)}) fusion(bf16[512,1024]{1,0:T(8,128)(2,1)} %param.13, s32[]{:T(128)S(6)} %select_n.38, s32[]{:T(128)S(6)} %select_n.32), kind=kLoop, calls=%fused_computation.13 | loop fusion | bytes 2097160 | tf_op jit(solution)/shard_map/dynamic_slice | solution.py:521
  3.0 1.4 collective-permute-start
  4.4 4.8 %collective-permute-start.1 = (bf16[512,256]{1,0:T(8,128)(2,1)S(1)}, bf16[512,256]{1,0:T(8,128)(2,1)S(1)}, u32[]{:S(2)}, u32[]{:S(2)}) collective-permute-start(bf16[512,256]{1,0:T(8,128)(2,1)S(1)} %pad_maximum_fusion.1), channel_id=1, source_target_pairs={{0,8},{8,16},{16,24},{24,32},{32,40},{40,48},{48,56},{56,64},{64,7... | collective-permute-start | bytes 786440 | tf_op jit(solution)/shard_map/ppermute | solution.py:64
  9.3 0.1 concatenate.17.meta_ref
  9.4 3.1 %collective-permute-done.1.kv_ref = bf16[512,256]{1,0:T(8,128)(2,1)S(1)} collective-permute-done((bf16[512,256]{1,0:T(8,128)(2,1)S(1)}, bf16[512,256]{1,0:T(8,128)(2,1)S(1)}, u32[]{:S(2)}, u32[]{:S(2)}) %collective-permute-start.1) | collective-permute-done | bytes 262176 | tf_op jit(solution)/shard_map/ppermute | solution.py:64
  12.5 1.1 pad_maximum_fusion.refs_0_
  13.6 1.3 collective-permute-start.2
  14.9 1.5 collective-permute-start.3
  16.4 0.4 collective-permute-start.4
  16.8 1.6 collective-permute-start.10
  18.4 2.1 %collective-permute-start.11 = (bf16[512,1024]{1,0:T(8,128)(2,1)S(1)}, bf16[512,1024]{1,0:T(8,128)(2,1)S(1)}, u32[]{:S(2)}, u32[]{:S(2)}) collective-permute-start(bf16[512,1024]{1,0:T(8,128)(2,1)S(1)} %copy-done.4), channel_id=1, source_target_pairs={{0,96},{8,104},{16,112},{24,120},{32,0},{40,8},{48,16},{56,24},{64... | collective-permute-start | bytes 3145736 | tf_op jit(solution)/shard_map/ppermute | solution.py:50
  20.6 14.9 %attend.1 = (bf16[512,1024]{1,0:T(8,128)(2,1)S(1)}, f32[8,1,512]{2,1,0:T(1,128)S(1)}, f32[8,1,512]{2,1,0:T(1,128)S(1)}) custom-call(s32[24]{0:T(128)S(1)} %concatenate.17.meta_ref, bf16[512,1024]{1,0:T(8,128)(2,1)S(1)} %copy-done, bf16[512,256]{1,0:T(8,128)(2,1)S(1)} %collective-permute-done.1.kv_ref, bf16[512,128]{1,0:T(8,128)(2,1)S(1)} %copy-done.2, ...), custom_call_target="tpu_custom_call" | custom-call | flops 4294967296 | bytes 8388608 | tf_op jit(solution)/shard_map/attend/pallas_call | solution.py:148
  35.5 0.6 collective-permute-done.2.refs_1_
  36.0 0.4 collective-permute-done.3.refs_2_
  36.4 1.7 collective-permute-done.4.refs_3_
  38.1 1.6 collective-permute-start.7
  39.7 0.0 collective-permute-start.5
  39.7 2.7 %collective-permute-start.6 = (bf16[1024,512]{1,0:T(8,128)(2,1)S(1)}, bf16[1024,512]{1,0:T(8,128)(2,1)S(1)}, u32[]{:S(2)}, u32[]{:S(2)}) collective-permute-start(bf16[1024,512]{1,0:T(8,128)(2,1)S(1)} %collective-permute-done.4.refs_3_), channel_id=1, source_target_pairs={{0,3},{1,0},{2,1},{3,2},{4,7},{5,4},{6,5},{7,6},{8,11},{9,8},{10,9... | collective-permute-start | bytes 3145736 | tf_op jit(solution)/shard_map/ppermute | solution.py:58
  42.4 3.9 %collective-permute-start.12 = (bf16[512,1024]{1,0:T(8,128)(2,1)S(1)}, bf16[512,1024]{1,0:T(8,128)(2,1)S(1)}, u32[]{:S(2)}, u32[]{:S(2)}) collective-permute-start(bf16[512,1024]{1,0:T(8,128)(2,1)S(1)} %collective-permute-done.10.refs_9_), channel_id=1, source_target_pairs={{0,32},{8,40},{16,48},{24,56},{32,64},{40,72},{48,80},{56,88},{64,... | collective-permute-start | bytes 3145736 | tf_op jit(solution)/shard_map/ppermute | solution.py:50
  46.3 1.8 %collective-permute-start.13 = (bf16[512,1024]{1,0:T(8,128)(2,1)S(1)}, bf16[512,1024]{1,0:T(8,128)(2,1)S(1)}, u32[]{:S(2)}, u32[]{:S(2)}) collective-permute-start(bf16[512,1024]{1,0:T(8,128)(2,1)S(1)} %copy-done.4), channel_id=1, source_target_pairs={{0,16},{8,24},{16,0},{24,8},{32,48},{40,56},{48,32},{56,40},{64,80... | collective-permute-start | bytes 3145736 | tf_op jit(solution)/shard_map/ppermute | solution.py:50
  48.1 0.1 constant_dynamic-update-slice_fusion.1
  48.2 0.1 collective-permute-start.9
  48.3 0.1 constant_dynamic-update-slice_fusion.refs_4_.refs_2_.refs_1_
  48.4 6.7 %project.4.refs_3_ = bf16[2,64,256,1024]{3,2,1,0:T(8,128)(2,1)} custom-call(s32[24]{0:T(128)S(1)} %concatenate.17.meta_ref, bf16[1024,512]{1,0:T(8,128)(2,1)S(1)} %pad_maximum_fusion.refs_0_, bf16[1024,512]{1,0:T(8,128)(2,1)S(1)} %collective-permute-done.2.refs_1_, bf16[1024,512]{1,0:T(8,128)(2,1)S(1)} %collective-permute-done.3.refs_2_, ...), custom_call_target="tpu_custom_call" | custom-call | flops 4294967296 | bytes 10485760 | tf_op jit(solution)/shard_map/project/pallas_call | solution.py:324
  55.1 10.5 %collective-permute-done.5.refs_0_.refs_4_ = bf16[1024,512]{1,0:T(8,128)(2,1)S(1)} collective-permute-done((bf16[1024,512]{1,0:T(8,128)(2,1)S(1)}, bf16[1024,512]{1,0:T(8,128)(2,1)S(1)}, u32[]{:S(2)}, u32[]{:S(2)}) %collective-permute-start.5) | collective-permute-done | bytes 1048608 | tf_op jit(solution)/shard_map/ppermute | solution.py:58
  65.6 2.4 %collective-permute-start.8 = (bf16[1024,512]{1,0:T(8,128)(2,1)S(1)}, bf16[1024,512]{1,0:T(8,128)(2,1)S(1)}, u32[]{:S(2)}, u32[]{:S(2)}) collective-permute-start(bf16[1024,512]{1,0:T(8,128)(2,1)S(1)} %collective-permute-done.6.refs_1_.refs_5_), channel_id=1, source_target_pairs={{0,3},{1,0},{2,1},{3,2},{4,7},{5,4},{6,5},{7,6},{8,11},{9,8},{10,9... | collective-permute-start | bytes 3145736 | tf_op jit(solution)/shard_map/ppermute | solution.py:58
  68.0 3.4 %collective-permute-done.12.refs_15_ = bf16[512,1024]{1,0:T(8,128)(2,1)S(1)} collective-permute-done((bf16[512,1024]{1,0:T(8,128)(2,1)S(1)}, bf16[512,1024]{1,0:T(8,128)(2,1)S(1)}, u32[]{:S(2)}, u32[]{:S(2)}) %collective-permute-start.12) | collective-permute-done | bytes 1048608 | tf_op jit(solution)/shard_map/ppermute | solution.py:50
  71.4 0.2 collective-permute-done.13.refs_11_
  71.6 1.6 collective-permute-start.14
  73.3 1.0 collective-permute-start.15
  74.3 1.8 %collective-permute-start.16 = (bf16[512,1024]{1,0:T(8,128)(2,1)S(1)}, bf16[512,1024]{1,0:T(8,128)(2,1)S(1)}, u32[]{:S(2)}, u32[]{:S(2)}) collective-permute-start(bf16[512,1024]{1,0:T(8,128)(2,1)S(1)} %collective-permute-done.12.refs_15_), channel_id=1, source_target_pairs={{0,16},{8,24},{16,0},{24,8},{32,48},{40,56},{48,32},{56,40},{64,80... | collective-permute-start | bytes 3145736 | tf_op jit(solution)/shard_map/ppermute | solution.py:50
  76.2 4.2 %project.5.refs_2_ = bf16[2,64,256,1024]{3,2,1,0:T(8,128)(2,1)} custom-call(s32[24]{0:T(128)S(1)} %concatenate.17.meta_ref, bf16[1024,512]{1,0:T(8,128)(2,1)S(1)} %collective-permute-done.5.refs_0_.refs_4_, bf16[1024,512]{1,0:T(8,128)(2,1)S(1)} %collective-permute-done.6.refs_1_.refs_5_, ...), custom_call_target="tpu_custom_call", output_to_operand_aliasing={{}: (4, {})} | custom-call | flops 2147483648 | bytes 6291456 | tf_op jit(solution)/shard_map/project/pallas_call | solution.py:324
  80.4 7.7 %collective-permute-done.9.refs_0_.refs_6_ = bf16[1024,512]{1,0:T(8,128)(2,1)S(1)} collective-permute-done((bf16[1024,512]{1,0:T(8,128)(2,1)S(1)}, bf16[1024,512]{1,0:T(8,128)(2,1)S(1)}, u32[]{:S(2)}, u32[]{:S(2)}) %collective-permute-start.9) | collective-permute-done | bytes 1048608 | tf_op jit(solution)/shard_map/ppermute | solution.py:58
  88.1 2.8 %project.6.refs_2_ = bf16[2,64,256,1024]{3,2,1,0:T(8,128)(2,1)} custom-call(s32[24]{0:T(128)S(1)} %concatenate.17.meta_ref, bf16[1024,512]{1,0:T(8,128)(2,1)S(1)} %collective-permute-done.9.refs_0_.refs_6_, bf16[1024,1024]{1,0:T(8,128)(2,1)S(1)} %constant_dynamic-update-slice_fusion.refs_4_.refs_2_.refs_1_, ...), custom_call_target="tpu_custom_call", output_to_operand_aliasing={{}: (3, {})} | custom-call | flops 1073741824 | bytes 4194304 | tf_op jit(solution)/shard_map/project/pallas_call | solution.py:324
  90.9 3.9 %project.7 = (bf16[2,64,256,1024]{3,2,1,0:T(8,128)(2,1)}, bf16[512,1024]{1,0:T(8,128)(2,1)S(1)}, bf16[640,1024]{1,0:T(8,128)(2,1)S(1)}, bf16[640,1024]{1,0:T(8,1...) custom-call(s32[24]{0:T(128)S(1)} %concatenate.17.meta_ref, ...), custom_call_target="tpu_custom_call", output_to_operand_aliasing={{0}: (3, {})} | custom-call | flops 1073741824 | bytes 4194304 | tf_op jit(solution)/shard_map/project/pallas_call | solution.py:324
  94.8 0.9 collective-permute-done.14.refs_12_
  95.8 0.1 collective-permute-done.15.refs_13_
  95.9 2.3 %collective-permute-done.16.refs_14_ = bf16[512,1024]{1,0:T(8,128)(2,1)S(1)} collective-permute-done((bf16[512,1024]{1,0:T(8,128)(2,1)S(1)}, bf16[512,1024]{1,0:T(8,128)(2,1)S(1)}, u32[]{:S(2)}, u32[]{:S(2)}) %collective-permute-start.16) | collective-permute-done | bytes 1048608 | tf_op jit(solution)/shard_map/ppermute | solution.py:50
  98.2 0.9 collective-permute-start.22
  99.1 1.5 collective-permute-start.19
  100.6 2.1 %collective-permute-start.23 = (bf16[640,1024]{1,0:T(8,128)(2,1)S(1)}, bf16[640,1024]{1,0:T(8,128)(2,1)S(1)}, u32[]{:S(2)}, u32[]{:S(2)}) collective-permute-start(bf16[640,1024]{1,0:T(8,128)(2,1)S(1)} %get-tuple-element.122), channel_id=1, source_target_pairs={{0,96},{8,104},{16,112},{24,120},{32,0},{40,8},{48,16},{56,24},{64... | collective-permute-start | bytes 3932168 | tf_op jit(solution)/shard_map/ppermute | solution.py:50
  102.7 12.6 %attn_grad.1 = (f32[512,1024]{1,0:T(8,128)S(1)}, bf16[256,1024]{1,0:T(8,128)(2,1)S(1)}, bf16[256,1024]{1,0:T(8,128)(2,1)S(1)}) custom-call(s32[24]{0:T(128)S(1)} %concatenate.17.meta_ref, bf16[1024,512]{1,0:T(8,128)(2,1)S(1)} %pad_maximum_fusion.refs_0_, bf16[1024,512]{1,0:T(8,128)(2,1)S(1)} %collective-permute-done.2.refs_1_, ...), custom_call_target="tpu_custom_call" | custom-call | flops 8589934592 | bytes 20971520 | tf_op jit(solution)/shard_map/attn_grad/pallas_call | solution.py:419
  115.3 4.1 %collective-permute-start.17 = (bf16[256,1024]{1,0:T(8,128)(2,1)S(1)}, bf16[256,1024]{1,0:T(8,128)(2,1)S(1)}, u32[]{:S(2)}, u32[]{:S(2)}) collective-permute-start(bf16[256,1024]{1,0:T(8,128)(2,1)S(1)} %get-tuple-element.105), channel_id=1, source_target_pairs={{0,8},{8,0},{16,24},{24,16},{32,40},{40,32},{48,56},{56,48},{64,72... | collective-permute-start | bytes 1572872 | tf_op jit(solution)/shard_map/ppermute | solution.py:50
  119.4 0.1 collective-permute-start.18
  119.5 2.8 %fetch.1 = (bf16[512,1024]{1,0:T(8,128)(2,1)S(1)}, bf16[512,1024]{1,0:T(8,128)(2,1)S(1)}, bf16[512,1024]{1,0:T(8,128)(2,1)S(1)}, bf16[512,1024]{1,0:T(8,128)(2,1)S(1)}) custom-call(s32[24]{0:T(128)S(1)} %concatenate.17.meta_ref, bf16[2,64,256,1024]{3,2,1,0:T(8,128)(2,1)} %get-tuple-element.109.buffer_ref), custom_call_target="tpu_custom_call" | custom-call | bytes 65536 | tf_op jit(solution)/shard_map/fetch/pallas_call | solution.py:466
  122.3 0.2 add_rows.5.g_ref
  122.5 5.5 %attend_back.3 = (bf16[512,1024]{1,0:T(8,128)(2,1)}, f32[1024,128]{1,0:T(8,128)S(1)}, f32[1024,128]{1,0:T(8,128)S(1)}) custom-call(s32[24]{0:T(128)S(1)} %concatenate.17.meta_ref, bf16[512,1024]{1,0:T(8,128)(2,1)S(1)} %copy-done, bf16[512,1024]{1,0:T(8,128)(2,1)S(1)} %add_rows.5.g_ref, bf16[512,256]{1,0:T(8,128)(2,1)S(1)} %collective-permute-done.1.kv_ref, ...), custom_call_target="tpu_custom_call" | custom-call | flops 1048576 | bytes 65536 | tf_op jit(solution)/shard_map/attend_back/pallas_call | solution.py:226
  128.0 0.2 add_rows.6
  128.3 0.1 collective-permute-start.20
  128.4 2.7 %collective-permute-start.21 = (bf16[256,1024]{1,0:T(8,128)(2,1)S(1)}, bf16[256,1024]{1,0:T(8,128)(2,1)S(1)}, u32[]{:S(2)}, u32[]{:S(2)}) collective-permute-start(bf16[256,1024]{1,0:T(8,128)(2,1)S(1)} %get-tuple-element.117), channel_id=1, source_target_pairs={{0,96},{8,104},{16,112},{24,120},{32,0},{40,8},{48,16},{56,24},{64... | collective-permute-start | bytes 1572872 | tf_op jit(solution)/shard_map/ppermute | solution.py:50
  131.0 0.4 add_rows.7
  131.4 1.2 collective-permute-start.27
  132.6 2.7 %collective-permute-start.25 = (bf16[128,1024]{1,0:T(8,128)(2,1)S(1)}, bf16[128,1024]{1,0:T(8,128)(2,1)S(1)}, u32[]{:S(2)}, u32[]{:S(2)}) collective-permute-start(bf16[128,1024]{1,0:T(8,128)(2,1)S(1)} %get-tuple-element.137), channel_id=1, source_target_pairs={{0,96},{8,104},{16,112},{24,120},{32,0},{40,8},{48,16},{56,24},{64... | collective-permute-start | bytes 786440 | tf_op jit(solution)/shard_map/ppermute | solution.py:50
  135.3 7.5 %attend_back.4 = (bf16[512,1024]{1,0:T(8,128)(2,1)}, f32[1024,128]{1,0:T(8,128)S(1)}, f32[1024,128]{1,0:T(8,128)S(1)}) custom-call(s32[24]{0:T(128)S(1)} %concatenate.17.meta_ref, bf16[512,1024]{1,0:T(8,128)(2,1)S(1)} %copy-done, bf16[512,1024]{1,0:T(8,128)(2,1)S(1)} %add_rows.5.g_ref, ...), custom_call_target="tpu_custom_call", output_to_operand_aliasing={{0}: (11, {})} | custom-call | flops 4026531840 | bytes 6291456 | tf_op jit(solution)/shard_map/attend_back/pallas_call | solution.py:226
  142.8 0.2 add_rows.8
  143.1 0.1 collective-permute-start.28
  143.1 2.7 %collective-permute-start.29 = (bf16[256,1024]{1,0:T(8,128)(2,1)S(1)}, bf16[256,1024]{1,0:T(8,128)(2,1)S(1)}, u32[]{:S(2)}, u32[]{:S(2)}) collective-permute-start(bf16[256,1024]{1,0:T(8,128)(2,1)S(1)} %get-tuple-element.149), channel_id=1, source_target_pairs={{0,96},{8,104},{16,112},{24,120},{32,0},{40,8},{48,16},{56,24},{64... | collective-permute-start | bytes 1572872 | tf_op jit(solution)/shard_map/ppermute | solution.py:50
  145.8 2.5 %collective-permute-done.24.refs_5_ = bf16[128,1024]{1,0:T(8,128)(2,1)S(1)} collective-permute-done((bf16[128,1024]{1,0:T(8,128)(2,1)S(1)}, bf16[128,1024]{1,0:T(8,128)(2,1)S(1)}, u32[]{:S(2)}, u32[]{:S(2)}) %collective-permute-start.24) | collective-permute-done | bytes 262176 | tf_op jit(solution)/shard_map/ppermute | solution.py:50
  148.3 7.6 %attend_back.5 = (bf16[512,1024]{1,0:T(8,128)(2,1)}, f32[1024,128]{1,0:T(8,128)S(1)}, f32[1024,128]{1,0:T(8,128)S(1)}) custom-call(s32[24]{0:T(128)S(1)} %concatenate.17.meta_ref, bf16[512,1024]{1,0:T(8,128)(2,1)S(1)} %copy-done, bf16[512,1024]{1,0:T(8,128)(2,1)S(1)} %add_rows.5.g_ref, ...), custom_call_target="tpu_custom_call", output_to_operand_aliasing={{0}: (11, {})} | custom-call | flops 4026531840 | bytes 6291456 | tf_op jit(solution)/shard_map/attend_back/pallas_call | solution.py:226
  155.9 4.0 %collective-permute-start.26 = (bf16[512,256]{1,0:T(8,128)(2,1)S(1)}, bf16[512,256]{1,0:T(8,128)(2,1)S(1)}, u32[]{:S(2)}, u32[]{:S(2)}) collective-permute-start(bf16[512,256]{1,0:T(8,128)(2,1)S(1)} %pad_maximum_fusion.2), channel_id=1, source_target_pairs={{8,0},{16,8},{24,16},{32,24},{40,32},{48,40},{56,48},{64,56},{72,6... | collective-permute-start | bytes 786440 | tf_op jit(solution)/shard_map/ppermute | solution.py:64
  160.0 5.1 %collective-permute-done.26 = bf16[512,256]{1,0:T(8,128)(2,1)S(1)} collective-permute-done((bf16[512,256]{1,0:T(8,128)(2,1)S(1)}, bf16[512,256]{1,0:T(8,128)(2,1)S(1)}, u32[]{:S(2)}, u32[]{:S(2)}) %collective-permute-start.26) | collective-permute-done | bytes 262176 | tf_op jit(solution)/shard_map/ppermute | solution.py:64
  165.1 0.8 fusion
  165.9 1.5 add_rows.9
  (39 shorter events, 0.2 us)
Async XLA Ops:
  0.6 8.7 %copy-start.5 = (s32[8]{0:T(128)S(1)}, s32[8]{0:T(128)}, u32[]{:S(2)}) copy-start(s32[8]{0:T(128)} %constant.79.clone) | copy-start | bytes 100
  0.6 8.7 %copy-start.6 = (s32[8]{0:T(128)S(1)}, s32[8]{0:T(128)}, u32[]{:S(2)}) copy-start(s32[8]{0:T(128)} %constant.80.clone) | copy-start | bytes 100
  0.7 8.7 %copy-start.7 = (s32[8]{0:T(128)S(1)}, s32[8]{0:T(128)}, u32[]{:S(2)}) copy-start(s32[8]{0:T(128)} %constant.81.clone) | copy-start | bytes 100
  0.7 3.7 %copy-start.2 = (bf16[512,128]{1,0:T(8,128)(2,1)S(1)}, bf16[512,128]{1,0:T(8,128)(2,1)}, u32[]{:S(2)}) copy-start(bf16[512,128]{1,0:T(8,128)(2,1)} %k_ref.7) | copy-start | bytes 393220
  0.7 3.7 %copy-start.1 = (bf16[512,128]{1,0:T(8,128)(2,1)S(1)}, bf16[512,128]{1,0:T(8,128)(2,1)}, u32[]{:S(2)}) copy-start(bf16[512,128]{1,0:T(8,128)(2,1)} %v_ref.7) | copy-start | bytes 393220
  0.7 16.1 %copy-start.4 = (bf16[512,1024]{1,0:T(8,128)(2,1)S(1)}, bf16[512,1024]{1,0:T(8,128)(2,1)}, u32[]{:S(2)}) copy-start(bf16[512,1024]{1,0:T(8,128)(2,1)} %refs_8_) | copy-start | bytes 3145732
  0.7 19.8 %copy-start = (bf16[512,1024]{1,0:T(8,128)(2,1)S(1)}, bf16[512,1024]{1,0:T(8,128)(2,1)}, u32[]{:S(2)}) copy-start(bf16[512,1024]{1,0:T(8,128)(2,1)} %q_ref.6) | copy-start | bytes 3145732
  0.7 19.8 %copy-start.3 = (s32[8192]{0:T(1024)S(1)}, s32[8192]{0:T(1024)}, u32[]{:S(2)}) copy-start(s32[8192]{0:T(1024)} %param.15) | copy-start | bytes 98308
  3.0 9.6 %collective-permute-start = (bf16[512,512]{1,0:T(8,128)(2,1)}, bf16[512,512]{1,0:T(8,128)(2,1)}, u32[]{:S(2)}, u32[]{:S(2)}) collective-permute-start(bf16[512,512]{1,0:T(8,128)(2,1)} %get-tuple-element.153), channel_id=1, source_target_pairs={{0,8},{8,0},{16,24},{24,16},{32,40},{40,32},{48,56},{56,48},{64,72... | collective-permute-start | bytes 1572872 | tf_op jit(solution)/shard_map/ppermute | solution.py:50
  4.4 8.1 %collective-permute-start.1 = (bf16[512,256]{1,0:T(8,128)(2,1)S(1)}, bf16[512,256]{1,0:T(8,128)(2,1)S(1)}, u32[]{:S(2)}, u32[]{:S(2)}) collective-permute-start(bf16[512,256]{1,0:T(8,128)(2,1)S(1)} %pad_maximum_fusion.1), channel_id=1, source_target_pairs={{0,8},{8,16},{16,24},{24,32},{32,40},{40,48},{48,56},{56,64},{64,7... | collective-permute-start | bytes 786440 | tf_op jit(solution)/shard_map/ppermute | solution.py:64
  13.6 22.4 %collective-permute-start.2 = (bf16[1024,512]{1,0:T(8,128)(2,1)S(1)}, bf16[1024,512]{1,0:T(8,128)(2,1)S(1)}, u32[]{:S(2)}, u32[]{:S(2)}) collective-permute-start(bf16[1024,512]{1,0:T(8,128)(2,1)S(1)} %pad_maximum_fusion.refs_0_), channel_id=1, source_target_pairs={{0,1},{1,2},{2,3},{3,0},{4,5},{5,6},{6,7},{7,4},{8,9},{9,10},{10,1... | collective-permute-start | bytes 3145736 | tf_op jit(solution)/shard_map/ppermute | solution.py:58
  14.9 21.5 %collective-permute-start.3 = (bf16[1024,512]{1,0:T(8,128)(2,1)S(1)}, bf16[1024,512]{1,0:T(8,128)(2,1)S(1)}, u32[]{:S(2)}, u32[]{:S(2)}) collective-permute-start(bf16[1024,512]{1,0:T(8,128)(2,1)S(1)} %pad_maximum_fusion.refs_0_), channel_id=1, source_target_pairs={{0,3},{1,0},{2,1},{3,2},{4,7},{5,4},{6,5},{7,6},{8,11},{9,8},{10,9... | collective-permute-start | bytes 3145736 | tf_op jit(solution)/shard_map/ppermute | solution.py:58
  16.4 21.7 %collective-permute-start.4 = (bf16[1024,512]{1,0:T(8,128)(2,1)S(1)}, bf16[1024,512]{1,0:T(8,128)(2,1)S(1)}, u32[]{:S(2)}, u32[]{:S(2)}) collective-permute-start(bf16[1024,512]{1,0:T(8,128)(2,1)S(1)} %pad_maximum_fusion.refs_0_), channel_id=1, source_target_pairs={{0,4},{1,5},{2,6},{3,7},{4,0},{5,1},{6,2},{7,3},{8,12},{9,13},{10,... | collective-permute-start | bytes 3145736 | tf_op jit(solution)/shard_map/ppermute | solution.py:58
  16.8 25.6 %collective-permute-start.10 = (bf16[512,1024]{1,0:T(8,128)(2,1)S(1)}, bf16[512,1024]{1,0:T(8,128)(2,1)S(1)}, u32[]{:S(2)}, u32[]{:S(2)}) collective-permute-start(bf16[512,1024]{1,0:T(8,128)(2,1)S(1)} %copy-done.4), channel_id=1, source_target_pairs={{0,32},{8,40},{16,48},{24,56},{32,64},{40,72},{48,80},{56,88},{64,... | collective-permute-start | bytes 3145736 | tf_op jit(solution)/shard_map/ppermute | solution.py:50
  18.4 23.9 %collective-permute-start.11 = (bf16[512,1024]{1,0:T(8,128)(2,1)S(1)}, bf16[512,1024]{1,0:T(8,128)(2,1)S(1)}, u32[]{:S(2)}, u32[]{:S(2)}) collective-permute-start(bf16[512,1024]{1,0:T(8,128)(2,1)S(1)} %copy-done.4), channel_id=1, source_target_pairs={{0,96},{8,104},{16,112},{24,120},{32,0},{40,8},{48,16},{56,24},{64... | collective-permute-start | bytes 3145736 | tf_op jit(solution)/shard_map/ppermute | solution.py:50
  38.1 10.2 %collective-permute-start.7 = (bf16[512,1024]{1,0:T(8,128)(2,1)S(1)}, bf16[512,1024]{1,0:T(8,128)(2,1)S(1)}, u32[]{:S(2)}, u32[]{:S(2)}) collective-permute-start(bf16[512,1024]{1,0:T(8,128)(2,1)S(1)} %get-tuple-element.86), channel_id=1, source_target_pairs={{0,8},{8,0},{16,24},{24,16},{32,40},{40,32},{48,56},{56,48},{64,72... | collective-permute-start | bytes 3145736 | tf_op jit(solution)/shard_map/ppermute | solution.py:50
  39.7 25.9 %collective-permute-start.5 = (bf16[1024,512]{1,0:T(8,128)(2,1)S(1)}, bf16[1024,512]{1,0:T(8,128)(2,1)S(1)}, u32[]{:S(2)}, u32[]{:S(2)}) collective-permute-start(bf16[1024,512]{1,0:T(8,128)(2,1)S(1)} %collective-permute-done.4.refs_3_), channel_id=1, source_target_pairs={{0,1},{1,2},{2,3},{3,0},{4,5},{5,6},{6,7},{7,4},{8,9},{9,10},{10,1... | collective-permute-start | bytes 3145736 | tf_op jit(solution)/shard_map/ppermute | solution.py:58
  39.7 25.9 %collective-permute-start.6 = (bf16[1024,512]{1,0:T(8,128)(2,1)S(1)}, bf16[1024,512]{1,0:T(8,128)(2,1)S(1)}, u32[]{:S(2)}, u32[]{:S(2)}) collective-permute-start(bf16[1024,512]{1,0:T(8,128)(2,1)S(1)} %collective-permute-done.4.refs_3_), channel_id=1, source_target_pairs={{0,3},{1,0},{2,1},{3,2},{4,7},{5,4},{6,5},{7,6},{8,11},{9,8},{10,9... | collective-permute-start | bytes 3145736 | tf_op jit(solution)/shard_map/ppermute | solution.py:58
  42.4 29.0 %collective-permute-start.12 = (bf16[512,1024]{1,0:T(8,128)(2,1)S(1)}, bf16[512,1024]{1,0:T(8,128)(2,1)S(1)}, u32[]{:S(2)}, u32[]{:S(2)}) collective-permute-start(bf16[512,1024]{1,0:T(8,128)(2,1)S(1)} %collective-permute-done.10.refs_9_), channel_id=1, source_target_pairs={{0,32},{8,40},{16,48},{24,56},{32,64},{40,72},{48,80},{56,88},{64,... | collective-permute-start | bytes 3145736 | tf_op jit(solution)/shard_map/ppermute | solution.py:50
  46.3 25.3 %collective-permute-start.13 = (bf16[512,1024]{1,0:T(8,128)(2,1)S(1)}, bf16[512,1024]{1,0:T(8,128)(2,1)S(1)}, u32[]{:S(2)}, u32[]{:S(2)}) collective-permute-start(bf16[512,1024]{1,0:T(8,128)(2,1)S(1)} %copy-done.4), channel_id=1, source_target_pairs={{0,16},{8,24},{16,0},{24,8},{32,48},{40,56},{48,32},{56,40},{64,80... | collective-permute-start | bytes 3145736 | tf_op jit(solution)/shard_map/ppermute | solution.py:50
  48.2 39.9 %collective-permute-start.9 = (bf16[1024,512]{1,0:T(8,128)(2,1)S(1)}, bf16[1024,512]{1,0:T(8,128)(2,1)S(1)}, u32[]{:S(2)}, u32[]{:S(2)}) collective-permute-start(bf16[1024,512]{1,0:T(8,128)(2,1)S(1)} %collective-permute-done.2.refs_1_), channel_id=1, source_target_pairs={{0,1},{1,2},{2,3},{3,0},{4,5},{5,6},{6,7},{7,4},{8,9},{9,10},{10,1... | collective-permute-start | bytes 3145736 | tf_op jit(solution)/shard_map/ppermute | solution.py:58
  65.6 25.3 %collective-permute-start.8 = (bf16[1024,512]{1,0:T(8,128)(2,1)S(1)}, bf16[1024,512]{1,0:T(8,128)(2,1)S(1)}, u32[]{:S(2)}, u32[]{:S(2)}) collective-permute-start(bf16[1024,512]{1,0:T(8,128)(2,1)S(1)} %collective-permute-done.6.refs_1_.refs_5_), channel_id=1, source_target_pairs={{0,3},{1,0},{2,1},{3,2},{4,7},{5,4},{6,5},{7,6},{8,11},{9,8},{10,9... | collective-permute-start | bytes 3145736 | tf_op jit(solution)/shard_map/ppermute | solution.py:58
  71.6 24.1 %collective-permute-start.14 = (bf16[512,1024]{1,0:T(8,128)(2,1)S(1)}, bf16[512,1024]{1,0:T(8,128)(2,1)S(1)}, u32[]{:S(2)}, u32[]{:S(2)}) collective-permute-start(bf16[512,1024]{1,0:T(8,128)(2,1)S(1)} %collective-permute-done.13.refs_11_), channel_id=1, source_target_pairs={{0,32},{8,40},{16,48},{24,56},{32,64},{40,72},{48,80},{56,88},{64,... | collective-permute-start | bytes 3145736 | tf_op jit(solution)/shard_map/ppermute | solution.py:50
  73.3 22.6 %collective-permute-start.15 = (bf16[512,1024]{1,0:T(8,128)(2,1)S(1)}, bf16[512,1024]{1,0:T(8,128)(2,1)S(1)}, u32[]{:S(2)}, u32[]{:S(2)}) collective-permute-start(bf16[512,1024]{1,0:T(8,128)(2,1)S(1)} %collective-permute-done.13.refs_11_), channel_id=1, source_target_pairs={{0,96},{8,104},{16,112},{24,120},{32,0},{40,8},{48,16},{56,24},{64... | collective-permute-start | bytes 3145736 | tf_op jit(solution)/shard_map/ppermute | solution.py:50
  74.3 23.9 %collective-permute-start.16 = (bf16[512,1024]{1,0:T(8,128)(2,1)S(1)}, bf16[512,1024]{1,0:T(8,128)(2,1)S(1)}, u32[]{:S(2)}, u32[]{:S(2)}) collective-permute-start(bf16[512,1024]{1,0:T(8,128)(2,1)S(1)} %collective-permute-done.12.refs_15_), channel_id=1, source_target_pairs={{0,16},{8,24},{16,0},{24,8},{32,48},{40,56},{48,32},{56,40},{64,80... | collective-permute-start | bytes 3145736 | tf_op jit(solution)/shard_map/ppermute | solution.py:50
  98.2 32.9 %collective-permute-start.22 = (bf16[640,1024]{1,0:T(8,128)(2,1)S(1)}, bf16[640,1024]{1,0:T(8,128)(2,1)S(1)}, u32[]{:S(2)}, u32[]{:S(2)}) collective-permute-start(bf16[640,1024]{1,0:T(8,128)(2,1)S(1)} %get-tuple-element.98), channel_id=1, source_target_pairs={{0,32},{8,40},{16,48},{24,56},{32,64},{40,72},{48,80},{56,88},{64,... | collective-permute-start | bytes 3932168 | tf_op jit(solution)/shard_map/ppermute | solution.py:50
  99.1 29.0 %collective-permute-start.19 = (bf16[512,1024]{1,0:T(8,128)(2,1)S(1)}, bf16[512,1024]{1,0:T(8,128)(2,1)S(1)}, u32[]{:S(2)}, u32[]{:S(2)}) collective-permute-start(bf16[512,1024]{1,0:T(8,128)(2,1)S(1)} %get-tuple-element.111), channel_id=1, source_target_pairs={{0,16},{8,24},{16,0},{24,8},{32,48},{40,56},{48,32},{56,40},{64,80... | collective-permute-start | bytes 3145736 | tf_op jit(solution)/shard_map/ppermute | solution.py:50
  100.6 30.4 %collective-permute-start.23 = (bf16[640,1024]{1,0:T(8,128)(2,1)S(1)}, bf16[640,1024]{1,0:T(8,128)(2,1)S(1)}, u32[]{:S(2)}, u32[]{:S(2)}) collective-permute-start(bf16[640,1024]{1,0:T(8,128)(2,1)S(1)} %get-tuple-element.122), channel_id=1, source_target_pairs={{0,96},{8,104},{16,112},{24,120},{32,0},{40,8},{48,16},{56,24},{64... | collective-permute-start | bytes 3932168 | tf_op jit(solution)/shard_map/ppermute | solution.py:50
  115.3 7.0 %collective-permute-start.17 = (bf16[256,1024]{1,0:T(8,128)(2,1)S(1)}, bf16[256,1024]{1,0:T(8,128)(2,1)S(1)}, u32[]{:S(2)}, u32[]{:S(2)}) collective-permute-start(bf16[256,1024]{1,0:T(8,128)(2,1)S(1)} %get-tuple-element.105), channel_id=1, source_target_pairs={{0,8},{8,0},{16,24},{24,16},{32,40},{40,32},{48,56},{56,48},{64,72... | collective-permute-start | bytes 1572872 | tf_op jit(solution)/shard_map/ppermute | solution.py:50
  119.4 2.9 %collective-permute-start.18 = (bf16[256,1024]{1,0:T(8,128)(2,1)S(1)}, bf16[256,1024]{1,0:T(8,128)(2,1)S(1)}, u32[]{:S(2)}, u32[]{:S(2)}) collective-permute-start(bf16[256,1024]{1,0:T(8,128)(2,1)S(1)} %get-tuple-element.106), channel_id=1, source_target_pairs={{0,8},{8,0},{16,24},{24,16},{32,40},{40,32},{48,56},{56,48},{64,72... | collective-permute-start | bytes 1572872 | tf_op jit(solution)/shard_map/ppermute | solution.py:50
  128.3 14.5 %collective-permute-start.20 = (bf16[256,1024]{1,0:T(8,128)(2,1)S(1)}, bf16[256,1024]{1,0:T(8,128)(2,1)S(1)}, u32[]{:S(2)}, u32[]{:S(2)}) collective-permute-start(bf16[256,1024]{1,0:T(8,128)(2,1)S(1)} %get-tuple-element.116), channel_id=1, source_target_pairs={{0,32},{8,40},{16,48},{24,56},{32,64},{40,72},{48,80},{56,88},{64,... | collective-permute-start | bytes 1572872 | tf_op jit(solution)/shard_map/ppermute | solution.py:50
  128.4 14.4 %collective-permute-start.21 = (bf16[256,1024]{1,0:T(8,128)(2,1)S(1)}, bf16[256,1024]{1,0:T(8,128)(2,1)S(1)}, u32[]{:S(2)}, u32[]{:S(2)}) collective-permute-start(bf16[256,1024]{1,0:T(8,128)(2,1)S(1)} %get-tuple-element.117), channel_id=1, source_target_pairs={{0,96},{8,104},{16,112},{24,120},{32,0},{40,8},{48,16},{56,24},{64... | collective-permute-start | bytes 1572872 | tf_op jit(solution)/shard_map/ppermute | solution.py:50
  131.4 34.5 %collective-permute-start.27 = (bf16[512,1024]{1,0:T(8,128)(2,1)S(1)}, bf16[512,1024]{1,0:T(8,128)(2,1)S(1)}, u32[]{:S(2)}, u32[]{:S(2)}) collective-permute-start(bf16[512,1024]{1,0:T(8,128)(2,1)S(1)} %add_rows.7), channel_id=1, source_target_pairs={{0,16},{8,24},{16,0},{24,8},{32,48},{40,56},{48,32},{56,40},{64,80... | collective-permute-start | bytes 3145736 | tf_op jit(solution)/shard_map/ppermute | solution.py:50
  132.6 15.6 %collective-permute-start.24 = (bf16[128,1024]{1,0:T(8,128)(2,1)S(1)}, bf16[128,1024]{1,0:T(8,128)(2,1)S(1)}, u32[]{:S(2)}, u32[]{:S(2)}) collective-permute-start(bf16[128,1024]{1,0:T(8,128)(2,1)S(1)} %get-tuple-element.136), channel_id=1, source_target_pairs={{0,32},{8,40},{16,48},{24,56},{32,64},{40,72},{48,80},{56,88},{64,... | collective-permute-start | bytes 786440 | tf_op jit(solution)/shard_map/ppermute | solution.py:50
  132.6 15.6 %collective-permute-start.25 = (bf16[128,1024]{1,0:T(8,128)(2,1)S(1)}, bf16[128,1024]{1,0:T(8,128)(2,1)S(1)}, u32[]{:S(2)}, u32[]{:S(2)}) collective-permute-start(bf16[128,1024]{1,0:T(8,128)(2,1)S(1)} %get-tuple-element.137), channel_id=1, source_target_pairs={{0,96},{8,104},{16,112},{24,120},{32,0},{40,8},{48,16},{56,24},{64... | collective-permute-start | bytes 786440 | tf_op jit(solution)/shard_map/ppermute | solution.py:50
  143.1 22.9 %collective-permute-start.28 = (bf16[256,1024]{1,0:T(8,128)(2,1)S(1)}, bf16[256,1024]{1,0:T(8,128)(2,1)S(1)}, u32[]{:S(2)}, u32[]{:S(2)}) collective-permute-start(bf16[256,1024]{1,0:T(8,128)(2,1)S(1)} %get-tuple-element.141), channel_id=1, source_target_pairs={{0,32},{8,40},{16,48},{24,56},{32,64},{40,72},{48,80},{56,88},{64,... | collective-permute-start | bytes 1572872 | tf_op jit(solution)/shard_map/ppermute | solution.py:50
  143.1 22.8 %collective-permute-start.29 = (bf16[256,1024]{1,0:T(8,128)(2,1)S(1)}, bf16[256,1024]{1,0:T(8,128)(2,1)S(1)}, u32[]{:S(2)}, u32[]{:S(2)}) collective-permute-start(bf16[256,1024]{1,0:T(8,128)(2,1)S(1)} %get-tuple-element.149), channel_id=1, source_target_pairs={{0,96},{8,104},{16,112},{24,120},{32,0},{40,8},{48,16},{56,24},{64... | collective-permute-start | bytes 1572872 | tf_op jit(solution)/shard_map/ppermute | solution.py:50
  155.9 9.2 %collective-permute-start.26 = (bf16[512,256]{1,0:T(8,128)(2,1)S(1)}, bf16[512,256]{1,0:T(8,128)(2,1)S(1)}, u32[]{:S(2)}, u32[]{:S(2)}) collective-permute-start(bf16[512,256]{1,0:T(8,128)(2,1)S(1)} %pad_maximum_fusion.2), channel_id=1, source_target_pairs={{8,0},{16,8},{24,16},{32,24},{40,32},{48,40},{56,48},{64,56},{72,6... | collective-permute-start | bytes 786440 | tf_op jit(solution)/shard_map/ppermute | solution.py:64

commit v10 on v9

--- a/solution.py
+++ b/solution.py
@@ -161,7 +161,7 @@
         ],
         compiler_params=params(16),
         cost_estimate=pl.CostEstimate(
-            flops=heads * 4 * 2 * 2 * count * count * HD,
+            flops=heads * 64 * 2 * 2 * count * count * HD,
             bytes_accessed=8 * 2**20,
             transcendentals=heads * 2 * count * count,
         ),
@@ -521,11 +521,11 @@
     g_keep = lax.dynamic_slice_in_dim(output_grad, k * half_d, half_d, 1)
     g_give = lax.dynamic_slice_in_dim(output_grad, (1 - k) * half_d, half_d, 1)
     kv_earlier = passed_along(jnp.concatenate([key_rows, value_rows], 1), "row", 1)
-    g_got, kv_earlier, meta = tied((move_row(g_give, dk=1), kv_earlier, meta))
+    g_got, meta = tied((move_row(g_give, dk=1), meta))
     g0 = jnp.concatenate([g_keep, g_got], 0)
     segments = segment_ids.reshape(-1, LANES)
 
-    (out_proj,) = tied((out_proj,), g0)
+    out_proj, kv_earlier = tied((out_proj, kv_earlier), g0)
     gxm = move_col(g0, dx=1)
     gxp = move_col(g0, dx=-1)
     gy = move_col(g0, dyl=1)

time: 168 us -> 164 us (0.976)
  waiting for transfers between devices: 38.5 us -> 35.8 us
    ppermute x7, waiting for transfers between devices: 20.8 us -> 24.2 us  [move_col(): return lax.ppermute(value, 'col', pairs)]
    ppermute x2, waiting for transfers between devices: 8.24 us -> 5.16 us  [passed_along(): lax.ppermute(value, axis, [(source, source + steps) for source in range(f...]
    ppermute x21, waiting for transfers between devices: 9.47 us -> 6.48 us  [move_row(): return lax.ppermute(value, 'row', pairs)]
  transfers between devices with their start and end apart: 30 -> 30, of which waited for: 13 -> 12; matrix products, arithmetic and copies ran while one was open for 1% -> 1% of each run, Pallas kernels for 42% -> 43%
where the time goes in v10:
time: 164 us
  Pallas kernels  71.1 us (43%)
  starting transfers between devices  51.1 us (31%)
  waiting for transfers between devices  35.8 us (22%)
  local copies, waits for them, and re-layouts  2.52 us (2%)
  other arithmetic  1.97 us (1%)
    ppermute x21, starting transfers between devices, move_row(): return lax.ppermute(value, 'row', pairs)  34 us
    ppermute x7, waiting for transfers between devices, move_col(): return lax.ppermute(value, 'col', pairs)  24.2 us
    pallas_call x3, Pallas kernels, attend_back(): pl.pallas_call(functools.partial(bwd_kernel, len(earlier), last), grid_sp...  20.6 us
    pallas_call x4, Pallas kernels, project(): pl.pallas_call(functools.partial(proj_kernel, tuple(slots), held, plan),...  17.7 us
    pallas_call x1, Pallas kernels, attend(): pl.pallas_call(fwd_kernel, grid_spec=pltpu.PrefetchScalarGridSpec(num_sca...  14.9 us
    pallas_call x1, Pallas kernels, attn_grad_part(): pl.pallas_call(kernel, grid_spec=pltpu.PrefetchScalarGridSpec(num_scalar_...  12.6 us
    ppermute x2, starting transfers between devices, passed_along(): lax.ppermute(value, axis, [(source, source + steps) for source in range(f...  8.83 us
    ppermute x7, starting transfers between devices, move_col(): return lax.ppermute(value, 'col', pairs)  8.25 us
  transfers between devices with their start and end apart: 30, of which 12 were waited for; matrix products, arithmetic and copies ran while one was open for 1% of the time, Pallas kernels for 43%

profile of v10, /device:TPU:1, one launch (start us, length us, event | category | flops | bytes accessed | tf_op | source)
XLA Modules:
  0.0 163.5 jit_solution(4825365539116208739)
XLA Ops:
  0.6 0.0 copy-start.5
  0.7 0.0 copy-start.7
  0.7 2.2 %constant_dynamic-slice_fusion = (bf16[512,512]{1,0:T(8,128)(2,1)S(1)}, bf16[512,512]{1,0:T(8,128)(2,1)}) fusion(bf16[512,1024]{1,0:T(8,128)(2,1)} %param.13, s32[]{:T(128)S(6)} %select_n.38, s32[]{:T(128)S(6)} %select_n.32), kind=kLoop, calls=%fused_computation.13 | loop fusion | bytes 2097160 | tf_op jit(solution)/shard_map/dynamic_slice | solution.py:521
  3.0 1.4 collective-permute-start
  4.4 4.8 %collective-permute-start.4 = (bf16[512,256]{1,0:T(8,128)(2,1)S(1)}, bf16[512,256]{1,0:T(8,128)(2,1)S(1)}, u32[]{:S(2)}, u32[]{:S(2)}) collective-permute-start(bf16[512,256]{1,0:T(8,128)(2,1)S(1)} %pad_maximum_fusion.1), channel_id=1, source_target_pairs={{0,8},{8,16},{16,24},{24,32},{32,40},{40,48},{48,56},{56,64},{64,7... | collective-permute-start | bytes 786440 | tf_op jit(solution)/shard_map/ppermute | solution.py:64
  9.3 0.1 concatenate.16.meta_ref
  9.4 1.1 pad_maximum_fusion.refs_0_
  10.6 1.3 collective-permute-start.1
  11.8 1.5 collective-permute-start.2
  13.3 0.4 collective-permute-start.3
  13.7 1.6 %collective-permute-start.10 = (bf16[512,1024]{1,0:T(8,128)(2,1)S(1)}, bf16[512,1024]{1,0:T(8,128)(2,1)S(1)}, u32[]{:S(2)}, u32[]{:S(2)}) collective-permute-start(bf16[512,1024]{1,0:T(8,128)(2,1)S(1)} %copy-done.4), channel_id=1, source_target_pairs={{0,32},{8,40},{16,48},{24,56},{32,64},{40,72},{48,80},{56,88},{64,... | collective-permute-start | bytes 3145736 | tf_op jit(solution)/shard_map/ppermute | solution.py:50
  15.3 2.2 %collective-permute-start.11 = (bf16[512,1024]{1,0:T(8,128)(2,1)S(1)}, bf16[512,1024]{1,0:T(8,128)(2,1)S(1)}, u32[]{:S(2)}, u32[]{:S(2)}) collective-permute-start(bf16[512,1024]{1,0:T(8,128)(2,1)S(1)} %copy-done.4), channel_id=1, source_target_pairs={{0,96},{8,104},{16,112},{24,120},{32,0},{40,8},{48,16},{56,24},{64... | collective-permute-start | bytes 3145736 | tf_op jit(solution)/shard_map/ppermute | solution.py:50
  17.5 14.9 %attend.1 = (bf16[512,1024]{1,0:T(8,128)(2,1)S(1)}, f32[8,1,512]{2,1,0:T(1,128)S(1)}, f32[8,1,512]{2,1,0:T(1,128)S(1)}) custom-call(s32[24]{0:T(128)S(1)} %concatenate.16.meta_ref, bf16[512,1024]{1,0:T(8,128)(2,1)S(1)} %copy-done, bf16[512,256]{1,0:T(8,128)(2,1)S(1)} %collective-permute-done.4.kv_ref, bf16[512,128]{1,0:T(8,128)(2,1)S(1)} %copy-done.2, ...), custom_call_target="tpu_custom_call" | custom-call | flops 68719476736 | bytes 8388608 | tf_op jit(solution)/shard_map/attend/pallas_call | solution.py:148
  32.5 2.7 %collective-permute-done.1.refs_1_ = bf16[1024,512]{1,0:T(8,128)(2,1)S(1)} collective-permute-done((bf16[1024,512]{1,0:T(8,128)(2,1)S(1)}, bf16[1024,512]{1,0:T(8,128)(2,1)S(1)}, u32[]{:S(2)}, u32[]{:S(2)}) %collective-permute-start.1) | collective-permute-done | bytes 1048608 | tf_op jit(solution)/shard_map/ppermute | solution.py:58
  35.1 0.4 collective-permute-done.2.refs_2_
  35.5 1.7 %collective-permute-done.3.refs_3_ = bf16[1024,512]{1,0:T(8,128)(2,1)S(1)} collective-permute-done((bf16[1024,512]{1,0:T(8,128)(2,1)S(1)}, bf16[1024,512]{1,0:T(8,128)(2,1)S(1)}, u32[]{:S(2)}, u32[]{:S(2)}) %collective-permute-start.3) | collective-permute-done | bytes 1048608 | tf_op jit(solution)/shard_map/ppermute | solution.py:58
  37.1 0.2 collective-permute-start.5
  37.3 2.5 %collective-permute-start.6 = (bf16[1024,512]{1,0:T(8,128)(2,1)S(1)}, bf16[1024,512]{1,0:T(8,128)(2,1)S(1)}, u32[]{:S(2)}, u32[]{:S(2)}) collective-permute-start(bf16[1024,512]{1,0:T(8,128)(2,1)S(1)} %collective-permute-done.3.refs_3_), channel_id=1, source_target_pairs={{0,3},{1,0},{2,1},{3,2},{4,7},{5,4},{6,5},{7,6},{8,11},{9,8},{10,9... | collective-permute-start | bytes 3145736 | tf_op jit(solution)/shard_map/ppermute | solution.py:58
  39.8 0.3 collective-permute-done.10.refs_9_
  40.1 1.4 collective-permute-start.12
  41.5 3.1 %collective-permute-start.13 = (bf16[512,1024]{1,0:T(8,128)(2,1)S(1)}, bf16[512,1024]{1,0:T(8,128)(2,1)S(1)}, u32[]{:S(2)}, u32[]{:S(2)}) collective-permute-start(bf16[512,1024]{1,0:T(8,128)(2,1)S(1)} %copy-done.4), channel_id=1, source_target_pairs={{0,16},{8,24},{16,0},{24,8},{32,48},{40,56},{48,32},{56,40},{64,80... | collective-permute-start | bytes 3145736 | tf_op jit(solution)/shard_map/ppermute | solution.py:50
  44.6 0.1 constant_dynamic-update-slice_fusion.1
  44.7 0.1 collective-permute-start.9
  44.8 0.1 constant_dynamic-update-slice_fusion.refs_4_.refs_2_.refs_1_
  44.9 6.8 %project.4.refs_3_ = bf16[2,64,256,1024]{3,2,1,0:T(8,128)(2,1)} custom-call(s32[24]{0:T(128)S(1)} %concatenate.16.meta_ref, bf16[1024,512]{1,0:T(8,128)(2,1)S(1)} %pad_maximum_fusion.refs_0_, bf16[1024,512]{1,0:T(8,128)(2,1)S(1)} %collective-permute-done.1.refs_1_, bf16[1024,512]{1,0:T(8,128)(2,1)S(1)} %collective-permute-done.2.refs_2_, ...), custom_call_target="tpu_custom_call" | custom-call | flops 4294967296 | bytes 10485760 | tf_op jit(solution)/shard_map/project/pallas_call | solution.py:324
  51.6 10.9 %collective-permute-done.5.refs_0_.refs_4_ = bf16[1024,512]{1,0:T(8,128)(2,1)S(1)} collective-permute-done((bf16[1024,512]{1,0:T(8,128)(2,1)S(1)}, bf16[1024,512]{1,0:T(8,128)(2,1)S(1)}, u32[]{:S(2)}, u32[]{:S(2)}) %collective-permute-start.5) | collective-permute-done | bytes 1048608 | tf_op jit(solution)/shard_map/ppermute | solution.py:58
  62.6 2.4 %collective-permute-start.8 = (bf16[1024,512]{1,0:T(8,128)(2,1)S(1)}, bf16[1024,512]{1,0:T(8,128)(2,1)S(1)}, u32[]{:S(2)}, u32[]{:S(2)}) collective-permute-start(bf16[1024,512]{1,0:T(8,128)(2,1)S(1)} %collective-permute-done.6.refs_1_.refs_5_), channel_id=1, source_target_pairs={{0,3},{1,0},{2,1},{3,2},{4,7},{5,4},{6,5},{7,6},{8,11},{9,8},{10,9... | collective-permute-start | bytes 3145736 | tf_op jit(solution)/shard_map/ppermute | solution.py:58
  64.9 1.2 collective-permute-done.12.refs_15_
  66.1 0.5 collective-permute-done.13.refs_11_
  66.6 1.9 %collective-permute-start.14 = (bf16[512,1024]{1,0:T(8,128)(2,1)S(1)}, bf16[512,1024]{1,0:T(8,128)(2,1)S(1)}, u32[]{:S(2)}, u32[]{:S(2)}) collective-permute-start(bf16[512,1024]{1,0:T(8,128)(2,1)S(1)} %collective-permute-done.13.refs_11_), channel_id=1, source_target_pairs={{0,32},{8,40},{16,48},{24,56},{32,64},{40,72},{48,80},{56,88},{64,... | collective-permute-start | bytes 3145736 | tf_op jit(solution)/shard_map/ppermute | solution.py:50
  68.5 0.8 collective-permute-start.15
  69.3 3.0 %collective-permute-start.16 = (bf16[512,1024]{1,0:T(8,128)(2,1)S(1)}, bf16[512,1024]{1,0:T(8,128)(2,1)S(1)}, u32[]{:S(2)}, u32[]{:S(2)}) collective-permute-start(bf16[512,1024]{1,0:T(8,128)(2,1)S(1)} %collective-permute-done.12.refs_15_), channel_id=1, source_target_pairs={{0,16},{8,24},{16,0},{24,8},{32,48},{40,56},{48,32},{56,40},{64,80... | collective-permute-start | bytes 3145736 | tf_op jit(solution)/shard_map/ppermute | solution.py:50
  72.3 4.2 %project.5.refs_2_ = bf16[2,64,256,1024]{3,2,1,0:T(8,128)(2,1)} custom-call(s32[24]{0:T(128)S(1)} %concatenate.16.meta_ref, bf16[1024,512]{1,0:T(8,128)(2,1)S(1)} %collective-permute-done.5.refs_0_.refs_4_, bf16[1024,512]{1,0:T(8,128)(2,1)S(1)} %collective-permute-done.6.refs_1_.refs_5_, ...), custom_call_target="tpu_custom_call", output_to_operand_aliasing={{}: (4, {})} | custom-call | flops 2147483648 | bytes 6291456 | tf_op jit(solution)/shard_map/project/pallas_call | solution.py:324
  76.5 8.6 %collective-permute-done.9.refs_0_.refs_6_ = bf16[1024,512]{1,0:T(8,128)(2,1)S(1)} collective-permute-done((bf16[1024,512]{1,0:T(8,128)(2,1)S(1)}, bf16[1024,512]{1,0:T(8,128)(2,1)S(1)}, u32[]{:S(2)}, u32[]{:S(2)}) %collective-permute-start.9) | collective-permute-done | bytes 1048608 | tf_op jit(solution)/shard_map/ppermute | solution.py:58
  85.0 2.8 %project.6.refs_2_ = bf16[2,64,256,1024]{3,2,1,0:T(8,128)(2,1)} custom-call(s32[24]{0:T(128)S(1)} %concatenate.16.meta_ref, bf16[1024,512]{1,0:T(8,128)(2,1)S(1)} %collective-permute-done.9.refs_0_.refs_6_, bf16[1024,1024]{1,0:T(8,128)(2,1)S(1)} %constant_dynamic-update-slice_fusion.refs_4_.refs_2_.refs_1_, ...), custom_call_target="tpu_custom_call", output_to_operand_aliasing={{}: (3, {})} | custom-call | flops 1073741824 | bytes 4194304 | tf_op jit(solution)/shard_map/project/pallas_call | solution.py:324
  87.9 3.9 %project.7 = (bf16[2,64,256,1024]{3,2,1,0:T(8,128)(2,1)}, bf16[512,1024]{1,0:T(8,128)(2,1)S(1)}, bf16[640,1024]{1,0:T(8,128)(2,1)S(1)}, bf16[640,1024]{1,0:T(8,1...) custom-call(s32[24]{0:T(128)S(1)} %concatenate.16.meta_ref, ...), custom_call_target="tpu_custom_call", output_to_operand_aliasing={{0}: (3, {})} | custom-call | flops 1073741824 | bytes 4194304 | tf_op jit(solution)/shard_map/project/pallas_call | solution.py:324
  91.8 1.0 collective-permute-done.16.refs_14_
  92.8 1.2 collective-permute-start.22
  94.0 3.0 %collective-permute-start.19 = (bf16[512,1024]{1,0:T(8,128)(2,1)S(1)}, bf16[512,1024]{1,0:T(8,128)(2,1)S(1)}, u32[]{:S(2)}, u32[]{:S(2)}) collective-permute-start(bf16[512,1024]{1,0:T(8,128)(2,1)S(1)} %get-tuple-element.111), channel_id=1, source_target_pairs={{0,16},{8,24},{16,0},{24,8},{32,48},{40,56},{48,32},{56,40},{64,80... | collective-permute-start | bytes 3145736 | tf_op jit(solution)/shard_map/ppermute | solution.py:50
  97.0 1.5 collective-permute-start.23
  98.5 12.6 %attn_grad.1 = (f32[512,1024]{1,0:T(8,128)S(1)}, bf16[256,1024]{1,0:T(8,128)(2,1)S(1)}, bf16[256,1024]{1,0:T(8,128)(2,1)S(1)}) custom-call(s32[24]{0:T(128)S(1)} %concatenate.16.meta_ref, bf16[1024,512]{1,0:T(8,128)(2,1)S(1)} %pad_maximum_fusion.refs_0_, bf16[1024,512]{1,0:T(8,128)(2,1)S(1)} %collective-permute-done.1.refs_1_, ...), custom_call_target="tpu_custom_call" | custom-call | flops 8589934592 | bytes 20971520 | tf_op jit(solution)/shard_map/attn_grad/pallas_call | solution.py:419
  111.1 4.5 %collective-permute-start.17 = (bf16[256,1024]{1,0:T(8,128)(2,1)S(1)}, bf16[256,1024]{1,0:T(8,128)(2,1)S(1)}, u32[]{:S(2)}, u32[]{:S(2)}) collective-permute-start(bf16[256,1024]{1,0:T(8,128)(2,1)S(1)} %get-tuple-element.105), channel_id=1, source_target_pairs={{0,8},{8,0},{16,24},{24,16},{32,40},{40,32},{48,56},{56,48},{64,72... | collective-permute-start | bytes 1572872 | tf_op jit(solution)/shard_map/ppermute | solution.py:50
  115.6 0.1 collective-permute-start.18
  115.7 2.8 %fetch.1 = (bf16[512,1024]{1,0:T(8,128)(2,1)S(1)}, bf16[512,1024]{1,0:T(8,128)(2,1)S(1)}, bf16[512,1024]{1,0:T(8,128)(2,1)S(1)}, bf16[512,1024]{1,0:T(8,128)(2,1)S(1)}) custom-call(s32[24]{0:T(128)S(1)} %concatenate.16.meta_ref, bf16[2,64,256,1024]{3,2,1,0:T(8,128)(2,1)} %get-tuple-element.109.buffer_ref), custom_call_target="tpu_custom_call" | custom-call | bytes 65536 | tf_op jit(solution)/shard_map/fetch/pallas_call | solution.py:466
  118.4 0.2 add_rows.5.g_ref
  118.6 5.5 %attend_back.3 = (bf16[512,1024]{1,0:T(8,128)(2,1)}, f32[1024,128]{1,0:T(8,128)S(1)}, f32[1024,128]{1,0:T(8,128)S(1)}) custom-call(s32[24]{0:T(128)S(1)} %concatenate.16.meta_ref, bf16[512,1024]{1,0:T(8,128)(2,1)S(1)} %copy-done, bf16[512,1024]{1,0:T(8,128)(2,1)S(1)} %add_rows.5.g_ref, bf16[512,256]{1,0:T(8,128)(2,1)S(1)} %collective-permute-done.4.kv_ref, ...), custom_call_target="tpu_custom_call" | custom-call | flops 1048576 | bytes 65536 | tf_op jit(solution)/shard_map/attend_back/pallas_call | solution.py:226
  124.2 0.2 add_rows.6
  124.4 0.1 collective-permute-start.20
  124.5 2.7 %collective-permute-start.21 = (bf16[256,1024]{1,0:T(8,128)(2,1)S(1)}, bf16[256,1024]{1,0:T(8,128)(2,1)S(1)}, u32[]{:S(2)}, u32[]{:S(2)}) collective-permute-start(bf16[256,1024]{1,0:T(8,128)(2,1)S(1)} %get-tuple-element.117), channel_id=1, source_target_pairs={{0,96},{8,104},{16,112},{24,120},{32,0},{40,8},{48,16},{56,24},{64... | collective-permute-start | bytes 1572872 | tf_op jit(solution)/shard_map/ppermute | solution.py:50
  127.2 0.4 add_rows.7
  127.5 0.1 collective-permute-start.27
  127.6 0.1 collective-permute-start.24
  127.7 2.7 %collective-permute-start.25 = (bf16[128,1024]{1,0:T(8,128)(2,1)S(1)}, bf16[128,1024]{1,0:T(8,128)(2,1)S(1)}, u32[]{:S(2)}, u32[]{:S(2)}) collective-permute-start(bf16[128,1024]{1,0:T(8,128)(2,1)S(1)} %get-tuple-element.137), channel_id=1, source_target_pairs={{0,96},{8,104},{16,112},{24,120},{32,0},{40,8},{48,16},{56,24},{64... | collective-permute-start | bytes 786440 | tf_op jit(solution)/shard_map/ppermute | solution.py:50
  130.4 7.5 %attend_back.4 = (bf16[512,1024]{1,0:T(8,128)(2,1)}, f32[1024,128]{1,0:T(8,128)S(1)}, f32[1024,128]{1,0:T(8,128)S(1)}) custom-call(s32[24]{0:T(128)S(1)} %concatenate.16.meta_ref, bf16[512,1024]{1,0:T(8,128)(2,1)S(1)} %copy-done, bf16[512,1024]{1,0:T(8,128)(2,1)S(1)} %add_rows.5.g_ref, ...), custom_call_target="tpu_custom_call", output_to_operand_aliasing={{0}: (11, {})} | custom-call | flops 4026531840 | bytes 6291456 | tf_op jit(solution)/shard_map/attend_back/pallas_call | solution.py:226
  137.9 0.9 collective-permute-done.20.refs_1_
  138.8 0.2 add_rows.8
  139.0 0.1 collective-permute-start.28
  139.1 2.7 %collective-permute-start.29 = (bf16[256,1024]{1,0:T(8,128)(2,1)S(1)}, bf16[256,1024]{1,0:T(8,128)(2,1)S(1)}, u32[]{:S(2)}, u32[]{:S(2)}) collective-permute-start(bf16[256,1024]{1,0:T(8,128)(2,1)S(1)} %get-tuple-element.149), channel_id=1, source_target_pairs={{0,96},{8,104},{16,112},{24,120},{32,0},{40,8},{48,16},{56,24},{64... | collective-permute-start | bytes 1572872 | tf_op jit(solution)/shard_map/ppermute | solution.py:50
  141.8 2.6 %collective-permute-done.24.refs_5_ = bf16[128,1024]{1,0:T(8,128)(2,1)S(1)} collective-permute-done((bf16[128,1024]{1,0:T(8,128)(2,1)S(1)}, bf16[128,1024]{1,0:T(8,128)(2,1)S(1)}, u32[]{:S(2)}, u32[]{:S(2)}) %collective-permute-start.24) | collective-permute-done | bytes 262176 | tf_op jit(solution)/shard_map/ppermute | solution.py:50
  144.4 7.6 %attend_back.5 = (bf16[512,1024]{1,0:T(8,128)(2,1)}, f32[1024,128]{1,0:T(8,128)S(1)}, f32[1024,128]{1,0:T(8,128)S(1)}) custom-call(s32[24]{0:T(128)S(1)} %concatenate.16.meta_ref, bf16[512,1024]{1,0:T(8,128)(2,1)S(1)} %copy-done, bf16[512,1024]{1,0:T(8,128)(2,1)S(1)} %add_rows.5.g_ref, ...), custom_call_target="tpu_custom_call", output_to_operand_aliasing={{0}: (11, {})} | custom-call | flops 4026531840 | bytes 6291456 | tf_op jit(solution)/shard_map/attend_back/pallas_call | solution.py:226
  152.0 4.0 %collective-permute-start.26 = (bf16[512,256]{1,0:T(8,128)(2,1)S(1)}, bf16[512,256]{1,0:T(8,128)(2,1)S(1)}, u32[]{:S(2)}, u32[]{:S(2)}) collective-permute-start(bf16[512,256]{1,0:T(8,128)(2,1)S(1)} %pad_maximum_fusion.2), channel_id=1, source_target_pairs={{8,0},{16,8},{24,16},{32,24},{40,32},{48,40},{56,48},{64,56},{72,6... | collective-permute-start | bytes 786440 | tf_op jit(solution)/shard_map/ppermute | solution.py:64
  156.1 5.2 %collective-permute-done.26 = bf16[512,256]{1,0:T(8,128)(2,1)S(1)} collective-permute-done((bf16[512,256]{1,0:T(8,128)(2,1)S(1)}, bf16[512,256]{1,0:T(8,128)(2,1)S(1)}, u32[]{:S(2)}, u32[]{:S(2)}) %collective-permute-start.26) | collective-permute-done | bytes 262176 | tf_op jit(solution)/shard_map/ppermute | solution.py:64
  161.3 0.8 fusion
  162.0 1.5 add_rows.9
  (39 shorter events, 0.2 us)
Async XLA Ops:
  0.6 8.7 %copy-start.5 = (s32[8]{0:T(128)S(1)}, s32[8]{0:T(128)}, u32[]{:S(2)}) copy-start(s32[8]{0:T(128)} %constant.79.clone) | copy-start | bytes 100
  0.6 8.7 %copy-start.6 = (s32[8]{0:T(128)S(1)}, s32[8]{0:T(128)}, u32[]{:S(2)}) copy-start(s32[8]{0:T(128)} %constant.80.clone) | copy-start | bytes 100
  0.7 8.7 %copy-start.7 = (s32[8]{0:T(128)S(1)}, s32[8]{0:T(128)}, u32[]{:S(2)}) copy-start(s32[8]{0:T(128)} %constant.81.clone) | copy-start | bytes 100
  0.7 3.7 %copy-start.2 = (bf16[512,128]{1,0:T(8,128)(2,1)S(1)}, bf16[512,128]{1,0:T(8,128)(2,1)}, u32[]{:S(2)}) copy-start(bf16[512,128]{1,0:T(8,128)(2,1)} %k_ref.7) | copy-start | bytes 393220
  0.7 3.7 %copy-start.1 = (bf16[512,128]{1,0:T(8,128)(2,1)S(1)}, bf16[512,128]{1,0:T(8,128)(2,1)}, u32[]{:S(2)}) copy-start(bf16[512,128]{1,0:T(8,128)(2,1)} %v_ref.7) | copy-start | bytes 393220
  0.7 13.0 %copy-start.4 = (bf16[512,1024]{1,0:T(8,128)(2,1)S(1)}, bf16[512,1024]{1,0:T(8,128)(2,1)}, u32[]{:S(2)}) copy-start(bf16[512,1024]{1,0:T(8,128)(2,1)} %refs_8_) | copy-start | bytes 3145732
  0.7 16.8 %copy-start = (bf16[512,1024]{1,0:T(8,128)(2,1)S(1)}, bf16[512,1024]{1,0:T(8,128)(2,1)}, u32[]{:S(2)}) copy-start(bf16[512,1024]{1,0:T(8,128)(2,1)} %q_ref.6) | copy-start | bytes 3145732
  0.7 16.8 %copy-start.3 = (s32[8192]{0:T(1024)S(1)}, s32[8192]{0:T(1024)}, u32[]{:S(2)}) copy-start(s32[8192]{0:T(1024)} %param.15) | copy-start | bytes 98308
  3.0 6.5 %collective-permute-start = (bf16[512,512]{1,0:T(8,128)(2,1)}, bf16[512,512]{1,0:T(8,128)(2,1)}, u32[]{:S(2)}, u32[]{:S(2)}) collective-permute-start(bf16[512,512]{1,0:T(8,128)(2,1)} %get-tuple-element.153), channel_id=1, source_target_pairs={{0,8},{8,0},{16,24},{24,16},{32,40},{40,32},{48,56},{56,48},{64,72... | collective-permute-start | bytes 1572872 | tf_op jit(solution)/shard_map/ppermute | solution.py:50
  4.4 9.3 %collective-permute-start.4 = (bf16[512,256]{1,0:T(8,128)(2,1)S(1)}, bf16[512,256]{1,0:T(8,128)(2,1)S(1)}, u32[]{:S(2)}, u32[]{:S(2)}) collective-permute-start(bf16[512,256]{1,0:T(8,128)(2,1)S(1)} %pad_maximum_fusion.1), channel_id=1, source_target_pairs={{0,8},{8,16},{16,24},{24,32},{32,40},{40,48},{48,56},{56,64},{64,7... | collective-permute-start | bytes 786440 | tf_op jit(solution)/shard_map/ppermute | solution.py:64
  10.6 24.5 %collective-permute-start.1 = (bf16[1024,512]{1,0:T(8,128)(2,1)S(1)}, bf16[1024,512]{1,0:T(8,128)(2,1)S(1)}, u32[]{:S(2)}, u32[]{:S(2)}) collective-permute-start(bf16[1024,512]{1,0:T(8,128)(2,1)S(1)} %pad_maximum_fusion.refs_0_), channel_id=1, source_target_pairs={{0,1},{1,2},{2,3},{3,0},{4,5},{5,6},{6,7},{7,4},{8,9},{9,10},{10,1... | collective-permute-start | bytes 3145736 | tf_op jit(solution)/shard_map/ppermute | solution.py:58
  11.8 23.6 %collective-permute-start.2 = (bf16[1024,512]{1,0:T(8,128)(2,1)S(1)}, bf16[1024,512]{1,0:T(8,128)(2,1)S(1)}, u32[]{:S(2)}, u32[]{:S(2)}) collective-permute-start(bf16[1024,512]{1,0:T(8,128)(2,1)S(1)} %pad_maximum_fusion.refs_0_), channel_id=1, source_target_pairs={{0,3},{1,0},{2,1},{3,2},{4,7},{5,4},{6,5},{7,6},{8,11},{9,8},{10,9... | collective-permute-start | bytes 3145736 | tf_op jit(solution)/shard_map/ppermute | solution.py:58
  13.3 23.8 %collective-permute-start.3 = (bf16[1024,512]{1,0:T(8,128)(2,1)S(1)}, bf16[1024,512]{1,0:T(8,128)(2,1)S(1)}, u32[]{:S(2)}, u32[]{:S(2)}) collective-permute-start(bf16[1024,512]{1,0:T(8,128)(2,1)S(1)} %pad_maximum_fusion.refs_0_), channel_id=1, source_target_pairs={{0,4},{1,5},{2,6},{3,7},{4,0},{5,1},{6,2},{7,3},{8,12},{9,13},{10,... | collective-permute-start | bytes 3145736 | tf_op jit(solution)/shard_map/ppermute | solution.py:58
  13.7 26.4 %collective-permute-start.10 = (bf16[512,1024]{1,0:T(8,128)(2,1)S(1)}, bf16[512,1024]{1,0:T(8,128)(2,1)S(1)}, u32[]{:S(2)}, u32[]{:S(2)}) collective-permute-start(bf16[512,1024]{1,0:T(8,128)(2,1)S(1)} %copy-done.4), channel_id=1, source_target_pairs={{0,32},{8,40},{16,48},{24,56},{32,64},{40,72},{48,80},{56,88},{64,... | collective-permute-start | bytes 3145736 | tf_op jit(solution)/shard_map/ppermute | solution.py:50
  15.3 24.7 %collective-permute-start.11 = (bf16[512,1024]{1,0:T(8,128)(2,1)S(1)}, bf16[512,1024]{1,0:T(8,128)(2,1)S(1)}, u32[]{:S(2)}, u32[]{:S(2)}) collective-permute-start(bf16[512,1024]{1,0:T(8,128)(2,1)S(1)} %copy-done.4), channel_id=1, source_target_pairs={{0,96},{8,104},{16,112},{24,120},{32,0},{40,8},{48,16},{56,24},{64... | collective-permute-start | bytes 3145736 | tf_op jit(solution)/shard_map/ppermute | solution.py:50
  37.1 7.6 %collective-permute-start.7 = (bf16[512,1024]{1,0:T(8,128)(2,1)S(1)}, bf16[512,1024]{1,0:T(8,128)(2,1)S(1)}, u32[]{:S(2)}, u32[]{:S(2)}) collective-permute-start(bf16[512,1024]{1,0:T(8,128)(2,1)S(1)} %get-tuple-element.86), channel_id=1, source_target_pairs={{0,8},{8,0},{16,24},{24,16},{32,40},{40,32},{48,56},{56,48},{64,72... | collective-permute-start | bytes 3145736 | tf_op jit(solution)/shard_map/ppermute | solution.py:50
  37.1 25.4 %collective-permute-start.5 = (bf16[1024,512]{1,0:T(8,128)(2,1)S(1)}, bf16[1024,512]{1,0:T(8,128)(2,1)S(1)}, u32[]{:S(2)}, u32[]{:S(2)}) collective-permute-start(bf16[1024,512]{1,0:T(8,128)(2,1)S(1)} %collective-permute-done.3.refs_3_), channel_id=1, source_target_pairs={{0,1},{1,2},{2,3},{3,0},{4,5},{5,6},{6,7},{7,4},{8,9},{9,10},{10,1... | collective-permute-start | bytes 3145736 | tf_op jit(solution)/shard_map/ppermute | solution.py:58
  37.3 25.2 %collective-permute-start.6 = (bf16[1024,512]{1,0:T(8,128)(2,1)S(1)}, bf16[1024,512]{1,0:T(8,128)(2,1)S(1)}, u32[]{:S(2)}, u32[]{:S(2)}) collective-permute-start(bf16[1024,512]{1,0:T(8,128)(2,1)S(1)} %collective-permute-done.3.refs_3_), channel_id=1, source_target_pairs={{0,3},{1,0},{2,1},{3,2},{4,7},{5,4},{6,5},{7,6},{8,11},{9,8},{10,9... | collective-permute-start | bytes 3145736 | tf_op jit(solution)/shard_map/ppermute | solution.py:58
  40.1 26.0 %collective-permute-start.12 = (bf16[512,1024]{1,0:T(8,128)(2,1)S(1)}, bf16[512,1024]{1,0:T(8,128)(2,1)S(1)}, u32[]{:S(2)}, u32[]{:S(2)}) collective-permute-start(bf16[512,1024]{1,0:T(8,128)(2,1)S(1)} %collective-permute-done.10.refs_9_), channel_id=1, source_target_pairs={{0,32},{8,40},{16,48},{24,56},{32,64},{40,72},{48,80},{56,88},{64,... | collective-permute-start | bytes 3145736 | tf_op jit(solution)/shard_map/ppermute | solution.py:50
  41.5 25.0 %collective-permute-start.13 = (bf16[512,1024]{1,0:T(8,128)(2,1)S(1)}, bf16[512,1024]{1,0:T(8,128)(2,1)S(1)}, u32[]{:S(2)}, u32[]{:S(2)}) collective-permute-start(bf16[512,1024]{1,0:T(8,128)(2,1)S(1)} %copy-done.4), channel_id=1, source_target_pairs={{0,16},{8,24},{16,0},{24,8},{32,48},{40,56},{48,32},{56,40},{64,80... | collective-permute-start | bytes 3145736 | tf_op jit(solution)/shard_map/ppermute | solution.py:50
  44.7 40.3 %collective-permute-start.9 = (bf16[1024,512]{1,0:T(8,128)(2,1)S(1)}, bf16[1024,512]{1,0:T(8,128)(2,1)S(1)}, u32[]{:S(2)}, u32[]{:S(2)}) collective-permute-start(bf16[1024,512]{1,0:T(8,128)(2,1)S(1)} %collective-permute-done.1.refs_1_), channel_id=1, source_target_pairs={{0,1},{1,2},{2,3},{3,0},{4,5},{5,6},{6,7},{7,4},{8,9},{9,10},{10,1... | collective-permute-start | bytes 3145736 | tf_op jit(solution)/shard_map/ppermute | solution.py:58
  62.6 25.3 %collective-permute-start.8 = (bf16[1024,512]{1,0:T(8,128)(2,1)S(1)}, bf16[1024,512]{1,0:T(8,128)(2,1)S(1)}, u32[]{:S(2)}, u32[]{:S(2)}) collective-permute-start(bf16[1024,512]{1,0:T(8,128)(2,1)S(1)} %collective-permute-done.6.refs_1_.refs_5_), channel_id=1, source_target_pairs={{0,3},{1,0},{2,1},{3,2},{4,7},{5,4},{6,5},{7,6},{8,11},{9,8},{10,9... | collective-permute-start | bytes 3145736 | tf_op jit(solution)/shard_map/ppermute | solution.py:58
  66.6 25.2 %collective-permute-start.14 = (bf16[512,1024]{1,0:T(8,128)(2,1)S(1)}, bf16[512,1024]{1,0:T(8,128)(2,1)S(1)}, u32[]{:S(2)}, u32[]{:S(2)}) collective-permute-start(bf16[512,1024]{1,0:T(8,128)(2,1)S(1)} %collective-permute-done.13.refs_11_), channel_id=1, source_target_pairs={{0,32},{8,40},{16,48},{24,56},{32,64},{40,72},{48,80},{56,88},{64,... | collective-permute-start | bytes 3145736 | tf_op jit(solution)/shard_map/ppermute | solution.py:50
  68.5 23.3 %collective-permute-start.15 = (bf16[512,1024]{1,0:T(8,128)(2,1)S(1)}, bf16[512,1024]{1,0:T(8,128)(2,1)S(1)}, u32[]{:S(2)}, u32[]{:S(2)}) collective-permute-start(bf16[512,1024]{1,0:T(8,128)(2,1)S(1)} %collective-permute-done.13.refs_11_), channel_id=1, source_target_pairs={{0,96},{8,104},{16,112},{24,120},{32,0},{40,8},{48,16},{56,24},{64... | collective-permute-start | bytes 3145736 | tf_op jit(solution)/shard_map/ppermute | solution.py:50
  69.3 23.6 %collective-permute-start.16 = (bf16[512,1024]{1,0:T(8,128)(2,1)S(1)}, bf16[512,1024]{1,0:T(8,128)(2,1)S(1)}, u32[]{:S(2)}, u32[]{:S(2)}) collective-permute-start(bf16[512,1024]{1,0:T(8,128)(2,1)S(1)} %collective-permute-done.12.refs_15_), channel_id=1, source_target_pairs={{0,16},{8,24},{16,0},{24,8},{32,48},{40,56},{48,32},{56,40},{64,80... | collective-permute-start | bytes 3145736 | tf_op jit(solution)/shard_map/ppermute | solution.py:50
  92.8 34.3 %collective-permute-start.22 = (bf16[640,1024]{1,0:T(8,128)(2,1)S(1)}, bf16[640,1024]{1,0:T(8,128)(2,1)S(1)}, u32[]{:S(2)}, u32[]{:S(2)}) collective-permute-start(bf16[640,1024]{1,0:T(8,128)(2,1)S(1)} %get-tuple-element.98), channel_id=1, source_target_pairs={{0,32},{8,40},{16,48},{24,56},{32,64},{40,72},{48,80},{56,88},{64,... | collective-permute-start | bytes 3932168 | tf_op jit(solution)/shard_map/ppermute | solution.py:50
  94.0 30.1 %collective-permute-start.19 = (bf16[512,1024]{1,0:T(8,128)(2,1)S(1)}, bf16[512,1024]{1,0:T(8,128)(2,1)S(1)}, u32[]{:S(2)}, u32[]{:S(2)}) collective-permute-start(bf16[512,1024]{1,0:T(8,128)(2,1)S(1)} %get-tuple-element.111), channel_id=1, source_target_pairs={{0,16},{8,24},{16,0},{24,8},{32,48},{40,56},{48,32},{56,40},{64,80... | collective-permute-start | bytes 3145736 | tf_op jit(solution)/shard_map/ppermute | solution.py:50
  97.0 30.2 %collective-permute-start.23 = (bf16[640,1024]{1,0:T(8,128)(2,1)S(1)}, bf16[640,1024]{1,0:T(8,128)(2,1)S(1)}, u32[]{:S(2)}, u32[]{:S(2)}) collective-permute-start(bf16[640,1024]{1,0:T(8,128)(2,1)S(1)} %get-tuple-element.122), channel_id=1, source_target_pairs={{0,96},{8,104},{16,112},{24,120},{32,0},{40,8},{48,16},{56,24},{64... | collective-permute-start | bytes 3932168 | tf_op jit(solution)/shard_map/ppermute | solution.py:50
  111.1 7.4 %collective-permute-start.17 = (bf16[256,1024]{1,0:T(8,128)(2,1)S(1)}, bf16[256,1024]{1,0:T(8,128)(2,1)S(1)}, u32[]{:S(2)}, u32[]{:S(2)}) collective-permute-start(bf16[256,1024]{1,0:T(8,128)(2,1)S(1)} %get-tuple-element.105), channel_id=1, source_target_pairs={{0,8},{8,0},{16,24},{24,16},{32,40},{40,32},{48,56},{56,48},{64,72... | collective-permute-start | bytes 1572872 | tf_op jit(solution)/shard_map/ppermute | solution.py:50
  115.6 2.9 %collective-permute-start.18 = (bf16[256,1024]{1,0:T(8,128)(2,1)S(1)}, bf16[256,1024]{1,0:T(8,128)(2,1)S(1)}, u32[]{:S(2)}, u32[]{:S(2)}) collective-permute-start(bf16[256,1024]{1,0:T(8,128)(2,1)S(1)} %get-tuple-element.106), channel_id=1, source_target_pairs={{0,8},{8,0},{16,24},{24,16},{32,40},{40,32},{48,56},{56,48},{64,72... | collective-permute-start | bytes 1572872 | tf_op jit(solution)/shard_map/ppermute | solution.py:50
  124.4 14.4 %collective-permute-start.20 = (bf16[256,1024]{1,0:T(8,128)(2,1)S(1)}, bf16[256,1024]{1,0:T(8,128)(2,1)S(1)}, u32[]{:S(2)}, u32[]{:S(2)}) collective-permute-start(bf16[256,1024]{1,0:T(8,128)(2,1)S(1)} %get-tuple-element.116), channel_id=1, source_target_pairs={{0,32},{8,40},{16,48},{24,56},{32,64},{40,72},{48,80},{56,88},{64,... | collective-permute-start | bytes 1572872 | tf_op jit(solution)/shard_map/ppermute | solution.py:50
  124.5 14.3 %collective-permute-start.21 = (bf16[256,1024]{1,0:T(8,128)(2,1)S(1)}, bf16[256,1024]{1,0:T(8,128)(2,1)S(1)}, u32[]{:S(2)}, u32[]{:S(2)}) collective-permute-start(bf16[256,1024]{1,0:T(8,128)(2,1)S(1)} %get-tuple-element.117), channel_id=1, source_target_pairs={{0,96},{8,104},{16,112},{24,120},{32,0},{40,8},{48,16},{56,24},{64... | collective-permute-start | bytes 1572872 | tf_op jit(solution)/shard_map/ppermute | solution.py:50
  127.5 34.5 %collective-permute-start.27 = (bf16[512,1024]{1,0:T(8,128)(2,1)S(1)}, bf16[512,1024]{1,0:T(8,128)(2,1)S(1)}, u32[]{:S(2)}, u32[]{:S(2)}) collective-permute-start(bf16[512,1024]{1,0:T(8,128)(2,1)S(1)} %add_rows.7), channel_id=1, source_target_pairs={{0,16},{8,24},{16,0},{24,8},{32,48},{40,56},{48,32},{56,40},{64,80... | collective-permute-start | bytes 3145736 | tf_op jit(solution)/shard_map/ppermute | solution.py:50
  127.6 16.8 %collective-permute-start.24 = (bf16[128,1024]{1,0:T(8,128)(2,1)S(1)}, bf16[128,1024]{1,0:T(8,128)(2,1)S(1)}, u32[]{:S(2)}, u32[]{:S(2)}) collective-permute-start(bf16[128,1024]{1,0:T(8,128)(2,1)S(1)} %get-tuple-element.136), channel_id=1, source_target_pairs={{0,32},{8,40},{16,48},{24,56},{32,64},{40,72},{48,80},{56,88},{64,... | collective-permute-start | bytes 786440 | tf_op jit(solution)/shard_map/ppermute | solution.py:50
  127.7 16.7 %collective-permute-start.25 = (bf16[128,1024]{1,0:T(8,128)(2,1)S(1)}, bf16[128,1024]{1,0:T(8,128)(2,1)S(1)}, u32[]{:S(2)}, u32[]{:S(2)}) collective-permute-start(bf16[128,1024]{1,0:T(8,128)(2,1)S(1)} %get-tuple-element.137), channel_id=1, source_target_pairs={{0,96},{8,104},{16,112},{24,120},{32,0},{40,8},{48,16},{56,24},{64... | collective-permute-start | bytes 786440 | tf_op jit(solution)/shard_map/ppermute | solution.py:50
  139.0 23.0 %collective-permute-start.28 = (bf16[256,1024]{1,0:T(8,128)(2,1)S(1)}, bf16[256,1024]{1,0:T(8,128)(2,1)S(1)}, u32[]{:S(2)}, u32[]{:S(2)}) collective-permute-start(bf16[256,1024]{1,0:T(8,128)(2,1)S(1)} %get-tuple-element.141), channel_id=1, source_target_pairs={{0,32},{8,40},{16,48},{24,56},{32,64},{40,72},{48,80},{56,88},{64,... | collective-permute-start | bytes 1572872 | tf_op jit(solution)/shard_map/ppermute | solution.py:50
  139.1 22.9 %collective-permute-start.29 = (bf16[256,1024]{1,0:T(8,128)(2,1)S(1)}, bf16[256,1024]{1,0:T(8,128)(2,1)S(1)}, u32[]{:S(2)}, u32[]{:S(2)}) collective-permute-start(bf16[256,1024]{1,0:T(8,128)(2,1)S(1)} %get-tuple-element.149), channel_id=1, source_target_pairs={{0,96},{8,104},{16,112},{24,120},{32,0},{40,8},{48,16},{56,24},{64... | collective-permute-start | bytes 1572872 | tf_op jit(solution)/shard_map/ppermute | solution.py:50
  152.0 9.2 %collective-permute-start.26 = (bf16[512,256]{1,0:T(8,128)(2,1)S(1)}, bf16[512,256]{1,0:T(8,128)(2,1)S(1)}, u32[]{:S(2)}, u32[]{:S(2)}) collective-permute-start(bf16[512,256]{1,0:T(8,128)(2,1)S(1)} %pad_maximum_fusion.2), channel_id=1, source_target_pairs={{8,0},{16,8},{24,16},{32,24},{40,32},{48,40},{56,48},{64,56},{72,6... | collective-permute-start | bytes 786440 | tf_op jit(solution)/shard_map/ppermute | solution.py:64

commit v11 on v10

--- a/solution.py
+++ b/solution.py
@@ -518,24 +518,25 @@
     meta = positions(row, col)
     k = row % 2
 
+    g_give = lax.dynamic_slice_in_dim(output_grad, (1 - k) * half_d, half_d, 1)
+    (output_grad,) = tied((output_grad,), g_give)
     g_keep = lax.dynamic_slice_in_dim(output_grad, k * half_d, half_d, 1)
-    g_give = lax.dynamic_slice_in_dim(output_grad, (1 - k) * half_d, half_d, 1)
     kv_earlier = passed_along(jnp.concatenate([key_rows, value_rows], 1), "row", 1)
     g_got, meta = tied((move_row(g_give, dk=1), meta))
     g0 = jnp.concatenate([g_keep, g_got], 0)
     segments = segment_ids.reshape(-1, LANES)
 
     out_proj, kv_earlier = tied((out_proj, kv_earlier), g0)
+    gy = move_col(g0, dyl=1)
     gxm = move_col(g0, dx=1)
     gxp = move_col(g0, dx=-1)
-    gy = move_col(g0, dyl=1)
     wzm = move_row(out_proj, dz=1)
     wzp = move_row(out_proj, dz=-1)
 
     (query_held,) = tied((query_rows,), g0)
     attn_out, top, total = attend(meta, query_held, kv_earlier, key_rows, value_rows, segments)
 
-    gxm, gxp, gy, attn_out = tied((gxm, gxp, gy, attn_out))
+    gy, gxm, gxp, attn_out = tied((gy, gxm, gxp, attn_out))
     wzm, wzp, out_proj = tied((wzm, wzp, out_proj), gxm)
 
     hw = out_proj.shape[0] // 2
@@ -576,9 +577,6 @@
             (4, 0, own_dn, 0, q, q),
         ),
     )
-    give_far, give_up, give_dn, wyzm, wyzp, wyo = tied(
-        (give_far, give_up, give_dn, wyzm, wyzp, wyo)
-    )
     ry = move_row(give_far, dyh=1)
     rup = move_row(give_up, dz=1)
     rdn = move_row(give_dn, dz=-1)

time: 164 us -> 165 us (level)
  other arithmetic: 1.97 us -> 3.71 us
    ppermute x21, starting transfers between devices: 34 us -> 30.5 us  [move_row(): return lax.ppermute(value, 'row', pairs)]
    ppermute x2, starting transfers between devices: 8.83 us -> 11.7 us  [passed_along(): lax.ppermute(value, axis, [(source, source + steps) for source in range(f...]
    dynamic_slice x1, local copies, waits for them, and re-layouts: 2.22 us -> 0.04 us  [local(): g_keep = lax.dynamic_slice_in_dim(output_grad, k * half_d, half_d, 1)]
  transfers between devices with their start and end apart: 30 -> 30, of which waited for: 12 -> 11; matrix products, arithmetic and copies ran while one was open for 1% -> 2% of each run, Pallas kernels for 43% -> 42%
where the time goes in v11:
time: 165 us; the launch traced here: 164 us
  Pallas kernels  71.3 us (43%)
  starting transfers between devices  50.4 us (31%)
  waiting for transfers between devices  36.3 us (22%)
  other arithmetic  3.71 us (2%)
    ppermute x21, starting transfers between devices, move_row(): return lax.ppermute(value, 'row', pairs)  30.5 us
    ppermute x7, waiting for transfers between devices, move_col(): return lax.ppermute(value, 'col', pairs)  25.6 us
    pallas_call x3, Pallas kernels, attend_back(): pl.pallas_call(functools.partial(bwd_kernel, len(earlier), last), grid_sp...  20.8 us
    pallas_call x4, Pallas kernels, project(): pl.pallas_call(functools.partial(proj_kernel, tuple(slots), held, plan),...  17.6 us
    pallas_call x1, Pallas kernels, attend(): pl.pallas_call(fwd_kernel, grid_spec=pltpu.PrefetchScalarGridSpec(num_sca...  14.9 us
    pallas_call x1, Pallas kernels, attn_grad_part(): pl.pallas_call(kernel, grid_spec=pltpu.PrefetchScalarGridSpec(num_scalar_...  12.6 us
    ppermute x2, starting transfers between devices, passed_along(): lax.ppermute(value, axis, [(source, source + steps) for source in range(f...  11.7 us
    ppermute x7, starting transfers between devices, move_col(): return lax.ppermute(value, 'col', pairs)  8.26 us
  transfers between devices with their start and end apart: 30, of which 11 were waited for; matrix products, arithmetic and copies ran while one was open for 2% of the time, Pallas kernels for 42%

profile of v11, /device:TPU:1, one launch (start us, length us, event | category | flops | bytes accessed | tf_op | source)
XLA Modules:
  0.0 164.3 jit_solution(18055885897862375635)
XLA Ops:
  0.7 1.2 copy-done
  1.9 1.5 collective-permute-start
  3.5 1.0 pad_maximum_fusion.1
  4.4 4.9 %collective-permute-start.4 = (bf16[512,256]{1,0:T(8,128)(2,1)S(1)}, bf16[512,256]{1,0:T(8,128)(2,1)S(1)}, u32[]{:S(2)}, u32[]{:S(2)}) collective-permute-start(bf16[512,256]{1,0:T(8,128)(2,1)S(1)} %pad_maximum_fusion.1), channel_id=1, source_target_pairs={{0,8},{8,16},{16,24},{24,32},{32,40},{40,48},{48,56},{56,64},{64,7... | collective-permute-start | bytes 786440 | tf_op jit(solution)/shard_map/ppermute | solution.py:64
  9.4 0.7 and_add_fusion
  10.1 0.1 concatenate.16.meta_ref
  10.3 1.2 pad_maximum_fusion.refs_0_
  11.5 0.5 collective-permute-start.1
  11.9 1.2 collective-permute-start.2
  13.1 1.5 collective-permute-start.3
  14.6 1.7 %collective-permute-start.10 = (bf16[512,1024]{1,0:T(8,128)(2,1)S(1)}, bf16[512,1024]{1,0:T(8,128)(2,1)S(1)}, u32[]{:S(2)}, u32[]{:S(2)}) collective-permute-start(bf16[512,1024]{1,0:T(8,128)(2,1)S(1)} %copy-done.5), channel_id=1, source_target_pairs={{0,32},{8,40},{16,48},{24,56},{32,64},{40,72},{48,80},{56,88},{64,... | collective-permute-start | bytes 3145736 | tf_op jit(solution)/shard_map/ppermute | solution.py:50
  16.3 2.2 %collective-permute-start.11 = (bf16[512,1024]{1,0:T(8,128)(2,1)S(1)}, bf16[512,1024]{1,0:T(8,128)(2,1)S(1)}, u32[]{:S(2)}, u32[]{:S(2)}) collective-permute-start(bf16[512,1024]{1,0:T(8,128)(2,1)S(1)} %copy-done.5), channel_id=1, source_target_pairs={{0,96},{8,104},{16,112},{24,120},{32,0},{40,8},{48,16},{56,24},{64... | collective-permute-start | bytes 3145736 | tf_op jit(solution)/shard_map/ppermute | solution.py:50
  18.5 14.9 %attend.1 = (bf16[512,1024]{1,0:T(8,128)(2,1)S(1)}, f32[8,1,512]{2,1,0:T(1,128)S(1)}, f32[8,1,512]{2,1,0:T(1,128)S(1)}) custom-call(s32[24]{0:T(128)S(1)} %concatenate.16.meta_ref, bf16[512,1024]{1,0:T(8,128)(2,1)S(1)} %copy-done.1, bf16[512,256]{1,0:T(8,128)(2,1)S(1)} %collective-permute-done.4.kv_ref, bf16[512,128]{1,0:T(8,128)(2,1)S(1)} %copy-done.3, ...), custom_call_target="tpu_custom_call" | custom-call | flops 68719476736 | bytes 8388608 | tf_op jit(solution)/shard_map/attend/pallas_call | solution.py:148
  33.4 2.9 %collective-permute-done.1.refs_3_ = bf16[1024,512]{1,0:T(8,128)(2,1)S(1)} collective-permute-done((bf16[1024,512]{1,0:T(8,128)(2,1)S(1)}, bf16[1024,512]{1,0:T(8,128)(2,1)S(1)}, u32[]{:S(2)}, u32[]{:S(2)}) %collective-permute-start.1) | collective-permute-done | bytes 1048608 | tf_op jit(solution)/shard_map/ppermute | solution.py:58
  36.2 1.4 collective-permute-done.2.refs_1_
  37.6 0.3 collective-permute-done.3.refs_2_
  37.9 0.0 collective-permute-start.7
  37.9 1.2 collective-permute-start.5
  39.1 1.5 collective-permute-start.6
  40.6 1.2 collective-permute-done.10.refs_9_
  41.8 0.5 collective-permute-start.12
  42.3 2.5 %collective-permute-start.13 = (bf16[512,1024]{1,0:T(8,128)(2,1)S(1)}, bf16[512,1024]{1,0:T(8,128)(2,1)S(1)}, u32[]{:S(2)}, u32[]{:S(2)}) collective-permute-start(bf16[512,1024]{1,0:T(8,128)(2,1)S(1)} %copy-done.5), channel_id=1, source_target_pairs={{0,16},{8,24},{16,0},{24,8},{32,48},{40,56},{48,32},{56,40},{64,80... | collective-permute-start | bytes 3145736 | tf_op jit(solution)/shard_map/ppermute | solution.py:50
  44.8 0.1 constant_dynamic-update-slice_fusion.1
  44.9 0.1 collective-permute-start.9
  45.0 0.1 constant_dynamic-update-slice_fusion.refs_4_.refs_2_.refs_1_
  45.1 6.8 %project.4.refs_3_ = bf16[2,64,256,1024]{3,2,1,0:T(8,128)(2,1)} custom-call(s32[24]{0:T(128)S(1)} %concatenate.16.meta_ref, bf16[1024,512]{1,0:T(8,128)(2,1)S(1)} %pad_maximum_fusion.refs_0_, bf16[1024,512]{1,0:T(8,128)(2,1)S(1)} %collective-permute-done.2.refs_1_, bf16[1024,512]{1,0:T(8,128)(2,1)S(1)} %collective-permute-done.3.refs_2_, ...), custom_call_target="tpu_custom_call" | custom-call | flops 4294967296 | bytes 10485760 | tf_op jit(solution)/shard_map/project/pallas_call | solution.py:324
  51.8 11.5 %collective-permute-done.5.refs_0_.refs_4_ = bf16[1024,512]{1,0:T(8,128)(2,1)S(1)} collective-permute-done((bf16[1024,512]{1,0:T(8,128)(2,1)S(1)}, bf16[1024,512]{1,0:T(8,128)(2,1)S(1)}, u32[]{:S(2)}, u32[]{:S(2)}) %collective-permute-start.5) | collective-permute-done | bytes 1048608 | tf_op jit(solution)/shard_map/ppermute | solution.py:58
  63.3 2.4 %collective-permute-start.8 = (bf16[1024,512]{1,0:T(8,128)(2,1)S(1)}, bf16[1024,512]{1,0:T(8,128)(2,1)S(1)}, u32[]{:S(2)}, u32[]{:S(2)}) collective-permute-start(bf16[1024,512]{1,0:T(8,128)(2,1)S(1)} %collective-permute-done.6.refs_1_.refs_5_), channel_id=1, source_target_pairs={{0,3},{1,0},{2,1},{3,2},{4,7},{5,4},{6,5},{7,6},{8,11},{9,8},{10,9... | collective-permute-start | bytes 3145736 | tf_op jit(solution)/shard_map/ppermute | solution.py:58
  65.7 1.3 collective-permute-done.12.refs_15_
  67.1 1.6 collective-permute-start.14
  68.6 1.1 collective-permute-start.15
  69.7 2.4 %collective-permute-start.16 = (bf16[512,1024]{1,0:T(8,128)(2,1)S(1)}, bf16[512,1024]{1,0:T(8,128)(2,1)S(1)}, u32[]{:S(2)}, u32[]{:S(2)}) collective-permute-start(bf16[512,1024]{1,0:T(8,128)(2,1)S(1)} %collective-permute-done.12.refs_15_), channel_id=1, source_target_pairs={{0,16},{8,24},{16,0},{24,8},{32,48},{40,56},{48,32},{56,40},{64,80... | collective-permute-start | bytes 3145736 | tf_op jit(solution)/shard_map/ppermute | solution.py:50
  72.1 4.2 %project.5.refs_2_ = bf16[2,64,256,1024]{3,2,1,0:T(8,128)(2,1)} custom-call(s32[24]{0:T(128)S(1)} %concatenate.16.meta_ref, bf16[1024,512]{1,0:T(8,128)(2,1)S(1)} %collective-permute-done.5.refs_0_.refs_4_, bf16[1024,512]{1,0:T(8,128)(2,1)S(1)} %collective-permute-done.6.refs_1_.refs_5_, ...), custom_call_target="tpu_custom_call", output_to_operand_aliasing={{}: (4, {})} | custom-call | flops 2147483648 | bytes 6291456 | tf_op jit(solution)/shard_map/project/pallas_call | solution.py:324
  76.3 9.5 %collective-permute-done.9.refs_0_.refs_6_ = bf16[1024,512]{1,0:T(8,128)(2,1)S(1)} collective-permute-done((bf16[1024,512]{1,0:T(8,128)(2,1)S(1)}, bf16[1024,512]{1,0:T(8,128)(2,1)S(1)}, u32[]{:S(2)}, u32[]{:S(2)}) %collective-permute-start.9) | collective-permute-done | bytes 1048608 | tf_op jit(solution)/shard_map/ppermute | solution.py:58
  85.8 2.8 %project.6.refs_2_ = bf16[2,64,256,1024]{3,2,1,0:T(8,128)(2,1)} custom-call(s32[24]{0:T(128)S(1)} %concatenate.16.meta_ref, bf16[1024,512]{1,0:T(8,128)(2,1)S(1)} %collective-permute-done.9.refs_0_.refs_6_, bf16[1024,1024]{1,0:T(8,128)(2,1)S(1)} %constant_dynamic-update-slice_fusion.refs_4_.refs_2_.refs_1_, ...), custom_call_target="tpu_custom_call", output_to_operand_aliasing={{}: (3, {})} | custom-call | flops 1073741824 | bytes 4194304 | tf_op jit(solution)/shard_map/project/pallas_call | solution.py:324
  88.6 3.9 %project.7 = (bf16[2,64,256,1024]{3,2,1,0:T(8,128)(2,1)}, bf16[512,1024]{1,0:T(8,128)(2,1)S(1)}, bf16[640,1024]{1,0:T(8,128)(2,1)S(1)}, bf16[640,1024]{1,0:T(8,1...) custom-call(s32[24]{0:T(128)S(1)} %concatenate.16.meta_ref, ...), custom_call_target="tpu_custom_call", output_to_operand_aliasing={{0}: (3, {})} | custom-call | flops 1073741824 | bytes 4194304 | tf_op jit(solution)/shard_map/project/pallas_call | solution.py:324
  92.5 1.8 %collective-permute-start.22 = (bf16[640,1024]{1,0:T(8,128)(2,1)S(1)}, bf16[640,1024]{1,0:T(8,128)(2,1)S(1)}, u32[]{:S(2)}, u32[]{:S(2)}) collective-permute-start(bf16[640,1024]{1,0:T(8,128)(2,1)S(1)} %get-tuple-element.86), channel_id=1, source_target_pairs={{0,32},{8,40},{16,48},{24,56},{32,64},{40,72},{48,80},{56,88},{64,... | collective-permute-start | bytes 3932168 | tf_op jit(solution)/shard_map/ppermute | solution.py:50
  94.4 2.3 %collective-permute-start.19 = (bf16[512,1024]{1,0:T(8,128)(2,1)S(1)}, bf16[512,1024]{1,0:T(8,128)(2,1)S(1)}, u32[]{:S(2)}, u32[]{:S(2)}) collective-permute-start(bf16[512,1024]{1,0:T(8,128)(2,1)S(1)} %get-tuple-element.101), channel_id=1, source_target_pairs={{0,16},{8,24},{16,0},{24,8},{32,48},{40,56},{48,32},{56,40},{64,80... | collective-permute-start | bytes 3145736 | tf_op jit(solution)/shard_map/ppermute | solution.py:50
  96.7 1.3 collective-permute-start.23
  98.0 12.6 %attn_grad.1 = (f32[512,1024]{1,0:T(8,128)S(1)}, bf16[256,1024]{1,0:T(8,128)(2,1)S(1)}, bf16[256,1024]{1,0:T(8,128)(2,1)S(1)}) custom-call(s32[24]{0:T(128)S(1)} %concatenate.16.meta_ref, bf16[1024,512]{1,0:T(8,128)(2,1)S(1)} %pad_maximum_fusion.refs_0_, bf16[1024,512]{1,0:T(8,128)(2,1)S(1)} %collective-permute-done.2.refs_1_, ...), custom_call_target="tpu_custom_call" | custom-call | flops 8589934592 | bytes 20971520 | tf_op jit(solution)/shard_map/attn_grad/pallas_call | solution.py:419
  110.6 2.0 %collective-permute-start.17 = (bf16[256,1024]{1,0:T(8,128)(2,1)S(1)}, bf16[256,1024]{1,0:T(8,128)(2,1)S(1)}, u32[]{:S(2)}, u32[]{:S(2)}) collective-permute-start(bf16[256,1024]{1,0:T(8,128)(2,1)S(1)} %get-tuple-element.95), channel_id=1, source_target_pairs={{0,8},{8,0},{16,24},{24,16},{32,40},{40,32},{48,56},{56,48},{64,72... | collective-permute-start | bytes 1572872 | tf_op jit(solution)/shard_map/ppermute | solution.py:50
  112.6 0.1 collective-permute-start.18
  112.7 2.8 %fetch.1 = (bf16[512,1024]{1,0:T(8,128)(2,1)S(1)}, bf16[512,1024]{1,0:T(8,128)(2,1)S(1)}, bf16[512,1024]{1,0:T(8,128)(2,1)S(1)}, bf16[512,1024]{1,0:T(8,128)(2,1)S(1)}) custom-call(s32[24]{0:T(128)S(1)} %concatenate.16.meta_ref, bf16[2,64,256,1024]{3,2,1,0:T(8,128)(2,1)} %get-tuple-element.99.buffer_ref), custom_call_target="tpu_custom_call" | custom-call | bytes 65536 | tf_op jit(solution)/shard_map/fetch/pallas_call | solution.py:466
  115.5 0.2 add_rows.5.g_ref
  115.7 5.6 %attend_back.3 = (bf16[512,1024]{1,0:T(8,128)(2,1)}, f32[1024,128]{1,0:T(8,128)S(1)}, f32[1024,128]{1,0:T(8,128)S(1)}) custom-call(s32[24]{0:T(128)S(1)} %concatenate.16.meta_ref, bf16[512,1024]{1,0:T(8,128)(2,1)S(1)} %copy-done.1, bf16[512,1024]{1,0:T(8,128)(2,1)S(1)} %add_rows.5.g_ref, bf16[512,256]{1,0:T(8,128)(2,1)S(1)} %collective-permute-done.4.kv_ref, ...), custom_call_target="tpu_custom_call" | custom-call | flops 1048576 | bytes 65536 | tf_op jit(solution)/shard_map/attend_back/pallas_call | solution.py:226
  121.3 0.2 add_rows.6
  121.5 0.5 collective-permute-start.20
  122.0 2.2 %collective-permute-start.21 = (bf16[256,1024]{1,0:T(8,128)(2,1)S(1)}, bf16[256,1024]{1,0:T(8,128)(2,1)S(1)}, u32[]{:S(2)}, u32[]{:S(2)}) collective-permute-start(bf16[256,1024]{1,0:T(8,128)(2,1)S(1)} %get-tuple-element.107), channel_id=1, source_target_pairs={{0,96},{8,104},{16,112},{24,120},{32,0},{40,8},{48,16},{56,24},{64... | collective-permute-start | bytes 1572872 | tf_op jit(solution)/shard_map/ppermute | solution.py:50
  124.3 1.1 collective-permute-done.23.refs_2_.refs_6_
  125.4 0.4 add_rows.7
  125.8 0.7 collective-permute-start.27
  126.4 1.3 collective-permute-start.24
  127.7 2.2 %collective-permute-start.25 = (bf16[128,1024]{1,0:T(8,128)(2,1)S(1)}, bf16[128,1024]{1,0:T(8,128)(2,1)S(1)}, u32[]{:S(2)}, u32[]{:S(2)}) collective-permute-start(bf16[128,1024]{1,0:T(8,128)(2,1)S(1)} %get-tuple-element.127), channel_id=1, source_target_pairs={{0,96},{8,104},{16,112},{24,120},{32,0},{40,8},{48,16},{56,24},{64... | collective-permute-start | bytes 786440 | tf_op jit(solution)/shard_map/ppermute | solution.py:50
  129.9 7.6 %attend_back.4 = (bf16[512,1024]{1,0:T(8,128)(2,1)}, f32[1024,128]{1,0:T(8,128)S(1)}, f32[1024,128]{1,0:T(8,128)S(1)}) custom-call(s32[24]{0:T(128)S(1)} %concatenate.16.meta_ref, bf16[512,1024]{1,0:T(8,128)(2,1)S(1)} %copy-done.1, bf16[512,1024]{1,0:T(8,128)(2,1)S(1)} %add_rows.5.g_ref, ...), custom_call_target="tpu_custom_call", output_to_operand_aliasing={{0}: (11, {})} | custom-call | flops 4026531840 | bytes 6291456 | tf_op jit(solution)/shard_map/attend_back/pallas_call | solution.py:226
  137.4 0.2 add_rows.8
  137.7 0.5 collective-permute-start.28
  138.2 2.2 %collective-permute-start.29 = (bf16[256,1024]{1,0:T(8,128)(2,1)S(1)}, bf16[256,1024]{1,0:T(8,128)(2,1)S(1)}, u32[]{:S(2)}, u32[]{:S(2)}) collective-permute-start(bf16[256,1024]{1,0:T(8,128)(2,1)S(1)} %get-tuple-element.139), channel_id=1, source_target_pairs={{0,96},{8,104},{16,112},{24,120},{32,0},{40,8},{48,16},{56,24},{64... | collective-permute-start | bytes 1572872 | tf_op jit(solution)/shard_map/ppermute | solution.py:50
  140.4 1.7 %collective-permute-done.24.refs_5_ = bf16[128,1024]{1,0:T(8,128)(2,1)S(1)} collective-permute-done((bf16[128,1024]{1,0:T(8,128)(2,1)S(1)}, bf16[128,1024]{1,0:T(8,128)(2,1)S(1)}, u32[]{:S(2)}, u32[]{:S(2)}) %collective-permute-start.24) | collective-permute-done | bytes 262176 | tf_op jit(solution)/shard_map/ppermute | solution.py:50
  142.1 0.1 collective-permute-done.25.refs_7_
  142.2 7.6 %attend_back.5 = (bf16[512,1024]{1,0:T(8,128)(2,1)}, f32[1024,128]{1,0:T(8,128)S(1)}, f32[1024,128]{1,0:T(8,128)S(1)}) custom-call(s32[24]{0:T(128)S(1)} %concatenate.16.meta_ref, bf16[512,1024]{1,0:T(8,128)(2,1)S(1)} %copy-done.1, bf16[512,1024]{1,0:T(8,128)(2,1)S(1)} %add_rows.5.g_ref, ...), custom_call_target="tpu_custom_call", output_to_operand_aliasing={{0}: (11, {})} | custom-call | flops 4026531840 | bytes 6291456 | tf_op jit(solution)/shard_map/attend_back/pallas_call | solution.py:226
  150.0 6.8 %collective-permute-start.26 = (bf16[512,256]{1,0:T(8,128)(2,1)S(1)}, bf16[512,256]{1,0:T(8,128)(2,1)S(1)}, u32[]{:S(2)}, u32[]{:S(2)}) collective-permute-start(bf16[512,256]{1,0:T(8,128)(2,1)S(1)} %pad_maximum_fusion.2), channel_id=1, source_target_pairs={{8,0},{16,8},{24,16},{32,24},{40,32},{48,40},{56,48},{64,56},{72,6... | collective-permute-start | bytes 786440 | tf_op jit(solution)/shard_map/ppermute | solution.py:64
  156.8 5.2 %collective-permute-done.26 = bf16[512,256]{1,0:T(8,128)(2,1)S(1)} collective-permute-done((bf16[512,256]{1,0:T(8,128)(2,1)S(1)}, bf16[512,256]{1,0:T(8,128)(2,1)S(1)}, u32[]{:S(2)}, u32[]{:S(2)}) %collective-permute-start.26) | collective-permute-done | bytes 262176 | tf_op jit(solution)/shard_map/ppermute | solution.py:64
  162.0 0.8 fusion
  162.8 1.5 add_rows.9
  (36 shorter events, 0.3 us)
Async XLA Ops:
  0.6 1.2 copy-start
  1.9 16.6 %copy-start.1 = (bf16[512,1024]{1,0:T(8,128)(2,1)S(1)}, bf16[512,1024]{1,0:T(8,128)(2,1)}, u32[]{:S(2)}) copy-start(bf16[512,1024]{1,0:T(8,128)(2,1)} %q_ref.6) | copy-start | bytes 3145732
  1.9 16.5 %copy-start.2 = (bf16[512,128]{1,0:T(8,128)(2,1)S(1)}, bf16[512,128]{1,0:T(8,128)(2,1)}, u32[]{:S(2)}) copy-start(bf16[512,128]{1,0:T(8,128)(2,1)} %v_ref.7) | copy-start | bytes 393220
  1.9 16.5 %copy-start.3 = (bf16[512,128]{1,0:T(8,128)(2,1)S(1)}, bf16[512,128]{1,0:T(8,128)(2,1)}, u32[]{:S(2)}) copy-start(bf16[512,128]{1,0:T(8,128)(2,1)} %k_ref.7) | copy-start | bytes 393220
  1.9 16.5 %copy-start.4 = (s32[8192]{0:T(1024)S(1)}, s32[8192]{0:T(1024)}, u32[]{:S(2)}) copy-start(s32[8192]{0:T(1024)} %param.15) | copy-start | bytes 98308
  1.9 8.3 %collective-permute-start = (bf16[512,512]{1,0:T(8,128)(2,1)S(1)}, bf16[512,512]{1,0:T(8,128)(2,1)}, u32[]{:S(2)}, u32[]{:S(2)}) collective-permute-start(bf16[512,512]{1,0:T(8,128)(2,1)S(1)} %constant_dynamic-slice_fusion.1), channel_id=1, source_target_pairs={{0,8},{8,0},{16,24},{24,16},{32,40},{40,32},{48,56},{56,48},{64,72... | collective-permute-start | bytes 1572872 | tf_op jit(solution)/shard_map/ppermute | solution.py:50
  4.4 10.2 %collective-permute-start.4 = (bf16[512,256]{1,0:T(8,128)(2,1)S(1)}, bf16[512,256]{1,0:T(8,128)(2,1)S(1)}, u32[]{:S(2)}, u32[]{:S(2)}) collective-permute-start(bf16[512,256]{1,0:T(8,128)(2,1)S(1)} %pad_maximum_fusion.1), channel_id=1, source_target_pairs={{0,8},{8,16},{16,24},{24,32},{32,40},{40,48},{48,56},{56,64},{64,7... | collective-permute-start | bytes 786440 | tf_op jit(solution)/shard_map/ppermute | solution.py:64
  10.2 4.4 %copy-start.5 = (bf16[512,1024]{1,0:T(8,128)(2,1)S(1)}, bf16[512,1024]{1,0:T(8,128)(2,1)}, u32[]{:S(2)}) copy-start(bf16[512,1024]{1,0:T(8,128)(2,1)} %refs_8_) | copy-start | bytes 3145732
  11.5 24.8 %collective-permute-start.1 = (bf16[1024,512]{1,0:T(8,128)(2,1)S(1)}, bf16[1024,512]{1,0:T(8,128)(2,1)S(1)}, u32[]{:S(2)}, u32[]{:S(2)}) collective-permute-start(bf16[1024,512]{1,0:T(8,128)(2,1)S(1)} %pad_maximum_fusion.refs_0_), channel_id=1, source_target_pairs={{0,4},{1,5},{2,6},{3,7},{4,0},{5,1},{6,2},{7,3},{8,12},{9,13},{10,... | collective-permute-start | bytes 3145736 | tf_op jit(solution)/shard_map/ppermute | solution.py:58
  11.9 25.7 %collective-permute-start.2 = (bf16[1024,512]{1,0:T(8,128)(2,1)S(1)}, bf16[1024,512]{1,0:T(8,128)(2,1)S(1)}, u32[]{:S(2)}, u32[]{:S(2)}) collective-permute-start(bf16[1024,512]{1,0:T(8,128)(2,1)S(1)} %pad_maximum_fusion.refs_0_), channel_id=1, source_target_pairs={{0,1},{1,2},{2,3},{3,0},{4,5},{5,6},{6,7},{7,4},{8,9},{9,10},{10,1... | collective-permute-start | bytes 3145736 | tf_op jit(solution)/shard_map/ppermute | solution.py:58
  13.1 24.7 %collective-permute-start.3 = (bf16[1024,512]{1,0:T(8,128)(2,1)S(1)}, bf16[1024,512]{1,0:T(8,128)(2,1)S(1)}, u32[]{:S(2)}, u32[]{:S(2)}) collective-permute-start(bf16[1024,512]{1,0:T(8,128)(2,1)S(1)} %pad_maximum_fusion.refs_0_), channel_id=1, source_target_pairs={{0,3},{1,0},{2,1},{3,2},{4,7},{5,4},{6,5},{7,6},{8,11},{9,8},{10,9... | collective-permute-start | bytes 3145736 | tf_op jit(solution)/shard_map/ppermute | solution.py:58
  14.6 27.2 %collective-permute-start.10 = (bf16[512,1024]{1,0:T(8,128)(2,1)S(1)}, bf16[512,1024]{1,0:T(8,128)(2,1)S(1)}, u32[]{:S(2)}, u32[]{:S(2)}) collective-permute-start(bf16[512,1024]{1,0:T(8,128)(2,1)S(1)} %copy-done.5), channel_id=1, source_target_pairs={{0,32},{8,40},{16,48},{24,56},{32,64},{40,72},{48,80},{56,88},{64,... | collective-permute-start | bytes 3145736 | tf_op jit(solution)/shard_map/ppermute | solution.py:50
  16.3 25.5 %collective-permute-start.11 = (bf16[512,1024]{1,0:T(8,128)(2,1)S(1)}, bf16[512,1024]{1,0:T(8,128)(2,1)S(1)}, u32[]{:S(2)}, u32[]{:S(2)}) collective-permute-start(bf16[512,1024]{1,0:T(8,128)(2,1)S(1)} %copy-done.5), channel_id=1, source_target_pairs={{0,96},{8,104},{16,112},{24,120},{32,0},{40,8},{48,16},{56,24},{64... | collective-permute-start | bytes 3145736 | tf_op jit(solution)/shard_map/ppermute | solution.py:50
  37.9 7.0 %collective-permute-start.7 = (bf16[512,1024]{1,0:T(8,128)(2,1)S(1)}, bf16[512,1024]{1,0:T(8,128)(2,1)S(1)}, u32[]{:S(2)}, u32[]{:S(2)}) collective-permute-start(bf16[512,1024]{1,0:T(8,128)(2,1)S(1)} %get-tuple-element.82), channel_id=1, source_target_pairs={{0,8},{8,0},{16,24},{24,16},{32,40},{40,32},{48,56},{56,48},{64,72... | collective-permute-start | bytes 3145736 | tf_op jit(solution)/shard_map/ppermute | solution.py:50
  37.9 25.4 %collective-permute-start.5 = (bf16[1024,512]{1,0:T(8,128)(2,1)S(1)}, bf16[1024,512]{1,0:T(8,128)(2,1)S(1)}, u32[]{:S(2)}, u32[]{:S(2)}) collective-permute-start(bf16[1024,512]{1,0:T(8,128)(2,1)S(1)} %collective-permute-done.1.refs_3_), channel_id=1, source_target_pairs={{0,1},{1,2},{2,3},{3,0},{4,5},{5,6},{6,7},{7,4},{8,9},{9,10},{10,1... | collective-permute-start | bytes 3145736 | tf_op jit(solution)/shard_map/ppermute | solution.py:58
  39.1 24.2 %collective-permute-start.6 = (bf16[1024,512]{1,0:T(8,128)(2,1)S(1)}, bf16[1024,512]{1,0:T(8,128)(2,1)S(1)}, u32[]{:S(2)}, u32[]{:S(2)}) collective-permute-start(bf16[1024,512]{1,0:T(8,128)(2,1)S(1)} %collective-permute-done.1.refs_3_), channel_id=1, source_target_pairs={{0,3},{1,0},{2,1},{3,2},{4,7},{5,4},{6,5},{7,6},{8,11},{9,8},{10,9... | collective-permute-start | bytes 3145736 | tf_op jit(solution)/shard_map/ppermute | solution.py:58
  41.8 25.2 %collective-permute-start.12 = (bf16[512,1024]{1,0:T(8,128)(2,1)S(1)}, bf16[512,1024]{1,0:T(8,128)(2,1)S(1)}, u32[]{:S(2)}, u32[]{:S(2)}) collective-permute-start(bf16[512,1024]{1,0:T(8,128)(2,1)S(1)} %collective-permute-done.10.refs_9_), channel_id=1, source_target_pairs={{0,32},{8,40},{16,48},{24,56},{32,64},{40,72},{48,80},{56,88},{64,... | collective-permute-start | bytes 3145736 | tf_op jit(solution)/shard_map/ppermute | solution.py:50
  42.3 24.7 %collective-permute-start.13 = (bf16[512,1024]{1,0:T(8,128)(2,1)S(1)}, bf16[512,1024]{1,0:T(8,128)(2,1)S(1)}, u32[]{:S(2)}, u32[]{:S(2)}) collective-permute-start(bf16[512,1024]{1,0:T(8,128)(2,1)S(1)} %copy-done.5), channel_id=1, source_target_pairs={{0,16},{8,24},{16,0},{24,8},{32,48},{40,56},{48,32},{56,40},{64,80... | collective-permute-start | bytes 3145736 | tf_op jit(solution)/shard_map/ppermute | solution.py:50
  44.9 40.9 %collective-permute-start.9 = (bf16[1024,512]{1,0:T(8,128)(2,1)S(1)}, bf16[1024,512]{1,0:T(8,128)(2,1)S(1)}, u32[]{:S(2)}, u32[]{:S(2)}) collective-permute-start(bf16[1024,512]{1,0:T(8,128)(2,1)S(1)} %collective-permute-done.2.refs_1_), channel_id=1, source_target_pairs={{0,1},{1,2},{2,3},{3,0},{4,5},{5,6},{6,7},{7,4},{8,9},{9,10},{10,1... | collective-permute-start | bytes 3145736 | tf_op jit(solution)/shard_map/ppermute | solution.py:58
  63.3 25.3 %collective-permute-start.8 = (bf16[1024,512]{1,0:T(8,128)(2,1)S(1)}, bf16[1024,512]{1,0:T(8,128)(2,1)S(1)}, u32[]{:S(2)}, u32[]{:S(2)}) collective-permute-start(bf16[1024,512]{1,0:T(8,128)(2,1)S(1)} %collective-permute-done.6.refs_1_.refs_5_), channel_id=1, source_target_pairs={{0,3},{1,0},{2,1},{3,2},{4,7},{5,4},{6,5},{7,6},{8,11},{9,8},{10,9... | collective-permute-start | bytes 3145736 | tf_op jit(solution)/shard_map/ppermute | solution.py:58
  67.1 29.6 %collective-permute-start.14 = (bf16[512,1024]{1,0:T(8,128)(2,1)S(1)}, bf16[512,1024]{1,0:T(8,128)(2,1)S(1)}, u32[]{:S(2)}, u32[]{:S(2)}) collective-permute-start(bf16[512,1024]{1,0:T(8,128)(2,1)S(1)} %collective-permute-done.13.refs_11_), channel_id=1, source_target_pairs={{0,32},{8,40},{16,48},{24,56},{32,64},{40,72},{48,80},{56,88},{64,... | collective-permute-start | bytes 3145736 | tf_op jit(solution)/shard_map/ppermute | solution.py:50
  68.6 29.4 %collective-permute-start.15 = (bf16[512,1024]{1,0:T(8,128)(2,1)S(1)}, bf16[512,1024]{1,0:T(8,128)(2,1)S(1)}, u32[]{:S(2)}, u32[]{:S(2)}) collective-permute-start(bf16[512,1024]{1,0:T(8,128)(2,1)S(1)} %collective-permute-done.13.refs_11_), channel_id=1, source_target_pairs={{0,96},{8,104},{16,112},{24,120},{32,0},{40,8},{48,16},{56,24},{64... | collective-permute-start | bytes 3145736 | tf_op jit(solution)/shard_map/ppermute | solution.py:50
  69.7 28.3 %collective-permute-start.16 = (bf16[512,1024]{1,0:T(8,128)(2,1)S(1)}, bf16[512,1024]{1,0:T(8,128)(2,1)S(1)}, u32[]{:S(2)}, u32[]{:S(2)}) collective-permute-start(bf16[512,1024]{1,0:T(8,128)(2,1)S(1)} %collective-permute-done.12.refs_15_), channel_id=1, source_target_pairs={{0,16},{8,24},{16,0},{24,8},{32,48},{40,56},{48,32},{56,40},{64,80... | collective-permute-start | bytes 3145736 | tf_op jit(solution)/shard_map/ppermute | solution.py:50
  92.5 31.7 %collective-permute-start.22 = (bf16[640,1024]{1,0:T(8,128)(2,1)S(1)}, bf16[640,1024]{1,0:T(8,128)(2,1)S(1)}, u32[]{:S(2)}, u32[]{:S(2)}) collective-permute-start(bf16[640,1024]{1,0:T(8,128)(2,1)S(1)} %get-tuple-element.86), channel_id=1, source_target_pairs={{0,32},{8,40},{16,48},{24,56},{32,64},{40,72},{48,80},{56,88},{64,... | collective-permute-start | bytes 3932168 | tf_op jit(solution)/shard_map/ppermute | solution.py:50
  94.4 26.9 %collective-permute-start.19 = (bf16[512,1024]{1,0:T(8,128)(2,1)S(1)}, bf16[512,1024]{1,0:T(8,128)(2,1)S(1)}, u32[]{:S(2)}, u32[]{:S(2)}) collective-permute-start(bf16[512,1024]{1,0:T(8,128)(2,1)S(1)} %get-tuple-element.101), channel_id=1, source_target_pairs={{0,16},{8,24},{16,0},{24,8},{32,48},{40,56},{48,32},{56,40},{64,80... | collective-permute-start | bytes 3145736 | tf_op jit(solution)/shard_map/ppermute | solution.py:50
  96.7 28.7 %collective-permute-start.23 = (bf16[640,1024]{1,0:T(8,128)(2,1)S(1)}, bf16[640,1024]{1,0:T(8,128)(2,1)S(1)}, u32[]{:S(2)}, u32[]{:S(2)}) collective-permute-start(bf16[640,1024]{1,0:T(8,128)(2,1)S(1)} %get-tuple-element.112), channel_id=1, source_target_pairs={{0,96},{8,104},{16,112},{24,120},{32,0},{40,8},{48,16},{56,24},{64... | collective-permute-start | bytes 3932168 | tf_op jit(solution)/shard_map/ppermute | solution.py:50
  110.6 4.8 %collective-permute-start.17 = (bf16[256,1024]{1,0:T(8,128)(2,1)S(1)}, bf16[256,1024]{1,0:T(8,128)(2,1)S(1)}, u32[]{:S(2)}, u32[]{:S(2)}) collective-permute-start(bf16[256,1024]{1,0:T(8,128)(2,1)S(1)} %get-tuple-element.95), channel_id=1, source_target_pairs={{0,8},{8,0},{16,24},{24,16},{32,40},{40,32},{48,56},{56,48},{64,72... | collective-permute-start | bytes 1572872 | tf_op jit(solution)/shard_map/ppermute | solution.py:50
  112.6 2.9 %collective-permute-start.18 = (bf16[256,1024]{1,0:T(8,128)(2,1)S(1)}, bf16[256,1024]{1,0:T(8,128)(2,1)S(1)}, u32[]{:S(2)}, u32[]{:S(2)}) collective-permute-start(bf16[256,1024]{1,0:T(8,128)(2,1)S(1)} %get-tuple-element.96), channel_id=1, source_target_pairs={{0,8},{8,0},{16,24},{24,16},{32,40},{40,32},{48,56},{56,48},{64,72... | collective-permute-start | bytes 1572872 | tf_op jit(solution)/shard_map/ppermute | solution.py:50
  121.5 15.9 %collective-permute-start.20 = (bf16[256,1024]{1,0:T(8,128)(2,1)S(1)}, bf16[256,1024]{1,0:T(8,128)(2,1)S(1)}, u32[]{:S(2)}, u32[]{:S(2)}) collective-permute-start(bf16[256,1024]{1,0:T(8,128)(2,1)S(1)} %get-tuple-element.106), channel_id=1, source_target_pairs={{0,32},{8,40},{16,48},{24,56},{32,64},{40,72},{48,80},{56,88},{64,... | collective-permute-start | bytes 1572872 | tf_op jit(solution)/shard_map/ppermute | solution.py:50
  122.0 15.4 %collective-permute-start.21 = (bf16[256,1024]{1,0:T(8,128)(2,1)S(1)}, bf16[256,1024]{1,0:T(8,128)(2,1)S(1)}, u32[]{:S(2)}, u32[]{:S(2)}) collective-permute-start(bf16[256,1024]{1,0:T(8,128)(2,1)S(1)} %get-tuple-element.107), channel_id=1, source_target_pairs={{0,96},{8,104},{16,112},{24,120},{32,0},{40,8},{48,16},{56,24},{64... | collective-permute-start | bytes 1572872 | tf_op jit(solution)/shard_map/ppermute | solution.py:50
  125.8 37.0 %collective-permute-start.27 = (bf16[512,1024]{1,0:T(8,128)(2,1)S(1)}, bf16[512,1024]{1,0:T(8,128)(2,1)S(1)}, u32[]{:S(2)}, u32[]{:S(2)}) collective-permute-start(bf16[512,1024]{1,0:T(8,128)(2,1)S(1)} %add_rows.7), channel_id=1, source_target_pairs={{0,16},{8,24},{16,0},{24,8},{32,48},{40,56},{48,32},{56,40},{64,80... | collective-permute-start | bytes 3145736 | tf_op jit(solution)/shard_map/ppermute | solution.py:50
  126.4 15.7 %collective-permute-start.24 = (bf16[128,1024]{1,0:T(8,128)(2,1)S(1)}, bf16[128,1024]{1,0:T(8,128)(2,1)S(1)}, u32[]{:S(2)}, u32[]{:S(2)}) collective-permute-start(bf16[128,1024]{1,0:T(8,128)(2,1)S(1)} %get-tuple-element.126), channel_id=1, source_target_pairs={{0,32},{8,40},{16,48},{24,56},{32,64},{40,72},{48,80},{56,88},{64,... | collective-permute-start | bytes 786440 | tf_op jit(solution)/shard_map/ppermute | solution.py:50
  127.7 14.5 %collective-permute-start.25 = (bf16[128,1024]{1,0:T(8,128)(2,1)S(1)}, bf16[128,1024]{1,0:T(8,128)(2,1)S(1)}, u32[]{:S(2)}, u32[]{:S(2)}) collective-permute-start(bf16[128,1024]{1,0:T(8,128)(2,1)S(1)} %get-tuple-element.127), channel_id=1, source_target_pairs={{0,96},{8,104},{16,112},{24,120},{32,0},{40,8},{48,16},{56,24},{64... | collective-permute-start | bytes 786440 | tf_op jit(solution)/shard_map/ppermute | solution.py:50
  137.7 25.1 %collective-permute-start.28 = (bf16[256,1024]{1,0:T(8,128)(2,1)S(1)}, bf16[256,1024]{1,0:T(8,128)(2,1)S(1)}, u32[]{:S(2)}, u32[]{:S(2)}) collective-permute-start(bf16[256,1024]{1,0:T(8,128)(2,1)S(1)} %get-tuple-element.131), channel_id=1, source_target_pairs={{0,32},{8,40},{16,48},{24,56},{32,64},{40,72},{48,80},{56,88},{64,... | collective-permute-start | bytes 1572872 | tf_op jit(solution)/shard_map/ppermute | solution.py:50
  138.2 24.5 %collective-permute-start.29 = (bf16[256,1024]{1,0:T(8,128)(2,1)S(1)}, bf16[256,1024]{1,0:T(8,128)(2,1)S(1)}, u32[]{:S(2)}, u32[]{:S(2)}) collective-permute-start(bf16[256,1024]{1,0:T(8,128)(2,1)S(1)} %get-tuple-element.139), channel_id=1, source_target_pairs={{0,96},{8,104},{16,112},{24,120},{32,0},{40,8},{48,16},{56,24},{64... | collective-permute-start | bytes 1572872 | tf_op jit(solution)/shard_map/ppermute | solution.py:50
  150.0 12.0 %collective-permute-start.26 = (bf16[512,256]{1,0:T(8,128)(2,1)S(1)}, bf16[512,256]{1,0:T(8,128)(2,1)S(1)}, u32[]{:S(2)}, u32[]{:S(2)}) collective-permute-start(bf16[512,256]{1,0:T(8,128)(2,1)S(1)} %pad_maximum_fusion.2), channel_id=1, source_target_pairs={{8,0},{16,8},{24,16},{32,24},{40,32},{48,40},{56,48},{64,56},{72,6... | collective-permute-start | bytes 786440 | tf_op jit(solution)/shard_map/ppermute | solution.py:64

commit v12 on v11

--- a/solution.py
+++ b/solution.py
@@ -518,9 +518,8 @@
     meta = positions(row, col)
     k = row % 2
 
+    g_keep = lax.dynamic_slice_in_dim(output_grad, k * half_d, half_d, 1)
     g_give = lax.dynamic_slice_in_dim(output_grad, (1 - k) * half_d, half_d, 1)
-    (output_grad,) = tied((output_grad,), g_give)
-    g_keep = lax.dynamic_slice_in_dim(output_grad, k * half_d, half_d, 1)
     kv_earlier = passed_along(jnp.concatenate([key_rows, value_rows], 1), "row", 1)
     g_got, meta = tied((move_row(g_give, dk=1), meta))
     g0 = jnp.concatenate([g_keep, g_got], 0)
@@ -536,7 +535,8 @@
     (query_held,) = tied((query_rows,), g0)
     attn_out, top, total = attend(meta, query_held, kv_earlier, key_rows, value_rows, segments)
 
-    gy, gxm, gxp, attn_out = tied((gy, gxm, gxp, attn_out))
+    gy, attn_out = tied((gy, attn_out))
+    gxm, gxp = tied((gxm, gxp), gy)
     wzm, wzp, out_proj = tied((wzm, wzp, out_proj), gxm)
 
     hw = out_proj.shape[0] // 2

time: 165 us -> 163 us (0.988)
  other arithmetic: 3.71 us -> 1.97 us
    dynamic_slice x1, local copies, waits for them, and re-layouts: 0.04 us -> 2.22 us  [local(): g_keep = lax.dynamic_slice_in_dim(output_grad, k * half_d, half_d, 1)]
  transfers between devices with their start and end apart: 30 -> 30, of which waited for: 11 -> 12; matrix products, arithmetic and copies ran while one was open for 2% -> 1% of each run, Pallas kernels for 42% -> 43%
where the time goes in v12:
time: 163 us
  Pallas kernels  71.1 us (44%)
  starting transfers between devices  49.4 us (30%)
  waiting for transfers between devices  36.8 us (23%)
  local copies, waits for them, and re-layouts  2.52 us (2%)
  other arithmetic  1.97 us (1%)
    ppermute x21, starting transfers between devices, move_row(): return lax.ppermute(value, 'row', pairs)  29.4 us
    ppermute x7, waiting for transfers between devices, move_col(): return lax.ppermute(value, 'col', pairs)  26.1 us
    pallas_call x3, Pallas kernels, attend_back(): pl.pallas_call(functools.partial(bwd_kernel, len(earlier), last), grid_sp...  20.6 us
    pallas_call x4, Pallas kernels, project(): pl.pallas_call(functools.partial(proj_kernel, tuple(slots), held, plan),...  17.7 us
    pallas_call x1, Pallas kernels, attend(): pl.pallas_call(fwd_kernel, grid_spec=pltpu.PrefetchScalarGridSpec(num_sca...  14.9 us
    pallas_call x1, Pallas kernels, attn_grad_part(): pl.pallas_call(kernel, grid_spec=pltpu.PrefetchScalarGridSpec(num_scalar_...  12.6 us
    ppermute x2, starting transfers between devices, passed_along(): lax.ppermute(value, axis, [(source, source + steps) for source in range(f...  10.9 us
    ppermute x7, starting transfers between devices, move_col(): return lax.ppermute(value, 'col', pairs)  9.05 us
  transfers between devices with their start and end apart: 30, of which 12 were waited for; matrix products, arithmetic and copies ran while one was open for 1% of the time, Pallas kernels for 43%

profile of v12, /device:TPU:1, one launch (start us, length us, event | category | flops | bytes accessed | tf_op | source)
XLA Modules:
  0.0 162.7 jit_solution(853377251205257693)
XLA Ops:
  0.6 0.0 copy-start.5
  0.6 0.0 copy-start.6
  0.7 2.2 %constant_dynamic-slice_fusion = (bf16[512,512]{1,0:T(8,128)(2,1)S(1)}, bf16[512,512]{1,0:T(8,128)(2,1)}) fusion(bf16[512,1024]{1,0:T(8,128)(2,1)} %param.13, s32[]{:T(128)S(6)} %select_n.38, s32[]{:T(128)S(6)} %select_n.32), kind=kLoop, calls=%fused_computation.13 | loop fusion | bytes 2097160 | tf_op jit(solution)/shard_map/dynamic_slice | solution.py:521
  3.0 1.4 collective-permute-start
  4.4 4.8 %collective-permute-start.2 = (bf16[512,256]{1,0:T(8,128)(2,1)S(1)}, bf16[512,256]{1,0:T(8,128)(2,1)S(1)}, u32[]{:S(2)}, u32[]{:S(2)}) collective-permute-start(bf16[512,256]{1,0:T(8,128)(2,1)S(1)} %pad_maximum_fusion.1), channel_id=1, source_target_pairs={{0,8},{8,16},{16,24},{24,32},{32,40},{40,48},{48,56},{56,64},{64,7... | collective-permute-start | bytes 786440 | tf_op jit(solution)/shard_map/ppermute | solution.py:64
  9.3 0.1 concatenate.16.meta_ref
  9.4 1.1 pad_maximum_fusion.refs_0_
  10.6 0.5 collective-permute-start.1
  11.0 1.2 collective-permute-start.5
  12.2 1.5 collective-permute-start.6
  13.7 0.7 collective-permute-done.2.kv_ref
  14.5 1.6 %collective-permute-start.10 = (bf16[512,1024]{1,0:T(8,128)(2,1)S(1)}, bf16[512,1024]{1,0:T(8,128)(2,1)S(1)}, u32[]{:S(2)}, u32[]{:S(2)}) collective-permute-start(bf16[512,1024]{1,0:T(8,128)(2,1)S(1)} %copy-done.4), channel_id=1, source_target_pairs={{0,32},{8,40},{16,48},{24,56},{32,64},{40,72},{48,80},{56,88},{64,... | collective-permute-start | bytes 3145736 | tf_op jit(solution)/shard_map/ppermute | solution.py:50
  16.1 2.1 %collective-permute-start.11 = (bf16[512,1024]{1,0:T(8,128)(2,1)S(1)}, bf16[512,1024]{1,0:T(8,128)(2,1)S(1)}, u32[]{:S(2)}, u32[]{:S(2)}) collective-permute-start(bf16[512,1024]{1,0:T(8,128)(2,1)S(1)} %copy-done.4), channel_id=1, source_target_pairs={{0,96},{8,104},{16,112},{24,120},{32,0},{40,8},{48,16},{56,24},{64... | collective-permute-start | bytes 3145736 | tf_op jit(solution)/shard_map/ppermute | solution.py:50
  18.2 14.9 %attend.1 = (bf16[512,1024]{1,0:T(8,128)(2,1)S(1)}, f32[8,1,512]{2,1,0:T(1,128)S(1)}, f32[8,1,512]{2,1,0:T(1,128)S(1)}) custom-call(s32[24]{0:T(128)S(1)} %concatenate.16.meta_ref, bf16[512,1024]{1,0:T(8,128)(2,1)S(1)} %copy-done, bf16[512,256]{1,0:T(8,128)(2,1)S(1)} %collective-permute-done.2.kv_ref, bf16[512,128]{1,0:T(8,128)(2,1)S(1)} %copy-done.2, ...), custom_call_target="tpu_custom_call" | custom-call | flops 68719476736 | bytes 8388608 | tf_op jit(solution)/shard_map/attend/pallas_call | solution.py:148
  33.1 3.0 %collective-permute-done.1.refs_3_ = bf16[1024,512]{1,0:T(8,128)(2,1)S(1)} collective-permute-done((bf16[1024,512]{1,0:T(8,128)(2,1)S(1)}, bf16[1024,512]{1,0:T(8,128)(2,1)S(1)}, u32[]{:S(2)}, u32[]{:S(2)}) %collective-permute-start.1) | collective-permute-done | bytes 1048608 | tf_op jit(solution)/shard_map/ppermute | solution.py:58
  36.1 0.6 collective-permute-done.5.refs_1_
  36.8 0.6 collective-permute-start.3
  37.4 2.4 %collective-permute-start.4 = (bf16[1024,512]{1,0:T(8,128)(2,1)S(1)}, bf16[1024,512]{1,0:T(8,128)(2,1)S(1)}, u32[]{:S(2)}, u32[]{:S(2)}) collective-permute-start(bf16[1024,512]{1,0:T(8,128)(2,1)S(1)} %collective-permute-done.1.refs_3_), channel_id=1, source_target_pairs={{0,3},{1,0},{2,1},{3,2},{4,7},{5,4},{6,5},{7,6},{8,11},{9,8},{10,9... | collective-permute-start | bytes 3145736 | tf_op jit(solution)/shard_map/ppermute | solution.py:58
  39.8 1.5 collective-permute-done.10.refs_9_
  41.3 0.0 collective-permute-start.12
  41.3 2.4 %collective-permute-start.13 = (bf16[512,1024]{1,0:T(8,128)(2,1)S(1)}, bf16[512,1024]{1,0:T(8,128)(2,1)S(1)}, u32[]{:S(2)}, u32[]{:S(2)}) collective-permute-start(bf16[512,1024]{1,0:T(8,128)(2,1)S(1)} %copy-done.4), channel_id=1, source_target_pairs={{0,16},{8,24},{16,0},{24,8},{32,48},{40,56},{48,32},{56,40},{64,80... | collective-permute-start | bytes 3145736 | tf_op jit(solution)/shard_map/ppermute | solution.py:50
  43.7 0.1 constant_dynamic-update-slice_fusion.1
  43.8 0.1 collective-permute-start.9
  43.9 0.1 constant_dynamic-update-slice_fusion.refs_4_.refs_2_.refs_1_
  43.9 6.7 %project.4.refs_3_ = bf16[2,64,256,1024]{3,2,1,0:T(8,128)(2,1)} custom-call(s32[24]{0:T(128)S(1)} %concatenate.16.meta_ref, bf16[1024,512]{1,0:T(8,128)(2,1)S(1)} %pad_maximum_fusion.refs_0_, bf16[1024,512]{1,0:T(8,128)(2,1)S(1)} %collective-permute-done.5.refs_1_, bf16[1024,512]{1,0:T(8,128)(2,1)S(1)} %collective-permute-done.6.refs_2_, ...), custom_call_target="tpu_custom_call" | custom-call | flops 4294967296 | bytes 10485760 | tf_op jit(solution)/shard_map/project/pallas_call | solution.py:324
  50.7 12.2 %collective-permute-done.3.refs_0_.refs_4_ = bf16[1024,512]{1,0:T(8,128)(2,1)S(1)} collective-permute-done((bf16[1024,512]{1,0:T(8,128)(2,1)S(1)}, bf16[1024,512]{1,0:T(8,128)(2,1)S(1)}, u32[]{:S(2)}, u32[]{:S(2)}) %collective-permute-start.3) | collective-permute-done | bytes 1048608 | tf_op jit(solution)/shard_map/ppermute | solution.py:58
  62.8 2.8 %collective-permute-start.8 = (bf16[1024,512]{1,0:T(8,128)(2,1)S(1)}, bf16[1024,512]{1,0:T(8,128)(2,1)S(1)}, u32[]{:S(2)}, u32[]{:S(2)}) collective-permute-start(bf16[1024,512]{1,0:T(8,128)(2,1)S(1)} %collective-permute-done.4.refs_1_.refs_5_), channel_id=1, source_target_pairs={{0,3},{1,0},{2,1},{3,2},{4,7},{5,4},{6,5},{7,6},{8,11},{9,8},{10,9... | collective-permute-start | bytes 3145736 | tf_op jit(solution)/shard_map/ppermute | solution.py:58
  65.7 0.5 collective-permute-done.12.refs_15_
  66.2 1.0 collective-permute-start.14
  67.2 2.3 %collective-permute-start.15 = (bf16[512,1024]{1,0:T(8,128)(2,1)S(1)}, bf16[512,1024]{1,0:T(8,128)(2,1)S(1)}, u32[]{:S(2)}, u32[]{:S(2)}) collective-permute-start(bf16[512,1024]{1,0:T(8,128)(2,1)S(1)} %collective-permute-done.13.refs_11_), channel_id=1, source_target_pairs={{0,96},{8,104},{16,112},{24,120},{32,0},{40,8},{48,16},{56,24},{64... | collective-permute-start | bytes 3145736 | tf_op jit(solution)/shard_map/ppermute | solution.py:50
  69.5 1.3 collective-permute-start.16
  70.8 4.2 %project.5.refs_2_ = bf16[2,64,256,1024]{3,2,1,0:T(8,128)(2,1)} custom-call(s32[24]{0:T(128)S(1)} %concatenate.16.meta_ref, bf16[1024,512]{1,0:T(8,128)(2,1)S(1)} %collective-permute-done.3.refs_0_.refs_4_, bf16[1024,512]{1,0:T(8,128)(2,1)S(1)} %collective-permute-done.4.refs_1_.refs_5_, ...), custom_call_target="tpu_custom_call", output_to_operand_aliasing={{}: (4, {})} | custom-call | flops 2147483648 | bytes 6291456 | tf_op jit(solution)/shard_map/project/pallas_call | solution.py:324
  75.0 10.3 %collective-permute-done.9.refs_0_.refs_6_ = bf16[1024,512]{1,0:T(8,128)(2,1)S(1)} collective-permute-done((bf16[1024,512]{1,0:T(8,128)(2,1)S(1)}, bf16[1024,512]{1,0:T(8,128)(2,1)S(1)}, u32[]{:S(2)}, u32[]{:S(2)}) %collective-permute-start.9) | collective-permute-done | bytes 1048608 | tf_op jit(solution)/shard_map/ppermute | solution.py:58
  85.3 2.8 %project.6.refs_2_ = bf16[2,64,256,1024]{3,2,1,0:T(8,128)(2,1)} custom-call(s32[24]{0:T(128)S(1)} %concatenate.16.meta_ref, bf16[1024,512]{1,0:T(8,128)(2,1)S(1)} %collective-permute-done.9.refs_0_.refs_6_, bf16[1024,1024]{1,0:T(8,128)(2,1)S(1)} %constant_dynamic-update-slice_fusion.refs_4_.refs_2_.refs_1_, ...), custom_call_target="tpu_custom_call", output_to_operand_aliasing={{}: (3, {})} | custom-call | flops 1073741824 | bytes 4194304 | tf_op jit(solution)/shard_map/project/pallas_call | solution.py:324
  88.1 3.9 %project.7 = (bf16[2,64,256,1024]{3,2,1,0:T(8,128)(2,1)}, bf16[512,1024]{1,0:T(8,128)(2,1)S(1)}, bf16[640,1024]{1,0:T(8,128)(2,1)S(1)}, bf16[640,1024]{1,0:T(8,1...) custom-call(s32[24]{0:T(128)S(1)} %concatenate.16.meta_ref, ...), custom_call_target="tpu_custom_call", output_to_operand_aliasing={{0}: (3, {})} | custom-call | flops 1073741824 | bytes 4194304 | tf_op jit(solution)/shard_map/project/pallas_call | solution.py:324
  92.1 1.3 collective-permute-start.22
  93.4 2.0 %collective-permute-start.19 = (bf16[512,1024]{1,0:T(8,128)(2,1)S(1)}, bf16[512,1024]{1,0:T(8,128)(2,1)S(1)}, u32[]{:S(2)}, u32[]{:S(2)}) collective-permute-start(bf16[512,1024]{1,0:T(8,128)(2,1)S(1)} %get-tuple-element.99), channel_id=1, source_target_pairs={{0,16},{8,24},{16,0},{24,8},{32,48},{40,56},{48,32},{56,40},{64,80... | collective-permute-start | bytes 3145736 | tf_op jit(solution)/shard_map/ppermute | solution.py:50
  95.3 1.7 %collective-permute-start.23 = (bf16[640,1024]{1,0:T(8,128)(2,1)S(1)}, bf16[640,1024]{1,0:T(8,128)(2,1)S(1)}, u32[]{:S(2)}, u32[]{:S(2)}) collective-permute-start(bf16[640,1024]{1,0:T(8,128)(2,1)S(1)} %get-tuple-element.110), channel_id=1, source_target_pairs={{0,96},{8,104},{16,112},{24,120},{32,0},{40,8},{48,16},{56,24},{64... | collective-permute-start | bytes 3932168 | tf_op jit(solution)/shard_map/ppermute | solution.py:50
  97.0 12.6 %attn_grad.1 = (f32[512,1024]{1,0:T(8,128)S(1)}, bf16[256,1024]{1,0:T(8,128)(2,1)S(1)}, bf16[256,1024]{1,0:T(8,128)(2,1)S(1)}) custom-call(s32[24]{0:T(128)S(1)} %concatenate.16.meta_ref, bf16[1024,512]{1,0:T(8,128)(2,1)S(1)} %pad_maximum_fusion.refs_0_, bf16[1024,512]{1,0:T(8,128)(2,1)S(1)} %collective-permute-done.5.refs_1_, ...), custom_call_target="tpu_custom_call" | custom-call | flops 8589934592 | bytes 20971520 | tf_op jit(solution)/shard_map/attn_grad/pallas_call | solution.py:419
  109.6 1.9 %collective-permute-start.17 = (bf16[256,1024]{1,0:T(8,128)(2,1)S(1)}, bf16[256,1024]{1,0:T(8,128)(2,1)S(1)}, u32[]{:S(2)}, u32[]{:S(2)}) collective-permute-start(bf16[256,1024]{1,0:T(8,128)(2,1)S(1)} %get-tuple-element.93), channel_id=1, source_target_pairs={{0,8},{8,0},{16,24},{24,16},{32,40},{40,32},{48,56},{56,48},{64,72... | collective-permute-start | bytes 1572872 | tf_op jit(solution)/shard_map/ppermute | solution.py:50
  111.6 0.1 collective-permute-start.18
  111.7 2.8 %fetch.1 = (bf16[512,1024]{1,0:T(8,128)(2,1)S(1)}, bf16[512,1024]{1,0:T(8,128)(2,1)S(1)}, bf16[512,1024]{1,0:T(8,128)(2,1)S(1)}, bf16[512,1024]{1,0:T(8,128)(2,1)S(1)}) custom-call(s32[24]{0:T(128)S(1)} %concatenate.16.meta_ref, bf16[2,64,256,1024]{3,2,1,0:T(8,128)(2,1)} %get-tuple-element.97.buffer_ref), custom_call_target="tpu_custom_call" | custom-call | bytes 65536 | tf_op jit(solution)/shard_map/fetch/pallas_call | solution.py:466
  114.4 0.2 add_rows.5.g_ref
  114.6 5.5 %attend_back.3 = (bf16[512,1024]{1,0:T(8,128)(2,1)}, f32[1024,128]{1,0:T(8,128)S(1)}, f32[1024,128]{1,0:T(8,128)S(1)}) custom-call(s32[24]{0:T(128)S(1)} %concatenate.16.meta_ref, bf16[512,1024]{1,0:T(8,128)(2,1)S(1)} %copy-done, bf16[512,1024]{1,0:T(8,128)(2,1)S(1)} %add_rows.5.g_ref, bf16[512,256]{1,0:T(8,128)(2,1)S(1)} %collective-permute-done.2.kv_ref, ...), custom_call_target="tpu_custom_call" | custom-call | flops 1048576 | bytes 65536 | tf_op jit(solution)/shard_map/attend_back/pallas_call | solution.py:226
  120.2 0.2 add_rows.6
  120.4 0.2 collective-permute-start.20
  120.6 2.6 %collective-permute-start.21 = (bf16[256,1024]{1,0:T(8,128)(2,1)S(1)}, bf16[256,1024]{1,0:T(8,128)(2,1)S(1)}, u32[]{:S(2)}, u32[]{:S(2)}) collective-permute-start(bf16[256,1024]{1,0:T(8,128)(2,1)S(1)} %get-tuple-element.105), channel_id=1, source_target_pairs={{0,96},{8,104},{16,112},{24,120},{32,0},{40,8},{48,16},{56,24},{64... | collective-permute-start | bytes 1572872 | tf_op jit(solution)/shard_map/ppermute | solution.py:50
  123.2 1.1 collective-permute-done.22.refs_1_.refs_4_
  124.3 0.5 collective-permute-done.23.refs_2_.refs_6_
  124.8 0.4 add_rows.7
  125.1 1.3 collective-permute-start.27
  126.4 1.5 collective-permute-start.24
  127.9 1.9 %collective-permute-start.25 = (bf16[128,1024]{1,0:T(8,128)(2,1)S(1)}, bf16[128,1024]{1,0:T(8,128)(2,1)S(1)}, u32[]{:S(2)}, u32[]{:S(2)}) collective-permute-start(bf16[128,1024]{1,0:T(8,128)(2,1)S(1)} %get-tuple-element.125), channel_id=1, source_target_pairs={{0,96},{8,104},{16,112},{24,120},{32,0},{40,8},{48,16},{56,24},{64... | collective-permute-start | bytes 786440 | tf_op jit(solution)/shard_map/ppermute | solution.py:50
  129.8 7.5 %attend_back.4 = (bf16[512,1024]{1,0:T(8,128)(2,1)}, f32[1024,128]{1,0:T(8,128)S(1)}, f32[1024,128]{1,0:T(8,128)S(1)}) custom-call(s32[24]{0:T(128)S(1)} %concatenate.16.meta_ref, bf16[512,1024]{1,0:T(8,128)(2,1)S(1)} %copy-done, bf16[512,1024]{1,0:T(8,128)(2,1)S(1)} %add_rows.5.g_ref, ...), custom_call_target="tpu_custom_call", output_to_operand_aliasing={{0}: (11, {})} | custom-call | flops 4026531840 | bytes 6291456 | tf_op jit(solution)/shard_map/attend_back/pallas_call | solution.py:226
  137.4 0.2 add_rows.8
  137.6 0.1 collective-permute-start.28
  137.7 2.7 %collective-permute-start.29 = (bf16[256,1024]{1,0:T(8,128)(2,1)S(1)}, bf16[256,1024]{1,0:T(8,128)(2,1)S(1)}, u32[]{:S(2)}, u32[]{:S(2)}) collective-permute-start(bf16[256,1024]{1,0:T(8,128)(2,1)S(1)} %get-tuple-element.137), channel_id=1, source_target_pairs={{0,96},{8,104},{16,112},{24,120},{32,0},{40,8},{48,16},{56,24},{64... | collective-permute-start | bytes 1572872 | tf_op jit(solution)/shard_map/ppermute | solution.py:50
  140.4 1.0 collective-permute-done.24.refs_5_
  141.3 0.3 collective-permute-done.25.refs_7_
  141.6 7.6 %attend_back.5 = (bf16[512,1024]{1,0:T(8,128)(2,1)}, f32[1024,128]{1,0:T(8,128)S(1)}, f32[1024,128]{1,0:T(8,128)S(1)}) custom-call(s32[24]{0:T(128)S(1)} %concatenate.16.meta_ref, bf16[512,1024]{1,0:T(8,128)(2,1)S(1)} %copy-done, bf16[512,1024]{1,0:T(8,128)(2,1)S(1)} %add_rows.5.g_ref, ...), custom_call_target="tpu_custom_call", output_to_operand_aliasing={{0}: (11, {})} | custom-call | flops 4026531840 | bytes 6291456 | tf_op jit(solution)/shard_map/attend_back/pallas_call | solution.py:226
  149.3 6.1 %collective-permute-start.26 = (bf16[512,256]{1,0:T(8,128)(2,1)S(1)}, bf16[512,256]{1,0:T(8,128)(2,1)S(1)}, u32[]{:S(2)}, u32[]{:S(2)}) collective-permute-start(bf16[512,256]{1,0:T(8,128)(2,1)S(1)} %pad_maximum_fusion.2), channel_id=1, source_target_pairs={{8,0},{16,8},{24,16},{32,24},{40,32},{48,40},{56,48},{64,56},{72,6... | collective-permute-start | bytes 786440 | tf_op jit(solution)/shard_map/ppermute | solution.py:64
  155.4 5.1 %collective-permute-done.26 = bf16[512,256]{1,0:T(8,128)(2,1)S(1)} collective-permute-done((bf16[512,256]{1,0:T(8,128)(2,1)S(1)}, bf16[512,256]{1,0:T(8,128)(2,1)S(1)}, u32[]{:S(2)}, u32[]{:S(2)}) %collective-permute-start.26) | collective-permute-done | bytes 262176 | tf_op jit(solution)/shard_map/ppermute | solution.py:64
  160.5 0.8 fusion
  161.3 1.5 add_rows.9
  (39 shorter events, 0.2 us)
Async XLA Ops:
  0.6 8.7 %copy-start.5 = (s32[8]{0:T(128)S(1)}, s32[8]{0:T(128)}, u32[]{:S(2)}) copy-start(s32[8]{0:T(128)} %constant.79.clone) | copy-start | bytes 100
  0.6 8.7 %copy-start.6 = (s32[8]{0:T(128)S(1)}, s32[8]{0:T(128)}, u32[]{:S(2)}) copy-start(s32[8]{0:T(128)} %constant.80.clone) | copy-start | bytes 100
  0.7 8.7 %copy-start.7 = (s32[8]{0:T(128)S(1)}, s32[8]{0:T(128)}, u32[]{:S(2)}) copy-start(s32[8]{0:T(128)} %constant.81.clone) | copy-start | bytes 100
  0.7 3.7 %copy-start.2 = (bf16[512,128]{1,0:T(8,128)(2,1)S(1)}, bf16[512,128]{1,0:T(8,128)(2,1)}, u32[]{:S(2)}) copy-start(bf16[512,128]{1,0:T(8,128)(2,1)} %k_ref.7) | copy-start | bytes 393220
  0.7 3.7 %copy-start.1 = (bf16[512,128]{1,0:T(8,128)(2,1)S(1)}, bf16[512,128]{1,0:T(8,128)(2,1)}, u32[]{:S(2)}) copy-start(bf16[512,128]{1,0:T(8,128)(2,1)} %v_ref.7) | copy-start | bytes 393220
  0.7 13.7 %copy-start.4 = (bf16[512,1024]{1,0:T(8,128)(2,1)S(1)}, bf16[512,1024]{1,0:T(8,128)(2,1)}, u32[]{:S(2)}) copy-start(bf16[512,1024]{1,0:T(8,128)(2,1)} %refs_8_) | copy-start | bytes 3145732
  0.7 17.5 %copy-start = (bf16[512,1024]{1,0:T(8,128)(2,1)S(1)}, bf16[512,1024]{1,0:T(8,128)(2,1)}, u32[]{:S(2)}) copy-start(bf16[512,1024]{1,0:T(8,128)(2,1)} %q_ref.6) | copy-start | bytes 3145732
  0.7 17.5 %copy-start.3 = (s32[8192]{0:T(1024)S(1)}, s32[8192]{0:T(1024)}, u32[]{:S(2)}) copy-start(s32[8192]{0:T(1024)} %param.15) | copy-start | bytes 98308
  3.0 6.5 %collective-permute-start = (bf16[512,512]{1,0:T(8,128)(2,1)}, bf16[512,512]{1,0:T(8,128)(2,1)}, u32[]{:S(2)}, u32[]{:S(2)}) collective-permute-start(bf16[512,512]{1,0:T(8,128)(2,1)} %get-tuple-element.141), channel_id=1, source_target_pairs={{0,8},{8,0},{16,24},{24,16},{32,40},{40,32},{48,56},{56,48},{64,72... | collective-permute-start | bytes 1572872 | tf_op jit(solution)/shard_map/ppermute | solution.py:50
  4.4 10.0 %collective-permute-start.2 = (bf16[512,256]{1,0:T(8,128)(2,1)S(1)}, bf16[512,256]{1,0:T(8,128)(2,1)S(1)}, u32[]{:S(2)}, u32[]{:S(2)}) collective-permute-start(bf16[512,256]{1,0:T(8,128)(2,1)S(1)} %pad_maximum_fusion.1), channel_id=1, source_target_pairs={{0,8},{8,16},{16,24},{24,32},{32,40},{40,48},{48,56},{56,64},{64,7... | collective-permute-start | bytes 786440 | tf_op jit(solution)/shard_map/ppermute | solution.py:64
  10.6 25.6 %collective-permute-start.1 = (bf16[1024,512]{1,0:T(8,128)(2,1)S(1)}, bf16[1024,512]{1,0:T(8,128)(2,1)S(1)}, u32[]{:S(2)}, u32[]{:S(2)}) collective-permute-start(bf16[1024,512]{1,0:T(8,128)(2,1)S(1)} %pad_maximum_fusion.refs_0_), channel_id=1, source_target_pairs={{0,4},{1,5},{2,6},{3,7},{4,0},{5,1},{6,2},{7,3},{8,12},{9,13},{10,... | collective-permute-start | bytes 3145736 | tf_op jit(solution)/shard_map/ppermute | solution.py:58
  11.0 25.7 %collective-permute-start.5 = (bf16[1024,512]{1,0:T(8,128)(2,1)S(1)}, bf16[1024,512]{1,0:T(8,128)(2,1)S(1)}, u32[]{:S(2)}, u32[]{:S(2)}) collective-permute-start(bf16[1024,512]{1,0:T(8,128)(2,1)S(1)} %pad_maximum_fusion.refs_0_), channel_id=1, source_target_pairs={{0,1},{1,2},{2,3},{3,0},{4,5},{5,6},{6,7},{7,4},{8,9},{9,10},{10,1... | collective-permute-start | bytes 3145736 | tf_op jit(solution)/shard_map/ppermute | solution.py:58
  12.2 25.1 %collective-permute-start.6 = (bf16[1024,512]{1,0:T(8,128)(2,1)S(1)}, bf16[1024,512]{1,0:T(8,128)(2,1)S(1)}, u32[]{:S(2)}, u32[]{:S(2)}) collective-permute-start(bf16[1024,512]{1,0:T(8,128)(2,1)S(1)} %pad_maximum_fusion.refs_0_), channel_id=1, source_target_pairs={{0,3},{1,0},{2,1},{3,2},{4,7},{5,4},{6,5},{7,6},{8,11},{9,8},{10,9... | collective-permute-start | bytes 3145736 | tf_op jit(solution)/shard_map/ppermute | solution.py:58
  14.5 26.9 %collective-permute-start.10 = (bf16[512,1024]{1,0:T(8,128)(2,1)S(1)}, bf16[512,1024]{1,0:T(8,128)(2,1)S(1)}, u32[]{:S(2)}, u32[]{:S(2)}) collective-permute-start(bf16[512,1024]{1,0:T(8,128)(2,1)S(1)} %copy-done.4), channel_id=1, source_target_pairs={{0,32},{8,40},{16,48},{24,56},{32,64},{40,72},{48,80},{56,88},{64,... | collective-permute-start | bytes 3145736 | tf_op jit(solution)/shard_map/ppermute | solution.py:50
  16.1 25.2 %collective-permute-start.11 = (bf16[512,1024]{1,0:T(8,128)(2,1)S(1)}, bf16[512,1024]{1,0:T(8,128)(2,1)S(1)}, u32[]{:S(2)}, u32[]{:S(2)}) collective-permute-start(bf16[512,1024]{1,0:T(8,128)(2,1)S(1)} %copy-done.4), channel_id=1, source_target_pairs={{0,96},{8,104},{16,112},{24,120},{32,0},{40,8},{48,16},{56,24},{64... | collective-permute-start | bytes 3145736 | tf_op jit(solution)/shard_map/ppermute | solution.py:50
  36.1 7.6 %collective-permute-start.7 = (bf16[512,1024]{1,0:T(8,128)(2,1)S(1)}, bf16[512,1024]{1,0:T(8,128)(2,1)S(1)}, u32[]{:S(2)}, u32[]{:S(2)}) collective-permute-start(bf16[512,1024]{1,0:T(8,128)(2,1)S(1)} %get-tuple-element.80), channel_id=1, source_target_pairs={{0,8},{8,0},{16,24},{24,16},{32,40},{40,32},{48,56},{56,48},{64,72... | collective-permute-start | bytes 3145736 | tf_op jit(solution)/shard_map/ppermute | solution.py:50
  36.8 26.1 %collective-permute-start.3 = (bf16[1024,512]{1,0:T(8,128)(2,1)S(1)}, bf16[1024,512]{1,0:T(8,128)(2,1)S(1)}, u32[]{:S(2)}, u32[]{:S(2)}) collective-permute-start(bf16[1024,512]{1,0:T(8,128)(2,1)S(1)} %collective-permute-done.1.refs_3_), channel_id=1, source_target_pairs={{0,1},{1,2},{2,3},{3,0},{4,5},{5,6},{6,7},{7,4},{8,9},{9,10},{10,1... | collective-permute-start | bytes 3145736 | tf_op jit(solution)/shard_map/ppermute | solution.py:58
  37.4 25.5 %collective-permute-start.4 = (bf16[1024,512]{1,0:T(8,128)(2,1)S(1)}, bf16[1024,512]{1,0:T(8,128)(2,1)S(1)}, u32[]{:S(2)}, u32[]{:S(2)}) collective-permute-start(bf16[1024,512]{1,0:T(8,128)(2,1)S(1)} %collective-permute-done.1.refs_3_), channel_id=1, source_target_pairs={{0,3},{1,0},{2,1},{3,2},{4,7},{5,4},{6,5},{7,6},{8,11},{9,8},{10,9... | collective-permute-start | bytes 3145736 | tf_op jit(solution)/shard_map/ppermute | solution.py:58
  41.3 24.8 %collective-permute-start.12 = (bf16[512,1024]{1,0:T(8,128)(2,1)S(1)}, bf16[512,1024]{1,0:T(8,128)(2,1)S(1)}, u32[]{:S(2)}, u32[]{:S(2)}) collective-permute-start(bf16[512,1024]{1,0:T(8,128)(2,1)S(1)} %collective-permute-done.10.refs_9_), channel_id=1, source_target_pairs={{0,32},{8,40},{16,48},{24,56},{32,64},{40,72},{48,80},{56,88},{64,... | collective-permute-start | bytes 3145736 | tf_op jit(solution)/shard_map/ppermute | solution.py:50
  41.3 24.8 %collective-permute-start.13 = (bf16[512,1024]{1,0:T(8,128)(2,1)S(1)}, bf16[512,1024]{1,0:T(8,128)(2,1)S(1)}, u32[]{:S(2)}, u32[]{:S(2)}) collective-permute-start(bf16[512,1024]{1,0:T(8,128)(2,1)S(1)} %copy-done.4), channel_id=1, source_target_pairs={{0,16},{8,24},{16,0},{24,8},{32,48},{40,56},{48,32},{56,40},{64,80... | collective-permute-start | bytes 3145736 | tf_op jit(solution)/shard_map/ppermute | solution.py:50
  43.8 41.5 %collective-permute-start.9 = (bf16[1024,512]{1,0:T(8,128)(2,1)S(1)}, bf16[1024,512]{1,0:T(8,128)(2,1)S(1)}, u32[]{:S(2)}, u32[]{:S(2)}) collective-permute-start(bf16[1024,512]{1,0:T(8,128)(2,1)S(1)} %collective-permute-done.5.refs_1_), channel_id=1, source_target_pairs={{0,1},{1,2},{2,3},{3,0},{4,5},{5,6},{6,7},{7,4},{8,9},{9,10},{10,1... | collective-permute-start | bytes 3145736 | tf_op jit(solution)/shard_map/ppermute | solution.py:58
  62.8 25.3 %collective-permute-start.8 = (bf16[1024,512]{1,0:T(8,128)(2,1)S(1)}, bf16[1024,512]{1,0:T(8,128)(2,1)S(1)}, u32[]{:S(2)}, u32[]{:S(2)}) collective-permute-start(bf16[1024,512]{1,0:T(8,128)(2,1)S(1)} %collective-permute-done.4.refs_1_.refs_5_), channel_id=1, source_target_pairs={{0,3},{1,0},{2,1},{3,2},{4,7},{5,4},{6,5},{7,6},{8,11},{9,8},{10,9... | collective-permute-start | bytes 3145736 | tf_op jit(solution)/shard_map/ppermute | solution.py:58
  66.2 29.2 %collective-permute-start.14 = (bf16[512,1024]{1,0:T(8,128)(2,1)S(1)}, bf16[512,1024]{1,0:T(8,128)(2,1)S(1)}, u32[]{:S(2)}, u32[]{:S(2)}) collective-permute-start(bf16[512,1024]{1,0:T(8,128)(2,1)S(1)} %collective-permute-done.13.refs_11_), channel_id=1, source_target_pairs={{0,32},{8,40},{16,48},{24,56},{32,64},{40,72},{48,80},{56,88},{64,... | collective-permute-start | bytes 3145736 | tf_op jit(solution)/shard_map/ppermute | solution.py:50
  67.2 29.8 %collective-permute-start.15 = (bf16[512,1024]{1,0:T(8,128)(2,1)S(1)}, bf16[512,1024]{1,0:T(8,128)(2,1)S(1)}, u32[]{:S(2)}, u32[]{:S(2)}) collective-permute-start(bf16[512,1024]{1,0:T(8,128)(2,1)S(1)} %collective-permute-done.13.refs_11_), channel_id=1, source_target_pairs={{0,96},{8,104},{16,112},{24,120},{32,0},{40,8},{48,16},{56,24},{64... | collective-permute-start | bytes 3145736 | tf_op jit(solution)/shard_map/ppermute | solution.py:50
  69.5 27.5 %collective-permute-start.16 = (bf16[512,1024]{1,0:T(8,128)(2,1)S(1)}, bf16[512,1024]{1,0:T(8,128)(2,1)S(1)}, u32[]{:S(2)}, u32[]{:S(2)}) collective-permute-start(bf16[512,1024]{1,0:T(8,128)(2,1)S(1)} %collective-permute-done.12.refs_15_), channel_id=1, source_target_pairs={{0,16},{8,24},{16,0},{24,8},{32,48},{40,56},{48,32},{56,40},{64,80... | collective-permute-start | bytes 3145736 | tf_op jit(solution)/shard_map/ppermute | solution.py:50
  92.1 32.2 %collective-permute-start.22 = (bf16[640,1024]{1,0:T(8,128)(2,1)S(1)}, bf16[640,1024]{1,0:T(8,128)(2,1)S(1)}, u32[]{:S(2)}, u32[]{:S(2)}) collective-permute-start(bf16[640,1024]{1,0:T(8,128)(2,1)S(1)} %get-tuple-element.84), channel_id=1, source_target_pairs={{0,32},{8,40},{16,48},{24,56},{32,64},{40,72},{48,80},{56,88},{64,... | collective-permute-start | bytes 3932168 | tf_op jit(solution)/shard_map/ppermute | solution.py:50
  93.4 26.8 %collective-permute-start.19 = (bf16[512,1024]{1,0:T(8,128)(2,1)S(1)}, bf16[512,1024]{1,0:T(8,128)(2,1)S(1)}, u32[]{:S(2)}, u32[]{:S(2)}) collective-permute-start(bf16[512,1024]{1,0:T(8,128)(2,1)S(1)} %get-tuple-element.99), channel_id=1, source_target_pairs={{0,16},{8,24},{16,0},{24,8},{32,48},{40,56},{48,32},{56,40},{64,80... | collective-permute-start | bytes 3145736 | tf_op jit(solution)/shard_map/ppermute | solution.py:50
  95.3 29.4 %collective-permute-start.23 = (bf16[640,1024]{1,0:T(8,128)(2,1)S(1)}, bf16[640,1024]{1,0:T(8,128)(2,1)S(1)}, u32[]{:S(2)}, u32[]{:S(2)}) collective-permute-start(bf16[640,1024]{1,0:T(8,128)(2,1)S(1)} %get-tuple-element.110), channel_id=1, source_target_pairs={{0,96},{8,104},{16,112},{24,120},{32,0},{40,8},{48,16},{56,24},{64... | collective-permute-start | bytes 3932168 | tf_op jit(solution)/shard_map/ppermute | solution.py:50
  109.6 4.8 %collective-permute-start.17 = (bf16[256,1024]{1,0:T(8,128)(2,1)S(1)}, bf16[256,1024]{1,0:T(8,128)(2,1)S(1)}, u32[]{:S(2)}, u32[]{:S(2)}) collective-permute-start(bf16[256,1024]{1,0:T(8,128)(2,1)S(1)} %get-tuple-element.93), channel_id=1, source_target_pairs={{0,8},{8,0},{16,24},{24,16},{32,40},{40,32},{48,56},{56,48},{64,72... | collective-permute-start | bytes 1572872 | tf_op jit(solution)/shard_map/ppermute | solution.py:50
  111.6 2.9 %collective-permute-start.18 = (bf16[256,1024]{1,0:T(8,128)(2,1)S(1)}, bf16[256,1024]{1,0:T(8,128)(2,1)S(1)}, u32[]{:S(2)}, u32[]{:S(2)}) collective-permute-start(bf16[256,1024]{1,0:T(8,128)(2,1)S(1)} %get-tuple-element.94), channel_id=1, source_target_pairs={{0,8},{8,0},{16,24},{24,16},{32,40},{40,32},{48,56},{56,48},{64,72... | collective-permute-start | bytes 1572872 | tf_op jit(solution)/shard_map/ppermute | solution.py:50
  120.4 17.0 %collective-permute-start.20 = (bf16[256,1024]{1,0:T(8,128)(2,1)S(1)}, bf16[256,1024]{1,0:T(8,128)(2,1)S(1)}, u32[]{:S(2)}, u32[]{:S(2)}) collective-permute-start(bf16[256,1024]{1,0:T(8,128)(2,1)S(1)} %get-tuple-element.104), channel_id=1, source_target_pairs={{0,32},{8,40},{16,48},{24,56},{32,64},{40,72},{48,80},{56,88},{64,... | collective-permute-start | bytes 1572872 | tf_op jit(solution)/shard_map/ppermute | solution.py:50
  120.6 16.8 %collective-permute-start.21 = (bf16[256,1024]{1,0:T(8,128)(2,1)S(1)}, bf16[256,1024]{1,0:T(8,128)(2,1)S(1)}, u32[]{:S(2)}, u32[]{:S(2)}) collective-permute-start(bf16[256,1024]{1,0:T(8,128)(2,1)S(1)} %get-tuple-element.105), channel_id=1, source_target_pairs={{0,96},{8,104},{16,112},{24,120},{32,0},{40,8},{48,16},{56,24},{64... | collective-permute-start | bytes 1572872 | tf_op jit(solution)/shard_map/ppermute | solution.py:50
  125.1 36.1 %collective-permute-start.27 = (bf16[512,1024]{1,0:T(8,128)(2,1)S(1)}, bf16[512,1024]{1,0:T(8,128)(2,1)S(1)}, u32[]{:S(2)}, u32[]{:S(2)}) collective-permute-start(bf16[512,1024]{1,0:T(8,128)(2,1)S(1)} %add_rows.7), channel_id=1, source_target_pairs={{0,16},{8,24},{16,0},{24,8},{32,48},{40,56},{48,32},{56,40},{64,80... | collective-permute-start | bytes 3145736 | tf_op jit(solution)/shard_map/ppermute | solution.py:50
  126.4 14.9 %collective-permute-start.24 = (bf16[128,1024]{1,0:T(8,128)(2,1)S(1)}, bf16[128,1024]{1,0:T(8,128)(2,1)S(1)}, u32[]{:S(2)}, u32[]{:S(2)}) collective-permute-start(bf16[128,1024]{1,0:T(8,128)(2,1)S(1)} %get-tuple-element.124), channel_id=1, source_target_pairs={{0,32},{8,40},{16,48},{24,56},{32,64},{40,72},{48,80},{56,88},{64,... | collective-permute-start | bytes 786440 | tf_op jit(solution)/shard_map/ppermute | solution.py:50
  127.9 13.7 %collective-permute-start.25 = (bf16[128,1024]{1,0:T(8,128)(2,1)S(1)}, bf16[128,1024]{1,0:T(8,128)(2,1)S(1)}, u32[]{:S(2)}, u32[]{:S(2)}) collective-permute-start(bf16[128,1024]{1,0:T(8,128)(2,1)S(1)} %get-tuple-element.125), channel_id=1, source_target_pairs={{0,96},{8,104},{16,112},{24,120},{32,0},{40,8},{48,16},{56,24},{64... | collective-permute-start | bytes 786440 | tf_op jit(solution)/shard_map/ppermute | solution.py:50
  137.6 23.6 %collective-permute-start.28 = (bf16[256,1024]{1,0:T(8,128)(2,1)S(1)}, bf16[256,1024]{1,0:T(8,128)(2,1)S(1)}, u32[]{:S(2)}, u32[]{:S(2)}) collective-permute-start(bf16[256,1024]{1,0:T(8,128)(2,1)S(1)} %get-tuple-element.129), channel_id=1, source_target_pairs={{0,32},{8,40},{16,48},{24,56},{32,64},{40,72},{48,80},{56,88},{64,... | collective-permute-start | bytes 1572872 | tf_op jit(solution)/shard_map/ppermute | solution.py:50
  137.7 23.6 %collective-permute-start.29 = (bf16[256,1024]{1,0:T(8,128)(2,1)S(1)}, bf16[256,1024]{1,0:T(8,128)(2,1)S(1)}, u32[]{:S(2)}, u32[]{:S(2)}) collective-permute-start(bf16[256,1024]{1,0:T(8,128)(2,1)S(1)} %get-tuple-element.137), channel_id=1, source_target_pairs={{0,96},{8,104},{16,112},{24,120},{32,0},{40,8},{48,16},{56,24},{64... | collective-permute-start | bytes 1572872 | tf_op jit(solution)/shard_map/ppermute | solution.py:50
  149.3 11.2 %collective-permute-start.26 = (bf16[512,256]{1,0:T(8,128)(2,1)S(1)}, bf16[512,256]{1,0:T(8,128)(2,1)S(1)}, u32[]{:S(2)}, u32[]{:S(2)}) collective-permute-start(bf16[512,256]{1,0:T(8,128)(2,1)S(1)} %pad_maximum_fusion.2), channel_id=1, source_target_pairs={{8,0},{16,8},{24,16},{32,24},{40,32},{48,40},{56,48},{64,56},{72,6... | collective-permute-start | bytes 786440 | tf_op jit(solution)/shard_map/ppermute | solution.py:64

commit v13 on v12

--- a/solution.py
+++ b/solution.py
@@ -605,7 +605,7 @@
         attend_back, meta, query_rows, attn_grad, kv_earlier, key_rows, value_rows, segments, top, total
     )
     heads = query_rows.shape[1] // HD
-    cuts = heads // 4, 5 * heads // 8
+    cuts = heads // 4, heads // 2
     held = part((0, cuts[0]), None)
 
     ry, *held = tied((ry, *held))
@@ -635,10 +635,7 @@
     query_grad, dkey, dvalue = part((cuts[1], heads), held)
     back = passed_along(
         jnp.concatenate([dkey[:count], dvalue[:count]], 1).astype(BF), "row", -1
-    ).astype(F32)
-    key_grad = (dkey[count:] + back[:, :HD]).astype(BF)
-    value_grad = (dvalue[count:] + back[:, HD:]).astype(BF)
-
+    )
     (proj_grad,) = add_rows(
         [own, across, nup, ndn, rup, up2, rdn, dn2],
         (
@@ -649,6 +646,10 @@
         ),
         result=True,
     )
+    proj_grad, back = tied((proj_grad, back))
+    back = back.astype(F32)
+    key_grad = (dkey[count:] + back[:, :HD]).astype(BF)
+    value_grad = (dvalue[count:] + back[:, HD:]).astype(BF)
     return (query_grad, key_grad, value_grad, proj_grad)
 
 

time: 163 us -> 165 us (1.012)
  waiting for transfers between devices: 36.8 us -> 39.6 us
    ppermute x21, waiting for transfers between devices: 4.9 us -> 8.27 us  [move_row(): return lax.ppermute(value, 'row', pairs)]
  transfers between devices with their start and end apart: 30 -> 30, of which waited for: 12 -> 14; matrix products, arithmetic and copies ran while one was open for 1% -> 1% of each run, Pallas kernels for 43% -> 43%
where the time goes in v13:
time: 165 us
  Pallas kernels  71.1 us (43%)
  starting transfers between devices  48.8 us (30%)
  waiting for transfers between devices  39.6 us (24%)
  local copies, waits for them, and re-layouts  2.52 us (2%)
  other arithmetic  1.97 us (1%)
    ppermute x21, starting transfers between devices, move_row(): return lax.ppermute(value, 'row', pairs)  30.4 us
    ppermute x7, waiting for transfers between devices, move_col(): return lax.ppermute(value, 'col', pairs)  26.1 us
    pallas_call x3, Pallas kernels, attend_back(): pl.pallas_call(functools.partial(bwd_kernel, len(earlier), last), grid_sp...  20.6 us
    pallas_call x4, Pallas kernels, project(): pl.pallas_call(functools.partial(proj_kernel, tuple(slots), held, plan),...  17.7 us
    pallas_call x1, Pallas kernels, attend(): pl.pallas_call(fwd_kernel, grid_spec=pltpu.PrefetchScalarGridSpec(num_sca...  14.9 us
    pallas_call x1, Pallas kernels, attn_grad_part(): pl.pallas_call(kernel, grid_spec=pltpu.PrefetchScalarGridSpec(num_scalar_...  12.6 us
    ppermute x2, starting transfers between devices, passed_along(): lax.ppermute(value, axis, [(source, source + steps) for source in range(f...  9.26 us
    ppermute x7, starting transfers between devices, move_col(): return lax.ppermute(value, 'col', pairs)  9.05 us
  transfers between devices with their start and end apart: 30, of which 14 were waited for; matrix products, arithmetic and copies ran while one was open for 1% of the time, Pallas kernels for 43%

profile of v13, /device:TPU:1, one launch (start us, length us, event | category | flops | bytes accessed | tf_op | source)
XLA Modules:
  0.0 164.9 jit_solution(2104972517509234477)
XLA Ops:
  0.7 2.2 %constant_dynamic-slice_fusion = (bf16[512,512]{1,0:T(8,128)(2,1)S(1)}, bf16[512,512]{1,0:T(8,128)(2,1)}) fusion(bf16[512,1024]{1,0:T(8,128)(2,1)} %param.13, s32[]{:T(128)S(6)} %select_n.38, s32[]{:T(128)S(6)} %select_n.32), kind=kLoop, calls=%fused_computation.13 | loop fusion | bytes 2097160 | tf_op jit(solution)/shard_map/dynamic_slice | solution.py:521
  3.0 1.4 collective-permute-start
  4.4 4.8 %collective-permute-start.2 = (bf16[512,256]{1,0:T(8,128)(2,1)S(1)}, bf16[512,256]{1,0:T(8,128)(2,1)S(1)}, u32[]{:S(2)}, u32[]{:S(2)}) collective-permute-start(bf16[512,256]{1,0:T(8,128)(2,1)S(1)} %pad_maximum_fusion.1), channel_id=1, source_target_pairs={{0,8},{8,16},{16,24},{24,32},{32,40},{40,48},{48,56},{56,64},{64,7... | collective-permute-start | bytes 786440 | tf_op jit(solution)/shard_map/ppermute | solution.py:64
  9.3 0.1 concatenate.16.meta_ref
  9.4 1.1 pad_maximum_fusion.refs_0_
  10.6 0.5 collective-permute-start.1
  11.0 1.2 collective-permute-start.5
  12.2 1.5 collective-permute-start.6
  13.7 0.7 collective-permute-done.2.kv_ref
  14.5 1.6 collective-permute-start.10
  16.1 2.1 %collective-permute-start.11 = (bf16[512,1024]{1,0:T(8,128)(2,1)S(1)}, bf16[512,1024]{1,0:T(8,128)(2,1)S(1)}, u32[]{:S(2)}, u32[]{:S(2)}) collective-permute-start(bf16[512,1024]{1,0:T(8,128)(2,1)S(1)} %copy-done.4), channel_id=1, source_target_pairs={{0,96},{8,104},{16,112},{24,120},{32,0},{40,8},{48,16},{56,24},{64... | collective-permute-start | bytes 3145736 | tf_op jit(solution)/shard_map/ppermute | solution.py:50
  18.2 14.9 %attend.1 = (bf16[512,1024]{1,0:T(8,128)(2,1)S(1)}, f32[8,1,512]{2,1,0:T(1,128)S(1)}, f32[8,1,512]{2,1,0:T(1,128)S(1)}) custom-call(s32[24]{0:T(128)S(1)} %concatenate.16.meta_ref, bf16[512,1024]{1,0:T(8,128)(2,1)S(1)} %copy-done, bf16[512,256]{1,0:T(8,128)(2,1)S(1)} %collective-permute-done.2.kv_ref, bf16[512,128]{1,0:T(8,128)(2,1)S(1)} %copy-done.2, ...), custom_call_target="tpu_custom_call" | custom-call | flops 68719476736 | bytes 8388608 | tf_op jit(solution)/shard_map/attend/pallas_call | solution.py:148
  33.1 3.0 %collective-permute-done.1.refs_3_ = bf16[1024,512]{1,0:T(8,128)(2,1)S(1)} collective-permute-done((bf16[1024,512]{1,0:T(8,128)(2,1)S(1)}, bf16[1024,512]{1,0:T(8,128)(2,1)S(1)}, u32[]{:S(2)}, u32[]{:S(2)}) %collective-permute-start.1) | collective-permute-done | bytes 1048608 | tf_op jit(solution)/shard_map/ppermute | solution.py:58
  36.1 0.6 collective-permute-done.5.refs_1_
  36.8 0.6 collective-permute-start.3
  37.4 2.4 %collective-permute-start.4 = (bf16[1024,512]{1,0:T(8,128)(2,1)S(1)}, bf16[1024,512]{1,0:T(8,128)(2,1)S(1)}, u32[]{:S(2)}, u32[]{:S(2)}) collective-permute-start(bf16[1024,512]{1,0:T(8,128)(2,1)S(1)} %collective-permute-done.1.refs_3_), channel_id=1, source_target_pairs={{0,3},{1,0},{2,1},{3,2},{4,7},{5,4},{6,5},{7,6},{8,11},{9,8},{10,9... | collective-permute-start | bytes 3145736 | tf_op jit(solution)/shard_map/ppermute | solution.py:58
  39.8 1.5 collective-permute-done.10.refs_9_
  41.3 0.0 collective-permute-start.12
  41.3 2.4 %collective-permute-start.13 = (bf16[512,1024]{1,0:T(8,128)(2,1)S(1)}, bf16[512,1024]{1,0:T(8,128)(2,1)S(1)}, u32[]{:S(2)}, u32[]{:S(2)}) collective-permute-start(bf16[512,1024]{1,0:T(8,128)(2,1)S(1)} %copy-done.4), channel_id=1, source_target_pairs={{0,16},{8,24},{16,0},{24,8},{32,48},{40,56},{48,32},{56,40},{64,80... | collective-permute-start | bytes 3145736 | tf_op jit(solution)/shard_map/ppermute | solution.py:50
  43.7 0.1 constant_dynamic-update-slice_fusion.1
  43.8 0.1 collective-permute-start.9
  43.9 0.1 constant_dynamic-update-slice_fusion.refs_4_.refs_2_.refs_1_
  43.9 6.7 %project.4.refs_3_ = bf16[2,64,256,1024]{3,2,1,0:T(8,128)(2,1)} custom-call(s32[24]{0:T(128)S(1)} %concatenate.16.meta_ref, bf16[1024,512]{1,0:T(8,128)(2,1)S(1)} %pad_maximum_fusion.refs_0_, bf16[1024,512]{1,0:T(8,128)(2,1)S(1)} %collective-permute-done.5.refs_1_, bf16[1024,512]{1,0:T(8,128)(2,1)S(1)} %collective-permute-done.6.refs_2_, ...), custom_call_target="tpu_custom_call" | custom-call | flops 4294967296 | bytes 10485760 | tf_op jit(solution)/shard_map/project/pallas_call | solution.py:324
  50.7 12.2 %collective-permute-done.3.refs_0_.refs_4_ = bf16[1024,512]{1,0:T(8,128)(2,1)S(1)} collective-permute-done((bf16[1024,512]{1,0:T(8,128)(2,1)S(1)}, bf16[1024,512]{1,0:T(8,128)(2,1)S(1)}, u32[]{:S(2)}, u32[]{:S(2)}) %collective-permute-start.3) | collective-permute-done | bytes 1048608 | tf_op jit(solution)/shard_map/ppermute | solution.py:58
  62.8 2.8 %collective-permute-start.8 = (bf16[1024,512]{1,0:T(8,128)(2,1)S(1)}, bf16[1024,512]{1,0:T(8,128)(2,1)S(1)}, u32[]{:S(2)}, u32[]{:S(2)}) collective-permute-start(bf16[1024,512]{1,0:T(8,128)(2,1)S(1)} %collective-permute-done.4.refs_1_.refs_5_), channel_id=1, source_target_pairs={{0,3},{1,0},{2,1},{3,2},{4,7},{5,4},{6,5},{7,6},{8,11},{9,8},{10,9... | collective-permute-start | bytes 3145736 | tf_op jit(solution)/shard_map/ppermute | solution.py:58
  65.7 0.5 collective-permute-done.12.refs_15_
  66.2 1.0 collective-permute-start.14
  67.2 2.3 %collective-permute-start.15 = (bf16[512,1024]{1,0:T(8,128)(2,1)S(1)}, bf16[512,1024]{1,0:T(8,128)(2,1)S(1)}, u32[]{:S(2)}, u32[]{:S(2)}) collective-permute-start(bf16[512,1024]{1,0:T(8,128)(2,1)S(1)} %collective-permute-done.13.refs_11_), channel_id=1, source_target_pairs={{0,96},{8,104},{16,112},{24,120},{32,0},{40,8},{48,16},{56,24},{64... | collective-permute-start | bytes 3145736 | tf_op jit(solution)/shard_map/ppermute | solution.py:50
  69.5 1.3 collective-permute-start.16
  70.8 4.2 %project.5.refs_2_ = bf16[2,64,256,1024]{3,2,1,0:T(8,128)(2,1)} custom-call(s32[24]{0:T(128)S(1)} %concatenate.16.meta_ref, bf16[1024,512]{1,0:T(8,128)(2,1)S(1)} %collective-permute-done.3.refs_0_.refs_4_, bf16[1024,512]{1,0:T(8,128)(2,1)S(1)} %collective-permute-done.4.refs_1_.refs_5_, ...), custom_call_target="tpu_custom_call", output_to_operand_aliasing={{}: (4, {})} | custom-call | flops 2147483648 | bytes 6291456 | tf_op jit(solution)/shard_map/project/pallas_call | solution.py:324
  75.0 10.3 %collective-permute-done.9.refs_0_.refs_6_ = bf16[1024,512]{1,0:T(8,128)(2,1)S(1)} collective-permute-done((bf16[1024,512]{1,0:T(8,128)(2,1)S(1)}, bf16[1024,512]{1,0:T(8,128)(2,1)S(1)}, u32[]{:S(2)}, u32[]{:S(2)}) %collective-permute-start.9) | collective-permute-done | bytes 1048608 | tf_op jit(solution)/shard_map/ppermute | solution.py:58
  85.3 2.8 %project.6.refs_2_ = bf16[2,64,256,1024]{3,2,1,0:T(8,128)(2,1)} custom-call(s32[24]{0:T(128)S(1)} %concatenate.16.meta_ref, bf16[1024,512]{1,0:T(8,128)(2,1)S(1)} %collective-permute-done.9.refs_0_.refs_6_, bf16[1024,1024]{1,0:T(8,128)(2,1)S(1)} %constant_dynamic-update-slice_fusion.refs_4_.refs_2_.refs_1_, ...), custom_call_target="tpu_custom_call", output_to_operand_aliasing={{}: (3, {})} | custom-call | flops 1073741824 | bytes 4194304 | tf_op jit(solution)/shard_map/project/pallas_call | solution.py:324
  88.1 3.9 %project.7 = (bf16[2,64,256,1024]{3,2,1,0:T(8,128)(2,1)}, bf16[512,1024]{1,0:T(8,128)(2,1)S(1)}, bf16[640,1024]{1,0:T(8,128)(2,1)S(1)}, bf16[640,1024]{1,0:T(8,1...) custom-call(s32[24]{0:T(128)S(1)} %concatenate.16.meta_ref, ...), custom_call_target="tpu_custom_call", output_to_operand_aliasing={{0}: (3, {})} | custom-call | flops 1073741824 | bytes 4194304 | tf_op jit(solution)/shard_map/project/pallas_call | solution.py:324
  92.1 1.3 collective-permute-start.22
  93.4 2.0 %collective-permute-start.19 = (bf16[512,1024]{1,0:T(8,128)(2,1)S(1)}, bf16[512,1024]{1,0:T(8,128)(2,1)S(1)}, u32[]{:S(2)}, u32[]{:S(2)}) collective-permute-start(bf16[512,1024]{1,0:T(8,128)(2,1)S(1)} %get-tuple-element.101), channel_id=1, source_target_pairs={{0,16},{8,24},{16,0},{24,8},{32,48},{40,56},{48,32},{56,40},{64,80... | collective-permute-start | bytes 3145736 | tf_op jit(solution)/shard_map/ppermute | solution.py:50
  95.3 1.7 %collective-permute-start.23 = (bf16[640,1024]{1,0:T(8,128)(2,1)S(1)}, bf16[640,1024]{1,0:T(8,128)(2,1)S(1)}, u32[]{:S(2)}, u32[]{:S(2)}) collective-permute-start(bf16[640,1024]{1,0:T(8,128)(2,1)S(1)} %get-tuple-element.112), channel_id=1, source_target_pairs={{0,96},{8,104},{16,112},{24,120},{32,0},{40,8},{48,16},{56,24},{64... | collective-permute-start | bytes 3932168 | tf_op jit(solution)/shard_map/ppermute | solution.py:50
  97.0 12.6 %attn_grad.1 = (f32[512,1024]{1,0:T(8,128)S(1)}, bf16[256,1024]{1,0:T(8,128)(2,1)S(1)}, bf16[256,1024]{1,0:T(8,128)(2,1)S(1)}) custom-call(s32[24]{0:T(128)S(1)} %concatenate.16.meta_ref, bf16[1024,512]{1,0:T(8,128)(2,1)S(1)} %pad_maximum_fusion.refs_0_, bf16[1024,512]{1,0:T(8,128)(2,1)S(1)} %collective-permute-done.5.refs_1_, ...), custom_call_target="tpu_custom_call" | custom-call | flops 8589934592 | bytes 20971520 | tf_op jit(solution)/shard_map/attn_grad/pallas_call | solution.py:419
  109.6 1.9 %collective-permute-start.17 = (bf16[256,1024]{1,0:T(8,128)(2,1)S(1)}, bf16[256,1024]{1,0:T(8,128)(2,1)S(1)}, u32[]{:S(2)}, u32[]{:S(2)}) collective-permute-start(bf16[256,1024]{1,0:T(8,128)(2,1)S(1)} %get-tuple-element.95), channel_id=1, source_target_pairs={{0,8},{8,0},{16,24},{24,16},{32,40},{40,32},{48,56},{56,48},{64,72... | collective-permute-start | bytes 1572872 | tf_op jit(solution)/shard_map/ppermute | solution.py:50
  111.6 0.1 collective-permute-start.18
  111.7 2.8 %fetch.1 = (bf16[512,1024]{1,0:T(8,128)(2,1)S(1)}, bf16[512,1024]{1,0:T(8,128)(2,1)S(1)}, bf16[512,1024]{1,0:T(8,128)(2,1)S(1)}, bf16[512,1024]{1,0:T(8,128)(2,1)S(1)}) custom-call(s32[24]{0:T(128)S(1)} %concatenate.16.meta_ref, bf16[2,64,256,1024]{3,2,1,0:T(8,128)(2,1)} %get-tuple-element.99.buffer_ref), custom_call_target="tpu_custom_call" | custom-call | bytes 65536 | tf_op jit(solution)/shard_map/fetch/pallas_call | solution.py:466
  114.4 0.2 add_rows.5.g_ref
  114.6 5.5 %attend_back.3 = (bf16[512,1024]{1,0:T(8,128)(2,1)}, f32[1024,128]{1,0:T(8,128)S(1)}, f32[1024,128]{1,0:T(8,128)S(1)}) custom-call(s32[24]{0:T(128)S(1)} %concatenate.16.meta_ref, bf16[512,1024]{1,0:T(8,128)(2,1)S(1)} %copy-done, bf16[512,1024]{1,0:T(8,128)(2,1)S(1)} %add_rows.5.g_ref, bf16[512,256]{1,0:T(8,128)(2,1)S(1)} %collective-permute-done.2.kv_ref, ...), custom_call_target="tpu_custom_call" | custom-call | flops 1048576 | bytes 65536 | tf_op jit(solution)/shard_map/attend_back/pallas_call | solution.py:226
  120.2 0.2 add_rows.6
  120.4 0.2 collective-permute-start.20
  120.6 2.6 %collective-permute-start.21 = (bf16[256,1024]{1,0:T(8,128)(2,1)S(1)}, bf16[256,1024]{1,0:T(8,128)(2,1)S(1)}, u32[]{:S(2)}, u32[]{:S(2)}) collective-permute-start(bf16[256,1024]{1,0:T(8,128)(2,1)S(1)} %get-tuple-element.107), channel_id=1, source_target_pairs={{0,96},{8,104},{16,112},{24,120},{32,0},{40,8},{48,16},{56,24},{64... | collective-permute-start | bytes 1572872 | tf_op jit(solution)/shard_map/ppermute | solution.py:50
  123.2 1.1 collective-permute-done.22.refs_1_.refs_4_
  124.3 0.5 collective-permute-done.23.refs_2_.refs_6_
  124.8 1.3 collective-permute-start.24
  126.0 1.4 collective-permute-start.25
  127.4 0.4 add_rows.7
  127.8 2.0 %collective-permute-start.26 = (bf16[512,1024]{1,0:T(8,128)(2,1)S(1)}, bf16[512,1024]{1,0:T(8,128)(2,1)S(1)}, u32[]{:S(2)}, u32[]{:S(2)}) collective-permute-start(bf16[512,1024]{1,0:T(8,128)(2,1)S(1)} %add_rows.7), channel_id=1, source_target_pairs={{0,16},{8,24},{16,0},{24,8},{32,48},{40,56},{48,32},{56,40},{64,80... | collective-permute-start | bytes 3145736 | tf_op jit(solution)/shard_map/ppermute | solution.py:50
  129.8 5.5 %attend_back.4 = (bf16[512,1024]{1,0:T(8,128)(2,1)}, f32[1024,128]{1,0:T(8,128)S(1)}, f32[1024,128]{1,0:T(8,128)S(1)}) custom-call(s32[24]{0:T(128)S(1)} %concatenate.16.meta_ref, bf16[512,1024]{1,0:T(8,128)(2,1)S(1)} %copy-done, bf16[512,1024]{1,0:T(8,128)(2,1)S(1)} %add_rows.5.g_ref, ...), custom_call_target="tpu_custom_call", output_to_operand_aliasing={{0}: (11, {})} | custom-call | flops 2684354560 | bytes 6291456 | tf_op jit(solution)/shard_map/attend_back/pallas_call | solution.py:226
  135.4 0.3 collective-permute-done.20.refs_1_
  135.7 0.3 collective-permute-done.21.refs_2_
  136.0 0.2 add_rows.8
  136.2 1.4 collective-permute-start.27
  137.6 3.7 %collective-permute-done.24.refs_5_ = bf16[128,1024]{1,0:T(8,128)(2,1)S(1)} collective-permute-done((bf16[128,1024]{1,0:T(8,128)(2,1)S(1)}, bf16[128,1024]{1,0:T(8,128)(2,1)S(1)}, u32[]{:S(2)}, u32[]{:S(2)}) %collective-permute-start.24) | collective-permute-done | bytes 262176 | tf_op jit(solution)/shard_map/ppermute | solution.py:50
  141.3 0.3 collective-permute-done.25.refs_7_
  141.6 2.4 %collective-permute-start.28 = (bf16[256,1024]{1,0:T(8,128)(2,1)S(1)}, bf16[256,1024]{1,0:T(8,128)(2,1)S(1)}, u32[]{:S(2)}, u32[]{:S(2)}) collective-permute-start(bf16[256,1024]{1,0:T(8,128)(2,1)S(1)} %get-tuple-element.138), channel_id=1, source_target_pairs={{0,96},{8,104},{16,112},{24,120},{32,0},{40,8},{48,16},{56,24},{64... | collective-permute-start | bytes 1572872 | tf_op jit(solution)/shard_map/ppermute | solution.py:50
  144.0 9.6 %attend_back.5 = (bf16[512,1024]{1,0:T(8,128)(2,1)}, f32[1024,128]{1,0:T(8,128)S(1)}, f32[1024,128]{1,0:T(8,128)S(1)}) custom-call(s32[24]{0:T(128)S(1)} %concatenate.16.meta_ref, bf16[512,1024]{1,0:T(8,128)(2,1)S(1)} %copy-done, bf16[512,1024]{1,0:T(8,128)(2,1)S(1)} %add_rows.5.g_ref, ...), custom_call_target="tpu_custom_call", output_to_operand_aliasing={{0}: (11, {})} | custom-call | flops 5368709120 | bytes 6291456 | tf_op jit(solution)/shard_map/attend_back/pallas_call | solution.py:226
  153.7 4.5 %collective-permute-start.29 = (bf16[512,256]{1,0:T(8,128)(2,1)S(1)}, bf16[512,256]{1,0:T(8,128)(2,1)S(1)}, u32[]{:S(2)}, u32[]{:S(2)}) collective-permute-start(bf16[512,256]{1,0:T(8,128)(2,1)S(1)} %pad_maximum_fusion.2), channel_id=1, source_target_pairs={{8,0},{16,8},{24,16},{32,24},{40,32},{48,40},{56,48},{64,56},{72,6... | collective-permute-start | bytes 786440 | tf_op jit(solution)/shard_map/ppermute | solution.py:64
  158.2 1.5 add_rows.9
  159.6 4.5 %collective-permute-done.29 = bf16[512,256]{1,0:T(8,128)(2,1)S(1)} collective-permute-done((bf16[512,256]{1,0:T(8,128)(2,1)S(1)}, bf16[512,256]{1,0:T(8,128)(2,1)S(1)}, u32[]{:S(2)}, u32[]{:S(2)}) %collective-permute-start.29) | collective-permute-done | bytes 262176 | tf_op jit(solution)/shard_map/ppermute | solution.py:64
  164.2 0.8 fusion
  (39 shorter events, 0.2 us)
Async XLA Ops:
  0.6 8.7 %copy-start.5 = (s32[8]{0:T(128)S(1)}, s32[8]{0:T(128)}, u32[]{:S(2)}) copy-start(s32[8]{0:T(128)} %constant.79.clone) | copy-start | bytes 100
  0.6 8.7 %copy-start.6 = (s32[8]{0:T(128)S(1)}, s32[8]{0:T(128)}, u32[]{:S(2)}) copy-start(s32[8]{0:T(128)} %constant.80.clone) | copy-start | bytes 100
  0.7 8.7 %copy-start.7 = (s32[8]{0:T(128)S(1)}, s32[8]{0:T(128)}, u32[]{:S(2)}) copy-start(s32[8]{0:T(128)} %constant.81.clone) | copy-start | bytes 100
  0.7 3.7 %copy-start.2 = (bf16[512,128]{1,0:T(8,128)(2,1)S(1)}, bf16[512,128]{1,0:T(8,128)(2,1)}, u32[]{:S(2)}) copy-start(bf16[512,128]{1,0:T(8,128)(2,1)} %k_ref.7) | copy-start | bytes 393220
  0.7 3.7 %copy-start.1 = (bf16[512,128]{1,0:T(8,128)(2,1)S(1)}, bf16[512,128]{1,0:T(8,128)(2,1)}, u32[]{:S(2)}) copy-start(bf16[512,128]{1,0:T(8,128)(2,1)} %v_ref.7) | copy-start | bytes 393220
  0.7 13.7 %copy-start.4 = (bf16[512,1024]{1,0:T(8,128)(2,1)S(1)}, bf16[512,1024]{1,0:T(8,128)(2,1)}, u32[]{:S(2)}) copy-start(bf16[512,1024]{1,0:T(8,128)(2,1)} %refs_8_) | copy-start | bytes 3145732
  0.7 17.5 %copy-start = (bf16[512,1024]{1,0:T(8,128)(2,1)S(1)}, bf16[512,1024]{1,0:T(8,128)(2,1)}, u32[]{:S(2)}) copy-start(bf16[512,1024]{1,0:T(8,128)(2,1)} %q_ref.6) | copy-start | bytes 3145732
  0.7 17.5 %copy-start.3 = (s32[8192]{0:T(1024)S(1)}, s32[8192]{0:T(1024)}, u32[]{:S(2)}) copy-start(s32[8192]{0:T(1024)} %param.15) | copy-start | bytes 98308
  3.0 6.5 %collective-permute-start = (bf16[512,512]{1,0:T(8,128)(2,1)}, bf16[512,512]{1,0:T(8,128)(2,1)}, u32[]{:S(2)}, u32[]{:S(2)}) collective-permute-start(bf16[512,512]{1,0:T(8,128)(2,1)} %get-tuple-element.145), channel_id=1, source_target_pairs={{0,8},{8,0},{16,24},{24,16},{32,40},{40,32},{48,56},{56,48},{64,72... | collective-permute-start | bytes 1572872 | tf_op jit(solution)/shard_map/ppermute | solution.py:50
  4.4 10.0 %collective-permute-start.2 = (bf16[512,256]{1,0:T(8,128)(2,1)S(1)}, bf16[512,256]{1,0:T(8,128)(2,1)S(1)}, u32[]{:S(2)}, u32[]{:S(2)}) collective-permute-start(bf16[512,256]{1,0:T(8,128)(2,1)S(1)} %pad_maximum_fusion.1), channel_id=1, source_target_pairs={{0,8},{8,16},{16,24},{24,32},{32,40},{40,48},{48,56},{56,64},{64,7... | collective-permute-start | bytes 786440 | tf_op jit(solution)/shard_map/ppermute | solution.py:64
  10.6 25.6 %collective-permute-start.1 = (bf16[1024,512]{1,0:T(8,128)(2,1)S(1)}, bf16[1024,512]{1,0:T(8,128)(2,1)S(1)}, u32[]{:S(2)}, u32[]{:S(2)}) collective-permute-start(bf16[1024,512]{1,0:T(8,128)(2,1)S(1)} %pad_maximum_fusion.refs_0_), channel_id=1, source_target_pairs={{0,4},{1,5},{2,6},{3,7},{4,0},{5,1},{6,2},{7,3},{8,12},{9,13},{10,... | collective-permute-start | bytes 3145736 | tf_op jit(solution)/shard_map/ppermute | solution.py:58
  11.0 25.7 %collective-permute-start.5 = (bf16[1024,512]{1,0:T(8,128)(2,1)S(1)}, bf16[1024,512]{1,0:T(8,128)(2,1)S(1)}, u32[]{:S(2)}, u32[]{:S(2)}) collective-permute-start(bf16[1024,512]{1,0:T(8,128)(2,1)S(1)} %pad_maximum_fusion.refs_0_), channel_id=1, source_target_pairs={{0,1},{1,2},{2,3},{3,0},{4,5},{5,6},{6,7},{7,4},{8,9},{9,10},{10,1... | collective-permute-start | bytes 3145736 | tf_op jit(solution)/shard_map/ppermute | solution.py:58
  12.2 25.1 %collective-permute-start.6 = (bf16[1024,512]{1,0:T(8,128)(2,1)S(1)}, bf16[1024,512]{1,0:T(8,128)(2,1)S(1)}, u32[]{:S(2)}, u32[]{:S(2)}) collective-permute-start(bf16[1024,512]{1,0:T(8,128)(2,1)S(1)} %pad_maximum_fusion.refs_0_), channel_id=1, source_target_pairs={{0,3},{1,0},{2,1},{3,2},{4,7},{5,4},{6,5},{7,6},{8,11},{9,8},{10,9... | collective-permute-start | bytes 3145736 | tf_op jit(solution)/shard_map/ppermute | solution.py:58
  14.5 26.9 %collective-permute-start.10 = (bf16[512,1024]{1,0:T(8,128)(2,1)S(1)}, bf16[512,1024]{1,0:T(8,128)(2,1)S(1)}, u32[]{:S(2)}, u32[]{:S(2)}) collective-permute-start(bf16[512,1024]{1,0:T(8,128)(2,1)S(1)} %copy-done.4), channel_id=1, source_target_pairs={{0,32},{8,40},{16,48},{24,56},{32,64},{40,72},{48,80},{56,88},{64,... | collective-permute-start | bytes 3145736 | tf_op jit(solution)/shard_map/ppermute | solution.py:50
  16.1 25.2 %collective-permute-start.11 = (bf16[512,1024]{1,0:T(8,128)(2,1)S(1)}, bf16[512,1024]{1,0:T(8,128)(2,1)S(1)}, u32[]{:S(2)}, u32[]{:S(2)}) collective-permute-start(bf16[512,1024]{1,0:T(8,128)(2,1)S(1)} %copy-done.4), channel_id=1, source_target_pairs={{0,96},{8,104},{16,112},{24,120},{32,0},{40,8},{48,16},{56,24},{64... | collective-permute-start | bytes 3145736 | tf_op jit(solution)/shard_map/ppermute | solution.py:50
  36.1 7.6 %collective-permute-start.7 = (bf16[512,1024]{1,0:T(8,128)(2,1)S(1)}, bf16[512,1024]{1,0:T(8,128)(2,1)S(1)}, u32[]{:S(2)}, u32[]{:S(2)}) collective-permute-start(bf16[512,1024]{1,0:T(8,128)(2,1)S(1)} %get-tuple-element.82), channel_id=1, source_target_pairs={{0,8},{8,0},{16,24},{24,16},{32,40},{40,32},{48,56},{56,48},{64,72... | collective-permute-start | bytes 3145736 | tf_op jit(solution)/shard_map/ppermute | solution.py:50
  36.8 26.1 %collective-permute-start.3 = (bf16[1024,512]{1,0:T(8,128)(2,1)S(1)}, bf16[1024,512]{1,0:T(8,128)(2,1)S(1)}, u32[]{:S(2)}, u32[]{:S(2)}) collective-permute-start(bf16[1024,512]{1,0:T(8,128)(2,1)S(1)} %collective-permute-done.1.refs_3_), channel_id=1, source_target_pairs={{0,1},{1,2},{2,3},{3,0},{4,5},{5,6},{6,7},{7,4},{8,9},{9,10},{10,1... | collective-permute-start | bytes 3145736 | tf_op jit(solution)/shard_map/ppermute | solution.py:58
  37.4 25.5 %collective-permute-start.4 = (bf16[1024,512]{1,0:T(8,128)(2,1)S(1)}, bf16[1024,512]{1,0:T(8,128)(2,1)S(1)}, u32[]{:S(2)}, u32[]{:S(2)}) collective-permute-start(bf16[1024,512]{1,0:T(8,128)(2,1)S(1)} %collective-permute-done.1.refs_3_), channel_id=1, source_target_pairs={{0,3},{1,0},{2,1},{3,2},{4,7},{5,4},{6,5},{7,6},{8,11},{9,8},{10,9... | collective-permute-start | bytes 3145736 | tf_op jit(solution)/shard_map/ppermute | solution.py:58
  41.3 24.8 %collective-permute-start.12 = (bf16[512,1024]{1,0:T(8,128)(2,1)S(1)}, bf16[512,1024]{1,0:T(8,128)(2,1)S(1)}, u32[]{:S(2)}, u32[]{:S(2)}) collective-permute-start(bf16[512,1024]{1,0:T(8,128)(2,1)S(1)} %collective-permute-done.10.refs_9_), channel_id=1, source_target_pairs={{0,32},{8,40},{16,48},{24,56},{32,64},{40,72},{48,80},{56,88},{64,... | collective-permute-start | bytes 3145736 | tf_op jit(solution)/shard_map/ppermute | solution.py:50
  41.3 24.8 %collective-permute-start.13 = (bf16[512,1024]{1,0:T(8,128)(2,1)S(1)}, bf16[512,1024]{1,0:T(8,128)(2,1)S(1)}, u32[]{:S(2)}, u32[]{:S(2)}) collective-permute-start(bf16[512,1024]{1,0:T(8,128)(2,1)S(1)} %copy-done.4), channel_id=1, source_target_pairs={{0,16},{8,24},{16,0},{24,8},{32,48},{40,56},{48,32},{56,40},{64,80... | collective-permute-start | bytes 3145736 | tf_op jit(solution)/shard_map/ppermute | solution.py:50
  43.8 41.5 %collective-permute-start.9 = (bf16[1024,512]{1,0:T(8,128)(2,1)S(1)}, bf16[1024,512]{1,0:T(8,128)(2,1)S(1)}, u32[]{:S(2)}, u32[]{:S(2)}) collective-permute-start(bf16[1024,512]{1,0:T(8,128)(2,1)S(1)} %collective-permute-done.5.refs_1_), channel_id=1, source_target_pairs={{0,1},{1,2},{2,3},{3,0},{4,5},{5,6},{6,7},{7,4},{8,9},{9,10},{10,1... | collective-permute-start | bytes 3145736 | tf_op jit(solution)/shard_map/ppermute | solution.py:58
  62.8 25.3 %collective-permute-start.8 = (bf16[1024,512]{1,0:T(8,128)(2,1)S(1)}, bf16[1024,512]{1,0:T(8,128)(2,1)S(1)}, u32[]{:S(2)}, u32[]{:S(2)}) collective-permute-start(bf16[1024,512]{1,0:T(8,128)(2,1)S(1)} %collective-permute-done.4.refs_1_.refs_5_), channel_id=1, source_target_pairs={{0,3},{1,0},{2,1},{3,2},{4,7},{5,4},{6,5},{7,6},{8,11},{9,8},{10,9... | collective-permute-start | bytes 3145736 | tf_op jit(solution)/shard_map/ppermute | solution.py:58
  66.2 29.2 %collective-permute-start.14 = (bf16[512,1024]{1,0:T(8,128)(2,1)S(1)}, bf16[512,1024]{1,0:T(8,128)(2,1)S(1)}, u32[]{:S(2)}, u32[]{:S(2)}) collective-permute-start(bf16[512,1024]{1,0:T(8,128)(2,1)S(1)} %collective-permute-done.13.refs_11_), channel_id=1, source_target_pairs={{0,32},{8,40},{16,48},{24,56},{32,64},{40,72},{48,80},{56,88},{64,... | collective-permute-start | bytes 3145736 | tf_op jit(solution)/shard_map/ppermute | solution.py:50
  67.2 29.8 %collective-permute-start.15 = (bf16[512,1024]{1,0:T(8,128)(2,1)S(1)}, bf16[512,1024]{1,0:T(8,128)(2,1)S(1)}, u32[]{:S(2)}, u32[]{:S(2)}) collective-permute-start(bf16[512,1024]{1,0:T(8,128)(2,1)S(1)} %collective-permute-done.13.refs_11_), channel_id=1, source_target_pairs={{0,96},{8,104},{16,112},{24,120},{32,0},{40,8},{48,16},{56,24},{64... | collective-permute-start | bytes 3145736 | tf_op jit(solution)/shard_map/ppermute | solution.py:50
  69.5 27.5 %collective-permute-start.16 = (bf16[512,1024]{1,0:T(8,128)(2,1)S(1)}, bf16[512,1024]{1,0:T(8,128)(2,1)S(1)}, u32[]{:S(2)}, u32[]{:S(2)}) collective-permute-start(bf16[512,1024]{1,0:T(8,128)(2,1)S(1)} %collective-permute-done.12.refs_15_), channel_id=1, source_target_pairs={{0,16},{8,24},{16,0},{24,8},{32,48},{40,56},{48,32},{56,40},{64,80... | collective-permute-start | bytes 3145736 | tf_op jit(solution)/shard_map/ppermute | solution.py:50
  92.1 32.2 %collective-permute-start.22 = (bf16[640,1024]{1,0:T(8,128)(2,1)S(1)}, bf16[640,1024]{1,0:T(8,128)(2,1)S(1)}, u32[]{:S(2)}, u32[]{:S(2)}) collective-permute-start(bf16[640,1024]{1,0:T(8,128)(2,1)S(1)} %get-tuple-element.86), channel_id=1, source_target_pairs={{0,32},{8,40},{16,48},{24,56},{32,64},{40,72},{48,80},{56,88},{64,... | collective-permute-start | bytes 3932168 | tf_op jit(solution)/shard_map/ppermute | solution.py:50
  93.4 26.8 %collective-permute-start.19 = (bf16[512,1024]{1,0:T(8,128)(2,1)S(1)}, bf16[512,1024]{1,0:T(8,128)(2,1)S(1)}, u32[]{:S(2)}, u32[]{:S(2)}) collective-permute-start(bf16[512,1024]{1,0:T(8,128)(2,1)S(1)} %get-tuple-element.101), channel_id=1, source_target_pairs={{0,16},{8,24},{16,0},{24,8},{32,48},{40,56},{48,32},{56,40},{64,80... | collective-permute-start | bytes 3145736 | tf_op jit(solution)/shard_map/ppermute | solution.py:50
  95.3 29.4 %collective-permute-start.23 = (bf16[640,1024]{1,0:T(8,128)(2,1)S(1)}, bf16[640,1024]{1,0:T(8,128)(2,1)S(1)}, u32[]{:S(2)}, u32[]{:S(2)}) collective-permute-start(bf16[640,1024]{1,0:T(8,128)(2,1)S(1)} %get-tuple-element.112), channel_id=1, source_target_pairs={{0,96},{8,104},{16,112},{24,120},{32,0},{40,8},{48,16},{56,24},{64... | collective-permute-start | bytes 3932168 | tf_op jit(solution)/shard_map/ppermute | solution.py:50
  109.6 4.8 %collective-permute-start.17 = (bf16[256,1024]{1,0:T(8,128)(2,1)S(1)}, bf16[256,1024]{1,0:T(8,128)(2,1)S(1)}, u32[]{:S(2)}, u32[]{:S(2)}) collective-permute-start(bf16[256,1024]{1,0:T(8,128)(2,1)S(1)} %get-tuple-element.95), channel_id=1, source_target_pairs={{0,8},{8,0},{16,24},{24,16},{32,40},{40,32},{48,56},{56,48},{64,72... | collective-permute-start | bytes 1572872 | tf_op jit(solution)/shard_map/ppermute | solution.py:50
  111.6 2.9 %collective-permute-start.18 = (bf16[256,1024]{1,0:T(8,128)(2,1)S(1)}, bf16[256,1024]{1,0:T(8,128)(2,1)S(1)}, u32[]{:S(2)}, u32[]{:S(2)}) collective-permute-start(bf16[256,1024]{1,0:T(8,128)(2,1)S(1)} %get-tuple-element.96), channel_id=1, source_target_pairs={{0,8},{8,0},{16,24},{24,16},{32,40},{40,32},{48,56},{56,48},{64,72... | collective-permute-start | bytes 1572872 | tf_op jit(solution)/shard_map/ppermute | solution.py:50
  120.4 15.3 %collective-permute-start.20 = (bf16[256,1024]{1,0:T(8,128)(2,1)S(1)}, bf16[256,1024]{1,0:T(8,128)(2,1)S(1)}, u32[]{:S(2)}, u32[]{:S(2)}) collective-permute-start(bf16[256,1024]{1,0:T(8,128)(2,1)S(1)} %get-tuple-element.106), channel_id=1, source_target_pairs={{0,32},{8,40},{16,48},{24,56},{32,64},{40,72},{48,80},{56,88},{64,... | collective-permute-start | bytes 1572872 | tf_op jit(solution)/shard_map/ppermute | solution.py:50
  120.6 15.4 %collective-permute-start.21 = (bf16[256,1024]{1,0:T(8,128)(2,1)S(1)}, bf16[256,1024]{1,0:T(8,128)(2,1)S(1)}, u32[]{:S(2)}, u32[]{:S(2)}) collective-permute-start(bf16[256,1024]{1,0:T(8,128)(2,1)S(1)} %get-tuple-element.107), channel_id=1, source_target_pairs={{0,96},{8,104},{16,112},{24,120},{32,0},{40,8},{48,16},{56,24},{64... | collective-permute-start | bytes 1572872 | tf_op jit(solution)/shard_map/ppermute | solution.py:50
  124.8 16.6 %collective-permute-start.24 = (bf16[128,1024]{1,0:T(8,128)(2,1)S(1)}, bf16[128,1024]{1,0:T(8,128)(2,1)S(1)}, u32[]{:S(2)}, u32[]{:S(2)}) collective-permute-start(bf16[128,1024]{1,0:T(8,128)(2,1)S(1)} %get-tuple-element.126), channel_id=1, source_target_pairs={{0,32},{8,40},{16,48},{24,56},{32,64},{40,72},{48,80},{56,88},{64,... | collective-permute-start | bytes 786440 | tf_op jit(solution)/shard_map/ppermute | solution.py:50
  126.0 15.6 %collective-permute-start.25 = (bf16[128,1024]{1,0:T(8,128)(2,1)S(1)}, bf16[128,1024]{1,0:T(8,128)(2,1)S(1)}, u32[]{:S(2)}, u32[]{:S(2)}) collective-permute-start(bf16[128,1024]{1,0:T(8,128)(2,1)S(1)} %get-tuple-element.127), channel_id=1, source_target_pairs={{0,96},{8,104},{16,112},{24,120},{32,0},{40,8},{48,16},{56,24},{64... | collective-permute-start | bytes 786440 | tf_op jit(solution)/shard_map/ppermute | solution.py:50
  127.8 30.3 %collective-permute-start.26 = (bf16[512,1024]{1,0:T(8,128)(2,1)S(1)}, bf16[512,1024]{1,0:T(8,128)(2,1)S(1)}, u32[]{:S(2)}, u32[]{:S(2)}) collective-permute-start(bf16[512,1024]{1,0:T(8,128)(2,1)S(1)} %add_rows.7), channel_id=1, source_target_pairs={{0,16},{8,24},{16,0},{24,8},{32,48},{40,56},{48,32},{56,40},{64,80... | collective-permute-start | bytes 3145736 | tf_op jit(solution)/shard_map/ppermute | solution.py:50
  136.2 21.9 %collective-permute-start.27 = (bf16[256,1024]{1,0:T(8,128)(2,1)S(1)}, bf16[256,1024]{1,0:T(8,128)(2,1)S(1)}, u32[]{:S(2)}, u32[]{:S(2)}) collective-permute-start(bf16[256,1024]{1,0:T(8,128)(2,1)S(1)} %get-tuple-element.131), channel_id=1, source_target_pairs={{0,32},{8,40},{16,48},{24,56},{32,64},{40,72},{48,80},{56,88},{64,... | collective-permute-start | bytes 1572872 | tf_op jit(solution)/shard_map/ppermute | solution.py:50
  141.6 16.5 %collective-permute-start.28 = (bf16[256,1024]{1,0:T(8,128)(2,1)S(1)}, bf16[256,1024]{1,0:T(8,128)(2,1)S(1)}, u32[]{:S(2)}, u32[]{:S(2)}) collective-permute-start(bf16[256,1024]{1,0:T(8,128)(2,1)S(1)} %get-tuple-element.138), channel_id=1, source_target_pairs={{0,96},{8,104},{16,112},{24,120},{32,0},{40,8},{48,16},{56,24},{64... | collective-permute-start | bytes 1572872 | tf_op jit(solution)/shard_map/ppermute | solution.py:50
  153.7 10.5 %collective-permute-start.29 = (bf16[512,256]{1,0:T(8,128)(2,1)S(1)}, bf16[512,256]{1,0:T(8,128)(2,1)S(1)}, u32[]{:S(2)}, u32[]{:S(2)}) collective-permute-start(bf16[512,256]{1,0:T(8,128)(2,1)S(1)} %pad_maximum_fusion.2), channel_id=1, source_target_pairs={{8,0},{16,8},{24,16},{32,24},{40,32},{48,40},{56,48},{64,56},{72,6... | collective-permute-start | bytes 786440 | tf_op jit(solution)/shard_map/ppermute | solution.py:64

commit v14 on v13

--- a/solution.py
+++ b/solution.py
@@ -605,7 +605,7 @@
         attend_back, meta, query_rows, attn_grad, kv_earlier, key_rows, value_rows, segments, top, total
     )
     heads = query_rows.shape[1] // HD
-    cuts = heads // 4, heads // 2
+    cuts = heads // 4, 5 * heads // 8
     held = part((0, cuts[0]), None)
 
     ry, *held = tied((ry, *held))
@@ -615,7 +615,8 @@
     )
     fup = move_row(far_up, dz=1)
     fdn = move_row(far_dn, dz=-1)
-    rup, rdn, up2, dn2 = tied((rup, rdn, up2, dn2), far_up)
+    rup, rdn = tied((rup, rdn), far_up)
+    up2, dn2 = tied((up2, dn2), far_up)
     (across,) = add_rows([middle, rup, rdn], ((0, 0, 2 * hw, ((0, 0), (1, 0), (2, 0))),))
     held = tied(held, across)
     across = move_row(across, dyh=1)

time: 165 us -> 163 us (0.988)
  transfers between devices with their start and end apart: 30 -> 30, of which waited for: 14 -> 13; matrix products, arithmetic and copies ran while one was open for 1% -> 1% of each run, Pallas kernels for 43% -> 44%
where the time goes in v14:
time: 163 us
  Pallas kernels  71 us (44%)
  starting transfers between devices  47.4 us (29%)
  waiting for transfers between devices  39 us (24%)
  local copies, waits for them, and re-layouts  2.52 us (2%)
  other arithmetic  1.97 us (1%)
    ppermute x21, starting transfers between devices, move_row(): return lax.ppermute(value, 'row', pairs)  29 us
    ppermute x7, waiting for transfers between devices, move_col(): return lax.ppermute(value, 'col', pairs)  26.1 us
    pallas_call x3, Pallas kernels, attend_back(): pl.pallas_call(functools.partial(bwd_kernel, len(earlier), last), grid_sp...  20.6 us
    pallas_call x4, Pallas kernels, project(): pl.pallas_call(functools.partial(proj_kernel, tuple(slots), held, plan),...  17.7 us
    pallas_call x1, Pallas kernels, attend(): pl.pallas_call(fwd_kernel, grid_spec=pltpu.PrefetchScalarGridSpec(num_sca...  14.9 us
    pallas_call x1, Pallas kernels, attn_grad_part(): pl.pallas_call(kernel, grid_spec=pltpu.PrefetchScalarGridSpec(num_scalar_...  12.6 us
    ppermute x2, starting transfers between devices, passed_along(): lax.ppermute(value, axis, [(source, source + steps) for source in range(f...  9.26 us
    ppermute x7, starting transfers between devices, move_col(): return lax.ppermute(value, 'col', pairs)  9.05 us
  transfers between devices with their start and end apart: 30, of which 13 were waited for; matrix products, arithmetic and copies ran while one was open for 1% of the time, Pallas kernels for 44%

profile of v14, /device:TPU:1, one launch (start us, length us, event | category | flops | bytes accessed | tf_op | source)
XLA Modules:
  0.0 162.9 jit_solution(1543974227448786001)
XLA Ops:
  0.6 0.0 copy-start.5
  0.6 0.0 copy-start.6
  0.7 2.2 %constant_dynamic-slice_fusion = (bf16[512,512]{1,0:T(8,128)(2,1)S(1)}, bf16[512,512]{1,0:T(8,128)(2,1)}) fusion(bf16[512,1024]{1,0:T(8,128)(2,1)} %param.13, s32[]{:T(128)S(6)} %select_n.38, s32[]{:T(128)S(6)} %select_n.32), kind=kLoop, calls=%fused_computation.13 | loop fusion | bytes 2097160 | tf_op jit(solution)/shard_map/dynamic_slice | solution.py:521
  3.0 1.4 collective-permute-start
  4.4 4.8 %collective-permute-start.2 = (bf16[512,256]{1,0:T(8,128)(2,1)S(1)}, bf16[512,256]{1,0:T(8,128)(2,1)S(1)}, u32[]{:S(2)}, u32[]{:S(2)}) collective-permute-start(bf16[512,256]{1,0:T(8,128)(2,1)S(1)} %pad_maximum_fusion.1), channel_id=1, source_target_pairs={{0,8},{8,16},{16,24},{24,32},{32,40},{40,48},{48,56},{56,64},{64,7... | collective-permute-start | bytes 786440 | tf_op jit(solution)/shard_map/ppermute | solution.py:64
  9.3 0.1 concatenate.16.meta_ref
  9.4 1.1 pad_maximum_fusion.refs_0_
  10.6 0.5 collective-permute-start.1
  11.0 1.2 collective-permute-start.5
  12.2 1.5 collective-permute-start.6
  13.7 0.7 collective-permute-done.2.kv_ref
  14.5 1.6 %collective-permute-start.10 = (bf16[512,1024]{1,0:T(8,128)(2,1)S(1)}, bf16[512,1024]{1,0:T(8,128)(2,1)S(1)}, u32[]{:S(2)}, u32[]{:S(2)}) collective-permute-start(bf16[512,1024]{1,0:T(8,128)(2,1)S(1)} %copy-done.4), channel_id=1, source_target_pairs={{0,32},{8,40},{16,48},{24,56},{32,64},{40,72},{48,80},{56,88},{64,... | collective-permute-start | bytes 3145736 | tf_op jit(solution)/shard_map/ppermute | solution.py:50
  16.1 2.1 %collective-permute-start.11 = (bf16[512,1024]{1,0:T(8,128)(2,1)S(1)}, bf16[512,1024]{1,0:T(8,128)(2,1)S(1)}, u32[]{:S(2)}, u32[]{:S(2)}) collective-permute-start(bf16[512,1024]{1,0:T(8,128)(2,1)S(1)} %copy-done.4), channel_id=1, source_target_pairs={{0,96},{8,104},{16,112},{24,120},{32,0},{40,8},{48,16},{56,24},{64... | collective-permute-start | bytes 3145736 | tf_op jit(solution)/shard_map/ppermute | solution.py:50
  18.2 14.9 %attend.1 = (bf16[512,1024]{1,0:T(8,128)(2,1)S(1)}, f32[8,1,512]{2,1,0:T(1,128)S(1)}, f32[8,1,512]{2,1,0:T(1,128)S(1)}) custom-call(s32[24]{0:T(128)S(1)} %concatenate.16.meta_ref, bf16[512,1024]{1,0:T(8,128)(2,1)S(1)} %copy-done, bf16[512,256]{1,0:T(8,128)(2,1)S(1)} %collective-permute-done.2.kv_ref, bf16[512,128]{1,0:T(8,128)(2,1)S(1)} %copy-done.2, ...), custom_call_target="tpu_custom_call" | custom-call | flops 68719476736 | bytes 8388608 | tf_op jit(solution)/shard_map/attend/pallas_call | solution.py:148
  33.1 3.0 %collective-permute-done.1.refs_3_ = bf16[1024,512]{1,0:T(8,128)(2,1)S(1)} collective-permute-done((bf16[1024,512]{1,0:T(8,128)(2,1)S(1)}, bf16[1024,512]{1,0:T(8,128)(2,1)S(1)}, u32[]{:S(2)}, u32[]{:S(2)}) %collective-permute-start.1) | collective-permute-done | bytes 1048608 | tf_op jit(solution)/shard_map/ppermute | solution.py:58
  36.1 0.6 collective-permute-done.5.refs_1_
  36.8 0.6 collective-permute-start.3
  37.4 2.4 %collective-permute-start.4 = (bf16[1024,512]{1,0:T(8,128)(2,1)S(1)}, bf16[1024,512]{1,0:T(8,128)(2,1)S(1)}, u32[]{:S(2)}, u32[]{:S(2)}) collective-permute-start(bf16[1024,512]{1,0:T(8,128)(2,1)S(1)} %collective-permute-done.1.refs_3_), channel_id=1, source_target_pairs={{0,3},{1,0},{2,1},{3,2},{4,7},{5,4},{6,5},{7,6},{8,11},{9,8},{10,9... | collective-permute-start | bytes 3145736 | tf_op jit(solution)/shard_map/ppermute | solution.py:58
  39.8 1.5 collective-permute-done.10.refs_9_
  41.3 0.0 collective-permute-start.12
  41.3 2.4 %collective-permute-start.13 = (bf16[512,1024]{1,0:T(8,128)(2,1)S(1)}, bf16[512,1024]{1,0:T(8,128)(2,1)S(1)}, u32[]{:S(2)}, u32[]{:S(2)}) collective-permute-start(bf16[512,1024]{1,0:T(8,128)(2,1)S(1)} %copy-done.4), channel_id=1, source_target_pairs={{0,16},{8,24},{16,0},{24,8},{32,48},{40,56},{48,32},{56,40},{64,80... | collective-permute-start | bytes 3145736 | tf_op jit(solution)/shard_map/ppermute | solution.py:50
  43.7 0.1 constant_dynamic-update-slice_fusion.1
  43.8 0.1 collective-permute-start.9
  43.9 0.1 constant_dynamic-update-slice_fusion.refs_4_.refs_2_.refs_1_
  43.9 6.7 %project.4.refs_3_ = bf16[2,64,256,1024]{3,2,1,0:T(8,128)(2,1)} custom-call(s32[24]{0:T(128)S(1)} %concatenate.16.meta_ref, bf16[1024,512]{1,0:T(8,128)(2,1)S(1)} %pad_maximum_fusion.refs_0_, bf16[1024,512]{1,0:T(8,128)(2,1)S(1)} %collective-permute-done.5.refs_1_, bf16[1024,512]{1,0:T(8,128)(2,1)S(1)} %collective-permute-done.6.refs_2_, ...), custom_call_target="tpu_custom_call" | custom-call | flops 4294967296 | bytes 10485760 | tf_op jit(solution)/shard_map/project/pallas_call | solution.py:324
  50.7 12.2 %collective-permute-done.3.refs_0_.refs_4_ = bf16[1024,512]{1,0:T(8,128)(2,1)S(1)} collective-permute-done((bf16[1024,512]{1,0:T(8,128)(2,1)S(1)}, bf16[1024,512]{1,0:T(8,128)(2,1)S(1)}, u32[]{:S(2)}, u32[]{:S(2)}) %collective-permute-start.3) | collective-permute-done | bytes 1048608 | tf_op jit(solution)/shard_map/ppermute | solution.py:58
  62.8 2.8 %collective-permute-start.8 = (bf16[1024,512]{1,0:T(8,128)(2,1)S(1)}, bf16[1024,512]{1,0:T(8,128)(2,1)S(1)}, u32[]{:S(2)}, u32[]{:S(2)}) collective-permute-start(bf16[1024,512]{1,0:T(8,128)(2,1)S(1)} %collective-permute-done.4.refs_1_.refs_5_), channel_id=1, source_target_pairs={{0,3},{1,0},{2,1},{3,2},{4,7},{5,4},{6,5},{7,6},{8,11},{9,8},{10,9... | collective-permute-start | bytes 3145736 | tf_op jit(solution)/shard_map/ppermute | solution.py:58
  65.7 0.5 collective-permute-done.12.refs_15_
  66.2 1.0 collective-permute-start.14
  67.2 2.3 %collective-permute-start.15 = (bf16[512,1024]{1,0:T(8,128)(2,1)S(1)}, bf16[512,1024]{1,0:T(8,128)(2,1)S(1)}, u32[]{:S(2)}, u32[]{:S(2)}) collective-permute-start(bf16[512,1024]{1,0:T(8,128)(2,1)S(1)} %collective-permute-done.13.refs_11_), channel_id=1, source_target_pairs={{0,96},{8,104},{16,112},{24,120},{32,0},{40,8},{48,16},{56,24},{64... | collective-permute-start | bytes 3145736 | tf_op jit(solution)/shard_map/ppermute | solution.py:50
  69.5 1.3 collective-permute-start.16
  70.8 4.2 %project.5.refs_2_ = bf16[2,64,256,1024]{3,2,1,0:T(8,128)(2,1)} custom-call(s32[24]{0:T(128)S(1)} %concatenate.16.meta_ref, bf16[1024,512]{1,0:T(8,128)(2,1)S(1)} %collective-permute-done.3.refs_0_.refs_4_, bf16[1024,512]{1,0:T(8,128)(2,1)S(1)} %collective-permute-done.4.refs_1_.refs_5_, ...), custom_call_target="tpu_custom_call", output_to_operand_aliasing={{}: (4, {})} | custom-call | flops 2147483648 | bytes 6291456 | tf_op jit(solution)/shard_map/project/pallas_call | solution.py:324
  75.0 10.3 %collective-permute-done.9.refs_0_.refs_6_ = bf16[1024,512]{1,0:T(8,128)(2,1)S(1)} collective-permute-done((bf16[1024,512]{1,0:T(8,128)(2,1)S(1)}, bf16[1024,512]{1,0:T(8,128)(2,1)S(1)}, u32[]{:S(2)}, u32[]{:S(2)}) %collective-permute-start.9) | collective-permute-done | bytes 1048608 | tf_op jit(solution)/shard_map/ppermute | solution.py:58
  85.3 2.8 %project.6.refs_2_ = bf16[2,64,256,1024]{3,2,1,0:T(8,128)(2,1)} custom-call(s32[24]{0:T(128)S(1)} %concatenate.16.meta_ref, bf16[1024,512]{1,0:T(8,128)(2,1)S(1)} %collective-permute-done.9.refs_0_.refs_6_, bf16[1024,1024]{1,0:T(8,128)(2,1)S(1)} %constant_dynamic-update-slice_fusion.refs_4_.refs_2_.refs_1_, ...), custom_call_target="tpu_custom_call", output_to_operand_aliasing={{}: (3, {})} | custom-call | flops 1073741824 | bytes 4194304 | tf_op jit(solution)/shard_map/project/pallas_call | solution.py:324
  88.1 3.9 %project.7 = (bf16[2,64,256,1024]{3,2,1,0:T(8,128)(2,1)}, bf16[512,1024]{1,0:T(8,128)(2,1)S(1)}, bf16[640,1024]{1,0:T(8,128)(2,1)S(1)}, bf16[640,1024]{1,0:T(8,1...) custom-call(s32[24]{0:T(128)S(1)} %concatenate.16.meta_ref, ...), custom_call_target="tpu_custom_call", output_to_operand_aliasing={{0}: (3, {})} | custom-call | flops 1073741824 | bytes 4194304 | tf_op jit(solution)/shard_map/project/pallas_call | solution.py:324
  92.1 1.3 collective-permute-start.22
  93.4 2.0 %collective-permute-start.19 = (bf16[512,1024]{1,0:T(8,128)(2,1)S(1)}, bf16[512,1024]{1,0:T(8,128)(2,1)S(1)}, u32[]{:S(2)}, u32[]{:S(2)}) collective-permute-start(bf16[512,1024]{1,0:T(8,128)(2,1)S(1)} %get-tuple-element.101), channel_id=1, source_target_pairs={{0,16},{8,24},{16,0},{24,8},{32,48},{40,56},{48,32},{56,40},{64,80... | collective-permute-start | bytes 3145736 | tf_op jit(solution)/shard_map/ppermute | solution.py:50
  95.3 1.7 %collective-permute-start.23 = (bf16[640,1024]{1,0:T(8,128)(2,1)S(1)}, bf16[640,1024]{1,0:T(8,128)(2,1)S(1)}, u32[]{:S(2)}, u32[]{:S(2)}) collective-permute-start(bf16[640,1024]{1,0:T(8,128)(2,1)S(1)} %get-tuple-element.112), channel_id=1, source_target_pairs={{0,96},{8,104},{16,112},{24,120},{32,0},{40,8},{48,16},{56,24},{64... | collective-permute-start | bytes 3932168 | tf_op jit(solution)/shard_map/ppermute | solution.py:50
  97.0 12.6 %attn_grad.1 = (f32[512,1024]{1,0:T(8,128)S(1)}, bf16[256,1024]{1,0:T(8,128)(2,1)S(1)}, bf16[256,1024]{1,0:T(8,128)(2,1)S(1)}) custom-call(s32[24]{0:T(128)S(1)} %concatenate.16.meta_ref, bf16[1024,512]{1,0:T(8,128)(2,1)S(1)} %pad_maximum_fusion.refs_0_, bf16[1024,512]{1,0:T(8,128)(2,1)S(1)} %collective-permute-done.5.refs_1_, ...), custom_call_target="tpu_custom_call" | custom-call | flops 8589934592 | bytes 20971520 | tf_op jit(solution)/shard_map/attn_grad/pallas_call | solution.py:419
  109.6 1.9 %collective-permute-start.17 = (bf16[256,1024]{1,0:T(8,128)(2,1)S(1)}, bf16[256,1024]{1,0:T(8,128)(2,1)S(1)}, u32[]{:S(2)}, u32[]{:S(2)}) collective-permute-start(bf16[256,1024]{1,0:T(8,128)(2,1)S(1)} %get-tuple-element.95), channel_id=1, source_target_pairs={{0,8},{8,0},{16,24},{24,16},{32,40},{40,32},{48,56},{56,48},{64,72... | collective-permute-start | bytes 1572872 | tf_op jit(solution)/shard_map/ppermute | solution.py:50
  111.6 0.1 collective-permute-start.18
  111.7 2.8 %fetch.1 = (bf16[512,1024]{1,0:T(8,128)(2,1)S(1)}, bf16[512,1024]{1,0:T(8,128)(2,1)S(1)}, bf16[512,1024]{1,0:T(8,128)(2,1)S(1)}, bf16[512,1024]{1,0:T(8,128)(2,1)S(1)}) custom-call(s32[24]{0:T(128)S(1)} %concatenate.16.meta_ref, bf16[2,64,256,1024]{3,2,1,0:T(8,128)(2,1)} %get-tuple-element.99.buffer_ref), custom_call_target="tpu_custom_call" | custom-call | bytes 65536 | tf_op jit(solution)/shard_map/fetch/pallas_call | solution.py:466
  114.4 0.2 add_rows.5.g_ref
  114.6 5.5 %attend_back.3 = (bf16[512,1024]{1,0:T(8,128)(2,1)}, f32[1024,128]{1,0:T(8,128)S(1)}, f32[1024,128]{1,0:T(8,128)S(1)}) custom-call(s32[24]{0:T(128)S(1)} %concatenate.16.meta_ref, bf16[512,1024]{1,0:T(8,128)(2,1)S(1)} %copy-done, bf16[512,1024]{1,0:T(8,128)(2,1)S(1)} %add_rows.5.g_ref, bf16[512,256]{1,0:T(8,128)(2,1)S(1)} %collective-permute-done.2.kv_ref, ...), custom_call_target="tpu_custom_call" | custom-call | flops 1048576 | bytes 65536 | tf_op jit(solution)/shard_map/attend_back/pallas_call | solution.py:226
  120.2 0.2 add_rows.6
  120.4 0.2 collective-permute-start.20
  120.6 2.6 %collective-permute-start.21 = (bf16[256,1024]{1,0:T(8,128)(2,1)S(1)}, bf16[256,1024]{1,0:T(8,128)(2,1)S(1)}, u32[]{:S(2)}, u32[]{:S(2)}) collective-permute-start(bf16[256,1024]{1,0:T(8,128)(2,1)S(1)} %get-tuple-element.107), channel_id=1, source_target_pairs={{0,96},{8,104},{16,112},{24,120},{32,0},{40,8},{48,16},{56,24},{64... | collective-permute-start | bytes 1572872 | tf_op jit(solution)/shard_map/ppermute | solution.py:50
  123.2 1.1 collective-permute-done.22.refs_1_.refs_4_
  124.3 1.6 collective-permute-start.25
  125.8 0.4 add_rows.7
  126.2 1.8 %collective-permute-start.26 = (bf16[512,1024]{1,0:T(8,128)(2,1)S(1)}, bf16[512,1024]{1,0:T(8,128)(2,1)S(1)}, u32[]{:S(2)}, u32[]{:S(2)}) collective-permute-start(bf16[512,1024]{1,0:T(8,128)(2,1)S(1)} %add_rows.7), channel_id=1, source_target_pairs={{0,16},{8,24},{16,0},{24,8},{32,48},{40,56},{48,32},{56,40},{64,80... | collective-permute-start | bytes 3145736 | tf_op jit(solution)/shard_map/ppermute | solution.py:50
  128.0 7.5 %attend_back.4 = (bf16[512,1024]{1,0:T(8,128)(2,1)}, f32[1024,128]{1,0:T(8,128)S(1)}, f32[1024,128]{1,0:T(8,128)S(1)}) custom-call(s32[24]{0:T(128)S(1)} %concatenate.16.meta_ref, bf16[512,1024]{1,0:T(8,128)(2,1)S(1)} %copy-done, bf16[512,1024]{1,0:T(8,128)(2,1)S(1)} %add_rows.5.g_ref, ...), custom_call_target="tpu_custom_call", output_to_operand_aliasing={{0}: (11, {})} | custom-call | flops 4026531840 | bytes 6291456 | tf_op jit(solution)/shard_map/attend_back/pallas_call | solution.py:226
  135.5 0.2 collective-permute-done.20.refs_1_
  135.7 0.3 collective-permute-done.21.refs_2_
  136.0 0.2 add_rows.8
  136.2 1.4 collective-permute-start.27
  137.6 3.7 %collective-permute-done.24.refs_5_ = bf16[128,1024]{1,0:T(8,128)(2,1)S(1)} collective-permute-done((bf16[128,1024]{1,0:T(8,128)(2,1)S(1)}, bf16[128,1024]{1,0:T(8,128)(2,1)S(1)}, u32[]{:S(2)}, u32[]{:S(2)}) %collective-permute-start.24) | collective-permute-done | bytes 262176 | tf_op jit(solution)/shard_map/ppermute | solution.py:50
  141.3 0.3 collective-permute-done.25.refs_7_
  141.6 2.4 %collective-permute-start.28 = (bf16[256,1024]{1,0:T(8,128)(2,1)S(1)}, bf16[256,1024]{1,0:T(8,128)(2,1)S(1)}, u32[]{:S(2)}, u32[]{:S(2)}) collective-permute-start(bf16[256,1024]{1,0:T(8,128)(2,1)S(1)} %get-tuple-element.138), channel_id=1, source_target_pairs={{0,96},{8,104},{16,112},{24,120},{32,0},{40,8},{48,16},{56,24},{64... | collective-permute-start | bytes 1572872 | tf_op jit(solution)/shard_map/ppermute | solution.py:50
  144.0 7.6 %attend_back.5 = (bf16[512,1024]{1,0:T(8,128)(2,1)}, f32[1024,128]{1,0:T(8,128)S(1)}, f32[1024,128]{1,0:T(8,128)S(1)}) custom-call(s32[24]{0:T(128)S(1)} %concatenate.16.meta_ref, bf16[512,1024]{1,0:T(8,128)(2,1)S(1)} %copy-done, bf16[512,1024]{1,0:T(8,128)(2,1)S(1)} %add_rows.5.g_ref, ...), custom_call_target="tpu_custom_call", output_to_operand_aliasing={{0}: (11, {})} | custom-call | flops 4026531840 | bytes 6291456 | tf_op jit(solution)/shard_map/attend_back/pallas_call | solution.py:226
  151.7 4.5 %collective-permute-start.29 = (bf16[512,256]{1,0:T(8,128)(2,1)S(1)}, bf16[512,256]{1,0:T(8,128)(2,1)S(1)}, u32[]{:S(2)}, u32[]{:S(2)}) collective-permute-start(bf16[512,256]{1,0:T(8,128)(2,1)S(1)} %pad_maximum_fusion.2), channel_id=1, source_target_pairs={{8,0},{16,8},{24,16},{32,24},{40,32},{48,40},{56,48},{64,56},{72,6... | collective-permute-start | bytes 786440 | tf_op jit(solution)/shard_map/ppermute | solution.py:64
  156.2 1.5 add_rows.9
  157.6 4.5 %collective-permute-done.29 = bf16[512,256]{1,0:T(8,128)(2,1)S(1)} collective-permute-done((bf16[512,256]{1,0:T(8,128)(2,1)S(1)}, bf16[512,256]{1,0:T(8,128)(2,1)S(1)}, u32[]{:S(2)}, u32[]{:S(2)}) %collective-permute-start.29) | collective-permute-done | bytes 262176 | tf_op jit(solution)/shard_map/ppermute | solution.py:64
  162.2 0.8 fusion
  (39 shorter events, 0.2 us)
Async XLA Ops:
  0.6 8.7 %copy-start.5 = (s32[8]{0:T(128)S(1)}, s32[8]{0:T(128)}, u32[]{:S(2)}) copy-start(s32[8]{0:T(128)} %constant.79.clone) | copy-start | bytes 100
  0.6 8.7 %copy-start.6 = (s32[8]{0:T(128)S(1)}, s32[8]{0:T(128)}, u32[]{:S(2)}) copy-start(s32[8]{0:T(128)} %constant.80.clone) | copy-start | bytes 100
  0.7 8.7 %copy-start.7 = (s32[8]{0:T(128)S(1)}, s32[8]{0:T(128)}, u32[]{:S(2)}) copy-start(s32[8]{0:T(128)} %constant.81.clone) | copy-start | bytes 100
  0.7 3.7 %copy-start.2 = (bf16[512,128]{1,0:T(8,128)(2,1)S(1)}, bf16[512,128]{1,0:T(8,128)(2,1)}, u32[]{:S(2)}) copy-start(bf16[512,128]{1,0:T(8,128)(2,1)} %k_ref.7) | copy-start | bytes 393220
  0.7 3.7 %copy-start.1 = (bf16[512,128]{1,0:T(8,128)(2,1)S(1)}, bf16[512,128]{1,0:T(8,128)(2,1)}, u32[]{:S(2)}) copy-start(bf16[512,128]{1,0:T(8,128)(2,1)} %v_ref.7) | copy-start | bytes 393220
  0.7 13.7 %copy-start.4 = (bf16[512,1024]{1,0:T(8,128)(2,1)S(1)}, bf16[512,1024]{1,0:T(8,128)(2,1)}, u32[]{:S(2)}) copy-start(bf16[512,1024]{1,0:T(8,128)(2,1)} %refs_8_) | copy-start | bytes 3145732
  0.7 17.5 %copy-start = (bf16[512,1024]{1,0:T(8,128)(2,1)S(1)}, bf16[512,1024]{1,0:T(8,128)(2,1)}, u32[]{:S(2)}) copy-start(bf16[512,1024]{1,0:T(8,128)(2,1)} %q_ref.6) | copy-start | bytes 3145732
  0.7 17.5 %copy-start.3 = (s32[8192]{0:T(1024)S(1)}, s32[8192]{0:T(1024)}, u32[]{:S(2)}) copy-start(s32[8192]{0:T(1024)} %param.15) | copy-start | bytes 98308
  3.0 6.5 %collective-permute-start = (bf16[512,512]{1,0:T(8,128)(2,1)}, bf16[512,512]{1,0:T(8,128)(2,1)}, u32[]{:S(2)}, u32[]{:S(2)}) collective-permute-start(bf16[512,512]{1,0:T(8,128)(2,1)} %get-tuple-element.145), channel_id=1, source_target_pairs={{0,8},{8,0},{16,24},{24,16},{32,40},{40,32},{48,56},{56,48},{64,72... | collective-permute-start | bytes 1572872 | tf_op jit(solution)/shard_map/ppermute | solution.py:50
  4.4 10.0 %collective-permute-start.2 = (bf16[512,256]{1,0:T(8,128)(2,1)S(1)}, bf16[512,256]{1,0:T(8,128)(2,1)S(1)}, u32[]{:S(2)}, u32[]{:S(2)}) collective-permute-start(bf16[512,256]{1,0:T(8,128)(2,1)S(1)} %pad_maximum_fusion.1), channel_id=1, source_target_pairs={{0,8},{8,16},{16,24},{24,32},{32,40},{40,48},{48,56},{56,64},{64,7... | collective-permute-start | bytes 786440 | tf_op jit(solution)/shard_map/ppermute | solution.py:64
  10.6 25.6 %collective-permute-start.1 = (bf16[1024,512]{1,0:T(8,128)(2,1)S(1)}, bf16[1024,512]{1,0:T(8,128)(2,1)S(1)}, u32[]{:S(2)}, u32[]{:S(2)}) collective-permute-start(bf16[1024,512]{1,0:T(8,128)(2,1)S(1)} %pad_maximum_fusion.refs_0_), channel_id=1, source_target_pairs={{0,4},{1,5},{2,6},{3,7},{4,0},{5,1},{6,2},{7,3},{8,12},{9,13},{10,... | collective-permute-start | bytes 3145736 | tf_op jit(solution)/shard_map/ppermute | solution.py:58
  11.0 25.7 %collective-permute-start.5 = (bf16[1024,512]{1,0:T(8,128)(2,1)S(1)}, bf16[1024,512]{1,0:T(8,128)(2,1)S(1)}, u32[]{:S(2)}, u32[]{:S(2)}) collective-permute-start(bf16[1024,512]{1,0:T(8,128)(2,1)S(1)} %pad_maximum_fusion.refs_0_), channel_id=1, source_target_pairs={{0,1},{1,2},{2,3},{3,0},{4,5},{5,6},{6,7},{7,4},{8,9},{9,10},{10,1... | collective-permute-start | bytes 3145736 | tf_op jit(solution)/shard_map/ppermute | solution.py:58
  12.2 25.1 %collective-permute-start.6 = (bf16[1024,512]{1,0:T(8,128)(2,1)S(1)}, bf16[1024,512]{1,0:T(8,128)(2,1)S(1)}, u32[]{:S(2)}, u32[]{:S(2)}) collective-permute-start(bf16[1024,512]{1,0:T(8,128)(2,1)S(1)} %pad_maximum_fusion.refs_0_), channel_id=1, source_target_pairs={{0,3},{1,0},{2,1},{3,2},{4,7},{5,4},{6,5},{7,6},{8,11},{9,8},{10,9... | collective-permute-start | bytes 3145736 | tf_op jit(solution)/shard_map/ppermute | solution.py:58
  14.5 26.9 %collective-permute-start.10 = (bf16[512,1024]{1,0:T(8,128)(2,1)S(1)}, bf16[512,1024]{1,0:T(8,128)(2,1)S(1)}, u32[]{:S(2)}, u32[]{:S(2)}) collective-permute-start(bf16[512,1024]{1,0:T(8,128)(2,1)S(1)} %copy-done.4), channel_id=1, source_target_pairs={{0,32},{8,40},{16,48},{24,56},{32,64},{40,72},{48,80},{56,88},{64,... | collective-permute-start | bytes 3145736 | tf_op jit(solution)/shard_map/ppermute | solution.py:50
  16.1 25.2 %collective-permute-start.11 = (bf16[512,1024]{1,0:T(8,128)(2,1)S(1)}, bf16[512,1024]{1,0:T(8,128)(2,1)S(1)}, u32[]{:S(2)}, u32[]{:S(2)}) collective-permute-start(bf16[512,1024]{1,0:T(8,128)(2,1)S(1)} %copy-done.4), channel_id=1, source_target_pairs={{0,96},{8,104},{16,112},{24,120},{32,0},{40,8},{48,16},{56,24},{64... | collective-permute-start | bytes 3145736 | tf_op jit(solution)/shard_map/ppermute | solution.py:50
  36.1 7.6 %collective-permute-start.7 = (bf16[512,1024]{1,0:T(8,128)(2,1)S(1)}, bf16[512,1024]{1,0:T(8,128)(2,1)S(1)}, u32[]{:S(2)}, u32[]{:S(2)}) collective-permute-start(bf16[512,1024]{1,0:T(8,128)(2,1)S(1)} %get-tuple-element.82), channel_id=1, source_target_pairs={{0,8},{8,0},{16,24},{24,16},{32,40},{40,32},{48,56},{56,48},{64,72... | collective-permute-start | bytes 3145736 | tf_op jit(solution)/shard_map/ppermute | solution.py:50
  36.8 26.1 %collective-permute-start.3 = (bf16[1024,512]{1,0:T(8,128)(2,1)S(1)}, bf16[1024,512]{1,0:T(8,128)(2,1)S(1)}, u32[]{:S(2)}, u32[]{:S(2)}) collective-permute-start(bf16[1024,512]{1,0:T(8,128)(2,1)S(1)} %collective-permute-done.1.refs_3_), channel_id=1, source_target_pairs={{0,1},{1,2},{2,3},{3,0},{4,5},{5,6},{6,7},{7,4},{8,9},{9,10},{10,1... | collective-permute-start | bytes 3145736 | tf_op jit(solution)/shard_map/ppermute | solution.py:58
  37.4 25.5 %collective-permute-start.4 = (bf16[1024,512]{1,0:T(8,128)(2,1)S(1)}, bf16[1024,512]{1,0:T(8,128)(2,1)S(1)}, u32[]{:S(2)}, u32[]{:S(2)}) collective-permute-start(bf16[1024,512]{1,0:T(8,128)(2,1)S(1)} %collective-permute-done.1.refs_3_), channel_id=1, source_target_pairs={{0,3},{1,0},{2,1},{3,2},{4,7},{5,4},{6,5},{7,6},{8,11},{9,8},{10,9... | collective-permute-start | bytes 3145736 | tf_op jit(solution)/shard_map/ppermute | solution.py:58
  41.3 24.8 %collective-permute-start.12 = (bf16[512,1024]{1,0:T(8,128)(2,1)S(1)}, bf16[512,1024]{1,0:T(8,128)(2,1)S(1)}, u32[]{:S(2)}, u32[]{:S(2)}) collective-permute-start(bf16[512,1024]{1,0:T(8,128)(2,1)S(1)} %collective-permute-done.10.refs_9_), channel_id=1, source_target_pairs={{0,32},{8,40},{16,48},{24,56},{32,64},{40,72},{48,80},{56,88},{64,... | collective-permute-start | bytes 3145736 | tf_op jit(solution)/shard_map/ppermute | solution.py:50
  41.3 24.8 %collective-permute-start.13 = (bf16[512,1024]{1,0:T(8,128)(2,1)S(1)}, bf16[512,1024]{1,0:T(8,128)(2,1)S(1)}, u32[]{:S(2)}, u32[]{:S(2)}) collective-permute-start(bf16[512,1024]{1,0:T(8,128)(2,1)S(1)} %copy-done.4), channel_id=1, source_target_pairs={{0,16},{8,24},{16,0},{24,8},{32,48},{40,56},{48,32},{56,40},{64,80... | collective-permute-start | bytes 3145736 | tf_op jit(solution)/shard_map/ppermute | solution.py:50
  43.8 41.5 %collective-permute-start.9 = (bf16[1024,512]{1,0:T(8,128)(2,1)S(1)}, bf16[1024,512]{1,0:T(8,128)(2,1)S(1)}, u32[]{:S(2)}, u32[]{:S(2)}) collective-permute-start(bf16[1024,512]{1,0:T(8,128)(2,1)S(1)} %collective-permute-done.5.refs_1_), channel_id=1, source_target_pairs={{0,1},{1,2},{2,3},{3,0},{4,5},{5,6},{6,7},{7,4},{8,9},{9,10},{10,1... | collective-permute-start | bytes 3145736 | tf_op jit(solution)/shard_map/ppermute | solution.py:58
  62.8 25.3 %collective-permute-start.8 = (bf16[1024,512]{1,0:T(8,128)(2,1)S(1)}, bf16[1024,512]{1,0:T(8,128)(2,1)S(1)}, u32[]{:S(2)}, u32[]{:S(2)}) collective-permute-start(bf16[1024,512]{1,0:T(8,128)(2,1)S(1)} %collective-permute-done.4.refs_1_.refs_5_), channel_id=1, source_target_pairs={{0,3},{1,0},{2,1},{3,2},{4,7},{5,4},{6,5},{7,6},{8,11},{9,8},{10,9... | collective-permute-start | bytes 3145736 | tf_op jit(solution)/shard_map/ppermute | solution.py:58
  66.2 29.2 %collective-permute-start.14 = (bf16[512,1024]{1,0:T(8,128)(2,1)S(1)}, bf16[512,1024]{1,0:T(8,128)(2,1)S(1)}, u32[]{:S(2)}, u32[]{:S(2)}) collective-permute-start(bf16[512,1024]{1,0:T(8,128)(2,1)S(1)} %collective-permute-done.13.refs_11_), channel_id=1, source_target_pairs={{0,32},{8,40},{16,48},{24,56},{32,64},{40,72},{48,80},{56,88},{64,... | collective-permute-start | bytes 3145736 | tf_op jit(solution)/shard_map/ppermute | solution.py:50
  67.2 29.8 %collective-permute-start.15 = (bf16[512,1024]{1,0:T(8,128)(2,1)S(1)}, bf16[512,1024]{1,0:T(8,128)(2,1)S(1)}, u32[]{:S(2)}, u32[]{:S(2)}) collective-permute-start(bf16[512,1024]{1,0:T(8,128)(2,1)S(1)} %collective-permute-done.13.refs_11_), channel_id=1, source_target_pairs={{0,96},{8,104},{16,112},{24,120},{32,0},{40,8},{48,16},{56,24},{64... | collective-permute-start | bytes 3145736 | tf_op jit(solution)/shard_map/ppermute | solution.py:50
  69.5 27.5 %collective-permute-start.16 = (bf16[512,1024]{1,0:T(8,128)(2,1)S(1)}, bf16[512,1024]{1,0:T(8,128)(2,1)S(1)}, u32[]{:S(2)}, u32[]{:S(2)}) collective-permute-start(bf16[512,1024]{1,0:T(8,128)(2,1)S(1)} %collective-permute-done.12.refs_15_), channel_id=1, source_target_pairs={{0,16},{8,24},{16,0},{24,8},{32,48},{40,56},{48,32},{56,40},{64,80... | collective-permute-start | bytes 3145736 | tf_op jit(solution)/shard_map/ppermute | solution.py:50
  92.1 32.2 %collective-permute-start.22 = (bf16[640,1024]{1,0:T(8,128)(2,1)S(1)}, bf16[640,1024]{1,0:T(8,128)(2,1)S(1)}, u32[]{:S(2)}, u32[]{:S(2)}) collective-permute-start(bf16[640,1024]{1,0:T(8,128)(2,1)S(1)} %get-tuple-element.86), channel_id=1, source_target_pairs={{0,32},{8,40},{16,48},{24,56},{32,64},{40,72},{48,80},{56,88},{64,... | collective-permute-start | bytes 3932168 | tf_op jit(solution)/shard_map/ppermute | solution.py:50
  93.4 26.8 %collective-permute-start.19 = (bf16[512,1024]{1,0:T(8,128)(2,1)S(1)}, bf16[512,1024]{1,0:T(8,128)(2,1)S(1)}, u32[]{:S(2)}, u32[]{:S(2)}) collective-permute-start(bf16[512,1024]{1,0:T(8,128)(2,1)S(1)} %get-tuple-element.101), channel_id=1, source_target_pairs={{0,16},{8,24},{16,0},{24,8},{32,48},{40,56},{48,32},{56,40},{64,80... | collective-permute-start | bytes 3145736 | tf_op jit(solution)/shard_map/ppermute | solution.py:50
  95.3 30.5 %collective-permute-start.23 = (bf16[640,1024]{1,0:T(8,128)(2,1)S(1)}, bf16[640,1024]{1,0:T(8,128)(2,1)S(1)}, u32[]{:S(2)}, u32[]{:S(2)}) collective-permute-start(bf16[640,1024]{1,0:T(8,128)(2,1)S(1)} %get-tuple-element.112), channel_id=1, source_target_pairs={{0,96},{8,104},{16,112},{24,120},{32,0},{40,8},{48,16},{56,24},{64... | collective-permute-start | bytes 3932168 | tf_op jit(solution)/shard_map/ppermute | solution.py:50
  109.6 4.8 %collective-permute-start.17 = (bf16[256,1024]{1,0:T(8,128)(2,1)S(1)}, bf16[256,1024]{1,0:T(8,128)(2,1)S(1)}, u32[]{:S(2)}, u32[]{:S(2)}) collective-permute-start(bf16[256,1024]{1,0:T(8,128)(2,1)S(1)} %get-tuple-element.95), channel_id=1, source_target_pairs={{0,8},{8,0},{16,24},{24,16},{32,40},{40,32},{48,56},{56,48},{64,72... | collective-permute-start | bytes 1572872 | tf_op jit(solution)/shard_map/ppermute | solution.py:50
  111.6 2.9 %collective-permute-start.18 = (bf16[256,1024]{1,0:T(8,128)(2,1)S(1)}, bf16[256,1024]{1,0:T(8,128)(2,1)S(1)}, u32[]{:S(2)}, u32[]{:S(2)}) collective-permute-start(bf16[256,1024]{1,0:T(8,128)(2,1)S(1)} %get-tuple-element.96), channel_id=1, source_target_pairs={{0,8},{8,0},{16,24},{24,16},{32,40},{40,32},{48,56},{56,48},{64,72... | collective-permute-start | bytes 1572872 | tf_op jit(solution)/shard_map/ppermute | solution.py:50
  120.4 15.3 %collective-permute-start.20 = (bf16[256,1024]{1,0:T(8,128)(2,1)S(1)}, bf16[256,1024]{1,0:T(8,128)(2,1)S(1)}, u32[]{:S(2)}, u32[]{:S(2)}) collective-permute-start(bf16[256,1024]{1,0:T(8,128)(2,1)S(1)} %get-tuple-element.106), channel_id=1, source_target_pairs={{0,32},{8,40},{16,48},{24,56},{32,64},{40,72},{48,80},{56,88},{64,... | collective-permute-start | bytes 1572872 | tf_op jit(solution)/shard_map/ppermute | solution.py:50
  120.6 15.4 %collective-permute-start.21 = (bf16[256,1024]{1,0:T(8,128)(2,1)S(1)}, bf16[256,1024]{1,0:T(8,128)(2,1)S(1)}, u32[]{:S(2)}, u32[]{:S(2)}) collective-permute-start(bf16[256,1024]{1,0:T(8,128)(2,1)S(1)} %get-tuple-element.107), channel_id=1, source_target_pairs={{0,96},{8,104},{16,112},{24,120},{32,0},{40,8},{48,16},{56,24},{64... | collective-permute-start | bytes 1572872 | tf_op jit(solution)/shard_map/ppermute | solution.py:50
  123.2 18.2 %collective-permute-start.24 = (bf16[128,1024]{1,0:T(8,128)(2,1)S(1)}, bf16[128,1024]{1,0:T(8,128)(2,1)S(1)}, u32[]{:S(2)}, u32[]{:S(2)}) collective-permute-start(bf16[128,1024]{1,0:T(8,128)(2,1)S(1)} %get-tuple-element.126), channel_id=1, source_target_pairs={{0,32},{8,40},{16,48},{24,56},{32,64},{40,72},{48,80},{56,88},{64,... | collective-permute-start | bytes 786440 | tf_op jit(solution)/shard_map/ppermute | solution.py:50
  124.3 17.3 %collective-permute-start.25 = (bf16[128,1024]{1,0:T(8,128)(2,1)S(1)}, bf16[128,1024]{1,0:T(8,128)(2,1)S(1)}, u32[]{:S(2)}, u32[]{:S(2)}) collective-permute-start(bf16[128,1024]{1,0:T(8,128)(2,1)S(1)} %get-tuple-element.127), channel_id=1, source_target_pairs={{0,96},{8,104},{16,112},{24,120},{32,0},{40,8},{48,16},{56,24},{64... | collective-permute-start | bytes 786440 | tf_op jit(solution)/shard_map/ppermute | solution.py:50
  126.2 29.9 %collective-permute-start.26 = (bf16[512,1024]{1,0:T(8,128)(2,1)S(1)}, bf16[512,1024]{1,0:T(8,128)(2,1)S(1)}, u32[]{:S(2)}, u32[]{:S(2)}) collective-permute-start(bf16[512,1024]{1,0:T(8,128)(2,1)S(1)} %add_rows.7), channel_id=1, source_target_pairs={{0,16},{8,24},{16,0},{24,8},{32,48},{40,56},{48,32},{56,40},{64,80... | collective-permute-start | bytes 3145736 | tf_op jit(solution)/shard_map/ppermute | solution.py:50
  136.2 19.9 %collective-permute-start.27 = (bf16[256,1024]{1,0:T(8,128)(2,1)S(1)}, bf16[256,1024]{1,0:T(8,128)(2,1)S(1)}, u32[]{:S(2)}, u32[]{:S(2)}) collective-permute-start(bf16[256,1024]{1,0:T(8,128)(2,1)S(1)} %get-tuple-element.131), channel_id=1, source_target_pairs={{0,32},{8,40},{16,48},{24,56},{32,64},{40,72},{48,80},{56,88},{64,... | collective-permute-start | bytes 1572872 | tf_op jit(solution)/shard_map/ppermute | solution.py:50
  141.6 14.5 %collective-permute-start.28 = (bf16[256,1024]{1,0:T(8,128)(2,1)S(1)}, bf16[256,1024]{1,0:T(8,128)(2,1)S(1)}, u32[]{:S(2)}, u32[]{:S(2)}) collective-permute-start(bf16[256,1024]{1,0:T(8,128)(2,1)S(1)} %get-tuple-element.138), channel_id=1, source_target_pairs={{0,96},{8,104},{16,112},{24,120},{32,0},{40,8},{48,16},{56,24},{64... | collective-permute-start | bytes 1572872 | tf_op jit(solution)/shard_map/ppermute | solution.py:50
  151.7 10.5 %collective-permute-start.29 = (bf16[512,256]{1,0:T(8,128)(2,1)S(1)}, bf16[512,256]{1,0:T(8,128)(2,1)S(1)}, u32[]{:S(2)}, u32[]{:S(2)}) collective-permute-start(bf16[512,256]{1,0:T(8,128)(2,1)S(1)} %pad_maximum_fusion.2), channel_id=1, source_target_pairs={{8,0},{16,8},{24,16},{32,24},{40,32},{48,40},{56,48},{64,56},{72,6... | collective-permute-start | bytes 786440 | tf_op jit(solution)/shard_map/ppermute | solution.py:64

commit v15 on v14

--- a/solution.py
+++ b/solution.py
@@ -260,8 +260,9 @@
     step = pl.program_id(0)
     rows = done.shape[2]
 
-    def put(j):
-        return pltpu.make_async_copy(done.at[j], buffer_ref.at[:, meta_ref[AT_G + slots[j]]], sems.at[j])
+    def put(j, half):
+        place = meta_ref[AT_G + slots[j]]
+        return pltpu.make_async_copy(done.at[j, half], buffer_ref.at[half, place], sems.at[j, half])
 
     def take(i, made):
         out, start, at, half, first, count = plan[i]
@@ -290,22 +291,24 @@
 
         @pl.when(step == j)
         def _():
-            value = lax.dot_general(
-                pieces[j][...], a_ref[...], (((0,), (0,)), ((), ())), preferred_element_type=F32
-            ).astype(BF)
-            done[j, 0] = value[:rows]
-            done[j, 1] = value[rows:]
-            put(j).start()
-            for i in range(len(plan)):
-
-                @pl.when(made_here(i, j))
-                def _():
-                    take(i, j).start()
+            for half in range(2):
+                part = pieces[j][:, half * rows:(half + 1) * rows]
+                done[j, half] = lax.dot_general(
+                    part, a_ref[...], (((0,), (0,)), ((), ())), preferred_element_type=F32
+                ).astype(BF)
+                put(j, half).start()
+                for i in range(len(plan)):
+                    if plan[i][3] == half:
+
+                        @pl.when(made_here(i, j))
+                        def _(i=i):
+                            take(i, j).start()
 
     @pl.when(step == n_in - 1)
     def _():
         for j in range(n_in):
-            put(j).wait()
+            for half in range(2):
+                put(j, half).wait()
         for i in range(len(plan)):
             take(i, None).wait()
 
@@ -330,7 +333,7 @@
             out_specs=[there] + [here] * n_taken,
             scratch_shapes=[
                 pltpu.VMEM((n_blocks, *shape), BF),
-                pltpu.SemaphoreType.DMA((n_blocks,)),
+                pltpu.SemaphoreType.DMA((n_blocks, 2)),
                 pltpu.SemaphoreType.DMA((max(len(plan), 1),)),
             ],
         ),

time: 163 us -> 162 us (level)
  transfers between devices with their start and end apart: 30 -> 30, of which waited for: 13 -> 13; matrix products, arithmetic and copies ran while one was open for 1% -> 1% of each run, Pallas kernels for 44% -> 43%
where the time goes in v15:
time: 162 us
  Pallas kernels  69.7 us (43%)
  starting transfers between devices  48.1 us (30%)
  waiting for transfers between devices  38.3 us (24%)
  local copies, waits for them, and re-layouts  2.52 us (2%)
  other arithmetic  1.97 us (1%)
    ppermute x21, starting transfers between devices, move_row(): return lax.ppermute(value, 'row', pairs)  30 us
    ppermute x7, waiting for transfers between devices, move_col(): return lax.ppermute(value, 'col', pairs)  26.4 us
    pallas_call x3, Pallas kernels, attend_back(): pl.pallas_call(functools.partial(bwd_kernel, len(earlier), last), grid_sp...  20.6 us
    pallas_call x4, Pallas kernels, project(): pl.pallas_call(functools.partial(proj_kernel, tuple(slots), held, plan),...  16.3 us
    pallas_call x1, Pallas kernels, attend(): pl.pallas_call(fwd_kernel, grid_spec=pltpu.PrefetchScalarGridSpec(num_sca...  14.9 us
    pallas_call x1, Pallas kernels, attn_grad_part(): pl.pallas_call(kernel, grid_spec=pltpu.PrefetchScalarGridSpec(num_scalar_...  12.6 us
    ppermute x2, starting transfers between devices, passed_along(): lax.ppermute(value, axis, [(source, source + steps) for source in range(f...  9.07 us
    ppermute x7, starting transfers between devices, move_col(): return lax.ppermute(value, 'col', pairs)  9.05 us
  transfers between devices with their start and end apart: 30, of which 13 were waited for; matrix products, arithmetic and copies ran while one was open for 1% of the time, Pallas kernels for 43%

profile of v15, /device:TPU:1, one launch (start us, length us, event | category | flops | bytes accessed | tf_op | source)
XLA Modules:
  0.0 161.7 jit_solution(3451839029377536233)
XLA Ops:
  0.6 0.0 copy-start.5
  0.6 0.0 copy-start.6
  0.7 2.2 %constant_dynamic-slice_fusion = (bf16[512,512]{1,0:T(8,128)(2,1)S(1)}, bf16[512,512]{1,0:T(8,128)(2,1)}) fusion(bf16[512,1024]{1,0:T(8,128)(2,1)} %param.13, s32[]{:T(128)S(6)} %select_n.38, s32[]{:T(128)S(6)} %select_n.32), kind=kLoop, calls=%fused_computation.13 | loop fusion | bytes 2097160 | tf_op jit(solution)/shard_map/dynamic_slice | solution.py:524
  3.0 1.4 collective-permute-start
  4.4 4.8 %collective-permute-start.2 = (bf16[512,256]{1,0:T(8,128)(2,1)S(1)}, bf16[512,256]{1,0:T(8,128)(2,1)S(1)}, u32[]{:S(2)}, u32[]{:S(2)}) collective-permute-start(bf16[512,256]{1,0:T(8,128)(2,1)S(1)} %pad_maximum_fusion.1), channel_id=1, source_target_pairs={{0,8},{8,16},{16,24},{24,32},{32,40},{40,48},{48,56},{56,64},{64,7... | collective-permute-start | bytes 786440 | tf_op jit(solution)/shard_map/ppermute | solution.py:64
  9.3 0.1 concatenate.16.meta_ref
  9.4 1.1 pad_maximum_fusion.refs_0_
  10.6 0.5 collective-permute-start.1
  11.0 1.2 collective-permute-start.5
  12.2 1.5 collective-permute-start.6
  13.7 0.7 collective-permute-done.2.kv_ref
  14.5 1.6 %collective-permute-start.10 = (bf16[512,1024]{1,0:T(8,128)(2,1)S(1)}, bf16[512,1024]{1,0:T(8,128)(2,1)S(1)}, u32[]{:S(2)}, u32[]{:S(2)}) collective-permute-start(bf16[512,1024]{1,0:T(8,128)(2,1)S(1)} %copy-done.4), channel_id=1, source_target_pairs={{0,32},{8,40},{16,48},{24,56},{32,64},{40,72},{48,80},{56,88},{64,... | collective-permute-start | bytes 3145736 | tf_op jit(solution)/shard_map/ppermute | solution.py:50
  16.1 2.1 %collective-permute-start.11 = (bf16[512,1024]{1,0:T(8,128)(2,1)S(1)}, bf16[512,1024]{1,0:T(8,128)(2,1)S(1)}, u32[]{:S(2)}, u32[]{:S(2)}) collective-permute-start(bf16[512,1024]{1,0:T(8,128)(2,1)S(1)} %copy-done.4), channel_id=1, source_target_pairs={{0,96},{8,104},{16,112},{24,120},{32,0},{40,8},{48,16},{56,24},{64... | collective-permute-start | bytes 3145736 | tf_op jit(solution)/shard_map/ppermute | solution.py:50
  18.2 14.9 %attend.1 = (bf16[512,1024]{1,0:T(8,128)(2,1)S(1)}, f32[8,1,512]{2,1,0:T(1,128)S(1)}, f32[8,1,512]{2,1,0:T(1,128)S(1)}) custom-call(s32[24]{0:T(128)S(1)} %concatenate.16.meta_ref, bf16[512,1024]{1,0:T(8,128)(2,1)S(1)} %copy-done, bf16[512,256]{1,0:T(8,128)(2,1)S(1)} %collective-permute-done.2.kv_ref, bf16[512,128]{1,0:T(8,128)(2,1)S(1)} %copy-done.2, ...), custom_call_target="tpu_custom_call" | custom-call | flops 68719476736 | bytes 8388608 | tf_op jit(solution)/shard_map/attend/pallas_call | solution.py:148
  33.1 3.0 %collective-permute-done.1.refs_3_ = bf16[1024,512]{1,0:T(8,128)(2,1)S(1)} collective-permute-done((bf16[1024,512]{1,0:T(8,128)(2,1)S(1)}, bf16[1024,512]{1,0:T(8,128)(2,1)S(1)}, u32[]{:S(2)}, u32[]{:S(2)}) %collective-permute-start.1) | collective-permute-done | bytes 1048608 | tf_op jit(solution)/shard_map/ppermute | solution.py:58
  36.1 0.6 collective-permute-done.5.refs_1_
  36.8 0.6 collective-permute-start.3
  37.4 2.4 %collective-permute-start.4 = (bf16[1024,512]{1,0:T(8,128)(2,1)S(1)}, bf16[1024,512]{1,0:T(8,128)(2,1)S(1)}, u32[]{:S(2)}, u32[]{:S(2)}) collective-permute-start(bf16[1024,512]{1,0:T(8,128)(2,1)S(1)} %collective-permute-done.1.refs_3_), channel_id=1, source_target_pairs={{0,3},{1,0},{2,1},{3,2},{4,7},{5,4},{6,5},{7,6},{8,11},{9,8},{10,9... | collective-permute-start | bytes 3145736 | tf_op jit(solution)/shard_map/ppermute | solution.py:58
  39.8 1.5 collective-permute-done.10.refs_9_
  41.3 0.0 collective-permute-start.12
  41.3 2.4 %collective-permute-start.13 = (bf16[512,1024]{1,0:T(8,128)(2,1)S(1)}, bf16[512,1024]{1,0:T(8,128)(2,1)S(1)}, u32[]{:S(2)}, u32[]{:S(2)}) collective-permute-start(bf16[512,1024]{1,0:T(8,128)(2,1)S(1)} %copy-done.4), channel_id=1, source_target_pairs={{0,16},{8,24},{16,0},{24,8},{32,48},{40,56},{48,32},{56,40},{64,80... | collective-permute-start | bytes 3145736 | tf_op jit(solution)/shard_map/ppermute | solution.py:50
  43.7 0.1 constant_dynamic-update-slice_fusion.1
  43.8 0.1 collective-permute-start.9
  43.9 0.1 constant_dynamic-update-slice_fusion.refs_4_.refs_2_.refs_1_
  43.9 6.6 %project.4.refs_3_ = bf16[2,64,256,1024]{3,2,1,0:T(8,128)(2,1)} custom-call(s32[24]{0:T(128)S(1)} %concatenate.16.meta_ref, bf16[1024,512]{1,0:T(8,128)(2,1)S(1)} %pad_maximum_fusion.refs_0_, bf16[1024,512]{1,0:T(8,128)(2,1)S(1)} %collective-permute-done.5.refs_1_, bf16[1024,512]{1,0:T(8,128)(2,1)S(1)} %collective-permute-done.6.refs_2_, ...), custom_call_target="tpu_custom_call" | custom-call | flops 4294967296 | bytes 10485760 | tf_op jit(solution)/shard_map/project/pallas_call | solution.py:327
  50.6 12.3 %collective-permute-done.3.refs_0_.refs_4_ = bf16[1024,512]{1,0:T(8,128)(2,1)S(1)} collective-permute-done((bf16[1024,512]{1,0:T(8,128)(2,1)S(1)}, bf16[1024,512]{1,0:T(8,128)(2,1)S(1)}, u32[]{:S(2)}, u32[]{:S(2)}) %collective-permute-start.3) | collective-permute-done | bytes 1048608 | tf_op jit(solution)/shard_map/ppermute | solution.py:58
  62.8 2.8 %collective-permute-start.8 = (bf16[1024,512]{1,0:T(8,128)(2,1)S(1)}, bf16[1024,512]{1,0:T(8,128)(2,1)S(1)}, u32[]{:S(2)}, u32[]{:S(2)}) collective-permute-start(bf16[1024,512]{1,0:T(8,128)(2,1)S(1)} %collective-permute-done.4.refs_1_.refs_5_), channel_id=1, source_target_pairs={{0,3},{1,0},{2,1},{3,2},{4,7},{5,4},{6,5},{7,6},{8,11},{9,8},{10,9... | collective-permute-start | bytes 3145736 | tf_op jit(solution)/shard_map/ppermute | solution.py:58
  65.7 0.5 collective-permute-done.12.refs_15_
  66.2 1.0 collective-permute-start.14
  67.2 2.3 %collective-permute-start.15 = (bf16[512,1024]{1,0:T(8,128)(2,1)S(1)}, bf16[512,1024]{1,0:T(8,128)(2,1)S(1)}, u32[]{:S(2)}, u32[]{:S(2)}) collective-permute-start(bf16[512,1024]{1,0:T(8,128)(2,1)S(1)} %collective-permute-done.13.refs_11_), channel_id=1, source_target_pairs={{0,96},{8,104},{16,112},{24,120},{32,0},{40,8},{48,16},{56,24},{64... | collective-permute-start | bytes 3145736 | tf_op jit(solution)/shard_map/ppermute | solution.py:50
  69.5 1.3 collective-permute-start.16
  70.8 4.0 %project.5.refs_2_ = bf16[2,64,256,1024]{3,2,1,0:T(8,128)(2,1)} custom-call(s32[24]{0:T(128)S(1)} %concatenate.16.meta_ref, bf16[1024,512]{1,0:T(8,128)(2,1)S(1)} %collective-permute-done.3.refs_0_.refs_4_, bf16[1024,512]{1,0:T(8,128)(2,1)S(1)} %collective-permute-done.4.refs_1_.refs_5_, ...), custom_call_target="tpu_custom_call", output_to_operand_aliasing={{}: (4, {})} | custom-call | flops 2147483648 | bytes 6291456 | tf_op jit(solution)/shard_map/project/pallas_call | solution.py:327
  74.9 10.5 %collective-permute-done.9.refs_0_.refs_6_ = bf16[1024,512]{1,0:T(8,128)(2,1)S(1)} collective-permute-done((bf16[1024,512]{1,0:T(8,128)(2,1)S(1)}, bf16[1024,512]{1,0:T(8,128)(2,1)S(1)}, u32[]{:S(2)}, u32[]{:S(2)}) %collective-permute-start.9) | collective-permute-done | bytes 1048608 | tf_op jit(solution)/shard_map/ppermute | solution.py:58
  85.3 2.6 %project.6.refs_2_ = bf16[2,64,256,1024]{3,2,1,0:T(8,128)(2,1)} custom-call(s32[24]{0:T(128)S(1)} %concatenate.16.meta_ref, bf16[1024,512]{1,0:T(8,128)(2,1)S(1)} %collective-permute-done.9.refs_0_.refs_6_, bf16[1024,1024]{1,0:T(8,128)(2,1)S(1)} %constant_dynamic-update-slice_fusion.refs_4_.refs_2_.refs_1_, ...), custom_call_target="tpu_custom_call", output_to_operand_aliasing={{}: (3, {})} | custom-call | flops 1073741824 | bytes 4194304 | tf_op jit(solution)/shard_map/project/pallas_call | solution.py:327
  88.0 3.0 %project.7 = (bf16[2,64,256,1024]{3,2,1,0:T(8,128)(2,1)}, bf16[512,1024]{1,0:T(8,128)(2,1)S(1)}, bf16[640,1024]{1,0:T(8,128)(2,1)S(1)}, bf16[640,1024]{1,0:T(8,1...) custom-call(s32[24]{0:T(128)S(1)} %concatenate.16.meta_ref, ...), custom_call_target="tpu_custom_call", output_to_operand_aliasing={{0}: (3, {})} | custom-call | flops 1073741824 | bytes 4194304 | tf_op jit(solution)/shard_map/project/pallas_call | solution.py:327
  91.0 1.1 collective-permute-start.22
  92.1 2.3 %collective-permute-start.19 = (bf16[512,1024]{1,0:T(8,128)(2,1)S(1)}, bf16[512,1024]{1,0:T(8,128)(2,1)S(1)}, u32[]{:S(2)}, u32[]{:S(2)}) collective-permute-start(bf16[512,1024]{1,0:T(8,128)(2,1)S(1)} %get-tuple-element.101), channel_id=1, source_target_pairs={{0,16},{8,24},{16,0},{24,8},{32,48},{40,56},{48,32},{56,40},{64,80... | collective-permute-start | bytes 3145736 | tf_op jit(solution)/shard_map/ppermute | solution.py:50
  94.4 1.7 %collective-permute-start.23 = (bf16[640,1024]{1,0:T(8,128)(2,1)S(1)}, bf16[640,1024]{1,0:T(8,128)(2,1)S(1)}, u32[]{:S(2)}, u32[]{:S(2)}) collective-permute-start(bf16[640,1024]{1,0:T(8,128)(2,1)S(1)} %get-tuple-element.112), channel_id=1, source_target_pairs={{0,96},{8,104},{16,112},{24,120},{32,0},{40,8},{48,16},{56,24},{64... | collective-permute-start | bytes 3932168 | tf_op jit(solution)/shard_map/ppermute | solution.py:50
  96.1 12.6 %attn_grad.1 = (f32[512,1024]{1,0:T(8,128)S(1)}, bf16[256,1024]{1,0:T(8,128)(2,1)S(1)}, bf16[256,1024]{1,0:T(8,128)(2,1)S(1)}) custom-call(s32[24]{0:T(128)S(1)} %concatenate.16.meta_ref, bf16[1024,512]{1,0:T(8,128)(2,1)S(1)} %pad_maximum_fusion.refs_0_, bf16[1024,512]{1,0:T(8,128)(2,1)S(1)} %collective-permute-done.5.refs_1_, ...), custom_call_target="tpu_custom_call" | custom-call | flops 8589934592 | bytes 20971520 | tf_op jit(solution)/shard_map/attn_grad/pallas_call | solution.py:422
  108.7 2.1 %collective-permute-start.17 = (bf16[256,1024]{1,0:T(8,128)(2,1)S(1)}, bf16[256,1024]{1,0:T(8,128)(2,1)S(1)}, u32[]{:S(2)}, u32[]{:S(2)}) collective-permute-start(bf16[256,1024]{1,0:T(8,128)(2,1)S(1)} %get-tuple-element.95), channel_id=1, source_target_pairs={{0,8},{8,0},{16,24},{24,16},{32,40},{40,32},{48,56},{56,48},{64,72... | collective-permute-start | bytes 1572872 | tf_op jit(solution)/shard_map/ppermute | solution.py:50
  110.8 0.1 collective-permute-start.18
  110.9 2.8 %fetch.1 = (bf16[512,1024]{1,0:T(8,128)(2,1)S(1)}, bf16[512,1024]{1,0:T(8,128)(2,1)S(1)}, bf16[512,1024]{1,0:T(8,128)(2,1)S(1)}, bf16[512,1024]{1,0:T(8,128)(2,1)S(1)}) custom-call(s32[24]{0:T(128)S(1)} %concatenate.16.meta_ref, bf16[2,64,256,1024]{3,2,1,0:T(8,128)(2,1)} %get-tuple-element.99.buffer_ref), custom_call_target="tpu_custom_call" | custom-call | bytes 65536 | tf_op jit(solution)/shard_map/fetch/pallas_call | solution.py:469
  113.7 0.2 add_rows.5.g_ref
  113.9 5.5 %attend_back.3 = (bf16[512,1024]{1,0:T(8,128)(2,1)}, f32[1024,128]{1,0:T(8,128)S(1)}, f32[1024,128]{1,0:T(8,128)S(1)}) custom-call(s32[24]{0:T(128)S(1)} %concatenate.16.meta_ref, bf16[512,1024]{1,0:T(8,128)(2,1)S(1)} %copy-done, bf16[512,1024]{1,0:T(8,128)(2,1)S(1)} %add_rows.5.g_ref, bf16[512,256]{1,0:T(8,128)(2,1)S(1)} %collective-permute-done.2.kv_ref, ...), custom_call_target="tpu_custom_call" | custom-call | flops 1048576 | bytes 65536 | tf_op jit(solution)/shard_map/attend_back/pallas_call | solution.py:226
  119.4 0.2 add_rows.6
  119.7 0.1 collective-permute-start.20
  119.8 2.7 %collective-permute-start.21 = (bf16[256,1024]{1,0:T(8,128)(2,1)S(1)}, bf16[256,1024]{1,0:T(8,128)(2,1)S(1)}, u32[]{:S(2)}, u32[]{:S(2)}) collective-permute-start(bf16[256,1024]{1,0:T(8,128)(2,1)S(1)} %get-tuple-element.107), channel_id=1, source_target_pairs={{0,96},{8,104},{16,112},{24,120},{32,0},{40,8},{48,16},{56,24},{64... | collective-permute-start | bytes 1572872 | tf_op jit(solution)/shard_map/ppermute | solution.py:50
  122.4 0.4 collective-permute-done.22.refs_1_.refs_4_
  122.8 2.3 %collective-permute-start.25 = (bf16[128,1024]{1,0:T(8,128)(2,1)S(1)}, bf16[128,1024]{1,0:T(8,128)(2,1)S(1)}, u32[]{:S(2)}, u32[]{:S(2)}) collective-permute-start(bf16[128,1024]{1,0:T(8,128)(2,1)S(1)} %get-tuple-element.127), channel_id=1, source_target_pairs={{0,96},{8,104},{16,112},{24,120},{32,0},{40,8},{48,16},{56,24},{64... | collective-permute-start | bytes 786440 | tf_op jit(solution)/shard_map/ppermute | solution.py:50
  125.1 0.4 add_rows.7
  125.5 1.4 collective-permute-start.26
  126.9 7.5 %attend_back.4 = (bf16[512,1024]{1,0:T(8,128)(2,1)}, f32[1024,128]{1,0:T(8,128)S(1)}, f32[1024,128]{1,0:T(8,128)S(1)}) custom-call(s32[24]{0:T(128)S(1)} %concatenate.16.meta_ref, bf16[512,1024]{1,0:T(8,128)(2,1)S(1)} %copy-done, bf16[512,1024]{1,0:T(8,128)(2,1)S(1)} %add_rows.5.g_ref, ...), custom_call_target="tpu_custom_call", output_to_operand_aliasing={{0}: (11, {})} | custom-call | flops 4026531840 | bytes 6291456 | tf_op jit(solution)/shard_map/attend_back/pallas_call | solution.py:226
  134.4 0.5 collective-permute-done.20.refs_1_
  134.9 0.2 collective-permute-done.21.refs_2_
  135.1 0.2 add_rows.8
  135.3 1.4 collective-permute-start.27
  136.7 3.8 %collective-permute-done.24.refs_5_ = bf16[128,1024]{1,0:T(8,128)(2,1)S(1)} collective-permute-done((bf16[128,1024]{1,0:T(8,128)(2,1)S(1)}, bf16[128,1024]{1,0:T(8,128)(2,1)S(1)}, u32[]{:S(2)}, u32[]{:S(2)}) %collective-permute-start.24) | collective-permute-done | bytes 262176 | tf_op jit(solution)/shard_map/ppermute | solution.py:50
  140.5 0.2 collective-permute-done.25.refs_7_
  140.7 2.6 %collective-permute-start.28 = (bf16[256,1024]{1,0:T(8,128)(2,1)S(1)}, bf16[256,1024]{1,0:T(8,128)(2,1)S(1)}, u32[]{:S(2)}, u32[]{:S(2)}) collective-permute-start(bf16[256,1024]{1,0:T(8,128)(2,1)S(1)} %get-tuple-element.138), channel_id=1, source_target_pairs={{0,96},{8,104},{16,112},{24,120},{32,0},{40,8},{48,16},{56,24},{64... | collective-permute-start | bytes 1572872 | tf_op jit(solution)/shard_map/ppermute | solution.py:50
  143.2 7.6 %attend_back.5 = (bf16[512,1024]{1,0:T(8,128)(2,1)}, f32[1024,128]{1,0:T(8,128)S(1)}, f32[1024,128]{1,0:T(8,128)S(1)}) custom-call(s32[24]{0:T(128)S(1)} %concatenate.16.meta_ref, bf16[512,1024]{1,0:T(8,128)(2,1)S(1)} %copy-done, bf16[512,1024]{1,0:T(8,128)(2,1)S(1)} %add_rows.5.g_ref, ...), custom_call_target="tpu_custom_call", output_to_operand_aliasing={{0}: (11, {})} | custom-call | flops 4026531840 | bytes 6291456 | tf_op jit(solution)/shard_map/attend_back/pallas_call | solution.py:226
  150.9 4.3 %collective-permute-start.29 = (bf16[512,256]{1,0:T(8,128)(2,1)S(1)}, bf16[512,256]{1,0:T(8,128)(2,1)S(1)}, u32[]{:S(2)}, u32[]{:S(2)}) collective-permute-start(bf16[512,256]{1,0:T(8,128)(2,1)S(1)} %pad_maximum_fusion.2), channel_id=1, source_target_pairs={{8,0},{16,8},{24,16},{32,24},{40,32},{48,40},{56,48},{64,56},{72,6... | collective-permute-start | bytes 786440 | tf_op jit(solution)/shard_map/ppermute | solution.py:64
  155.2 1.5 add_rows.9
  156.7 4.2 %collective-permute-done.29 = bf16[512,256]{1,0:T(8,128)(2,1)S(1)} collective-permute-done((bf16[512,256]{1,0:T(8,128)(2,1)S(1)}, bf16[512,256]{1,0:T(8,128)(2,1)S(1)}, u32[]{:S(2)}, u32[]{:S(2)}) %collective-permute-start.29) | collective-permute-done | bytes 262176 | tf_op jit(solution)/shard_map/ppermute | solution.py:64
  160.9 0.8 fusion
  (39 shorter events, 0.2 us)
Async XLA Ops:
  0.6 8.7 %copy-start.5 = (s32[8]{0:T(128)S(1)}, s32[8]{0:T(128)}, u32[]{:S(2)}) copy-start(s32[8]{0:T(128)} %constant.79.clone) | copy-start | bytes 100
  0.6 8.7 %copy-start.6 = (s32[8]{0:T(128)S(1)}, s32[8]{0:T(128)}, u32[]{:S(2)}) copy-start(s32[8]{0:T(128)} %constant.80.clone) | copy-start | bytes 100
  0.7 8.7 %copy-start.7 = (s32[8]{0:T(128)S(1)}, s32[8]{0:T(128)}, u32[]{:S(2)}) copy-start(s32[8]{0:T(128)} %constant.81.clone) | copy-start | bytes 100
  0.7 3.7 %copy-start.2 = (bf16[512,128]{1,0:T(8,128)(2,1)S(1)}, bf16[512,128]{1,0:T(8,128)(2,1)}, u32[]{:S(2)}) copy-start(bf16[512,128]{1,0:T(8,128)(2,1)} %k_ref.7) | copy-start | bytes 393220
  0.7 3.7 %copy-start.1 = (bf16[512,128]{1,0:T(8,128)(2,1)S(1)}, bf16[512,128]{1,0:T(8,128)(2,1)}, u32[]{:S(2)}) copy-start(bf16[512,128]{1,0:T(8,128)(2,1)} %v_ref.7) | copy-start | bytes 393220
  0.7 13.7 %copy-start.4 = (bf16[512,1024]{1,0:T(8,128)(2,1)S(1)}, bf16[512,1024]{1,0:T(8,128)(2,1)}, u32[]{:S(2)}) copy-start(bf16[512,1024]{1,0:T(8,128)(2,1)} %refs_8_) | copy-start | bytes 3145732
  0.7 17.5 %copy-start = (bf16[512,1024]{1,0:T(8,128)(2,1)S(1)}, bf16[512,1024]{1,0:T(8,128)(2,1)}, u32[]{:S(2)}) copy-start(bf16[512,1024]{1,0:T(8,128)(2,1)} %q_ref.6) | copy-start | bytes 3145732
  0.7 17.5 %copy-start.3 = (s32[8192]{0:T(1024)S(1)}, s32[8192]{0:T(1024)}, u32[]{:S(2)}) copy-start(s32[8192]{0:T(1024)} %param.15) | copy-start | bytes 98308
  3.0 6.5 %collective-permute-start = (bf16[512,512]{1,0:T(8,128)(2,1)}, bf16[512,512]{1,0:T(8,128)(2,1)}, u32[]{:S(2)}, u32[]{:S(2)}) collective-permute-start(bf16[512,512]{1,0:T(8,128)(2,1)} %get-tuple-element.145), channel_id=1, source_target_pairs={{0,8},{8,0},{16,24},{24,16},{32,40},{40,32},{48,56},{56,48},{64,72... | collective-permute-start | bytes 1572872 | tf_op jit(solution)/shard_map/ppermute | solution.py:50
  4.4 10.0 %collective-permute-start.2 = (bf16[512,256]{1,0:T(8,128)(2,1)S(1)}, bf16[512,256]{1,0:T(8,128)(2,1)S(1)}, u32[]{:S(2)}, u32[]{:S(2)}) collective-permute-start(bf16[512,256]{1,0:T(8,128)(2,1)S(1)} %pad_maximum_fusion.1), channel_id=1, source_target_pairs={{0,8},{8,16},{16,24},{24,32},{32,40},{40,48},{48,56},{56,64},{64,7... | collective-permute-start | bytes 786440 | tf_op jit(solution)/shard_map/ppermute | solution.py:64
  10.6 25.6 %collective-permute-start.1 = (bf16[1024,512]{1,0:T(8,128)(2,1)S(1)}, bf16[1024,512]{1,0:T(8,128)(2,1)S(1)}, u32[]{:S(2)}, u32[]{:S(2)}) collective-permute-start(bf16[1024,512]{1,0:T(8,128)(2,1)S(1)} %pad_maximum_fusion.refs_0_), channel_id=1, source_target_pairs={{0,4},{1,5},{2,6},{3,7},{4,0},{5,1},{6,2},{7,3},{8,12},{9,13},{10,... | collective-permute-start | bytes 3145736 | tf_op jit(solution)/shard_map/ppermute | solution.py:58
  11.0 25.7 %collective-permute-start.5 = (bf16[1024,512]{1,0:T(8,128)(2,1)S(1)}, bf16[1024,512]{1,0:T(8,128)(2,1)S(1)}, u32[]{:S(2)}, u32[]{:S(2)}) collective-permute-start(bf16[1024,512]{1,0:T(8,128)(2,1)S(1)} %pad_maximum_fusion.refs_0_), channel_id=1, source_target_pairs={{0,1},{1,2},{2,3},{3,0},{4,5},{5,6},{6,7},{7,4},{8,9},{9,10},{10,1... | collective-permute-start | bytes 3145736 | tf_op jit(solution)/shard_map/ppermute | solution.py:58
  12.2 25.1 %collective-permute-start.6 = (bf16[1024,512]{1,0:T(8,128)(2,1)S(1)}, bf16[1024,512]{1,0:T(8,128)(2,1)S(1)}, u32[]{:S(2)}, u32[]{:S(2)}) collective-permute-start(bf16[1024,512]{1,0:T(8,128)(2,1)S(1)} %pad_maximum_fusion.refs_0_), channel_id=1, source_target_pairs={{0,3},{1,0},{2,1},{3,2},{4,7},{5,4},{6,5},{7,6},{8,11},{9,8},{10,9... | collective-permute-start | bytes 3145736 | tf_op jit(solution)/shard_map/ppermute | solution.py:58
  14.5 26.9 %collective-permute-start.10 = (bf16[512,1024]{1,0:T(8,128)(2,1)S(1)}, bf16[512,1024]{1,0:T(8,128)(2,1)S(1)}, u32[]{:S(2)}, u32[]{:S(2)}) collective-permute-start(bf16[512,1024]{1,0:T(8,128)(2,1)S(1)} %copy-done.4), channel_id=1, source_target_pairs={{0,32},{8,40},{16,48},{24,56},{32,64},{40,72},{48,80},{56,88},{64,... | collective-permute-start | bytes 3145736 | tf_op jit(solution)/shard_map/ppermute | solution.py:50
  16.1 25.2 %collective-permute-start.11 = (bf16[512,1024]{1,0:T(8,128)(2,1)S(1)}, bf16[512,1024]{1,0:T(8,128)(2,1)S(1)}, u32[]{:S(2)}, u32[]{:S(2)}) collective-permute-start(bf16[512,1024]{1,0:T(8,128)(2,1)S(1)} %copy-done.4), channel_id=1, source_target_pairs={{0,96},{8,104},{16,112},{24,120},{32,0},{40,8},{48,16},{56,24},{64... | collective-permute-start | bytes 3145736 | tf_op jit(solution)/shard_map/ppermute | solution.py:50
  36.1 7.6 %collective-permute-start.7 = (bf16[512,1024]{1,0:T(8,128)(2,1)S(1)}, bf16[512,1024]{1,0:T(8,128)(2,1)S(1)}, u32[]{:S(2)}, u32[]{:S(2)}) collective-permute-start(bf16[512,1024]{1,0:T(8,128)(2,1)S(1)} %get-tuple-element.82), channel_id=1, source_target_pairs={{0,8},{8,0},{16,24},{24,16},{32,40},{40,32},{48,56},{56,48},{64,72... | collective-permute-start | bytes 3145736 | tf_op jit(solution)/shard_map/ppermute | solution.py:50
  36.8 26.1 %collective-permute-start.3 = (bf16[1024,512]{1,0:T(8,128)(2,1)S(1)}, bf16[1024,512]{1,0:T(8,128)(2,1)S(1)}, u32[]{:S(2)}, u32[]{:S(2)}) collective-permute-start(bf16[1024,512]{1,0:T(8,128)(2,1)S(1)} %collective-permute-done.1.refs_3_), channel_id=1, source_target_pairs={{0,1},{1,2},{2,3},{3,0},{4,5},{5,6},{6,7},{7,4},{8,9},{9,10},{10,1... | collective-permute-start | bytes 3145736 | tf_op jit(solution)/shard_map/ppermute | solution.py:58
  37.4 25.5 %collective-permute-start.4 = (bf16[1024,512]{1,0:T(8,128)(2,1)S(1)}, bf16[1024,512]{1,0:T(8,128)(2,1)S(1)}, u32[]{:S(2)}, u32[]{:S(2)}) collective-permute-start(bf16[1024,512]{1,0:T(8,128)(2,1)S(1)} %collective-permute-done.1.refs_3_), channel_id=1, source_target_pairs={{0,3},{1,0},{2,1},{3,2},{4,7},{5,4},{6,5},{7,6},{8,11},{9,8},{10,9... | collective-permute-start | bytes 3145736 | tf_op jit(solution)/shard_map/ppermute | solution.py:58
  41.3 24.8 %collective-permute-start.12 = (bf16[512,1024]{1,0:T(8,128)(2,1)S(1)}, bf16[512,1024]{1,0:T(8,128)(2,1)S(1)}, u32[]{:S(2)}, u32[]{:S(2)}) collective-permute-start(bf16[512,1024]{1,0:T(8,128)(2,1)S(1)} %collective-permute-done.10.refs_9_), channel_id=1, source_target_pairs={{0,32},{8,40},{16,48},{24,56},{32,64},{40,72},{48,80},{56,88},{64,... | collective-permute-start | bytes 3145736 | tf_op jit(solution)/shard_map/ppermute | solution.py:50
  41.3 24.8 %collective-permute-start.13 = (bf16[512,1024]{1,0:T(8,128)(2,1)S(1)}, bf16[512,1024]{1,0:T(8,128)(2,1)S(1)}, u32[]{:S(2)}, u32[]{:S(2)}) collective-permute-start(bf16[512,1024]{1,0:T(8,128)(2,1)S(1)} %copy-done.4), channel_id=1, source_target_pairs={{0,16},{8,24},{16,0},{24,8},{32,48},{40,56},{48,32},{56,40},{64,80... | collective-permute-start | bytes 3145736 | tf_op jit(solution)/shard_map/ppermute | solution.py:50
  43.8 41.5 %collective-permute-start.9 = (bf16[1024,512]{1,0:T(8,128)(2,1)S(1)}, bf16[1024,512]{1,0:T(8,128)(2,1)S(1)}, u32[]{:S(2)}, u32[]{:S(2)}) collective-permute-start(bf16[1024,512]{1,0:T(8,128)(2,1)S(1)} %collective-permute-done.5.refs_1_), channel_id=1, source_target_pairs={{0,1},{1,2},{2,3},{3,0},{4,5},{5,6},{6,7},{7,4},{8,9},{9,10},{10,1... | collective-permute-start | bytes 3145736 | tf_op jit(solution)/shard_map/ppermute | solution.py:58
  62.8 25.1 %collective-permute-start.8 = (bf16[1024,512]{1,0:T(8,128)(2,1)S(1)}, bf16[1024,512]{1,0:T(8,128)(2,1)S(1)}, u32[]{:S(2)}, u32[]{:S(2)}) collective-permute-start(bf16[1024,512]{1,0:T(8,128)(2,1)S(1)} %collective-permute-done.4.refs_1_.refs_5_), channel_id=1, source_target_pairs={{0,3},{1,0},{2,1},{3,2},{4,7},{5,4},{6,5},{7,6},{8,11},{9,8},{10,9... | collective-permute-start | bytes 3145736 | tf_op jit(solution)/shard_map/ppermute | solution.py:58
  66.2 28.3 %collective-permute-start.14 = (bf16[512,1024]{1,0:T(8,128)(2,1)S(1)}, bf16[512,1024]{1,0:T(8,128)(2,1)S(1)}, u32[]{:S(2)}, u32[]{:S(2)}) collective-permute-start(bf16[512,1024]{1,0:T(8,128)(2,1)S(1)} %collective-permute-done.13.refs_11_), channel_id=1, source_target_pairs={{0,32},{8,40},{16,48},{24,56},{32,64},{40,72},{48,80},{56,88},{64,... | collective-permute-start | bytes 3145736 | tf_op jit(solution)/shard_map/ppermute | solution.py:50
  67.2 28.9 %collective-permute-start.15 = (bf16[512,1024]{1,0:T(8,128)(2,1)S(1)}, bf16[512,1024]{1,0:T(8,128)(2,1)S(1)}, u32[]{:S(2)}, u32[]{:S(2)}) collective-permute-start(bf16[512,1024]{1,0:T(8,128)(2,1)S(1)} %collective-permute-done.13.refs_11_), channel_id=1, source_target_pairs={{0,96},{8,104},{16,112},{24,120},{32,0},{40,8},{48,16},{56,24},{64... | collective-permute-start | bytes 3145736 | tf_op jit(solution)/shard_map/ppermute | solution.py:50
  69.5 26.6 %collective-permute-start.16 = (bf16[512,1024]{1,0:T(8,128)(2,1)S(1)}, bf16[512,1024]{1,0:T(8,128)(2,1)S(1)}, u32[]{:S(2)}, u32[]{:S(2)}) collective-permute-start(bf16[512,1024]{1,0:T(8,128)(2,1)S(1)} %collective-permute-done.12.refs_15_), channel_id=1, source_target_pairs={{0,16},{8,24},{16,0},{24,8},{32,48},{40,56},{48,32},{56,40},{64,80... | collective-permute-start | bytes 3145736 | tf_op jit(solution)/shard_map/ppermute | solution.py:50
  91.0 31.8 %collective-permute-start.22 = (bf16[640,1024]{1,0:T(8,128)(2,1)S(1)}, bf16[640,1024]{1,0:T(8,128)(2,1)S(1)}, u32[]{:S(2)}, u32[]{:S(2)}) collective-permute-start(bf16[640,1024]{1,0:T(8,128)(2,1)S(1)} %get-tuple-element.86), channel_id=1, source_target_pairs={{0,32},{8,40},{16,48},{24,56},{32,64},{40,72},{48,80},{56,88},{64,... | collective-permute-start | bytes 3932168 | tf_op jit(solution)/shard_map/ppermute | solution.py:50
  92.1 27.3 %collective-permute-start.19 = (bf16[512,1024]{1,0:T(8,128)(2,1)S(1)}, bf16[512,1024]{1,0:T(8,128)(2,1)S(1)}, u32[]{:S(2)}, u32[]{:S(2)}) collective-permute-start(bf16[512,1024]{1,0:T(8,128)(2,1)S(1)} %get-tuple-element.101), channel_id=1, source_target_pairs={{0,16},{8,24},{16,0},{24,8},{32,48},{40,56},{48,32},{56,40},{64,80... | collective-permute-start | bytes 3145736 | tf_op jit(solution)/shard_map/ppermute | solution.py:50
  94.4 30.7 %collective-permute-start.23 = (bf16[640,1024]{1,0:T(8,128)(2,1)S(1)}, bf16[640,1024]{1,0:T(8,128)(2,1)S(1)}, u32[]{:S(2)}, u32[]{:S(2)}) collective-permute-start(bf16[640,1024]{1,0:T(8,128)(2,1)S(1)} %get-tuple-element.112), channel_id=1, source_target_pairs={{0,96},{8,104},{16,112},{24,120},{32,0},{40,8},{48,16},{56,24},{64... | collective-permute-start | bytes 3932168 | tf_op jit(solution)/shard_map/ppermute | solution.py:50
  108.7 5.0 %collective-permute-start.17 = (bf16[256,1024]{1,0:T(8,128)(2,1)S(1)}, bf16[256,1024]{1,0:T(8,128)(2,1)S(1)}, u32[]{:S(2)}, u32[]{:S(2)}) collective-permute-start(bf16[256,1024]{1,0:T(8,128)(2,1)S(1)} %get-tuple-element.95), channel_id=1, source_target_pairs={{0,8},{8,0},{16,24},{24,16},{32,40},{40,32},{48,56},{56,48},{64,72... | collective-permute-start | bytes 1572872 | tf_op jit(solution)/shard_map/ppermute | solution.py:50
  110.8 2.9 %collective-permute-start.18 = (bf16[256,1024]{1,0:T(8,128)(2,1)S(1)}, bf16[256,1024]{1,0:T(8,128)(2,1)S(1)}, u32[]{:S(2)}, u32[]{:S(2)}) collective-permute-start(bf16[256,1024]{1,0:T(8,128)(2,1)S(1)} %get-tuple-element.96), channel_id=1, source_target_pairs={{0,8},{8,0},{16,24},{24,16},{32,40},{40,32},{48,56},{56,48},{64,72... | collective-permute-start | bytes 1572872 | tf_op jit(solution)/shard_map/ppermute | solution.py:50
  119.7 15.2 %collective-permute-start.20 = (bf16[256,1024]{1,0:T(8,128)(2,1)S(1)}, bf16[256,1024]{1,0:T(8,128)(2,1)S(1)}, u32[]{:S(2)}, u32[]{:S(2)}) collective-permute-start(bf16[256,1024]{1,0:T(8,128)(2,1)S(1)} %get-tuple-element.106), channel_id=1, source_target_pairs={{0,32},{8,40},{16,48},{24,56},{32,64},{40,72},{48,80},{56,88},{64,... | collective-permute-start | bytes 1572872 | tf_op jit(solution)/shard_map/ppermute | solution.py:50
  119.8 15.3 %collective-permute-start.21 = (bf16[256,1024]{1,0:T(8,128)(2,1)S(1)}, bf16[256,1024]{1,0:T(8,128)(2,1)S(1)}, u32[]{:S(2)}, u32[]{:S(2)}) collective-permute-start(bf16[256,1024]{1,0:T(8,128)(2,1)S(1)} %get-tuple-element.107), channel_id=1, source_target_pairs={{0,96},{8,104},{16,112},{24,120},{32,0},{40,8},{48,16},{56,24},{64... | collective-permute-start | bytes 1572872 | tf_op jit(solution)/shard_map/ppermute | solution.py:50
  122.4 18.1 %collective-permute-start.24 = (bf16[128,1024]{1,0:T(8,128)(2,1)S(1)}, bf16[128,1024]{1,0:T(8,128)(2,1)S(1)}, u32[]{:S(2)}, u32[]{:S(2)}) collective-permute-start(bf16[128,1024]{1,0:T(8,128)(2,1)S(1)} %get-tuple-element.126), channel_id=1, source_target_pairs={{0,32},{8,40},{16,48},{24,56},{32,64},{40,72},{48,80},{56,88},{64,... | collective-permute-start | bytes 786440 | tf_op jit(solution)/shard_map/ppermute | solution.py:50
  122.8 17.9 %collective-permute-start.25 = (bf16[128,1024]{1,0:T(8,128)(2,1)S(1)}, bf16[128,1024]{1,0:T(8,128)(2,1)S(1)}, u32[]{:S(2)}, u32[]{:S(2)}) collective-permute-start(bf16[128,1024]{1,0:T(8,128)(2,1)S(1)} %get-tuple-element.127), channel_id=1, source_target_pairs={{0,96},{8,104},{16,112},{24,120},{32,0},{40,8},{48,16},{56,24},{64... | collective-permute-start | bytes 786440 | tf_op jit(solution)/shard_map/ppermute | solution.py:50
  125.5 29.7 %collective-permute-start.26 = (bf16[512,1024]{1,0:T(8,128)(2,1)S(1)}, bf16[512,1024]{1,0:T(8,128)(2,1)S(1)}, u32[]{:S(2)}, u32[]{:S(2)}) collective-permute-start(bf16[512,1024]{1,0:T(8,128)(2,1)S(1)} %add_rows.7), channel_id=1, source_target_pairs={{0,16},{8,24},{16,0},{24,8},{32,48},{40,56},{48,32},{56,40},{64,80... | collective-permute-start | bytes 3145736 | tf_op jit(solution)/shard_map/ppermute | solution.py:50
  135.3 19.9 %collective-permute-start.27 = (bf16[256,1024]{1,0:T(8,128)(2,1)S(1)}, bf16[256,1024]{1,0:T(8,128)(2,1)S(1)}, u32[]{:S(2)}, u32[]{:S(2)}) collective-permute-start(bf16[256,1024]{1,0:T(8,128)(2,1)S(1)} %get-tuple-element.131), channel_id=1, source_target_pairs={{0,32},{8,40},{16,48},{24,56},{32,64},{40,72},{48,80},{56,88},{64,... | collective-permute-start | bytes 1572872 | tf_op jit(solution)/shard_map/ppermute | solution.py:50
  140.7 14.5 %collective-permute-start.28 = (bf16[256,1024]{1,0:T(8,128)(2,1)S(1)}, bf16[256,1024]{1,0:T(8,128)(2,1)S(1)}, u32[]{:S(2)}, u32[]{:S(2)}) collective-permute-start(bf16[256,1024]{1,0:T(8,128)(2,1)S(1)} %get-tuple-element.138), channel_id=1, source_target_pairs={{0,96},{8,104},{16,112},{24,120},{32,0},{40,8},{48,16},{56,24},{64... | collective-permute-start | bytes 1572872 | tf_op jit(solution)/shard_map/ppermute | solution.py:50
  150.9 9.9 %collective-permute-start.29 = (bf16[512,256]{1,0:T(8,128)(2,1)S(1)}, bf16[512,256]{1,0:T(8,128)(2,1)S(1)}, u32[]{:S(2)}, u32[]{:S(2)}) collective-permute-start(bf16[512,256]{1,0:T(8,128)(2,1)S(1)} %pad_maximum_fusion.2), channel_id=1, source_target_pairs={{8,0},{16,8},{24,16},{32,24},{40,32},{48,40},{56,48},{64,56},{72,6... | collective-permute-start | bytes 786440 | tf_op jit(solution)/shard_map/ppermute | solution.py:64

commit v16 on v15

--- a/solution.py
+++ b/solution.py
@@ -550,16 +550,17 @@
     wy = move_row(out_proj, dyh=1)
 
     a_pair = jnp.concatenate([attn_out, a_other], 0)
-    proj = project([g0, gxm, gxp, gy], a_pair, meta, range(4), None)
 
     go = move_col(gxm, dx=1)
-    gyxm, gyxp, proj = tied((gyxm, gyxp, proj))
+    gyxm, gyxp = tied((gyxm, gyxp))
     gyo = move_col(gyxp, dx=-1)
     wo, wy = tied((wo, wy), gyxp)
     wyzm = move_row(wy, dz=1)
     wyzp = move_row(wy, dz=-1)
     wyo = move_row(wo, dyh=1)
 
+    (a_pair,) = tied((a_pair,), gyxp)
+    proj = project([g0, gxm, gxp, gy], a_pair, meta, range(4), None)
     proj = project([gyxm, gyxp], a_pair, meta, (4, 5), proj)
     proj = project([go], a_pair, meta, (6,), proj)
 

time: 162 us -> 165 us (1.019)
  waiting for transfers between devices: 38.3 us -> 40.9 us
    ppermute x21, waiting for transfers between devices: 7.09 us -> 11.3 us  [move_row(): return lax.ppermute(value, 'row', pairs)]
  transfers between devices with their start and end apart: 30 -> 30, of which waited for: 13 -> 13; matrix products, arithmetic and copies ran while one was open for 1% -> 1% of each run, Pallas kernels for 43% -> 42%
where the time goes in v16:
time: 165 us; the launch traced here: 164 us
  Pallas kernels  69.7 us (42%)
  starting transfers between devices  48.2 us (29%)
  waiting for transfers between devices  40.9 us (25%)
  local copies, waits for them, and re-layouts  2.38 us (1%)
  other arithmetic  2.15 us (1%)
    ppermute x21, starting transfers between devices, move_row(): return lax.ppermute(value, 'row', pairs)  31.1 us
    ppermute x7, waiting for transfers between devices, move_col(): return lax.ppermute(value, 'col', pairs)  25.1 us
    pallas_call x3, Pallas kernels, attend_back(): pl.pallas_call(functools.partial(bwd_kernel, len(earlier), last), grid_sp...  20.6 us
    pallas_call x4, Pallas kernels, project(): pl.pallas_call(functools.partial(proj_kernel, tuple(slots), held, plan),...  16.3 us
    pallas_call x1, Pallas kernels, attend(): pl.pallas_call(fwd_kernel, grid_spec=pltpu.PrefetchScalarGridSpec(num_sca...  14.9 us
    pallas_call x1, Pallas kernels, attn_grad_part(): pl.pallas_call(kernel, grid_spec=pltpu.PrefetchScalarGridSpec(num_scalar_...  12.6 us
    ppermute x21, waiting for transfers between devices, move_row(): return lax.ppermute(value, 'row', pairs)  11.3 us
    ppermute x2, starting transfers between devices, passed_along(): lax.ppermute(value, axis, [(source, source + steps) for source in range(f...  8.7 us
  transfers between devices with their start and end apart: 30, of which 13 were waited for; matrix products, arithmetic and copies ran while one was open for 1% of the time, Pallas kernels for 42%

profile of v16, /device:TPU:1, one launch (start us, length us, event | category | flops | bytes accessed | tf_op | source)
XLA Modules:
  0.0 164.3 jit_solution(12180193603328633402)
XLA Ops:
  0.6 0.0 copy-start.5
  0.6 0.0 copy-start.6
  0.7 2.2 %constant_dynamic-slice_fusion = (bf16[512,512]{1,0:T(8,128)(2,1)S(1)}, bf16[512,512]{1,0:T(8,128)(2,1)}) fusion(bf16[512,1024]{1,0:T(8,128)(2,1)} %param.13, s32[]{:T(128)S(6)} %select_n.38, s32[]{:T(128)S(6)} %select_n.32), kind=kLoop, calls=%fused_computation.12 | loop fusion | bytes 2097160 | tf_op jit(solution)/shard_map/dynamic_slice | solution.py:524
  3.0 1.4 collective-permute-start
  4.4 4.8 %collective-permute-start.2 = (bf16[512,256]{1,0:T(8,128)(2,1)S(1)}, bf16[512,256]{1,0:T(8,128)(2,1)S(1)}, u32[]{:S(2)}, u32[]{:S(2)}) collective-permute-start(bf16[512,256]{1,0:T(8,128)(2,1)S(1)} %pad_maximum_fusion.2), channel_id=1, source_target_pairs={{0,8},{8,16},{16,24},{24,32},{32,40},{40,48},{48,56},{56,64},{64,7... | collective-permute-start | bytes 786440 | tf_op jit(solution)/shard_map/ppermute | solution.py:64
  9.3 0.1 concatenate.16.meta_ref
  9.4 1.1 pad_maximum_fusion.1.refs_0_
  10.6 0.5 collective-permute-start.1
  11.0 1.2 collective-permute-start.7
  12.2 1.5 collective-permute-start.8
  13.7 0.7 collective-permute-done.2.kv_ref
  14.5 1.6 %collective-permute-start.10 = (bf16[512,1024]{1,0:T(8,128)(2,1)S(1)}, bf16[512,1024]{1,0:T(8,128)(2,1)S(1)}, u32[]{:S(2)}, u32[]{:S(2)}) collective-permute-start(bf16[512,1024]{1,0:T(8,128)(2,1)S(1)} %copy-done.4), channel_id=1, source_target_pairs={{0,32},{8,40},{16,48},{24,56},{32,64},{40,72},{48,80},{56,88},{64,... | collective-permute-start | bytes 3145736 | tf_op jit(solution)/shard_map/ppermute | solution.py:50
  16.1 2.1 %collective-permute-start.11 = (bf16[512,1024]{1,0:T(8,128)(2,1)S(1)}, bf16[512,1024]{1,0:T(8,128)(2,1)S(1)}, u32[]{:S(2)}, u32[]{:S(2)}) collective-permute-start(bf16[512,1024]{1,0:T(8,128)(2,1)S(1)} %copy-done.4), channel_id=1, source_target_pairs={{0,96},{8,104},{16,112},{24,120},{32,0},{40,8},{48,16},{56,24},{64... | collective-permute-start | bytes 3145736 | tf_op jit(solution)/shard_map/ppermute | solution.py:50
  18.2 14.9 %attend.1 = (bf16[512,1024]{1,0:T(8,128)(2,1)S(1)}, f32[8,1,512]{2,1,0:T(1,128)S(1)}, f32[8,1,512]{2,1,0:T(1,128)S(1)}) custom-call(s32[24]{0:T(128)S(1)} %concatenate.16.meta_ref, bf16[512,1024]{1,0:T(8,128)(2,1)S(1)} %copy-done, bf16[512,256]{1,0:T(8,128)(2,1)S(1)} %collective-permute-done.2.kv_ref, bf16[512,128]{1,0:T(8,128)(2,1)S(1)} %copy-done.2, ...), custom_call_target="tpu_custom_call" | custom-call | flops 68719476736 | bytes 8388608 | tf_op jit(solution)/shard_map/attend/pallas_call | solution.py:148
  33.1 3.0 %collective-permute-done.1.refs_3_ = bf16[1024,512]{1,0:T(8,128)(2,1)S(1)} collective-permute-done((bf16[1024,512]{1,0:T(8,128)(2,1)S(1)}, bf16[1024,512]{1,0:T(8,128)(2,1)S(1)}, u32[]{:S(2)}, u32[]{:S(2)}) %collective-permute-start.1) | collective-permute-done | bytes 1048608 | tf_op jit(solution)/shard_map/ppermute | solution.py:58
  36.1 1.2 collective-permute-start.3
  37.3 1.5 collective-permute-start.4
  38.8 2.5 %collective-permute-done.10.refs_9_ = bf16[512,1024]{1,0:T(8,128)(2,1)S(1)} collective-permute-done((bf16[512,1024]{1,0:T(8,128)(2,1)S(1)}, bf16[512,1024]{1,0:T(8,128)(2,1)S(1)}, u32[]{:S(2)}, u32[]{:S(2)}) %collective-permute-start.10) | collective-permute-done | bytes 1048608 | tf_op jit(solution)/shard_map/ppermute | solution.py:50
  41.3 0.0 collective-permute-start.12
  41.3 2.1 %collective-permute-start.13 = (bf16[512,1024]{1,0:T(8,128)(2,1)S(1)}, bf16[512,1024]{1,0:T(8,128)(2,1)S(1)}, u32[]{:S(2)}, u32[]{:S(2)}) collective-permute-start(bf16[512,1024]{1,0:T(8,128)(2,1)S(1)} %copy-done.4), channel_id=1, source_target_pairs={{0,16},{8,24},{16,0},{24,8},{32,48},{40,56},{48,32},{56,40},{64,80... | collective-permute-start | bytes 3145736 | tf_op jit(solution)/shard_map/ppermute | solution.py:50
  43.4 2.3 %collective-permute-start.6 = (bf16[512,1024]{1,0:T(8,128)(2,1)S(1)}, bf16[512,1024]{1,0:T(8,128)(2,1)S(1)}, u32[]{:S(2)}, u32[]{:S(2)}) collective-permute-start(bf16[512,1024]{1,0:T(8,128)(2,1)S(1)} %get-tuple-element.81), channel_id=1, source_target_pairs={{0,8},{8,0},{16,24},{24,16},{32,40},{40,32},{48,56},{56,48},{64,72... | collective-permute-start | bytes 3145736 | tf_op jit(solution)/shard_map/ppermute | solution.py:50
  45.8 15.3 %collective-permute-done.3.refs_0_.refs_4_ = bf16[1024,512]{1,0:T(8,128)(2,1)S(1)} collective-permute-done((bf16[1024,512]{1,0:T(8,128)(2,1)S(1)}, bf16[1024,512]{1,0:T(8,128)(2,1)S(1)}, u32[]{:S(2)}, u32[]{:S(2)}) %collective-permute-start.3) | collective-permute-done | bytes 1048608 | tf_op jit(solution)/shard_map/ppermute | solution.py:58
  61.1 0.1 collective-permute-start.9
  61.2 1.0 collective-permute-done.4.refs_1_.refs_5_
  62.2 2.5 %collective-permute-start.5 = (bf16[1024,512]{1,0:T(8,128)(2,1)S(1)}, bf16[1024,512]{1,0:T(8,128)(2,1)S(1)}, u32[]{:S(2)}, u32[]{:S(2)}) collective-permute-start(bf16[1024,512]{1,0:T(8,128)(2,1)S(1)} %collective-permute-done.4.refs_1_.refs_5_), channel_id=1, source_target_pairs={{0,3},{1,0},{2,1},{3,2},{4,7},{5,4},{6,5},{7,6},{8,11},{9,8},{10,9... | collective-permute-start | bytes 3145736 | tf_op jit(solution)/shard_map/ppermute | solution.py:58
  64.7 1.5 collective-permute-done.12.refs_15_
  66.2 1.0 collective-permute-start.14
  67.2 1.6 collective-permute-start.15
  68.9 1.4 collective-permute-start.16
  70.3 0.2 pad_maximum_fusion.refs_4_.refs_2_.refs_1_
  70.4 6.6 %project.4.refs_3_ = bf16[2,64,256,1024]{3,2,1,0:T(8,128)(2,1)} custom-call(s32[24]{0:T(128)S(1)} %concatenate.16.meta_ref, bf16[1024,512]{1,0:T(8,128)(2,1)S(1)} %pad_maximum_fusion.1.refs_0_, bf16[1024,512]{1,0:T(8,128)(2,1)S(1)} %collective-permute-done.7.refs_1_, bf16[1024,512]{1,0:T(8,128)(2,1)S(1)} %collective-permute-done.8.refs_2_, ...), custom_call_target="tpu_custom_call" | custom-call | flops 4294967296 | bytes 10485760 | tf_op jit(solution)/shard_map/project/pallas_call | solution.py:327
  77.1 4.0 %project.5.refs_2_ = bf16[2,64,256,1024]{3,2,1,0:T(8,128)(2,1)} custom-call(s32[24]{0:T(128)S(1)} %concatenate.16.meta_ref, bf16[1024,512]{1,0:T(8,128)(2,1)S(1)} %collective-permute-done.3.refs_0_.refs_4_, bf16[1024,512]{1,0:T(8,128)(2,1)S(1)} %collective-permute-done.4.refs_1_.refs_5_, ...), custom_call_target="tpu_custom_call", output_to_operand_aliasing={{}: (4, {})} | custom-call | flops 2147483648 | bytes 6291456 | tf_op jit(solution)/shard_map/project/pallas_call | solution.py:327
  81.1 5.8 %collective-permute-done.9.refs_0_.refs_6_ = bf16[1024,512]{1,0:T(8,128)(2,1)S(1)} collective-permute-done((bf16[1024,512]{1,0:T(8,128)(2,1)S(1)}, bf16[1024,512]{1,0:T(8,128)(2,1)S(1)}, u32[]{:S(2)}, u32[]{:S(2)}) %collective-permute-start.9) | collective-permute-done | bytes 1048608 | tf_op jit(solution)/shard_map/ppermute | solution.py:58
  86.8 2.6 %project.6.refs_2_ = bf16[2,64,256,1024]{3,2,1,0:T(8,128)(2,1)} custom-call(s32[24]{0:T(128)S(1)} %concatenate.16.meta_ref, bf16[1024,512]{1,0:T(8,128)(2,1)S(1)} %collective-permute-done.9.refs_0_.refs_6_, bf16[1024,1024]{1,0:T(8,128)(2,1)S(1)} %pad_maximum_fusion.refs_4_.refs_2_.refs_1_, ...), custom_call_target="tpu_custom_call", output_to_operand_aliasing={{}: (3, {})} | custom-call | flops 1073741824 | bytes 4194304 | tf_op jit(solution)/shard_map/project/pallas_call | solution.py:327
  89.5 3.0 %project.7 = (bf16[2,64,256,1024]{3,2,1,0:T(8,128)(2,1)}, bf16[512,1024]{1,0:T(8,128)(2,1)S(1)}, bf16[640,1024]{1,0:T(8,128)(2,1)S(1)}, bf16[640,1024]{1,0:T(8,1...) custom-call(s32[24]{0:T(128)S(1)} %concatenate.16.meta_ref, ...), custom_call_target="tpu_custom_call", output_to_operand_aliasing={{0}: (3, {})} | custom-call | flops 1073741824 | bytes 4194304 | tf_op jit(solution)/shard_map/project/pallas_call | solution.py:327
  92.5 1.9 %collective-permute-start.22 = (bf16[640,1024]{1,0:T(8,128)(2,1)S(1)}, bf16[640,1024]{1,0:T(8,128)(2,1)S(1)}, u32[]{:S(2)}, u32[]{:S(2)}) collective-permute-start(bf16[640,1024]{1,0:T(8,128)(2,1)S(1)} %get-tuple-element.86), channel_id=1, source_target_pairs={{0,32},{8,40},{16,48},{24,56},{32,64},{40,72},{48,80},{56,88},{64,... | collective-permute-start | bytes 3932168 | tf_op jit(solution)/shard_map/ppermute | solution.py:50
  94.4 2.8 %collective-permute-start.19 = (bf16[512,1024]{1,0:T(8,128)(2,1)S(1)}, bf16[512,1024]{1,0:T(8,128)(2,1)S(1)}, u32[]{:S(2)}, u32[]{:S(2)}) collective-permute-start(bf16[512,1024]{1,0:T(8,128)(2,1)S(1)} %get-tuple-element.101), channel_id=1, source_target_pairs={{0,16},{8,24},{16,0},{24,8},{32,48},{40,56},{48,32},{56,40},{64,80... | collective-permute-start | bytes 3145736 | tf_op jit(solution)/shard_map/ppermute | solution.py:50
  97.2 2.0 %collective-permute-start.23 = (bf16[640,1024]{1,0:T(8,128)(2,1)S(1)}, bf16[640,1024]{1,0:T(8,128)(2,1)S(1)}, u32[]{:S(2)}, u32[]{:S(2)}) collective-permute-start(bf16[640,1024]{1,0:T(8,128)(2,1)S(1)} %get-tuple-element.112), channel_id=1, source_target_pairs={{0,96},{8,104},{16,112},{24,120},{32,0},{40,8},{48,16},{56,24},{64... | collective-permute-start | bytes 3932168 | tf_op jit(solution)/shard_map/ppermute | solution.py:50
  99.1 12.6 %attn_grad.1 = (f32[512,1024]{1,0:T(8,128)S(1)}, bf16[256,1024]{1,0:T(8,128)(2,1)S(1)}, bf16[256,1024]{1,0:T(8,128)(2,1)S(1)}) custom-call(s32[24]{0:T(128)S(1)} %concatenate.16.meta_ref, bf16[1024,512]{1,0:T(8,128)(2,1)S(1)} %pad_maximum_fusion.1.refs_0_, bf16[1024,512]{1,0:T(8,128)(2,1)S(1)} %collective-permute-done.7.refs_1_, ...), custom_call_target="tpu_custom_call" | custom-call | flops 8589934592 | bytes 20971520 | tf_op jit(solution)/shard_map/attn_grad/pallas_call | solution.py:422
  111.7 1.2 collective-permute-start.17
  112.9 0.3 collective-permute-start.18
  113.2 2.8 %fetch.1 = (bf16[512,1024]{1,0:T(8,128)(2,1)S(1)}, bf16[512,1024]{1,0:T(8,128)(2,1)S(1)}, bf16[512,1024]{1,0:T(8,128)(2,1)S(1)}, bf16[512,1024]{1,0:T(8,128)(2,1)S(1)}) custom-call(s32[24]{0:T(128)S(1)} %concatenate.16.meta_ref, bf16[2,64,256,1024]{3,2,1,0:T(8,128)(2,1)} %get-tuple-element.99.buffer_ref), custom_call_target="tpu_custom_call" | custom-call | bytes 65536 | tf_op jit(solution)/shard_map/fetch/pallas_call | solution.py:469
  116.0 0.2 add_rows.5.g_ref
  116.2 5.5 %attend_back.3 = (bf16[512,1024]{1,0:T(8,128)(2,1)}, f32[1024,128]{1,0:T(8,128)S(1)}, f32[1024,128]{1,0:T(8,128)S(1)}) custom-call(s32[24]{0:T(128)S(1)} %concatenate.16.meta_ref, bf16[512,1024]{1,0:T(8,128)(2,1)S(1)} %copy-done, bf16[512,1024]{1,0:T(8,128)(2,1)S(1)} %add_rows.5.g_ref, bf16[512,256]{1,0:T(8,128)(2,1)S(1)} %collective-permute-done.2.kv_ref, ...), custom_call_target="tpu_custom_call" | custom-call | flops 1048576 | bytes 65536 | tf_op jit(solution)/shard_map/attend_back/pallas_call | solution.py:226
  121.7 0.2 add_rows.6
  122.0 0.6 collective-permute-start.20
  122.5 2.2 %collective-permute-start.21 = (bf16[256,1024]{1,0:T(8,128)(2,1)S(1)}, bf16[256,1024]{1,0:T(8,128)(2,1)S(1)}, u32[]{:S(2)}, u32[]{:S(2)}) collective-permute-start(bf16[256,1024]{1,0:T(8,128)(2,1)S(1)} %get-tuple-element.107), channel_id=1, source_target_pairs={{0,96},{8,104},{16,112},{24,120},{32,0},{40,8},{48,16},{56,24},{64... | collective-permute-start | bytes 1572872 | tf_op jit(solution)/shard_map/ppermute | solution.py:50
  124.7 1.0 collective-permute-done.22.refs_1_.refs_4_
  125.7 1.7 %collective-permute-start.25 = (bf16[128,1024]{1,0:T(8,128)(2,1)S(1)}, bf16[128,1024]{1,0:T(8,128)(2,1)S(1)}, u32[]{:S(2)}, u32[]{:S(2)}) collective-permute-start(bf16[128,1024]{1,0:T(8,128)(2,1)S(1)} %get-tuple-element.127), channel_id=1, source_target_pairs={{0,96},{8,104},{16,112},{24,120},{32,0},{40,8},{48,16},{56,24},{64... | collective-permute-start | bytes 786440 | tf_op jit(solution)/shard_map/ppermute | solution.py:50
  127.4 0.1 collective-permute-done.23.refs_2_.refs_6_
  127.5 0.4 add_rows.7
  127.9 1.3 collective-permute-start.26
  129.2 7.5 %attend_back.4 = (bf16[512,1024]{1,0:T(8,128)(2,1)}, f32[1024,128]{1,0:T(8,128)S(1)}, f32[1024,128]{1,0:T(8,128)S(1)}) custom-call(s32[24]{0:T(128)S(1)} %concatenate.16.meta_ref, bf16[512,1024]{1,0:T(8,128)(2,1)S(1)} %copy-done, bf16[512,1024]{1,0:T(8,128)(2,1)S(1)} %add_rows.5.g_ref, ...), custom_call_target="tpu_custom_call", output_to_operand_aliasing={{0}: (11, {})} | custom-call | flops 4026531840 | bytes 6291456 | tf_op jit(solution)/shard_map/attend_back/pallas_call | solution.py:226
  136.7 2.0 %collective-permute-done.21.refs_2_ = bf16[256,1024]{1,0:T(8,128)(2,1)S(1)} collective-permute-done((bf16[256,1024]{1,0:T(8,128)(2,1)S(1)}, bf16[256,1024]{1,0:T(8,128)(2,1)S(1)}, u32[]{:S(2)}, u32[]{:S(2)}) %collective-permute-start.21) | collective-permute-done | bytes 524320 | tf_op jit(solution)/shard_map/ppermute | solution.py:50
  138.8 0.2 add_rows.8
  139.0 1.2 collective-permute-start.27
  140.2 2.0 %collective-permute-done.24.refs_5_ = bf16[128,1024]{1,0:T(8,128)(2,1)S(1)} collective-permute-done((bf16[128,1024]{1,0:T(8,128)(2,1)S(1)}, bf16[128,1024]{1,0:T(8,128)(2,1)S(1)}, u32[]{:S(2)}, u32[]{:S(2)}) %collective-permute-start.24) | collective-permute-done | bytes 262176 | tf_op jit(solution)/shard_map/ppermute | solution.py:50
  142.2 2.2 %collective-permute-done.25.refs_7_ = bf16[128,1024]{1,0:T(8,128)(2,1)S(1)} collective-permute-done((bf16[128,1024]{1,0:T(8,128)(2,1)S(1)}, bf16[128,1024]{1,0:T(8,128)(2,1)S(1)}, u32[]{:S(2)}, u32[]{:S(2)}) %collective-permute-start.25) | collective-permute-done | bytes 262176 | tf_op jit(solution)/shard_map/ppermute | solution.py:50
  144.4 2.3 %collective-permute-start.28 = (bf16[256,1024]{1,0:T(8,128)(2,1)S(1)}, bf16[256,1024]{1,0:T(8,128)(2,1)S(1)}, u32[]{:S(2)}, u32[]{:S(2)}) collective-permute-start(bf16[256,1024]{1,0:T(8,128)(2,1)S(1)} %get-tuple-element.138), channel_id=1, source_target_pairs={{0,96},{8,104},{16,112},{24,120},{32,0},{40,8},{48,16},{56,24},{64... | collective-permute-start | bytes 1572872 | tf_op jit(solution)/shard_map/ppermute | solution.py:50
  146.7 7.6 %attend_back.5 = (bf16[512,1024]{1,0:T(8,128)(2,1)}, f32[1024,128]{1,0:T(8,128)S(1)}, f32[1024,128]{1,0:T(8,128)S(1)}) custom-call(s32[24]{0:T(128)S(1)} %concatenate.16.meta_ref, bf16[512,1024]{1,0:T(8,128)(2,1)S(1)} %copy-done, bf16[512,1024]{1,0:T(8,128)(2,1)S(1)} %add_rows.5.g_ref, ...), custom_call_target="tpu_custom_call", output_to_operand_aliasing={{0}: (11, {})} | custom-call | flops 4026531840 | bytes 6291456 | tf_op jit(solution)/shard_map/attend_back/pallas_call | solution.py:226
  154.3 3.9 %collective-permute-start.29 = (bf16[512,256]{1,0:T(8,128)(2,1)S(1)}, bf16[512,256]{1,0:T(8,128)(2,1)S(1)}, u32[]{:S(2)}, u32[]{:S(2)}) collective-permute-start(bf16[512,256]{1,0:T(8,128)(2,1)S(1)} %pad_maximum_fusion.3), channel_id=1, source_target_pairs={{8,0},{16,8},{24,16},{32,24},{40,32},{48,40},{56,48},{64,56},{72,6... | collective-permute-start | bytes 786440 | tf_op jit(solution)/shard_map/ppermute | solution.py:64
  158.3 1.5 add_rows.9
  159.8 3.8 %collective-permute-done.29 = bf16[512,256]{1,0:T(8,128)(2,1)S(1)} collective-permute-done((bf16[512,256]{1,0:T(8,128)(2,1)S(1)}, bf16[512,256]{1,0:T(8,128)(2,1)S(1)}, u32[]{:S(2)}, u32[]{:S(2)}) %collective-permute-start.29) | collective-permute-done | bytes 262176 | tf_op jit(solution)/shard_map/ppermute | solution.py:64
  163.6 0.8 fusion
  (38 shorter events, 0.2 us)
Async XLA Ops:
  0.6 8.7 %copy-start.5 = (s32[8]{0:T(128)S(1)}, s32[8]{0:T(128)}, u32[]{:S(2)}) copy-start(s32[8]{0:T(128)} %constant.79.clone) | copy-start | bytes 100
  0.6 8.7 %copy-start.6 = (s32[8]{0:T(128)S(1)}, s32[8]{0:T(128)}, u32[]{:S(2)}) copy-start(s32[8]{0:T(128)} %constant.80.clone) | copy-start | bytes 100
  0.7 8.7 %copy-start.7 = (s32[8]{0:T(128)S(1)}, s32[8]{0:T(128)}, u32[]{:S(2)}) copy-start(s32[8]{0:T(128)} %constant.81.clone) | copy-start | bytes 100
  0.7 3.7 %copy-start.2 = (bf16[512,128]{1,0:T(8,128)(2,1)S(1)}, bf16[512,128]{1,0:T(8,128)(2,1)}, u32[]{:S(2)}) copy-start(bf16[512,128]{1,0:T(8,128)(2,1)} %k_ref.7) | copy-start | bytes 393220
  0.7 3.7 %copy-start.1 = (bf16[512,128]{1,0:T(8,128)(2,1)S(1)}, bf16[512,128]{1,0:T(8,128)(2,1)}, u32[]{:S(2)}) copy-start(bf16[512,128]{1,0:T(8,128)(2,1)} %v_ref.7) | copy-start | bytes 393220
  0.7 13.7 %copy-start.4 = (bf16[512,1024]{1,0:T(8,128)(2,1)S(1)}, bf16[512,1024]{1,0:T(8,128)(2,1)}, u32[]{:S(2)}) copy-start(bf16[512,1024]{1,0:T(8,128)(2,1)} %refs_8_) | copy-start | bytes 3145732
  0.7 17.5 %copy-start = (bf16[512,1024]{1,0:T(8,128)(2,1)S(1)}, bf16[512,1024]{1,0:T(8,128)(2,1)}, u32[]{:S(2)}) copy-start(bf16[512,1024]{1,0:T(8,128)(2,1)} %q_ref.6) | copy-start | bytes 3145732
  0.7 17.5 %copy-start.3 = (s32[8192]{0:T(1024)S(1)}, s32[8192]{0:T(1024)}, u32[]{:S(2)}) copy-start(s32[8192]{0:T(1024)} %param.15) | copy-start | bytes 98308
  3.0 6.5 %collective-permute-start = (bf16[512,512]{1,0:T(8,128)(2,1)}, bf16[512,512]{1,0:T(8,128)(2,1)}, u32[]{:S(2)}, u32[]{:S(2)}) collective-permute-start(bf16[512,512]{1,0:T(8,128)(2,1)} %get-tuple-element.145), channel_id=1, source_target_pairs={{0,8},{8,0},{16,24},{24,16},{32,40},{40,32},{48,56},{56,48},{64,72... | collective-permute-start | bytes 1572872 | tf_op jit(solution)/shard_map/ppermute | solution.py:50
  4.4 10.0 %collective-permute-start.2 = (bf16[512,256]{1,0:T(8,128)(2,1)S(1)}, bf16[512,256]{1,0:T(8,128)(2,1)S(1)}, u32[]{:S(2)}, u32[]{:S(2)}) collective-permute-start(bf16[512,256]{1,0:T(8,128)(2,1)S(1)} %pad_maximum_fusion.2), channel_id=1, source_target_pairs={{0,8},{8,16},{16,24},{24,32},{32,40},{40,48},{48,56},{56,64},{64,7... | collective-permute-start | bytes 786440 | tf_op jit(solution)/shard_map/ppermute | solution.py:64
  10.6 25.6 %collective-permute-start.1 = (bf16[1024,512]{1,0:T(8,128)(2,1)S(1)}, bf16[1024,512]{1,0:T(8,128)(2,1)S(1)}, u32[]{:S(2)}, u32[]{:S(2)}) collective-permute-start(bf16[1024,512]{1,0:T(8,128)(2,1)S(1)} %pad_maximum_fusion.1.refs_0_), channel_id=1, source_target_pairs={{0,4},{1,5},{2,6},{3,7},{4,0},{5,1},{6,2},{7,3},{8,12},{9,13},{10,... | collective-permute-start | bytes 3145736 | tf_op jit(solution)/shard_map/ppermute | solution.py:58
  11.0 26.3 %collective-permute-start.7 = (bf16[1024,512]{1,0:T(8,128)(2,1)S(1)}, bf16[1024,512]{1,0:T(8,128)(2,1)S(1)}, u32[]{:S(2)}, u32[]{:S(2)}) collective-permute-start(bf16[1024,512]{1,0:T(8,128)(2,1)S(1)} %pad_maximum_fusion.1.refs_0_), channel_id=1, source_target_pairs={{0,1},{1,2},{2,3},{3,0},{4,5},{5,6},{6,7},{7,4},{8,9},{9,10},{10,1... | collective-permute-start | bytes 3145736 | tf_op jit(solution)/shard_map/ppermute | solution.py:58
  12.2 26.6 %collective-permute-start.8 = (bf16[1024,512]{1,0:T(8,128)(2,1)S(1)}, bf16[1024,512]{1,0:T(8,128)(2,1)S(1)}, u32[]{:S(2)}, u32[]{:S(2)}) collective-permute-start(bf16[1024,512]{1,0:T(8,128)(2,1)S(1)} %pad_maximum_fusion.1.refs_0_), channel_id=1, source_target_pairs={{0,3},{1,0},{2,1},{3,2},{4,7},{5,4},{6,5},{7,6},{8,11},{9,8},{10,9... | collective-permute-start | bytes 3145736 | tf_op jit(solution)/shard_map/ppermute | solution.py:58
  14.5 26.9 %collective-permute-start.10 = (bf16[512,1024]{1,0:T(8,128)(2,1)S(1)}, bf16[512,1024]{1,0:T(8,128)(2,1)S(1)}, u32[]{:S(2)}, u32[]{:S(2)}) collective-permute-start(bf16[512,1024]{1,0:T(8,128)(2,1)S(1)} %copy-done.4), channel_id=1, source_target_pairs={{0,32},{8,40},{16,48},{24,56},{32,64},{40,72},{48,80},{56,88},{64,... | collective-permute-start | bytes 3145736 | tf_op jit(solution)/shard_map/ppermute | solution.py:50
  16.1 25.2 %collective-permute-start.11 = (bf16[512,1024]{1,0:T(8,128)(2,1)S(1)}, bf16[512,1024]{1,0:T(8,128)(2,1)S(1)}, u32[]{:S(2)}, u32[]{:S(2)}) collective-permute-start(bf16[512,1024]{1,0:T(8,128)(2,1)S(1)} %copy-done.4), channel_id=1, source_target_pairs={{0,96},{8,104},{16,112},{24,120},{32,0},{40,8},{48,16},{56,24},{64... | collective-permute-start | bytes 3145736 | tf_op jit(solution)/shard_map/ppermute | solution.py:50
  36.1 25.0 %collective-permute-start.3 = (bf16[1024,512]{1,0:T(8,128)(2,1)S(1)}, bf16[1024,512]{1,0:T(8,128)(2,1)S(1)}, u32[]{:S(2)}, u32[]{:S(2)}) collective-permute-start(bf16[1024,512]{1,0:T(8,128)(2,1)S(1)} %collective-permute-done.1.refs_3_), channel_id=1, source_target_pairs={{0,1},{1,2},{2,3},{3,0},{4,5},{5,6},{6,7},{7,4},{8,9},{9,10},{10,1... | collective-permute-start | bytes 3145736 | tf_op jit(solution)/shard_map/ppermute | solution.py:58
  37.3 24.9 %collective-permute-start.4 = (bf16[1024,512]{1,0:T(8,128)(2,1)S(1)}, bf16[1024,512]{1,0:T(8,128)(2,1)S(1)}, u32[]{:S(2)}, u32[]{:S(2)}) collective-permute-start(bf16[1024,512]{1,0:T(8,128)(2,1)S(1)} %collective-permute-done.1.refs_3_), channel_id=1, source_target_pairs={{0,3},{1,0},{2,1},{3,2},{4,7},{5,4},{6,5},{7,6},{8,11},{9,8},{10,9... | collective-permute-start | bytes 3145736 | tf_op jit(solution)/shard_map/ppermute | solution.py:58
  41.3 24.8 %collective-permute-start.12 = (bf16[512,1024]{1,0:T(8,128)(2,1)S(1)}, bf16[512,1024]{1,0:T(8,128)(2,1)S(1)}, u32[]{:S(2)}, u32[]{:S(2)}) collective-permute-start(bf16[512,1024]{1,0:T(8,128)(2,1)S(1)} %collective-permute-done.10.refs_9_), channel_id=1, source_target_pairs={{0,32},{8,40},{16,48},{24,56},{32,64},{40,72},{48,80},{56,88},{64,... | collective-permute-start | bytes 3145736 | tf_op jit(solution)/shard_map/ppermute | solution.py:50
  41.3 24.8 %collective-permute-start.13 = (bf16[512,1024]{1,0:T(8,128)(2,1)S(1)}, bf16[512,1024]{1,0:T(8,128)(2,1)S(1)}, u32[]{:S(2)}, u32[]{:S(2)}) collective-permute-start(bf16[512,1024]{1,0:T(8,128)(2,1)S(1)} %copy-done.4), channel_id=1, source_target_pairs={{0,16},{8,24},{16,0},{24,8},{32,48},{40,56},{48,32},{56,40},{64,80... | collective-permute-start | bytes 3145736 | tf_op jit(solution)/shard_map/ppermute | solution.py:50
  43.4 25.4 %collective-permute-start.6 = (bf16[512,1024]{1,0:T(8,128)(2,1)S(1)}, bf16[512,1024]{1,0:T(8,128)(2,1)S(1)}, u32[]{:S(2)}, u32[]{:S(2)}) collective-permute-start(bf16[512,1024]{1,0:T(8,128)(2,1)S(1)} %get-tuple-element.81), channel_id=1, source_target_pairs={{0,8},{8,0},{16,24},{24,16},{32,40},{40,32},{48,56},{56,48},{64,72... | collective-permute-start | bytes 3145736 | tf_op jit(solution)/shard_map/ppermute | solution.py:50
  61.1 25.7 %collective-permute-start.9 = (bf16[1024,512]{1,0:T(8,128)(2,1)S(1)}, bf16[1024,512]{1,0:T(8,128)(2,1)S(1)}, u32[]{:S(2)}, u32[]{:S(2)}) collective-permute-start(bf16[1024,512]{1,0:T(8,128)(2,1)S(1)} %collective-permute-done.7.refs_1_), channel_id=1, source_target_pairs={{0,1},{1,2},{2,3},{3,0},{4,5},{5,6},{6,7},{7,4},{8,9},{9,10},{10,1... | collective-permute-start | bytes 3145736 | tf_op jit(solution)/shard_map/ppermute | solution.py:58
  62.2 27.3 %collective-permute-start.5 = (bf16[1024,512]{1,0:T(8,128)(2,1)S(1)}, bf16[1024,512]{1,0:T(8,128)(2,1)S(1)}, u32[]{:S(2)}, u32[]{:S(2)}) collective-permute-start(bf16[1024,512]{1,0:T(8,128)(2,1)S(1)} %collective-permute-done.4.refs_1_.refs_5_), channel_id=1, source_target_pairs={{0,3},{1,0},{2,1},{3,2},{4,7},{5,4},{6,5},{7,6},{8,11},{9,8},{10,9... | collective-permute-start | bytes 3145736 | tf_op jit(solution)/shard_map/ppermute | solution.py:58
  66.2 31.0 %collective-permute-start.14 = (bf16[512,1024]{1,0:T(8,128)(2,1)S(1)}, bf16[512,1024]{1,0:T(8,128)(2,1)S(1)}, u32[]{:S(2)}, u32[]{:S(2)}) collective-permute-start(bf16[512,1024]{1,0:T(8,128)(2,1)S(1)} %collective-permute-done.13.refs_11_), channel_id=1, source_target_pairs={{0,32},{8,40},{16,48},{24,56},{32,64},{40,72},{48,80},{56,88},{64,... | collective-permute-start | bytes 3145736 | tf_op jit(solution)/shard_map/ppermute | solution.py:50
  67.2 31.9 %collective-permute-start.15 = (bf16[512,1024]{1,0:T(8,128)(2,1)S(1)}, bf16[512,1024]{1,0:T(8,128)(2,1)S(1)}, u32[]{:S(2)}, u32[]{:S(2)}) collective-permute-start(bf16[512,1024]{1,0:T(8,128)(2,1)S(1)} %collective-permute-done.13.refs_11_), channel_id=1, source_target_pairs={{0,96},{8,104},{16,112},{24,120},{32,0},{40,8},{48,16},{56,24},{64... | collective-permute-start | bytes 3145736 | tf_op jit(solution)/shard_map/ppermute | solution.py:50
  68.9 30.3 %collective-permute-start.16 = (bf16[512,1024]{1,0:T(8,128)(2,1)S(1)}, bf16[512,1024]{1,0:T(8,128)(2,1)S(1)}, u32[]{:S(2)}, u32[]{:S(2)}) collective-permute-start(bf16[512,1024]{1,0:T(8,128)(2,1)S(1)} %collective-permute-done.12.refs_15_), channel_id=1, source_target_pairs={{0,16},{8,24},{16,0},{24,8},{32,48},{40,56},{48,32},{56,40},{64,80... | collective-permute-start | bytes 3145736 | tf_op jit(solution)/shard_map/ppermute | solution.py:50
  92.5 33.2 %collective-permute-start.22 = (bf16[640,1024]{1,0:T(8,128)(2,1)S(1)}, bf16[640,1024]{1,0:T(8,128)(2,1)S(1)}, u32[]{:S(2)}, u32[]{:S(2)}) collective-permute-start(bf16[640,1024]{1,0:T(8,128)(2,1)S(1)} %get-tuple-element.86), channel_id=1, source_target_pairs={{0,32},{8,40},{16,48},{24,56},{32,64},{40,72},{48,80},{56,88},{64,... | collective-permute-start | bytes 3932168 | tf_op jit(solution)/shard_map/ppermute | solution.py:50
  94.4 27.4 %collective-permute-start.19 = (bf16[512,1024]{1,0:T(8,128)(2,1)S(1)}, bf16[512,1024]{1,0:T(8,128)(2,1)S(1)}, u32[]{:S(2)}, u32[]{:S(2)}) collective-permute-start(bf16[512,1024]{1,0:T(8,128)(2,1)S(1)} %get-tuple-element.101), channel_id=1, source_target_pairs={{0,16},{8,24},{16,0},{24,8},{32,48},{40,56},{48,32},{56,40},{64,80... | collective-permute-start | bytes 3145736 | tf_op jit(solution)/shard_map/ppermute | solution.py:50
  97.2 30.4 %collective-permute-start.23 = (bf16[640,1024]{1,0:T(8,128)(2,1)S(1)}, bf16[640,1024]{1,0:T(8,128)(2,1)S(1)}, u32[]{:S(2)}, u32[]{:S(2)}) collective-permute-start(bf16[640,1024]{1,0:T(8,128)(2,1)S(1)} %get-tuple-element.112), channel_id=1, source_target_pairs={{0,96},{8,104},{16,112},{24,120},{32,0},{40,8},{48,16},{56,24},{64... | collective-permute-start | bytes 3932168 | tf_op jit(solution)/shard_map/ppermute | solution.py:50
  111.7 4.3 %collective-permute-start.17 = (bf16[256,1024]{1,0:T(8,128)(2,1)S(1)}, bf16[256,1024]{1,0:T(8,128)(2,1)S(1)}, u32[]{:S(2)}, u32[]{:S(2)}) collective-permute-start(bf16[256,1024]{1,0:T(8,128)(2,1)S(1)} %get-tuple-element.95), channel_id=1, source_target_pairs={{0,8},{8,0},{16,24},{24,16},{32,40},{40,32},{48,56},{56,48},{64,72... | collective-permute-start | bytes 1572872 | tf_op jit(solution)/shard_map/ppermute | solution.py:50
  112.9 3.1 %collective-permute-start.18 = (bf16[256,1024]{1,0:T(8,128)(2,1)S(1)}, bf16[256,1024]{1,0:T(8,128)(2,1)S(1)}, u32[]{:S(2)}, u32[]{:S(2)}) collective-permute-start(bf16[256,1024]{1,0:T(8,128)(2,1)S(1)} %get-tuple-element.96), channel_id=1, source_target_pairs={{0,8},{8,0},{16,24},{24,16},{32,40},{40,32},{48,56},{56,48},{64,72... | collective-permute-start | bytes 1572872 | tf_op jit(solution)/shard_map/ppermute | solution.py:50
  122.0 14.8 %collective-permute-start.20 = (bf16[256,1024]{1,0:T(8,128)(2,1)S(1)}, bf16[256,1024]{1,0:T(8,128)(2,1)S(1)}, u32[]{:S(2)}, u32[]{:S(2)}) collective-permute-start(bf16[256,1024]{1,0:T(8,128)(2,1)S(1)} %get-tuple-element.106), channel_id=1, source_target_pairs={{0,32},{8,40},{16,48},{24,56},{32,64},{40,72},{48,80},{56,88},{64,... | collective-permute-start | bytes 1572872 | tf_op jit(solution)/shard_map/ppermute | solution.py:50
  122.5 16.2 %collective-permute-start.21 = (bf16[256,1024]{1,0:T(8,128)(2,1)S(1)}, bf16[256,1024]{1,0:T(8,128)(2,1)S(1)}, u32[]{:S(2)}, u32[]{:S(2)}) collective-permute-start(bf16[256,1024]{1,0:T(8,128)(2,1)S(1)} %get-tuple-element.107), channel_id=1, source_target_pairs={{0,96},{8,104},{16,112},{24,120},{32,0},{40,8},{48,16},{56,24},{64... | collective-permute-start | bytes 1572872 | tf_op jit(solution)/shard_map/ppermute | solution.py:50
  124.7 17.5 %collective-permute-start.24 = (bf16[128,1024]{1,0:T(8,128)(2,1)S(1)}, bf16[128,1024]{1,0:T(8,128)(2,1)S(1)}, u32[]{:S(2)}, u32[]{:S(2)}) collective-permute-start(bf16[128,1024]{1,0:T(8,128)(2,1)S(1)} %get-tuple-element.126), channel_id=1, source_target_pairs={{0,32},{8,40},{16,48},{24,56},{32,64},{40,72},{48,80},{56,88},{64,... | collective-permute-start | bytes 786440 | tf_op jit(solution)/shard_map/ppermute | solution.py:50
  125.7 18.7 %collective-permute-start.25 = (bf16[128,1024]{1,0:T(8,128)(2,1)S(1)}, bf16[128,1024]{1,0:T(8,128)(2,1)S(1)}, u32[]{:S(2)}, u32[]{:S(2)}) collective-permute-start(bf16[128,1024]{1,0:T(8,128)(2,1)S(1)} %get-tuple-element.127), channel_id=1, source_target_pairs={{0,96},{8,104},{16,112},{24,120},{32,0},{40,8},{48,16},{56,24},{64... | collective-permute-start | bytes 786440 | tf_op jit(solution)/shard_map/ppermute | solution.py:50
  127.9 30.4 %collective-permute-start.26 = (bf16[512,1024]{1,0:T(8,128)(2,1)S(1)}, bf16[512,1024]{1,0:T(8,128)(2,1)S(1)}, u32[]{:S(2)}, u32[]{:S(2)}) collective-permute-start(bf16[512,1024]{1,0:T(8,128)(2,1)S(1)} %add_rows.7), channel_id=1, source_target_pairs={{0,16},{8,24},{16,0},{24,8},{32,48},{40,56},{48,32},{56,40},{64,80... | collective-permute-start | bytes 3145736 | tf_op jit(solution)/shard_map/ppermute | solution.py:50
  139.0 19.2 %collective-permute-start.27 = (bf16[256,1024]{1,0:T(8,128)(2,1)S(1)}, bf16[256,1024]{1,0:T(8,128)(2,1)S(1)}, u32[]{:S(2)}, u32[]{:S(2)}) collective-permute-start(bf16[256,1024]{1,0:T(8,128)(2,1)S(1)} %get-tuple-element.131), channel_id=1, source_target_pairs={{0,32},{8,40},{16,48},{24,56},{32,64},{40,72},{48,80},{56,88},{64,... | collective-permute-start | bytes 1572872 | tf_op jit(solution)/shard_map/ppermute | solution.py:50
  144.4 13.9 %collective-permute-start.28 = (bf16[256,1024]{1,0:T(8,128)(2,1)S(1)}, bf16[256,1024]{1,0:T(8,128)(2,1)S(1)}, u32[]{:S(2)}, u32[]{:S(2)}) collective-permute-start(bf16[256,1024]{1,0:T(8,128)(2,1)S(1)} %get-tuple-element.138), channel_id=1, source_target_pairs={{0,96},{8,104},{16,112},{24,120},{32,0},{40,8},{48,16},{56,24},{64... | collective-permute-start | bytes 1572872 | tf_op jit(solution)/shard_map/ppermute | solution.py:50
  154.3 9.2 %collective-permute-start.29 = (bf16[512,256]{1,0:T(8,128)(2,1)S(1)}, bf16[512,256]{1,0:T(8,128)(2,1)S(1)}, u32[]{:S(2)}, u32[]{:S(2)}) collective-permute-start(bf16[512,256]{1,0:T(8,128)(2,1)S(1)} %pad_maximum_fusion.3), channel_id=1, source_target_pairs={{8,0},{16,8},{24,16},{32,24},{40,32},{48,40},{56,48},{64,56},{72,6... | collective-permute-start | bytes 786440 | tf_op jit(solution)/shard_map/ppermute | solution.py:64
